TPU v7x, 32 devices: a whole 2x2x4 slice. The times are simulated.
32 devices in a mesh: blk: 4 (over y, x), grp: 8 (over z, core).
Axes of the slice: x: 2, y: 2, z: 4, core: 2. Of those that a mesh axis runs over, the one named last changes fastest.
Arguments:
- picture_vectors: bfloat16 [4096, 1152], P(('blk', 'grp')), may hold values from -1.1953125 to 1.1953125
- caption_vectors: bfloat16 [4096, 1152], P(('blk', 'grp')), may hold values from -1.1953125 to 1.1953125
- matching_caption: int32 [4096], P(('blk', 'grp')), may hold values from 0 to 4095, each once
- sharpness_parameter: float32 [1], replicated, may hold values from 1 to 4
- additive_intercept: float32 [1], replicated, may hold values from -6 to -2
Outputs:
- picture_derivative: float32 [4096, 1152], P(('blk', 'grp'))
- text_grad: float32 [4096, 1152], P(('blk', 'grp'))
Inputs may be any that keep to these rules, and one draw needn't show every extreme that they name: matching_caption is a permutation: each text is the positive of exactly one image.
All inputs are finite; a program needn't handle non-finite values.
Results may differ from a plain program's by a relative error of at most 0.0011.
Values may be sent and summed in bfloat16 or wider, within the bound.
No kernel may reach another device: no remote copies, remote signals or barrier semaphores. Data moves between devices by JAX's collectives and lax.ppermute only.
A program may use at most 64 MiB of HBM per device.

v0:
```python
import jax
import jax.numpy as jnp
from jax import lax
from jax.sharding import PartitionSpec as P


def passed_along(block, axis, distance):
    devices = range(lax.axis_size(axis))
    route = [((i - distance) % len(devices), i) for i in devices]
    return lax.ppermute(block, axis, route)


def rotation_step(
    cohort_pictures,
    cohort_labels,
    guest_captions,
    caption_numbers,
    sharpness_factor,
    moved_intercept,
):
    similarity_matrix = lax.dot_general(
        cohort_pictures,
        guest_captions,
        (((1,), (1,)), ((), ())),
        preferred_element_type=jnp.float32,
    )
    matching_pair = (cohort_labels[:, None] == caption_numbers[None, :]).astype(jnp.float32)
    pair_coefficients = (
        jax.nn.sigmoid(sharpness_factor * similarity_matrix + moved_intercept) - matching_pair
    ).astype(jnp.bfloat16)
    image_part = jnp.dot(pair_coefficients, guest_captions, preferred_element_type=jnp.float32)
    partial_value = lax.dot_general(
        pair_coefficients,
        cohort_pictures,
        (((0,), (0,)), ((), ())),
        preferred_element_type=jnp.float32,
    )
    return (image_part, partial_value)


def per_device(
    picture_vectors, caption_vectors, matching_caption, sharpness_parameter, additive_intercept
):
    sharpness_factor = sharpness_parameter[0]
    moved_intercept = additive_intercept[0]
    local_count = picture_vectors.shape[0]
    width = picture_vectors.shape[1]
    block_total = lax.axis_size("blk")
    grp_count = lax.axis_size("grp")
    current_block = lax.axis_index("blk")
    current_group = lax.axis_index("grp")
    local_ids = jnp.arange(local_count, dtype=jnp.int32)
    cohort_pictures, cohort_labels = (
        lax.all_gather(picture_vectors, "grp", axis=0, tiled=True),
        lax.all_gather(matching_caption, "grp", axis=0, tiled=True),
    )
    image_total = jnp.zeros((cohort_pictures.shape[0], width), jnp.float32)
    holding_buffer = jnp.zeros((block_total, local_count, width), jnp.float32)
    guest_captions = caption_vectors
    for turn in range(block_total):
        source = (current_block - turn + block_total) % block_total
        caption_numbers = (source * grp_count + current_group) * local_count + local_ids
        image_part, partial_value = rotation_step(
            cohort_pictures,
            cohort_labels,
            guest_captions,
            caption_numbers,
            sharpness_factor,
            moved_intercept,
        )
        image_total = image_total + image_part
        holding_buffer = lax.dynamic_update_index_in_dim(holding_buffer, partial_value, source, 0)
        if turn + 1 < block_total:
            guest_captions = passed_along(guest_captions, "blk", 1)
    picture_derivative = sharpness_factor * lax.psum_scatter(
        image_total, "grp", scatter_dimension=0, tiled=True
    )
    text_grad = (
        sharpness_factor
        * lax.psum_scatter(holding_buffer, "blk", scatter_dimension=0, tiled=True)[0]
    )
    return (picture_derivative, text_grad)


def solution(mesh):
    placed = (P(("blk", "grp"), None), P(("blk", "grp"), None), P(("blk", "grp")), P(), P())
    return jax.shard_map(
        per_device,
        mesh=mesh,
        in_specs=placed,
        out_specs=(P(("blk", "grp"), None), P(("blk", "grp"), None)),
        check_vma=False,
    )
```

profile of v0, /device:TPU:0, one launch (start us, length us, event | category | flops | bytes accessed | tf_op | source)
XLA Modules:
  0.0 156.4 jit_solution(13518862472954573141)
XLA Ops:
  7.2 0.0 all-gather.3.cloned.1.call-start
  7.2 0.7 all-gather.3.cloned.1.call-update
  7.9 0.0 reduce-scatter.7.cloned.1.call-start
  7.9 3.0 %collective-permute-start = (bf16[128,1152]{1,0:T(8,128)(2,1)}, bf16[128,1152]{1,0:T(8,128)(2,1)S(1)}, u32[]{:S(2)}, u32[]{:S(2)}) collective-permute-start(bf16[128,1152]{1,0:T(8,128)(2,1)} %param.6), channel_id=1, source_target_pairs={{24,0},{0,8},{8,16},{16,24},{25,1},{1,9},{9,17},{17,25},{26,2},{2,... | collective-permute-start | bytes 884744 | tf_op jit(solution)/shard_map/ppermute | solution.py:10
  12.2 12.1 %all-gather = s32[8,1,128]{2,1,0:T(1,128)S(1)} all-gather(s32[1,1,128]{2,1,0:T(1,128)} %bitcast.61), channel_id=1, replica_groups=mesh['blk'=4,'grp'=8] {'grp'}, dimensions={0}, use_global_device_ids=true | all-gather | bytes 4608 | tf_op jit(solution)/shard_map/all_gather | solution.py:55
  24.4 0.0 collective-permute-done
  24.4 0.0 copy-start.2
  24.4 1.5 collective-permute-start.1
  25.9 8.6 %collective-permute-done.1 = bf16[128,1152]{1,0:T(8,128)(2,1)S(1)} collective-permute-done((bf16[128,1152]{1,0:T(8,128)(2,1)S(1)}, bf16[128,1152]{1,0:T(8,128)(2,1)S(1)}, u32[]{:S(2)}, u32[]{:S(2)}) %collective-permute-start.1) | collective-permute-done | bytes 294944 | tf_op jit(solution)/shard_map/ppermute | solution.py:10
  34.5 0.0 copy-start.4
  34.5 0.6 collective-permute-start.2
  35.1 8.9 %all-gather.3.cloned.1.call-done = bf16[1024,1152]{1,0:T(8,128)(2,1)} async-done(((bf16[128,1152]{1,0:T(8,128)(2,1)}), bf16[1024,1152]{1,0:T(8,128)(2,1)}) %all-gather.3.cloned.1.call-update) | async-done | bytes 2359312 | tf_op jit(solution)/shard_map/all_gather | solution.py:54
  44.0 0.0 copy-start
  44.0 2.6 %fusion.28 = bf16[1024,128]{1,0:T(8,128)(2,1)S(1)} fusion(bf16[1024,1152]{1,0:T(8,128)(2,1)} %all-gather.3.cloned.1.call-done, bf16[128,1152]{1,0:T(8,128)(2,1)} %param.6, s32[128]{0:T(128)S(1)} %iota_add_fusion.3, f32[]{:T(128)} %bitcast.53, f32[]{:T(128)} %bitcast.48, s32[1024]{0:T(1024)S(1)} %bitcast.57), kind=kOutput, calls=%fused_computation.39 | convolution fusion | flops 303169536 | bytes 2920968 | tf_op jit(solution)/shard_map/dot_general | solution.py:21
  46.7 0.0 copy-done.2
  46.7 0.0 copy-done
  46.7 0.8 fusion.29
  47.5 0.0 copy-done.4
  47.5 0.8 fusion.30
  48.4 0.2 broadcast_in_dim.24
  48.5 0.5 fusion.3
  49.1 0.6 fusion.2
  49.6 0.5 fusion.1
  50.2 0.0 collective-permute-done.2
  50.2 1.8 %fusion.31 = bf16[1024,128]{1,0:T(8,128)(2,1)S(1)} fusion(bf16[1024,1152]{1,0:T(8,128)(2,1)S(1)} %copy-done, bf16[128,1152]{1,0:T(8,128)(2,1)} %collective-permute-done.2, s32[128]{0:T(128)S(1)} %iota_add_fusion, f32[]{:T(128)} %bitcast.54, f32[]{:T(128)} %bitcast.50, s32[1024]{0:T(1024)S(1)} %bitcast.60), kind=kOutput, calls=%fused_computation.42 | convolution fusion | flops 303169536 | bytes 2920968 | tf_op jit(solution)/shard_map/dot_general | solution.py:21
  52.0 0.5 fusion
  52.6 0.0 copy-start.1
  52.6 1.4 copy-done.1
  54.0 0.0 reduce-scatter.7.cloned.1.call-update
  54.0 0.0 copy-start.3
  54.0 0.0 reduce-scatter.5.cloned.1.call-start
  54.1 1.8 %fusion.32 = f32[1024,1152]{1,0:T(8,128)S(1)} fusion(bf16[1024,128]{1,0:T(8,128)(2,1)S(1)} %fusion.28, bf16[128,1152]{1,0:T(8,128)(2,1)} %param.6), kind=kOutput, calls=%fused_computation.49 | convolution fusion | flops 301989888 | bytes 5275648 | tf_op jit(solution)/shard_map/dot_general | solution.py:31
  55.8 0.0 copy-done.3
  55.8 0.0 copy-start.5
  55.9 0.8 convolution_add_fusion.2
  56.6 0.2 copy-done.5
  56.8 0.8 convolution_add_fusion.1
  57.6 3.9 %convolution_add_fusion = f32[1024,1152]{1,0:T(8,128)} fusion(f32[1024,1152]{1,0:T(8,128)S(1)} %convolution_add_fusion.1, bf16[1024,128]{1,0:T(8,128)(2,1)S(1)} %fusion.31, bf16[128,1152]{1,0:T(8,128)(2,1)} %collective-permute-done.2), kind=kOutput, calls=%fused_computation | convolution fusion | flops 303169536 | bytes 9994240 | tf_op jit(solution)/shard_map/dot_general | solution.py:31
  61.5 0.0 reduce-scatter.5.cloned.1.call-update
  61.5 29.2 %reduce-scatter.7.cloned.1.call-done = f32[1,128,1152]{2,1,0:T(8,128)} async-done(((f32[4,128,1152]{2,1,0:T(8,128)}), f32[1,128,1152]{2,1,0:T(8,128)}) %reduce-scatter.7.cloned.1.call-update) | async-done | bytes 589840
  90.7 1.9 %multiply_bitcast_fusion = f32[128,1152]{1,0:T(8,128)} fusion(f32[1,128,1152]{2,1,0:T(8,128)} %reduce-scatter.7.cloned.1.call-done, f32[]{:T(128)} %bitcast.49), kind=kLoop, calls=%fused_computation.43 | loop fusion | flops 147456 | bytes 1179652 | tf_op jit(solution)/shard_map/mul | solution.py:79
  92.6 55.4 %reduce-scatter.5.cloned.1.call-done = f32[128,1152]{1,0:T(8,128)} async-done(((f32[1024,1152]{1,0:T(8,128)}), f32[128,1152]{1,0:T(8,128)}) %reduce-scatter.5.cloned.1.call-update) | async-done | bytes 589840 | tf_op jit(solution)/shard_map/reduce_scatter | solution.py:75
  148.0 1.9 %broadcast_multiply_fusion = f32[128,1152]{1,0:T(8,128)} fusion(f32[128,1152]{1,0:T(8,128)} %reduce-scatter.5.cloned.1.call-done, f32[]{:T(128)} %bitcast.47), kind=kLoop, calls=%fused_computation.44 | loop fusion | flops 147456 | bytes 1179652 | tf_op jit(solution)/shard_map/mul | solution.py:75
  (4 shorter events, 0.0 us)
Async XLA Ops:
  7.2 36.8 %all-gather.3.cloned.1.call-start = ((), (), s32[]{:S(2)}) async-start(), calls=%async_computation.2 | async-start | bytes 2654208 | tf_op jit(solution)/shard_map/all_gather | solution.py:54
  7.9 82.8 %reduce-scatter.7.cloned.1.call-start = ((), (), s32[]{:S(2)}) async-start(), calls=%async_computation.4 | async-start | bytes 2949120
  7.9 16.4 %collective-permute-start = (bf16[128,1152]{1,0:T(8,128)(2,1)}, bf16[128,1152]{1,0:T(8,128)(2,1)S(1)}, u32[]{:S(2)}, u32[]{:S(2)}) collective-permute-start(bf16[128,1152]{1,0:T(8,128)(2,1)} %param.6), channel_id=1, source_target_pairs={{24,0},{0,8},{8,16},{16,24},{25,1},{1,9},{9,17},{17,25},{26,2},{2,... | collective-permute-start | bytes 884744 | tf_op jit(solution)/shard_map/ppermute | solution.py:10
  24.4 22.3 %copy-start.2 = (bf16[128,1152]{1,0:T(8,128)(2,1)}, bf16[128,1152]{1,0:T(8,128)(2,1)S(1)}, u32[]{:S(2)}) copy-start(bf16[128,1152]{1,0:T(8,128)(2,1)S(1)} %collective-permute-done) | copy-start | bytes 884740
  24.4 10.2 %collective-permute-start.1 = (bf16[128,1152]{1,0:T(8,128)(2,1)S(1)}, bf16[128,1152]{1,0:T(8,128)(2,1)S(1)}, u32[]{:S(2)}, u32[]{:S(2)}) collective-permute-start(bf16[128,1152]{1,0:T(8,128)(2,1)S(1)} %collective-permute-done), channel_id=1, source_target_pairs={{24,0},{0,8},{8,16},{16,24},{25,1},{1,9},{9,17},{17,25},{26,2},{2,... | collective-permute-start | bytes 884744 | tf_op jit(solution)/shard_map/ppermute | solution.py:10
  34.5 13.0 %copy-start.4 = (bf16[128,1152]{1,0:T(8,128)(2,1)}, bf16[128,1152]{1,0:T(8,128)(2,1)S(1)}, u32[]{:S(2)}) copy-start(bf16[128,1152]{1,0:T(8,128)(2,1)S(1)} %collective-permute-done.1) | copy-start | bytes 884740
  34.5 15.7 %collective-permute-start.2 = (bf16[128,1152]{1,0:T(8,128)(2,1)S(1)}, bf16[128,1152]{1,0:T(8,128)(2,1)}, u32[]{:S(2)}, u32[]{:S(2)}) collective-permute-start(bf16[128,1152]{1,0:T(8,128)(2,1)S(1)} %collective-permute-done.1), channel_id=1, source_target_pairs={{24,0},{0,8},{8,16},{16,24},{25,1},{1,9},{9,17},{17,25},{26,2},{2,... | collective-permute-start | bytes 884744 | tf_op jit(solution)/shard_map/ppermute | solution.py:10
  44.0 2.7 %copy-start = (bf16[1024,1152]{1,0:T(8,128)(2,1)S(1)}, bf16[1024,1152]{1,0:T(8,128)(2,1)}, u32[]{:S(2)}) copy-start(bf16[1024,1152]{1,0:T(8,128)(2,1)} %all-gather.3.cloned.1.call-done) | copy-start | bytes 7077892
  52.6 1.4 copy-start.1
  54.0 1.8 %copy-start.3 = (bf16[128,1152]{1,0:T(8,128)(2,1)S(1)}, bf16[128,1152]{1,0:T(8,128)(2,1)}, u32[]{:S(2)}) copy-start(bf16[128,1152]{1,0:T(8,128)(2,1)} %copy-done.2) | copy-start | bytes 884740
  54.0 94.0 %reduce-scatter.5.cloned.1.call-start = ((), (), s32[]{:S(2)}) async-start(), calls=%async_computation.3 | async-start | bytes 5308416 | tf_op jit(solution)/shard_map/reduce_scatter | solution.py:75
  55.8 1.0 copy-start.5
Sparse Core Ops, SparseCore 0:
  9.6 34.3 all-gather.2
  54.1 36.5 reduce-scatter.6
  93.0 54.9 reduce-scatter.4
where the time goes:
time: 157 us; the launch traced here: 156 us
  waiting for transfers between devices  103 us (66%)
  matrix products  15.5 us (10%)
  between operations  15.2 us (10%)
  blocking collectives  12.1 us (8%)
  starting transfers between devices  5.24 us (3%)
  other arithmetic  3.85 us (2%)
  local copies, waits for them, and re-layouts  1.78 us (1%)
    reduce_scatter x1, waiting for transfers between devices, per_device(): lax.psum_scatter(image_total, 'grp', scatter_dimension=0, tiled=True)  55.4 us
    unnamed x4, waiting for transfers between devices  29.9 us
    all_gather x1, blocking collectives, per_device(): lax.all_gather(matching_caption, 'grp', axis=0, tiled=True)  12.1 us
    all_gather x1, waiting for transfers between devices, per_device(): lax.all_gather(picture_vectors, 'grp', axis=0, tiled=True)  8.87 us
    ppermute x3, waiting for transfers between devices, passed_along(): return lax.ppermute(block, axis, route)  8.62 us
    dot_general x4, matrix products, rotation_step(): jnp.dot(pair_coefficients, guest_captions, preferred_element_type=jnp.flo...  7.18 us
    dot_general x4, matrix products, rotation_step(): lax.dot_general(cohort_pictures, guest_captions, (((1,), (1,)), ((), ()))...  6.12 us
    ppermute x3, starting transfers between devices, passed_along(): return lax.ppermute(block, axis, route)  5.13 us
  transfers between devices with their start and end apart: 6, of which 4 were waited for; matrix products, arithmetic and copies ran while one was open for 10% of the time, Pallas kernels for 0%

commit v1 on v0

v1 whole, which is shorter than its diff:
```python
import math

import jax
import jax.numpy as jnp
from jax import lax
from jax.experimental import pallas as pl
from jax.experimental.pallas import tpu as pltpu
from jax.sharding import PartitionSpec as P

LOG2E = 1.4426950408889634
CODE_TOP = 32000.0
CODE_STEPS = 32.0
CODE_ROWS = 16
TILE = 256


def scale_code(top):
    return jnp.ceil(jnp.log(jnp.maximum(top, 1e-30)) * (CODE_STEPS * LOG2E))


def encoded(value):
    code = scale_code(jnp.max(jnp.abs(value), axis=0, keepdims=True))
    gain = CODE_TOP * jnp.exp(code * (-1.0 / (CODE_STEPS * LOG2E)))
    whole = jnp.round(value * gain).astype(jnp.int32).astype(jnp.int16)
    scales = jnp.broadcast_to(code.astype(jnp.int32), (CODE_ROWS, value.shape[1]))
    return whole, scales.astype(jnp.int16)


def decoded(ref, rows, columns):
    code = ref[pl.ds(rows, CODE_ROWS), columns].astype(jnp.int32).astype(jnp.float32)[:1]
    gain = jnp.exp(code * (1.0 / (CODE_STEPS * LOG2E))) * (1.0 / CODE_TOP)
    return ref[pl.ds(0, rows), columns].astype(jnp.int32).astype(jnp.float32) * gain


def gradient_kernel(row_count, column_count, kept, *refs):
    scalars, row_keys, column_keys = refs[:3]
    x_parts = refs[3 : 3 + row_count]
    y_parts = refs[3 + row_count : 3 + row_count + column_count]
    outs = refs[3 + row_count + column_count : 3 + 2 * row_count + column_count]
    x_all, y_all, weights, x_sems, y_sems = refs[3 + 2 * row_count + column_count :]
    size, width = x_parts[0].shape
    x_copies = [
        pltpu.make_async_copy(p, x_all.at[pl.ds(i * size, size)], x_sems.at[i])
        for i, p in enumerate(x_parts)
    ]
    y_copies = [
        pltpu.make_async_copy(p, y_all.at[pl.ds(i * size, size)], y_sems.at[i])
        for i, p in enumerate(y_parts)
    ]
    for c in x_copies + y_copies:
        c.start()
    slope = scalars[0] * LOG2E
    shift = scalars[1] * LOG2E
    for c in x_copies:
        c.wait()
    per_tile = TILE // size
    keys = [
        jnp.tile(jnp.broadcast_to(row_keys[i : i + 1, :], (size, size)).T, (1, per_tile))
        for i in range(row_count)
    ]
    for n in range(column_count // per_tile):
        for c in y_copies[n * per_tile : (n + 1) * per_tile]:
            c.wait()
        other = jnp.concatenate(
            [column_keys[n * per_tile + k : n * per_tile + k + 1, :] for k in range(per_tile)], axis=1
        )
        scores = lax.dot_general(
            x_all[...],
            y_all[pl.ds(n * TILE, TILE), :],
            (((1,), (1,)), ((), ())),
            preferred_element_type=jnp.float32,
        )
        for i in range(row_count):
            z = scores[i * size : (i + 1) * size] * slope + shift
            sig = 1.0 / (1.0 + jnp.exp2(-z))
            w = jnp.where(keys[i] == other, sig - 1.0, sig)
            weights[pl.ds(i * size, size), pl.ds(n * TILE, TILE)] = w.astype(jnp.bfloat16)
    start = 0
    while start < width:
        span = min(TILE, width - start)
        columns = pl.ds(start, span)
        sums = jnp.dot(weights[...], y_all[:, columns], preferred_element_type=jnp.float32)
        for i in range(row_count):
            block = sums[i * size : (i + 1) * size]
            if i < kept:
                outs[i][:, columns] = block
            else:
                whole, scales = encoded(block)
                outs[i][pl.ds(0, size), columns] = whole
                outs[i][pl.ds(size, CODE_ROWS), columns] = scales
        start += span


def gradient_parts(scalars, row_keys, column_keys, x_parts, y_parts, kept):
    size, width = x_parts[0].shape
    rows, columns = len(x_parts), len(y_parts)
    whole = jax.ShapeDtypeStruct((size, width), jnp.float32)
    coded = jax.ShapeDtypeStruct((size + CODE_ROWS, width), jnp.int16)
    smem = pl.BlockSpec(memory_space=pltpu.SMEM)
    vmem = pl.BlockSpec(memory_space=pltpu.VMEM)
    anywhere = pl.BlockSpec(memory_space=pl.ANY)
    return pl.pallas_call(
        lambda *refs: gradient_kernel(rows, columns, kept, *refs),
        out_shape=[whole if i < kept else coded for i in range(rows)],
        in_specs=[smem, vmem, vmem] + [anywhere] * (rows + columns),
        out_specs=[vmem] * rows,
        scratch_shapes=[
            pltpu.VMEM((rows * size, width), jnp.bfloat16),
            pltpu.VMEM((columns * size, width), jnp.bfloat16),
            pltpu.VMEM((rows * size, columns * size), jnp.bfloat16),
            pltpu.SemaphoreType.DMA((rows,)),
            pltpu.SemaphoreType.DMA((columns,)),
        ],
        compiler_params=pltpu.CompilerParams(vmem_limit_bytes=48 * 2**20),
        cost_estimate=pl.CostEstimate(
            flops=4 * rows * columns * size * size * width,
            bytes_accessed=(rows + columns) * size * width * 2 + rows * size * width * 4,
            transcendentals=rows * columns * size * size,
        ),
        name="gradient_parts",
    )(scalars, row_keys, column_keys, *x_parts, *y_parts)


def combined(scalars, kept, received, final):
    size, width = kept.shape

    def kernel(scalars, kept, *refs):
        out = refs[-1]
        for start in range(0, width, 128):
            columns = pl.ds(start, 128)
            total = kept[:, columns]
            for r in refs[:-1]:
                total = total + decoded(r, size, columns)
            if final:
                out[:, columns] = total * scalars[0]
            else:
                whole, scales = encoded(total)
                out[pl.ds(0, size), columns] = whole
                out[pl.ds(size, CODE_ROWS), columns] = scales

    smem = pl.BlockSpec(memory_space=pltpu.SMEM)
    vmem = pl.BlockSpec(memory_space=pltpu.VMEM)
    shape = (size, width) if final else (size + CODE_ROWS, width)
    return pl.pallas_call(
        kernel,
        out_shape=jax.ShapeDtypeStruct(shape, jnp.float32 if final else jnp.int16),
        in_specs=[smem] + [vmem] * (1 + len(received)),
        out_specs=vmem,
        cost_estimate=pl.CostEstimate(
            flops=8 * size * width, bytes_accessed=12 * size * width, transcendentals=0
        ),
        name="output_sum" if final else "passed_sum",
    )(scalars, kept, *received)


def swapped(block, step):
    axis, bit = step
    return lax.ppermute(block, axis, [(i, i ^ bit) for i in range(lax.axis_size(axis))])


def gathered(block, steps):
    blocks = [block]
    for step in steps:
        blocks = blocks + [swapped(b, step) for b in blocks]
    return blocks


def scattered_sum(scalars, parts, steps):
    received = [[] for _ in parts]
    for s in reversed(range(len(steps))):
        half = 1 << s
        for m in reversed(range(half)):
            top = parts[half + m]
            if s + 1 < len(steps):
                top = combined(scalars, top, received[half + m], False)
            received[m].append(swapped(top, steps[s]))
    return combined(scalars, parts[0], received[0], True)


def bit_steps(axis):
    return [(axis, 1 << k) for k in range(int(math.log2(lax.axis_size(axis))))]


def owner_keys(steps, size):
    owners = [(lax.axis_index("blk"), lax.axis_index("grp"))]
    for axis, bit in steps:
        owners = owners + [(b ^ bit, g) if axis == "blk" else (b, g ^ bit) for b, g in owners]
    grp_count = lax.axis_size("grp")
    firsts = jnp.stack([(b * grp_count + g) * size for b, g in owners])
    return firsts[:, None] + jnp.arange(size, dtype=jnp.int32)[None, :]


def per_device(
    picture_vectors, caption_vectors, matching_caption, sharpness_parameter, additive_intercept
):
    size = picture_vectors.shape[0]
    scalars = jnp.concatenate([sharpness_parameter, additive_intercept])
    core, *grp_steps = bit_steps("grp")
    blk_steps = bit_steps("blk")
    every = grp_steps + blk_steps
    image_steps, text_steps = every[0::2], every[1::2]

    images = gathered(picture_vectors, image_steps)
    texts = gathered(caption_vectors, text_steps)
    labels = matching_caption[None, :]
    for step in image_steps + [core]:
        labels = jnp.concatenate([labels, swapped(labels, step)])
    all_images = images + [swapped(b, core) for b in images]
    all_texts = texts + [swapped(b, core) for b in texts]
    ids = owner_keys(text_steps + [core], size)

    image_parts = gradient_parts(
        scalars, labels[: len(images)], ids, images, all_texts, len(images) // 2
    )
    text_parts = gradient_parts(
        scalars, ids[: len(texts)], labels, texts, all_images, len(texts) // 2
    )
    picture_derivative = scattered_sum(scalars, image_parts, image_steps)
    text_grad = scattered_sum(scalars, text_parts, text_steps)
    return (picture_derivative, text_grad)


def solution(mesh):
    placed = (P(("blk", "grp"), None), P(("blk", "grp"), None), P(("blk", "grp")), P(), P())
    return jax.shard_map(
        per_device,
        mesh=mesh,
        in_specs=placed,
        out_specs=(P(("blk", "grp"), None), P(("blk", "grp"), None)),
        check_vma=False,
    )
```

time: 157 us -> 88.7 us (0.56)
  waiting for transfers between devices: 103 us -> 37.9 us
  Pallas kernels: 0 us -> 20.9 us
  matrix products: 15.5 us -> 0 us
  starting transfers between devices: 5.24 us -> 19.1 us
  between operations: 15.2 us -> 2.07 us
  blocking collectives: 12.1 us -> 0 us
  local copies, waits for them, and re-layouts: 1.78 us -> 8.21 us
  other arithmetic: 3.85 us -> 0.17 us
    reduce_scatter x1 -> x0, waiting for transfers between devices: 55.4 us -> none  [per_device(): lax.psum_scatter(image_total, 'grp', scatter_dimension=0, tiled=True)]
    unnamed x4 -> x0, waiting for transfers between devices: 29.9 us -> none
    ppermute x3 -> x23, waiting for transfers between devices: 8.62 us -> 37.9 us  [swapped(): lax.ppermute(block, axis, [(i, i ^ bit) for i in range(lax.axis_size(axis...]
    pallas_call x0 -> x6, Pallas kernels: none -> 20.9 us  [the longest x2 12.2 us: gradient_parts(): pl.pallas_call(lambda *refs: gradient_kernel(rows, columns, kept, *refs),...]
    dot_general x12 -> x0, matrix products: 15.5 us -> none  [the longest x4 7.18 us: rotation_step(): jnp.dot(pair_coefficients, guest_captions, preferred_element_type=jnp.flo...]
    ppermute x3 -> x23, starting transfers between devices: 5.13 us -> 19.1 us  [swapped(): lax.ppermute(block, axis, [(i, i ^ bit) for i in range(lax.axis_size(axis...]
    all_gather x1 -> x0, blocking collectives: 12.1 us -> none  [per_device(): lax.all_gather(matching_caption, 'grp', axis=0, tiled=True)]
    all_gather x1 -> x0, waiting for transfers between devices: 8.87 us -> none  [per_device(): lax.all_gather(picture_vectors, 'grp', axis=0, tiled=True)]
  transfers between devices with their start and end apart: 6 -> 23, of which waited for: 4 -> 8; matrix products, arithmetic and copies ran while one was open for 10% -> 0% of each run, Pallas kernels for 0% -> 21%
where the time goes in v1:
time: 88.7 us; the launch traced here: 88.4 us
  waiting for transfers between devices  37.9 us (43%)
  Pallas kernels  20.9 us (24%)
  starting transfers between devices  19.1 us (22%)
  local copies, waits for them, and re-layouts  8.21 us (9%)
  between operations  2.07 us (2%)
    ppermute x23, waiting for transfers between devices, swapped(): lax.ppermute(block, axis, [(i, i ^ bit) for i in range(lax.axis_size(axis...  37.9 us
    ppermute x23, starting transfers between devices, swapped(): lax.ppermute(block, axis, [(i, i ^ bit) for i in range(lax.axis_size(axis...  19.1 us
    pallas_call x2, Pallas kernels, gradient_parts(): pl.pallas_call(lambda *refs: gradient_kernel(rows, columns, kept, *refs),...  12.2 us
    pallas_call x4, Pallas kernels, combined(): pl.pallas_call(kernel, out_shape=jax.ShapeDtypeStruct(shape, jnp.float32...  8.72 us
    unnamed x30, local copies, waits for them, and re-layouts  8.12 us
  transfers between devices with their start and end apart: 23, of which 8 were waited for; matrix products, arithmetic and copies ran while one was open for 0% of the time, Pallas kernels for 21%

profile of v1, /device:TPU:0, one launch (start us, length us, event | category | flops | bytes accessed | tf_op | source)
XLA Modules:
  0.0 88.4 jit_solution(10522904911644534125)
XLA Ops:
  0.6 3.1 %collective-permute-start.2 = (bf16[128,1152]{1,0:T(8,128)(2,1)}, bf16[128,1152]{1,0:T(8,128)(2,1)S(1)}, u32[]{:S(2)}, u32[]{:S(2)}) collective-permute-start(bf16[128,1152]{1,0:T(8,128)(2,1)} %refs_7_.3), channel_id=1, source_target_pairs={{0,2},{1,3},{2,0},{3,1},{4,6},{5,7},{6,4},{7,5},{8,10},{9,11},{10,... | collective-permute-start | bytes 884744 | tf_op jit(solution)/shard_map/ppermute | solution.py:158
  3.7 2.6 %collective-permute-start.5 = (bf16[128,1152]{1,0:T(8,128)(2,1)}, bf16[128,1152]{1,0:T(8,128)(2,1)S(1)}, u32[]{:S(2)}, u32[]{:S(2)}) collective-permute-start(bf16[128,1152]{1,0:T(8,128)(2,1)} %refs_3_.3), channel_id=1, source_target_pairs={{0,4},{1,5},{2,6},{3,7},{4,0},{5,1},{6,2},{7,3},{8,12},{9,13},{10,... | collective-permute-start | bytes 884744 | tf_op jit(solution)/shard_map/ppermute | solution.py:158
  6.3 1.5 %collective-permute-start.3 = (bf16[128,1152]{1,0:T(8,128)(2,1)}, bf16[128,1152]{1,0:T(8,128)(2,1)S(1)}, u32[]{:S(2)}, u32[]{:S(2)}) collective-permute-start(bf16[128,1152]{1,0:T(8,128)(2,1)} %refs_7_.3), channel_id=1, source_target_pairs={{0,8},{8,0},{16,24},{24,16},{1,9},{9,1},{17,25},{25,17},{2,10},{10... | collective-permute-start | bytes 884744 | tf_op jit(solution)/shard_map/ppermute | solution.py:158
  7.8 1.5 %collective-permute-start.6 = (bf16[128,1152]{1,0:T(8,128)(2,1)}, bf16[128,1152]{1,0:T(8,128)(2,1)S(1)}, u32[]{:S(2)}, u32[]{:S(2)}) collective-permute-start(bf16[128,1152]{1,0:T(8,128)(2,1)} %refs_3_.3), channel_id=1, source_target_pairs={{0,16},{8,24},{16,0},{24,8},{1,17},{9,25},{17,1},{25,9},{2,18},{10... | collective-permute-start | bytes 884744 | tf_op jit(solution)/shard_map/ppermute | solution.py:158
  9.3 7.8 %collective-permute-done.2.refs_4_.refs_8_ = bf16[128,1152]{1,0:T(8,128)(2,1)S(1)} collective-permute-done((bf16[128,1152]{1,0:T(8,128)(2,1)}, bf16[128,1152]{1,0:T(8,128)(2,1)S(1)}, u32[]{:S(2)}, u32[]{:S(2)}) %collective-permute-start.2) | collective-permute-done | bytes 294944 | tf_op jit(solution)/shard_map/ppermute | solution.py:158
  17.2 1.7 %collective-permute-start.4 = (bf16[128,1152]{1,0:T(8,128)(2,1)S(1)}, bf16[128,1152]{1,0:T(8,128)(2,1)S(1)}, u32[]{:S(2)}, u32[]{:S(2)}) collective-permute-start(bf16[128,1152]{1,0:T(8,128)(2,1)S(1)} %collective-permute-done.2.refs_4_.refs_8_), channel_id=1, source_target_pairs={{0,8},{8,0},{16,24},{24,16},{1,9},{9,1},{17,25},{25,17},{2,10},{10... | collective-permute-start | bytes 884744 | tf_op jit(solution)/shard_map/ppermute | solution.py:158
  18.8 0.0 collective-permute-start
  18.8 3.5 %collective-permute-done = s32[1,128]{1,0:T(1,128)S(1)} collective-permute-done((s32[1,128]{1,0:T(1,128)S(1)}, s32[1,128]{1,0:T(1,128)S(1)}, u32[]{:S(2)}, u32[]{:S(2)}) %collective-permute-start) | collective-permute-done | bytes 544 | tf_op jit(solution)/shard_map/ppermute | solution.py:158
  22.4 0.4 collective-permute-start.1
  22.7 3.2 %collective-permute-done.1 = s32[2,128]{1,0:T(2,128)S(1)} collective-permute-done((s32[2,128]{1,0:T(2,128)S(1)}, s32[2,128]{1,0:T(2,128)S(1)}, u32[]{:S(2)}, u32[]{:S(2)}) %collective-permute-start.1) | collective-permute-done | bytes 1056 | tf_op jit(solution)/shard_map/ppermute | solution.py:158
  25.9 0.1 collective-permute-start.15
  26.0 0.1 stack.35
  26.1 1.0 %collective-permute-done.15 = s32[4,128]{1,0:T(4,128)S(1)} collective-permute-done((s32[4,128]{1,0:T(4,128)S(1)}, s32[4,128]{1,0:T(4,128)S(1)}, u32[]{:S(2)}, u32[]{:S(2)}) %collective-permute-start.15) | collective-permute-done | bytes 2080 | tf_op jit(solution)/shard_map/ppermute | solution.py:158
  27.2 0.2 collective-permute-start.16
  27.3 0.0 collective-permute-done.5.refs_8_.refs_4_
  27.3 0.3 collective-permute-start.17
  27.7 0.0 collective-permute-done.3.refs_5_.refs_9_
  27.7 1.5 %collective-permute-start.7 = (bf16[128,1152]{1,0:T(8,128)(2,1)S(1)}, bf16[128,1152]{1,0:T(8,128)(2,1)S(1)}, u32[]{:S(2)}, u32[]{:S(2)}) collective-permute-start(bf16[128,1152]{1,0:T(8,128)(2,1)S(1)} %collective-permute-done.5.refs_8_.refs_4_), channel_id=1, source_target_pairs={{0,16},{8,24},{16,0},{24,8},{1,17},{9,25},{17,1},{25,9},{2,18},{10... | collective-permute-start | bytes 884744 | tf_op jit(solution)/shard_map/ppermute | solution.py:158
  29.2 0.0 collective-permute-done.6.refs_9_.refs_5_
  29.2 0.0 collective-permute-start.18
  29.2 0.0 collective-permute-done.4.refs_6_.refs_10_
  29.2 0.5 collective-permute-start.19
  29.7 0.1 iota_add_fusion.refs_2_
  31.1 0.1 pad_maximum_fusion.refs_0_.scalars
  31.2 0.0 collective-permute-done.16.refs_11_
  31.2 0.1 collective-permute-start.8
  31.3 5.5 %collective-permute-done.7.refs_10_.refs_6_ = bf16[128,1152]{1,0:T(8,128)(2,1)S(1)} collective-permute-done((bf16[128,1152]{1,0:T(8,128)(2,1)S(1)}, bf16[128,1152]{1,0:T(8,128)(2,1)S(1)}, u32[]{:S(2)}, u32[]{:S(2)}) %collective-permute-start.7) | collective-permute-done | bytes 294944 | tf_op jit(solution)/shard_map/ppermute | solution.py:158
  36.8 0.0 collective-permute-start.9
  36.8 0.0 collective-permute-done.17.refs_12_
  36.8 0.5 collective-permute-start.10
  37.3 0.0 collective-permute-done.18.refs_13_
  37.3 0.1 collective-permute-start.11
  37.4 0.0 collective-permute-done.19.refs_14_
  37.4 0.0 copy-start.5
  37.4 1.0 %copy-done.5 = bf16[128,1152]{1,0:T(8,128)(2,1)S(1)} copy-done((bf16[128,1152]{1,0:T(8,128)(2,1)S(1)}, bf16[128,1152]{1,0:T(8,128)(2,1)}, u32[]{:S(2)}) %copy-start.5) | copy-done | bytes 294936
  38.3 1.0 %copy-done.6 = bf16[128,1152]{1,0:T(8,128)(2,1)S(1)} copy-done((bf16[128,1152]{1,0:T(8,128)(2,1)S(1)}, bf16[128,1152]{1,0:T(8,128)(2,1)}, u32[]{:S(2)}) %copy-start.6) | copy-done | bytes 294936
  39.3 6.1 %gradient_parts.3 = (f32[128,1152]{1,0:T(8,128)S(1)}, f32[128,1152]{1,0:T(8,128)S(1)}, s16[144,1152]{1,0:T(8,128)(2,1)S(1)}, s16[144,1152]{1,0:T(8,128)(2,1)S(1)}) custom-call(f32[2]{0:T(128)S(1)} %pad_maximum_fusion.refs_0_.scalars, s32[4,128]{1,0:T(4,128)S(1)} %slice.3.refs_1_, s32[8,128]{1,0:T(8,128)S(1)} %pad_add_fusion.refs_2_, ...), custom_call_target="tpu_custom_call" | custom-call | flops 2415919104 | bytes 5898240 | tf_op jit(solution)/shard_map/gradient_parts/pallas_call | solution.py:102
  45.4 0.8 copy-done
  46.3 0.8 copy-done.2
  47.1 1.5 %collective-permute-start.21 = (s16[144,1152]{1,0:T(8,128)(2,1)S(1)}, s16[144,1152]{1,0:T(8,128)(2,1)S(1)}, u32[]{:S(2)}, u32[]{:S(2)}) collective-permute-start(s16[144,1152]{1,0:T(8,128)(2,1)S(1)} %get-tuple-element.17), channel_id=1, source_target_pairs={{0,16},{8,24},{16,0},{24,8},{1,17},{9,25},{17,1},{25,9},{2,18},{10... | collective-permute-start | bytes 995336 | tf_op jit(solution)/shard_map/ppermute | solution.py:158
  48.6 0.0 collective-permute-done.8.refs_11_
  48.6 0.0 collective-permute-done.9.refs_12_
  48.6 0.0 collective-permute-done.10.refs_13_
  48.6 6.1 %gradient_parts.2 = (f32[128,1152]{1,0:T(8,128)S(1)}, f32[128,1152]{1,0:T(8,128)S(1)}, s16[144,1152]{1,0:T(8,128)(2,1)S(1)}, s16[144,1152]{1,0:T(8,128)(2,1)S(1)}) custom-call(f32[2]{0:T(128)S(1)} %pad_maximum_fusion.refs_0_.scalars, s32[4,128]{1,0:T(4,128)S(1)} %pad_add_fusion.1.refs_1_, s32[8,128]{1,0:T(8,128)S(1)} %iota_add_fusion.refs_2_, ...), custom_call_target="tpu_custom_call" | custom-call | flops 2415919104 | bytes 5898240 | tf_op jit(solution)/shard_map/gradient_parts/pallas_call | solution.py:102
  54.7 0.0 copy-start.1
  54.8 0.8 copy-done.1
  55.6 0.8 copy-done.3
  56.4 0.8 collective-permute-start.13
  57.2 0.5 collective-permute-start.20
  57.7 1.2 %collective-permute-start.12 = (s16[144,1152]{1,0:T(8,128)(2,1)S(1)}, s16[144,1152]{1,0:T(8,128)(2,1)S(1)}, u32[]{:S(2)}, u32[]{:S(2)}) collective-permute-start(s16[144,1152]{1,0:T(8,128)(2,1)S(1)} %get-tuple-element.11), channel_id=1, source_target_pairs={{0,8},{8,0},{16,24},{24,16},{1,9},{9,1},{17,25},{25,17},{2,10},{10... | collective-permute-start | bytes 995336 | tf_op jit(solution)/shard_map/ppermute | solution.py:158
  58.9 0.7 copy-done.8
  59.6 2.1 %passed_sum.3 = s16[144,1152]{1,0:T(8,128)(2,1)} custom-call(f32[2]{0:T(128)} %copy-done.4, f32[128,1152]{1,0:T(8,128)} %copy-done, s16[144,1152]{1,0:T(8,128)(2,1)} %copy-done.8), custom_call_target="tpu_custom_call" | custom-call | flops 1179648 | bytes 1769472 | tf_op jit(solution)/shard_map/passed_sum/pallas_call | solution.py:144
  61.7 1.0 %collective-permute-start.22 = (s16[144,1152]{1,0:T(8,128)(2,1)}, s16[144,1152]{1,0:T(8,128)(2,1)S(1)}, u32[]{:S(2)}, u32[]{:S(2)}) collective-permute-start(s16[144,1152]{1,0:T(8,128)(2,1)} %passed_sum.3), channel_id=1, source_target_pairs={{0,4},{1,5},{2,6},{3,7},{4,0},{5,1},{6,2},{7,3},{8,12},{9,13},{10,... | collective-permute-start | bytes 995336 | tf_op jit(solution)/shard_map/ppermute | solution.py:158
  62.8 4.3 %collective-permute-done.13.refs_0_ = s16[144,1152]{1,0:T(8,128)(2,1)S(1)} collective-permute-done((s16[144,1152]{1,0:T(8,128)(2,1)S(1)}, s16[144,1152]{1,0:T(8,128)(2,1)S(1)}, u32[]{:S(2)}, u32[]{:S(2)}) %collective-permute-start.13) | collective-permute-done | bytes 331808 | tf_op jit(solution)/shard_map/ppermute | solution.py:158
  67.0 0.7 copy-done.12
  67.7 2.1 %passed_sum.2 = s16[144,1152]{1,0:T(8,128)(2,1)} custom-call(f32[2]{0:T(128)} %copy-done.4, f32[128,1152]{1,0:T(8,128)} %copy-done.1, s16[144,1152]{1,0:T(8,128)(2,1)} %copy-done.12), custom_call_target="tpu_custom_call" | custom-call | flops 1179648 | bytes 1769472 | tf_op jit(solution)/shard_map/passed_sum/pallas_call | solution.py:144
  69.8 0.0 collective-permute-done.20.refs_0_
  69.9 9.1 %collective-permute-done.22.refs_1_ = s16[144,1152]{1,0:T(8,128)(2,1)S(1)} collective-permute-done((s16[144,1152]{1,0:T(8,128)(2,1)}, s16[144,1152]{1,0:T(8,128)(2,1)S(1)}, u32[]{:S(2)}, u32[]{:S(2)}) %collective-permute-start.22) | collective-permute-done | bytes 331808 | tf_op jit(solution)/shard_map/ppermute | solution.py:158
  78.9 0.7 copy-done.13
  79.7 2.3 %output_sum.3 = f32[128,1152]{1,0:T(8,128)} custom-call(f32[2]{0:T(128)} %copy-done.4, f32[128,1152]{1,0:T(8,128)} %copy-done.2, s16[144,1152]{1,0:T(8,128)(2,1)} %copy-done.10, s16[144,1152]{1,0:T(8,128)(2,1)} %copy-done.13), custom_call_target="tpu_custom_call" | custom-call | flops 1179648 | bytes 1769472 | tf_op jit(solution)/shard_map/output_sum/pallas_call | solution.py:144
  81.9 0.0 collective-permute-done.12.refs_0_
  81.9 3.4 %collective-permute-done.14.refs_1_ = s16[144,1152]{1,0:T(8,128)(2,1)S(1)} collective-permute-done((s16[144,1152]{1,0:T(8,128)(2,1)}, s16[144,1152]{1,0:T(8,128)(2,1)S(1)}, u32[]{:S(2)}, u32[]{:S(2)}) %collective-permute-start.14) | collective-permute-done | bytes 331808 | tf_op jit(solution)/shard_map/ppermute | solution.py:158
  85.4 0.7 copy-done.11
  86.1 2.3 %output_sum.2 = f32[128,1152]{1,0:T(8,128)} custom-call(f32[2]{0:T(128)} %copy-done.4, f32[128,1152]{1,0:T(8,128)} %copy-done.3, s16[144,1152]{1,0:T(8,128)(2,1)} %copy-done.9, s16[144,1152]{1,0:T(8,128)(2,1)} %copy-done.11), custom_call_target="tpu_custom_call" | custom-call | flops 1179648 | bytes 1769472 | tf_op jit(solution)/shard_map/output_sum/pallas_call | solution.py:144
  (25 shorter events, 0.1 us)
Async XLA Ops:
  0.6 18.2 %copy-start.14 = (s32[128]{0:T(128)S(1)}, s32[128]{0:T(128)}, u32[]{:S(2)}) copy-start(s32[128]{0:T(128)} %param.7) | copy-start | bytes 1540
  0.6 16.5 %collective-permute-start.2 = (bf16[128,1152]{1,0:T(8,128)(2,1)}, bf16[128,1152]{1,0:T(8,128)(2,1)S(1)}, u32[]{:S(2)}, u32[]{:S(2)}) collective-permute-start(bf16[128,1152]{1,0:T(8,128)(2,1)} %refs_7_.3), channel_id=1, source_target_pairs={{0,2},{1,3},{2,0},{3,1},{4,6},{5,7},{6,4},{7,5},{8,10},{9,11},{10,... | collective-permute-start | bytes 884744 | tf_op jit(solution)/shard_map/ppermute | solution.py:158
  3.7 23.6 %collective-permute-start.5 = (bf16[128,1152]{1,0:T(8,128)(2,1)}, bf16[128,1152]{1,0:T(8,128)(2,1)S(1)}, u32[]{:S(2)}, u32[]{:S(2)}) collective-permute-start(bf16[128,1152]{1,0:T(8,128)(2,1)} %refs_3_.3), channel_id=1, source_target_pairs={{0,4},{1,5},{2,6},{3,7},{4,0},{5,1},{6,2},{7,3},{8,12},{9,13},{10,... | collective-permute-start | bytes 884744 | tf_op jit(solution)/shard_map/ppermute | solution.py:158
  6.3 21.4 %collective-permute-start.3 = (bf16[128,1152]{1,0:T(8,128)(2,1)}, bf16[128,1152]{1,0:T(8,128)(2,1)S(1)}, u32[]{:S(2)}, u32[]{:S(2)}) collective-permute-start(bf16[128,1152]{1,0:T(8,128)(2,1)} %refs_7_.3), channel_id=1, source_target_pairs={{0,8},{8,0},{16,24},{24,16},{1,9},{9,1},{17,25},{25,17},{2,10},{10... | collective-permute-start | bytes 884744 | tf_op jit(solution)/shard_map/ppermute | solution.py:158
  7.8 21.4 %collective-permute-start.6 = (bf16[128,1152]{1,0:T(8,128)(2,1)}, bf16[128,1152]{1,0:T(8,128)(2,1)S(1)}, u32[]{:S(2)}, u32[]{:S(2)}) collective-permute-start(bf16[128,1152]{1,0:T(8,128)(2,1)} %refs_3_.3), channel_id=1, source_target_pairs={{0,16},{8,24},{16,0},{24,8},{1,17},{9,25},{17,1},{25,9},{2,18},{10... | collective-permute-start | bytes 884744 | tf_op jit(solution)/shard_map/ppermute | solution.py:158
  17.2 12.0 %collective-permute-start.4 = (bf16[128,1152]{1,0:T(8,128)(2,1)S(1)}, bf16[128,1152]{1,0:T(8,128)(2,1)S(1)}, u32[]{:S(2)}, u32[]{:S(2)}) collective-permute-start(bf16[128,1152]{1,0:T(8,128)(2,1)S(1)} %collective-permute-done.2.refs_4_.refs_8_), channel_id=1, source_target_pairs={{0,8},{8,0},{16,24},{24,16},{1,9},{9,1},{17,25},{25,17},{2,10},{10... | collective-permute-start | bytes 884744 | tf_op jit(solution)/shard_map/ppermute | solution.py:158
  18.8 3.5 %collective-permute-start = (s32[1,128]{1,0:T(1,128)S(1)}, s32[1,128]{1,0:T(1,128)S(1)}, u32[]{:S(2)}, u32[]{:S(2)}) collective-permute-start(s32[1,128]{1,0:T(1,128)S(1)} %bitcast.9), channel_id=1, source_target_pairs={{0,2},{1,3},{2,0},{3,1},{4,6},{5,7},{6,4},{7,5},{8,10},{9,11},{10,... | collective-permute-start | bytes 1544 | tf_op jit(solution)/shard_map/ppermute | solution.py:158
  22.4 3.6 %collective-permute-start.1 = (s32[2,128]{1,0:T(2,128)S(1)}, s32[2,128]{1,0:T(2,128)S(1)}, u32[]{:S(2)}, u32[]{:S(2)}) collective-permute-start(s32[2,128]{1,0:T(2,128)S(1)} %pad_add_fusion.2), channel_id=1, source_target_pairs={{0,8},{8,0},{16,24},{24,16},{1,9},{9,1},{17,25},{25,17},{2,10},{10... | collective-permute-start | bytes 3080 | tf_op jit(solution)/shard_map/ppermute | solution.py:158
  25.9 1.2 %collective-permute-start.15 = (s32[4,128]{1,0:T(4,128)S(1)}, s32[4,128]{1,0:T(4,128)S(1)}, u32[]{:S(2)}, u32[]{:S(2)}) collective-permute-start(s32[4,128]{1,0:T(4,128)S(1)} %pad_add_fusion.1.refs_1_), channel_id=1, source_target_pairs={{0,1},{1,0},{2,3},{3,2},{4,5},{5,4},{6,7},{7,6},{8,9},{9,8},{10,11... | collective-permute-start | bytes 6152 | tf_op jit(solution)/shard_map/ppermute | solution.py:158
  27.2 4.0 %collective-permute-start.16 = (bf16[128,1152]{1,0:T(8,128)(2,1)}, bf16[128,1152]{1,0:T(8,128)(2,1)S(1)}, u32[]{:S(2)}, u32[]{:S(2)}) collective-permute-start(bf16[128,1152]{1,0:T(8,128)(2,1)} %refs_7_.3), channel_id=1, source_target_pairs={{0,1},{1,0},{2,3},{3,2},{4,5},{5,4},{6,7},{7,6},{8,9},{9,8},{10,11... | collective-permute-start | bytes 884744 | tf_op jit(solution)/shard_map/ppermute | solution.py:158
  27.3 9.4 %collective-permute-start.17 = (bf16[128,1152]{1,0:T(8,128)(2,1)S(1)}, bf16[128,1152]{1,0:T(8,128)(2,1)S(1)}, u32[]{:S(2)}, u32[]{:S(2)}) collective-permute-start(bf16[128,1152]{1,0:T(8,128)(2,1)S(1)} %collective-permute-done.2.refs_4_.refs_8_), channel_id=1, source_target_pairs={{0,1},{1,0},{2,3},{3,2},{4,5},{5,4},{6,7},{7,6},{8,9},{9,8},{10,11... | collective-permute-start | bytes 884744 | tf_op jit(solution)/shard_map/ppermute | solution.py:158
  27.7 9.1 %collective-permute-start.7 = (bf16[128,1152]{1,0:T(8,128)(2,1)S(1)}, bf16[128,1152]{1,0:T(8,128)(2,1)S(1)}, u32[]{:S(2)}, u32[]{:S(2)}) collective-permute-start(bf16[128,1152]{1,0:T(8,128)(2,1)S(1)} %collective-permute-done.5.refs_8_.refs_4_), channel_id=1, source_target_pairs={{0,16},{8,24},{16,0},{24,8},{1,17},{9,25},{17,1},{25,9},{2,18},{10... | collective-permute-start | bytes 884744 | tf_op jit(solution)/shard_map/ppermute | solution.py:158
  29.2 8.1 %collective-permute-start.18 = (bf16[128,1152]{1,0:T(8,128)(2,1)S(1)}, bf16[128,1152]{1,0:T(8,128)(2,1)S(1)}, u32[]{:S(2)}, u32[]{:S(2)}) collective-permute-start(bf16[128,1152]{1,0:T(8,128)(2,1)S(1)} %collective-permute-done.3.refs_5_.refs_9_), channel_id=1, source_target_pairs={{0,1},{1,0},{2,3},{3,2},{4,5},{5,4},{6,7},{7,6},{8,9},{9,8},{10,11... | collective-permute-start | bytes 884744 | tf_op jit(solution)/shard_map/ppermute | solution.py:158
  29.2 8.2 %collective-permute-start.19 = (bf16[128,1152]{1,0:T(8,128)(2,1)S(1)}, bf16[128,1152]{1,0:T(8,128)(2,1)S(1)}, u32[]{:S(2)}, u32[]{:S(2)}) collective-permute-start(bf16[128,1152]{1,0:T(8,128)(2,1)S(1)} %collective-permute-done.4.refs_6_.refs_10_), channel_id=1, source_target_pairs={{0,1},{1,0},{2,3},{3,2},{4,5},{5,4},{6,7},{7,6},{8,9},{9,8},{10,11... | collective-permute-start | bytes 884744 | tf_op jit(solution)/shard_map/ppermute | solution.py:158
  31.2 17.4 %copy-start.4 = (f32[2]{0:T(128)}, f32[2]{0:T(128)S(1)}, u32[]{:S(2)}) copy-start(f32[2]{0:T(128)S(1)} %pad_maximum_fusion.refs_0_.scalars) | copy-start | bytes 28
  31.2 17.4 %collective-permute-start.8 = (bf16[128,1152]{1,0:T(8,128)(2,1)}, bf16[128,1152]{1,0:T(8,128)(2,1)S(1)}, u32[]{:S(2)}, u32[]{:S(2)}) collective-permute-start(bf16[128,1152]{1,0:T(8,128)(2,1)} %refs_3_.3), channel_id=1, source_target_pairs={{0,1},{1,0},{2,3},{3,2},{4,5},{5,4},{6,7},{7,6},{8,9},{9,8},{10,11... | collective-permute-start | bytes 884744 | tf_op jit(solution)/shard_map/ppermute | solution.py:158
  36.8 11.8 %collective-permute-start.9 = (bf16[128,1152]{1,0:T(8,128)(2,1)S(1)}, bf16[128,1152]{1,0:T(8,128)(2,1)S(1)}, u32[]{:S(2)}, u32[]{:S(2)}) collective-permute-start(bf16[128,1152]{1,0:T(8,128)(2,1)S(1)} %collective-permute-done.5.refs_8_.refs_4_), channel_id=1, source_target_pairs={{0,1},{1,0},{2,3},{3,2},{4,5},{5,4},{6,7},{7,6},{8,9},{9,8},{10,11... | collective-permute-start | bytes 884744 | tf_op jit(solution)/shard_map/ppermute | solution.py:158
  36.8 11.8 %collective-permute-start.10 = (bf16[128,1152]{1,0:T(8,128)(2,1)S(1)}, bf16[128,1152]{1,0:T(8,128)(2,1)S(1)}, u32[]{:S(2)}, u32[]{:S(2)}) collective-permute-start(bf16[128,1152]{1,0:T(8,128)(2,1)S(1)} %collective-permute-done.6.refs_9_.refs_5_), channel_id=1, source_target_pairs={{0,1},{1,0},{2,3},{3,2},{4,5},{5,4},{6,7},{7,6},{8,9},{9,8},{10,11... | collective-permute-start | bytes 884744 | tf_op jit(solution)/shard_map/ppermute | solution.py:158
  37.3 11.3 %collective-permute-start.11 = (bf16[128,1152]{1,0:T(8,128)(2,1)S(1)}, bf16[128,1152]{1,0:T(8,128)(2,1)S(1)}, u32[]{:S(2)}, u32[]{:S(2)}) collective-permute-start(bf16[128,1152]{1,0:T(8,128)(2,1)S(1)} %collective-permute-done.7.refs_10_.refs_6_), channel_id=1, source_target_pairs={{0,1},{1,0},{2,3},{3,2},{4,5},{5,4},{6,7},{7,6},{8,9},{9,8},{10,11... | collective-permute-start | bytes 884744 | tf_op jit(solution)/shard_map/ppermute | solution.py:158
  37.4 1.0 %copy-start.5 = (bf16[128,1152]{1,0:T(8,128)(2,1)S(1)}, bf16[128,1152]{1,0:T(8,128)(2,1)}, u32[]{:S(2)}) copy-start(bf16[128,1152]{1,0:T(8,128)(2,1)} %refs_7_.3) | copy-start | bytes 884740
  38.3 1.0 %copy-start.6 = (bf16[128,1152]{1,0:T(8,128)(2,1)S(1)}, bf16[128,1152]{1,0:T(8,128)(2,1)}, u32[]{:S(2)}) copy-start(bf16[128,1152]{1,0:T(8,128)(2,1)} %refs_3_.3) | copy-start | bytes 884740
  39.3 9.3 %copy-start.7 = (bf16[128,1152]{1,0:T(8,128)(2,1)S(1)}, bf16[128,1152]{1,0:T(8,128)(2,1)}, u32[]{:S(2)}) copy-start(bf16[128,1152]{1,0:T(8,128)(2,1)} %refs_3_.3) | copy-start | bytes 884740
  45.4 0.9 copy-start
  46.2 0.8 copy-start.2
  47.1 11.9 %collective-permute-start.21 = (s16[144,1152]{1,0:T(8,128)(2,1)S(1)}, s16[144,1152]{1,0:T(8,128)(2,1)S(1)}, u32[]{:S(2)}, u32[]{:S(2)}) collective-permute-start(s16[144,1152]{1,0:T(8,128)(2,1)S(1)} %get-tuple-element.17), channel_id=1, source_target_pairs={{0,16},{8,24},{16,0},{24,8},{1,17},{9,25},{17,1},{25,9},{2,18},{10... | collective-permute-start | bytes 995336 | tf_op jit(solution)/shard_map/ppermute | solution.py:158
  54.7 0.8 copy-start.1
  55.6 0.8 copy-start.3
  56.4 10.6 %collective-permute-start.13 = (s16[144,1152]{1,0:T(8,128)(2,1)S(1)}, s16[144,1152]{1,0:T(8,128)(2,1)S(1)}, u32[]{:S(2)}, u32[]{:S(2)}) collective-permute-start(s16[144,1152]{1,0:T(8,128)(2,1)S(1)} %get-tuple-element.13), channel_id=1, source_target_pairs={{0,8},{8,0},{16,24},{24,16},{1,9},{9,1},{17,25},{25,17},{2,10},{10... | collective-permute-start | bytes 995336 | tf_op jit(solution)/shard_map/ppermute | solution.py:158
  57.2 12.7 %collective-permute-start.20 = (s16[144,1152]{1,0:T(8,128)(2,1)S(1)}, s16[144,1152]{1,0:T(8,128)(2,1)S(1)}, u32[]{:S(2)}, u32[]{:S(2)}) collective-permute-start(s16[144,1152]{1,0:T(8,128)(2,1)S(1)} %get-tuple-element.15), channel_id=1, source_target_pairs={{0,16},{8,24},{16,0},{24,8},{1,17},{9,25},{17,1},{25,9},{2,18},{10... | collective-permute-start | bytes 995336 | tf_op jit(solution)/shard_map/ppermute | solution.py:158
  57.7 24.2 %collective-permute-start.12 = (s16[144,1152]{1,0:T(8,128)(2,1)S(1)}, s16[144,1152]{1,0:T(8,128)(2,1)S(1)}, u32[]{:S(2)}, u32[]{:S(2)}) collective-permute-start(s16[144,1152]{1,0:T(8,128)(2,1)S(1)} %get-tuple-element.11), channel_id=1, source_target_pairs={{0,8},{8,0},{16,24},{24,16},{1,9},{9,1},{17,25},{25,17},{2,10},{10... | collective-permute-start | bytes 995336 | tf_op jit(solution)/shard_map/ppermute | solution.py:158
  58.9 0.7 copy-start.8
  61.7 17.2 %collective-permute-start.22 = (s16[144,1152]{1,0:T(8,128)(2,1)}, s16[144,1152]{1,0:T(8,128)(2,1)S(1)}, u32[]{:S(2)}, u32[]{:S(2)}) collective-permute-start(s16[144,1152]{1,0:T(8,128)(2,1)} %passed_sum.3), channel_id=1, source_target_pairs={{0,4},{1,5},{2,6},{3,7},{4,0},{5,1},{6,2},{7,3},{8,12},{9,13},{10,... | collective-permute-start | bytes 995336 | tf_op jit(solution)/shard_map/ppermute | solution.py:158
  67.0 0.7 copy-start.12
  69.8 15.5 %collective-permute-start.14 = (s16[144,1152]{1,0:T(8,128)(2,1)}, s16[144,1152]{1,0:T(8,128)(2,1)S(1)}, u32[]{:S(2)}, u32[]{:S(2)}) collective-permute-start(s16[144,1152]{1,0:T(8,128)(2,1)} %passed_sum.2), channel_id=1, source_target_pairs={{0,2},{1,3},{2,0},{3,1},{4,6},{5,7},{6,4},{7,5},{8,10},{9,11},{10,... | collective-permute-start | bytes 995336 | tf_op jit(solution)/shard_map/ppermute | solution.py:158
  69.8 9.1 %copy-start.10 = (s16[144,1152]{1,0:T(8,128)(2,1)}, s16[144,1152]{1,0:T(8,128)(2,1)S(1)}, u32[]{:S(2)}) copy-start(s16[144,1152]{1,0:T(8,128)(2,1)S(1)} %collective-permute-done.20.refs_0_) | copy-start | bytes 995332
  78.9 0.7 copy-start.13
  81.9 3.4 %copy-start.9 = (s16[144,1152]{1,0:T(8,128)(2,1)}, s16[144,1152]{1,0:T(8,128)(2,1)S(1)}, u32[]{:S(2)}) copy-start(s16[144,1152]{1,0:T(8,128)(2,1)S(1)} %collective-permute-done.12.refs_0_) | copy-start | bytes 995332
  85.4 0.7 copy-start.11

commit v2 on v1

v2 whole, which is shorter than its diff:
```python
import math

import jax
import jax.numpy as jnp
from jax import lax
from jax.experimental import pallas as pl
from jax.experimental.pallas import tpu as pltpu
from jax.sharding import PartitionSpec as P

LOG2E = 1.4426950408889634
CODE_TOP = 32000.0
CODE_STEPS = 32.0
CODE_ROWS = 16
TILE = 256


def scale_code(top):
    return jnp.ceil(jnp.log(jnp.maximum(top, 1e-30)) * (CODE_STEPS * LOG2E))


def encoded(value):
    code = scale_code(jnp.max(jnp.abs(value), axis=0, keepdims=True))
    gain = CODE_TOP * jnp.exp(code * (-1.0 / (CODE_STEPS * LOG2E)))
    whole = jnp.round(value * gain).astype(jnp.int32).astype(jnp.int16)
    scales = jnp.broadcast_to(code.astype(jnp.int32), (CODE_ROWS, value.shape[1]))
    return whole, scales.astype(jnp.int16)


def decoded(ref, rows, columns):
    code = ref[pl.ds(rows, CODE_ROWS), columns].astype(jnp.int32).astype(jnp.float32)[:1]
    gain = jnp.exp(code * (1.0 / (CODE_STEPS * LOG2E))) * (1.0 / CODE_TOP)
    return ref[pl.ds(0, rows), columns].astype(jnp.int32).astype(jnp.float32) * gain


def key_column(keys, index):
    size = keys.shape[1]
    return jnp.broadcast_to(keys[index : index + 1, :], (size, size)).T


def add_products(refs, rows, columns, before, emit):
    scalars, row_keys, column_keys, x_parts, y_parts, weights = refs
    size, width = x_parts[0].shape
    slope = scalars[0] * LOG2E
    shift = scalars[1] * LOG2E
    x_all = jnp.concatenate([x_parts[r][...] for r in rows], axis=0)
    per_tile = TILE // size
    keys = [jnp.tile(key_column(row_keys, r), (1, per_tile)) for r in rows]
    for n in range(0, len(columns), per_tile):
        tile = columns[n : n + per_tile]
        y_tile = jnp.concatenate([y_parts[c][...] for c in tile], axis=0)
        other = jnp.concatenate([column_keys[c : c + 1, :] for c in tile], axis=1)
        scores = lax.dot_general(
            x_all, y_tile, (((1,), (1,)), ((), ())), preferred_element_type=jnp.float32
        )
        for i in range(len(rows)):
            z = scores[i * size : (i + 1) * size] * slope + shift
            sig = 1.0 / (1.0 + jnp.exp2(-z))
            w = jnp.where(keys[i] == other, sig - 1.0, sig)
            weights[pl.ds(i * size, size), pl.ds(n * size, TILE)] = w.astype(jnp.bfloat16)
    for start in range(0, width, TILE):
        span = min(TILE, width - start)
        part = pl.ds(start, span)
        y_part = jnp.concatenate([y_parts[c][:, part] for c in columns], axis=0)
        sums = jnp.dot(
            weights[pl.ds(0, len(rows) * size), pl.ds(0, len(columns) * size)],
            y_part,
            preferred_element_type=jnp.float32,
        )
        for i, r in enumerate(rows):
            block = sums[i * size : (i + 1) * size]
            emit(r, part, block if before is None else before[r][:, part] + block)


def gradient_call(kernel, name, scalars, keys, x_parts, y_parts, before, out_shape, pairs):
    size, width = x_parts[0].shape
    rows, columns, sums = len(x_parts), len(y_parts), len(before)

    def body(*refs):
        x_refs, refs_left = refs[3 : 3 + rows], refs[3 + rows :]
        y_refs, refs_left = refs_left[:columns], refs_left[columns:]
        sum_refs, outs = refs_left[:sums], refs_left[sums:-1]
        kernel((*refs[:3], x_refs, y_refs, refs[-1]), sum_refs, outs)

    smem = pl.BlockSpec(memory_space=pltpu.SMEM)
    vmem = pl.BlockSpec(memory_space=pltpu.VMEM)
    held = sum(math.prod(o.shape) * o.dtype.itemsize for o in out_shape)
    held += sum(math.prod(o.shape) * o.dtype.itemsize for o in [*x_parts, *y_parts, *before])
    held += rows * columns * size * size * 2
    return pl.pallas_call(
        body,
        out_shape=out_shape,
        in_specs=[smem] + [vmem] * (2 + rows + columns + sums),
        out_specs=[vmem] * len(out_shape),
        scratch_shapes=[pltpu.VMEM((rows * size, columns * size), jnp.bfloat16)],
        compiler_params=pltpu.CompilerParams(vmem_limit_bytes=held + 8 * 2**20),
        cost_estimate=pl.CostEstimate(
            flops=pairs * size,
            bytes_accessed=pairs * size,
            transcendentals=0,
        ),
        name=name,
    )(scalars, *keys, *x_parts, *y_parts, *before)


def early_sums(scalars, keys, x_parts, y_parts):
    size, width = x_parts[0].shape
    rows, columns = list(range(len(x_parts))), list(range(len(y_parts)))

    def kernel(refs, _, outs):
        def emit(r, part, block):
            outs[r][:, part] = block

        add_products(refs, rows, columns, None, emit)

    shapes = [jax.ShapeDtypeStruct((size, width), jnp.float32)] * len(rows)
    return gradient_call(
        kernel, "early_sums", scalars, keys, x_parts, y_parts, [], shapes, len(rows) * len(columns)
    )


def late_sums(scalars, keys, x_parts, y_parts, early_rows, late_columns, before, kept):
    size, width = x_parts[0].shape
    late_rows = [r for r in range(len(x_parts)) if r not in early_rows]
    slot = {r: i for i, r in enumerate(early_rows)}

    def kernel(refs, sums, outs):
        def emit(r, part, block):
            if r < kept:
                outs[r][:, part] = block
            else:
                whole, scales = encoded(block)
                outs[r][pl.ds(0, size), part] = whole
                outs[r][pl.ds(size, CODE_ROWS), part] = scales

        add_products(refs, late_rows, list(range(len(y_parts))), None, emit)
        add_products(refs, early_rows, late_columns, {r: sums[slot[r]] for r in early_rows}, emit)

    whole = jax.ShapeDtypeStruct((size, width), jnp.float32)
    coded = jax.ShapeDtypeStruct((size + CODE_ROWS, width), jnp.int16)
    shapes = [whole if r < kept else coded for r in range(len(x_parts))]
    pairs = len(late_rows) * len(y_parts) + len(early_rows) * len(late_columns)
    return gradient_call(
        kernel, "late_sums", scalars, keys, x_parts, y_parts, before, shapes, pairs
    )


def picked(keys, chosen):
    return jnp.stack([keys[i] for i in chosen])


def combined(scalars, kept, received, final):
    size, width = kept.shape

    def kernel(scalars, kept, *refs):
        out = refs[-1]
        for start in range(0, width, 128):
            columns = pl.ds(start, 128)
            total = kept[:, columns]
            for r in refs[:-1]:
                total = total + decoded(r, size, columns)
            if final:
                out[:, columns] = total * scalars[0]
            else:
                whole, scales = encoded(total)
                out[pl.ds(0, size), columns] = whole
                out[pl.ds(size, CODE_ROWS), columns] = scales

    smem = pl.BlockSpec(memory_space=pltpu.SMEM)
    vmem = pl.BlockSpec(memory_space=pltpu.VMEM)
    shape = (size, width) if final else (size + CODE_ROWS, width)
    return pl.pallas_call(
        kernel,
        out_shape=jax.ShapeDtypeStruct(shape, jnp.float32 if final else jnp.int16),
        in_specs=[smem] + [vmem] * (1 + len(received)),
        out_specs=vmem,
        compiler_params=pltpu.CompilerParams(vmem_limit_bytes=8 * 2**20),
        cost_estimate=pl.CostEstimate(
            flops=8 * size * width, bytes_accessed=12 * size * width, transcendentals=0
        ),
        name="output_sum" if final else "passed_sum",
    )(scalars, kept, *received)


def swapped(block, step):
    axis, bit = step
    return lax.ppermute(block, axis, [(i, i ^ bit) for i in range(lax.axis_size(axis))])


def gathered(block, steps):
    blocks = [block]
    for step in steps:
        blocks = blocks + [swapped(b, step) for b in blocks]
    return blocks


def scattered_sum(scalars, parts, steps):
    received = [[] for _ in parts]
    for s in reversed(range(len(steps))):
        half = 1 << s
        for m in reversed(range(half)):
            top = parts[half + m]
            if s + 1 < len(steps):
                top = combined(scalars, top, received[half + m], False)
            received[m].append(swapped(top, steps[s]))
    return combined(scalars, parts[0], received[0], True)


def bit_steps(axis):
    return [(axis, 1 << k) for k in range(int(math.log2(lax.axis_size(axis))))]


def owner_keys(steps, size):
    owners = [(lax.axis_index("blk"), lax.axis_index("grp"))]
    for axis, bit in steps:
        owners = owners + [(b ^ bit, g) if axis == "blk" else (b, g ^ bit) for b, g in owners]
    grp_count = lax.axis_size("grp")
    firsts = jnp.stack([(b * grp_count + g) * size for b, g in owners])
    return firsts[:, None] + jnp.arange(size, dtype=jnp.int32)[None, :]


def per_device(
    picture_vectors, caption_vectors, matching_caption, sharpness_parameter, additive_intercept
):
    size = picture_vectors.shape[0]
    scalars = jnp.concatenate([sharpness_parameter, additive_intercept])
    core, *grp_steps = bit_steps("grp")
    blk_steps = bit_steps("blk")
    every = grp_steps + blk_steps
    image_steps, text_steps = every[0::2], every[1::2]

    images = gathered(picture_vectors, image_steps)
    texts = gathered(caption_vectors, text_steps)
    labels = matching_caption[None, :]
    for step in image_steps + [core]:
        labels = jnp.concatenate([labels, swapped(labels, step)])
    ids = owner_keys(text_steps + [core], size)

    def split(count):
        early = [m for m in range(count) if m <= count // 2]
        return early, [m for m in range(count) if m not in early]

    image_count, text_count = len(images), len(texts)
    early_images, late_images = split(image_count)
    early_texts, late_texts = split(text_count)
    other_images = {m: swapped(images[m], core) for m in early_images}
    other_texts = {m: swapped(texts[m], core) for m in early_texts}

    def columns(chosen, count):
        return chosen + [count + m for m in chosen]

    text_before = early_sums(
        scalars,
        (picked(ids, early_texts), picked(labels, columns(early_images, image_count))),
        [texts[m] for m in early_texts],
        [images[m] for m in early_images] + [other_images[m] for m in early_images],
    )
    image_before = early_sums(
        scalars,
        (picked(labels, early_images), picked(ids, columns(early_texts, text_count))),
        [images[m] for m in early_images],
        [texts[m] for m in early_texts] + [other_texts[m] for m in early_texts],
    )
    images, texts, text_before, image_before = lax.optimization_barrier(
        (images, texts, text_before, image_before)
    )
    other_images |= {m: swapped(images[m], core) for m in late_images}
    other_texts |= {m: swapped(texts[m], core) for m in late_texts}
    text_parts = late_sums(
        scalars,
        (ids[:text_count], labels),
        texts,
        images + [other_images[m] for m in range(image_count)],
        early_texts,
        columns(late_images, image_count),
        text_before,
        text_count // 2,
    )
    text_parts, image_scalars = lax.optimization_barrier((text_parts, scalars))
    image_parts = late_sums(
        image_scalars,
        (labels[:image_count], ids),
        images,
        texts + [other_texts[m] for m in range(text_count)],
        early_images,
        columns(late_texts, text_count),
        image_before,
        image_count // 2,
    )
    picture_derivative = scattered_sum(scalars, image_parts, image_steps)
    text_grad = scattered_sum(scalars, text_parts, text_steps)
    return (picture_derivative, text_grad)


def solution(mesh):
    placed = (P(("blk", "grp"), None), P(("blk", "grp"), None), P(("blk", "grp")), P(), P())
    return jax.shard_map(
        per_device,
        mesh=mesh,
        in_specs=placed,
        out_specs=(P(("blk", "grp"), None), P(("blk", "grp"), None)),
        check_vma=False,
    )
```

time: 88.7 us -> 73.3 us (0.83)
  local copies, waits for them, and re-layouts: 8.21 us -> 2.02 us
  waiting for transfers between devices: 37.9 us -> 32.3 us
  Pallas kernels: 20.9 us -> 15.6 us
  starting transfers between devices: 19.1 us -> 20.9 us
    unnamed x30 -> x10, local copies, waits for them, and re-layouts: 8.12 us -> 1.93 us
    ppermute x23, waiting for transfers between devices: 37.9 us -> 32.3 us  [swapped(): lax.ppermute(block, axis, [(i, i ^ bit) for i in range(lax.axis_size(axis...]
    pallas_call x4, Pallas kernels: 8.72 us -> 4.59 us  [combined(): pl.pallas_call(kernel, out_shape=jax.ShapeDtypeStruct(shape, jnp.float32...]
    ppermute x23, starting transfers between devices: 19.1 us -> 20.9 us  [swapped(): lax.ppermute(block, axis, [(i, i ^ bit) for i in range(lax.axis_size(axis...]
    pallas_call x2 -> x4, Pallas kernels: 12.2 us -> 11 us  [gradient_call(): pl.pallas_call(body, out_shape=out_shape, in_specs=[smem] + [vmem] * (2 +...]
  transfers between devices with their start and end apart: 23 -> 23, of which waited for: 8 -> 10; matrix products, arithmetic and copies ran while one was open for 0% -> 0% of each run, Pallas kernels for 21% -> 19%
where the time goes in v2:
time: 73.3 us; the launch traced here: 73.1 us
  waiting for transfers between devices  32.3 us (44%)
  starting transfers between devices  20.9 us (29%)
  Pallas kernels  15.6 us (21%)
  between operations  2.08 us (3%)
  local copies, waits for them, and re-layouts  2.02 us (3%)
    ppermute x23, waiting for transfers between devices, swapped(): lax.ppermute(block, axis, [(i, i ^ bit) for i in range(lax.axis_size(axis...  32.3 us
    ppermute x23, starting transfers between devices, swapped(): lax.ppermute(block, axis, [(i, i ^ bit) for i in range(lax.axis_size(axis...  20.9 us
    pallas_call x4, Pallas kernels, gradient_call(): pl.pallas_call(body, out_shape=out_shape, in_specs=[smem] + [vmem] * (2 +...  11 us
    pallas_call x4, Pallas kernels, combined(): pl.pallas_call(kernel, out_shape=jax.ShapeDtypeStruct(shape, jnp.float32...  4.59 us
    unnamed x10, local copies, waits for them, and re-layouts  1.93 us
  transfers between devices with their start and end apart: 23, of which 10 were waited for; matrix products, arithmetic and copies ran while one was open for 0% of the time, Pallas kernels for 19%

profile of v2, /device:TPU:0, one launch (start us, length us, event | category | flops | bytes accessed | tf_op | source)
XLA Modules:
  0.0 73.1 jit_solution(1055592605190379303)
XLA Ops:
  0.6 0.0 copy-start.4
  0.6 4.1 %collective-permute-start.6 = (bf16[128,1152]{1,0:T(8,128)(2,1)}, bf16[128,1152]{1,0:T(8,128)(2,1)S(1)}, u32[]{:S(2)}, u32[]{:S(2)}) collective-permute-start(bf16[128,1152]{1,0:T(8,128)(2,1)} %refs_7_.1), channel_id=1, source_target_pairs={{0,4},{1,5},{2,6},{3,7},{4,0},{5,1},{6,2},{7,3},{8,12},{9,13},{10,... | collective-permute-start | bytes 884744 | tf_op jit(solution)/shard_map/ppermute | solution.py:186
  4.7 1.5 %collective-permute-start.7 = (bf16[128,1152]{1,0:T(8,128)(2,1)}, bf16[128,1152]{1,0:T(8,128)(2,1)S(1)}, u32[]{:S(2)}, u32[]{:S(2)}) collective-permute-start(bf16[128,1152]{1,0:T(8,128)(2,1)} %refs_7_.1), channel_id=1, source_target_pairs={{0,16},{8,24},{16,0},{24,8},{1,17},{9,25},{17,1},{25,9},{2,18},{10... | collective-permute-start | bytes 884744 | tf_op jit(solution)/shard_map/ppermute | solution.py:186
  6.3 1.6 %collective-permute-start.3 = (bf16[128,1152]{1,0:T(8,128)(2,1)}, bf16[128,1152]{1,0:T(8,128)(2,1)S(1)}, u32[]{:S(2)}, u32[]{:S(2)}) collective-permute-start(bf16[128,1152]{1,0:T(8,128)(2,1)} %refs_3_.5), channel_id=1, source_target_pairs={{0,2},{1,3},{2,0},{3,1},{4,6},{5,7},{6,4},{7,5},{8,10},{9,11},{10,... | collective-permute-start | bytes 884744 | tf_op jit(solution)/shard_map/ppermute | solution.py:186
  7.8 1.5 %collective-permute-start.4 = (bf16[128,1152]{1,0:T(8,128)(2,1)}, bf16[128,1152]{1,0:T(8,128)(2,1)S(1)}, u32[]{:S(2)}, u32[]{:S(2)}) collective-permute-start(bf16[128,1152]{1,0:T(8,128)(2,1)} %refs_3_.5), channel_id=1, source_target_pairs={{0,8},{8,0},{16,24},{24,16},{1,9},{9,1},{17,25},{25,17},{2,10},{10... | collective-permute-start | bytes 884744 | tf_op jit(solution)/shard_map/ppermute | solution.py:186
  9.3 0.0 copy-done.4
  9.3 0.4 collective-permute-start
  9.8 10.1 %collective-permute-done = s32[1,128]{1,0:T(1,128)S(1)} collective-permute-done((s32[1,128]{1,0:T(1,128)S(1)}, s32[1,128]{1,0:T(1,128)S(1)}, u32[]{:S(2)}, u32[]{:S(2)}) %collective-permute-start) | collective-permute-done | bytes 544 | tf_op jit(solution)/shard_map/ppermute | solution.py:186
  19.9 1.5 %collective-permute-start.1 = (s32[2,128]{1,0:T(2,128)S(1)}, s32[2,128]{1,0:T(2,128)S(1)}, u32[]{:S(2)}, u32[]{:S(2)}) collective-permute-start(s32[2,128]{1,0:T(2,128)S(1)} %pad_add_fusion.5), channel_id=1, source_target_pairs={{0,8},{8,0},{16,24},{24,16},{1,9},{9,1},{17,25},{25,17},{2,10},{10... | collective-permute-start | bytes 3080 | tf_op jit(solution)/shard_map/ppermute | solution.py:186
  21.4 0.1 stack.45
  21.5 1.9 %collective-permute-done.1 = s32[2,128]{1,0:T(2,128)S(1)} collective-permute-done((s32[2,128]{1,0:T(2,128)S(1)}, s32[2,128]{1,0:T(2,128)S(1)}, u32[]{:S(2)}, u32[]{:S(2)}) %collective-permute-start.1) | collective-permute-done | bytes 1056 | tf_op jit(solution)/shard_map/ppermute | solution.py:186
  23.5 0.1 collective-permute-start.2
  23.5 0.1 iota_add_fusion.refs_2_
  24.9 0.0 collective-permute-done.2
  24.9 0.6 collective-permute-start.9
  25.5 0.0 collective-permute-done.3.refs_7_.refs_4_.refs_8_
  25.5 0.1 collective-permute-start.10
  25.6 0.0 collective-permute-done.4.refs_8_.refs_5_.refs_9_
  25.6 0.4 collective-permute-start.11
  26.0 0.0 collective-permute-done.6.refs_4_.refs_7_.refs_8_
  26.0 0.2 collective-permute-start.12
  26.2 0.0 collective-permute-done.7.refs_5_.refs_8_.refs_9_
  26.2 1.5 %collective-permute-start.5 = (bf16[128,1152]{1,0:T(8,128)(2,1)S(1)}, bf16[128,1152]{1,0:T(8,128)(2,1)S(1)}, u32[]{:S(2)}, u32[]{:S(2)}) collective-permute-start(bf16[128,1152]{1,0:T(8,128)(2,1)S(1)} %collective-permute-done.3.refs_7_.refs_4_.refs_8_), channel_id=1, source_target_pairs={{0,8},{8,0},{16,24},{24,16},{1,9},{9,1},{17,25},{25,17},{2,10},{10... | collective-permute-start | bytes 884744 | tf_op jit(solution)/shard_map/ppermute | solution.py:186
  27.7 0.0 collective-permute-done.9.refs_9_.refs_11_
  27.7 0.2 collective-permute-start.13
  27.9 0.0 collective-permute-done.10.refs_10_.refs_12_
  27.9 0.5 collective-permute-start.8
  28.4 0.0 collective-permute-done.11.refs_11_.refs_13_
  28.4 0.1 collective-permute-start.14
  28.5 0.1 pad_maximum_fusion.refs_0_.scalars
  28.6 0.0 copy-start
  28.6 1.0 %copy-done = bf16[128,1152]{1,0:T(8,128)(2,1)S(1)} copy-done((bf16[128,1152]{1,0:T(8,128)(2,1)S(1)}, bf16[128,1152]{1,0:T(8,128)(2,1)}, u32[]{:S(2)}) %copy-start) | copy-done | bytes 294936
  29.5 1.0 %copy-done.2 = bf16[128,1152]{1,0:T(8,128)(2,1)S(1)} copy-done((bf16[128,1152]{1,0:T(8,128)(2,1)S(1)}, bf16[128,1152]{1,0:T(8,128)(2,1)}, u32[]{:S(2)}) %copy-start.2) | copy-done | bytes 294936
  30.5 2.5 %early_sums.2 = (f32[128,1152]{1,0:T(8,128)S(1)}, f32[128,1152]{1,0:T(8,128)S(1)}, f32[128,1152]{1,0:T(8,128)S(1)}) custom-call(f32[2]{0:T(128)S(1)} %pad_maximum_fusion.refs_0_.scalars, s32[3,128]{1,0:T(4,128)S(1)} %get-tuple-element.69.refs_1_, s32[6,128]{1,0:T(8,128)S(1)} %pad_add_fusion.1.refs_2_, bf16[128,1152]{1,0:T(8,128)(2,1)S(1)} %copy-done.2, ...), custom_call_target="tpu_custom_call" | custom-call | flops 2304 | bytes 2304 | tf_op jit(solution)/shard_map/early_sums/pallas_call | solution.py:89
  33.0 0.0 collective-permute-done.12.refs_9_.refs_11_
  33.0 0.0 collective-permute-done.13.refs_10_.refs_12_
  33.0 0.0 collective-permute-done.14.refs_11_.refs_13_
  33.0 0.0 copy-done.1
  33.0 0.0 copy-done.3
  33.0 2.5 %early_sums.3 = (f32[128,1152]{1,0:T(8,128)S(1)}, f32[128,1152]{1,0:T(8,128)S(1)}, f32[128,1152]{1,0:T(8,128)S(1)}) custom-call(f32[2]{0:T(128)S(1)} %pad_maximum_fusion.refs_0_.scalars, s32[3,128]{1,0:T(4,128)S(1)} %pad_add_fusion.4.refs_1_, s32[6,128]{1,0:T(8,128)S(1)} %pad_add_fusion.2.refs_2_, bf16[128,1152]{1,0:T(8,128)(2,1)S(1)} %copy-done.1, ...), custom_call_target="tpu_custom_call" | custom-call | flops 2304 | bytes 2304 | tf_op jit(solution)/shard_map/early_sums/pallas_call | solution.py:89
  35.5 0.1 collective-permute-done.5.refs_10_.refs_6_
  35.5 1.6 %collective-permute-done.8.refs_6_.refs_10_ = bf16[128,1152]{1,0:T(8,128)(2,1)S(1)} collective-permute-done((bf16[128,1152]{1,0:T(8,128)(2,1)S(1)}, bf16[128,1152]{1,0:T(8,128)(2,1)S(1)}, u32[]{:S(2)}, u32[]{:S(2)}) %collective-permute-start.8) | collective-permute-done | bytes 294944 | tf_op jit(solution)/shard_map/ppermute | solution.py:186
  37.2 0.0 collective-permute-start.15
  37.2 0.5 collective-permute-start.16
  37.7 1.1 %collective-permute-done.15.refs_14_ = bf16[128,1152]{1,0:T(8,128)(2,1)S(1)} collective-permute-done((bf16[128,1152]{1,0:T(8,128)(2,1)S(1)}, bf16[128,1152]{1,0:T(8,128)(2,1)S(1)}, u32[]{:S(2)}, u32[]{:S(2)}) %collective-permute-start.15) | collective-permute-done | bytes 294944 | tf_op jit(solution)/shard_map/ppermute | solution.py:186
  38.7 3.0 %late_sums.2 = (f32[128,1152]{1,0:T(8,128)S(1)}, f32[128,1152]{1,0:T(8,128)S(1)}, s16[144,1152]{1,0:T(8,128)(2,1)S(1)}, s16[144,1152]{1,0:T(8,128)(2,1)S(1)}) custom-call(f32[2]{0:T(128)S(1)} %pad_maximum_fusion.refs_0_.scalars, s32[4,128]{1,0:T(4,128)S(1)} %slice.14.refs_1_, s32[8,128]{1,0:T(8,128)S(1)} %pad_add_fusion.refs_2_, ...), custom_call_target="tpu_custom_call" | custom-call | flops 1792 | bytes 1792 | tf_op jit(solution)/shard_map/late_sums/pallas_call | solution.py:89
  41.8 0.6 collective-permute-start.21
  42.4 0.0 collective-permute-done.16.refs_14_
  42.4 3.0 %late_sums.3 = (f32[128,1152]{1,0:T(8,128)S(1)}, f32[128,1152]{1,0:T(8,128)S(1)}, s16[144,1152]{1,0:T(8,128)(2,1)S(1)}, s16[144,1152]{1,0:T(8,128)(2,1)S(1)}) custom-call(f32[2]{0:T(128)S(1)} %pad_maximum_fusion.refs_0_.scalars, s32[4,128]{1,0:T(4,128)S(1)} %pad_add_fusion.3.refs_1_, s32[8,128]{1,0:T(8,128)S(1)} %iota_add_fusion.refs_2_, ...), custom_call_target="tpu_custom_call" | custom-call | flops 1792 | bytes 1792 | tf_op jit(solution)/shard_map/late_sums/pallas_call | solution.py:89
  45.4 0.8 %collective-permute-start.18 = (s16[144,1152]{1,0:T(8,128)(2,1)S(1)}, s16[144,1152]{1,0:T(8,128)(2,1)S(1)}, u32[]{:S(2)}, u32[]{:S(2)}) collective-permute-start(s16[144,1152]{1,0:T(8,128)(2,1)S(1)} %get-tuple-element.63), channel_id=1, source_target_pairs={{0,8},{8,0},{16,24},{24,16},{1,9},{9,1},{17,25},{25,17},{2,10},{10... | collective-permute-start | bytes 995336 | tf_op jit(solution)/shard_map/ppermute | solution.py:186
  46.2 1.5 %collective-permute-start.20 = (s16[144,1152]{1,0:T(8,128)(2,1)S(1)}, s16[144,1152]{1,0:T(8,128)(2,1)S(1)}, u32[]{:S(2)}, u32[]{:S(2)}) collective-permute-start(s16[144,1152]{1,0:T(8,128)(2,1)S(1)} %get-tuple-element.65), channel_id=1, source_target_pairs={{0,16},{8,24},{16,0},{24,8},{1,17},{9,25},{17,1},{25,9},{2,18},{10... | collective-permute-start | bytes 995336 | tf_op jit(solution)/shard_map/ppermute | solution.py:186
  47.8 1.2 %collective-permute-start.17 = (s16[144,1152]{1,0:T(8,128)(2,1)S(1)}, s16[144,1152]{1,0:T(8,128)(2,1)S(1)}, u32[]{:S(2)}, u32[]{:S(2)}) collective-permute-start(s16[144,1152]{1,0:T(8,128)(2,1)S(1)} %get-tuple-element.61), channel_id=1, source_target_pairs={{0,8},{8,0},{16,24},{24,16},{1,9},{9,1},{17,25},{25,17},{2,10},{10... | collective-permute-start | bytes 995336 | tf_op jit(solution)/shard_map/ppermute | solution.py:186
  49.0 3.5 %collective-permute-done.21.refs_0_ = s16[144,1152]{1,0:T(8,128)(2,1)S(1)} collective-permute-done((s16[144,1152]{1,0:T(8,128)(2,1)S(1)}, s16[144,1152]{1,0:T(8,128)(2,1)S(1)}, u32[]{:S(2)}, u32[]{:S(2)}) %collective-permute-start.21) | collective-permute-done | bytes 331808 | tf_op jit(solution)/shard_map/ppermute | solution.py:186
  52.5 0.7 %passed_sum.3 = s16[144,1152]{1,0:T(8,128)(2,1)S(1)} custom-call(f32[2]{0:T(128)S(1)} %pad_maximum_fusion.refs_0_.scalars, f32[128,1152]{1,0:T(8,128)S(1)} %get-tuple-element.66.kept, s16[144,1152]{1,0:T(8,128)(2,1)S(1)} %collective-permute-done.21.refs_0_), custom_call_target="tpu_custom_call" | custom-call | flops 1179648 | bytes 1769472 | tf_op jit(solution)/shard_map/passed_sum/pallas_call | solution.py:171
  53.2 0.7 collective-permute-start.22
  53.9 2.2 %collective-permute-done.18.refs_0_ = s16[144,1152]{1,0:T(8,128)(2,1)S(1)} collective-permute-done((s16[144,1152]{1,0:T(8,128)(2,1)S(1)}, s16[144,1152]{1,0:T(8,128)(2,1)S(1)}, u32[]{:S(2)}, u32[]{:S(2)}) %collective-permute-start.18) | collective-permute-done | bytes 331808 | tf_op jit(solution)/shard_map/ppermute | solution.py:186
  56.2 0.7 %passed_sum.2 = s16[144,1152]{1,0:T(8,128)(2,1)S(1)} custom-call(f32[2]{0:T(128)S(1)} %pad_maximum_fusion.refs_0_.scalars, f32[128,1152]{1,0:T(8,128)S(1)} %get-tuple-element.62.kept, s16[144,1152]{1,0:T(8,128)(2,1)S(1)} %collective-permute-done.18.refs_0_), custom_call_target="tpu_custom_call" | custom-call | flops 1179648 | bytes 1769472 | tf_op jit(solution)/shard_map/passed_sum/pallas_call | solution.py:171
  56.9 1.3 %collective-permute-start.19 = (s16[144,1152]{1,0:T(8,128)(2,1)S(1)}, s16[144,1152]{1,0:T(8,128)(2,1)S(1)}, u32[]{:S(2)}, u32[]{:S(2)}) collective-permute-start(s16[144,1152]{1,0:T(8,128)(2,1)S(1)} %passed_sum.2), channel_id=1, source_target_pairs={{0,2},{1,3},{2,0},{3,1},{4,6},{5,7},{6,4},{7,5},{8,10},{9,11},{10,... | collective-permute-start | bytes 995336 | tf_op jit(solution)/shard_map/ppermute | solution.py:186
  58.2 0.6 collective-permute-done.20.refs_0_
  58.8 10.6 %collective-permute-done.22.refs_1_ = s16[144,1152]{1,0:T(8,128)(2,1)S(1)} collective-permute-done((s16[144,1152]{1,0:T(8,128)(2,1)S(1)}, s16[144,1152]{1,0:T(8,128)(2,1)S(1)}, u32[]{:S(2)}, u32[]{:S(2)}) %collective-permute-start.22) | collective-permute-done | bytes 331808 | tf_op jit(solution)/shard_map/ppermute | solution.py:186
  69.4 1.6 %output_sum.3 = f32[128,1152]{1,0:T(8,128)} custom-call(f32[2]{0:T(128)S(1)} %pad_maximum_fusion.refs_0_.scalars, f32[128,1152]{1,0:T(8,128)S(1)} %get-tuple-element.64.kept, s16[144,1152]{1,0:T(8,128)(2,1)S(1)} %collective-permute-done.20.refs_0_, s16[144,1152]{1,0:T(8,128)(2,1)S(1)} %collective-permute-done.22.refs_1_), custom_call_target="tpu_custom_call" | custom-call | flops 1179648 | bytes 1769472 | tf_op jit(solution)/shard_map/output_sum/pallas_call | solution.py:171
  71.0 0.0 collective-permute-done.17.refs_0_
  71.0 0.5 collective-permute-done.19.refs_1_
  71.5 1.6 %output_sum.2 = f32[128,1152]{1,0:T(8,128)} custom-call(f32[2]{0:T(128)S(1)} %pad_maximum_fusion.refs_0_.scalars, f32[128,1152]{1,0:T(8,128)S(1)} %get-tuple-element.60.kept, s16[144,1152]{1,0:T(8,128)(2,1)S(1)} %collective-permute-done.17.refs_0_, s16[144,1152]{1,0:T(8,128)(2,1)S(1)} %collective-permute-done.19.refs_1_), custom_call_target="tpu_custom_call" | custom-call | flops 1179648 | bytes 1769472 | tf_op jit(solution)/shard_map/output_sum/pallas_call | solution.py:171
  (12 shorter events, 0.1 us)
Async XLA Ops:
  0.6 8.7 %copy-start.4 = (s32[128]{0:T(128)S(1)}, s32[128]{0:T(128)}, u32[]{:S(2)}) copy-start(s32[128]{0:T(128)} %param.7) | copy-start | bytes 1540
  0.6 25.4 %collective-permute-start.6 = (bf16[128,1152]{1,0:T(8,128)(2,1)}, bf16[128,1152]{1,0:T(8,128)(2,1)S(1)}, u32[]{:S(2)}, u32[]{:S(2)}) collective-permute-start(bf16[128,1152]{1,0:T(8,128)(2,1)} %refs_7_.1), channel_id=1, source_target_pairs={{0,4},{1,5},{2,6},{3,7},{4,0},{5,1},{6,2},{7,3},{8,12},{9,13},{10,... | collective-permute-start | bytes 884744 | tf_op jit(solution)/shard_map/ppermute | solution.py:186
  4.7 21.4 %collective-permute-start.7 = (bf16[128,1152]{1,0:T(8,128)(2,1)}, bf16[128,1152]{1,0:T(8,128)(2,1)S(1)}, u32[]{:S(2)}, u32[]{:S(2)}) collective-permute-start(bf16[128,1152]{1,0:T(8,128)(2,1)} %refs_7_.1), channel_id=1, source_target_pairs={{0,16},{8,24},{16,0},{24,8},{1,17},{9,25},{17,1},{25,9},{2,18},{10... | collective-permute-start | bytes 884744 | tf_op jit(solution)/shard_map/ppermute | solution.py:186
  6.3 19.2 %collective-permute-start.3 = (bf16[128,1152]{1,0:T(8,128)(2,1)}, bf16[128,1152]{1,0:T(8,128)(2,1)S(1)}, u32[]{:S(2)}, u32[]{:S(2)}) collective-permute-start(bf16[128,1152]{1,0:T(8,128)(2,1)} %refs_3_.5), channel_id=1, source_target_pairs={{0,2},{1,3},{2,0},{3,1},{4,6},{5,7},{6,4},{7,5},{8,10},{9,11},{10,... | collective-permute-start | bytes 884744 | tf_op jit(solution)/shard_map/ppermute | solution.py:186
  7.8 17.7 %collective-permute-start.4 = (bf16[128,1152]{1,0:T(8,128)(2,1)}, bf16[128,1152]{1,0:T(8,128)(2,1)S(1)}, u32[]{:S(2)}, u32[]{:S(2)}) collective-permute-start(bf16[128,1152]{1,0:T(8,128)(2,1)} %refs_3_.5), channel_id=1, source_target_pairs={{0,8},{8,0},{16,24},{24,16},{1,9},{9,1},{17,25},{25,17},{2,10},{10... | collective-permute-start | bytes 884744 | tf_op jit(solution)/shard_map/ppermute | solution.py:186
  9.3 10.6 %collective-permute-start = (s32[1,128]{1,0:T(1,128)S(1)}, s32[1,128]{1,0:T(1,128)S(1)}, u32[]{:S(2)}, u32[]{:S(2)}) collective-permute-start(s32[1,128]{1,0:T(1,128)S(1)} %bitcast.10), channel_id=1, source_target_pairs={{0,2},{1,3},{2,0},{3,1},{4,6},{5,7},{6,4},{7,5},{8,10},{9,11},{10,... | collective-permute-start | bytes 1544 | tf_op jit(solution)/shard_map/ppermute | solution.py:186
  19.9 3.6 %collective-permute-start.1 = (s32[2,128]{1,0:T(2,128)S(1)}, s32[2,128]{1,0:T(2,128)S(1)}, u32[]{:S(2)}, u32[]{:S(2)}) collective-permute-start(s32[2,128]{1,0:T(2,128)S(1)} %pad_add_fusion.5), channel_id=1, source_target_pairs={{0,8},{8,0},{16,24},{24,16},{1,9},{9,1},{17,25},{25,17},{2,10},{10... | collective-permute-start | bytes 3080 | tf_op jit(solution)/shard_map/ppermute | solution.py:186
  23.5 1.4 %collective-permute-start.2 = (s32[4,128]{1,0:T(4,128)S(1)}, s32[4,128]{1,0:T(4,128)S(1)}, u32[]{:S(2)}, u32[]{:S(2)}) collective-permute-start(s32[4,128]{1,0:T(4,128)S(1)} %pad_add_fusion.3.refs_1_), channel_id=1, source_target_pairs={{0,1},{1,0},{2,3},{3,2},{4,5},{5,4},{6,7},{7,6},{8,9},{9,8},{10,11... | collective-permute-start | bytes 6152 | tf_op jit(solution)/shard_map/ppermute | solution.py:186
  24.9 2.8 %collective-permute-start.9 = (bf16[128,1152]{1,0:T(8,128)(2,1)}, bf16[128,1152]{1,0:T(8,128)(2,1)S(1)}, u32[]{:S(2)}, u32[]{:S(2)}) collective-permute-start(bf16[128,1152]{1,0:T(8,128)(2,1)} %refs_3_.5), channel_id=1, source_target_pairs={{0,1},{1,0},{2,3},{3,2},{4,5},{5,4},{6,7},{7,6},{8,9},{9,8},{10,11... | collective-permute-start | bytes 884744 | tf_op jit(solution)/shard_map/ppermute | solution.py:186
  25.5 2.4 %collective-permute-start.10 = (bf16[128,1152]{1,0:T(8,128)(2,1)S(1)}, bf16[128,1152]{1,0:T(8,128)(2,1)S(1)}, u32[]{:S(2)}, u32[]{:S(2)}) collective-permute-start(bf16[128,1152]{1,0:T(8,128)(2,1)S(1)} %collective-permute-done.3.refs_7_.refs_4_.refs_8_), channel_id=1, source_target_pairs={{0,1},{1,0},{2,3},{3,2},{4,5},{5,4},{6,7},{7,6},{8,9},{9,8},{10,11... | collective-permute-start | bytes 884744 | tf_op jit(solution)/shard_map/ppermute | solution.py:186
  25.6 2.8 %collective-permute-start.11 = (bf16[128,1152]{1,0:T(8,128)(2,1)S(1)}, bf16[128,1152]{1,0:T(8,128)(2,1)S(1)}, u32[]{:S(2)}, u32[]{:S(2)}) collective-permute-start(bf16[128,1152]{1,0:T(8,128)(2,1)S(1)} %collective-permute-done.4.refs_8_.refs_5_.refs_9_), channel_id=1, source_target_pairs={{0,1},{1,0},{2,3},{3,2},{4,5},{5,4},{6,7},{7,6},{8,9},{9,8},{10,11... | collective-permute-start | bytes 884744 | tf_op jit(solution)/shard_map/ppermute | solution.py:186
  26.0 6.9 %collective-permute-start.12 = (bf16[128,1152]{1,0:T(8,128)(2,1)}, bf16[128,1152]{1,0:T(8,128)(2,1)S(1)}, u32[]{:S(2)}, u32[]{:S(2)}) collective-permute-start(bf16[128,1152]{1,0:T(8,128)(2,1)} %refs_7_.1), channel_id=1, source_target_pairs={{0,1},{1,0},{2,3},{3,2},{4,5},{5,4},{6,7},{7,6},{8,9},{9,8},{10,11... | collective-permute-start | bytes 884744 | tf_op jit(solution)/shard_map/ppermute | solution.py:186
  26.2 9.4 %collective-permute-start.5 = (bf16[128,1152]{1,0:T(8,128)(2,1)S(1)}, bf16[128,1152]{1,0:T(8,128)(2,1)S(1)}, u32[]{:S(2)}, u32[]{:S(2)}) collective-permute-start(bf16[128,1152]{1,0:T(8,128)(2,1)S(1)} %collective-permute-done.3.refs_7_.refs_4_.refs_8_), channel_id=1, source_target_pairs={{0,8},{8,0},{16,24},{24,16},{1,9},{9,1},{17,25},{25,17},{2,10},{10... | collective-permute-start | bytes 884744 | tf_op jit(solution)/shard_map/ppermute | solution.py:186
  27.7 5.3 %collective-permute-start.13 = (bf16[128,1152]{1,0:T(8,128)(2,1)S(1)}, bf16[128,1152]{1,0:T(8,128)(2,1)S(1)}, u32[]{:S(2)}, u32[]{:S(2)}) collective-permute-start(bf16[128,1152]{1,0:T(8,128)(2,1)S(1)} %collective-permute-done.6.refs_4_.refs_7_.refs_8_), channel_id=1, source_target_pairs={{0,1},{1,0},{2,3},{3,2},{4,5},{5,4},{6,7},{7,6},{8,9},{9,8},{10,11... | collective-permute-start | bytes 884744 | tf_op jit(solution)/shard_map/ppermute | solution.py:186
  27.9 9.3 %collective-permute-start.8 = (bf16[128,1152]{1,0:T(8,128)(2,1)S(1)}, bf16[128,1152]{1,0:T(8,128)(2,1)S(1)}, u32[]{:S(2)}, u32[]{:S(2)}) collective-permute-start(bf16[128,1152]{1,0:T(8,128)(2,1)S(1)} %collective-permute-done.6.refs_4_.refs_7_.refs_8_), channel_id=1, source_target_pairs={{0,16},{8,24},{16,0},{24,8},{1,17},{9,25},{17,1},{25,9},{2,18},{10... | collective-permute-start | bytes 884744 | tf_op jit(solution)/shard_map/ppermute | solution.py:186
  28.4 4.6 %collective-permute-start.14 = (bf16[128,1152]{1,0:T(8,128)(2,1)S(1)}, bf16[128,1152]{1,0:T(8,128)(2,1)S(1)}, u32[]{:S(2)}, u32[]{:S(2)}) collective-permute-start(bf16[128,1152]{1,0:T(8,128)(2,1)S(1)} %collective-permute-done.7.refs_5_.refs_8_.refs_9_), channel_id=1, source_target_pairs={{0,1},{1,0},{2,3},{3,2},{4,5},{5,4},{6,7},{7,6},{8,9},{9,8},{10,11... | collective-permute-start | bytes 884744 | tf_op jit(solution)/shard_map/ppermute | solution.py:186
  28.6 1.0 %copy-start = (bf16[128,1152]{1,0:T(8,128)(2,1)S(1)}, bf16[128,1152]{1,0:T(8,128)(2,1)}, u32[]{:S(2)}) copy-start(bf16[128,1152]{1,0:T(8,128)(2,1)} %refs_3_.5) | copy-start | bytes 884740
  29.5 1.0 %copy-start.2 = (bf16[128,1152]{1,0:T(8,128)(2,1)S(1)}, bf16[128,1152]{1,0:T(8,128)(2,1)}, u32[]{:S(2)}) copy-start(bf16[128,1152]{1,0:T(8,128)(2,1)} %refs_7_.1) | copy-start | bytes 884740
  30.5 2.5 %copy-start.1 = (bf16[128,1152]{1,0:T(8,128)(2,1)S(1)}, bf16[128,1152]{1,0:T(8,128)(2,1)}, u32[]{:S(2)}) copy-start(bf16[128,1152]{1,0:T(8,128)(2,1)} %refs_3_.5) | copy-start | bytes 884740
  30.5 2.5 %copy-start.3 = (bf16[128,1152]{1,0:T(8,128)(2,1)S(1)}, bf16[128,1152]{1,0:T(8,128)(2,1)}, u32[]{:S(2)}) copy-start(bf16[128,1152]{1,0:T(8,128)(2,1)} %refs_7_.1) | copy-start | bytes 884740
  37.2 1.6 %collective-permute-start.15 = (bf16[128,1152]{1,0:T(8,128)(2,1)S(1)}, bf16[128,1152]{1,0:T(8,128)(2,1)S(1)}, u32[]{:S(2)}, u32[]{:S(2)}) collective-permute-start(bf16[128,1152]{1,0:T(8,128)(2,1)S(1)} %collective-permute-done.5.refs_10_.refs_6_), channel_id=1, source_target_pairs={{0,1},{1,0},{2,3},{3,2},{4,5},{5,4},{6,7},{7,6},{8,9},{9,8},{10,11... | collective-permute-start | bytes 884744 | tf_op jit(solution)/shard_map/ppermute | solution.py:186
  37.2 5.2 %collective-permute-start.16 = (bf16[128,1152]{1,0:T(8,128)(2,1)S(1)}, bf16[128,1152]{1,0:T(8,128)(2,1)S(1)}, u32[]{:S(2)}, u32[]{:S(2)}) collective-permute-start(bf16[128,1152]{1,0:T(8,128)(2,1)S(1)} %collective-permute-done.8.refs_6_.refs_10_), channel_id=1, source_target_pairs={{0,1},{1,0},{2,3},{3,2},{4,5},{5,4},{6,7},{7,6},{8,9},{9,8},{10,11... | collective-permute-start | bytes 884744 | tf_op jit(solution)/shard_map/ppermute | solution.py:186
  41.8 10.7 %collective-permute-start.21 = (s16[144,1152]{1,0:T(8,128)(2,1)S(1)}, s16[144,1152]{1,0:T(8,128)(2,1)S(1)}, u32[]{:S(2)}, u32[]{:S(2)}) collective-permute-start(s16[144,1152]{1,0:T(8,128)(2,1)S(1)} %get-tuple-element.67), channel_id=1, source_target_pairs={{0,16},{8,24},{16,0},{24,8},{1,17},{9,25},{17,1},{25,9},{2,18},{10... | collective-permute-start | bytes 995336 | tf_op jit(solution)/shard_map/ppermute | solution.py:186
  45.4 10.8 %collective-permute-start.18 = (s16[144,1152]{1,0:T(8,128)(2,1)S(1)}, s16[144,1152]{1,0:T(8,128)(2,1)S(1)}, u32[]{:S(2)}, u32[]{:S(2)}) collective-permute-start(s16[144,1152]{1,0:T(8,128)(2,1)S(1)} %get-tuple-element.63), channel_id=1, source_target_pairs={{0,8},{8,0},{16,24},{24,16},{1,9},{9,1},{17,25},{25,17},{2,10},{10... | collective-permute-start | bytes 995336 | tf_op jit(solution)/shard_map/ppermute | solution.py:186
  46.2 12.5 %collective-permute-start.20 = (s16[144,1152]{1,0:T(8,128)(2,1)S(1)}, s16[144,1152]{1,0:T(8,128)(2,1)S(1)}, u32[]{:S(2)}, u32[]{:S(2)}) collective-permute-start(s16[144,1152]{1,0:T(8,128)(2,1)S(1)} %get-tuple-element.65), channel_id=1, source_target_pairs={{0,16},{8,24},{16,0},{24,8},{1,17},{9,25},{17,1},{25,9},{2,18},{10... | collective-permute-start | bytes 995336 | tf_op jit(solution)/shard_map/ppermute | solution.py:186
  47.8 23.2 %collective-permute-start.17 = (s16[144,1152]{1,0:T(8,128)(2,1)S(1)}, s16[144,1152]{1,0:T(8,128)(2,1)S(1)}, u32[]{:S(2)}, u32[]{:S(2)}) collective-permute-start(s16[144,1152]{1,0:T(8,128)(2,1)S(1)} %get-tuple-element.61), channel_id=1, source_target_pairs={{0,8},{8,0},{16,24},{24,16},{1,9},{9,1},{17,25},{25,17},{2,10},{10... | collective-permute-start | bytes 995336 | tf_op jit(solution)/shard_map/ppermute | solution.py:186
  53.2 16.2 %collective-permute-start.22 = (s16[144,1152]{1,0:T(8,128)(2,1)S(1)}, s16[144,1152]{1,0:T(8,128)(2,1)S(1)}, u32[]{:S(2)}, u32[]{:S(2)}) collective-permute-start(s16[144,1152]{1,0:T(8,128)(2,1)S(1)} %passed_sum.3), channel_id=1, source_target_pairs={{0,4},{1,5},{2,6},{3,7},{4,0},{5,1},{6,2},{7,3},{8,12},{9,13},{10,... | collective-permute-start | bytes 995336 | tf_op jit(solution)/shard_map/ppermute | solution.py:186
  56.9 14.6 %collective-permute-start.19 = (s16[144,1152]{1,0:T(8,128)(2,1)S(1)}, s16[144,1152]{1,0:T(8,128)(2,1)S(1)}, u32[]{:S(2)}, u32[]{:S(2)}) collective-permute-start(s16[144,1152]{1,0:T(8,128)(2,1)S(1)} %passed_sum.2), channel_id=1, source_target_pairs={{0,2},{1,3},{2,0},{3,1},{4,6},{5,7},{6,4},{7,5},{8,10},{9,11},{10,... | collective-permute-start | bytes 995336 | tf_op jit(solution)/shard_map/ppermute | solution.py:186

commit v3 on v2

--- a/solution.py
+++ b/solution.py
@@ -10,7 +10,9 @@
 LOG2E = 1.4426950408889634
 CODE_TOP = 32000.0
 CODE_STEPS = 32.0
-CODE_ROWS = 16
+CODE_ROWS = 8
+LABEL_ROWS = 8
+LABEL_BASE = 128
 TILE = 256
 
 
@@ -32,23 +34,42 @@
     return ref[pl.ds(0, rows), columns].astype(jnp.int32).astype(jnp.float32) * gain
 
 
-def key_column(keys, index):
-    size = keys.shape[1]
-    return jnp.broadcast_to(keys[index : index + 1, :], (size, size)).T
+def keys_of(block, size, first):
+    if block.shape[0] == size:
+        ids = lax.broadcasted_iota(jnp.int32, (1, size), 1) + first
+        return ids.astype(jnp.float32)
+    parts = block[pl.ds(size, LABEL_ROWS), pl.ds(0, size)].astype(jnp.float32)
+    return parts[0:1] * LABEL_BASE + parts[1:2]
+
+
+def labelled(images, labels):
+    size, width = images.shape
+    parts = jnp.stack([labels // LABEL_BASE, labels % LABEL_BASE]).astype(jnp.bfloat16)
+    parts = jnp.pad(parts, ((0, LABEL_ROWS - 2), (0, width - size)))
+    return jnp.concatenate([images, parts])
 
 
 def add_products(refs, rows, columns, before, emit):
-    scalars, row_keys, column_keys, x_parts, y_parts, weights = refs
-    size, width = x_parts[0].shape
+    scalars, row_firsts, column_firsts, x_parts, y_parts, weights = refs
+    width = x_parts[0].shape[1]
+    size = min(x_parts[0].shape[0], y_parts[0].shape[0])
     slope = scalars[0] * LOG2E
     shift = scalars[1] * LOG2E
-    x_all = jnp.concatenate([x_parts[r][...] for r in rows], axis=0)
+    x_all = jnp.concatenate([x_parts[r][pl.ds(0, size), :] for r in rows], axis=0)
     per_tile = TILE // size
-    keys = [jnp.tile(key_column(row_keys, r), (1, per_tile)) for r in rows]
+    keys = [
+        jnp.tile(
+            jnp.broadcast_to(keys_of(x_parts[r], size, row_firsts[r]), (size, size)).T,
+            (1, per_tile),
+        )
+        for r in rows
+    ]
     for n in range(0, len(columns), per_tile):
         tile = columns[n : n + per_tile]
-        y_tile = jnp.concatenate([y_parts[c][...] for c in tile], axis=0)
-        other = jnp.concatenate([column_keys[c : c + 1, :] for c in tile], axis=1)
+        y_tile = jnp.concatenate([y_parts[c][pl.ds(0, size), :] for c in tile], axis=0)
+        other = jnp.concatenate(
+            [keys_of(y_parts[c], size, column_firsts[c]) for c in tile], axis=1
+        )
         scores = lax.dot_general(
             x_all, y_tile, (((1,), (1,)), ((), ())), preferred_element_type=jnp.float32
         )
@@ -60,7 +81,7 @@
     for start in range(0, width, TILE):
         span = min(TILE, width - start)
         part = pl.ds(start, span)
-        y_part = jnp.concatenate([y_parts[c][:, part] for c in columns], axis=0)
+        y_part = jnp.concatenate([y_parts[c][pl.ds(0, size), part] for c in columns], axis=0)
         sums = jnp.dot(
             weights[pl.ds(0, len(rows) * size), pl.ds(0, len(columns) * size)],
             y_part,
@@ -71,8 +92,8 @@
             emit(r, part, block if before is None else before[r][:, part] + block)
 
 
-def gradient_call(kernel, name, scalars, keys, x_parts, y_parts, before, out_shape, pairs):
-    size, width = x_parts[0].shape
+def gradient_call(kernel, name, scalars, firsts, x_parts, y_parts, before, out_shape, pairs):
+    size = min(x_parts[0].shape[0], y_parts[0].shape[0])
     rows, columns, sums = len(x_parts), len(y_parts), len(before)
 
     def body(*refs):
@@ -89,7 +110,7 @@
     return pl.pallas_call(
         body,
         out_shape=out_shape,
-        in_specs=[smem] + [vmem] * (2 + rows + columns + sums),
+        in_specs=[smem] * 3 + [vmem] * (rows + columns + sums),
         out_specs=[vmem] * len(out_shape),
         scratch_shapes=[pltpu.VMEM((rows * size, columns * size), jnp.bfloat16)],
         compiler_params=pltpu.CompilerParams(vmem_limit_bytes=held + 8 * 2**20),
@@ -99,11 +120,11 @@
             transcendentals=0,
         ),
         name=name,
-    )(scalars, *keys, *x_parts, *y_parts, *before)
-
-
-def early_sums(scalars, keys, x_parts, y_parts):
-    size, width = x_parts[0].shape
+    )(scalars, *firsts, *x_parts, *y_parts, *before)
+
+
+def early_sums(scalars, firsts, x_parts, y_parts):
+    size, width = min(x_parts[0].shape[0], y_parts[0].shape[0]), x_parts[0].shape[1]
     rows, columns = list(range(len(x_parts))), list(range(len(y_parts)))
 
     def kernel(refs, _, outs):
@@ -114,12 +135,12 @@
 
     shapes = [jax.ShapeDtypeStruct((size, width), jnp.float32)] * len(rows)
     return gradient_call(
-        kernel, "early_sums", scalars, keys, x_parts, y_parts, [], shapes, len(rows) * len(columns)
-    )
-
-
-def late_sums(scalars, keys, x_parts, y_parts, early_rows, late_columns, before, kept):
-    size, width = x_parts[0].shape
+        kernel, "early_sums", scalars, firsts, x_parts, y_parts, [], shapes, len(rows) * len(columns)
+    )
+
+
+def late_sums(scalars, firsts, x_parts, y_parts, early_rows, late_columns, before, kept):
+    size, width = min(x_parts[0].shape[0], y_parts[0].shape[0]), x_parts[0].shape[1]
     late_rows = [r for r in range(len(x_parts)) if r not in early_rows]
     slot = {r: i for i, r in enumerate(early_rows)}
 
@@ -140,12 +161,12 @@
     shapes = [whole if r < kept else coded for r in range(len(x_parts))]
     pairs = len(late_rows) * len(y_parts) + len(early_rows) * len(late_columns)
     return gradient_call(
-        kernel, "late_sums", scalars, keys, x_parts, y_parts, before, shapes, pairs
-    )
-
-
-def picked(keys, chosen):
-    return jnp.stack([keys[i] for i in chosen])
+        kernel, "late_sums", scalars, firsts, x_parts, y_parts, before, shapes, pairs
+    )
+
+
+def picked(firsts, chosen):
+    return jnp.stack([firsts[i] for i in chosen])
 
 
 def combined(scalars, kept, received, final):
@@ -209,13 +230,12 @@
     return [(axis, 1 << k) for k in range(int(math.log2(lax.axis_size(axis))))]
 
 
-def owner_keys(steps, size):
+def first_rows(steps, size):
     owners = [(lax.axis_index("blk"), lax.axis_index("grp"))]
     for axis, bit in steps:
         owners = owners + [(b ^ bit, g) if axis == "blk" else (b, g ^ bit) for b, g in owners]
     grp_count = lax.axis_size("grp")
-    firsts = jnp.stack([(b * grp_count + g) * size for b, g in owners])
-    return firsts[:, None] + jnp.arange(size, dtype=jnp.int32)[None, :]
+    return [(b * grp_count + g) * size for b, g in owners]
 
 
 def per_device(
@@ -228,12 +248,10 @@
     every = grp_steps + blk_steps
     image_steps, text_steps = every[0::2], every[1::2]
 
-    images = gathered(picture_vectors, image_steps)
+    images = gathered(labelled(picture_vectors, matching_caption), image_steps)
     texts = gathered(caption_vectors, text_steps)
-    labels = matching_caption[None, :]
-    for step in image_steps + [core]:
-        labels = jnp.concatenate([labels, swapped(labels, step)])
-    ids = owner_keys(text_steps + [core], size)
+    image_firsts = first_rows(image_steps + [core], size)
+    text_firsts = first_rows(text_steps + [core], size)
 
     def split(count):
         early = [m for m in range(count) if m <= count // 2]
@@ -250,13 +268,13 @@
 
     text_before = early_sums(
         scalars,
-        (picked(ids, early_texts), picked(labels, columns(early_images, image_count))),
+        (picked(text_firsts, early_texts), picked(image_firsts, columns(early_images, image_count))),
         [texts[m] for m in early_texts],
         [images[m] for m in early_images] + [other_images[m] for m in early_images],
     )
     image_before = early_sums(
         scalars,
-        (picked(labels, early_images), picked(ids, columns(early_texts, text_count))),
+        (picked(image_firsts, early_images), picked(text_firsts, columns(early_texts, text_count))),
         [images[m] for m in early_images],
         [texts[m] for m in early_texts] + [other_texts[m] for m in early_texts],
     )
@@ -267,7 +285,7 @@
     other_texts |= {m: swapped(texts[m], core) for m in late_texts}
     text_parts = late_sums(
         scalars,
-        (ids[:text_count], labels),
+        (jnp.stack(text_firsts[:text_count]), jnp.stack(image_firsts)),
         texts,
         images + [other_images[m] for m in range(image_count)],
         early_texts,
@@ -278,7 +296,7 @@
     text_parts, image_scalars = lax.optimization_barrier((text_parts, scalars))
     image_parts = late_sums(
         image_scalars,
-        (labels[:image_count], ids),
+        (jnp.stack(image_firsts[:image_count]), jnp.stack(text_firsts)),
         images,
         texts + [other_texts[m] for m in range(text_count)],
         early_images,

time: 73.3 us -> 75.9 us (1.035)
  local copies, waits for them, and re-layouts: 2.02 us -> 9.35 us
  waiting for transfers between devices: 32.3 us -> 27.9 us
  starting transfers between devices: 20.9 us -> 16.9 us
  other arithmetic: 0.21 us -> 2.09 us
  Pallas kernels: 15.6 us -> 17.2 us
    unnamed x10 -> x32, local copies, waits for them, and re-layouts: 1.93 us -> 9.01 us
    ppermute x23 -> x20, waiting for transfers between devices: 32.3 us -> 27.9 us  [swapped(): lax.ppermute(block, axis, [(i, i ^ bit) for i in range(lax.axis_size(axis...]
    ppermute x23 -> x20, starting transfers between devices: 20.9 us -> 16.9 us  [swapped(): lax.ppermute(block, axis, [(i, i ^ bit) for i in range(lax.axis_size(axis...]
    pallas_call x4, Pallas kernels: 11 us -> 12.6 us  [gradient_call(): pl.pallas_call(body, out_shape=out_shape, in_specs=[smem] * 3 + [vmem] *...]
    concatenate x3 -> x1, other arithmetic: 0.03 us -> 1.03 us  [labelled(): return jnp.concatenate([images, parts])]
    another operation x3 -> x6, other arithmetic: 0.03 us -> 0.98 us  [the longest x2 0.68 us: labelled(): jnp.stack([labels // LABEL_BASE, labels % LABEL_BASE]).astype(jnp.bfloat16)]
  transfers between devices with their start and end apart: 23 -> 20, of which waited for: 10 -> 7; matrix products, arithmetic and copies ran while one was open for 0% -> 3% of each run, Pallas kernels for 19% -> 21%
where the time goes in v3:
time: 75.9 us; the launch traced here: 75.5 us
  waiting for transfers between devices  27.9 us (37%)
  Pallas kernels  17.2 us (23%)
  starting transfers between devices  16.9 us (22%)
  local copies, waits for them, and re-layouts  9.35 us (12%)
  between operations  2.12 us (3%)
  other arithmetic  2.09 us (3%)
    ppermute x20, waiting for transfers between devices, swapped(): lax.ppermute(block, axis, [(i, i ^ bit) for i in range(lax.axis_size(axis...  27.9 us
    ppermute x20, starting transfers between devices, swapped(): lax.ppermute(block, axis, [(i, i ^ bit) for i in range(lax.axis_size(axis...  16.9 us
    pallas_call x4, Pallas kernels, gradient_call(): pl.pallas_call(body, out_shape=out_shape, in_specs=[smem] * 3 + [vmem] *...  12.6 us
    unnamed x32, local copies, waits for them, and re-layouts  9.01 us
    pallas_call x4, Pallas kernels, combined(): pl.pallas_call(kernel, out_shape=jax.ShapeDtypeStruct(shape, jnp.float32...  4.6 us
  transfers between devices with their start and end apart: 20, of which 7 were waited for; matrix products, arithmetic and copies ran while one was open for 3% of the time, Pallas kernels for 21%

profile of v3, /device:TPU:0, one launch (start us, length us, event | category | flops | bytes accessed | tf_op | source)
XLA Modules:
  0.0 75.5 jit_solution(9931914536446863461)
XLA Ops:
  0.6 4.1 %collective-permute-start.3 = (bf16[128,1152]{1,0:T(8,128)(2,1)}, bf16[128,1152]{1,0:T(8,128)(2,1)S(1)}, u32[]{:S(2)}, u32[]{:S(2)}) collective-permute-start(bf16[128,1152]{1,0:T(8,128)(2,1)} %refs_7_), channel_id=1, source_target_pairs={{0,4},{1,5},{2,6},{3,7},{4,0},{5,1},{6,2},{7,3},{8,12},{9,13},{10,... | collective-permute-start | bytes 884744 | tf_op jit(solution)/shard_map/ppermute | solution.py:207
  4.7 1.5 %collective-permute-start.4 = (bf16[128,1152]{1,0:T(8,128)(2,1)}, bf16[128,1152]{1,0:T(8,128)(2,1)S(1)}, u32[]{:S(2)}, u32[]{:S(2)}) collective-permute-start(bf16[128,1152]{1,0:T(8,128)(2,1)} %refs_7_), channel_id=1, source_target_pairs={{0,16},{8,24},{16,0},{24,8},{1,17},{9,25},{17,1},{25,9},{2,18},{10... | collective-permute-start | bytes 884744 | tf_op jit(solution)/shard_map/ppermute | solution.py:207
  6.3 0.7 convert_bitcast_fusion
  6.9 0.0 copy-start
  6.9 1.0 %pad_maximum_fusion.refs_6_.refs_3_.refs_7_ = bf16[136,1152]{1,0:T(8,128)(2,1)S(1)} fusion(bf16[8,1152]{1,0:T(8,128)(2,1)S(1)} %fusion.5, bf16[128,1152]{1,0:T(8,128)(2,1)} %param.5), kind=kLoop, calls=%fused_computation | loop fusion | flops 626688 | bytes 626688 | tf_op jit(solution)/shard_map/concatenate | solution.py:49
  8.0 1.6 %collective-permute-start = (bf16[136,1152]{1,0:T(8,128)(2,1)S(1)}, bf16[136,1152]{1,0:T(8,128)(2,1)S(1)}, u32[]{:S(2)}, u32[]{:S(2)}) collective-permute-start(bf16[136,1152]{1,0:T(8,128)(2,1)S(1)} %pad_maximum_fusion.refs_6_.refs_3_.refs_7_), channel_id=1, source_target_pairs={{0,2},{1,3},{2,0},{3,1},{4,6},{5,7},{6,4},{7,5},{8,10},{9,11},{10,... | collective-permute-start | bytes 940040 | tf_op jit(solution)/shard_map/ppermute | solution.py:207
  9.6 1.5 %collective-permute-start.1 = (bf16[136,1152]{1,0:T(8,128)(2,1)S(1)}, bf16[136,1152]{1,0:T(8,128)(2,1)S(1)}, u32[]{:S(2)}, u32[]{:S(2)}) collective-permute-start(bf16[136,1152]{1,0:T(8,128)(2,1)S(1)} %pad_maximum_fusion.refs_6_.refs_3_.refs_7_), channel_id=1, source_target_pairs={{0,8},{8,0},{16,24},{24,16},{1,9},{9,1},{17,25},{25,17},{2,10},{10... | collective-permute-start | bytes 940040 | tf_op jit(solution)/shard_map/ppermute | solution.py:207
  11.1 7.3 %collective-permute-done.3.refs_4_.refs_7_.refs_8_ = bf16[128,1152]{1,0:T(8,128)(2,1)S(1)} collective-permute-done((bf16[128,1152]{1,0:T(8,128)(2,1)}, bf16[128,1152]{1,0:T(8,128)(2,1)S(1)}, u32[]{:S(2)}, u32[]{:S(2)}) %collective-permute-start.3) | collective-permute-done | bytes 294944 | tf_op jit(solution)/shard_map/ppermute | solution.py:207
  18.4 0.0 collective-permute-start.10
  18.4 0.0 collective-permute-done.4.refs_5_.refs_8_.refs_9_
  18.4 0.5 collective-permute-start.11
  20.2 0.1 stack.127.refs_2_
  20.3 0.0 collective-permute-start.6
  20.3 1.5 %collective-permute-done.refs_7_.refs_4_.refs_8_ = bf16[136,1152]{1,0:T(8,128)(2,1)S(1)} collective-permute-done((bf16[136,1152]{1,0:T(8,128)(2,1)S(1)}, bf16[136,1152]{1,0:T(8,128)(2,1)S(1)}, u32[]{:S(2)}, u32[]{:S(2)}) %collective-permute-start) | collective-permute-done | bytes 313376 | tf_op jit(solution)/shard_map/ppermute | solution.py:207
  21.8 0.6 collective-permute-start.5
  22.3 0.0 collective-permute-done.1.refs_8_.refs_5_.refs_9_
  22.3 0.0 collective-permute-start.7
  22.3 0.0 collective-permute-done.10.refs_10_.refs_12_
  22.4 0.7 copy-done.1
  23.1 1.5 %collective-permute-start.2 = (bf16[136,1152]{1,0:T(8,128)(2,1)S(1)}, bf16[136,1152]{1,0:T(8,128)(2,1)S(1)}, u32[]{:S(2)}, u32[]{:S(2)}) collective-permute-start(bf16[136,1152]{1,0:T(8,128)(2,1)S(1)} %collective-permute-done.refs_7_.refs_4_.refs_8_), channel_id=1, source_target_pairs={{0,8},{8,0},{16,24},{24,16},{1,9},{9,1},{17,25},{25,17},{2,10},{10... | collective-permute-start | bytes 940040 | tf_op jit(solution)/shard_map/ppermute | solution.py:207
  24.6 0.2 collective-permute-start.8
  24.8 0.1 pad_add_fusion.1.refs_1_
  24.9 0.1 pad_add_fusion.2.refs_1_
  24.9 0.1 pad_maximum_fusion.1.refs_0_.scalars
  25.0 0.1 stack.123.refs_2_
  25.1 1.0 %copy-done.2 = bf16[128,1152]{1,0:T(8,128)(2,1)S(1)} copy-done((bf16[128,1152]{1,0:T(8,128)(2,1)S(1)}, bf16[128,1152]{1,0:T(8,128)(2,1)}, u32[]{:S(2)}) %copy-start.2) | copy-done | bytes 294936
  26.1 2.9 %early_sums.3 = (f32[128,1152]{1,0:T(8,128)S(1)}, f32[128,1152]{1,0:T(8,128)S(1)}, f32[128,1152]{1,0:T(8,128)S(1)}) custom-call(f32[2]{0:T(128)S(1)} %pad_maximum_fusion.1.refs_0_.scalars, s32[3]{0:T(128)S(1)} %pad_add_fusion.2.refs_1_, s32[6]{0:T(128)S(1)} %stack.127.refs_2_, bf16[136,1152]{1,0:T(8,128)(2,1)S(1)} %pad_maximum_fusion.refs_6_.refs_3_.refs_7_, ...), custom_call_target="tpu_custom_call" | custom-call | flops 2304 | bytes 2304 | tf_op jit(solution)/shard_map/early_sums/pallas_call | solution.py:110
  29.0 0.0 copy-start.4
  29.0 0.8 %copy-done.4 = f32[128,1152]{1,0:T(8,128)} copy-done((f32[128,1152]{1,0:T(8,128)}, f32[128,1152]{1,0:T(8,128)S(1)}, u32[]{:S(2)}) %copy-start.4) | copy-done | bytes 589848
  29.8 0.8 %copy-done.6 = f32[128,1152]{1,0:T(8,128)} copy-done((f32[128,1152]{1,0:T(8,128)}, f32[128,1152]{1,0:T(8,128)S(1)}, u32[]{:S(2)}) %copy-start.6) | copy-done | bytes 589848
  30.6 0.0 collective-permute-done.8.refs_11_.refs_13_
  30.6 2.5 %early_sums.2 = (f32[128,1152]{1,0:T(8,128)S(1)}, f32[128,1152]{1,0:T(8,128)S(1)}, f32[128,1152]{1,0:T(8,128)S(1)}) custom-call(f32[2]{0:T(128)S(1)} %pad_maximum_fusion.1.refs_0_.scalars, s32[3]{0:T(128)S(1)} %pad_add_fusion.1.refs_1_, s32[6]{0:T(128)S(1)} %stack.123.refs_2_, bf16[128,1152]{1,0:T(8,128)(2,1)S(1)} %copy-done, ...), custom_call_target="tpu_custom_call" | custom-call | flops 2304 | bytes 2304 | tf_op jit(solution)/shard_map/early_sums/pallas_call | solution.py:110
  33.1 0.8 %copy-done.10 = f32[128,1152]{1,0:T(8,128)} copy-done((f32[128,1152]{1,0:T(8,128)}, f32[128,1152]{1,0:T(8,128)S(1)}, u32[]{:S(2)}) %copy-start.10) | copy-done | bytes 589848
  33.9 0.8 %copy-done.12 = f32[128,1152]{1,0:T(8,128)} copy-done((f32[128,1152]{1,0:T(8,128)}, f32[128,1152]{1,0:T(8,128)S(1)}, u32[]{:S(2)}) %copy-start.12) | copy-done | bytes 589848
  34.8 0.8 %copy-done.14 = f32[128,1152]{1,0:T(8,128)} copy-done((f32[128,1152]{1,0:T(8,128)}, f32[128,1152]{1,0:T(8,128)S(1)}, u32[]{:S(2)}) %copy-start.14) | copy-done | bytes 589848
  35.6 0.0 collective-permute-done.2.refs_10_.refs_6_
  35.6 0.3 collective-permute-start.12
  35.9 0.2 collective-permute-start.13
  36.1 0.1 stack.118.refs_2_
  36.2 0.1 stack.130.refs_2_
  36.3 0.1 pad_add_fusion.refs_1_
  36.4 0.1 pad_add_fusion.3.refs_1_
  36.5 0.0 copy-start.9
  36.5 0.9 %collective-permute-done.12.refs_14_ = bf16[136,1152]{1,0:T(8,128)(2,1)} collective-permute-done((bf16[136,1152]{1,0:T(8,128)(2,1)S(1)}, bf16[136,1152]{1,0:T(8,128)(2,1)}, u32[]{:S(2)}, u32[]{:S(2)}) %collective-permute-start.12) | collective-permute-done | bytes 313376 | tf_op jit(solution)/shard_map/ppermute | solution.py:207
  37.4 1.1 %copy-done.11 = f32[128,1152]{1,0:T(8,128)S(1)} copy-done((f32[128,1152]{1,0:T(8,128)S(1)}, f32[128,1152]{1,0:T(8,128)}, u32[]{:S(2)}) %copy-start.11) | copy-done | bytes 589848
  38.4 1.1 %copy-done.13 = f32[128,1152]{1,0:T(8,128)S(1)} copy-done((f32[128,1152]{1,0:T(8,128)S(1)}, f32[128,1152]{1,0:T(8,128)}, u32[]{:S(2)}) %copy-start.13) | copy-done | bytes 589848
  39.5 1.1 %copy-done.15 = f32[128,1152]{1,0:T(8,128)S(1)} copy-done((f32[128,1152]{1,0:T(8,128)S(1)}, f32[128,1152]{1,0:T(8,128)}, u32[]{:S(2)}) %copy-start.15) | copy-done | bytes 589848
  40.6 3.6 %late_sums.2 = (f32[128,1152]{1,0:T(8,128)S(1)}, f32[128,1152]{1,0:T(8,128)S(1)}, s16[136,1152]{1,0:T(8,128)(2,1)S(1)}, s16[136,1152]{1,0:T(8,128)(2,1)S(1)}) custom-call(f32[2]{0:T(128)S(1)} %pad_maximum_fusion.1.refs_0_.scalars, s32[4]{0:T(128)S(1)} %pad_add_fusion.refs_1_, s32[8]{0:T(128)S(1)} %stack.118.refs_2_, bf16[128,1152]{1,0:T(8,128)(2,1)S(1)} %copy-done, ...), custom_call_target="tpu_custom_call" | custom-call | flops 1792 | bytes 1792 | tf_op jit(solution)/shard_map/late_sums/pallas_call | solution.py:110
  44.1 1.6 %collective-permute-start.18 = (s16[136,1152]{1,0:T(8,128)(2,1)S(1)}, s16[136,1152]{1,0:T(8,128)(2,1)S(1)}, u32[]{:S(2)}, u32[]{:S(2)}) collective-permute-start(s16[136,1152]{1,0:T(8,128)(2,1)S(1)} %get-tuple-element.67), channel_id=1, source_target_pairs={{0,16},{8,24},{16,0},{24,8},{1,17},{9,25},{17,1},{25,9},{2,18},{10... | collective-permute-start | bytes 940040 | tf_op jit(solution)/shard_map/ppermute | solution.py:207
  45.8 3.7 %late_sums.3 = (f32[128,1152]{1,0:T(8,128)S(1)}, f32[128,1152]{1,0:T(8,128)S(1)}, s16[136,1152]{1,0:T(8,128)(2,1)S(1)}, s16[136,1152]{1,0:T(8,128)(2,1)S(1)}) custom-call(f32[2]{0:T(128)S(1)} %pad_maximum_fusion.1.refs_0_.scalars, s32[4]{0:T(128)S(1)} %pad_add_fusion.3.refs_1_, s32[8]{0:T(128)S(1)} %stack.130.refs_2_, ...), custom_call_target="tpu_custom_call" | custom-call | flops 1792 | bytes 1792 | tf_op jit(solution)/shard_map/late_sums/pallas_call | solution.py:110
  49.4 0.5 collective-permute-start.15
  50.0 0.6 collective-permute-start.17
  50.5 1.5 %collective-permute-start.14 = (s16[136,1152]{1,0:T(8,128)(2,1)S(1)}, s16[136,1152]{1,0:T(8,128)(2,1)S(1)}, u32[]{:S(2)}, u32[]{:S(2)}) collective-permute-start(s16[136,1152]{1,0:T(8,128)(2,1)S(1)} %get-tuple-element.61), channel_id=1, source_target_pairs={{0,8},{8,0},{16,24},{24,16},{1,9},{9,1},{17,25},{25,17},{2,10},{10... | collective-permute-start | bytes 940040 | tf_op jit(solution)/shard_map/ppermute | solution.py:207
  52.0 2.4 %collective-permute-done.18.refs_0_ = s16[136,1152]{1,0:T(8,128)(2,1)S(1)} collective-permute-done((s16[136,1152]{1,0:T(8,128)(2,1)S(1)}, s16[136,1152]{1,0:T(8,128)(2,1)S(1)}, u32[]{:S(2)}, u32[]{:S(2)}) %collective-permute-start.18) | collective-permute-done | bytes 313376 | tf_op jit(solution)/shard_map/ppermute | solution.py:207
  54.4 0.7 passed_sum.3
  55.2 0.6 collective-permute-start.19
  55.7 4.0 %collective-permute-done.15.refs_0_ = s16[136,1152]{1,0:T(8,128)(2,1)S(1)} collective-permute-done((s16[136,1152]{1,0:T(8,128)(2,1)S(1)}, s16[136,1152]{1,0:T(8,128)(2,1)S(1)}, u32[]{:S(2)}, u32[]{:S(2)}) %collective-permute-start.15) | collective-permute-done | bytes 313376 | tf_op jit(solution)/shard_map/ppermute | solution.py:207
  59.8 0.7 passed_sum.2
  60.5 0.1 collective-permute-start.16
  60.6 10.5 %collective-permute-done.19.refs_1_ = s16[136,1152]{1,0:T(8,128)(2,1)S(1)} collective-permute-done((s16[136,1152]{1,0:T(8,128)(2,1)S(1)}, s16[136,1152]{1,0:T(8,128)(2,1)S(1)}, u32[]{:S(2)}, u32[]{:S(2)}) %collective-permute-start.19) | collective-permute-done | bytes 313376 | tf_op jit(solution)/shard_map/ppermute | solution.py:207
  71.1 1.6 %output_sum.3 = f32[128,1152]{1,0:T(8,128)} custom-call(f32[2]{0:T(128)S(1)} %pad_maximum_fusion.1.refs_0_.scalars, f32[128,1152]{1,0:T(8,128)S(1)} %get-tuple-element.64.kept, s16[136,1152]{1,0:T(8,128)(2,1)S(1)} %collective-permute-done.17.refs_0_, s16[136,1152]{1,0:T(8,128)(2,1)S(1)} %collective-permute-done.19.refs_1_), custom_call_target="tpu_custom_call" | custom-call | flops 1179648 | bytes 1769472 | tf_op jit(solution)/shard_map/output_sum/pallas_call | solution.py:192
  72.7 0.0 collective-permute-done.14.refs_0_
  72.7 1.3 %collective-permute-done.16.refs_1_ = s16[136,1152]{1,0:T(8,128)(2,1)S(1)} collective-permute-done((s16[136,1152]{1,0:T(8,128)(2,1)S(1)}, s16[136,1152]{1,0:T(8,128)(2,1)S(1)}, u32[]{:S(2)}, u32[]{:S(2)}) %collective-permute-start.16) | collective-permute-done | bytes 313376 | tf_op jit(solution)/shard_map/ppermute | solution.py:207
  74.0 1.6 %output_sum.2 = f32[128,1152]{1,0:T(8,128)} custom-call(f32[2]{0:T(128)S(1)} %pad_maximum_fusion.1.refs_0_.scalars, f32[128,1152]{1,0:T(8,128)S(1)} %get-tuple-element.60.kept, s16[136,1152]{1,0:T(8,128)(2,1)S(1)} %collective-permute-done.14.refs_0_, s16[136,1152]{1,0:T(8,128)(2,1)S(1)} %collective-permute-done.16.refs_1_), custom_call_target="tpu_custom_call" | custom-call | flops 1179648 | bytes 1769472 | tf_op jit(solution)/shard_map/output_sum/pallas_call | solution.py:192
  (28 shorter events, 0.1 us)
Async XLA Ops:
  0.6 17.7 %collective-permute-start.3 = (bf16[128,1152]{1,0:T(8,128)(2,1)}, bf16[128,1152]{1,0:T(8,128)(2,1)S(1)}, u32[]{:S(2)}, u32[]{:S(2)}) collective-permute-start(bf16[128,1152]{1,0:T(8,128)(2,1)} %refs_7_), channel_id=1, source_target_pairs={{0,4},{1,5},{2,6},{3,7},{4,0},{5,1},{6,2},{7,3},{8,12},{9,13},{10,... | collective-permute-start | bytes 884744 | tf_op jit(solution)/shard_map/ppermute | solution.py:207
  4.7 13.7 %collective-permute-start.4 = (bf16[128,1152]{1,0:T(8,128)(2,1)}, bf16[128,1152]{1,0:T(8,128)(2,1)S(1)}, u32[]{:S(2)}, u32[]{:S(2)}) collective-permute-start(bf16[128,1152]{1,0:T(8,128)(2,1)} %refs_7_), channel_id=1, source_target_pairs={{0,16},{8,24},{16,0},{24,8},{1,17},{9,25},{17,1},{25,9},{2,18},{10... | collective-permute-start | bytes 884744 | tf_op jit(solution)/shard_map/ppermute | solution.py:207
  6.9 4.2 %copy-start = (bf16[128,1152]{1,0:T(8,128)(2,1)S(1)}, bf16[128,1152]{1,0:T(8,128)(2,1)}, u32[]{:S(2)}) copy-start(bf16[128,1152]{1,0:T(8,128)(2,1)} %refs_7_) | copy-start | bytes 884740
  8.0 13.8 %collective-permute-start = (bf16[136,1152]{1,0:T(8,128)(2,1)S(1)}, bf16[136,1152]{1,0:T(8,128)(2,1)S(1)}, u32[]{:S(2)}, u32[]{:S(2)}) collective-permute-start(bf16[136,1152]{1,0:T(8,128)(2,1)S(1)} %pad_maximum_fusion.refs_6_.refs_3_.refs_7_), channel_id=1, source_target_pairs={{0,2},{1,3},{2,0},{3,1},{4,6},{5,7},{6,4},{7,5},{8,10},{9,11},{10,... | collective-permute-start | bytes 940040 | tf_op jit(solution)/shard_map/ppermute | solution.py:207
  9.6 12.7 %collective-permute-start.1 = (bf16[136,1152]{1,0:T(8,128)(2,1)S(1)}, bf16[136,1152]{1,0:T(8,128)(2,1)S(1)}, u32[]{:S(2)}, u32[]{:S(2)}) collective-permute-start(bf16[136,1152]{1,0:T(8,128)(2,1)S(1)} %pad_maximum_fusion.refs_6_.refs_3_.refs_7_), channel_id=1, source_target_pairs={{0,8},{8,0},{16,24},{24,16},{1,9},{9,1},{17,25},{25,17},{2,10},{10... | collective-permute-start | bytes 940040 | tf_op jit(solution)/shard_map/ppermute | solution.py:207
  11.1 9.2 %collective-permute-start.9 = (bf16[128,1152]{1,0:T(8,128)(2,1)S(1)}, bf16[128,1152]{1,0:T(8,128)(2,1)S(1)}, u32[]{:S(2)}, u32[]{:S(2)}) collective-permute-start(bf16[128,1152]{1,0:T(8,128)(2,1)S(1)} %copy-done), channel_id=1, source_target_pairs={{0,1},{1,0},{2,3},{3,2},{4,5},{5,4},{6,7},{7,6},{8,9},{9,8},{10,11... | collective-permute-start | bytes 884744 | tf_op jit(solution)/shard_map/ppermute | solution.py:207
  18.4 4.0 %collective-permute-start.10 = (bf16[128,1152]{1,0:T(8,128)(2,1)S(1)}, bf16[128,1152]{1,0:T(8,128)(2,1)S(1)}, u32[]{:S(2)}, u32[]{:S(2)}) collective-permute-start(bf16[128,1152]{1,0:T(8,128)(2,1)S(1)} %collective-permute-done.3.refs_4_.refs_7_.refs_8_), channel_id=1, source_target_pairs={{0,1},{1,0},{2,3},{3,2},{4,5},{5,4},{6,7},{7,6},{8,9},{9,8},{10,11... | collective-permute-start | bytes 884744 | tf_op jit(solution)/shard_map/ppermute | solution.py:207
  18.4 6.2 %collective-permute-start.11 = (bf16[128,1152]{1,0:T(8,128)(2,1)S(1)}, bf16[128,1152]{1,0:T(8,128)(2,1)}, u32[]{:S(2)}, u32[]{:S(2)}) collective-permute-start(bf16[128,1152]{1,0:T(8,128)(2,1)S(1)} %collective-permute-done.4.refs_5_.refs_8_.refs_9_), channel_id=1, source_target_pairs={{0,1},{1,0},{2,3},{3,2},{4,5},{5,4},{6,7},{7,6},{8,9},{9,8},{10,11... | collective-permute-start | bytes 884744 | tf_op jit(solution)/shard_map/ppermute | solution.py:207
  20.3 10.3 %collective-permute-start.6 = (bf16[136,1152]{1,0:T(8,128)(2,1)S(1)}, bf16[136,1152]{1,0:T(8,128)(2,1)S(1)}, u32[]{:S(2)}, u32[]{:S(2)}) collective-permute-start(bf16[136,1152]{1,0:T(8,128)(2,1)S(1)} %pad_maximum_fusion.refs_6_.refs_3_.refs_7_), channel_id=1, source_target_pairs={{0,1},{1,0},{2,3},{3,2},{4,5},{5,4},{6,7},{7,6},{8,9},{9,8},{10,11... | collective-permute-start | bytes 940040 | tf_op jit(solution)/shard_map/ppermute | solution.py:207
  21.8 13.8 %collective-permute-start.5 = (bf16[128,1152]{1,0:T(8,128)(2,1)S(1)}, bf16[128,1152]{1,0:T(8,128)(2,1)}, u32[]{:S(2)}, u32[]{:S(2)}) collective-permute-start(bf16[128,1152]{1,0:T(8,128)(2,1)S(1)} %collective-permute-done.3.refs_4_.refs_7_.refs_8_), channel_id=1, source_target_pairs={{0,16},{8,24},{16,0},{24,8},{1,17},{9,25},{17,1},{25,9},{2,18},{10... | collective-permute-start | bytes 884744 | tf_op jit(solution)/shard_map/ppermute | solution.py:207
  22.3 8.3 %collective-permute-start.7 = (bf16[136,1152]{1,0:T(8,128)(2,1)S(1)}, bf16[136,1152]{1,0:T(8,128)(2,1)S(1)}, u32[]{:S(2)}, u32[]{:S(2)}) collective-permute-start(bf16[136,1152]{1,0:T(8,128)(2,1)S(1)} %collective-permute-done.refs_7_.refs_4_.refs_8_), channel_id=1, source_target_pairs={{0,1},{1,0},{2,3},{3,2},{4,5},{5,4},{6,7},{7,6},{8,9},{9,8},{10,11... | collective-permute-start | bytes 940040 | tf_op jit(solution)/shard_map/ppermute | solution.py:207
  22.4 0.7 copy-start.1
  23.1 12.5 %collective-permute-start.2 = (bf16[136,1152]{1,0:T(8,128)(2,1)S(1)}, bf16[136,1152]{1,0:T(8,128)(2,1)S(1)}, u32[]{:S(2)}, u32[]{:S(2)}) collective-permute-start(bf16[136,1152]{1,0:T(8,128)(2,1)S(1)} %collective-permute-done.refs_7_.refs_4_.refs_8_), channel_id=1, source_target_pairs={{0,8},{8,0},{16,24},{24,16},{1,9},{9,1},{17,25},{25,17},{2,10},{10... | collective-permute-start | bytes 940040 | tf_op jit(solution)/shard_map/ppermute | solution.py:207
  24.6 6.0 %collective-permute-start.8 = (bf16[136,1152]{1,0:T(8,128)(2,1)S(1)}, bf16[136,1152]{1,0:T(8,128)(2,1)S(1)}, u32[]{:S(2)}, u32[]{:S(2)}) collective-permute-start(bf16[136,1152]{1,0:T(8,128)(2,1)S(1)} %collective-permute-done.1.refs_8_.refs_5_.refs_9_), channel_id=1, source_target_pairs={{0,1},{1,0},{2,3},{3,2},{4,5},{5,4},{6,7},{7,6},{8,9},{9,8},{10,11... | collective-permute-start | bytes 940040 | tf_op jit(solution)/shard_map/ppermute | solution.py:207
  25.1 1.0 %copy-start.2 = (bf16[128,1152]{1,0:T(8,128)(2,1)S(1)}, bf16[128,1152]{1,0:T(8,128)(2,1)}, u32[]{:S(2)}) copy-start(bf16[128,1152]{1,0:T(8,128)(2,1)} %copy-done.1) | copy-start | bytes 884740
  29.0 0.8 %copy-start.4 = (f32[128,1152]{1,0:T(8,128)}, f32[128,1152]{1,0:T(8,128)S(1)}, u32[]{:S(2)}) copy-start(f32[128,1152]{1,0:T(8,128)S(1)} %get-tuple-element.57.refs_15_) | copy-start | bytes 1769476
  29.8 0.8 %copy-start.6 = (f32[128,1152]{1,0:T(8,128)}, f32[128,1152]{1,0:T(8,128)S(1)}, u32[]{:S(2)}) copy-start(f32[128,1152]{1,0:T(8,128)S(1)} %get-tuple-element.58.refs_16_) | copy-start | bytes 1769476
  30.6 2.5 %copy-start.8 = (f32[128,1152]{1,0:T(8,128)}, f32[128,1152]{1,0:T(8,128)S(1)}, u32[]{:S(2)}) copy-start(f32[128,1152]{1,0:T(8,128)S(1)} %get-tuple-element.59.refs_17_) | copy-start | bytes 1769476
  33.1 0.8 %copy-start.10 = (f32[128,1152]{1,0:T(8,128)}, f32[128,1152]{1,0:T(8,128)S(1)}, u32[]{:S(2)}) copy-start(f32[128,1152]{1,0:T(8,128)S(1)} %get-tuple-element.49.refs_15_) | copy-start | bytes 1769476
  33.9 0.8 %copy-start.12 = (f32[128,1152]{1,0:T(8,128)}, f32[128,1152]{1,0:T(8,128)S(1)}, u32[]{:S(2)}) copy-start(f32[128,1152]{1,0:T(8,128)S(1)} %get-tuple-element.50.refs_16_) | copy-start | bytes 1769476
  34.8 0.8 %copy-start.14 = (f32[128,1152]{1,0:T(8,128)}, f32[128,1152]{1,0:T(8,128)S(1)}, u32[]{:S(2)}) copy-start(f32[128,1152]{1,0:T(8,128)S(1)} %get-tuple-element.51.refs_17_) | copy-start | bytes 1769476
  35.6 1.7 %collective-permute-start.12 = (bf16[136,1152]{1,0:T(8,128)(2,1)S(1)}, bf16[136,1152]{1,0:T(8,128)(2,1)}, u32[]{:S(2)}, u32[]{:S(2)}) collective-permute-start(bf16[136,1152]{1,0:T(8,128)(2,1)S(1)} %collective-permute-done.2.refs_10_.refs_6_), channel_id=1, source_target_pairs={{0,1},{1,0},{2,3},{3,2},{4,5},{5,4},{6,7},{7,6},{8,9},{9,8},{10,11... | collective-permute-start | bytes 940040 | tf_op jit(solution)/shard_map/ppermute | solution.py:207
  35.9 9.8 %collective-permute-start.13 = (bf16[128,1152]{1,0:T(8,128)(2,1)}, bf16[128,1152]{1,0:T(8,128)(2,1)}, u32[]{:S(2)}, u32[]{:S(2)}) collective-permute-start(bf16[128,1152]{1,0:T(8,128)(2,1)} %collective-permute-done.5.refs_6_.refs_10_), channel_id=1, source_target_pairs={{0,1},{1,0},{2,3},{3,2},{4,5},{5,4},{6,7},{7,6},{8,9},{9,8},{10,11... | collective-permute-start | bytes 884744 | tf_op jit(solution)/shard_map/ppermute | solution.py:207
  36.4 9.3 %copy-start.3 = (bf16[128,1152]{1,0:T(8,128)(2,1)S(1)}, bf16[128,1152]{1,0:T(8,128)(2,1)}, u32[]{:S(2)}) copy-start(bf16[128,1152]{1,0:T(8,128)(2,1)} %copy-done.1) | copy-start | bytes 884740
  36.5 9.3 %copy-start.5 = (f32[128,1152]{1,0:T(8,128)S(1)}, f32[128,1152]{1,0:T(8,128)}, u32[]{:S(2)}) copy-start(f32[128,1152]{1,0:T(8,128)} %copy-done.4) | copy-start | bytes 1769476
  36.5 9.3 %copy-start.7 = (f32[128,1152]{1,0:T(8,128)S(1)}, f32[128,1152]{1,0:T(8,128)}, u32[]{:S(2)}) copy-start(f32[128,1152]{1,0:T(8,128)} %copy-done.6) | copy-start | bytes 1769476
  36.5 9.3 %copy-start.9 = (f32[128,1152]{1,0:T(8,128)S(1)}, f32[128,1152]{1,0:T(8,128)}, u32[]{:S(2)}) copy-start(f32[128,1152]{1,0:T(8,128)} %copy-done.8) | copy-start | bytes 1769476
  37.4 1.1 %copy-start.11 = (f32[128,1152]{1,0:T(8,128)S(1)}, f32[128,1152]{1,0:T(8,128)}, u32[]{:S(2)}) copy-start(f32[128,1152]{1,0:T(8,128)} %copy-done.10) | copy-start | bytes 1769476
  38.4 1.1 %copy-start.13 = (f32[128,1152]{1,0:T(8,128)S(1)}, f32[128,1152]{1,0:T(8,128)}, u32[]{:S(2)}) copy-start(f32[128,1152]{1,0:T(8,128)} %copy-done.12) | copy-start | bytes 1769476
  39.5 1.1 %copy-start.15 = (f32[128,1152]{1,0:T(8,128)S(1)}, f32[128,1152]{1,0:T(8,128)}, u32[]{:S(2)}) copy-start(f32[128,1152]{1,0:T(8,128)} %copy-done.14) | copy-start | bytes 1769476
  44.1 10.3 %collective-permute-start.18 = (s16[136,1152]{1,0:T(8,128)(2,1)S(1)}, s16[136,1152]{1,0:T(8,128)(2,1)S(1)}, u32[]{:S(2)}, u32[]{:S(2)}) collective-permute-start(s16[136,1152]{1,0:T(8,128)(2,1)S(1)} %get-tuple-element.67), channel_id=1, source_target_pairs={{0,16},{8,24},{16,0},{24,8},{1,17},{9,25},{17,1},{25,9},{2,18},{10... | collective-permute-start | bytes 940040 | tf_op jit(solution)/shard_map/ppermute | solution.py:207
  49.4 10.3 %collective-permute-start.15 = (s16[136,1152]{1,0:T(8,128)(2,1)S(1)}, s16[136,1152]{1,0:T(8,128)(2,1)S(1)}, u32[]{:S(2)}, u32[]{:S(2)}) collective-permute-start(s16[136,1152]{1,0:T(8,128)(2,1)S(1)} %get-tuple-element.63), channel_id=1, source_target_pairs={{0,8},{8,0},{16,24},{24,16},{1,9},{9,1},{17,25},{25,17},{2,10},{10... | collective-permute-start | bytes 940040 | tf_op jit(solution)/shard_map/ppermute | solution.py:207
  50.0 10.6 %collective-permute-start.17 = (s16[136,1152]{1,0:T(8,128)(2,1)S(1)}, s16[136,1152]{1,0:T(8,128)(2,1)S(1)}, u32[]{:S(2)}, u32[]{:S(2)}) collective-permute-start(s16[136,1152]{1,0:T(8,128)(2,1)S(1)} %get-tuple-element.65), channel_id=1, source_target_pairs={{0,16},{8,24},{16,0},{24,8},{1,17},{9,25},{17,1},{25,9},{2,18},{10... | collective-permute-start | bytes 940040 | tf_op jit(solution)/shard_map/ppermute | solution.py:207
  50.5 22.1 %collective-permute-start.14 = (s16[136,1152]{1,0:T(8,128)(2,1)S(1)}, s16[136,1152]{1,0:T(8,128)(2,1)S(1)}, u32[]{:S(2)}, u32[]{:S(2)}) collective-permute-start(s16[136,1152]{1,0:T(8,128)(2,1)S(1)} %get-tuple-element.61), channel_id=1, source_target_pairs={{0,8},{8,0},{16,24},{24,16},{1,9},{9,1},{17,25},{25,17},{2,10},{10... | collective-permute-start | bytes 940040 | tf_op jit(solution)/shard_map/ppermute | solution.py:207
  55.2 15.9 %collective-permute-start.19 = (s16[136,1152]{1,0:T(8,128)(2,1)S(1)}, s16[136,1152]{1,0:T(8,128)(2,1)S(1)}, u32[]{:S(2)}, u32[]{:S(2)}) collective-permute-start(s16[136,1152]{1,0:T(8,128)(2,1)S(1)} %passed_sum.3), channel_id=1, source_target_pairs={{0,4},{1,5},{2,6},{3,7},{4,0},{5,1},{6,2},{7,3},{8,12},{9,13},{10,... | collective-permute-start | bytes 940040 | tf_op jit(solution)/shard_map/ppermute | solution.py:207
  60.5 13.4 %collective-permute-start.16 = (s16[136,1152]{1,0:T(8,128)(2,1)S(1)}, s16[136,1152]{1,0:T(8,128)(2,1)S(1)}, u32[]{:S(2)}, u32[]{:S(2)}) collective-permute-start(s16[136,1152]{1,0:T(8,128)(2,1)S(1)} %passed_sum.2), channel_id=1, source_target_pairs={{0,2},{1,3},{2,0},{3,1},{4,6},{5,7},{6,4},{7,5},{8,10},{9,11},{10,... | collective-permute-start | bytes 940040 | tf_op jit(solution)/shard_map/ppermute | solution.py:207

commit v4 on v3

--- a/solution.py
+++ b/solution.py
@@ -34,9 +34,9 @@
     return ref[pl.ds(0, rows), columns].astype(jnp.int32).astype(jnp.float32) * gain
 
 
-def keys_of(block, size, first):
+def keys_of(block, size, mask):
     if block.shape[0] == size:
-        ids = lax.broadcasted_iota(jnp.int32, (1, size), 1) + first
+        ids = lax.broadcasted_iota(jnp.int32, (1, size), 1) + first_row(mask, size)
         return ids.astype(jnp.float32)
     parts = block[pl.ds(size, LABEL_ROWS), pl.ds(0, size)].astype(jnp.float32)
     return parts[0:1] * LABEL_BASE + parts[1:2]
@@ -44,22 +44,45 @@
 
 def labelled(images, labels):
     size, width = images.shape
-    parts = jnp.stack([labels // LABEL_BASE, labels % LABEL_BASE]).astype(jnp.bfloat16)
-    parts = jnp.pad(parts, ((0, LABEL_ROWS - 2), (0, width - size)))
-    return jnp.concatenate([images, parts])
+
+    def kernel(images, labels, out):
+        out[pl.ds(0, size), :] = images[...]
+        out[pl.ds(size, LABEL_ROWS), :] = jnp.zeros((LABEL_ROWS, width), jnp.bfloat16)
+        row = labels[...]
+        low = lax.rem(row, LABEL_BASE)
+        high = lax.div(row, LABEL_BASE)
+        at = lax.broadcasted_iota(jnp.int32, (LABEL_ROWS, size), 0)
+        parts = jnp.where(at == 0, high, jnp.where(at == 1, low, 0))
+        out[pl.ds(size, LABEL_ROWS), pl.ds(0, size)] = parts.astype(jnp.float32).astype(jnp.bfloat16)
+
+    vmem = pl.BlockSpec(memory_space=pltpu.VMEM)
+    return pl.pallas_call(
+        kernel,
+        out_shape=jax.ShapeDtypeStruct((size + LABEL_ROWS, width), jnp.bfloat16),
+        in_specs=[vmem, vmem],
+        out_specs=vmem,
+        compiler_params=pltpu.CompilerParams(vmem_limit_bytes=4 * 2**20),
+        cost_estimate=pl.CostEstimate(flops=size, bytes_accessed=size, transcendentals=0),
+        name="labelled_rows",
+    )(images, labels[None, :])
+
+
+def first_row(mask, size):
+    owner = (lax.axis_index("blk") ^ mask[0]) * lax.axis_size("grp") + (lax.axis_index("grp") ^ mask[1])
+    return owner * size
 
 
 def add_products(refs, rows, columns, before, emit):
-    scalars, row_firsts, column_firsts, x_parts, y_parts, weights = refs
+    scalars, row_masks, column_masks, x_parts, y_parts, weights = refs
     width = x_parts[0].shape[1]
     size = min(x_parts[0].shape[0], y_parts[0].shape[0])
-    slope = scalars[0] * LOG2E
-    shift = scalars[1] * LOG2E
+    slope = scalars[0][0] * LOG2E
+    shift = scalars[1][0] * LOG2E
     x_all = jnp.concatenate([x_parts[r][pl.ds(0, size), :] for r in rows], axis=0)
     per_tile = TILE // size
     keys = [
         jnp.tile(
-            jnp.broadcast_to(keys_of(x_parts[r], size, row_firsts[r]), (size, size)).T,
+            jnp.broadcast_to(keys_of(x_parts[r], size, row_masks[r]), (size, size)).T,
             (1, per_tile),
         )
         for r in rows
@@ -68,7 +91,7 @@
         tile = columns[n : n + per_tile]
         y_tile = jnp.concatenate([y_parts[c][pl.ds(0, size), :] for c in tile], axis=0)
         other = jnp.concatenate(
-            [keys_of(y_parts[c], size, column_firsts[c]) for c in tile], axis=1
+            [keys_of(y_parts[c], size, column_masks[c]) for c in tile], axis=1
         )
         scores = lax.dot_general(
             x_all, y_tile, (((1,), (1,)), ((), ())), preferred_element_type=jnp.float32
@@ -92,15 +115,17 @@
             emit(r, part, block if before is None else before[r][:, part] + block)
 
 
-def gradient_call(kernel, name, scalars, firsts, x_parts, y_parts, before, out_shape, pairs):
+def gradient_call(
+    kernel, name, scalars, masks, x_parts, y_parts, before, out_shape, pairs, after=()
+):
     size = min(x_parts[0].shape[0], y_parts[0].shape[0])
     rows, columns, sums = len(x_parts), len(y_parts), len(before)
 
     def body(*refs):
-        x_refs, refs_left = refs[3 : 3 + rows], refs[3 + rows :]
+        x_refs, refs_left = refs[2 : 2 + rows], refs[2 + rows :]
         y_refs, refs_left = refs_left[:columns], refs_left[columns:]
-        sum_refs, outs = refs_left[:sums], refs_left[sums:-1]
-        kernel((*refs[:3], x_refs, y_refs, refs[-1]), sum_refs, outs)
+        sum_refs, outs = refs_left[:sums], refs_left[sums + len(after) : -1]
+        kernel((refs[:2], *masks, x_refs, y_refs, refs[-1]), sum_refs, outs)
 
     smem = pl.BlockSpec(memory_space=pltpu.SMEM)
     vmem = pl.BlockSpec(memory_space=pltpu.VMEM)
@@ -110,7 +135,9 @@
     return pl.pallas_call(
         body,
         out_shape=out_shape,
-        in_specs=[smem] * 3 + [vmem] * (rows + columns + sums),
+        in_specs=[smem] * 2
+        + [vmem] * (rows + columns + sums)
+        + [pl.BlockSpec(memory_space=pl.ANY)] * len(after),
         out_specs=[vmem] * len(out_shape),
         scratch_shapes=[pltpu.VMEM((rows * size, columns * size), jnp.bfloat16)],
         compiler_params=pltpu.CompilerParams(vmem_limit_bytes=held + 8 * 2**20),
@@ -120,10 +147,10 @@
             transcendentals=0,
         ),
         name=name,
-    )(scalars, *firsts, *x_parts, *y_parts, *before)
-
-
-def early_sums(scalars, firsts, x_parts, y_parts):
+    )(*scalars, *x_parts, *y_parts, *before, *after)
+
+
+def early_sums(scalars, masks, x_parts, y_parts):
     size, width = min(x_parts[0].shape[0], y_parts[0].shape[0]), x_parts[0].shape[1]
     rows, columns = list(range(len(x_parts))), list(range(len(y_parts)))
 
@@ -135,11 +162,13 @@
 
     shapes = [jax.ShapeDtypeStruct((size, width), jnp.float32)] * len(rows)
     return gradient_call(
-        kernel, "early_sums", scalars, firsts, x_parts, y_parts, [], shapes, len(rows) * len(columns)
-    )
-
-
-def late_sums(scalars, firsts, x_parts, y_parts, early_rows, late_columns, before, kept):
+        kernel, "early_sums", scalars, masks, x_parts, y_parts, [], shapes, len(rows) * len(columns)
+    )
+
+
+def late_sums(
+    scalars, masks, x_parts, y_parts, early_rows, late_columns, before, kept, after=()
+):
     size, width = min(x_parts[0].shape[0], y_parts[0].shape[0]), x_parts[0].shape[1]
     late_rows = [r for r in range(len(x_parts)) if r not in early_rows]
     slot = {r: i for i, r in enumerate(early_rows)}
@@ -161,18 +190,14 @@
     shapes = [whole if r < kept else coded for r in range(len(x_parts))]
     pairs = len(late_rows) * len(y_parts) + len(early_rows) * len(late_columns)
     return gradient_call(
-        kernel, "late_sums", scalars, firsts, x_parts, y_parts, before, shapes, pairs
-    )
-
-
-def picked(firsts, chosen):
-    return jnp.stack([firsts[i] for i in chosen])
+        kernel, "late_sums", scalars, masks, x_parts, y_parts, before, shapes, pairs, after
+    )
 
 
 def combined(scalars, kept, received, final):
     size, width = kept.shape
 
-    def kernel(scalars, kept, *refs):
+    def kernel(sharpness, kept, *refs):
         out = refs[-1]
         for start in range(0, width, 128):
             columns = pl.ds(start, 128)
@@ -180,7 +205,7 @@
             for r in refs[:-1]:
                 total = total + decoded(r, size, columns)
             if final:
-                out[:, columns] = total * scalars[0]
+                out[:, columns] = total * sharpness[0]
             else:
                 whole, scales = encoded(total)
                 out[pl.ds(0, size), columns] = whole
@@ -199,7 +224,7 @@
             flops=8 * size * width, bytes_accessed=12 * size * width, transcendentals=0
         ),
         name="output_sum" if final else "passed_sum",
-    )(scalars, kept, *received)
+    )(scalars[0], kept, *received)
 
 
 def swapped(block, step):
@@ -230,19 +255,17 @@
     return [(axis, 1 << k) for k in range(int(math.log2(lax.axis_size(axis))))]
 
 
-def first_rows(steps, size):
-    owners = [(lax.axis_index("blk"), lax.axis_index("grp"))]
+def owner_masks(steps):
+    masks = [(0, 0)]
     for axis, bit in steps:
-        owners = owners + [(b ^ bit, g) if axis == "blk" else (b, g ^ bit) for b, g in owners]
-    grp_count = lax.axis_size("grp")
-    return [(b * grp_count + g) * size for b, g in owners]
+        masks = masks + [(b ^ bit, g) if axis == "blk" else (b, g ^ bit) for b, g in masks]
+    return masks
 
 
 def per_device(
     picture_vectors, caption_vectors, matching_caption, sharpness_parameter, additive_intercept
 ):
-    size = picture_vectors.shape[0]
-    scalars = jnp.concatenate([sharpness_parameter, additive_intercept])
+    scalars = (sharpness_parameter, additive_intercept)
     core, *grp_steps = bit_steps("grp")
     blk_steps = bit_steps("blk")
     every = grp_steps + blk_steps
@@ -250,8 +273,8 @@
 
     images = gathered(labelled(picture_vectors, matching_caption), image_steps)
     texts = gathered(caption_vectors, text_steps)
-    image_firsts = first_rows(image_steps + [core], size)
-    text_firsts = first_rows(text_steps + [core], size)
+    image_masks = owner_masks(image_steps + [core])
+    text_masks = owner_masks(text_steps + [core])
 
     def split(count):
         early = [m for m in range(count) if m <= count // 2]
@@ -263,18 +286,21 @@
     other_images = {m: swapped(images[m], core) for m in early_images}
     other_texts = {m: swapped(texts[m], core) for m in early_texts}
 
+    def picked(masks, chosen):
+        return [masks[i] for i in chosen]
+
     def columns(chosen, count):
         return chosen + [count + m for m in chosen]
 
     text_before = early_sums(
         scalars,
-        (picked(text_firsts, early_texts), picked(image_firsts, columns(early_images, image_count))),
+        (picked(text_masks, early_texts), picked(image_masks, columns(early_images, image_count))),
         [texts[m] for m in early_texts],
         [images[m] for m in early_images] + [other_images[m] for m in early_images],
     )
     image_before = early_sums(
         scalars,
-        (picked(image_firsts, early_images), picked(text_firsts, columns(early_texts, text_count))),
+        (picked(image_masks, early_images), picked(text_masks, columns(early_texts, text_count))),
         [images[m] for m in early_images],
         [texts[m] for m in early_texts] + [other_texts[m] for m in early_texts],
     )
@@ -285,7 +311,7 @@
     other_texts |= {m: swapped(texts[m], core) for m in late_texts}
     text_parts = late_sums(
         scalars,
-        (jnp.stack(text_firsts[:text_count]), jnp.stack(image_firsts)),
+        (text_masks, image_masks),
         texts,
         images + [other_images[m] for m in range(image_count)],
         early_texts,
@@ -293,16 +319,16 @@
         text_before,
         text_count // 2,
     )
-    text_parts, image_scalars = lax.optimization_barrier((text_parts, scalars))
     image_parts = late_sums(
-        image_scalars,
-        (jnp.stack(image_firsts[:image_count]), jnp.stack(text_firsts)),
+        scalars,
+        (image_masks, text_masks),
         images,
         texts + [other_texts[m] for m in range(text_count)],
         early_images,
         columns(late_texts, text_count),
         image_before,
         image_count // 2,
+        text_parts[-1:],
     )
     picture_derivative = scattered_sum(scalars, image_parts, image_steps)
     text_grad = scattered_sum(scalars, text_parts, text_steps)

time: 75.9 us -> 64.7 us (0.85)
  local copies, waits for them, and re-layouts: 9.35 us -> 0.97 us
  Pallas kernels: 17.2 us -> 11.4 us
  waiting for transfers between devices: 27.9 us -> 32.6 us
  other arithmetic: 2.09 us -> 0 us
    unnamed x32 -> x6, local copies, waits for them, and re-layouts: 9.01 us -> 0.97 us
    ppermute x20, waiting for transfers between devices: 27.9 us -> 32.6 us  [swapped(): lax.ppermute(block, axis, [(i, i ^ bit) for i in range(lax.axis_size(axis...]
    pallas_call x4 -> x5, Pallas kernels: 12.6 us -> 8.94 us  [the longest x4 8.91 us: gradient_call(): pl.pallas_call(body, out_shape=out_shape, in_specs=[smem] * 2 + [vmem] *...]
    pallas_call x4, Pallas kernels: 4.6 us -> 2.42 us  [combined(): pl.pallas_call(kernel, out_shape=jax.ShapeDtypeStruct(shape, jnp.float32...]
    concatenate x2 -> x0, other arithmetic: 1.11 us -> none  [the longest x1 1.03 us: labelled(): return jnp.concatenate([images, parts])]
    another operation x6 -> x0, other arithmetic: 0.98 us -> none  [the longest x2 0.68 us: labelled(): jnp.stack([labels // LABEL_BASE, labels % LABEL_BASE]).astype(jnp.bfloat16)]
  transfers between devices with their start and end apart: 20 -> 20, of which waited for: 7 -> 9; matrix products, arithmetic and copies ran while one was open for 3% -> 0% of each run, Pallas kernels for 21% -> 16%
where the time goes in v4:
time: 64.7 us; the launch traced here: 64.5 us
  waiting for transfers between devices  32.6 us (50%)
  starting transfers between devices  17.5 us (27%)
  Pallas kernels  11.4 us (18%)
  between operations  2.02 us (3%)
  local copies, waits for them, and re-layouts  0.97 us (1%)
    ppermute x20, waiting for transfers between devices, swapped(): lax.ppermute(block, axis, [(i, i ^ bit) for i in range(lax.axis_size(axis...  32.6 us
    ppermute x20, starting transfers between devices, swapped(): lax.ppermute(block, axis, [(i, i ^ bit) for i in range(lax.axis_size(axis...  17.5 us
    pallas_call x4, Pallas kernels, gradient_call(): pl.pallas_call(body, out_shape=out_shape, in_specs=[smem] * 2 + [vmem] *...  8.91 us
    pallas_call x4, Pallas kernels, combined(): pl.pallas_call(kernel, out_shape=jax.ShapeDtypeStruct(shape, jnp.float32...  2.42 us
  transfers between devices with their start and end apart: 20, of which 9 were waited for; matrix products, arithmetic and copies ran while one was open for 0% of the time, Pallas kernels for 16%

profile of v4, /device:TPU:0, one launch (start us, length us, event | category | flops | bytes accessed | tf_op | source)
XLA Modules:
  0.0 64.5 jit_solution(12017735777528935986)
XLA Ops:
  0.6 0.0 copy-start.2
  0.6 4.1 %collective-permute-start.3 = (bf16[128,1152]{1,0:T(8,128)(2,1)}, bf16[128,1152]{1,0:T(8,128)(2,1)S(1)}, u32[]{:S(2)}, u32[]{:S(2)}) collective-permute-start(bf16[128,1152]{1,0:T(8,128)(2,1)} %refs_6_), channel_id=1, source_target_pairs={{0,4},{1,5},{2,6},{3,7},{4,0},{5,1},{6,2},{7,3},{8,12},{9,13},{10,... | collective-permute-start | bytes 884744 | tf_op jit(solution)/shard_map/ppermute | solution.py:232
  4.7 1.5 %collective-permute-start.4 = (bf16[128,1152]{1,0:T(8,128)(2,1)}, bf16[128,1152]{1,0:T(8,128)(2,1)S(1)}, u32[]{:S(2)}, u32[]{:S(2)}) collective-permute-start(bf16[128,1152]{1,0:T(8,128)(2,1)} %refs_6_), channel_id=1, source_target_pairs={{0,16},{8,24},{16,0},{24,8},{1,17},{9,25},{17,1},{25,9},{2,18},{10... | collective-permute-start | bytes 884744 | tf_op jit(solution)/shard_map/ppermute | solution.py:232
  6.3 0.0 copy-done.2
  6.3 0.0 copy-start.1
  6.3 1.0 %copy-done.1 = bf16[128,1152]{1,0:T(8,128)(2,1)S(1)} copy-done((bf16[128,1152]{1,0:T(8,128)(2,1)S(1)}, bf16[128,1152]{1,0:T(8,128)(2,1)}, u32[]{:S(2)}) %copy-start.1) | copy-done | bytes 294936
  7.2 0.0 copy-start
  7.3 1.6 %collective-permute-start = (bf16[136,1152]{1,0:T(8,128)(2,1)S(1)}, bf16[136,1152]{1,0:T(8,128)(2,1)S(1)}, u32[]{:S(2)}, u32[]{:S(2)}) collective-permute-start(bf16[136,1152]{1,0:T(8,128)(2,1)S(1)} %labelled_rows.1.refs_5_.refs_2_.refs_6_), channel_id=1, source_target_pairs={{0,2},{1,3},{2,0},{3,1},{4,6},{5,7},{6,4},{7,5},{8,10},{9,11},{10,... | collective-permute-start | bytes 940040 | tf_op jit(solution)/shard_map/ppermute | solution.py:232
  8.9 1.5 %collective-permute-start.1 = (bf16[136,1152]{1,0:T(8,128)(2,1)S(1)}, bf16[136,1152]{1,0:T(8,128)(2,1)S(1)}, u32[]{:S(2)}, u32[]{:S(2)}) collective-permute-start(bf16[136,1152]{1,0:T(8,128)(2,1)S(1)} %labelled_rows.1.refs_5_.refs_2_.refs_6_), channel_id=1, source_target_pairs={{0,8},{8,0},{16,24},{24,16},{1,9},{9,1},{17,25},{25,17},{2,10},{10... | collective-permute-start | bytes 940040 | tf_op jit(solution)/shard_map/ppermute | solution.py:232
  10.4 0.0 copy-done
  10.4 0.0 collective-permute-start.9
  10.4 8.0 %collective-permute-done.3.refs_3_.refs_6_.refs_7_ = bf16[128,1152]{1,0:T(8,128)(2,1)S(1)} collective-permute-done((bf16[128,1152]{1,0:T(8,128)(2,1)}, bf16[128,1152]{1,0:T(8,128)(2,1)S(1)}, u32[]{:S(2)}, u32[]{:S(2)}) %collective-permute-start.3) | collective-permute-done | bytes 294944 | tf_op jit(solution)/shard_map/ppermute | solution.py:232
  18.4 0.0 collective-permute-start.10
  18.4 0.0 collective-permute-done.4.refs_4_.refs_7_.refs_8_
  18.4 0.5 collective-permute-start.11
  18.9 0.0 collective-permute-done.9.refs_8_.refs_10_
  18.9 0.1 collective-permute-start.6
  19.0 2.1 %collective-permute-done.refs_6_.refs_3_.refs_7_ = bf16[136,1152]{1,0:T(8,128)(2,1)S(1)} collective-permute-done((bf16[136,1152]{1,0:T(8,128)(2,1)S(1)}, bf16[136,1152]{1,0:T(8,128)(2,1)S(1)}, u32[]{:S(2)}, u32[]{:S(2)}) %collective-permute-start) | collective-permute-done | bytes 313376 | tf_op jit(solution)/shard_map/ppermute | solution.py:232
  21.1 0.0 collective-permute-start.7
  21.1 0.0 collective-permute-done.1.refs_7_.refs_4_.refs_8_
  21.1 0.5 collective-permute-start.8
  21.6 0.0 collective-permute-done.10.refs_9_.refs_11_
  21.6 1.5 %collective-permute-start.2 = (bf16[136,1152]{1,0:T(8,128)(2,1)S(1)}, bf16[136,1152]{1,0:T(8,128)(2,1)S(1)}, u32[]{:S(2)}, u32[]{:S(2)}) collective-permute-start(bf16[136,1152]{1,0:T(8,128)(2,1)S(1)} %collective-permute-done.refs_6_.refs_3_.refs_7_), channel_id=1, source_target_pairs={{0,8},{8,0},{16,24},{24,16},{1,9},{9,1},{17,25},{25,17},{2,10},{10... | collective-permute-start | bytes 940040 | tf_op jit(solution)/shard_map/ppermute | solution.py:232
  23.1 0.0 collective-permute-done.11.refs_10_.refs_12_
  23.1 0.5 collective-permute-start.5
  24.9 1.9 %early_sums.3 = (f32[128,1152]{1,0:T(8,128)S(1)}, f32[128,1152]{1,0:T(8,128)S(1)}, f32[128,1152]{1,0:T(8,128)S(1)}) custom-call(f32[1]{0:T(128)S(6)} %copy.7.refs_0_.sharpness, f32[1]{0:T(128)S(6)} %copy.8.refs_1_, bf16[136,1152]{1,0:T(8,128)(2,1)S(1)} %labelled_rows.1.refs_5_.refs_2_.refs_6_, ...), custom_call_target="tpu_custom_call" | custom-call | flops 2304 | bytes 2304 | tf_op jit(solution)/shard_map/early_sums/pallas_call | solution.py:135
  26.9 0.0 collective-permute-done.6.refs_8_.refs_10_
  26.9 0.0 collective-permute-done.7.refs_9_.refs_11_
  26.9 0.0 collective-permute-done.8.refs_10_.refs_12_
  26.9 1.9 %early_sums.2 = (f32[128,1152]{1,0:T(8,128)S(1)}, f32[128,1152]{1,0:T(8,128)S(1)}, f32[128,1152]{1,0:T(8,128)S(1)}) custom-call(f32[1]{0:T(128)S(6)} %copy.7.refs_0_.sharpness, f32[1]{0:T(128)S(6)} %copy.8.refs_1_, bf16[128,1152]{1,0:T(8,128)(2,1)S(1)} %copy-done, bf16[128,1152]{1,0:T(8,128)(2,1)S(1)} %collective-permute-done.3.refs_3_.refs_6_.refs_7_, ...), custom_call_target="tpu_custom_call" | custom-call | flops 2304 | bytes 2304 | tf_op jit(solution)/shard_map/early_sums/pallas_call | solution.py:135
  28.8 3.0 %collective-permute-done.5.refs_5_.refs_9_ = bf16[128,1152]{1,0:T(8,128)(2,1)S(1)} collective-permute-done((bf16[128,1152]{1,0:T(8,128)(2,1)S(1)}, bf16[128,1152]{1,0:T(8,128)(2,1)S(1)}, u32[]{:S(2)}, u32[]{:S(2)}) %collective-permute-start.5) | collective-permute-done | bytes 294944 | tf_op jit(solution)/shard_map/ppermute | solution.py:232
  31.8 0.0 collective-permute-done.2.refs_9_.refs_5_
  31.8 0.0 collective-permute-start.13
  31.8 0.5 collective-permute-start.12
  32.3 1.1 %collective-permute-done.13.refs_13_ = bf16[136,1152]{1,0:T(8,128)(2,1)S(1)} collective-permute-done((bf16[136,1152]{1,0:T(8,128)(2,1)S(1)}, bf16[136,1152]{1,0:T(8,128)(2,1)S(1)}, u32[]{:S(2)}, u32[]{:S(2)}) %collective-permute-start.13) | collective-permute-done | bytes 313376 | tf_op jit(solution)/shard_map/ppermute | solution.py:232
  33.4 2.5 %late_sums.2 = (f32[128,1152]{1,0:T(8,128)S(1)}, f32[128,1152]{1,0:T(8,128)S(1)}, s16[136,1152]{1,0:T(8,128)(2,1)S(1)}, s16[136,1152]{1,0:T(8,128)(2,1)S(1)}) custom-call(f32[1]{0:T(128)S(6)} %copy.7.refs_0_.sharpness, f32[1]{0:T(128)S(6)} %copy.8.refs_1_, bf16[128,1152]{1,0:T(8,128)(2,1)S(1)} %copy-done, ...), custom_call_target="tpu_custom_call" | custom-call | flops 1792 | bytes 1792 | tf_op jit(solution)/shard_map/late_sums/pallas_call | solution.py:135
  36.0 0.6 collective-permute-start.18
  36.6 0.0 collective-permute-done.12.refs_13_
  36.6 2.5 %late_sums.3 = (f32[128,1152]{1,0:T(8,128)S(1)}, f32[128,1152]{1,0:T(8,128)S(1)}, s16[136,1152]{1,0:T(8,128)(2,1)S(1)}, s16[136,1152]{1,0:T(8,128)(2,1)S(1)}) custom-call(f32[1]{0:T(128)S(6)} %copy.7.refs_0_.sharpness, f32[1]{0:T(128)S(6)} %copy.8.refs_1_, bf16[136,1152]{1,0:T(8,128)(2,1)S(1)} %labelled_rows.1.refs_5_.refs_2_.refs_6_, ...), custom_call_target="tpu_custom_call" | custom-call | flops 1792 | bytes 1792 | tf_op jit(solution)/shard_map/late_sums/pallas_call | solution.py:135
  39.1 0.7 %collective-permute-start.15 = (s16[136,1152]{1,0:T(8,128)(2,1)S(1)}, s16[136,1152]{1,0:T(8,128)(2,1)S(1)}, u32[]{:S(2)}, u32[]{:S(2)}) collective-permute-start(s16[136,1152]{1,0:T(8,128)(2,1)S(1)} %get-tuple-element.54), channel_id=1, source_target_pairs={{0,8},{8,0},{16,24},{24,16},{1,9},{9,1},{17,25},{25,17},{2,10},{10... | collective-permute-start | bytes 940040 | tf_op jit(solution)/shard_map/ppermute | solution.py:232
  39.8 1.5 %collective-permute-start.17 = (s16[136,1152]{1,0:T(8,128)(2,1)S(1)}, s16[136,1152]{1,0:T(8,128)(2,1)S(1)}, u32[]{:S(2)}, u32[]{:S(2)}) collective-permute-start(s16[136,1152]{1,0:T(8,128)(2,1)S(1)} %get-tuple-element.56), channel_id=1, source_target_pairs={{0,16},{8,24},{16,0},{24,8},{1,17},{9,25},{17,1},{25,9},{2,18},{10... | collective-permute-start | bytes 940040 | tf_op jit(solution)/shard_map/ppermute | solution.py:232
  41.3 1.4 %collective-permute-start.14 = (s16[136,1152]{1,0:T(8,128)(2,1)S(1)}, s16[136,1152]{1,0:T(8,128)(2,1)S(1)}, u32[]{:S(2)}, u32[]{:S(2)}) collective-permute-start(s16[136,1152]{1,0:T(8,128)(2,1)S(1)} %get-tuple-element.52), channel_id=1, source_target_pairs={{0,8},{8,0},{16,24},{24,16},{1,9},{9,1},{17,25},{25,17},{2,10},{10... | collective-permute-start | bytes 940040 | tf_op jit(solution)/shard_map/ppermute | solution.py:232
  42.7 3.6 %collective-permute-done.18.refs_0_ = s16[136,1152]{1,0:T(8,128)(2,1)S(1)} collective-permute-done((s16[136,1152]{1,0:T(8,128)(2,1)S(1)}, s16[136,1152]{1,0:T(8,128)(2,1)S(1)}, u32[]{:S(2)}, u32[]{:S(2)}) %collective-permute-start.18) | collective-permute-done | bytes 313376 | tf_op jit(solution)/shard_map/ppermute | solution.py:232
  46.3 0.2 passed_sum.3
  46.5 0.5 collective-permute-start.19
  47.0 2.4 %collective-permute-done.15.refs_0_ = s16[136,1152]{1,0:T(8,128)(2,1)S(1)} collective-permute-done((s16[136,1152]{1,0:T(8,128)(2,1)S(1)}, s16[136,1152]{1,0:T(8,128)(2,1)S(1)}, u32[]{:S(2)}, u32[]{:S(2)}) %collective-permute-start.15) | collective-permute-done | bytes 313376 | tf_op jit(solution)/shard_map/ppermute | solution.py:232
  49.4 0.2 passed_sum.2
  49.7 0.4 collective-permute-start.16
  50.1 2.1 %collective-permute-done.17.refs_0_ = s16[136,1152]{1,0:T(8,128)(2,1)S(1)} collective-permute-done((s16[136,1152]{1,0:T(8,128)(2,1)S(1)}, s16[136,1152]{1,0:T(8,128)(2,1)S(1)}, u32[]{:S(2)}, u32[]{:S(2)}) %collective-permute-start.17) | collective-permute-done | bytes 313376 | tf_op jit(solution)/shard_map/ppermute | solution.py:232
  52.2 9.6 %collective-permute-done.19.refs_1_ = s16[136,1152]{1,0:T(8,128)(2,1)S(1)} collective-permute-done((s16[136,1152]{1,0:T(8,128)(2,1)S(1)}, s16[136,1152]{1,0:T(8,128)(2,1)S(1)}, u32[]{:S(2)}, u32[]{:S(2)}) %collective-permute-start.19) | collective-permute-done | bytes 313376 | tf_op jit(solution)/shard_map/ppermute | solution.py:232
  61.8 1.0 %output_sum.3 = f32[128,1152]{1,0:T(8,128)} custom-call(f32[1]{0:T(128)S(6)} %copy.7.refs_0_.sharpness, f32[128,1152]{1,0:T(8,128)S(1)} %get-tuple-element.55.kept, s16[136,1152]{1,0:T(8,128)(2,1)S(1)} %collective-permute-done.17.refs_0_, s16[136,1152]{1,0:T(8,128)(2,1)S(1)} %collective-permute-done.19.refs_1_), custom_call_target="tpu_custom_call" | custom-call | flops 1179648 | bytes 1769472 | tf_op jit(solution)/shard_map/output_sum/pallas_call | solution.py:217
  62.9 0.0 collective-permute-done.14.refs_0_
  62.9 0.6 collective-permute-done.16.refs_1_
  63.5 1.0 %output_sum.2 = f32[128,1152]{1,0:T(8,128)} custom-call(f32[1]{0:T(128)S(6)} %copy.7.refs_0_.sharpness, f32[128,1152]{1,0:T(8,128)S(1)} %get-tuple-element.51.kept, s16[136,1152]{1,0:T(8,128)(2,1)S(1)} %collective-permute-done.14.refs_0_, s16[136,1152]{1,0:T(8,128)(2,1)S(1)} %collective-permute-done.16.refs_1_), custom_call_target="tpu_custom_call" | custom-call | flops 1179648 | bytes 1769472 | tf_op jit(solution)/shard_map/output_sum/pallas_call | solution.py:217
  (1 shorter events, 0.0 us)
Async XLA Ops:
  0.6 5.6 %copy-start.2 = (s32[128]{0:T(128)S(1)}, s32[128]{0:T(128)}, u32[]{:S(2)}) copy-start(s32[128]{0:T(128)} %param.7) | copy-start | bytes 1540
  0.6 17.7 %collective-permute-start.3 = (bf16[128,1152]{1,0:T(8,128)(2,1)}, bf16[128,1152]{1,0:T(8,128)(2,1)S(1)}, u32[]{:S(2)}, u32[]{:S(2)}) collective-permute-start(bf16[128,1152]{1,0:T(8,128)(2,1)} %refs_6_), channel_id=1, source_target_pairs={{0,4},{1,5},{2,6},{3,7},{4,0},{5,1},{6,2},{7,3},{8,12},{9,13},{10,... | collective-permute-start | bytes 884744 | tf_op jit(solution)/shard_map/ppermute | solution.py:232
  4.7 13.6 %collective-permute-start.4 = (bf16[128,1152]{1,0:T(8,128)(2,1)}, bf16[128,1152]{1,0:T(8,128)(2,1)S(1)}, u32[]{:S(2)}, u32[]{:S(2)}) collective-permute-start(bf16[128,1152]{1,0:T(8,128)(2,1)} %refs_6_), channel_id=1, source_target_pairs={{0,16},{8,24},{16,0},{24,8},{1,17},{9,25},{17,1},{25,9},{2,18},{10... | collective-permute-start | bytes 884744 | tf_op jit(solution)/shard_map/ppermute | solution.py:232
  6.3 1.0 %copy-start.1 = (bf16[128,1152]{1,0:T(8,128)(2,1)S(1)}, bf16[128,1152]{1,0:T(8,128)(2,1)}, u32[]{:S(2)}) copy-start(bf16[128,1152]{1,0:T(8,128)(2,1)} %images.1) | copy-start | bytes 884740
  7.2 3.2 %copy-start = (bf16[128,1152]{1,0:T(8,128)(2,1)S(1)}, bf16[128,1152]{1,0:T(8,128)(2,1)}, u32[]{:S(2)}) copy-start(bf16[128,1152]{1,0:T(8,128)(2,1)} %refs_6_) | copy-start | bytes 884740
  7.3 13.8 %collective-permute-start = (bf16[136,1152]{1,0:T(8,128)(2,1)S(1)}, bf16[136,1152]{1,0:T(8,128)(2,1)S(1)}, u32[]{:S(2)}, u32[]{:S(2)}) collective-permute-start(bf16[136,1152]{1,0:T(8,128)(2,1)S(1)} %labelled_rows.1.refs_5_.refs_2_.refs_6_), channel_id=1, source_target_pairs={{0,2},{1,3},{2,0},{3,1},{4,6},{5,7},{6,4},{7,5},{8,10},{9,11},{10,... | collective-permute-start | bytes 940040 | tf_op jit(solution)/shard_map/ppermute | solution.py:232
  8.9 12.2 %collective-permute-start.1 = (bf16[136,1152]{1,0:T(8,128)(2,1)S(1)}, bf16[136,1152]{1,0:T(8,128)(2,1)S(1)}, u32[]{:S(2)}, u32[]{:S(2)}) collective-permute-start(bf16[136,1152]{1,0:T(8,128)(2,1)S(1)} %labelled_rows.1.refs_5_.refs_2_.refs_6_), channel_id=1, source_target_pairs={{0,8},{8,0},{16,24},{24,16},{1,9},{9,1},{17,25},{25,17},{2,10},{10... | collective-permute-start | bytes 940040 | tf_op jit(solution)/shard_map/ppermute | solution.py:232
  10.4 8.5 %collective-permute-start.9 = (bf16[128,1152]{1,0:T(8,128)(2,1)S(1)}, bf16[128,1152]{1,0:T(8,128)(2,1)S(1)}, u32[]{:S(2)}, u32[]{:S(2)}) collective-permute-start(bf16[128,1152]{1,0:T(8,128)(2,1)S(1)} %copy-done), channel_id=1, source_target_pairs={{0,1},{1,0},{2,3},{3,2},{4,5},{5,4},{6,7},{7,6},{8,9},{9,8},{10,11... | collective-permute-start | bytes 884744 | tf_op jit(solution)/shard_map/ppermute | solution.py:232
  18.4 3.2 %collective-permute-start.10 = (bf16[128,1152]{1,0:T(8,128)(2,1)S(1)}, bf16[128,1152]{1,0:T(8,128)(2,1)S(1)}, u32[]{:S(2)}, u32[]{:S(2)}) collective-permute-start(bf16[128,1152]{1,0:T(8,128)(2,1)S(1)} %collective-permute-done.3.refs_3_.refs_6_.refs_7_), channel_id=1, source_target_pairs={{0,1},{1,0},{2,3},{3,2},{4,5},{5,4},{6,7},{7,6},{8,9},{9,8},{10,11... | collective-permute-start | bytes 884744 | tf_op jit(solution)/shard_map/ppermute | solution.py:232
  18.4 4.7 %collective-permute-start.11 = (bf16[128,1152]{1,0:T(8,128)(2,1)S(1)}, bf16[128,1152]{1,0:T(8,128)(2,1)S(1)}, u32[]{:S(2)}, u32[]{:S(2)}) collective-permute-start(bf16[128,1152]{1,0:T(8,128)(2,1)S(1)} %collective-permute-done.4.refs_4_.refs_7_.refs_8_), channel_id=1, source_target_pairs={{0,1},{1,0},{2,3},{3,2},{4,5},{5,4},{6,7},{7,6},{8,9},{9,8},{10,11... | collective-permute-start | bytes 884744 | tf_op jit(solution)/shard_map/ppermute | solution.py:232
  18.9 8.0 %collective-permute-start.6 = (bf16[136,1152]{1,0:T(8,128)(2,1)S(1)}, bf16[136,1152]{1,0:T(8,128)(2,1)S(1)}, u32[]{:S(2)}, u32[]{:S(2)}) collective-permute-start(bf16[136,1152]{1,0:T(8,128)(2,1)S(1)} %labelled_rows.1.refs_5_.refs_2_.refs_6_), channel_id=1, source_target_pairs={{0,1},{1,0},{2,3},{3,2},{4,5},{5,4},{6,7},{7,6},{8,9},{9,8},{10,11... | collective-permute-start | bytes 940040 | tf_op jit(solution)/shard_map/ppermute | solution.py:232
  21.1 5.8 %collective-permute-start.7 = (bf16[136,1152]{1,0:T(8,128)(2,1)S(1)}, bf16[136,1152]{1,0:T(8,128)(2,1)S(1)}, u32[]{:S(2)}, u32[]{:S(2)}) collective-permute-start(bf16[136,1152]{1,0:T(8,128)(2,1)S(1)} %collective-permute-done.refs_6_.refs_3_.refs_7_), channel_id=1, source_target_pairs={{0,1},{1,0},{2,3},{3,2},{4,5},{5,4},{6,7},{7,6},{8,9},{9,8},{10,11... | collective-permute-start | bytes 940040 | tf_op jit(solution)/shard_map/ppermute | solution.py:232
  21.1 5.8 %collective-permute-start.8 = (bf16[136,1152]{1,0:T(8,128)(2,1)S(1)}, bf16[136,1152]{1,0:T(8,128)(2,1)S(1)}, u32[]{:S(2)}, u32[]{:S(2)}) collective-permute-start(bf16[136,1152]{1,0:T(8,128)(2,1)S(1)} %collective-permute-done.1.refs_7_.refs_4_.refs_8_), channel_id=1, source_target_pairs={{0,1},{1,0},{2,3},{3,2},{4,5},{5,4},{6,7},{7,6},{8,9},{9,8},{10,11... | collective-permute-start | bytes 940040 | tf_op jit(solution)/shard_map/ppermute | solution.py:232
  21.6 10.3 %collective-permute-start.2 = (bf16[136,1152]{1,0:T(8,128)(2,1)S(1)}, bf16[136,1152]{1,0:T(8,128)(2,1)S(1)}, u32[]{:S(2)}, u32[]{:S(2)}) collective-permute-start(bf16[136,1152]{1,0:T(8,128)(2,1)S(1)} %collective-permute-done.refs_6_.refs_3_.refs_7_), channel_id=1, source_target_pairs={{0,8},{8,0},{16,24},{24,16},{1,9},{9,1},{17,25},{25,17},{2,10},{10... | collective-permute-start | bytes 940040 | tf_op jit(solution)/shard_map/ppermute | solution.py:232
  23.1 8.7 %collective-permute-start.5 = (bf16[128,1152]{1,0:T(8,128)(2,1)S(1)}, bf16[128,1152]{1,0:T(8,128)(2,1)S(1)}, u32[]{:S(2)}, u32[]{:S(2)}) collective-permute-start(bf16[128,1152]{1,0:T(8,128)(2,1)S(1)} %collective-permute-done.3.refs_3_.refs_6_.refs_7_), channel_id=1, source_target_pairs={{0,16},{8,24},{16,0},{24,8},{1,17},{9,25},{17,1},{25,9},{2,18},{10... | collective-permute-start | bytes 884744 | tf_op jit(solution)/shard_map/ppermute | solution.py:232
  31.8 1.6 %collective-permute-start.13 = (bf16[136,1152]{1,0:T(8,128)(2,1)S(1)}, bf16[136,1152]{1,0:T(8,128)(2,1)S(1)}, u32[]{:S(2)}, u32[]{:S(2)}) collective-permute-start(bf16[136,1152]{1,0:T(8,128)(2,1)S(1)} %collective-permute-done.2.refs_9_.refs_5_), channel_id=1, source_target_pairs={{0,1},{1,0},{2,3},{3,2},{4,5},{5,4},{6,7},{7,6},{8,9},{9,8},{10,11... | collective-permute-start | bytes 940040 | tf_op jit(solution)/shard_map/ppermute | solution.py:232
  31.8 4.7 %collective-permute-start.12 = (bf16[128,1152]{1,0:T(8,128)(2,1)S(1)}, bf16[128,1152]{1,0:T(8,128)(2,1)S(1)}, u32[]{:S(2)}, u32[]{:S(2)}) collective-permute-start(bf16[128,1152]{1,0:T(8,128)(2,1)S(1)} %collective-permute-done.5.refs_5_.refs_9_), channel_id=1, source_target_pairs={{0,1},{1,0},{2,3},{3,2},{4,5},{5,4},{6,7},{7,6},{8,9},{9,8},{10,11... | collective-permute-start | bytes 884744 | tf_op jit(solution)/shard_map/ppermute | solution.py:232
  36.0 10.3 %collective-permute-start.18 = (s16[136,1152]{1,0:T(8,128)(2,1)S(1)}, s16[136,1152]{1,0:T(8,128)(2,1)S(1)}, u32[]{:S(2)}, u32[]{:S(2)}) collective-permute-start(s16[136,1152]{1,0:T(8,128)(2,1)S(1)} %get-tuple-element.50.refs_17_), channel_id=1, source_target_pairs={{0,16},{8,24},{16,0},{24,8},{1,17},{9,25},{17,1},{25,9},{2,18},{10... | collective-permute-start | bytes 940040 | tf_op jit(solution)/shard_map/ppermute | solution.py:232
  39.1 10.4 %collective-permute-start.15 = (s16[136,1152]{1,0:T(8,128)(2,1)S(1)}, s16[136,1152]{1,0:T(8,128)(2,1)S(1)}, u32[]{:S(2)}, u32[]{:S(2)}) collective-permute-start(s16[136,1152]{1,0:T(8,128)(2,1)S(1)} %get-tuple-element.54), channel_id=1, source_target_pairs={{0,8},{8,0},{16,24},{24,16},{1,9},{9,1},{17,25},{25,17},{2,10},{10... | collective-permute-start | bytes 940040 | tf_op jit(solution)/shard_map/ppermute | solution.py:232
  39.8 12.4 %collective-permute-start.17 = (s16[136,1152]{1,0:T(8,128)(2,1)S(1)}, s16[136,1152]{1,0:T(8,128)(2,1)S(1)}, u32[]{:S(2)}, u32[]{:S(2)}) collective-permute-start(s16[136,1152]{1,0:T(8,128)(2,1)S(1)} %get-tuple-element.56), channel_id=1, source_target_pairs={{0,16},{8,24},{16,0},{24,8},{1,17},{9,25},{17,1},{25,9},{2,18},{10... | collective-permute-start | bytes 940040 | tf_op jit(solution)/shard_map/ppermute | solution.py:232
  41.3 21.5 %collective-permute-start.14 = (s16[136,1152]{1,0:T(8,128)(2,1)S(1)}, s16[136,1152]{1,0:T(8,128)(2,1)S(1)}, u32[]{:S(2)}, u32[]{:S(2)}) collective-permute-start(s16[136,1152]{1,0:T(8,128)(2,1)S(1)} %get-tuple-element.52), channel_id=1, source_target_pairs={{0,8},{8,0},{16,24},{24,16},{1,9},{9,1},{17,25},{25,17},{2,10},{10... | collective-permute-start | bytes 940040 | tf_op jit(solution)/shard_map/ppermute | solution.py:232
  46.5 15.3 %collective-permute-start.19 = (s16[136,1152]{1,0:T(8,128)(2,1)S(1)}, s16[136,1152]{1,0:T(8,128)(2,1)S(1)}, u32[]{:S(2)}, u32[]{:S(2)}) collective-permute-start(s16[136,1152]{1,0:T(8,128)(2,1)S(1)} %passed_sum.3), channel_id=1, source_target_pairs={{0,4},{1,5},{2,6},{3,7},{4,0},{5,1},{6,2},{7,3},{8,12},{9,13},{10,... | collective-permute-start | bytes 940040 | tf_op jit(solution)/shard_map/ppermute | solution.py:232
  49.7 13.8 %collective-permute-start.16 = (s16[136,1152]{1,0:T(8,128)(2,1)S(1)}, s16[136,1152]{1,0:T(8,128)(2,1)S(1)}, u32[]{:S(2)}, u32[]{:S(2)}) collective-permute-start(s16[136,1152]{1,0:T(8,128)(2,1)S(1)} %passed_sum.2), channel_id=1, source_target_pairs={{0,2},{1,3},{2,0},{3,1},{4,6},{5,7},{6,4},{7,5},{8,10},{9,11},{10,... | collective-permute-start | bytes 940040 | tf_op jit(solution)/shard_map/ppermute | solution.py:232

commit v5 on v0

v5 whole, which is shorter than its diff:
```python
import math

import jax
import jax.numpy as jnp
from jax import lax
from jax.experimental import pallas as pl
from jax.experimental.pallas import tpu as pltpu
from jax.sharding import PartitionSpec as P

LOG2E = 1.4426950408889634
CODE_TOP = 32000.0
CODE_STEPS = 32.0
EXTRA_ROWS = 8
LABEL_BASE = 128
TILE = 256
LANES = 128
SMEM = pl.BlockSpec(memory_space=pltpu.SMEM)
VMEM = pl.BlockSpec(memory_space=pltpu.VMEM)
ANY = pl.BlockSpec(memory_space=pl.ANY)


def whole(array):
    return ((array, 0, 0),)


def part_widths(width):
    first = min(3 * TILE, width - LANES)
    return (first, width - first)


def column_tiles(width):
    tiles, begin = [], 0
    for p, w in enumerate(part_widths(width)):
        tiles += [(p, k, begin + k, min(TILE, w - k)) for k in range(0, w, TILE)]
        begin += w
    return tiles


def piece(block, rows, tile):
    p, inner, start, span = tile
    ref, row, column = block[0 if len(block) == 1 else p]
    first = start if len(block) == 1 else inner
    return ref.at[pl.ds(row + rows[0], rows[1]), pl.ds(column + first, span)]


class Operands:
    def __init__(self):
        self.pairs = []

    def add(self, array, spec):
        for i, (a, s) in enumerate(self.pairs):
            if a is array and s is spec:
                return i
        self.pairs.append((array, spec))
        return len(self.pairs) - 1

    def block(self, block):
        at = [(self.add(a, VMEM), row, column) for a, row, column in block]
        return lambda refs: tuple((refs[i], row, column) for i, row, column in at)


def scale_code(top):
    return jnp.ceil(jnp.log(jnp.maximum(top, 1e-30)) * (CODE_STEPS * LOG2E))


def encode(value, block, tile):
    size, span = value.shape
    code = scale_code(jnp.max(jnp.abs(value), axis=0, keepdims=True))
    gain = CODE_TOP * jnp.exp(code * (-1.0 / (CODE_STEPS * LOG2E)))
    piece(block, (0, size), tile)[...] = (
        jnp.round(value * gain).astype(jnp.int32).astype(jnp.int16)
    )
    scales = jnp.broadcast_to(code.astype(jnp.int32), (EXTRA_ROWS, span)).astype(jnp.int16)
    piece(block, (size, EXTRA_ROWS), tile)[...] = scales


def decoded(block, size, tile):
    code = piece(block, (size, EXTRA_ROWS), tile)[...].astype(jnp.int32).astype(jnp.float32)
    gain = jnp.exp(code[:1] * (1.0 / (CODE_STEPS * LOG2E))) * (1.0 / CODE_TOP)
    return piece(block, (0, size), tile)[...].astype(jnp.int32).astype(jnp.float32) * gain


def call(kernel, name, operands, out_shape, scratch, room, cost, after=(), held_back=()):
    arrays = [a for a, _ in operands]
    held = sum(math.prod(a.shape) * a.dtype.itemsize for a in [*arrays, *out_shape])

    def body(*refs):
        results = refs[len(arrays) + len(after) + len(held_back) :]
        kernel(refs[: len(arrays)], results[: len(out_shape)] + results[len(out_shape) + len(held_back) :])

    return pl.pallas_call(
        body,
        out_shape=[*out_shape, *(jax.ShapeDtypeStruct(a.shape, a.dtype) for a in held_back)],
        in_specs=[s for _, s in operands] + [ANY] * (len(after) + len(held_back)),
        out_specs=[VMEM] * len(out_shape) + [ANY] * len(held_back),
        input_output_aliases={
            len(arrays) + len(after) + i: len(out_shape) + i for i in range(len(held_back))
        },
        scratch_shapes=scratch,
        compiler_params=pltpu.CompilerParams(vmem_limit_bytes=held + room),
        cost_estimate=pl.CostEstimate(flops=cost, bytes_accessed=cost, transcendentals=0),
        name=name,
    )(*arrays, *after, *held_back)


def labelled(images, labels):
    size, width = images.shape

    def kernel(ins, outs):
        (out,) = outs
        row = ins[1][...]
        low, high = lax.rem(row, LABEL_BASE), lax.div(row, LABEL_BASE)
        at = lax.broadcasted_iota(jnp.int32, (EXTRA_ROWS, size), 0)
        parts = jnp.where(at == 0, high, jnp.where(at == 1, low, 0)).astype(jnp.float32)
        out[pl.ds(0, size), :] = ins[0][...]
        out[pl.ds(size, EXTRA_ROWS), :] = jnp.zeros((EXTRA_ROWS, width), jnp.bfloat16)
        out[pl.ds(size, EXTRA_ROWS), pl.ds(0, size)] = parts.astype(jnp.bfloat16)

    shape = jax.ShapeDtypeStruct((size + EXTRA_ROWS, width), jnp.bfloat16)
    operands = [(images, VMEM), (labels[None, :], VMEM)]
    return call(kernel, "labelled", operands, [shape], [], 2**21, size)[0]


def bundled(texts, images):
    size, width = texts[0][0].shape[0], texts[0][0].shape[1]
    operands = Operands()
    views = [operands.block(texts), operands.block(images)]

    def kernel(ins, outs):
        for view, first, count in zip(views, (0, size), (size, size + EXTRA_ROWS)):
            ((ref, row, column),) = view(ins)
            outs[0][pl.ds(first, count), :] = ref[pl.ds(row, count), pl.ds(column, width)]

    shape = jax.ShapeDtypeStruct((2 * size + EXTRA_ROWS, width), jnp.bfloat16)
    (both,) = call(kernel, "bundled", operands.pairs, [shape], [], 2**21, size)
    return both


def first_row(mask, size):
    owner = (lax.axis_index("blk") ^ mask[0]) * lax.axis_size("grp") + (lax.axis_index("grp") ^ mask[1])
    return owner * size


def keys_of(block, size, mask, is_image):
    if not is_image:
        ids = lax.broadcasted_iota(jnp.int32, (1, size), 1) + first_row(mask, size)
        return ids.astype(jnp.float32)
    parts = piece(block, (size, EXTRA_ROWS), (0, 0, 0, size))[...].astype(jnp.float32)
    return parts[0:1] * LABEL_BASE + parts[1:2]


def gradient_sums(name, size, scalars, x_blocks, y_blocks, masks, x_images, jobs, before, emits, after=()):
    width = x_blocks[0][0][0].shape[1]
    x_masks, y_masks = masks
    per_tile = TILE // size
    widths = part_widths(width)
    shapes, where = [], {}

    def result(extra, w, dtype):
        shapes.append(jax.ShapeDtypeStruct((size + extra, w), dtype))
        return len(shapes) - 1

    for r, kind in enumerate(emits):
        if kind == "float":
            where[r] = [(result(0, width, jnp.float32), 0, 0)]
        else:
            cut = widths if kind == "parts" else (width,)
            where[r] = [(result(EXTRA_ROWS, w, jnp.int16), 0, 0) for w in cut]
    operands = Operands()
    slope_at, shift_at = [operands.add(s, SMEM) for s in scalars]
    x_views = [operands.block(b) for b in x_blocks]
    y_views = [operands.block(b) for b in y_blocks]
    before_at = {r: operands.add(b, VMEM) for r, b in before.items()}

    def kernel(ins, refs):
        outs, weights = refs[:-1], refs[-1]
        slope, shift = ins[slope_at][0] * LOG2E, ins[shift_at][0] * LOG2E
        x_refs, y_refs = [v(ins) for v in x_views], [v(ins) for v in y_views]

        def stacked(chosen):
            return jnp.concatenate(
                [ref[pl.ds(row, size), pl.ds(column, width)] for ((ref, row, column),) in chosen],
                axis=0,
            )

        for rows, columns in jobs:
            x_all = stacked([x_refs[r] for r in rows])
            keys = [
                jnp.broadcast_to(keys_of(x_refs[r], size, x_masks[r], x_images), (size, size)).T
                for r in rows
            ]
            for n in range(0, len(columns), per_tile):
                chosen = columns[n : n + per_tile]
                other = jnp.concatenate(
                    [keys_of(y_refs[c], size, y_masks[c], not x_images) for c in chosen], axis=1
                )
                scores = lax.dot_general(
                    x_all,
                    stacked([y_refs[c] for c in chosen]),
                    (((1,), (1,)), ((), ())),
                    preferred_element_type=jnp.float32,
                )
                for i in range(len(rows)):
                    z = scores[i * size : (i + 1) * size] * slope + shift
                    sig = 1.0 / (1.0 + jnp.exp2(-z))
                    w = jnp.where(jnp.tile(keys[i], (1, per_tile)) == other, sig - 1.0, sig)
                    weights[pl.ds(i * size, size), pl.ds(n * size, TILE)] = w.astype(jnp.bfloat16)
            for tile in column_tiles(width):
                sums = jnp.dot(
                    weights[pl.ds(0, len(rows) * size), pl.ds(0, len(columns) * size)],
                    jnp.concatenate([piece(y_refs[c], (0, size), tile)[...] for c in columns], axis=0),
                    preferred_element_type=jnp.float32,
                )
                for i, r in enumerate(rows):
                    block = sums[i * size : (i + 1) * size]
                    if r in before_at:
                        block = block + piece(whole(ins[before_at[r]]), (0, size), tile)[...]
                    out = tuple((outs[o], row, column) for o, row, column in where[r])
                    if emits[r] == "float":
                        piece(out, (0, size), tile)[...] = block
                    else:
                        encode(block, out, tile)

    pairs = sum(len(rows) * len(columns) for rows, columns in jobs)
    scratch = [pltpu.VMEM((len(x_blocks) * size, len(y_blocks) * size), jnp.bfloat16)]
    room = len(x_blocks) * len(y_blocks) * size * size * 2 + 8 * 2**20
    results = call(kernel, name, operands.pairs, shapes, scratch, room, pairs * size, after)
    return [tuple(results[o] for o, _, _ in where[r]) for r in range(len(emits))]


def passed_sum(kept, received, part, held_back=()):
    size, width = kept.shape
    operands = Operands()
    kept_at = operands.add(kept, VMEM)
    views = [operands.block(b if part is None or len(b) == 1 else (b[part],) * 2) for b in received]

    def kernel(ins, outs):
        for tile in column_tiles(width):
            p, inner, _, span = tile
            if part is None or p == part:
                total = piece(whole(ins[kept_at]), (0, size), tile)[...]
                for view in views:
                    total = total + decoded(view(ins), size, tile)
                encode(total, whole(outs[0]), tile if part is None else (0, 0, inner, span))

    cut = width if part is None else part_widths(width)[part]
    shape = jax.ShapeDtypeStruct((size + EXTRA_ROWS, cut), jnp.int16)
    return call(kernel, "passed_sum", operands.pairs, [shape], [], 2**21, size, (), held_back)


def output_sum(sharpness, kept, received):
    size, width = kept.shape
    operands = Operands()
    sharpness_at = operands.add(sharpness, SMEM)
    kept_at = operands.add(kept, VMEM)
    views = [operands.block(b) for b in received]

    def kernel(ins, outs):
        for tile in column_tiles(width):
            total = piece(whole(ins[kept_at]), (0, size), tile)[...]
            for view in views:
                total = total + decoded(view(ins), size, tile)
            piece(whole(outs[0]), (0, size), tile)[...] = total * ins[sharpness_at][0]

    shape = jax.ShapeDtypeStruct((size, width), jnp.float32)
    return call(kernel, "output_sum", operands.pairs, [shape], [], 2**21, size)[0]


def swapped(array, step):
    axis, bit = step
    return lax.ppermute(array, axis, [(i, i ^ bit) for i in range(lax.axis_size(axis))])


def gathered(own, steps):
    arrays = [own]
    for step in steps:
        arrays = arrays + [swapped(a, step) for a in arrays]
    return [whole(a) for a in arrays]


def other_core(texts, images, core):
    both = swapped(bundled(texts, images), core)
    return ((both, 0, 0),), ((both, texts[0][0].shape[0], 0),)


def scattered_sum(sharpness, kept, coded, steps):
    def sent(block, step):
        return [(swapped(p, step), 0, 0) for p in block]

    last = steps[-1]
    if len(coded[-1]) == 1:
        received = [[sent(c, last)] for c in coded]
        begun = None
    else:
        received = [[None]] + [[sent(c[:1], last)] for c in coded[1:]]
        n = len(kept) - 1
        begun, *rest = passed_sum(
            kept[n], received[n], 0, [c[-1] for c in coded[1:]] + [coded[0][0]]
        )
        for r, c in zip(received[1:] + received[:1], rest):
            if r is received[0]:
                r[0] = sent([c], last)
            else:
                r[0] = r[0] + sent([c], last)
    for s in reversed(range(len(steps) - 1)):
        for m in reversed(range(1 << s)):
            n = m | 1 << s
            parts = range(2) if len(received[n][0]) == 2 else [None]
            passed = []
            for p in parts:
                if begun is not None:
                    passed.append(begun)
                    begun = None
                else:
                    passed += passed_sum(kept[n], received[n], p)
            received[m].append(sent(passed, steps[s]))
    return output_sum(sharpness, kept[0], received[0])


def bit_steps(axis):
    return [(axis, 1 << k) for k in range(int(math.log2(lax.axis_size(axis))))]


def owner_masks(steps):
    masks = [(0, 0)]
    for axis, bit in steps:
        masks = masks + [(b ^ bit, g) if axis == "blk" else (b, g ^ bit) for b, g in masks]
    return masks


def per_device(
    picture_vectors, caption_vectors, matching_caption, sharpness_parameter, additive_intercept
):
    scalars = (sharpness_parameter, additive_intercept)
    size = picture_vectors.shape[0]
    core, *grp_steps = bit_steps("grp")
    every = grp_steps + bit_steps("blk")
    steps = [every[0::2], every[1::2]]
    assert len(steps[0]) == len(steps[1]) >= 2
    masks = [owner_masks(s + [core]) for s in steps]
    count = 1 << len(steps[0])
    half = count // 2
    early, late = list(range(half + 1)), list(range(half + 1, count))
    own = [labelled(picture_vectors, matching_caption), caption_vectors]
    blocks = [gathered(o, s) for o, s in zip(own, steps)]
    others = [{}, {}]
    for m in early:
        others[1][m], others[0][m] = other_core(blocks[1][m], blocks[0][m], core)

    def sums(name, kind, rows, columns, jobs, before, emits, after=()):
        other = 1 - kind
        x_blocks = [blocks[kind][m] for m in rows]
        y_blocks = [blocks[other][m] for m in columns] + [others[other][m] for m in columns]
        x_masks = [masks[kind][m] for m in rows]
        y_masks = [masks[other][m + shift] for shift in (0, count) for m in columns]
        return gradient_sums(
            name,
            size,
            scalars,
            x_blocks,
            y_blocks,
            (x_masks, y_masks),
            kind == 0,
            jobs,
            before,
            emits,
            after,
        )

    before = []
    for k in range(2):
        jobs = [(early, list(range(2 * len(early))))]
        results = sums("early_sums", k, early, early, jobs, {}, ["float"] * len(early))
        before.append([s for (s,) in results])
    arrays = [[b[m][0][0] for m in late] for b in blocks]
    arrays, before = lax.optimization_barrier((arrays, before))
    for k in range(2):
        for m, a in zip(late, arrays[k]):
            blocks[k][m] = whole(a)
            others[k][m] = whole(swapped(a, core))
    every = list(range(count))
    jobs = [(late, every + [count + m for m in every]), (early, late + [count + m for m in late])]
    coded, kept, after = [None, None], [None, None], ()
    for k, cut in ((1, "whole"), (0, "whole")):
        emits = ["float"] * half + ["whole"] + [cut] * len(late)
        results = sums(
            "late_sums", k, every, every, jobs, dict(zip(early, before[k])), emits, after
        )
        kept[k] = [s for (s,) in results[:half]]
        coded[k] = results[half:]
        after = coded[k][0]
    return tuple(scattered_sum(scalars[0], kept[k], coded[k], steps[k]) for k in range(2))


def solution(mesh):
    placed = (P(("blk", "grp"), None), P(("blk", "grp"), None), P(("blk", "grp")), P(), P())
    return jax.shard_map(
        per_device,
        mesh=mesh,
        in_specs=placed,
        out_specs=(P(("blk", "grp"), None), P(("blk", "grp"), None)),
        check_vma=False,
    )
```

time: 157 us -> 66.1 us (0.42)
  waiting for transfers between devices: 103 us -> 34.4 us
  matrix products: 15.5 us -> 0 us
  between operations: 15.2 us -> 2.07 us
  blocking collectives: 12.1 us -> 0 us
  Pallas kernels: 0 us -> 11.4 us
  starting transfers between devices: 5.24 us -> 16.5 us
  other arithmetic: 3.85 us -> 0 us
    reduce_scatter x1 -> x0, waiting for transfers between devices: 55.4 us -> none  [per_device(): lax.psum_scatter(image_total, 'grp', scatter_dimension=0, tiled=True)]
    unnamed x4 -> x0, waiting for transfers between devices: 29.9 us -> none
    ppermute x3 -> x17, waiting for transfers between devices: 8.62 us -> 34.4 us  [swapped(): lax.ppermute(array, axis, [(i, i ^ bit) for i in range(lax.axis_size(axis...]
    dot_general x12 -> x0, matrix products: 15.5 us -> none  [the longest x4 7.18 us: rotation_step(): jnp.dot(pair_coefficients, guest_captions, preferred_element_type=jnp.flo...]
    all_gather x1 -> x0, blocking collectives: 12.1 us -> none  [per_device(): lax.all_gather(matching_caption, 'grp', axis=0, tiled=True)]
    pallas_call x0 -> x12, Pallas kernels: none -> 11.4 us  [call(): pl.pallas_call(body, out_shape=[*out_shape, *(jax.ShapeDtypeStruct(a.shap...]
    ppermute x3 -> x17, starting transfers between devices: 5.13 us -> 16.5 us  [swapped(): lax.ppermute(array, axis, [(i, i ^ bit) for i in range(lax.axis_size(axis...]
    all_gather x1 -> x0, waiting for transfers between devices: 8.87 us -> none  [per_device(): lax.all_gather(picture_vectors, 'grp', axis=0, tiled=True)]
  transfers between devices with their start and end apart: 6 -> 17, of which waited for: 4 -> 9; matrix products, arithmetic and copies ran while one was open for 10% -> 0% of each run, Pallas kernels for 0% -> 16%
where the time goes in v5:
time: 66.1 us; the launch traced here: 65.9 us
  waiting for transfers between devices  34.4 us (52%)
  starting transfers between devices  16.5 us (25%)
  Pallas kernels  11.4 us (17%)
  between operations  2.07 us (3%)
  local copies, waits for them, and re-layouts  1.61 us (2%)
    ppermute x17, waiting for transfers between devices, swapped(): lax.ppermute(array, axis, [(i, i ^ bit) for i in range(lax.axis_size(axis...  34.4 us
    ppermute x17, starting transfers between devices, swapped(): lax.ppermute(array, axis, [(i, i ^ bit) for i in range(lax.axis_size(axis...  16.5 us
    pallas_call x12, Pallas kernels, call(): pl.pallas_call(body, out_shape=[*out_shape, *(jax.ShapeDtypeStruct(a.shap...  11.4 us
    unnamed x6, local copies, waits for them, and re-layouts  1.61 us
  transfers between devices with their start and end apart: 17, of which 9 were waited for; matrix products, arithmetic and copies ran while one was open for 0% of the time, Pallas kernels for 16%

profile of v5, /device:TPU:0, one launch (start us, length us, event | category | flops | bytes accessed | tf_op | source)
XLA Modules:
  0.0 65.9 jit_solution(9596904132187876218)
XLA Ops:
  0.6 0.0 copy-start.2
  0.6 0.6 copy-done.2
  1.3 0.0 copy-start.1
  1.3 1.0 %copy-done.1 = bf16[128,1152]{1,0:T(8,128)(2,1)S(1)} copy-done((bf16[128,1152]{1,0:T(8,128)(2,1)S(1)}, bf16[128,1152]{1,0:T(8,128)(2,1)}, u32[]{:S(2)}) %copy-start.1) | copy-done | bytes 294936
  2.2 0.0 copy-start
  2.3 3.1 %collective-permute-start = (bf16[136,1152]{1,0:T(8,128)(2,1)S(1)}, bf16[136,1152]{1,0:T(8,128)(2,1)S(1)}, u32[]{:S(2)}, u32[]{:S(2)}) collective-permute-start(bf16[136,1152]{1,0:T(8,128)(2,1)S(1)} %labelled.1.refs_1_.refs_2_.refs_5_.refs_6_), channel_id=1, source_target_pairs={{0,2},{1,3},{2,0},{3,1},{4,6},{5,7},{6,4},{7,5},{8,10},{9,11},{10,... | collective-permute-start | bytes 940040 | tf_op jit(solution)/shard_map/ppermute | solution.py:271
  5.4 1.5 %collective-permute-start.1 = (bf16[136,1152]{1,0:T(8,128)(2,1)S(1)}, bf16[136,1152]{1,0:T(8,128)(2,1)S(1)}, u32[]{:S(2)}, u32[]{:S(2)}) collective-permute-start(bf16[136,1152]{1,0:T(8,128)(2,1)S(1)} %labelled.1.refs_1_.refs_2_.refs_5_.refs_6_), channel_id=1, source_target_pairs={{0,8},{8,0},{16,24},{24,16},{1,9},{9,1},{17,25},{25,17},{2,10},{10... | collective-permute-start | bytes 940040 | tf_op jit(solution)/shard_map/ppermute | solution.py:271
  6.9 0.0 copy-done
  6.9 2.6 %collective-permute-start.3 = (bf16[128,1152]{1,0:T(8,128)(2,1)S(1)}, bf16[128,1152]{1,0:T(8,128)(2,1)S(1)}, u32[]{:S(2)}, u32[]{:S(2)}) collective-permute-start(bf16[128,1152]{1,0:T(8,128)(2,1)S(1)} %copy-done), channel_id=1, source_target_pairs={{0,4},{1,5},{2,6},{3,7},{4,0},{5,1},{6,2},{7,3},{8,12},{9,13},{10,... | collective-permute-start | bytes 884744 | tf_op jit(solution)/shard_map/ppermute | solution.py:271
  9.5 1.5 %collective-permute-start.5 = (bf16[128,1152]{1,0:T(8,128)(2,1)S(1)}, bf16[128,1152]{1,0:T(8,128)(2,1)S(1)}, u32[]{:S(2)}, u32[]{:S(2)}) collective-permute-start(bf16[128,1152]{1,0:T(8,128)(2,1)S(1)} %copy-done), channel_id=1, source_target_pairs={{0,16},{8,24},{16,0},{24,8},{1,17},{9,25},{17,1},{25,9},{2,18},{10... | collective-permute-start | bytes 884744 | tf_op jit(solution)/shard_map/ppermute | solution.py:271
  11.0 0.1 collective-permute-start.6
  11.1 11.2 %collective-permute-done.3.refs_0_.refs_6_.refs_3_.refs_7_ = bf16[128,1152]{1,0:T(8,128)(2,1)S(1)} collective-permute-done((bf16[128,1152]{1,0:T(8,128)(2,1)S(1)}, bf16[128,1152]{1,0:T(8,128)(2,1)S(1)}, u32[]{:S(2)}, u32[]{:S(2)}) %collective-permute-start.3) | collective-permute-done | bytes 294944 | tf_op jit(solution)/shard_map/ppermute | solution.py:271
  22.3 0.0 collective-permute-done.refs_1_.refs_3_.refs_6_.refs_7_
  22.4 0.1 collective-permute-start.7
  22.5 0.0 collective-permute-done.5.refs_0_.refs_7_.refs_4_.refs_8_
  22.5 0.0 collective-permute-done.1.refs_1_.refs_4_.refs_7_.refs_8_
  22.5 0.5 collective-permute-start.8
  23.1 0.0 collective-permute-start.2
  23.1 1.5 %collective-permute-start.4 = (bf16[128,1152]{1,0:T(8,128)(2,1)S(1)}, bf16[128,1152]{1,0:T(8,128)(2,1)S(1)}, u32[]{:S(2)}, u32[]{:S(2)}) collective-permute-start(bf16[128,1152]{1,0:T(8,128)(2,1)S(1)} %collective-permute-done.3.refs_0_.refs_6_.refs_3_.refs_7_), channel_id=1, source_target_pairs={{0,16},{8,24},{16,0},{24,8},{1,17},{9,25},{17,1},{25,9},{2,18},{10... | collective-permute-start | bytes 884744 | tf_op jit(solution)/shard_map/ppermute | solution.py:271
  25.9 0.0 collective-permute-done.6.refs_8_.refs_10_
  25.9 0.0 collective-permute-done.7.refs_9_.refs_11_
  25.9 0.0 collective-permute-done.8.refs_10_.refs_12_
  25.9 1.9 %early_sums.3 = (f32[128,1152]{1,0:T(8,128)S(1)}, f32[128,1152]{1,0:T(8,128)S(1)}, f32[128,1152]{1,0:T(8,128)S(1)}) custom-call(f32[1]{0:T(128)S(6)} %copy.7.refs_0_, f32[1]{0:T(128)S(6)} %copy.8.refs_1_, bf16[128,1152]{1,0:T(8,128)(2,1)S(1)} %copy-done, bf16[128,1152]{1,0:T(8,128)(2,1)S(1)} %collective-permute-done.3.refs_0_.refs_6_.refs_3_.refs_7_, ...), custom_call_target="tpu_custom_call" | custom-call | flops 2304 | bytes 2304 | tf_op jit(solution)/shard_map/early_sums/pallas_call | solution.py:91
  27.9 1.9 %early_sums.2 = (f32[128,1152]{1,0:T(8,128)S(1)}, f32[128,1152]{1,0:T(8,128)S(1)}, f32[128,1152]{1,0:T(8,128)S(1)}) custom-call(f32[1]{0:T(128)S(6)} %copy.7.refs_0_, f32[1]{0:T(128)S(6)} %copy.8.refs_1_, bf16[136,1152]{1,0:T(8,128)(2,1)S(1)} %labelled.1.refs_1_.refs_2_.refs_5_.refs_6_, ...), custom_call_target="tpu_custom_call" | custom-call | flops 2304 | bytes 2304 | tf_op jit(solution)/shard_map/early_sums/pallas_call | solution.py:91
  29.8 2.4 %collective-permute-done.4.refs_5_.refs_9_ = bf16[128,1152]{1,0:T(8,128)(2,1)S(1)} collective-permute-done((bf16[128,1152]{1,0:T(8,128)(2,1)S(1)}, bf16[128,1152]{1,0:T(8,128)(2,1)S(1)}, u32[]{:S(2)}, u32[]{:S(2)}) %collective-permute-start.4) | collective-permute-done | bytes 294944 | tf_op jit(solution)/shard_map/ppermute | solution.py:271
  32.1 0.3 collective-permute-done.2.refs_9_.refs_5_
  32.5 0.0 collective-permute-start.10
  32.5 0.5 collective-permute-start.9
  33.0 1.1 %collective-permute-done.10.refs_13_ = bf16[136,1152]{1,0:T(8,128)(2,1)S(1)} collective-permute-done((bf16[136,1152]{1,0:T(8,128)(2,1)S(1)}, bf16[136,1152]{1,0:T(8,128)(2,1)S(1)}, u32[]{:S(2)}, u32[]{:S(2)}) %collective-permute-start.10) | collective-permute-done | bytes 313376 | tf_op jit(solution)/shard_map/ppermute | solution.py:271
  34.1 2.5 %late_sums.2 = (f32[128,1152]{1,0:T(8,128)S(1)}, f32[128,1152]{1,0:T(8,128)S(1)}, s16[136,1152]{1,0:T(8,128)(2,1)S(1)}, s16[136,1152]{1,0:T(8,128)(2,1)S(1)}) custom-call(f32[1]{0:T(128)S(6)} %copy.7.refs_0_, f32[1]{0:T(128)S(6)} %copy.8.refs_1_, bf16[128,1152]{1,0:T(8,128)(2,1)S(1)} %copy-done, ...), custom_call_target="tpu_custom_call" | custom-call | flops 1792 | bytes 1792 | tf_op jit(solution)/shard_map/late_sums/pallas_call | solution.py:91
  36.6 1.6 %collective-permute-start.15 = (s16[136,1152]{1,0:T(8,128)(2,1)S(1)}, s16[136,1152]{1,0:T(8,128)(2,1)S(1)}, u32[]{:S(2)}, u32[]{:S(2)}) collective-permute-start(s16[136,1152]{1,0:T(8,128)(2,1)S(1)} %get-tuple-element.45), channel_id=1, source_target_pairs={{0,16},{8,24},{16,0},{24,8},{1,17},{9,25},{17,1},{25,9},{2,18},{10... | collective-permute-start | bytes 940040 | tf_op jit(solution)/shard_map/ppermute | solution.py:271
  38.2 0.0 collective-permute-done.9.refs_13_
  38.2 2.5 %late_sums.3 = (f32[128,1152]{1,0:T(8,128)S(1)}, f32[128,1152]{1,0:T(8,128)S(1)}, s16[136,1152]{1,0:T(8,128)(2,1)S(1)}, s16[136,1152]{1,0:T(8,128)(2,1)S(1)}) custom-call(f32[1]{0:T(128)S(6)} %copy.7.refs_0_, f32[1]{0:T(128)S(6)} %copy.8.refs_1_, bf16[136,1152]{1,0:T(8,128)(2,1)S(1)} %labelled.1.refs_1_.refs_2_.refs_5_.refs_6_, ...), custom_call_target="tpu_custom_call" | custom-call | flops 1792 | bytes 1792 | tf_op jit(solution)/shard_map/late_sums/pallas_call | solution.py:91
  40.7 1.4 %collective-permute-start.12 = (s16[136,1152]{1,0:T(8,128)(2,1)S(1)}, s16[136,1152]{1,0:T(8,128)(2,1)S(1)}, u32[]{:S(2)}, u32[]{:S(2)}) collective-permute-start(s16[136,1152]{1,0:T(8,128)(2,1)S(1)} %get-tuple-element.42), channel_id=1, source_target_pairs={{0,8},{8,0},{16,24},{24,16},{1,9},{9,1},{17,25},{25,17},{2,10},{10... | collective-permute-start | bytes 940040 | tf_op jit(solution)/shard_map/ppermute | solution.py:271
  42.1 0.5 collective-permute-start.14
  42.6 0.7 %collective-permute-start.11 = (s16[136,1152]{1,0:T(8,128)(2,1)S(1)}, s16[136,1152]{1,0:T(8,128)(2,1)S(1)}, u32[]{:S(2)}, u32[]{:S(2)}) collective-permute-start(s16[136,1152]{1,0:T(8,128)(2,1)S(1)} %get-tuple-element.40), channel_id=1, source_target_pairs={{0,8},{8,0},{16,24},{24,16},{1,9},{9,1},{17,25},{25,17},{2,10},{10... | collective-permute-start | bytes 940040 | tf_op jit(solution)/shard_map/ppermute | solution.py:271
  43.3 3.6 %collective-permute-done.15.refs_1_ = s16[136,1152]{1,0:T(8,128)(2,1)S(1)} collective-permute-done((s16[136,1152]{1,0:T(8,128)(2,1)S(1)}, s16[136,1152]{1,0:T(8,128)(2,1)S(1)}, u32[]{:S(2)}, u32[]{:S(2)}) %collective-permute-start.15) | collective-permute-done | bytes 313376 | tf_op jit(solution)/shard_map/ppermute | solution.py:271
  46.9 0.2 passed_sum.3
  47.1 0.4 collective-permute-start.16
  47.5 3.6 %collective-permute-done.12.refs_1_ = s16[136,1152]{1,0:T(8,128)(2,1)S(1)} collective-permute-done((s16[136,1152]{1,0:T(8,128)(2,1)S(1)}, s16[136,1152]{1,0:T(8,128)(2,1)S(1)}, u32[]{:S(2)}, u32[]{:S(2)}) %collective-permute-start.12) | collective-permute-done | bytes 313376 | tf_op jit(solution)/shard_map/ppermute | solution.py:271
  51.0 0.2 passed_sum.2
  51.2 0.5 collective-permute-start.13
  51.7 1.1 %collective-permute-done.14.refs_2_ = s16[136,1152]{1,0:T(8,128)(2,1)S(1)} collective-permute-done((s16[136,1152]{1,0:T(8,128)(2,1)S(1)}, s16[136,1152]{1,0:T(8,128)(2,1)S(1)}, u32[]{:S(2)}, u32[]{:S(2)}) %collective-permute-start.14) | collective-permute-done | bytes 313376 | tf_op jit(solution)/shard_map/ppermute | solution.py:271
  52.8 9.9 %collective-permute-done.16.refs_3_ = s16[136,1152]{1,0:T(8,128)(2,1)S(1)} collective-permute-done((s16[136,1152]{1,0:T(8,128)(2,1)S(1)}, s16[136,1152]{1,0:T(8,128)(2,1)S(1)}, u32[]{:S(2)}, u32[]{:S(2)}) %collective-permute-start.16) | collective-permute-done | bytes 313376 | tf_op jit(solution)/shard_map/ppermute | solution.py:271
  62.7 1.0 %output_sum.3 = f32[128,1152]{1,0:T(8,128)} custom-call(f32[1]{0:T(128)S(6)} %copy.7.refs_0_, f32[128,1152]{1,0:T(8,128)S(1)} %get-tuple-element.43.refs_1_, s16[136,1152]{1,0:T(8,128)(2,1)S(1)} %collective-permute-done.14.refs_2_, s16[136,1152]{1,0:T(8,128)(2,1)S(1)} %collective-permute-done.16.refs_3_), custom_call_target="tpu_custom_call" | custom-call | flops 128 | bytes 128 | tf_op jit(solution)/shard_map/output_sum/pallas_call | solution.py:91
  63.7 0.0 collective-permute-done.11.refs_2_
  63.7 1.2 %collective-permute-done.13.refs_3_ = s16[136,1152]{1,0:T(8,128)(2,1)S(1)} collective-permute-done((s16[136,1152]{1,0:T(8,128)(2,1)S(1)}, s16[136,1152]{1,0:T(8,128)(2,1)S(1)}, u32[]{:S(2)}, u32[]{:S(2)}) %collective-permute-start.13) | collective-permute-done | bytes 313376 | tf_op jit(solution)/shard_map/ppermute | solution.py:271
  64.9 1.0 %output_sum.2 = f32[128,1152]{1,0:T(8,128)} custom-call(f32[1]{0:T(128)S(6)} %copy.7.refs_0_, f32[128,1152]{1,0:T(8,128)S(1)} %get-tuple-element.39.refs_1_, s16[136,1152]{1,0:T(8,128)(2,1)S(1)} %collective-permute-done.11.refs_2_, s16[136,1152]{1,0:T(8,128)(2,1)S(1)} %collective-permute-done.13.refs_3_), custom_call_target="tpu_custom_call" | custom-call | flops 128 | bytes 128 | tf_op jit(solution)/shard_map/output_sum/pallas_call | solution.py:91
  (4 shorter events, 0.2 us)
Async XLA Ops:
  0.6 0.7 copy-start.2
  1.3 1.0 %copy-start.1 = (bf16[128,1152]{1,0:T(8,128)(2,1)S(1)}, bf16[128,1152]{1,0:T(8,128)(2,1)}, u32[]{:S(2)}) copy-start(bf16[128,1152]{1,0:T(8,128)(2,1)} %refs_0_.8) | copy-start | bytes 884740
  2.2 4.6 %copy-start = (bf16[128,1152]{1,0:T(8,128)(2,1)S(1)}, bf16[128,1152]{1,0:T(8,128)(2,1)}, u32[]{:S(2)}) copy-start(bf16[128,1152]{1,0:T(8,128)(2,1)} %refs_6_.1) | copy-start | bytes 884740
  2.3 20.0 %collective-permute-start = (bf16[136,1152]{1,0:T(8,128)(2,1)S(1)}, bf16[136,1152]{1,0:T(8,128)(2,1)S(1)}, u32[]{:S(2)}, u32[]{:S(2)}) collective-permute-start(bf16[136,1152]{1,0:T(8,128)(2,1)S(1)} %labelled.1.refs_1_.refs_2_.refs_5_.refs_6_), channel_id=1, source_target_pairs={{0,2},{1,3},{2,0},{3,1},{4,6},{5,7},{6,4},{7,5},{8,10},{9,11},{10,... | collective-permute-start | bytes 940040 | tf_op jit(solution)/shard_map/ppermute | solution.py:271
  5.4 17.1 %collective-permute-start.1 = (bf16[136,1152]{1,0:T(8,128)(2,1)S(1)}, bf16[136,1152]{1,0:T(8,128)(2,1)S(1)}, u32[]{:S(2)}, u32[]{:S(2)}) collective-permute-start(bf16[136,1152]{1,0:T(8,128)(2,1)S(1)} %labelled.1.refs_1_.refs_2_.refs_5_.refs_6_), channel_id=1, source_target_pairs={{0,8},{8,0},{16,24},{24,16},{1,9},{9,1},{17,25},{25,17},{2,10},{10... | collective-permute-start | bytes 940040 | tf_op jit(solution)/shard_map/ppermute | solution.py:271
  6.9 15.5 %collective-permute-start.3 = (bf16[128,1152]{1,0:T(8,128)(2,1)S(1)}, bf16[128,1152]{1,0:T(8,128)(2,1)S(1)}, u32[]{:S(2)}, u32[]{:S(2)}) collective-permute-start(bf16[128,1152]{1,0:T(8,128)(2,1)S(1)} %copy-done), channel_id=1, source_target_pairs={{0,4},{1,5},{2,6},{3,7},{4,0},{5,1},{6,2},{7,3},{8,12},{9,13},{10,... | collective-permute-start | bytes 884744 | tf_op jit(solution)/shard_map/ppermute | solution.py:271
  9.5 13.0 %collective-permute-start.5 = (bf16[128,1152]{1,0:T(8,128)(2,1)S(1)}, bf16[128,1152]{1,0:T(8,128)(2,1)S(1)}, u32[]{:S(2)}, u32[]{:S(2)}) collective-permute-start(bf16[128,1152]{1,0:T(8,128)(2,1)S(1)} %copy-done), channel_id=1, source_target_pairs={{0,16},{8,24},{16,0},{24,8},{1,17},{9,25},{17,1},{25,9},{2,18},{10... | collective-permute-start | bytes 884744 | tf_op jit(solution)/shard_map/ppermute | solution.py:271
  11.0 14.9 %collective-permute-start.6 = (bf16[264,1152]{1,0:T(8,128)(2,1)S(1)}, bf16[264,1152]{1,0:T(8,128)(2,1)S(1)}, u32[]{:S(2)}, u32[]{:S(2)}) collective-permute-start(bf16[264,1152]{1,0:T(8,128)(2,1)S(1)} %bundled.3), channel_id=1, source_target_pairs={{0,1},{1,0},{2,3},{3,2},{4,5},{5,4},{6,7},{7,6},{8,9},{9,8},{10,11... | collective-permute-start | bytes 1824776 | tf_op jit(solution)/shard_map/ppermute | solution.py:271
  22.4 3.5 %collective-permute-start.7 = (bf16[264,1152]{1,0:T(8,128)(2,1)S(1)}, bf16[264,1152]{1,0:T(8,128)(2,1)S(1)}, u32[]{:S(2)}, u32[]{:S(2)}) collective-permute-start(bf16[264,1152]{1,0:T(8,128)(2,1)S(1)} %bundled.4), channel_id=1, source_target_pairs={{0,1},{1,0},{2,3},{3,2},{4,5},{5,4},{6,7},{7,6},{8,9},{9,8},{10,11... | collective-permute-start | bytes 1824776 | tf_op jit(solution)/shard_map/ppermute | solution.py:271
  22.5 3.4 %collective-permute-start.8 = (bf16[264,1152]{1,0:T(8,128)(2,1)S(1)}, bf16[264,1152]{1,0:T(8,128)(2,1)S(1)}, u32[]{:S(2)}, u32[]{:S(2)}) collective-permute-start(bf16[264,1152]{1,0:T(8,128)(2,1)S(1)} %bundled.5), channel_id=1, source_target_pairs={{0,1},{1,0},{2,3},{3,2},{4,5},{5,4},{6,7},{7,6},{8,9},{9,8},{10,11... | collective-permute-start | bytes 1824776 | tf_op jit(solution)/shard_map/ppermute | solution.py:271
  23.1 9.4 %collective-permute-start.2 = (bf16[136,1152]{1,0:T(8,128)(2,1)S(1)}, bf16[136,1152]{1,0:T(8,128)(2,1)S(1)}, u32[]{:S(2)}, u32[]{:S(2)}) collective-permute-start(bf16[136,1152]{1,0:T(8,128)(2,1)S(1)} %collective-permute-done.refs_1_.refs_3_.refs_6_.refs_7_), channel_id=1, source_target_pairs={{0,8},{8,0},{16,24},{24,16},{1,9},{9,1},{17,25},{25,17},{2,10},{10... | collective-permute-start | bytes 940040 | tf_op jit(solution)/shard_map/ppermute | solution.py:271
  23.1 9.1 %collective-permute-start.4 = (bf16[128,1152]{1,0:T(8,128)(2,1)S(1)}, bf16[128,1152]{1,0:T(8,128)(2,1)S(1)}, u32[]{:S(2)}, u32[]{:S(2)}) collective-permute-start(bf16[128,1152]{1,0:T(8,128)(2,1)S(1)} %collective-permute-done.3.refs_0_.refs_6_.refs_3_.refs_7_), channel_id=1, source_target_pairs={{0,16},{8,24},{16,0},{24,8},{1,17},{9,25},{17,1},{25,9},{2,18},{10... | collective-permute-start | bytes 884744 | tf_op jit(solution)/shard_map/ppermute | solution.py:271
  32.5 1.6 %collective-permute-start.10 = (bf16[136,1152]{1,0:T(8,128)(2,1)S(1)}, bf16[136,1152]{1,0:T(8,128)(2,1)S(1)}, u32[]{:S(2)}, u32[]{:S(2)}) collective-permute-start(bf16[136,1152]{1,0:T(8,128)(2,1)S(1)} %collective-permute-done.2.refs_9_.refs_5_), channel_id=1, source_target_pairs={{0,1},{1,0},{2,3},{3,2},{4,5},{5,4},{6,7},{7,6},{8,9},{9,8},{10,11... | collective-permute-start | bytes 940040 | tf_op jit(solution)/shard_map/ppermute | solution.py:271
  32.5 5.7 %collective-permute-start.9 = (bf16[128,1152]{1,0:T(8,128)(2,1)S(1)}, bf16[128,1152]{1,0:T(8,128)(2,1)S(1)}, u32[]{:S(2)}, u32[]{:S(2)}) collective-permute-start(bf16[128,1152]{1,0:T(8,128)(2,1)S(1)} %collective-permute-done.4.refs_5_.refs_9_), channel_id=1, source_target_pairs={{0,1},{1,0},{2,3},{3,2},{4,5},{5,4},{6,7},{7,6},{8,9},{9,8},{10,11... | collective-permute-start | bytes 884744 | tf_op jit(solution)/shard_map/ppermute | solution.py:271
  36.6 10.3 %collective-permute-start.15 = (s16[136,1152]{1,0:T(8,128)(2,1)S(1)}, s16[136,1152]{1,0:T(8,128)(2,1)S(1)}, u32[]{:S(2)}, u32[]{:S(2)}) collective-permute-start(s16[136,1152]{1,0:T(8,128)(2,1)S(1)} %get-tuple-element.45), channel_id=1, source_target_pairs={{0,16},{8,24},{16,0},{24,8},{1,17},{9,25},{17,1},{25,9},{2,18},{10... | collective-permute-start | bytes 940040 | tf_op jit(solution)/shard_map/ppermute | solution.py:271
  40.7 10.4 %collective-permute-start.12 = (s16[136,1152]{1,0:T(8,128)(2,1)S(1)}, s16[136,1152]{1,0:T(8,128)(2,1)S(1)}, u32[]{:S(2)}, u32[]{:S(2)}) collective-permute-start(s16[136,1152]{1,0:T(8,128)(2,1)S(1)} %get-tuple-element.42), channel_id=1, source_target_pairs={{0,8},{8,0},{16,24},{24,16},{1,9},{9,1},{17,25},{25,17},{2,10},{10... | collective-permute-start | bytes 940040 | tf_op jit(solution)/shard_map/ppermute | solution.py:271
  42.1 10.7 %collective-permute-start.14 = (s16[136,1152]{1,0:T(8,128)(2,1)S(1)}, s16[136,1152]{1,0:T(8,128)(2,1)S(1)}, u32[]{:S(2)}, u32[]{:S(2)}) collective-permute-start(s16[136,1152]{1,0:T(8,128)(2,1)S(1)} %get-tuple-element.38.refs_17_), channel_id=1, source_target_pairs={{0,16},{8,24},{16,0},{24,8},{1,17},{9,25},{17,1},{25,9},{2,18},{10... | collective-permute-start | bytes 940040 | tf_op jit(solution)/shard_map/ppermute | solution.py:271
  42.6 21.1 %collective-permute-start.11 = (s16[136,1152]{1,0:T(8,128)(2,1)S(1)}, s16[136,1152]{1,0:T(8,128)(2,1)S(1)}, u32[]{:S(2)}, u32[]{:S(2)}) collective-permute-start(s16[136,1152]{1,0:T(8,128)(2,1)S(1)} %get-tuple-element.40), channel_id=1, source_target_pairs={{0,8},{8,0},{16,24},{24,16},{1,9},{9,1},{17,25},{25,17},{2,10},{10... | collective-permute-start | bytes 940040 | tf_op jit(solution)/shard_map/ppermute | solution.py:271
  47.1 15.6 %collective-permute-start.16 = (s16[136,1152]{1,0:T(8,128)(2,1)S(1)}, s16[136,1152]{1,0:T(8,128)(2,1)S(1)}, u32[]{:S(2)}, u32[]{:S(2)}) collective-permute-start(s16[136,1152]{1,0:T(8,128)(2,1)S(1)} %passed_sum.3), channel_id=1, source_target_pairs={{0,4},{1,5},{2,6},{3,7},{4,0},{5,1},{6,2},{7,3},{8,12},{9,13},{10,... | collective-permute-start | bytes 940040 | tf_op jit(solution)/shard_map/ppermute | solution.py:271
  51.2 13.7 %collective-permute-start.13 = (s16[136,1152]{1,0:T(8,128)(2,1)S(1)}, s16[136,1152]{1,0:T(8,128)(2,1)S(1)}, u32[]{:S(2)}, u32[]{:S(2)}) collective-permute-start(s16[136,1152]{1,0:T(8,128)(2,1)S(1)} %passed_sum.2), channel_id=1, source_target_pairs={{0,2},{1,3},{2,0},{3,1},{4,6},{5,7},{6,4},{7,5},{8,10},{9,11},{10,... | collective-permute-start | bytes 940040 | tf_op jit(solution)/shard_map/ppermute | solution.py:271

commit v6 on v5

--- a/solution.py
+++ b/solution.py
@@ -14,9 +14,11 @@
 LABEL_BASE = 128
 TILE = 256
 LANES = 128
+VMEM_BYTES = 2**26
 SMEM = pl.BlockSpec(memory_space=pltpu.SMEM)
 VMEM = pl.BlockSpec(memory_space=pltpu.VMEM)
 ANY = pl.BlockSpec(memory_space=pl.ANY)
+HBM = pl.BlockSpec(memory_space=pltpu.HBM)
 
 
 def whole(array):
@@ -80,7 +82,7 @@
     return piece(block, (0, size), tile)[...].astype(jnp.int32).astype(jnp.float32) * gain
 
 
-def call(kernel, name, operands, out_shape, scratch, room, cost, after=(), held_back=()):
+def call(kernel, name, operands, out_shape, scratch, room, cost, after=(), held_back=(), limit=None):
     arrays = [a for a, _ in operands]
     held = sum(math.prod(a.shape) * a.dtype.itemsize for a in [*arrays, *out_shape])
 
@@ -97,28 +99,42 @@
             len(arrays) + len(after) + i: len(out_shape) + i for i in range(len(held_back))
         },
         scratch_shapes=scratch,
-        compiler_params=pltpu.CompilerParams(vmem_limit_bytes=held + room),
+        compiler_params=pltpu.CompilerParams(vmem_limit_bytes=limit or held + room),
         cost_estimate=pl.CostEstimate(flops=cost, bytes_accessed=cost, transcendentals=0),
         name=name,
     )(*arrays, *after, *held_back)
 
 
-def labelled(images, labels):
+def staged(images, texts, labels):
     size, width = images.shape
 
-    def kernel(ins, outs):
-        (out,) = outs
-        row = ins[1][...]
-        low, high = lax.rem(row, LABEL_BASE), lax.div(row, LABEL_BASE)
+    def kernel(ins, refs):
+        *outs, row, sems = refs
+        copies = [pltpu.make_async_copy(ins[2], row, sems.at[4])]
+        for k, (source, out, first) in enumerate(((1, 0, 0), (0, 1, 0), (1, 2, 0), (0, 2, size))):
+            target = outs[out].at[pl.ds(first, size)]
+            copies.append(pltpu.make_async_copy(ins[source], target, sems.at[k]))
+        for c in copies:
+            c.start()
+        copies[0].wait()
+        low, high = lax.rem(row[...], LABEL_BASE), lax.div(row[...], LABEL_BASE)
         at = lax.broadcasted_iota(jnp.int32, (EXTRA_ROWS, size), 0)
         parts = jnp.where(at == 0, high, jnp.where(at == 1, low, 0)).astype(jnp.float32)
-        out[pl.ds(0, size), :] = ins[0][...]
-        out[pl.ds(size, EXTRA_ROWS), :] = jnp.zeros((EXTRA_ROWS, width), jnp.bfloat16)
-        out[pl.ds(size, EXTRA_ROWS), pl.ds(0, size)] = parts.astype(jnp.bfloat16)
-
-    shape = jax.ShapeDtypeStruct((size + EXTRA_ROWS, width), jnp.bfloat16)
-    operands = [(images, VMEM), (labels[None, :], VMEM)]
-    return call(kernel, "labelled", operands, [shape], [], 2**21, size)[0]
+        for out, first in ((outs[1], size), (outs[2], 2 * size)):
+            rows = pl.ds(first, EXTRA_ROWS)
+            out[rows, :] = jnp.zeros((EXTRA_ROWS, width), jnp.bfloat16)
+            out[rows, pl.ds(0, size)] = parts.astype(jnp.bfloat16)
+        for c in copies[1:]:
+            c.wait()
+
+    shapes = [
+        jax.ShapeDtypeStruct((n, width), jnp.bfloat16)
+        for n in (size, size + EXTRA_ROWS, 2 * size + EXTRA_ROWS)
+    ]
+    scratch = [pltpu.VMEM((1, size), jnp.int32), pltpu.SemaphoreType.DMA((5,))]
+    operands = [(images, HBM), (texts, HBM), (labels[None, :], HBM)]
+    room = VMEM_BYTES - sum(2 * math.prod(o.shape) for o in shapes) - 2**17
+    return call(kernel, "staged", operands, shapes, scratch, room, size, limit=room)
 
 
 def bundled(texts, images):
@@ -149,7 +165,7 @@
     return parts[0:1] * LABEL_BASE + parts[1:2]
 
 
-def gradient_sums(name, size, scalars, x_blocks, y_blocks, masks, x_images, jobs, before, emits, after=()):
+def gradient_sums(name, size, scalars, x_blocks, y_blocks, masks, x_images, jobs, before, emits, sequence, after=()):
     width = x_blocks[0][0][0].shape[1]
     x_masks, y_masks = masks
     per_tile = TILE // size
@@ -168,6 +184,8 @@
             where[r] = [(result(EXTRA_ROWS, w, jnp.int16), 0, 0) for w in cut]
     operands = Operands()
     slope_at, shift_at = [operands.add(s, SMEM) for s in scalars]
+    for b in sequence:
+        operands.block(b)
     x_views = [operands.block(b) for b in x_blocks]
     y_views = [operands.block(b) for b in y_blocks]
     before_at = {r: operands.add(b, VMEM) for r, b in before.items()}
@@ -271,18 +289,6 @@
     return lax.ppermute(array, axis, [(i, i ^ bit) for i in range(lax.axis_size(axis))])
 
 
-def gathered(own, steps):
-    arrays = [own]
-    for step in steps:
-        arrays = arrays + [swapped(a, step) for a in arrays]
-    return [whole(a) for a in arrays]
-
-
-def other_core(texts, images, core):
-    both = swapped(bundled(texts, images), core)
-    return ((both, 0, 0),), ((both, texts[0][0].shape[0], 0),)
-
-
 def scattered_sum(sharpness, kept, coded, steps):
     def sent(block, step):
         return [(swapped(p, step), 0, 0) for p in block]
@@ -341,11 +347,25 @@
     count = 1 << len(steps[0])
     half = count // 2
     early, late = list(range(half + 1)), list(range(half + 1, count))
-    own = [labelled(picture_vectors, matching_caption), caption_vectors]
-    blocks = [gathered(o, s) for o, s in zip(own, steps)]
+    own_texts, own_images, own_both = staged(picture_vectors, caption_vectors, matching_caption)
+    arrays = [{0: own_images}, {0: own_texts}]
+    for i in range(len(steps[0])):
+        for k in (1, 0):
+            arrays[k][1 << i] = swapped(arrays[k][0], steps[k][i])
     others = [{}, {}]
-    for m in early:
-        others[1][m], others[0][m] = other_core(blocks[1][m], blocks[0][m], core)
+
+    def swap_cores(m, both):
+        both = swapped(both, core)
+        others[1][m], others[0][m] = whole(both), ((both, size, 0),)
+
+    swap_cores(0, own_both)
+    for i in range(1, len(steps[0])):
+        for m in range(1, 1 << i):
+            for k in (1, 0):
+                arrays[k][m | 1 << i] = swapped(arrays[k][m], steps[k][i])
+    blocks = [[whole(a[m]) for m in range(count)] for a in arrays]
+    for m in early[1:]:
+        swap_cores(m, bundled(blocks[1][m], blocks[0][m]))
 
     def sums(name, kind, rows, columns, jobs, before, emits, after=()):
         other = 1 - kind
@@ -364,6 +384,7 @@
             jobs,
             before,
             emits,
+            [blocks[k][m] for m in rows[1:] + rows[:1] for k in (1, 0)],
             after,
         )
 
@@ -372,10 +393,10 @@
         jobs = [(early, list(range(2 * len(early))))]
         results = sums("early_sums", k, early, early, jobs, {}, ["float"] * len(early))
         before.append([s for (s,) in results])
-    arrays = [[b[m][0][0] for m in late] for b in blocks]
+    arrays = [[b[m][0][0] for m in late] for b in blocks[::-1]]
     arrays, before = lax.optimization_barrier((arrays, before))
-    for k in range(2):
-        for m, a in zip(late, arrays[k]):
+    for k in (1, 0):
+        for m, a in zip(late, arrays[1 - k]):
             blocks[k][m] = whole(a)
             others[k][m] = whole(swapped(a, core))
     every = list(range(count))

time: 66.1 us -> 67.2 us (1.017)
  Pallas kernels: 11.4 us -> 13.7 us
  local copies, waits for them, and re-layouts: 1.61 us -> 0.01 us
    pallas_call x12 -> x11, Pallas kernels: 11.4 us -> 13.7 us  [call(): pl.pallas_call(body, out_shape=[*out_shape, *(jax.ShapeDtypeStruct(a.shap...]
    unnamed x6 -> x4, local copies, waits for them, and re-layouts: 1.61 us -> 0.01 us
  transfers between devices with their start and end apart: 17 -> 17, of which waited for: 9 -> 9; matrix products, arithmetic and copies ran while one was open for 0% -> 0% of each run, Pallas kernels for 16% -> 15%
where the time goes in v6:
time: 67.2 us; the launch traced here: 67 us
  waiting for transfers between devices  34.8 us (52%)
  starting transfers between devices  16.4 us (24%)
  Pallas kernels  13.7 us (20%)
  between operations  2.08 us (3%)
    ppermute x17, waiting for transfers between devices, swapped(): lax.ppermute(array, axis, [(i, i ^ bit) for i in range(lax.axis_size(axis...  34.8 us
    ppermute x17, starting transfers between devices, swapped(): lax.ppermute(array, axis, [(i, i ^ bit) for i in range(lax.axis_size(axis...  16.4 us
    pallas_call x11, Pallas kernels, call(): pl.pallas_call(body, out_shape=[*out_shape, *(jax.ShapeDtypeStruct(a.shap...  13.7 us
  transfers between devices with their start and end apart: 17, of which 9 were waited for; matrix products, arithmetic and copies ran while one was open for 0% of the time, Pallas kernels for 15%

profile of v6, /device:TPU:0, one launch (start us, length us, event | category | flops | bytes accessed | tf_op | source)
XLA Modules:
  0.0 67.0 jit_solution(7489940661345517742)
XLA Ops:
  0.6 2.3 %staged.1 = (bf16[128,1152]{1,0:T(8,128)(2,1)}, bf16[136,1152]{1,0:T(8,128)(2,1)}, bf16[264,1152]{1,0:T(8,128)(2,1)}) custom-call(bf16[128,1152]{1,0:T(8,128)(2,1)} %refs_0_.7, bf16[128,1152]{1,0:T(8,128)(2,1)} %refs_1_.5, s32[1,128]{1,0:T(1,128)} %bitcast.1), custom_call_target="tpu_custom_call" | custom-call | flops 128 | bytes 128 | tf_op jit(solution)/shard_map/staged/pallas_call | solution.py:93
  3.0 3.1 %collective-permute-start.1 = (bf16[136,1152]{1,0:T(8,128)(2,1)}, bf16[136,1152]{1,0:T(8,128)(2,1)S(1)}, u32[]{:S(2)}, u32[]{:S(2)}) collective-permute-start(bf16[136,1152]{1,0:T(8,128)(2,1)} %get-tuple-element.28.refs_7_.refs_9_), channel_id=1, source_target_pairs={{0,2},{1,3},{2,0},{3,1},{4,6},{5,7},{6,4},{7,5},{8,10},{9,11},{10,... | collective-permute-start | bytes 940040 | tf_op jit(solution)/shard_map/ppermute | solution.py:289
  6.0 1.5 %collective-permute-start.3 = (bf16[136,1152]{1,0:T(8,128)(2,1)}, bf16[136,1152]{1,0:T(8,128)(2,1)S(1)}, u32[]{:S(2)}, u32[]{:S(2)}) collective-permute-start(bf16[136,1152]{1,0:T(8,128)(2,1)} %get-tuple-element.28.refs_7_.refs_9_), channel_id=1, source_target_pairs={{0,8},{8,0},{16,24},{24,16},{1,9},{9,1},{17,25},{25,17},{2,10},{10... | collective-permute-start | bytes 940040 | tf_op jit(solution)/shard_map/ppermute | solution.py:289
  7.5 2.6 %collective-permute-start = (bf16[128,1152]{1,0:T(8,128)(2,1)}, bf16[128,1152]{1,0:T(8,128)(2,1)S(1)}, u32[]{:S(2)}, u32[]{:S(2)}) collective-permute-start(bf16[128,1152]{1,0:T(8,128)(2,1)} %get-tuple-element.27.refs_6_.refs_8_), channel_id=1, source_target_pairs={{0,4},{1,5},{2,6},{3,7},{4,0},{5,1},{6,2},{7,3},{8,12},{9,13},{10,... | collective-permute-start | bytes 884744 | tf_op jit(solution)/shard_map/ppermute | solution.py:289
  10.1 1.5 %collective-permute-start.2 = (bf16[128,1152]{1,0:T(8,128)(2,1)}, bf16[128,1152]{1,0:T(8,128)(2,1)S(1)}, u32[]{:S(2)}, u32[]{:S(2)}) collective-permute-start(bf16[128,1152]{1,0:T(8,128)(2,1)} %get-tuple-element.27.refs_6_.refs_8_), channel_id=1, source_target_pairs={{0,16},{8,24},{16,0},{24,8},{1,17},{9,25},{17,1},{25,9},{2,18},{10... | collective-permute-start | bytes 884744 | tf_op jit(solution)/shard_map/ppermute | solution.py:289
  11.6 0.0 collective-permute-start.6
  11.6 11.6 %collective-permute-done.refs_0_.refs_2_ = bf16[128,1152]{1,0:T(8,128)(2,1)S(1)} collective-permute-done((bf16[128,1152]{1,0:T(8,128)(2,1)}, bf16[128,1152]{1,0:T(8,128)(2,1)S(1)}, u32[]{:S(2)}, u32[]{:S(2)}) %collective-permute-start) | collective-permute-done | bytes 294944 | tf_op jit(solution)/shard_map/ppermute | solution.py:289
  23.2 0.0 collective-permute-done.1.refs_1_.refs_3_
  23.3 0.0 copy-start
  23.3 0.0 copy-start.1
  23.3 0.1 collective-permute-start.7
  23.4 0.0 collective-permute-done.2.refs_0_.refs_4_
  23.4 0.0 collective-permute-done.3.refs_1_.refs_5_
  23.4 0.5 collective-permute-start.8
  24.0 0.0 collective-permute-start.5
  24.0 1.5 %collective-permute-start.4 = (bf16[128,1152]{1,0:T(8,128)(2,1)S(1)}, bf16[128,1152]{1,0:T(8,128)(2,1)S(1)}, u32[]{:S(2)}, u32[]{:S(2)}) collective-permute-start(bf16[128,1152]{1,0:T(8,128)(2,1)S(1)} %collective-permute-done.refs_0_.refs_2_), channel_id=1, source_target_pairs={{0,16},{8,24},{16,0},{24,8},{1,17},{9,25},{17,1},{25,9},{2,18},{10... | collective-permute-start | bytes 884744 | tf_op jit(solution)/shard_map/ppermute | solution.py:289
  26.8 0.0 collective-permute-done.6.refs_8_.refs_10_
  26.8 0.0 collective-permute-done.7.refs_9_.refs_11_
  26.8 0.0 collective-permute-done.8.refs_10_.refs_12_
  26.8 0.0 copy-done
  26.8 0.0 copy-done.1
  26.9 1.9 %early_sums.3 = (f32[128,1152]{1,0:T(8,128)S(1)}, f32[128,1152]{1,0:T(8,128)S(1)}, f32[128,1152]{1,0:T(8,128)S(1)}) custom-call(f32[1]{0:T(128)S(6)} %copy.7.refs_0_, f32[1]{0:T(128)S(6)} %copy.8.refs_1_, bf16[128,1152]{1,0:T(8,128)(2,1)S(1)} %collective-permute-done.refs_0_.refs_2_, bf16[136,1152]{1,0:T(8,128)(2,1)S(1)} %collective-permute-done.1.refs_1_.refs_3_, ...), custom_call_target="tpu_custom_call" | custom-call | flops 2304 | bytes 2304 | tf_op jit(solution)/shard_map/early_sums/pallas_call | solution.py:93
  28.8 1.9 %early_sums.2 = (f32[128,1152]{1,0:T(8,128)S(1)}, f32[128,1152]{1,0:T(8,128)S(1)}, f32[128,1152]{1,0:T(8,128)S(1)}) custom-call(f32[1]{0:T(128)S(6)} %copy.7.refs_0_, f32[1]{0:T(128)S(6)} %copy.8.refs_1_, bf16[128,1152]{1,0:T(8,128)(2,1)S(1)} %collective-permute-done.refs_0_.refs_2_, bf16[136,1152]{1,0:T(8,128)(2,1)S(1)} %collective-permute-done.1.refs_1_.refs_3_, ...), custom_call_target="tpu_custom_call" | custom-call | flops 2304 | bytes 2304 | tf_op jit(solution)/shard_map/early_sums/pallas_call | solution.py:93
  30.7 2.3 %collective-permute-done.4.refs_6_ = bf16[128,1152]{1,0:T(8,128)(2,1)S(1)} collective-permute-done((bf16[128,1152]{1,0:T(8,128)(2,1)S(1)}, bf16[128,1152]{1,0:T(8,128)(2,1)S(1)}, u32[]{:S(2)}, u32[]{:S(2)}) %collective-permute-start.4) | collective-permute-done | bytes 294944 | tf_op jit(solution)/shard_map/ppermute | solution.py:289
  33.0 0.3 collective-permute-done.5.refs_7_
  33.4 0.0 collective-permute-start.10
  33.4 0.5 collective-permute-start.9
  33.9 1.1 %collective-permute-done.10.refs_13_ = bf16[136,1152]{1,0:T(8,128)(2,1)S(1)} collective-permute-done((bf16[136,1152]{1,0:T(8,128)(2,1)S(1)}, bf16[136,1152]{1,0:T(8,128)(2,1)S(1)}, u32[]{:S(2)}, u32[]{:S(2)}) %collective-permute-start.10) | collective-permute-done | bytes 313376 | tf_op jit(solution)/shard_map/ppermute | solution.py:289
  35.0 2.5 %late_sums.2 = (f32[128,1152]{1,0:T(8,128)S(1)}, f32[128,1152]{1,0:T(8,128)S(1)}, s16[136,1152]{1,0:T(8,128)(2,1)S(1)}, s16[136,1152]{1,0:T(8,128)(2,1)S(1)}) custom-call(f32[1]{0:T(128)S(6)} %copy.7.refs_0_, f32[1]{0:T(128)S(6)} %copy.8.refs_1_, bf16[128,1152]{1,0:T(8,128)(2,1)S(1)} %collective-permute-done.refs_0_.refs_2_, ...), custom_call_target="tpu_custom_call" | custom-call | flops 1792 | bytes 1792 | tf_op jit(solution)/shard_map/late_sums/pallas_call | solution.py:93
  37.5 1.6 %collective-permute-start.15 = (s16[136,1152]{1,0:T(8,128)(2,1)S(1)}, s16[136,1152]{1,0:T(8,128)(2,1)S(1)}, u32[]{:S(2)}, u32[]{:S(2)}) collective-permute-start(s16[136,1152]{1,0:T(8,128)(2,1)S(1)} %get-tuple-element.51), channel_id=1, source_target_pairs={{0,16},{8,24},{16,0},{24,8},{1,17},{9,25},{17,1},{25,9},{2,18},{10... | collective-permute-start | bytes 940040 | tf_op jit(solution)/shard_map/ppermute | solution.py:289
  39.1 0.0 collective-permute-done.9.refs_13_
  39.1 2.5 %late_sums.3 = (f32[128,1152]{1,0:T(8,128)S(1)}, f32[128,1152]{1,0:T(8,128)S(1)}, s16[136,1152]{1,0:T(8,128)(2,1)S(1)}, s16[136,1152]{1,0:T(8,128)(2,1)S(1)}) custom-call(f32[1]{0:T(128)S(6)} %copy.7.refs_0_, f32[1]{0:T(128)S(6)} %copy.8.refs_1_, bf16[128,1152]{1,0:T(8,128)(2,1)S(1)} %collective-permute-done.refs_0_.refs_2_, ...), custom_call_target="tpu_custom_call" | custom-call | flops 1792 | bytes 1792 | tf_op jit(solution)/shard_map/late_sums/pallas_call | solution.py:93
  41.6 1.4 %collective-permute-start.12 = (s16[136,1152]{1,0:T(8,128)(2,1)S(1)}, s16[136,1152]{1,0:T(8,128)(2,1)S(1)}, u32[]{:S(2)}, u32[]{:S(2)}) collective-permute-start(s16[136,1152]{1,0:T(8,128)(2,1)S(1)} %get-tuple-element.48), channel_id=1, source_target_pairs={{0,8},{8,0},{16,24},{24,16},{1,9},{9,1},{17,25},{25,17},{2,10},{10... | collective-permute-start | bytes 940040 | tf_op jit(solution)/shard_map/ppermute | solution.py:289
  43.0 0.5 collective-permute-start.14
  43.5 0.7 %collective-permute-start.11 = (s16[136,1152]{1,0:T(8,128)(2,1)S(1)}, s16[136,1152]{1,0:T(8,128)(2,1)S(1)}, u32[]{:S(2)}, u32[]{:S(2)}) collective-permute-start(s16[136,1152]{1,0:T(8,128)(2,1)S(1)} %get-tuple-element.46), channel_id=1, source_target_pairs={{0,8},{8,0},{16,24},{24,16},{1,9},{9,1},{17,25},{25,17},{2,10},{10... | collective-permute-start | bytes 940040 | tf_op jit(solution)/shard_map/ppermute | solution.py:289
  44.2 3.6 %collective-permute-done.15.refs_1_ = s16[136,1152]{1,0:T(8,128)(2,1)S(1)} collective-permute-done((s16[136,1152]{1,0:T(8,128)(2,1)S(1)}, s16[136,1152]{1,0:T(8,128)(2,1)S(1)}, u32[]{:S(2)}, u32[]{:S(2)}) %collective-permute-start.15) | collective-permute-done | bytes 313376 | tf_op jit(solution)/shard_map/ppermute | solution.py:289
  47.8 0.2 passed_sum.3
  48.0 0.4 collective-permute-start.16
  48.4 3.6 %collective-permute-done.12.refs_1_ = s16[136,1152]{1,0:T(8,128)(2,1)S(1)} collective-permute-done((s16[136,1152]{1,0:T(8,128)(2,1)S(1)}, s16[136,1152]{1,0:T(8,128)(2,1)S(1)}, u32[]{:S(2)}, u32[]{:S(2)}) %collective-permute-start.12) | collective-permute-done | bytes 313376 | tf_op jit(solution)/shard_map/ppermute | solution.py:289
  52.0 0.2 passed_sum.2
  52.1 0.5 collective-permute-start.13
  52.6 1.1 %collective-permute-done.14.refs_2_ = s16[136,1152]{1,0:T(8,128)(2,1)S(1)} collective-permute-done((s16[136,1152]{1,0:T(8,128)(2,1)S(1)}, s16[136,1152]{1,0:T(8,128)(2,1)S(1)}, u32[]{:S(2)}, u32[]{:S(2)}) %collective-permute-start.14) | collective-permute-done | bytes 313376 | tf_op jit(solution)/shard_map/ppermute | solution.py:289
  53.7 9.7 %collective-permute-done.16.refs_3_ = s16[136,1152]{1,0:T(8,128)(2,1)S(1)} collective-permute-done((s16[136,1152]{1,0:T(8,128)(2,1)S(1)}, s16[136,1152]{1,0:T(8,128)(2,1)S(1)}, u32[]{:S(2)}, u32[]{:S(2)}) %collective-permute-start.16) | collective-permute-done | bytes 313376 | tf_op jit(solution)/shard_map/ppermute | solution.py:289
  63.4 1.0 %output_sum.3 = f32[128,1152]{1,0:T(8,128)} custom-call(f32[1]{0:T(128)S(6)} %copy.7.refs_0_, f32[128,1152]{1,0:T(8,128)S(1)} %get-tuple-element.49.refs_1_, s16[136,1152]{1,0:T(8,128)(2,1)S(1)} %collective-permute-done.14.refs_2_, s16[136,1152]{1,0:T(8,128)(2,1)S(1)} %collective-permute-done.16.refs_3_), custom_call_target="tpu_custom_call" | custom-call | flops 128 | bytes 128 | tf_op jit(solution)/shard_map/output_sum/pallas_call | solution.py:93
  64.5 0.0 collective-permute-done.11.refs_2_
  64.5 1.5 %collective-permute-done.13.refs_3_ = s16[136,1152]{1,0:T(8,128)(2,1)S(1)} collective-permute-done((s16[136,1152]{1,0:T(8,128)(2,1)S(1)}, s16[136,1152]{1,0:T(8,128)(2,1)S(1)}, u32[]{:S(2)}, u32[]{:S(2)}) %collective-permute-start.13) | collective-permute-done | bytes 313376 | tf_op jit(solution)/shard_map/ppermute | solution.py:289
  66.0 1.0 %output_sum.2 = f32[128,1152]{1,0:T(8,128)} custom-call(f32[1]{0:T(128)S(6)} %copy.7.refs_0_, f32[128,1152]{1,0:T(8,128)S(1)} %get-tuple-element.45.refs_1_, s16[136,1152]{1,0:T(8,128)(2,1)S(1)} %collective-permute-done.11.refs_2_, s16[136,1152]{1,0:T(8,128)(2,1)S(1)} %collective-permute-done.13.refs_3_), custom_call_target="tpu_custom_call" | custom-call | flops 128 | bytes 128 | tf_op jit(solution)/shard_map/output_sum/pallas_call | solution.py:93
  (2 shorter events, 0.1 us)
Async XLA Ops:
  3.0 20.2 %collective-permute-start.1 = (bf16[136,1152]{1,0:T(8,128)(2,1)}, bf16[136,1152]{1,0:T(8,128)(2,1)S(1)}, u32[]{:S(2)}, u32[]{:S(2)}) collective-permute-start(bf16[136,1152]{1,0:T(8,128)(2,1)} %get-tuple-element.28.refs_7_.refs_9_), channel_id=1, source_target_pairs={{0,2},{1,3},{2,0},{3,1},{4,6},{5,7},{6,4},{7,5},{8,10},{9,11},{10,... | collective-permute-start | bytes 940040 | tf_op jit(solution)/shard_map/ppermute | solution.py:289
  6.0 17.3 %collective-permute-start.3 = (bf16[136,1152]{1,0:T(8,128)(2,1)}, bf16[136,1152]{1,0:T(8,128)(2,1)S(1)}, u32[]{:S(2)}, u32[]{:S(2)}) collective-permute-start(bf16[136,1152]{1,0:T(8,128)(2,1)} %get-tuple-element.28.refs_7_.refs_9_), channel_id=1, source_target_pairs={{0,8},{8,0},{16,24},{24,16},{1,9},{9,1},{17,25},{25,17},{2,10},{10... | collective-permute-start | bytes 940040 | tf_op jit(solution)/shard_map/ppermute | solution.py:289
  7.5 15.7 %collective-permute-start = (bf16[128,1152]{1,0:T(8,128)(2,1)}, bf16[128,1152]{1,0:T(8,128)(2,1)S(1)}, u32[]{:S(2)}, u32[]{:S(2)}) collective-permute-start(bf16[128,1152]{1,0:T(8,128)(2,1)} %get-tuple-element.27.refs_6_.refs_8_), channel_id=1, source_target_pairs={{0,4},{1,5},{2,6},{3,7},{4,0},{5,1},{6,2},{7,3},{8,12},{9,13},{10,... | collective-permute-start | bytes 884744 | tf_op jit(solution)/shard_map/ppermute | solution.py:289
  10.1 13.2 %collective-permute-start.2 = (bf16[128,1152]{1,0:T(8,128)(2,1)}, bf16[128,1152]{1,0:T(8,128)(2,1)S(1)}, u32[]{:S(2)}, u32[]{:S(2)}) collective-permute-start(bf16[128,1152]{1,0:T(8,128)(2,1)} %get-tuple-element.27.refs_6_.refs_8_), channel_id=1, source_target_pairs={{0,16},{8,24},{16,0},{24,8},{1,17},{9,25},{17,1},{25,9},{2,18},{10... | collective-permute-start | bytes 884744 | tf_op jit(solution)/shard_map/ppermute | solution.py:289
  11.6 15.2 %collective-permute-start.6 = (bf16[264,1152]{1,0:T(8,128)(2,1)}, bf16[264,1152]{1,0:T(8,128)(2,1)S(1)}, u32[]{:S(2)}, u32[]{:S(2)}) collective-permute-start(bf16[264,1152]{1,0:T(8,128)(2,1)} %get-tuple-element.29), channel_id=1, source_target_pairs={{0,1},{1,0},{2,3},{3,2},{4,5},{5,4},{6,7},{7,6},{8,9},{9,8},{10,11... | collective-permute-start | bytes 1824776 | tf_op jit(solution)/shard_map/ppermute | solution.py:289
  23.3 3.6 %copy-start = (bf16[136,1152]{1,0:T(8,128)(2,1)S(1)}, bf16[136,1152]{1,0:T(8,128)(2,1)}, u32[]{:S(2)}) copy-start(bf16[136,1152]{1,0:T(8,128)(2,1)} %get-tuple-element.28.refs_7_.refs_9_) | copy-start | bytes 940036
  23.3 3.6 %copy-start.1 = (bf16[128,1152]{1,0:T(8,128)(2,1)S(1)}, bf16[128,1152]{1,0:T(8,128)(2,1)}, u32[]{:S(2)}) copy-start(bf16[128,1152]{1,0:T(8,128)(2,1)} %get-tuple-element.27.refs_6_.refs_8_) | copy-start | bytes 884740
  23.3 3.5 %collective-permute-start.7 = (bf16[264,1152]{1,0:T(8,128)(2,1)S(1)}, bf16[264,1152]{1,0:T(8,128)(2,1)S(1)}, u32[]{:S(2)}, u32[]{:S(2)}) collective-permute-start(bf16[264,1152]{1,0:T(8,128)(2,1)S(1)} %bundled.2), channel_id=1, source_target_pairs={{0,1},{1,0},{2,3},{3,2},{4,5},{5,4},{6,7},{7,6},{8,9},{9,8},{10,11... | collective-permute-start | bytes 1824776 | tf_op jit(solution)/shard_map/ppermute | solution.py:289
  23.4 3.4 %collective-permute-start.8 = (bf16[264,1152]{1,0:T(8,128)(2,1)S(1)}, bf16[264,1152]{1,0:T(8,128)(2,1)S(1)}, u32[]{:S(2)}, u32[]{:S(2)}) collective-permute-start(bf16[264,1152]{1,0:T(8,128)(2,1)S(1)} %bundled.3), channel_id=1, source_target_pairs={{0,1},{1,0},{2,3},{3,2},{4,5},{5,4},{6,7},{7,6},{8,9},{9,8},{10,11... | collective-permute-start | bytes 1824776 | tf_op jit(solution)/shard_map/ppermute | solution.py:289
  24.0 9.4 %collective-permute-start.5 = (bf16[136,1152]{1,0:T(8,128)(2,1)S(1)}, bf16[136,1152]{1,0:T(8,128)(2,1)S(1)}, u32[]{:S(2)}, u32[]{:S(2)}) collective-permute-start(bf16[136,1152]{1,0:T(8,128)(2,1)S(1)} %collective-permute-done.1.refs_1_.refs_3_), channel_id=1, source_target_pairs={{0,8},{8,0},{16,24},{24,16},{1,9},{9,1},{17,25},{25,17},{2,10},{10... | collective-permute-start | bytes 940040 | tf_op jit(solution)/shard_map/ppermute | solution.py:289
  24.0 9.1 %collective-permute-start.4 = (bf16[128,1152]{1,0:T(8,128)(2,1)S(1)}, bf16[128,1152]{1,0:T(8,128)(2,1)S(1)}, u32[]{:S(2)}, u32[]{:S(2)}) collective-permute-start(bf16[128,1152]{1,0:T(8,128)(2,1)S(1)} %collective-permute-done.refs_0_.refs_2_), channel_id=1, source_target_pairs={{0,16},{8,24},{16,0},{24,8},{1,17},{9,25},{17,1},{25,9},{2,18},{10... | collective-permute-start | bytes 884744 | tf_op jit(solution)/shard_map/ppermute | solution.py:289
  33.4 1.6 %collective-permute-start.10 = (bf16[136,1152]{1,0:T(8,128)(2,1)S(1)}, bf16[136,1152]{1,0:T(8,128)(2,1)S(1)}, u32[]{:S(2)}, u32[]{:S(2)}) collective-permute-start(bf16[136,1152]{1,0:T(8,128)(2,1)S(1)} %collective-permute-done.5.refs_7_), channel_id=1, source_target_pairs={{0,1},{1,0},{2,3},{3,2},{4,5},{5,4},{6,7},{7,6},{8,9},{9,8},{10,11... | collective-permute-start | bytes 940040 | tf_op jit(solution)/shard_map/ppermute | solution.py:289
  33.4 5.7 %collective-permute-start.9 = (bf16[128,1152]{1,0:T(8,128)(2,1)S(1)}, bf16[128,1152]{1,0:T(8,128)(2,1)S(1)}, u32[]{:S(2)}, u32[]{:S(2)}) collective-permute-start(bf16[128,1152]{1,0:T(8,128)(2,1)S(1)} %collective-permute-done.4.refs_6_), channel_id=1, source_target_pairs={{0,1},{1,0},{2,3},{3,2},{4,5},{5,4},{6,7},{7,6},{8,9},{9,8},{10,11... | collective-permute-start | bytes 884744 | tf_op jit(solution)/shard_map/ppermute | solution.py:289
  37.5 10.3 %collective-permute-start.15 = (s16[136,1152]{1,0:T(8,128)(2,1)S(1)}, s16[136,1152]{1,0:T(8,128)(2,1)S(1)}, u32[]{:S(2)}, u32[]{:S(2)}) collective-permute-start(s16[136,1152]{1,0:T(8,128)(2,1)S(1)} %get-tuple-element.51), channel_id=1, source_target_pairs={{0,16},{8,24},{16,0},{24,8},{1,17},{9,25},{17,1},{25,9},{2,18},{10... | collective-permute-start | bytes 940040 | tf_op jit(solution)/shard_map/ppermute | solution.py:289
  41.6 10.4 %collective-permute-start.12 = (s16[136,1152]{1,0:T(8,128)(2,1)S(1)}, s16[136,1152]{1,0:T(8,128)(2,1)S(1)}, u32[]{:S(2)}, u32[]{:S(2)}) collective-permute-start(s16[136,1152]{1,0:T(8,128)(2,1)S(1)} %get-tuple-element.48), channel_id=1, source_target_pairs={{0,8},{8,0},{16,24},{24,16},{1,9},{9,1},{17,25},{25,17},{2,10},{10... | collective-permute-start | bytes 940040 | tf_op jit(solution)/shard_map/ppermute | solution.py:289
  43.0 10.7 %collective-permute-start.14 = (s16[136,1152]{1,0:T(8,128)(2,1)S(1)}, s16[136,1152]{1,0:T(8,128)(2,1)S(1)}, u32[]{:S(2)}, u32[]{:S(2)}) collective-permute-start(s16[136,1152]{1,0:T(8,128)(2,1)S(1)} %get-tuple-element.44.refs_17_), channel_id=1, source_target_pairs={{0,16},{8,24},{16,0},{24,8},{1,17},{9,25},{17,1},{25,9},{2,18},{10... | collective-permute-start | bytes 940040 | tf_op jit(solution)/shard_map/ppermute | solution.py:289
  43.5 20.9 %collective-permute-start.11 = (s16[136,1152]{1,0:T(8,128)(2,1)S(1)}, s16[136,1152]{1,0:T(8,128)(2,1)S(1)}, u32[]{:S(2)}, u32[]{:S(2)}) collective-permute-start(s16[136,1152]{1,0:T(8,128)(2,1)S(1)} %get-tuple-element.46), channel_id=1, source_target_pairs={{0,8},{8,0},{16,24},{24,16},{1,9},{9,1},{17,25},{25,17},{2,10},{10... | collective-permute-start | bytes 940040 | tf_op jit(solution)/shard_map/ppermute | solution.py:289
  48.0 15.4 %collective-permute-start.16 = (s16[136,1152]{1,0:T(8,128)(2,1)S(1)}, s16[136,1152]{1,0:T(8,128)(2,1)S(1)}, u32[]{:S(2)}, u32[]{:S(2)}) collective-permute-start(s16[136,1152]{1,0:T(8,128)(2,1)S(1)} %passed_sum.3), channel_id=1, source_target_pairs={{0,4},{1,5},{2,6},{3,7},{4,0},{5,1},{6,2},{7,3},{8,12},{9,13},{10,... | collective-permute-start | bytes 940040 | tf_op jit(solution)/shard_map/ppermute | solution.py:289
  52.1 13.8 %collective-permute-start.13 = (s16[136,1152]{1,0:T(8,128)(2,1)S(1)}, s16[136,1152]{1,0:T(8,128)(2,1)S(1)}, u32[]{:S(2)}, u32[]{:S(2)}) collective-permute-start(s16[136,1152]{1,0:T(8,128)(2,1)S(1)} %passed_sum.2), channel_id=1, source_target_pairs={{0,2},{1,3},{2,0},{3,1},{4,6},{5,7},{6,4},{7,5},{8,10},{9,11},{10,... | collective-permute-start | bytes 940040 | tf_op jit(solution)/shard_map/ppermute | solution.py:289

commit v7 on v5

--- a/solution.py
+++ b/solution.py
@@ -14,6 +14,7 @@
 LABEL_BASE = 128
 TILE = 256
 LANES = 128
+BUNDLE_COST = 6 * 10**8
 SMEM = pl.BlockSpec(memory_space=pltpu.SMEM)
 VMEM = pl.BlockSpec(memory_space=pltpu.VMEM)
 ANY = pl.BlockSpec(memory_space=pl.ANY)
@@ -103,37 +104,36 @@
     )(*arrays, *after, *held_back)
 
 
-def labelled(images, labels):
+def labelled(images, labels, after=()):
     size, width = images.shape
 
     def kernel(ins, outs):
-        (out,) = outs
+        outs[0][pl.ds(0, size), :] = ins[0][...]
+        outs[0][pl.ds(size, EXTRA_ROWS), :] = jnp.zeros((EXTRA_ROWS, width), jnp.bfloat16)
         row = ins[1][...]
         low, high = lax.rem(row, LABEL_BASE), lax.div(row, LABEL_BASE)
         at = lax.broadcasted_iota(jnp.int32, (EXTRA_ROWS, size), 0)
         parts = jnp.where(at == 0, high, jnp.where(at == 1, low, 0)).astype(jnp.float32)
-        out[pl.ds(0, size), :] = ins[0][...]
-        out[pl.ds(size, EXTRA_ROWS), :] = jnp.zeros((EXTRA_ROWS, width), jnp.bfloat16)
-        out[pl.ds(size, EXTRA_ROWS), pl.ds(0, size)] = parts.astype(jnp.bfloat16)
+        outs[0][pl.ds(size, EXTRA_ROWS), pl.ds(0, size)] = parts.astype(jnp.bfloat16)
 
     shape = jax.ShapeDtypeStruct((size + EXTRA_ROWS, width), jnp.bfloat16)
-    operands = [(images, VMEM), (labels[None, :], VMEM)]
-    return call(kernel, "labelled", operands, [shape], [], 2**21, size)[0]
-
-
-def bundled(texts, images):
-    size, width = texts[0][0].shape[0], texts[0][0].shape[1]
-    operands = Operands()
-    views = [operands.block(texts), operands.block(images)]
+    operands = [(images, VMEM), (labels, VMEM)]
+    return call(kernel, "labelled", operands, [shape], [], 2**21, size, after)[0]
+
+
+def bundled(texts, images, cost, after=()):
+    arrays = (texts, images)
+    width = arrays[0].shape[1]
 
     def kernel(ins, outs):
-        for view, first, count in zip(views, (0, size), (size, size + EXTRA_ROWS)):
-            ((ref, row, column),) = view(ins)
-            outs[0][pl.ds(first, count), :] = ref[pl.ds(row, count), pl.ds(column, width)]
-
-    shape = jax.ShapeDtypeStruct((2 * size + EXTRA_ROWS, width), jnp.bfloat16)
-    (both,) = call(kernel, "bundled", operands.pairs, [shape], [], 2**21, size)
-    return both
+        first = 0
+        for ref in ins:
+            outs[0][pl.ds(first, ref.shape[0]), :] = ref[...]
+            first += ref.shape[0]
+
+    shape = jax.ShapeDtypeStruct((sum(a.shape[0] for a in arrays), width), jnp.bfloat16)
+    operands = [(a, VMEM) for a in arrays]
+    return call(kernel, "bundled", operands, [shape], [], 2**21, cost, after)[0]
 
 
 def first_row(mask, size):
@@ -149,7 +149,7 @@
     return parts[0:1] * LABEL_BASE + parts[1:2]
 
 
-def gradient_sums(name, size, scalars, x_blocks, y_blocks, masks, x_images, jobs, before, emits, after=()):
+def gradient_sums(name, size, scalars, x_blocks, y_blocks, masks, x_images, jobs, before, emits, sequence, after=()):
     width = x_blocks[0][0][0].shape[1]
     x_masks, y_masks = masks
     per_tile = TILE // size
@@ -168,6 +168,8 @@
             where[r] = [(result(EXTRA_ROWS, w, jnp.int16), 0, 0) for w in cut]
     operands = Operands()
     slope_at, shift_at = [operands.add(s, SMEM) for s in scalars]
+    for b in sequence:
+        operands.block(b)
     x_views = [operands.block(b) for b in x_blocks]
     y_views = [operands.block(b) for b in y_blocks]
     before_at = {r: operands.add(b, VMEM) for r, b in before.items()}
@@ -203,8 +205,9 @@
                 for i in range(len(rows)):
                     z = scores[i * size : (i + 1) * size] * slope + shift
                     sig = 1.0 / (1.0 + jnp.exp2(-z))
-                    w = jnp.where(jnp.tile(keys[i], (1, per_tile)) == other, sig - 1.0, sig)
-                    weights[pl.ds(i * size, size), pl.ds(n * size, TILE)] = w.astype(jnp.bfloat16)
+                    w = jnp.where(jnp.tile(keys[i], (1, len(chosen))) == other, sig - 1.0, sig)
+                    there = pl.ds(n * size, len(chosen) * size)
+                    weights[pl.ds(i * size, size), there] = w.astype(jnp.bfloat16)
             for tile in column_tiles(width):
                 sums = jnp.dot(
                     weights[pl.ds(0, len(rows) * size), pl.ds(0, len(columns) * size)],
@@ -269,18 +272,6 @@
 def swapped(array, step):
     axis, bit = step
     return lax.ppermute(array, axis, [(i, i ^ bit) for i in range(lax.axis_size(axis))])
-
-
-def gathered(own, steps):
-    arrays = [own]
-    for step in steps:
-        arrays = arrays + [swapped(a, step) for a in arrays]
-    return [whole(a) for a in arrays]
-
-
-def other_core(texts, images, core):
-    both = swapped(bundled(texts, images), core)
-    return ((both, 0, 0),), ((both, texts[0][0].shape[0], 0),)
 
 
 def scattered_sum(sharpness, kept, coded, steps):
@@ -341,18 +332,30 @@
     count = 1 << len(steps[0])
     half = count // 2
     early, late = list(range(half + 1)), list(range(half + 1, count))
-    own = [labelled(picture_vectors, matching_caption), caption_vectors]
-    blocks = [gathered(o, s) for o, s in zip(own, steps)]
+    labels = matching_caption[None, :]
+    first_texts = swapped(caption_vectors, steps[1][0])
+    first_images = [swapped(a, steps[0][0]) for a in (picture_vectors, labels)]
+    arrays = [{0: labelled(picture_vectors, labels), 1: labelled(*first_images, [first_texts])}, {0: caption_vectors, 1: first_texts}]
+    for i in range(1, len(steps[0])):
+        for k in (1, 0):
+            for m in range(1 << i):
+                arrays[k][m | 1 << i] = swapped(arrays[k][m], steps[k][i])
+    blocks = [[whole(a[m]) for m in range(count)] for a in arrays]
     others = [{}, {}]
     for m in early:
-        others[1][m], others[0][m] = other_core(blocks[1][m], blocks[0][m], core)
-
-    def sums(name, kind, rows, columns, jobs, before, emits, after=()):
+        if m == 0:
+            cost, after = size, [arrays[1][half]]
+        else:
+            cost, after = (BUNDLE_COST if m == 1 else size), []
+        both = swapped(bundled(arrays[1][m], arrays[0][m], cost, after), core)
+        others[1][m], others[0][m] = whole(both), ((both, size, 0),)
+
+    def sums(name, kind, rows, columns, cores, jobs, before, emits, after=()):
         other = 1 - kind
         x_blocks = [blocks[kind][m] for m in rows]
-        y_blocks = [blocks[other][m] for m in columns] + [others[other][m] for m in columns]
+        y_blocks = [(blocks, others)[c][other][m] for c in cores for m in columns]
         x_masks = [masks[kind][m] for m in rows]
-        y_masks = [masks[other][m + shift] for shift in (0, count) for m in columns]
+        y_masks = [masks[other][m + c * count] for c in cores for m in columns]
         return gradient_sums(
             name,
             size,
@@ -364,18 +367,20 @@
             jobs,
             before,
             emits,
+            [blocks[k][m] for m in rows[1:] + rows[:1] for k in (1, 0)],
             after,
         )
 
-    before = []
-    for k in range(2):
-        jobs = [(early, list(range(2 * len(early))))]
-        results = sums("early_sums", k, early, early, jobs, {}, ["float"] * len(early))
-        before.append([s for (s,) in results])
-    arrays = [[b[m][0][0] for m in late] for b in blocks]
+    before = [{}, {}]
+    for c in range(2):
+        for k in range(2):
+            jobs = [(early, early)]
+            results = sums("early_sums", k, early, early, [c], jobs, before[k], ["float"] * len(early))
+            before[k] = {m: s for m, (s,) in zip(early, results)}
+    arrays = [[b[m][0][0] for m in late] for b in blocks[::-1]]
     arrays, before = lax.optimization_barrier((arrays, before))
-    for k in range(2):
-        for m, a in zip(late, arrays[k]):
+    for k in (1, 0):
+        for m, a in zip(late, arrays[1 - k]):
             blocks[k][m] = whole(a)
             others[k][m] = whole(swapped(a, core))
     every = list(range(count))
@@ -384,7 +389,7 @@
     for k, cut in ((1, "whole"), (0, "whole")):
         emits = ["float"] * half + ["whole"] + [cut] * len(late)
         results = sums(
-            "late_sums", k, every, every, jobs, dict(zip(early, before[k])), emits, after
+            "late_sums", k, every, every, (0, 1), jobs, before[k], emits, after
         )
         kept[k] = [s for (s,) in results[:half]]
         coded[k] = results[half:]

time: 66.1 us -> 63.2 us (0.956)
  waiting for transfers between devices: 34.4 us -> 26.2 us
  starting transfers between devices: 16.5 us -> 20.6 us
  Pallas kernels: 11.4 us -> 13.1 us
    ppermute x17 -> x18, waiting for transfers between devices: 34.4 us -> 26.2 us  [swapped(): lax.ppermute(array, axis, [(i, i ^ bit) for i in range(lax.axis_size(axis...]
    ppermute x17 -> x18, starting transfers between devices: 16.5 us -> 20.6 us  [swapped(): lax.ppermute(array, axis, [(i, i ^ bit) for i in range(lax.axis_size(axis...]
    pallas_call x12 -> x15, Pallas kernels: 11.4 us -> 13.1 us  [call(): pl.pallas_call(body, out_shape=[*out_shape, *(jax.ShapeDtypeStruct(a.shap...]
  transfers between devices with their start and end apart: 17 -> 18, of which waited for: 9 -> 8; matrix products, arithmetic and copies ran while one was open for 0% -> 0% of each run, Pallas kernels for 16% -> 19%
where the time goes in v7:
time: 63.2 us; the launch traced here: 63 us
  waiting for transfers between devices  26.2 us (41%)
  starting transfers between devices  20.6 us (33%)
  Pallas kernels  13.1 us (21%)
  between operations  2.07 us (3%)
  local copies, waits for them, and re-layouts  1 us (2%)
    ppermute x18, waiting for transfers between devices, swapped(): lax.ppermute(array, axis, [(i, i ^ bit) for i in range(lax.axis_size(axis...  26.2 us
    ppermute x18, starting transfers between devices, swapped(): lax.ppermute(array, axis, [(i, i ^ bit) for i in range(lax.axis_size(axis...  20.6 us
    pallas_call x15, Pallas kernels, call(): pl.pallas_call(body, out_shape=[*out_shape, *(jax.ShapeDtypeStruct(a.shap...  13.1 us
  transfers between devices with their start and end apart: 18, of which 8 were waited for; matrix products, arithmetic and copies ran while one was open for 0% of the time, Pallas kernels for 19%

profile of v7, /device:TPU:0, one launch (start us, length us, event | category | flops | bytes accessed | tf_op | source)
XLA Modules:
  0.0 63.0 jit_solution(5686118899287577198)
XLA Ops:
  0.6 0.0 copy-start.2
  0.6 4.1 %collective-permute-start = (bf16[128,1152]{1,0:T(8,128)(2,1)}, bf16[128,1152]{1,0:T(8,128)(2,1)S(1)}, u32[]{:S(2)}, u32[]{:S(2)}) collective-permute-start(bf16[128,1152]{1,0:T(8,128)(2,1)} %refs_8_.3), channel_id=1, source_target_pairs={{0,4},{1,5},{2,6},{3,7},{4,0},{5,1},{6,2},{7,3},{8,12},{9,13},{10,... | collective-permute-start | bytes 884744 | tf_op jit(solution)/shard_map/ppermute | solution.py:274
  4.7 1.6 %collective-permute-start.1 = (bf16[128,1152]{1,0:T(8,128)(2,1)}, bf16[128,1152]{1,0:T(8,128)(2,1)S(1)}, u32[]{:S(2)}, u32[]{:S(2)}) collective-permute-start(bf16[128,1152]{1,0:T(8,128)(2,1)} %refs_0_.10), channel_id=1, source_target_pairs={{0,2},{1,3},{2,0},{3,1},{4,6},{5,7},{6,4},{7,5},{8,10},{9,11},{10,... | collective-permute-start | bytes 884744 | tf_op jit(solution)/shard_map/ppermute | solution.py:274
  6.3 0.0 copy-done.2
  6.3 0.0 copy-start.1
  6.3 1.0 %copy-done.1 = bf16[128,1152]{1,0:T(8,128)(2,1)S(1)} copy-done((bf16[128,1152]{1,0:T(8,128)(2,1)S(1)}, bf16[128,1152]{1,0:T(8,128)(2,1)}, u32[]{:S(2)}) %copy-start.1) | copy-done | bytes 294936
  7.3 0.0 copy-start
  7.3 1.6 %collective-permute-start.4 = (bf16[136,1152]{1,0:T(8,128)(2,1)S(1)}, bf16[136,1152]{1,0:T(8,128)(2,1)S(1)}, u32[]{:S(2)}, u32[]{:S(2)}) collective-permute-start(bf16[136,1152]{1,0:T(8,128)(2,1)S(1)} %labelled.3.refs_1_.refs_7_.refs_9_), channel_id=1, source_target_pairs={{0,8},{8,0},{16,24},{24,16},{1,9},{9,1},{17,25},{25,17},{2,10},{10... | collective-permute-start | bytes 940040 | tf_op jit(solution)/shard_map/ppermute | solution.py:274
  8.9 0.0 copy-done
  8.9 1.5 %collective-permute-start.3 = (bf16[128,1152]{1,0:T(8,128)(2,1)S(1)}, bf16[128,1152]{1,0:T(8,128)(2,1)S(1)}, u32[]{:S(2)}, u32[]{:S(2)}) collective-permute-start(bf16[128,1152]{1,0:T(8,128)(2,1)S(1)} %copy-done), channel_id=1, source_target_pairs={{0,16},{8,24},{16,0},{24,8},{1,17},{9,25},{17,1},{25,9},{2,18},{10... | collective-permute-start | bytes 884744 | tf_op jit(solution)/shard_map/ppermute | solution.py:274
  10.4 0.4 collective-permute-start.2
  10.9 7.8 %collective-permute-done.2.refs_1_ = s32[1,128]{1,0:T(1,128)S(1)} collective-permute-done((s32[1,128]{1,0:T(1,128)S(1)}, s32[1,128]{1,0:T(1,128)S(1)}, u32[]{:S(2)}, u32[]{:S(2)}) %collective-permute-start.2) | collective-permute-done | bytes 544 | tf_op jit(solution)/shard_map/ppermute | solution.py:274
  18.6 0.0 collective-permute-done.refs_2_.refs_0_
  18.6 0.0 collective-permute-done.1.refs_0_
  18.7 0.1 collective-permute-start.8
  18.8 0.0 collective-permute-done.3.refs_2_.refs_0_.refs_4_
  18.9 0.5 collective-permute-start.7
  19.4 0.0 collective-permute-done.4.refs_1_.refs_5_
  19.5 0.1 collective-permute-start.9
  19.6 1.6 %collective-permute-start.6 = (bf16[136,1152]{1,0:T(8,128)(2,1)S(1)}, bf16[136,1152]{1,0:T(8,128)(2,1)S(1)}, u32[]{:S(2)}, u32[]{:S(2)}) collective-permute-start(bf16[136,1152]{1,0:T(8,128)(2,1)S(1)} %labelled.2.refs_1_.refs_3_), channel_id=1, source_target_pairs={{0,8},{8,0},{16,24},{24,16},{1,9},{9,1},{17,25},{25,17},{2,10},{10... | collective-permute-start | bytes 940040 | tf_op jit(solution)/shard_map/ppermute | solution.py:274
  21.2 1.5 %collective-permute-start.5 = (bf16[128,1152]{1,0:T(8,128)(2,1)S(1)}, bf16[128,1152]{1,0:T(8,128)(2,1)S(1)}, u32[]{:S(2)}, u32[]{:S(2)}) collective-permute-start(bf16[128,1152]{1,0:T(8,128)(2,1)S(1)} %collective-permute-done.refs_2_.refs_0_), channel_id=1, source_target_pairs={{0,16},{8,24},{16,0},{24,8},{1,17},{9,25},{17,1},{25,9},{2,18},{10... | collective-permute-start | bytes 884744 | tf_op jit(solution)/shard_map/ppermute | solution.py:274
  24.0 1.4 %early_sums.6 = (f32[128,1152]{1,0:T(8,128)S(1)}, f32[128,1152]{1,0:T(8,128)S(1)}, f32[128,1152]{1,0:T(8,128)S(1)}) custom-call(f32[1]{0:T(128)S(6)} %copy.7.refs_0_, f32[1]{0:T(128)S(6)} %copy.8.refs_1_, bf16[128,1152]{1,0:T(8,128)(2,1)S(1)} %collective-permute-done.refs_2_.refs_0_, bf16[136,1152]{1,0:T(8,128)(2,1)S(1)} %labelled.2.refs_1_.refs_3_, ...), custom_call_target="tpu_custom_call" | custom-call | flops 1152 | bytes 1152 | tf_op jit(solution)/shard_map/early_sums/pallas_call | solution.py:92
  25.4 1.4 %early_sums.4 = (f32[128,1152]{1,0:T(8,128)S(1)}, f32[128,1152]{1,0:T(8,128)S(1)}, f32[128,1152]{1,0:T(8,128)S(1)}) custom-call(f32[1]{0:T(128)S(6)} %copy.7.refs_0_, f32[1]{0:T(128)S(6)} %copy.8.refs_1_, bf16[128,1152]{1,0:T(8,128)(2,1)S(1)} %collective-permute-done.refs_2_.refs_0_, bf16[136,1152]{1,0:T(8,128)(2,1)S(1)} %labelled.2.refs_1_.refs_3_, ...), custom_call_target="tpu_custom_call" | custom-call | flops 1152 | bytes 1152 | tf_op jit(solution)/shard_map/early_sums/pallas_call | solution.py:92
  26.8 0.0 collective-permute-done.8.refs_9_.refs_11_
  26.8 0.0 collective-permute-done.7.refs_8_.refs_10_
  26.8 0.0 collective-permute-done.9.refs_10_.refs_12_
  26.8 1.4 %early_sums.7 = (f32[128,1152]{1,0:T(8,128)S(1)}, f32[128,1152]{1,0:T(8,128)S(1)}, f32[128,1152]{1,0:T(8,128)S(1)}) custom-call(f32[1]{0:T(128)S(6)} %copy.7.refs_0_, f32[1]{0:T(128)S(6)} %copy.8.refs_1_, bf16[128,1152]{1,0:T(8,128)(2,1)S(1)} %collective-permute-done.refs_2_.refs_0_, bf16[136,1152]{1,0:T(8,128)(2,1)S(1)} %labelled.2.refs_1_.refs_3_, ...), custom_call_target="tpu_custom_call" | custom-call | flops 1152 | bytes 1152 | tf_op jit(solution)/shard_map/early_sums/pallas_call | solution.py:92
  28.2 1.4 %early_sums.5 = (f32[128,1152]{1,0:T(8,128)S(1)}, f32[128,1152]{1,0:T(8,128)S(1)}, f32[128,1152]{1,0:T(8,128)S(1)}) custom-call(f32[1]{0:T(128)S(6)} %copy.7.refs_0_, f32[1]{0:T(128)S(6)} %copy.8.refs_1_, bf16[128,1152]{1,0:T(8,128)(2,1)S(1)} %collective-permute-done.refs_2_.refs_0_, bf16[136,1152]{1,0:T(8,128)(2,1)S(1)} %labelled.2.refs_1_.refs_3_, ...), custom_call_target="tpu_custom_call" | custom-call | flops 1152 | bytes 1152 | tf_op jit(solution)/shard_map/early_sums/pallas_call | solution.py:92
  29.6 0.7 %collective-permute-done.5.refs_6_ = bf16[128,1152]{1,0:T(8,128)(2,1)S(1)} collective-permute-done((bf16[128,1152]{1,0:T(8,128)(2,1)S(1)}, bf16[128,1152]{1,0:T(8,128)(2,1)S(1)}, u32[]{:S(2)}, u32[]{:S(2)}) %collective-permute-start.5) | collective-permute-done | bytes 294944 | tf_op jit(solution)/shard_map/ppermute | solution.py:274
  30.2 0.0 collective-permute-done.6.refs_7_
  30.3 0.0 collective-permute-start.11
  30.3 0.5 collective-permute-start.10
  30.8 1.1 %collective-permute-done.11.refs_13_ = bf16[136,1152]{1,0:T(8,128)(2,1)S(1)} collective-permute-done((bf16[136,1152]{1,0:T(8,128)(2,1)S(1)}, bf16[136,1152]{1,0:T(8,128)(2,1)S(1)}, u32[]{:S(2)}, u32[]{:S(2)}) %collective-permute-start.11) | collective-permute-done | bytes 313376 | tf_op jit(solution)/shard_map/ppermute | solution.py:274
  31.9 2.5 %late_sums.2 = (f32[128,1152]{1,0:T(8,128)S(1)}, f32[128,1152]{1,0:T(8,128)S(1)}, s16[136,1152]{1,0:T(8,128)(2,1)S(1)}, s16[136,1152]{1,0:T(8,128)(2,1)S(1)}) custom-call(f32[1]{0:T(128)S(6)} %copy.7.refs_0_, f32[1]{0:T(128)S(6)} %copy.8.refs_1_, bf16[128,1152]{1,0:T(8,128)(2,1)S(1)} %collective-permute-done.refs_2_.refs_0_, ...), custom_call_target="tpu_custom_call" | custom-call | flops 1792 | bytes 1792 | tf_op jit(solution)/shard_map/late_sums/pallas_call | solution.py:92
  34.4 1.6 %collective-permute-start.16 = (s16[136,1152]{1,0:T(8,128)(2,1)S(1)}, s16[136,1152]{1,0:T(8,128)(2,1)S(1)}, u32[]{:S(2)}, u32[]{:S(2)}) collective-permute-start(s16[136,1152]{1,0:T(8,128)(2,1)S(1)} %get-tuple-element.57), channel_id=1, source_target_pairs={{0,16},{8,24},{16,0},{24,8},{1,17},{9,25},{17,1},{25,9},{2,18},{10... | collective-permute-start | bytes 940040 | tf_op jit(solution)/shard_map/ppermute | solution.py:274
  36.0 0.0 collective-permute-done.10.refs_13_
  36.0 2.5 %late_sums.3 = (f32[128,1152]{1,0:T(8,128)S(1)}, f32[128,1152]{1,0:T(8,128)S(1)}, s16[136,1152]{1,0:T(8,128)(2,1)S(1)}, s16[136,1152]{1,0:T(8,128)(2,1)S(1)}) custom-call(f32[1]{0:T(128)S(6)} %copy.7.refs_0_, f32[1]{0:T(128)S(6)} %copy.8.refs_1_, bf16[128,1152]{1,0:T(8,128)(2,1)S(1)} %collective-permute-done.refs_2_.refs_0_, ...), custom_call_target="tpu_custom_call" | custom-call | flops 1792 | bytes 1792 | tf_op jit(solution)/shard_map/late_sums/pallas_call | solution.py:92
  38.5 0.7 %collective-permute-start.13 = (s16[136,1152]{1,0:T(8,128)(2,1)S(1)}, s16[136,1152]{1,0:T(8,128)(2,1)S(1)}, u32[]{:S(2)}, u32[]{:S(2)}) collective-permute-start(s16[136,1152]{1,0:T(8,128)(2,1)S(1)} %get-tuple-element.54), channel_id=1, source_target_pairs={{0,8},{8,0},{16,24},{24,16},{1,9},{9,1},{17,25},{25,17},{2,10},{10... | collective-permute-start | bytes 940040 | tf_op jit(solution)/shard_map/ppermute | solution.py:274
  39.2 0.5 collective-permute-start.15
  39.7 1.4 %collective-permute-start.12 = (s16[136,1152]{1,0:T(8,128)(2,1)S(1)}, s16[136,1152]{1,0:T(8,128)(2,1)S(1)}, u32[]{:S(2)}, u32[]{:S(2)}) collective-permute-start(s16[136,1152]{1,0:T(8,128)(2,1)S(1)} %get-tuple-element.52), channel_id=1, source_target_pairs={{0,8},{8,0},{16,24},{24,16},{1,9},{9,1},{17,25},{25,17},{2,10},{10... | collective-permute-start | bytes 940040 | tf_op jit(solution)/shard_map/ppermute | solution.py:274
  41.1 3.6 %collective-permute-done.16.refs_1_ = s16[136,1152]{1,0:T(8,128)(2,1)S(1)} collective-permute-done((s16[136,1152]{1,0:T(8,128)(2,1)S(1)}, s16[136,1152]{1,0:T(8,128)(2,1)S(1)}, u32[]{:S(2)}, u32[]{:S(2)}) %collective-permute-start.16) | collective-permute-done | bytes 313376 | tf_op jit(solution)/shard_map/ppermute | solution.py:274
  44.7 0.2 passed_sum.3
  44.9 1.4 %collective-permute-start.17 = (s16[136,1152]{1,0:T(8,128)(2,1)S(1)}, s16[136,1152]{1,0:T(8,128)(2,1)S(1)}, u32[]{:S(2)}, u32[]{:S(2)}) collective-permute-start(s16[136,1152]{1,0:T(8,128)(2,1)S(1)} %passed_sum.3), channel_id=1, source_target_pairs={{0,4},{1,5},{2,6},{3,7},{4,0},{5,1},{6,2},{7,3},{8,12},{9,13},{10,... | collective-permute-start | bytes 940040 | tf_op jit(solution)/shard_map/ppermute | solution.py:274
  46.3 2.6 %collective-permute-done.13.refs_1_ = s16[136,1152]{1,0:T(8,128)(2,1)S(1)} collective-permute-done((s16[136,1152]{1,0:T(8,128)(2,1)S(1)}, s16[136,1152]{1,0:T(8,128)(2,1)S(1)}, u32[]{:S(2)}, u32[]{:S(2)}) %collective-permute-start.13) | collective-permute-done | bytes 313376 | tf_op jit(solution)/shard_map/ppermute | solution.py:274
  48.8 0.2 passed_sum.2
  49.0 1.5 %collective-permute-start.14 = (s16[136,1152]{1,0:T(8,128)(2,1)S(1)}, s16[136,1152]{1,0:T(8,128)(2,1)S(1)}, u32[]{:S(2)}, u32[]{:S(2)}) collective-permute-start(s16[136,1152]{1,0:T(8,128)(2,1)S(1)} %passed_sum.2), channel_id=1, source_target_pairs={{0,2},{1,3},{2,0},{3,1},{4,6},{5,7},{6,4},{7,5},{8,10},{9,11},{10,... | collective-permute-start | bytes 940040 | tf_op jit(solution)/shard_map/ppermute | solution.py:274
  50.5 0.1 collective-permute-done.15.refs_2_
  50.6 9.9 %collective-permute-done.17.refs_3_ = s16[136,1152]{1,0:T(8,128)(2,1)S(1)} collective-permute-done((s16[136,1152]{1,0:T(8,128)(2,1)S(1)}, s16[136,1152]{1,0:T(8,128)(2,1)S(1)}, u32[]{:S(2)}, u32[]{:S(2)}) %collective-permute-start.17) | collective-permute-done | bytes 313376 | tf_op jit(solution)/shard_map/ppermute | solution.py:274
  60.5 1.0 %output_sum.3 = f32[128,1152]{1,0:T(8,128)} custom-call(f32[1]{0:T(128)S(6)} %copy.7.refs_0_, f32[128,1152]{1,0:T(8,128)S(1)} %get-tuple-element.55.refs_1_, s16[136,1152]{1,0:T(8,128)(2,1)S(1)} %collective-permute-done.15.refs_2_, s16[136,1152]{1,0:T(8,128)(2,1)S(1)} %collective-permute-done.17.refs_3_), custom_call_target="tpu_custom_call" | custom-call | flops 128 | bytes 128 | tf_op jit(solution)/shard_map/output_sum/pallas_call | solution.py:92
  61.5 0.0 collective-permute-done.12.refs_2_
  61.5 0.5 collective-permute-done.14.refs_3_
  62.0 1.0 %output_sum.2 = f32[128,1152]{1,0:T(8,128)} custom-call(f32[1]{0:T(128)S(6)} %copy.7.refs_0_, f32[128,1152]{1,0:T(8,128)S(1)} %get-tuple-element.51.refs_1_, s16[136,1152]{1,0:T(8,128)(2,1)S(1)} %collective-permute-done.12.refs_2_, s16[136,1152]{1,0:T(8,128)(2,1)S(1)} %collective-permute-done.14.refs_3_), custom_call_target="tpu_custom_call" | custom-call | flops 128 | bytes 128 | tf_op jit(solution)/shard_map/output_sum/pallas_call | solution.py:92
  (5 shorter events, 0.2 us)
Async XLA Ops:
  0.6 5.7 %copy-start.2 = (s32[128]{0:T(128)S(1)}, s32[128]{0:T(128)}, u32[]{:S(2)}) copy-start(s32[128]{0:T(128)} %param.7) | copy-start | bytes 1540
  0.6 18.0 %collective-permute-start = (bf16[128,1152]{1,0:T(8,128)(2,1)}, bf16[128,1152]{1,0:T(8,128)(2,1)S(1)}, u32[]{:S(2)}, u32[]{:S(2)}) collective-permute-start(bf16[128,1152]{1,0:T(8,128)(2,1)} %refs_8_.3), channel_id=1, source_target_pairs={{0,4},{1,5},{2,6},{3,7},{4,0},{5,1},{6,2},{7,3},{8,12},{9,13},{10,... | collective-permute-start | bytes 884744 | tf_op jit(solution)/shard_map/ppermute | solution.py:274
  4.7 13.9 %collective-permute-start.1 = (bf16[128,1152]{1,0:T(8,128)(2,1)}, bf16[128,1152]{1,0:T(8,128)(2,1)S(1)}, u32[]{:S(2)}, u32[]{:S(2)}) collective-permute-start(bf16[128,1152]{1,0:T(8,128)(2,1)} %refs_0_.10), channel_id=1, source_target_pairs={{0,2},{1,3},{2,0},{3,1},{4,6},{5,7},{6,4},{7,5},{8,10},{9,11},{10,... | collective-permute-start | bytes 884744 | tf_op jit(solution)/shard_map/ppermute | solution.py:274
  6.3 1.0 %copy-start.1 = (bf16[128,1152]{1,0:T(8,128)(2,1)S(1)}, bf16[128,1152]{1,0:T(8,128)(2,1)}, u32[]{:S(2)}) copy-start(bf16[128,1152]{1,0:T(8,128)(2,1)} %refs_0_.10) | copy-start | bytes 884740
  7.3 1.6 %copy-start = (bf16[128,1152]{1,0:T(8,128)(2,1)S(1)}, bf16[128,1152]{1,0:T(8,128)(2,1)}, u32[]{:S(2)}) copy-start(bf16[128,1152]{1,0:T(8,128)(2,1)} %refs_8_.3) | copy-start | bytes 884740
  7.3 12.1 %collective-permute-start.4 = (bf16[136,1152]{1,0:T(8,128)(2,1)S(1)}, bf16[136,1152]{1,0:T(8,128)(2,1)S(1)}, u32[]{:S(2)}, u32[]{:S(2)}) collective-permute-start(bf16[136,1152]{1,0:T(8,128)(2,1)S(1)} %labelled.3.refs_1_.refs_7_.refs_9_), channel_id=1, source_target_pairs={{0,8},{8,0},{16,24},{24,16},{1,9},{9,1},{17,25},{25,17},{2,10},{10... | collective-permute-start | bytes 940040 | tf_op jit(solution)/shard_map/ppermute | solution.py:274
  8.9 9.9 %collective-permute-start.3 = (bf16[128,1152]{1,0:T(8,128)(2,1)S(1)}, bf16[128,1152]{1,0:T(8,128)(2,1)S(1)}, u32[]{:S(2)}, u32[]{:S(2)}) collective-permute-start(bf16[128,1152]{1,0:T(8,128)(2,1)S(1)} %copy-done), channel_id=1, source_target_pairs={{0,16},{8,24},{16,0},{24,8},{1,17},{9,25},{17,1},{25,9},{2,18},{10... | collective-permute-start | bytes 884744 | tf_op jit(solution)/shard_map/ppermute | solution.py:274
  10.4 8.2 %collective-permute-start.2 = (s32[1,128]{1,0:T(1,128)S(1)}, s32[1,128]{1,0:T(1,128)S(1)}, u32[]{:S(2)}, u32[]{:S(2)}) collective-permute-start(s32[1,128]{1,0:T(1,128)S(1)} %bitcast.2), channel_id=1, source_target_pairs={{0,2},{1,3},{2,0},{3,1},{4,6},{5,7},{6,4},{7,5},{8,10},{9,11},{10,... | collective-permute-start | bytes 1544 | tf_op jit(solution)/shard_map/ppermute | solution.py:274
  18.7 8.0 %collective-permute-start.8 = (bf16[264,1152]{1,0:T(8,128)(2,1)S(1)}, bf16[264,1152]{1,0:T(8,128)(2,1)S(1)}, u32[]{:S(2)}, u32[]{:S(2)}) collective-permute-start(bf16[264,1152]{1,0:T(8,128)(2,1)S(1)} %bundled.4), channel_id=1, source_target_pairs={{0,1},{1,0},{2,3},{3,2},{4,5},{5,4},{6,7},{7,6},{8,9},{9,8},{10,11... | collective-permute-start | bytes 1824776 | tf_op jit(solution)/shard_map/ppermute | solution.py:274
  18.9 7.9 %collective-permute-start.7 = (bf16[264,1152]{1,0:T(8,128)(2,1)S(1)}, bf16[264,1152]{1,0:T(8,128)(2,1)S(1)}, u32[]{:S(2)}, u32[]{:S(2)}) collective-permute-start(bf16[264,1152]{1,0:T(8,128)(2,1)S(1)} %bundled.3), channel_id=1, source_target_pairs={{0,1},{1,0},{2,3},{3,2},{4,5},{5,4},{6,7},{7,6},{8,9},{9,8},{10,11... | collective-permute-start | bytes 1824776 | tf_op jit(solution)/shard_map/ppermute | solution.py:274
  19.5 7.3 %collective-permute-start.9 = (bf16[264,1152]{1,0:T(8,128)(2,1)S(1)}, bf16[264,1152]{1,0:T(8,128)(2,1)S(1)}, u32[]{:S(2)}, u32[]{:S(2)}) collective-permute-start(bf16[264,1152]{1,0:T(8,128)(2,1)S(1)} %bundled.5), channel_id=1, source_target_pairs={{0,1},{1,0},{2,3},{3,2},{4,5},{5,4},{6,7},{7,6},{8,9},{9,8},{10,11... | collective-permute-start | bytes 1824776 | tf_op jit(solution)/shard_map/ppermute | solution.py:274
  19.6 10.7 %collective-permute-start.6 = (bf16[136,1152]{1,0:T(8,128)(2,1)S(1)}, bf16[136,1152]{1,0:T(8,128)(2,1)S(1)}, u32[]{:S(2)}, u32[]{:S(2)}) collective-permute-start(bf16[136,1152]{1,0:T(8,128)(2,1)S(1)} %labelled.2.refs_1_.refs_3_), channel_id=1, source_target_pairs={{0,8},{8,0},{16,24},{24,16},{1,9},{9,1},{17,25},{25,17},{2,10},{10... | collective-permute-start | bytes 940040 | tf_op jit(solution)/shard_map/ppermute | solution.py:274
  21.2 9.1 %collective-permute-start.5 = (bf16[128,1152]{1,0:T(8,128)(2,1)S(1)}, bf16[128,1152]{1,0:T(8,128)(2,1)S(1)}, u32[]{:S(2)}, u32[]{:S(2)}) collective-permute-start(bf16[128,1152]{1,0:T(8,128)(2,1)S(1)} %collective-permute-done.refs_2_.refs_0_), channel_id=1, source_target_pairs={{0,16},{8,24},{16,0},{24,8},{1,17},{9,25},{17,1},{25,9},{2,18},{10... | collective-permute-start | bytes 884744 | tf_op jit(solution)/shard_map/ppermute | solution.py:274
  30.3 1.6 %collective-permute-start.11 = (bf16[136,1152]{1,0:T(8,128)(2,1)S(1)}, bf16[136,1152]{1,0:T(8,128)(2,1)S(1)}, u32[]{:S(2)}, u32[]{:S(2)}) collective-permute-start(bf16[136,1152]{1,0:T(8,128)(2,1)S(1)} %collective-permute-done.6.refs_7_), channel_id=1, source_target_pairs={{0,1},{1,0},{2,3},{3,2},{4,5},{5,4},{6,7},{7,6},{8,9},{9,8},{10,11... | collective-permute-start | bytes 940040 | tf_op jit(solution)/shard_map/ppermute | solution.py:274
  30.3 5.7 %collective-permute-start.10 = (bf16[128,1152]{1,0:T(8,128)(2,1)S(1)}, bf16[128,1152]{1,0:T(8,128)(2,1)S(1)}, u32[]{:S(2)}, u32[]{:S(2)}) collective-permute-start(bf16[128,1152]{1,0:T(8,128)(2,1)S(1)} %collective-permute-done.5.refs_6_), channel_id=1, source_target_pairs={{0,1},{1,0},{2,3},{3,2},{4,5},{5,4},{6,7},{7,6},{8,9},{9,8},{10,11... | collective-permute-start | bytes 884744 | tf_op jit(solution)/shard_map/ppermute | solution.py:274
  34.4 10.3 %collective-permute-start.16 = (s16[136,1152]{1,0:T(8,128)(2,1)S(1)}, s16[136,1152]{1,0:T(8,128)(2,1)S(1)}, u32[]{:S(2)}, u32[]{:S(2)}) collective-permute-start(s16[136,1152]{1,0:T(8,128)(2,1)S(1)} %get-tuple-element.57), channel_id=1, source_target_pairs={{0,16},{8,24},{16,0},{24,8},{1,17},{9,25},{17,1},{25,9},{2,18},{10... | collective-permute-start | bytes 940040 | tf_op jit(solution)/shard_map/ppermute | solution.py:274
  38.5 10.4 %collective-permute-start.13 = (s16[136,1152]{1,0:T(8,128)(2,1)S(1)}, s16[136,1152]{1,0:T(8,128)(2,1)S(1)}, u32[]{:S(2)}, u32[]{:S(2)}) collective-permute-start(s16[136,1152]{1,0:T(8,128)(2,1)S(1)} %get-tuple-element.54), channel_id=1, source_target_pairs={{0,8},{8,0},{16,24},{24,16},{1,9},{9,1},{17,25},{25,17},{2,10},{10... | collective-permute-start | bytes 940040 | tf_op jit(solution)/shard_map/ppermute | solution.py:274
  39.2 11.4 %collective-permute-start.15 = (s16[136,1152]{1,0:T(8,128)(2,1)S(1)}, s16[136,1152]{1,0:T(8,128)(2,1)S(1)}, u32[]{:S(2)}, u32[]{:S(2)}) collective-permute-start(s16[136,1152]{1,0:T(8,128)(2,1)S(1)} %get-tuple-element.50.refs_17_), channel_id=1, source_target_pairs={{0,16},{8,24},{16,0},{24,8},{1,17},{9,25},{17,1},{25,9},{2,18},{10... | collective-permute-start | bytes 940040 | tf_op jit(solution)/shard_map/ppermute | solution.py:274
  39.7 21.8 %collective-permute-start.12 = (s16[136,1152]{1,0:T(8,128)(2,1)S(1)}, s16[136,1152]{1,0:T(8,128)(2,1)S(1)}, u32[]{:S(2)}, u32[]{:S(2)}) collective-permute-start(s16[136,1152]{1,0:T(8,128)(2,1)S(1)} %get-tuple-element.52), channel_id=1, source_target_pairs={{0,8},{8,0},{16,24},{24,16},{1,9},{9,1},{17,25},{25,17},{2,10},{10... | collective-permute-start | bytes 940040 | tf_op jit(solution)/shard_map/ppermute | solution.py:274
  44.9 15.6 %collective-permute-start.17 = (s16[136,1152]{1,0:T(8,128)(2,1)S(1)}, s16[136,1152]{1,0:T(8,128)(2,1)S(1)}, u32[]{:S(2)}, u32[]{:S(2)}) collective-permute-start(s16[136,1152]{1,0:T(8,128)(2,1)S(1)} %passed_sum.3), channel_id=1, source_target_pairs={{0,4},{1,5},{2,6},{3,7},{4,0},{5,1},{6,2},{7,3},{8,12},{9,13},{10,... | collective-permute-start | bytes 940040 | tf_op jit(solution)/shard_map/ppermute | solution.py:274
  49.0 13.0 %collective-permute-start.14 = (s16[136,1152]{1,0:T(8,128)(2,1)S(1)}, s16[136,1152]{1,0:T(8,128)(2,1)S(1)}, u32[]{:S(2)}, u32[]{:S(2)}) collective-permute-start(s16[136,1152]{1,0:T(8,128)(2,1)S(1)} %passed_sum.2), channel_id=1, source_target_pairs={{0,2},{1,3},{2,0},{3,1},{4,6},{5,7},{6,4},{7,5},{8,10},{9,11},{10,... | collective-permute-start | bytes 940040 | tf_op jit(solution)/shard_map/ppermute | solution.py:274

commit v8 on v7

--- a/solution.py
+++ b/solution.py
@@ -121,8 +121,7 @@
     return call(kernel, "labelled", operands, [shape], [], 2**21, size, after)[0]
 
 
-def bundled(texts, images, cost, after=()):
-    arrays = (texts, images)
+def bundled(arrays, cost):
     width = arrays[0].shape[1]
 
     def kernel(ins, outs):
@@ -133,7 +132,7 @@
 
     shape = jax.ShapeDtypeStruct((sum(a.shape[0] for a in arrays), width), jnp.bfloat16)
     operands = [(a, VMEM) for a in arrays]
-    return call(kernel, "bundled", operands, [shape], [], 2**21, cost, after)[0]
+    return call(kernel, "bundled", operands, [shape], [], 2**21, cost)[0]
 
 
 def first_row(mask, size):
@@ -251,22 +250,22 @@
     return call(kernel, "passed_sum", operands.pairs, [shape], [], 2**21, size, (), held_back)
 
 
-def output_sum(sharpness, kept, received):
-    size, width = kept.shape
+def output_sums(sharpness, sums):
+    size, width = sums[0][0].shape
     operands = Operands()
     sharpness_at = operands.add(sharpness, SMEM)
-    kept_at = operands.add(kept, VMEM)
-    views = [operands.block(b) for b in received]
+    views = [(operands.add(kept, VMEM), [operands.block(b) for b in blocks]) for kept, blocks in sums]
 
     def kernel(ins, outs):
-        for tile in column_tiles(width):
-            total = piece(whole(ins[kept_at]), (0, size), tile)[...]
-            for view in views:
-                total = total + decoded(view(ins), size, tile)
-            piece(whole(outs[0]), (0, size), tile)[...] = total * ins[sharpness_at][0]
-
-    shape = jax.ShapeDtypeStruct((size, width), jnp.float32)
-    return call(kernel, "output_sum", operands.pairs, [shape], [], 2**21, size)[0]
+        for out, (kept_at, received) in zip(outs, views):
+            for tile in column_tiles(width):
+                total = piece(whole(ins[kept_at]), (0, size), tile)[...]
+                for view in received:
+                    total = total + decoded(view(ins), size, tile)
+                piece(whole(out), (0, size), tile)[...] = total * ins[sharpness_at][0]
+
+    shapes = [jax.ShapeDtypeStruct((size, width), jnp.float32)] * len(sums)
+    return call(kernel, "output_sums", operands.pairs, shapes, [], 2**21, size)
 
 
 def swapped(array, step):
@@ -274,7 +273,7 @@
     return lax.ppermute(array, axis, [(i, i ^ bit) for i in range(lax.axis_size(axis))])
 
 
-def scattered_sum(sharpness, kept, coded, steps):
+def scattered(kept, coded, steps):
     def sent(block, step):
         return [(swapped(p, step), 0, 0) for p in block]
 
@@ -305,7 +304,7 @@
                 else:
                     passed += passed_sum(kept[n], received[n], p)
             received[m].append(sent(passed, steps[s]))
-    return output_sum(sharpness, kept[0], received[0])
+    return kept[0], received[0]
 
 
 def bit_steps(axis):
@@ -342,13 +341,12 @@
                 arrays[k][m | 1 << i] = swapped(arrays[k][m], steps[k][i])
     blocks = [[whole(a[m]) for m in range(count)] for a in arrays]
     others = [{}, {}]
-    for m in early:
-        if m == 0:
-            cost, after = size, [arrays[1][half]]
-        else:
-            cost, after = (BUNDLE_COST if m == 1 else size), []
-        both = swapped(bundled(arrays[1][m], arrays[0][m], cost, after), core)
-        others[1][m], others[0][m] = whole(both), ((both, size, 0),)
+    both = bundled([arrays[1][1], arrays[0][1]], BUNDLE_COST)
+    rest = [m for m in early if m != 1]
+    both = swapped(bundled([both] + [arrays[k][m] for m in rest for k in (1, 0)], size), core)
+    for i, m in enumerate([1] + rest):
+        row = i * (2 * size + EXTRA_ROWS)
+        others[1][m], others[0][m] = ((both, row, 0),), ((both, row + size, 0),)
 
     def sums(name, kind, rows, columns, cores, jobs, before, emits, after=()):
         other = 1 - kind
@@ -371,12 +369,11 @@
             after,
         )
 
-    before = [{}, {}]
-    for c in range(2):
-        for k in range(2):
-            jobs = [(early, early)]
-            results = sums("early_sums", k, early, early, [c], jobs, before[k], ["float"] * len(early))
-            before[k] = {m: s for m, (s,) in zip(early, results)}
+    before = []
+    for k in range(2):
+        jobs = [(early, list(range(2 * len(early))))]
+        results = sums("early_sums", k, early, early, (0, 1), jobs, {}, ["float"] * len(early))
+        before.append({m: s for m, (s,) in zip(early, results)})
     arrays = [[b[m][0][0] for m in late] for b in blocks[::-1]]
     arrays, before = lax.optimization_barrier((arrays, before))
     for k in (1, 0):
@@ -394,7 +391,7 @@
         kept[k] = [s for (s,) in results[:half]]
         coded[k] = results[half:]
         after = coded[k][0]
-    return tuple(scattered_sum(scalars[0], kept[k], coded[k], steps[k]) for k in range(2))
+    return tuple(output_sums(scalars[0], [scattered(kept[k], coded[k], steps[k]) for k in range(2)]))
 
 
 def solution(mesh):

time: 63.2 us -> 62.8 us (level)
  Pallas kernels: 13.1 us -> 10.7 us
  waiting for transfers between devices: 26.2 us -> 28.2 us
  local copies, waits for them, and re-layouts: 1 us -> 1.65 us
    pallas_call x15 -> x11, Pallas kernels: 13.1 us -> 10.7 us  [call(): pl.pallas_call(body, out_shape=[*out_shape, *(jax.ShapeDtypeStruct(a.shap...]
    ppermute x18 -> x16, waiting for transfers between devices: 26.2 us -> 28.2 us  [swapped(): lax.ppermute(array, axis, [(i, i ^ bit) for i in range(lax.axis_size(axis...]
    unnamed x6, local copies, waits for them, and re-layouts: 1 us -> 1.65 us
    ppermute x18 -> x16, starting transfers between devices: 20.6 us -> 20 us  [swapped(): lax.ppermute(array, axis, [(i, i ^ bit) for i in range(lax.axis_size(axis...]
  transfers between devices with their start and end apart: 18 -> 16, of which waited for: 8 -> 8; matrix products, arithmetic and copies ran while one was open for 0% -> 0% of each run, Pallas kernels for 19% -> 15%
where the time goes in v8:
time: 62.8 us; the launch traced here: 62.6 us
  waiting for transfers between devices  28.2 us (45%)
  starting transfers between devices  20 us (32%)
  Pallas kernels  10.7 us (17%)
  between operations  2.04 us (3%)
  local copies, waits for them, and re-layouts  1.65 us (3%)
    ppermute x16, waiting for transfers between devices, swapped(): lax.ppermute(array, axis, [(i, i ^ bit) for i in range(lax.axis_size(axis...  28.2 us
    ppermute x16, starting transfers between devices, swapped(): lax.ppermute(array, axis, [(i, i ^ bit) for i in range(lax.axis_size(axis...  20 us
    pallas_call x11, Pallas kernels, call(): pl.pallas_call(body, out_shape=[*out_shape, *(jax.ShapeDtypeStruct(a.shap...  10.7 us
    unnamed x6, local copies, waits for them, and re-layouts  1.65 us
  transfers between devices with their start and end apart: 16, of which 8 were waited for; matrix products, arithmetic and copies ran while one was open for 0% of the time, Pallas kernels for 15%

profile of v8, /device:TPU:0, one launch (start us, length us, event | category | flops | bytes accessed | tf_op | source)
XLA Modules:
  0.0 62.6 jit_solution(1400205667715647247)
XLA Ops:
  0.6 4.1 %collective-permute-start = (bf16[128,1152]{1,0:T(8,128)(2,1)}, bf16[128,1152]{1,0:T(8,128)(2,1)S(1)}, u32[]{:S(2)}, u32[]{:S(2)}) collective-permute-start(bf16[128,1152]{1,0:T(8,128)(2,1)} %refs_8_.3), channel_id=1, source_target_pairs={{0,4},{1,5},{2,6},{3,7},{4,0},{5,1},{6,2},{7,3},{8,12},{9,13},{10,... | collective-permute-start | bytes 884744 | tf_op jit(solution)/shard_map/ppermute | solution.py:273
  4.7 1.6 %collective-permute-start.1 = (bf16[128,1152]{1,0:T(8,128)(2,1)}, bf16[128,1152]{1,0:T(8,128)(2,1)S(1)}, u32[]{:S(2)}, u32[]{:S(2)}) collective-permute-start(bf16[128,1152]{1,0:T(8,128)(2,1)} %refs_0_.6), channel_id=1, source_target_pairs={{0,2},{1,3},{2,0},{3,1},{4,6},{5,7},{6,4},{7,5},{8,10},{9,11},{10,... | collective-permute-start | bytes 884744 | tf_op jit(solution)/shard_map/ppermute | solution.py:273
  6.3 0.0 copy-start.1
  6.3 1.0 %copy-done.1 = bf16[128,1152]{1,0:T(8,128)(2,1)S(1)} copy-done((bf16[128,1152]{1,0:T(8,128)(2,1)S(1)}, bf16[128,1152]{1,0:T(8,128)(2,1)}, u32[]{:S(2)}) %copy-start.1) | copy-done | bytes 294936
  7.3 0.0 copy-start.2
  7.3 0.7 %copy-done.2 = s32[128]{0:T(128)S(1)} copy-done((s32[128]{0:T(128)S(1)}, s32[128]{0:T(128)}, u32[]{:S(2)}) %copy-start.2) | copy-done | bytes 536
  8.0 0.0 copy-start
  8.0 1.6 %collective-permute-start.4 = (bf16[136,1152]{1,0:T(8,128)(2,1)S(1)}, bf16[136,1152]{1,0:T(8,128)(2,1)S(1)}, u32[]{:S(2)}, u32[]{:S(2)}) collective-permute-start(bf16[136,1152]{1,0:T(8,128)(2,1)S(1)} %labelled.3.refs_2_.refs_7_.refs_9_), channel_id=1, source_target_pairs={{0,8},{8,0},{16,24},{24,16},{1,9},{9,1},{17,25},{25,17},{2,10},{10... | collective-permute-start | bytes 940040 | tf_op jit(solution)/shard_map/ppermute | solution.py:273
  9.6 1.5 %collective-permute-start.3 = (bf16[128,1152]{1,0:T(8,128)(2,1)}, bf16[128,1152]{1,0:T(8,128)(2,1)S(1)}, u32[]{:S(2)}, u32[]{:S(2)}) collective-permute-start(bf16[128,1152]{1,0:T(8,128)(2,1)} %refs_8_.3), channel_id=1, source_target_pairs={{0,16},{8,24},{16,0},{24,8},{1,17},{9,25},{17,1},{25,9},{2,18},{10... | collective-permute-start | bytes 884744 | tf_op jit(solution)/shard_map/ppermute | solution.py:273
  11.1 0.4 collective-permute-start.2
  11.5 7.1 %collective-permute-done.2.refs_1_ = s32[1,128]{1,0:T(1,128)S(1)} collective-permute-done((s32[1,128]{1,0:T(1,128)S(1)}, s32[1,128]{1,0:T(1,128)S(1)}, u32[]{:S(2)}, u32[]{:S(2)}) %collective-permute-start.2) | collective-permute-done | bytes 544 | tf_op jit(solution)/shard_map/ppermute | solution.py:273
  18.6 0.0 collective-permute-done.refs_2_.refs_0_
  18.6 0.0 collective-permute-done.1.refs_0_
  18.7 0.0 collective-permute-done.3.refs_3_.refs_4_
  18.7 0.0 collective-permute-done.4.refs_4_.refs_5_
  18.8 0.0 copy-done
  18.8 0.1 bundled.3
  18.9 0.1 collective-permute-start.7
  19.0 1.6 %collective-permute-start.6 = (bf16[136,1152]{1,0:T(8,128)(2,1)S(1)}, bf16[136,1152]{1,0:T(8,128)(2,1)S(1)}, u32[]{:S(2)}, u32[]{:S(2)}) collective-permute-start(bf16[136,1152]{1,0:T(8,128)(2,1)S(1)} %labelled.2.refs_1_.refs_3_), channel_id=1, source_target_pairs={{0,8},{8,0},{16,24},{24,16},{1,9},{9,1},{17,25},{25,17},{2,10},{10... | collective-permute-start | bytes 940040 | tf_op jit(solution)/shard_map/ppermute | solution.py:273
  20.6 1.5 %collective-permute-start.5 = (bf16[128,1152]{1,0:T(8,128)(2,1)S(1)}, bf16[128,1152]{1,0:T(8,128)(2,1)S(1)}, u32[]{:S(2)}, u32[]{:S(2)}) collective-permute-start(bf16[128,1152]{1,0:T(8,128)(2,1)S(1)} %collective-permute-done.refs_2_.refs_0_), channel_id=1, source_target_pairs={{0,16},{8,24},{16,0},{24,8},{1,17},{9,25},{17,1},{25,9},{2,18},{10... | collective-permute-start | bytes 884744 | tf_op jit(solution)/shard_map/ppermute | solution.py:273
  23.4 0.0 collective-permute-done.7.refs_8_.refs_10_
  23.4 1.9 %early_sums.3 = (f32[128,1152]{1,0:T(8,128)S(1)}, f32[128,1152]{1,0:T(8,128)S(1)}, f32[128,1152]{1,0:T(8,128)S(1)}) custom-call(f32[1]{0:T(128)S(6)} %copy.7.refs_0_, f32[1]{0:T(128)S(6)} %copy.8.refs_1_, bf16[128,1152]{1,0:T(8,128)(2,1)S(1)} %collective-permute-done.refs_2_.refs_0_, bf16[136,1152]{1,0:T(8,128)(2,1)S(1)} %labelled.2.refs_1_.refs_3_, ...), custom_call_target="tpu_custom_call" | custom-call | flops 2304 | bytes 2304 | tf_op jit(solution)/shard_map/early_sums/pallas_call | solution.py:92
  25.3 1.9 %early_sums.2 = (f32[128,1152]{1,0:T(8,128)S(1)}, f32[128,1152]{1,0:T(8,128)S(1)}, f32[128,1152]{1,0:T(8,128)S(1)}) custom-call(f32[1]{0:T(128)S(6)} %copy.7.refs_0_, f32[1]{0:T(128)S(6)} %copy.8.refs_1_, bf16[128,1152]{1,0:T(8,128)(2,1)S(1)} %collective-permute-done.refs_2_.refs_0_, bf16[136,1152]{1,0:T(8,128)(2,1)S(1)} %labelled.2.refs_1_.refs_3_, ...), custom_call_target="tpu_custom_call" | custom-call | flops 2304 | bytes 2304 | tf_op jit(solution)/shard_map/early_sums/pallas_call | solution.py:92
  27.3 2.4 %collective-permute-done.5.refs_6_ = bf16[128,1152]{1,0:T(8,128)(2,1)S(1)} collective-permute-done((bf16[128,1152]{1,0:T(8,128)(2,1)S(1)}, bf16[128,1152]{1,0:T(8,128)(2,1)S(1)}, u32[]{:S(2)}, u32[]{:S(2)}) %collective-permute-start.5) | collective-permute-done | bytes 294944 | tf_op jit(solution)/shard_map/ppermute | solution.py:273
  29.7 0.0 collective-permute-done.6.refs_7_
  29.7 0.0 collective-permute-start.9
  29.7 0.5 collective-permute-start.8
  30.2 1.1 %collective-permute-done.9.refs_11_ = bf16[136,1152]{1,0:T(8,128)(2,1)S(1)} collective-permute-done((bf16[136,1152]{1,0:T(8,128)(2,1)S(1)}, bf16[136,1152]{1,0:T(8,128)(2,1)S(1)}, u32[]{:S(2)}, u32[]{:S(2)}) %collective-permute-start.9) | collective-permute-done | bytes 313376 | tf_op jit(solution)/shard_map/ppermute | solution.py:273
  31.3 2.5 %late_sums.2 = (f32[128,1152]{1,0:T(8,128)S(1)}, f32[128,1152]{1,0:T(8,128)S(1)}, s16[136,1152]{1,0:T(8,128)(2,1)S(1)}, s16[136,1152]{1,0:T(8,128)(2,1)S(1)}) custom-call(f32[1]{0:T(128)S(6)} %copy.7.refs_0_, f32[1]{0:T(128)S(6)} %copy.8.refs_1_, bf16[128,1152]{1,0:T(8,128)(2,1)S(1)} %collective-permute-done.refs_2_.refs_0_, ...), custom_call_target="tpu_custom_call" | custom-call | flops 1792 | bytes 1792 | tf_op jit(solution)/shard_map/late_sums/pallas_call | solution.py:92
  33.8 1.6 %collective-permute-start.14 = (s16[136,1152]{1,0:T(8,128)(2,1)S(1)}, s16[136,1152]{1,0:T(8,128)(2,1)S(1)}, u32[]{:S(2)}, u32[]{:S(2)}) collective-permute-start(s16[136,1152]{1,0:T(8,128)(2,1)S(1)} %get-tuple-element.45), channel_id=1, source_target_pairs={{0,16},{8,24},{16,0},{24,8},{1,17},{9,25},{17,1},{25,9},{2,18},{10... | collective-permute-start | bytes 940040 | tf_op jit(solution)/shard_map/ppermute | solution.py:273
  35.4 0.0 collective-permute-done.8.refs_11_
  35.4 2.5 %late_sums.3 = (f32[128,1152]{1,0:T(8,128)S(1)}, f32[128,1152]{1,0:T(8,128)S(1)}, s16[136,1152]{1,0:T(8,128)(2,1)S(1)}, s16[136,1152]{1,0:T(8,128)(2,1)S(1)}) custom-call(f32[1]{0:T(128)S(6)} %copy.7.refs_0_, f32[1]{0:T(128)S(6)} %copy.8.refs_1_, bf16[128,1152]{1,0:T(8,128)(2,1)S(1)} %collective-permute-done.refs_2_.refs_0_, ...), custom_call_target="tpu_custom_call" | custom-call | flops 1792 | bytes 1792 | tf_op jit(solution)/shard_map/late_sums/pallas_call | solution.py:92
  37.9 0.7 %collective-permute-start.11 = (s16[136,1152]{1,0:T(8,128)(2,1)S(1)}, s16[136,1152]{1,0:T(8,128)(2,1)S(1)}, u32[]{:S(2)}, u32[]{:S(2)}) collective-permute-start(s16[136,1152]{1,0:T(8,128)(2,1)S(1)} %get-tuple-element.42), channel_id=1, source_target_pairs={{0,8},{8,0},{16,24},{24,16},{1,9},{9,1},{17,25},{25,17},{2,10},{10... | collective-permute-start | bytes 940040 | tf_op jit(solution)/shard_map/ppermute | solution.py:273
  38.6 0.5 collective-permute-start.13
  39.2 1.4 %collective-permute-start.10 = (s16[136,1152]{1,0:T(8,128)(2,1)S(1)}, s16[136,1152]{1,0:T(8,128)(2,1)S(1)}, u32[]{:S(2)}, u32[]{:S(2)}) collective-permute-start(s16[136,1152]{1,0:T(8,128)(2,1)S(1)} %get-tuple-element.40), channel_id=1, source_target_pairs={{0,8},{8,0},{16,24},{24,16},{1,9},{9,1},{17,25},{25,17},{2,10},{10... | collective-permute-start | bytes 940040 | tf_op jit(solution)/shard_map/ppermute | solution.py:273
  40.5 3.6 %collective-permute-done.14.refs_1_ = s16[136,1152]{1,0:T(8,128)(2,1)S(1)} collective-permute-done((s16[136,1152]{1,0:T(8,128)(2,1)S(1)}, s16[136,1152]{1,0:T(8,128)(2,1)S(1)}, u32[]{:S(2)}, u32[]{:S(2)}) %collective-permute-start.14) | collective-permute-done | bytes 313376 | tf_op jit(solution)/shard_map/ppermute | solution.py:273
  44.1 0.2 passed_sum.3
  44.3 1.4 %collective-permute-start.15 = (s16[136,1152]{1,0:T(8,128)(2,1)S(1)}, s16[136,1152]{1,0:T(8,128)(2,1)S(1)}, u32[]{:S(2)}, u32[]{:S(2)}) collective-permute-start(s16[136,1152]{1,0:T(8,128)(2,1)S(1)} %passed_sum.3), channel_id=1, source_target_pairs={{0,4},{1,5},{2,6},{3,7},{4,0},{5,1},{6,2},{7,3},{8,12},{9,13},{10,... | collective-permute-start | bytes 940040 | tf_op jit(solution)/shard_map/ppermute | solution.py:273
  45.7 2.6 %collective-permute-done.11.refs_1_ = s16[136,1152]{1,0:T(8,128)(2,1)S(1)} collective-permute-done((s16[136,1152]{1,0:T(8,128)(2,1)S(1)}, s16[136,1152]{1,0:T(8,128)(2,1)S(1)}, u32[]{:S(2)}, u32[]{:S(2)}) %collective-permute-start.11) | collective-permute-done | bytes 313376 | tf_op jit(solution)/shard_map/ppermute | solution.py:273
  48.2 0.2 passed_sum.2
  48.4 1.5 %collective-permute-start.12 = (s16[136,1152]{1,0:T(8,128)(2,1)S(1)}, s16[136,1152]{1,0:T(8,128)(2,1)S(1)}, u32[]{:S(2)}, u32[]{:S(2)}) collective-permute-start(s16[136,1152]{1,0:T(8,128)(2,1)S(1)} %passed_sum.2), channel_id=1, source_target_pairs={{0,2},{1,3},{2,0},{3,1},{4,6},{5,7},{6,4},{7,5},{8,10},{9,11},{10,... | collective-permute-start | bytes 940040 | tf_op jit(solution)/shard_map/ppermute | solution.py:273
  49.9 3.9 %collective-permute-done.10.refs_2_ = s16[136,1152]{1,0:T(8,128)(2,1)S(1)} collective-permute-done((s16[136,1152]{1,0:T(8,128)(2,1)S(1)}, s16[136,1152]{1,0:T(8,128)(2,1)S(1)}, u32[]{:S(2)}, u32[]{:S(2)}) %collective-permute-start.10) | collective-permute-done | bytes 313376 | tf_op jit(solution)/shard_map/ppermute | solution.py:273
  53.8 0.0 collective-permute-done.13.refs_5_
  53.8 6.1 %collective-permute-done.15.refs_6_ = s16[136,1152]{1,0:T(8,128)(2,1)S(1)} collective-permute-done((s16[136,1152]{1,0:T(8,128)(2,1)S(1)}, s16[136,1152]{1,0:T(8,128)(2,1)S(1)}, u32[]{:S(2)}, u32[]{:S(2)}) %collective-permute-start.15) | collective-permute-done | bytes 313376 | tf_op jit(solution)/shard_map/ppermute | solution.py:273
  59.9 1.5 %collective-permute-done.12.refs_3_ = s16[136,1152]{1,0:T(8,128)(2,1)S(1)} collective-permute-done((s16[136,1152]{1,0:T(8,128)(2,1)S(1)}, s16[136,1152]{1,0:T(8,128)(2,1)S(1)}, u32[]{:S(2)}, u32[]{:S(2)}) %collective-permute-start.12) | collective-permute-done | bytes 313376 | tf_op jit(solution)/shard_map/ppermute | solution.py:273
  61.4 1.2 %output_sums.1 = (f32[128,1152]{1,0:T(8,128)}, f32[128,1152]{1,0:T(8,128)}) custom-call(f32[1]{0:T(128)S(6)} %copy.7.refs_0_, f32[128,1152]{1,0:T(8,128)S(1)} %get-tuple-element.39.refs_1_, s16[136,1152]{1,0:T(8,128)(2,1)S(1)} %collective-permute-done.10.refs_2_, s16[136,1152]{1,0:T(8,128)(2,1)S(1)} %collective-permute-done.12.refs_3_, ...), custom_call_target="tpu_custom_call" | custom-call | flops 128 | bytes 128 | tf_op jit(solution)/shard_map/output_sums/pallas_call | solution.py:92
  (3 shorter events, 0.1 us)
Async XLA Ops:
  0.6 18.0 %collective-permute-start = (bf16[128,1152]{1,0:T(8,128)(2,1)}, bf16[128,1152]{1,0:T(8,128)(2,1)S(1)}, u32[]{:S(2)}, u32[]{:S(2)}) collective-permute-start(bf16[128,1152]{1,0:T(8,128)(2,1)} %refs_8_.3), channel_id=1, source_target_pairs={{0,4},{1,5},{2,6},{3,7},{4,0},{5,1},{6,2},{7,3},{8,12},{9,13},{10,... | collective-permute-start | bytes 884744 | tf_op jit(solution)/shard_map/ppermute | solution.py:273
  4.7 13.9 %collective-permute-start.1 = (bf16[128,1152]{1,0:T(8,128)(2,1)}, bf16[128,1152]{1,0:T(8,128)(2,1)S(1)}, u32[]{:S(2)}, u32[]{:S(2)}) collective-permute-start(bf16[128,1152]{1,0:T(8,128)(2,1)} %refs_0_.6), channel_id=1, source_target_pairs={{0,2},{1,3},{2,0},{3,1},{4,6},{5,7},{6,4},{7,5},{8,10},{9,11},{10,... | collective-permute-start | bytes 884744 | tf_op jit(solution)/shard_map/ppermute | solution.py:273
  6.3 1.0 %copy-start.1 = (bf16[128,1152]{1,0:T(8,128)(2,1)S(1)}, bf16[128,1152]{1,0:T(8,128)(2,1)}, u32[]{:S(2)}) copy-start(bf16[128,1152]{1,0:T(8,128)(2,1)} %refs_0_.6) | copy-start | bytes 884740
  7.3 0.7 %copy-start.2 = (s32[128]{0:T(128)S(1)}, s32[128]{0:T(128)}, u32[]{:S(2)}) copy-start(s32[128]{0:T(128)} %param.7) | copy-start | bytes 1540
  8.0 10.8 %copy-start = (bf16[128,1152]{1,0:T(8,128)(2,1)S(1)}, bf16[128,1152]{1,0:T(8,128)(2,1)}, u32[]{:S(2)}) copy-start(bf16[128,1152]{1,0:T(8,128)(2,1)} %refs_8_.3) | copy-start | bytes 884740
  8.0 10.7 %collective-permute-start.4 = (bf16[136,1152]{1,0:T(8,128)(2,1)S(1)}, bf16[136,1152]{1,0:T(8,128)(2,1)S(1)}, u32[]{:S(2)}, u32[]{:S(2)}) collective-permute-start(bf16[136,1152]{1,0:T(8,128)(2,1)S(1)} %labelled.3.refs_2_.refs_7_.refs_9_), channel_id=1, source_target_pairs={{0,8},{8,0},{16,24},{24,16},{1,9},{9,1},{17,25},{25,17},{2,10},{10... | collective-permute-start | bytes 940040 | tf_op jit(solution)/shard_map/ppermute | solution.py:273
  9.6 9.2 %collective-permute-start.3 = (bf16[128,1152]{1,0:T(8,128)(2,1)}, bf16[128,1152]{1,0:T(8,128)(2,1)S(1)}, u32[]{:S(2)}, u32[]{:S(2)}) collective-permute-start(bf16[128,1152]{1,0:T(8,128)(2,1)} %refs_8_.3), channel_id=1, source_target_pairs={{0,16},{8,24},{16,0},{24,8},{1,17},{9,25},{17,1},{25,9},{2,18},{10... | collective-permute-start | bytes 884744 | tf_op jit(solution)/shard_map/ppermute | solution.py:273
  11.1 7.6 %collective-permute-start.2 = (s32[1,128]{1,0:T(1,128)S(1)}, s32[1,128]{1,0:T(1,128)S(1)}, u32[]{:S(2)}, u32[]{:S(2)}) collective-permute-start(s32[1,128]{1,0:T(1,128)S(1)} %bitcast.2), channel_id=1, source_target_pairs={{0,2},{1,3},{2,0},{3,1},{4,6},{5,7},{6,4},{7,5},{8,10},{9,11},{10,... | collective-permute-start | bytes 1544 | tf_op jit(solution)/shard_map/ppermute | solution.py:273
  18.9 4.5 %collective-permute-start.7 = (bf16[792,1152]{1,0:T(8,128)(2,1)S(1)}, bf16[792,1152]{1,0:T(8,128)(2,1)S(1)}, u32[]{:S(2)}, u32[]{:S(2)}) collective-permute-start(bf16[792,1152]{1,0:T(8,128)(2,1)S(1)} %bundled.3), channel_id=1, source_target_pairs={{0,1},{1,0},{2,3},{3,2},{4,5},{5,4},{6,7},{7,6},{8,9},{9,8},{10,11... | collective-permute-start | bytes 5474312 | tf_op jit(solution)/shard_map/ppermute | solution.py:273
  19.0 10.7 %collective-permute-start.6 = (bf16[136,1152]{1,0:T(8,128)(2,1)S(1)}, bf16[136,1152]{1,0:T(8,128)(2,1)S(1)}, u32[]{:S(2)}, u32[]{:S(2)}) collective-permute-start(bf16[136,1152]{1,0:T(8,128)(2,1)S(1)} %labelled.2.refs_1_.refs_3_), channel_id=1, source_target_pairs={{0,8},{8,0},{16,24},{24,16},{1,9},{9,1},{17,25},{25,17},{2,10},{10... | collective-permute-start | bytes 940040 | tf_op jit(solution)/shard_map/ppermute | solution.py:273
  20.6 9.1 %collective-permute-start.5 = (bf16[128,1152]{1,0:T(8,128)(2,1)S(1)}, bf16[128,1152]{1,0:T(8,128)(2,1)S(1)}, u32[]{:S(2)}, u32[]{:S(2)}) collective-permute-start(bf16[128,1152]{1,0:T(8,128)(2,1)S(1)} %collective-permute-done.refs_2_.refs_0_), channel_id=1, source_target_pairs={{0,16},{8,24},{16,0},{24,8},{1,17},{9,25},{17,1},{25,9},{2,18},{10... | collective-permute-start | bytes 884744 | tf_op jit(solution)/shard_map/ppermute | solution.py:273
  29.7 1.6 %collective-permute-start.9 = (bf16[136,1152]{1,0:T(8,128)(2,1)S(1)}, bf16[136,1152]{1,0:T(8,128)(2,1)S(1)}, u32[]{:S(2)}, u32[]{:S(2)}) collective-permute-start(bf16[136,1152]{1,0:T(8,128)(2,1)S(1)} %collective-permute-done.6.refs_7_), channel_id=1, source_target_pairs={{0,1},{1,0},{2,3},{3,2},{4,5},{5,4},{6,7},{7,6},{8,9},{9,8},{10,11... | collective-permute-start | bytes 940040 | tf_op jit(solution)/shard_map/ppermute | solution.py:273
  29.7 5.7 %collective-permute-start.8 = (bf16[128,1152]{1,0:T(8,128)(2,1)S(1)}, bf16[128,1152]{1,0:T(8,128)(2,1)S(1)}, u32[]{:S(2)}, u32[]{:S(2)}) collective-permute-start(bf16[128,1152]{1,0:T(8,128)(2,1)S(1)} %collective-permute-done.5.refs_6_), channel_id=1, source_target_pairs={{0,1},{1,0},{2,3},{3,2},{4,5},{5,4},{6,7},{7,6},{8,9},{9,8},{10,11... | collective-permute-start | bytes 884744 | tf_op jit(solution)/shard_map/ppermute | solution.py:273
  33.8 10.3 %collective-permute-start.14 = (s16[136,1152]{1,0:T(8,128)(2,1)S(1)}, s16[136,1152]{1,0:T(8,128)(2,1)S(1)}, u32[]{:S(2)}, u32[]{:S(2)}) collective-permute-start(s16[136,1152]{1,0:T(8,128)(2,1)S(1)} %get-tuple-element.45), channel_id=1, source_target_pairs={{0,16},{8,24},{16,0},{24,8},{1,17},{9,25},{17,1},{25,9},{2,18},{10... | collective-permute-start | bytes 940040 | tf_op jit(solution)/shard_map/ppermute | solution.py:273
  37.9 10.4 %collective-permute-start.11 = (s16[136,1152]{1,0:T(8,128)(2,1)S(1)}, s16[136,1152]{1,0:T(8,128)(2,1)S(1)}, u32[]{:S(2)}, u32[]{:S(2)}) collective-permute-start(s16[136,1152]{1,0:T(8,128)(2,1)S(1)} %get-tuple-element.42), channel_id=1, source_target_pairs={{0,8},{8,0},{16,24},{24,16},{1,9},{9,1},{17,25},{25,17},{2,10},{10... | collective-permute-start | bytes 940040 | tf_op jit(solution)/shard_map/ppermute | solution.py:273
  38.6 15.2 %collective-permute-start.13 = (s16[136,1152]{1,0:T(8,128)(2,1)S(1)}, s16[136,1152]{1,0:T(8,128)(2,1)S(1)}, u32[]{:S(2)}, u32[]{:S(2)}) collective-permute-start(s16[136,1152]{1,0:T(8,128)(2,1)S(1)} %get-tuple-element.38.refs_15_), channel_id=1, source_target_pairs={{0,16},{8,24},{16,0},{24,8},{1,17},{9,25},{17,1},{25,9},{2,18},{10... | collective-permute-start | bytes 940040 | tf_op jit(solution)/shard_map/ppermute | solution.py:273
  39.2 14.7 %collective-permute-start.10 = (s16[136,1152]{1,0:T(8,128)(2,1)S(1)}, s16[136,1152]{1,0:T(8,128)(2,1)S(1)}, u32[]{:S(2)}, u32[]{:S(2)}) collective-permute-start(s16[136,1152]{1,0:T(8,128)(2,1)S(1)} %get-tuple-element.40), channel_id=1, source_target_pairs={{0,8},{8,0},{16,24},{24,16},{1,9},{9,1},{17,25},{25,17},{2,10},{10... | collective-permute-start | bytes 940040 | tf_op jit(solution)/shard_map/ppermute | solution.py:273
  44.3 15.6 %collective-permute-start.15 = (s16[136,1152]{1,0:T(8,128)(2,1)S(1)}, s16[136,1152]{1,0:T(8,128)(2,1)S(1)}, u32[]{:S(2)}, u32[]{:S(2)}) collective-permute-start(s16[136,1152]{1,0:T(8,128)(2,1)S(1)} %passed_sum.3), channel_id=1, source_target_pairs={{0,4},{1,5},{2,6},{3,7},{4,0},{5,1},{6,2},{7,3},{8,12},{9,13},{10,... | collective-permute-start | bytes 940040 | tf_op jit(solution)/shard_map/ppermute | solution.py:273
  48.4 13.0 %collective-permute-start.12 = (s16[136,1152]{1,0:T(8,128)(2,1)S(1)}, s16[136,1152]{1,0:T(8,128)(2,1)S(1)}, u32[]{:S(2)}, u32[]{:S(2)}) collective-permute-start(s16[136,1152]{1,0:T(8,128)(2,1)S(1)} %passed_sum.2), channel_id=1, source_target_pairs={{0,2},{1,3},{2,0},{3,1},{4,6},{5,7},{6,4},{7,5},{8,10},{9,11},{10,... | collective-permute-start | bytes 940040 | tf_op jit(solution)/shard_map/ppermute | solution.py:273

commit v9 on v8

--- a/solution.py
+++ b/solution.py
@@ -277,34 +277,18 @@
     def sent(block, step):
         return [(swapped(p, step), 0, 0) for p in block]
 
-    last = steps[-1]
-    if len(coded[-1]) == 1:
-        received = [[sent(c, last)] for c in coded]
-        begun = None
-    else:
-        received = [[None]] + [[sent(c[:1], last)] for c in coded[1:]]
-        n = len(kept) - 1
-        begun, *rest = passed_sum(
-            kept[n], received[n], 0, [c[-1] for c in coded[1:]] + [coded[0][0]]
-        )
-        for r, c in zip(received[1:] + received[:1], rest):
-            if r is received[0]:
-                r[0] = sent([c], last)
-            else:
-                r[0] = r[0] + sent([c], last)
+    half, waiting = len(kept), coded[0]
+    received = [[]] + [[sent(c, steps[-1])] for c in coded[1:]]
     for s in reversed(range(len(steps) - 1)):
         for m in reversed(range(1 << s)):
             n = m | 1 << s
-            parts = range(2) if len(received[n][0]) == 2 else [None]
-            passed = []
-            for p in parts:
-                if begun is not None:
-                    passed.append(begun)
-                    begun = None
-                else:
-                    passed += passed_sum(kept[n], received[n], p)
-            received[m].append(sent(passed, steps[s]))
-    return kept[0], received[0]
+            block = passed_sum(kept[n], received[n], None, waiting)
+            if n == half - 1:
+                block, *waiting = block
+                received[0].append(sent(waiting, steps[-1]))
+                waiting, block = (), [block]
+            received[m].append(sent(block, steps[s]))
+    return kept[0], received[0][::-1]
 
 
 def bit_steps(axis):

time: 62.8 us -> 62.8 us (level)
  transfers between devices with their start and end apart: 16 -> 16, of which waited for: 8 -> 7; matrix products, arithmetic and copies ran while one was open for 0% -> 0% of each run, Pallas kernels for 15% -> 15%
where the time goes in v9:
time: 62.8 us; the launch traced here: 62.6 us
  waiting for transfers between devices  27.8 us (44%)
  starting transfers between devices  20.5 us (33%)
  Pallas kernels  10.7 us (17%)
  between operations  2.04 us (3%)
  local copies, waits for them, and re-layouts  1.65 us (3%)
    ppermute x16, waiting for transfers between devices, swapped(): lax.ppermute(array, axis, [(i, i ^ bit) for i in range(lax.axis_size(axis...  27.8 us
    ppermute x16, starting transfers between devices, swapped(): lax.ppermute(array, axis, [(i, i ^ bit) for i in range(lax.axis_size(axis...  20.5 us
    pallas_call x11, Pallas kernels, call(): pl.pallas_call(body, out_shape=[*out_shape, *(jax.ShapeDtypeStruct(a.shap...  10.7 us
    unnamed x6, local copies, waits for them, and re-layouts  1.65 us
  transfers between devices with their start and end apart: 16, of which 7 were waited for; matrix products, arithmetic and copies ran while one was open for 0% of the time, Pallas kernels for 15%

profile of v9, /device:TPU:0, one launch (start us, length us, event | category | flops | bytes accessed | tf_op | source)
XLA Modules:
  0.0 62.6 jit_solution(12661591225922856575)
XLA Ops:
  0.6 4.1 %collective-permute-start = (bf16[128,1152]{1,0:T(8,128)(2,1)}, bf16[128,1152]{1,0:T(8,128)(2,1)S(1)}, u32[]{:S(2)}, u32[]{:S(2)}) collective-permute-start(bf16[128,1152]{1,0:T(8,128)(2,1)} %refs_8_.3), channel_id=1, source_target_pairs={{0,4},{1,5},{2,6},{3,7},{4,0},{5,1},{6,2},{7,3},{8,12},{9,13},{10,... | collective-permute-start | bytes 884744 | tf_op jit(solution)/shard_map/ppermute | solution.py:273
  4.7 1.6 %collective-permute-start.1 = (bf16[128,1152]{1,0:T(8,128)(2,1)}, bf16[128,1152]{1,0:T(8,128)(2,1)S(1)}, u32[]{:S(2)}, u32[]{:S(2)}) collective-permute-start(bf16[128,1152]{1,0:T(8,128)(2,1)} %refs_0_.6), channel_id=1, source_target_pairs={{0,2},{1,3},{2,0},{3,1},{4,6},{5,7},{6,4},{7,5},{8,10},{9,11},{10,... | collective-permute-start | bytes 884744 | tf_op jit(solution)/shard_map/ppermute | solution.py:273
  6.3 0.0 copy-start.1
  6.3 1.0 %copy-done.1 = bf16[128,1152]{1,0:T(8,128)(2,1)S(1)} copy-done((bf16[128,1152]{1,0:T(8,128)(2,1)S(1)}, bf16[128,1152]{1,0:T(8,128)(2,1)}, u32[]{:S(2)}) %copy-start.1) | copy-done | bytes 294936
  7.3 0.0 copy-start.2
  7.3 0.7 %copy-done.2 = s32[128]{0:T(128)S(1)} copy-done((s32[128]{0:T(128)S(1)}, s32[128]{0:T(128)}, u32[]{:S(2)}) %copy-start.2) | copy-done | bytes 536
  8.0 0.0 copy-start
  8.0 1.6 %collective-permute-start.4 = (bf16[136,1152]{1,0:T(8,128)(2,1)S(1)}, bf16[136,1152]{1,0:T(8,128)(2,1)S(1)}, u32[]{:S(2)}, u32[]{:S(2)}) collective-permute-start(bf16[136,1152]{1,0:T(8,128)(2,1)S(1)} %labelled.3.refs_2_.refs_7_.refs_9_), channel_id=1, source_target_pairs={{0,8},{8,0},{16,24},{24,16},{1,9},{9,1},{17,25},{25,17},{2,10},{10... | collective-permute-start | bytes 940040 | tf_op jit(solution)/shard_map/ppermute | solution.py:273
  9.6 1.5 %collective-permute-start.3 = (bf16[128,1152]{1,0:T(8,128)(2,1)}, bf16[128,1152]{1,0:T(8,128)(2,1)S(1)}, u32[]{:S(2)}, u32[]{:S(2)}) collective-permute-start(bf16[128,1152]{1,0:T(8,128)(2,1)} %refs_8_.3), channel_id=1, source_target_pairs={{0,16},{8,24},{16,0},{24,8},{1,17},{9,25},{17,1},{25,9},{2,18},{10... | collective-permute-start | bytes 884744 | tf_op jit(solution)/shard_map/ppermute | solution.py:273
  11.1 0.4 collective-permute-start.2
  11.5 7.1 %collective-permute-done.2.refs_1_ = s32[1,128]{1,0:T(1,128)S(1)} collective-permute-done((s32[1,128]{1,0:T(1,128)}, s32[1,128]{1,0:T(1,128)S(1)}, u32[]{:S(2)}, u32[]{:S(2)}) %collective-permute-start.2) | collective-permute-done | bytes 544 | tf_op jit(solution)/shard_map/ppermute | solution.py:273
  18.6 0.0 collective-permute-done.refs_2_.refs_0_
  18.6 0.0 collective-permute-done.1.refs_0_
  18.7 0.0 collective-permute-done.3.refs_3_.refs_4_
  18.7 0.0 collective-permute-done.4.refs_4_.refs_5_
  18.7 0.0 copy-done
  18.8 0.1 bundled.3
  18.9 0.1 collective-permute-start.7
  19.0 1.6 %collective-permute-start.6 = (bf16[136,1152]{1,0:T(8,128)(2,1)S(1)}, bf16[136,1152]{1,0:T(8,128)(2,1)S(1)}, u32[]{:S(2)}, u32[]{:S(2)}) collective-permute-start(bf16[136,1152]{1,0:T(8,128)(2,1)S(1)} %labelled.2.refs_1_.refs_3_), channel_id=1, source_target_pairs={{0,8},{8,0},{16,24},{24,16},{1,9},{9,1},{17,25},{25,17},{2,10},{10... | collective-permute-start | bytes 940040 | tf_op jit(solution)/shard_map/ppermute | solution.py:273
  20.6 1.5 %collective-permute-start.5 = (bf16[128,1152]{1,0:T(8,128)(2,1)S(1)}, bf16[128,1152]{1,0:T(8,128)(2,1)S(1)}, u32[]{:S(2)}, u32[]{:S(2)}) collective-permute-start(bf16[128,1152]{1,0:T(8,128)(2,1)S(1)} %collective-permute-done.refs_2_.refs_0_), channel_id=1, source_target_pairs={{0,16},{8,24},{16,0},{24,8},{1,17},{9,25},{17,1},{25,9},{2,18},{10... | collective-permute-start | bytes 884744 | tf_op jit(solution)/shard_map/ppermute | solution.py:273
  23.4 0.0 collective-permute-done.7.refs_8_.refs_10_
  23.4 1.9 %early_sums.3 = (f32[128,1152]{1,0:T(8,128)S(1)}, f32[128,1152]{1,0:T(8,128)S(1)}, f32[128,1152]{1,0:T(8,128)S(1)}) custom-call(f32[1]{0:T(128)S(6)} %copy.11.refs_0_, f32[1]{0:T(128)S(6)} %copy.12.refs_1_, bf16[128,1152]{1,0:T(8,128)(2,1)S(1)} %collective-permute-done.refs_2_.refs_0_, bf16[136,1152]{1,0:T(8,128)(2,1)S(1)} %labelled.2.refs_1_.refs_3_, ...), custom_call_target="tpu_custom_call" | custom-call | flops 2304 | bytes 2304 | tf_op jit(solution)/shard_map/early_sums/pallas_call | solution.py:92
  25.3 1.9 %early_sums.2 = (f32[128,1152]{1,0:T(8,128)S(1)}, f32[128,1152]{1,0:T(8,128)S(1)}, f32[128,1152]{1,0:T(8,128)S(1)}) custom-call(f32[1]{0:T(128)S(6)} %copy.11.refs_0_, f32[1]{0:T(128)S(6)} %copy.12.refs_1_, bf16[128,1152]{1,0:T(8,128)(2,1)S(1)} %collective-permute-done.refs_2_.refs_0_, bf16[136,1152]{1,0:T(8,128)(2,1)S(1)} %labelled.2.refs_1_.refs_3_, ...), custom_call_target="tpu_custom_call" | custom-call | flops 2304 | bytes 2304 | tf_op jit(solution)/shard_map/early_sums/pallas_call | solution.py:92
  27.3 2.4 %collective-permute-done.5.refs_6_ = bf16[128,1152]{1,0:T(8,128)(2,1)S(1)} collective-permute-done((bf16[128,1152]{1,0:T(8,128)(2,1)S(1)}, bf16[128,1152]{1,0:T(8,128)(2,1)S(1)}, u32[]{:S(2)}, u32[]{:S(2)}) %collective-permute-start.5) | collective-permute-done | bytes 294944 | tf_op jit(solution)/shard_map/ppermute | solution.py:273
  29.7 0.0 collective-permute-done.6.refs_7_
  29.7 0.0 collective-permute-start.9
  29.7 0.5 collective-permute-start.8
  30.2 1.1 %collective-permute-done.9.refs_11_ = bf16[136,1152]{1,0:T(8,128)(2,1)S(1)} collective-permute-done((bf16[136,1152]{1,0:T(8,128)(2,1)S(1)}, bf16[136,1152]{1,0:T(8,128)(2,1)S(1)}, u32[]{:S(2)}, u32[]{:S(2)}) %collective-permute-start.9) | collective-permute-done | bytes 313376 | tf_op jit(solution)/shard_map/ppermute | solution.py:273
  31.3 2.5 %late_sums.2 = (f32[128,1152]{1,0:T(8,128)S(1)}, f32[128,1152]{1,0:T(8,128)S(1)}, s16[136,1152]{1,0:T(8,128)(2,1)S(1)}, s16[136,1152]{1,0:T(8,128)(2,1)S(1)}) custom-call(f32[1]{0:T(128)S(6)} %copy.11.refs_0_, f32[1]{0:T(128)S(6)} %copy.12.refs_1_, bf16[128,1152]{1,0:T(8,128)(2,1)S(1)} %collective-permute-done.refs_2_.refs_0_, ...), custom_call_target="tpu_custom_call" | custom-call | flops 1792 | bytes 1792 | tf_op jit(solution)/shard_map/late_sums/pallas_call | solution.py:92
  33.8 1.6 %collective-permute-start.13 = (s16[136,1152]{1,0:T(8,128)(2,1)S(1)}, s16[136,1152]{1,0:T(8,128)(2,1)S(1)}, u32[]{:S(2)}, u32[]{:S(2)}) collective-permute-start(s16[136,1152]{1,0:T(8,128)(2,1)S(1)} %get-tuple-element.51), channel_id=1, source_target_pairs={{0,16},{8,24},{16,0},{24,8},{1,17},{9,25},{17,1},{25,9},{2,18},{10... | collective-permute-start | bytes 940040 | tf_op jit(solution)/shard_map/ppermute | solution.py:273
  35.4 0.0 collective-permute-done.8.refs_11_
  35.4 2.5 %late_sums.3 = (f32[128,1152]{1,0:T(8,128)S(1)}, f32[128,1152]{1,0:T(8,128)S(1)}, s16[136,1152]{1,0:T(8,128)(2,1)S(1)}, s16[136,1152]{1,0:T(8,128)(2,1)S(1)}) custom-call(f32[1]{0:T(128)S(6)} %copy.11.refs_0_, f32[1]{0:T(128)S(6)} %copy.12.refs_1_, bf16[128,1152]{1,0:T(8,128)(2,1)S(1)} %collective-permute-done.refs_2_.refs_0_, ...), custom_call_target="tpu_custom_call" | custom-call | flops 1792 | bytes 1792 | tf_op jit(solution)/shard_map/late_sums/pallas_call | solution.py:92
  37.9 0.8 %collective-permute-start.10 = (s16[136,1152]{1,0:T(8,128)(2,1)S(1)}, s16[136,1152]{1,0:T(8,128)(2,1)S(1)}, u32[]{:S(2)}, u32[]{:S(2)}) collective-permute-start(s16[136,1152]{1,0:T(8,128)(2,1)S(1)} %get-tuple-element.45), channel_id=1, source_target_pairs={{0,8},{8,0},{16,24},{24,16},{1,9},{9,1},{17,25},{25,17},{2,10},{10... | collective-permute-start | bytes 940040 | tf_op jit(solution)/shard_map/ppermute | solution.py:273
  38.6 4.7 %collective-permute-done.13.refs_1_ = s16[136,1152]{1,0:T(8,128)(2,1)S(1)} collective-permute-done((s16[136,1152]{1,0:T(8,128)(2,1)S(1)}, s16[136,1152]{1,0:T(8,128)(2,1)S(1)}, u32[]{:S(2)}, u32[]{:S(2)}) %collective-permute-start.13) | collective-permute-done | bytes 313376 | tf_op jit(solution)/shard_map/ppermute | solution.py:273
  43.3 0.2 passed_sum.3
  43.5 1.4 %collective-permute-start.14 = (s16[136,1152]{1,0:T(8,128)(2,1)S(1)}, s16[136,1152]{1,0:T(8,128)(2,1)S(1)}, u32[]{:S(2)}, u32[]{:S(2)}) collective-permute-start(s16[136,1152]{1,0:T(8,128)(2,1)S(1)} %get-tuple-element.52), channel_id=1, source_target_pairs={{0,4},{1,5},{2,6},{3,7},{4,0},{5,1},{6,2},{7,3},{8,12},{9,13},{10,... | collective-permute-start | bytes 940040 | tf_op jit(solution)/shard_map/ppermute | solution.py:273
  44.9 1.5 %collective-permute-start.15 = (s16[136,1152]{1,0:T(8,128)(2,1)S(1)}, s16[136,1152]{1,0:T(8,128)(2,1)S(1)}, u32[]{:S(2)}, u32[]{:S(2)}) collective-permute-start(s16[136,1152]{1,0:T(8,128)(2,1)S(1)} %get-tuple-element.53), channel_id=1, source_target_pairs={{0,16},{8,24},{16,0},{24,8},{1,17},{9,25},{17,1},{25,9},{2,18},{10... | collective-permute-start | bytes 940040 | tf_op jit(solution)/shard_map/ppermute | solution.py:273
  46.4 0.7 %collective-permute-done.10.refs_1_ = s16[136,1152]{1,0:T(8,128)(2,1)S(1)} collective-permute-done((s16[136,1152]{1,0:T(8,128)(2,1)S(1)}, s16[136,1152]{1,0:T(8,128)(2,1)S(1)}, u32[]{:S(2)}, u32[]{:S(2)}) %collective-permute-start.10) | collective-permute-done | bytes 313376 | tf_op jit(solution)/shard_map/ppermute | solution.py:273
  47.1 0.2 passed_sum.2
  47.3 1.7 %collective-permute-start.11 = (s16[136,1152]{1,0:T(8,128)(2,1)S(1)}, s16[136,1152]{1,0:T(8,128)(2,1)S(1)}, u32[]{:S(2)}, u32[]{:S(2)}) collective-permute-start(s16[136,1152]{1,0:T(8,128)(2,1)S(1)} %get-tuple-element.47), channel_id=1, source_target_pairs={{0,2},{1,3},{2,0},{3,1},{4,6},{5,7},{6,4},{7,5},{8,10},{9,11},{10,... | collective-permute-start | bytes 940040 | tf_op jit(solution)/shard_map/ppermute | solution.py:273
  49.0 0.7 %collective-permute-start.12 = (s16[136,1152]{1,0:T(8,128)(2,1)S(1)}, s16[136,1152]{1,0:T(8,128)(2,1)S(1)}, u32[]{:S(2)}, u32[]{:S(2)}) collective-permute-start(s16[136,1152]{1,0:T(8,128)(2,1)S(1)} %get-tuple-element.48), channel_id=1, source_target_pairs={{0,8},{8,0},{16,24},{24,16},{1,9},{9,1},{17,25},{25,17},{2,10},{10... | collective-permute-start | bytes 940040 | tf_op jit(solution)/shard_map/ppermute | solution.py:273
  49.7 10.2 %collective-permute-done.14.refs_5_ = s16[136,1152]{1,0:T(8,128)(2,1)S(1)} collective-permute-done((s16[136,1152]{1,0:T(8,128)(2,1)S(1)}, s16[136,1152]{1,0:T(8,128)(2,1)S(1)}, u32[]{:S(2)}, u32[]{:S(2)}) %collective-permute-start.14) | collective-permute-done | bytes 313376 | tf_op jit(solution)/shard_map/ppermute | solution.py:273
  59.9 0.0 collective-permute-done.15.refs_6_
  59.9 1.5 %collective-permute-done.11.refs_2_ = s16[136,1152]{1,0:T(8,128)(2,1)S(1)} collective-permute-done((s16[136,1152]{1,0:T(8,128)(2,1)S(1)}, s16[136,1152]{1,0:T(8,128)(2,1)S(1)}, u32[]{:S(2)}, u32[]{:S(2)}) %collective-permute-start.11) | collective-permute-done | bytes 313376 | tf_op jit(solution)/shard_map/ppermute | solution.py:273
  61.4 0.0 collective-permute-done.12.refs_3_
  61.4 1.2 %output_sums.1 = (f32[128,1152]{1,0:T(8,128)}, f32[128,1152]{1,0:T(8,128)}) custom-call(f32[1]{0:T(128)S(6)} %copy.11.refs_0_, f32[128,1152]{1,0:T(8,128)S(1)} %get-tuple-element.43.refs_1_, s16[136,1152]{1,0:T(8,128)(2,1)S(1)} %collective-permute-done.11.refs_2_, s16[136,1152]{1,0:T(8,128)(2,1)S(1)} %collective-permute-done.12.refs_3_, ...), custom_call_target="tpu_custom_call" | custom-call | flops 128 | bytes 128 | tf_op jit(solution)/shard_map/output_sums/pallas_call | solution.py:92
  (3 shorter events, 0.1 us)
Async XLA Ops:
  0.6 18.0 %collective-permute-start = (bf16[128,1152]{1,0:T(8,128)(2,1)}, bf16[128,1152]{1,0:T(8,128)(2,1)S(1)}, u32[]{:S(2)}, u32[]{:S(2)}) collective-permute-start(bf16[128,1152]{1,0:T(8,128)(2,1)} %refs_8_.3), channel_id=1, source_target_pairs={{0,4},{1,5},{2,6},{3,7},{4,0},{5,1},{6,2},{7,3},{8,12},{9,13},{10,... | collective-permute-start | bytes 884744 | tf_op jit(solution)/shard_map/ppermute | solution.py:273
  4.7 13.9 %collective-permute-start.1 = (bf16[128,1152]{1,0:T(8,128)(2,1)}, bf16[128,1152]{1,0:T(8,128)(2,1)S(1)}, u32[]{:S(2)}, u32[]{:S(2)}) collective-permute-start(bf16[128,1152]{1,0:T(8,128)(2,1)} %refs_0_.6), channel_id=1, source_target_pairs={{0,2},{1,3},{2,0},{3,1},{4,6},{5,7},{6,4},{7,5},{8,10},{9,11},{10,... | collective-permute-start | bytes 884744 | tf_op jit(solution)/shard_map/ppermute | solution.py:273
  6.3 1.0 %copy-start.1 = (bf16[128,1152]{1,0:T(8,128)(2,1)S(1)}, bf16[128,1152]{1,0:T(8,128)(2,1)}, u32[]{:S(2)}) copy-start(bf16[128,1152]{1,0:T(8,128)(2,1)} %refs_0_.6) | copy-start | bytes 884740
  7.3 0.7 %copy-start.2 = (s32[128]{0:T(128)S(1)}, s32[128]{0:T(128)}, u32[]{:S(2)}) copy-start(s32[128]{0:T(128)} %param.7) | copy-start | bytes 1540
  8.0 10.8 %copy-start = (bf16[128,1152]{1,0:T(8,128)(2,1)S(1)}, bf16[128,1152]{1,0:T(8,128)(2,1)}, u32[]{:S(2)}) copy-start(bf16[128,1152]{1,0:T(8,128)(2,1)} %refs_8_.3) | copy-start | bytes 884740
  8.0 10.7 %collective-permute-start.4 = (bf16[136,1152]{1,0:T(8,128)(2,1)S(1)}, bf16[136,1152]{1,0:T(8,128)(2,1)S(1)}, u32[]{:S(2)}, u32[]{:S(2)}) collective-permute-start(bf16[136,1152]{1,0:T(8,128)(2,1)S(1)} %labelled.3.refs_2_.refs_7_.refs_9_), channel_id=1, source_target_pairs={{0,8},{8,0},{16,24},{24,16},{1,9},{9,1},{17,25},{25,17},{2,10},{10... | collective-permute-start | bytes 940040 | tf_op jit(solution)/shard_map/ppermute | solution.py:273
  9.6 9.2 %collective-permute-start.3 = (bf16[128,1152]{1,0:T(8,128)(2,1)}, bf16[128,1152]{1,0:T(8,128)(2,1)S(1)}, u32[]{:S(2)}, u32[]{:S(2)}) collective-permute-start(bf16[128,1152]{1,0:T(8,128)(2,1)} %refs_8_.3), channel_id=1, source_target_pairs={{0,16},{8,24},{16,0},{24,8},{1,17},{9,25},{17,1},{25,9},{2,18},{10... | collective-permute-start | bytes 884744 | tf_op jit(solution)/shard_map/ppermute | solution.py:273
  11.1 7.6 %collective-permute-start.2 = (s32[1,128]{1,0:T(1,128)}, s32[1,128]{1,0:T(1,128)S(1)}, u32[]{:S(2)}, u32[]{:S(2)}) collective-permute-start(s32[1,128]{1,0:T(1,128)} %bitcast.1), channel_id=1, source_target_pairs={{0,2},{1,3},{2,0},{3,1},{4,6},{5,7},{6,4},{7,5},{8,10},{9,11},{10,... | collective-permute-start | bytes 1544 | tf_op jit(solution)/shard_map/ppermute | solution.py:273
  18.9 4.5 %collective-permute-start.7 = (bf16[792,1152]{1,0:T(8,128)(2,1)S(1)}, bf16[792,1152]{1,0:T(8,128)(2,1)S(1)}, u32[]{:S(2)}, u32[]{:S(2)}) collective-permute-start(bf16[792,1152]{1,0:T(8,128)(2,1)S(1)} %bundled.3), channel_id=1, source_target_pairs={{0,1},{1,0},{2,3},{3,2},{4,5},{5,4},{6,7},{7,6},{8,9},{9,8},{10,11... | collective-permute-start | bytes 5474312 | tf_op jit(solution)/shard_map/ppermute | solution.py:273
  19.0 10.7 %collective-permute-start.6 = (bf16[136,1152]{1,0:T(8,128)(2,1)S(1)}, bf16[136,1152]{1,0:T(8,128)(2,1)S(1)}, u32[]{:S(2)}, u32[]{:S(2)}) collective-permute-start(bf16[136,1152]{1,0:T(8,128)(2,1)S(1)} %labelled.2.refs_1_.refs_3_), channel_id=1, source_target_pairs={{0,8},{8,0},{16,24},{24,16},{1,9},{9,1},{17,25},{25,17},{2,10},{10... | collective-permute-start | bytes 940040 | tf_op jit(solution)/shard_map/ppermute | solution.py:273
  20.6 9.1 %collective-permute-start.5 = (bf16[128,1152]{1,0:T(8,128)(2,1)S(1)}, bf16[128,1152]{1,0:T(8,128)(2,1)S(1)}, u32[]{:S(2)}, u32[]{:S(2)}) collective-permute-start(bf16[128,1152]{1,0:T(8,128)(2,1)S(1)} %collective-permute-done.refs_2_.refs_0_), channel_id=1, source_target_pairs={{0,16},{8,24},{16,0},{24,8},{1,17},{9,25},{17,1},{25,9},{2,18},{10... | collective-permute-start | bytes 884744 | tf_op jit(solution)/shard_map/ppermute | solution.py:273
  29.7 1.6 %collective-permute-start.9 = (bf16[136,1152]{1,0:T(8,128)(2,1)S(1)}, bf16[136,1152]{1,0:T(8,128)(2,1)S(1)}, u32[]{:S(2)}, u32[]{:S(2)}) collective-permute-start(bf16[136,1152]{1,0:T(8,128)(2,1)S(1)} %collective-permute-done.6.refs_7_), channel_id=1, source_target_pairs={{0,1},{1,0},{2,3},{3,2},{4,5},{5,4},{6,7},{7,6},{8,9},{9,8},{10,11... | collective-permute-start | bytes 940040 | tf_op jit(solution)/shard_map/ppermute | solution.py:273
  29.7 5.7 %collective-permute-start.8 = (bf16[128,1152]{1,0:T(8,128)(2,1)S(1)}, bf16[128,1152]{1,0:T(8,128)(2,1)S(1)}, u32[]{:S(2)}, u32[]{:S(2)}) collective-permute-start(bf16[128,1152]{1,0:T(8,128)(2,1)S(1)} %collective-permute-done.5.refs_6_), channel_id=1, source_target_pairs={{0,1},{1,0},{2,3},{3,2},{4,5},{5,4},{6,7},{7,6},{8,9},{9,8},{10,11... | collective-permute-start | bytes 884744 | tf_op jit(solution)/shard_map/ppermute | solution.py:273
  33.8 9.5 %collective-permute-start.13 = (s16[136,1152]{1,0:T(8,128)(2,1)S(1)}, s16[136,1152]{1,0:T(8,128)(2,1)S(1)}, u32[]{:S(2)}, u32[]{:S(2)}) collective-permute-start(s16[136,1152]{1,0:T(8,128)(2,1)S(1)} %get-tuple-element.51), channel_id=1, source_target_pairs={{0,16},{8,24},{16,0},{24,8},{1,17},{9,25},{17,1},{25,9},{2,18},{10... | collective-permute-start | bytes 940040 | tf_op jit(solution)/shard_map/ppermute | solution.py:273
  37.9 9.3 %collective-permute-start.10 = (s16[136,1152]{1,0:T(8,128)(2,1)S(1)}, s16[136,1152]{1,0:T(8,128)(2,1)S(1)}, u32[]{:S(2)}, u32[]{:S(2)}) collective-permute-start(s16[136,1152]{1,0:T(8,128)(2,1)S(1)} %get-tuple-element.45), channel_id=1, source_target_pairs={{0,8},{8,0},{16,24},{24,16},{1,9},{9,1},{17,25},{25,17},{2,10},{10... | collective-permute-start | bytes 940040 | tf_op jit(solution)/shard_map/ppermute | solution.py:273
  43.5 16.4 %collective-permute-start.14 = (s16[136,1152]{1,0:T(8,128)(2,1)S(1)}, s16[136,1152]{1,0:T(8,128)(2,1)S(1)}, u32[]{:S(2)}, u32[]{:S(2)}) collective-permute-start(s16[136,1152]{1,0:T(8,128)(2,1)S(1)} %get-tuple-element.52), channel_id=1, source_target_pairs={{0,4},{1,5},{2,6},{3,7},{4,0},{5,1},{6,2},{7,3},{8,12},{9,13},{10,... | collective-permute-start | bytes 940040 | tf_op jit(solution)/shard_map/ppermute | solution.py:273
  44.9 15.0 %collective-permute-start.15 = (s16[136,1152]{1,0:T(8,128)(2,1)S(1)}, s16[136,1152]{1,0:T(8,128)(2,1)S(1)}, u32[]{:S(2)}, u32[]{:S(2)}) collective-permute-start(s16[136,1152]{1,0:T(8,128)(2,1)S(1)} %get-tuple-element.53), channel_id=1, source_target_pairs={{0,16},{8,24},{16,0},{24,8},{1,17},{9,25},{17,1},{25,9},{2,18},{10... | collective-permute-start | bytes 940040 | tf_op jit(solution)/shard_map/ppermute | solution.py:273
  47.3 14.1 %collective-permute-start.11 = (s16[136,1152]{1,0:T(8,128)(2,1)S(1)}, s16[136,1152]{1,0:T(8,128)(2,1)S(1)}, u32[]{:S(2)}, u32[]{:S(2)}) collective-permute-start(s16[136,1152]{1,0:T(8,128)(2,1)S(1)} %get-tuple-element.47), channel_id=1, source_target_pairs={{0,2},{1,3},{2,0},{3,1},{4,6},{5,7},{6,4},{7,5},{8,10},{9,11},{10,... | collective-permute-start | bytes 940040 | tf_op jit(solution)/shard_map/ppermute | solution.py:273
  49.0 12.4 %collective-permute-start.12 = (s16[136,1152]{1,0:T(8,128)(2,1)S(1)}, s16[136,1152]{1,0:T(8,128)(2,1)S(1)}, u32[]{:S(2)}, u32[]{:S(2)}) collective-permute-start(s16[136,1152]{1,0:T(8,128)(2,1)S(1)} %get-tuple-element.48), channel_id=1, source_target_pairs={{0,8},{8,0},{16,24},{24,16},{1,9},{9,1},{17,25},{25,17},{2,10},{10... | collective-permute-start | bytes 940040 | tf_op jit(solution)/shard_map/ppermute | solution.py:273

commit v10 on v9

--- a/solution.py
+++ b/solution.py
@@ -230,7 +230,7 @@
     return [tuple(results[o] for o, _, _ in where[r]) for r in range(len(emits))]
 
 
-def passed_sum(kept, received, part, held_back=()):
+def passed_sum(kept, received, part, held_back=(), after=()):
     size, width = kept.shape
     operands = Operands()
     kept_at = operands.add(kept, VMEM)
@@ -247,7 +247,7 @@
 
     cut = width if part is None else part_widths(width)[part]
     shape = jax.ShapeDtypeStruct((size + EXTRA_ROWS, cut), jnp.int16)
-    return call(kernel, "passed_sum", operands.pairs, [shape], [], 2**21, size, (), held_back)
+    return call(kernel, "passed_sum", operands.pairs, [shape], [], 2**21, size, after, held_back)
 
 
 def output_sums(sharpness, sums):
@@ -273,7 +273,7 @@
     return lax.ppermute(array, axis, [(i, i ^ bit) for i in range(lax.axis_size(axis))])
 
 
-def scattered(kept, coded, steps):
+def scattered(kept, coded, steps, after):
     def sent(block, step):
         return [(swapped(p, step), 0, 0) for p in block]
 
@@ -282,13 +282,18 @@
     for s in reversed(range(len(steps) - 1)):
         for m in reversed(range(1 << s)):
             n = m | 1 << s
-            block = passed_sum(kept[n], received[n], None, waiting)
+            block = passed_sum(kept[n], received[n], None, waiting, after)
+            after = block[:1]
             if n == half - 1:
                 block, *waiting = block
                 received[0].append(sent(waiting, steps[-1]))
                 waiting, block = (), [block]
             received[m].append(sent(block, steps[s]))
-    return kept[0], received[0][::-1]
+    return (kept[0], received[0][::-1]), after
+
+
+def in_order(arrays):
+    return call(lambda *refs: None, "held", [], [], [], 2**21, 1, (), arrays)
 
 
 def bit_steps(axis):
@@ -316,7 +321,7 @@
     half = count // 2
     early, late = list(range(half + 1)), list(range(half + 1, count))
     labels = matching_caption[None, :]
-    first_texts = swapped(caption_vectors, steps[1][0])
+    (first_texts,) = in_order([swapped(caption_vectors, steps[1][0])])
     first_images = [swapped(a, steps[0][0]) for a in (picture_vectors, labels)]
     arrays = [{0: labelled(picture_vectors, labels), 1: labelled(*first_images, [first_texts])}, {0: caption_vectors, 1: first_texts}]
     for i in range(1, len(steps[0])):
@@ -364,18 +369,21 @@
         for m, a in zip(late, arrays[1 - k]):
             blocks[k][m] = whole(a)
             others[k][m] = whole(swapped(a, core))
-    every = list(range(count))
-    jobs = [(late, every + [count + m for m in every]), (early, late + [count + m for m in late])]
-    coded, kept, after = [None, None], [None, None], ()
-    for k, cut in ((1, "whole"), (0, "whole")):
-        emits = ["float"] * half + ["whole"] + [cut] * len(late)
-        results = sums(
-            "late_sums", k, every, every, (0, 1), jobs, before[k], emits, after
-        )
-        kept[k] = [s for (s,) in results[:half]]
-        coded[k] = results[half:]
-        after = coded[k][0]
-    return tuple(output_sums(scalars[0], [scattered(kept[k], coded[k], steps[k]) for k in range(2)]))
+    every, after = list(range(count)), ()
+    coded, kept = [[None] * half, [None] * half], [None, None]
+    for k in (1, 0):
+        jobs, emits = [(list(range(len(late))), list(range(2 * count)))], ["whole"] * len(late)
+        coded[k][1:] = sums("late_rows", k, late, every, (0, 1), jobs, {}, emits, after)
+        after = coded[k][1]
+    for k in (1, 0):
+        jobs, emits = [(early, list(range(2 * len(late))))], ["float"] * half + ["whole"]
+        *whole_sums, coded[k][0] = sums("late_columns", k, early, late, (0, 1), jobs, before[k], emits, after)
+        kept[k], after = [s for (s,) in whole_sums], coded[k][0]
+    texts, after = scattered(kept[1], coded[1], steps[1], ())
+    images, _ = scattered(kept[0], coded[0], steps[0], after)
+    kept_texts, blocks_in = texts
+    blocks_in = [whole(a) for a in in_order([a for ((a, _, _),) in blocks_in[::-1]])]
+    return tuple(output_sums(scalars[0], [images, (kept_texts, blocks_in)]))
 
 
 def solution(mesh):

time: 62.8 us -> 61.4 us (0.978)
  waiting for transfers between devices: 27.8 us -> 25.2 us
  starting transfers between devices: 20.5 us -> 21.2 us
    ppermute x16, waiting for transfers between devices: 27.8 us -> 25.2 us  [swapped(): lax.ppermute(array, axis, [(i, i ^ bit) for i in range(lax.axis_size(axis...]
    ppermute x16, starting transfers between devices: 20.5 us -> 21.2 us  [swapped(): lax.ppermute(array, axis, [(i, i ^ bit) for i in range(lax.axis_size(axis...]
    pallas_call x11 -> x15, Pallas kernels: 10.7 us -> 11.1 us  [call(): pl.pallas_call(body, out_shape=[*out_shape, *(jax.ShapeDtypeStruct(a.shap...]
  transfers between devices with their start and end apart: 16 -> 16, of which waited for: 7 -> 7; matrix products, arithmetic and copies ran while one was open for 0% -> 0% of each run, Pallas kernels for 15% -> 16%
where the time goes in v10:
time: 61.4 us; the launch traced here: 61.2 us
  waiting for transfers between devices  25.2 us (41%)
  starting transfers between devices  21.2 us (35%)
  Pallas kernels  11.1 us (18%)
  between operations  2.07 us (3%)
  local copies, waits for them, and re-layouts  1.66 us (3%)
    ppermute x16, waiting for transfers between devices, swapped(): lax.ppermute(array, axis, [(i, i ^ bit) for i in range(lax.axis_size(axis...  25.2 us
    ppermute x16, starting transfers between devices, swapped(): lax.ppermute(array, axis, [(i, i ^ bit) for i in range(lax.axis_size(axis...  21.2 us
    pallas_call x15, Pallas kernels, call(): pl.pallas_call(body, out_shape=[*out_shape, *(jax.ShapeDtypeStruct(a.shap...  11.1 us
    unnamed x6, local copies, waits for them, and re-layouts  1.66 us
  transfers between devices with their start and end apart: 16, of which 7 were waited for; matrix products, arithmetic and copies ran while one was open for 0% of the time, Pallas kernels for 16%

profile of v10, /device:TPU:0, one launch (start us, length us, event | category | flops | bytes accessed | tf_op | source)
XLA Modules:
  0.0 61.2 jit_solution(4452677402365806750)
XLA Ops:
  0.6 4.1 %collective-permute-start = (bf16[128,1152]{1,0:T(8,128)(2,1)}, bf16[128,1152]{1,0:T(8,128)(2,1)S(1)}, u32[]{:S(2)}, u32[]{:S(2)}) collective-permute-start(bf16[128,1152]{1,0:T(8,128)(2,1)} %refs_6_.7), channel_id=1, source_target_pairs={{0,4},{1,5},{2,6},{3,7},{4,0},{5,1},{6,2},{7,3},{8,12},{9,13},{10,... | collective-permute-start | bytes 884744 | tf_op jit(solution)/shard_map/ppermute | solution.py:273
  4.7 1.6 %collective-permute-start.1 = (bf16[128,1152]{1,0:T(8,128)(2,1)}, bf16[128,1152]{1,0:T(8,128)(2,1)S(1)}, u32[]{:S(2)}, u32[]{:S(2)}) collective-permute-start(bf16[128,1152]{1,0:T(8,128)(2,1)} %refs_0_.8), channel_id=1, source_target_pairs={{0,2},{1,3},{2,0},{3,1},{4,6},{5,7},{6,4},{7,5},{8,10},{9,11},{10,... | collective-permute-start | bytes 884744 | tf_op jit(solution)/shard_map/ppermute | solution.py:273
  6.3 0.0 copy-start.1
  6.3 1.0 %copy-done.1 = bf16[128,1152]{1,0:T(8,128)(2,1)S(1)} copy-done((bf16[128,1152]{1,0:T(8,128)(2,1)S(1)}, bf16[128,1152]{1,0:T(8,128)(2,1)}, u32[]{:S(2)}) %copy-start.1) | copy-done | bytes 294936
  7.3 0.0 copy-start.2
  7.3 0.7 %copy-done.2 = s32[128]{0:T(128)S(1)} copy-done((s32[128]{0:T(128)S(1)}, s32[128]{0:T(128)}, u32[]{:S(2)}) %copy-start.2) | copy-done | bytes 536
  8.0 0.0 copy-start
  8.0 1.6 %collective-permute-start.4 = (bf16[136,1152]{1,0:T(8,128)(2,1)S(1)}, bf16[136,1152]{1,0:T(8,128)(2,1)S(1)}, u32[]{:S(2)}, u32[]{:S(2)}) collective-permute-start(bf16[136,1152]{1,0:T(8,128)(2,1)S(1)} %labelled.3.refs_2_.refs_7_.refs_4_), channel_id=1, source_target_pairs={{0,8},{8,0},{16,24},{24,16},{1,9},{9,1},{17,25},{25,17},{2,10},{10... | collective-permute-start | bytes 940040 | tf_op jit(solution)/shard_map/ppermute | solution.py:273
  9.6 1.5 %collective-permute-start.3 = (bf16[128,1152]{1,0:T(8,128)(2,1)}, bf16[128,1152]{1,0:T(8,128)(2,1)S(1)}, u32[]{:S(2)}, u32[]{:S(2)}) collective-permute-start(bf16[128,1152]{1,0:T(8,128)(2,1)} %refs_6_.7), channel_id=1, source_target_pairs={{0,16},{8,24},{16,0},{24,8},{1,17},{9,25},{17,1},{25,9},{2,18},{10... | collective-permute-start | bytes 884744 | tf_op jit(solution)/shard_map/ppermute | solution.py:273
  11.1 0.4 collective-permute-start.2
  11.5 6.8 %collective-permute-done.refs_0_ = bf16[128,1152]{1,0:T(8,128)(2,1)S(1)} collective-permute-done((bf16[128,1152]{1,0:T(8,128)(2,1)}, bf16[128,1152]{1,0:T(8,128)(2,1)S(1)}, u32[]{:S(2)}, u32[]{:S(2)}) %collective-permute-start) | collective-permute-done | bytes 294944 | tf_op jit(solution)/shard_map/ppermute | solution.py:273
  18.4 0.3 collective-permute-done.2.refs_1_
  18.6 0.0 collective-permute-done.1.refs_0_
  18.7 0.0 collective-permute-done.3.refs_3_.refs_4_.refs_6_
  18.7 0.0 collective-permute-done.4.refs_4_.refs_5_.refs_6_
  18.7 0.0 copy-done
  18.8 0.1 bundled.3
  18.9 0.1 collective-permute-start.7
  19.0 1.6 %collective-permute-start.6 = (bf16[136,1152]{1,0:T(8,128)(2,1)S(1)}, bf16[136,1152]{1,0:T(8,128)(2,1)S(1)}, u32[]{:S(2)}, u32[]{:S(2)}) collective-permute-start(bf16[136,1152]{1,0:T(8,128)(2,1)S(1)} %labelled.2.refs_1_.refs_3_.refs_5_), channel_id=1, source_target_pairs={{0,8},{8,0},{16,24},{24,16},{1,9},{9,1},{17,25},{25,17},{2,10},{10... | collective-permute-start | bytes 940040 | tf_op jit(solution)/shard_map/ppermute | solution.py:273
  20.6 1.5 %collective-permute-start.5 = (bf16[128,1152]{1,0:T(8,128)(2,1)S(1)}, bf16[128,1152]{1,0:T(8,128)(2,1)S(1)}, u32[]{:S(2)}, u32[]{:S(2)}) collective-permute-start(bf16[128,1152]{1,0:T(8,128)(2,1)S(1)} %held.2.refs_2_.refs_0_.refs_5_), channel_id=1, source_target_pairs={{0,16},{8,24},{16,0},{24,8},{1,17},{9,25},{17,1},{25,9},{2,18},{10... | collective-permute-start | bytes 884744 | tf_op jit(solution)/shard_map/ppermute | solution.py:273
  23.4 0.0 collective-permute-done.7.refs_8_.refs_7_
  23.4 1.9 %early_sums.3 = (f32[128,1152]{1,0:T(8,128)S(1)}, f32[128,1152]{1,0:T(8,128)S(1)}, f32[128,1152]{1,0:T(8,128)S(1)}) custom-call(f32[1]{0:T(128)S(6)} %copy.17.refs_0_, f32[1]{0:T(128)S(6)} %copy.18.refs_1_, bf16[128,1152]{1,0:T(8,128)(2,1)S(1)} %held.2.refs_2_.refs_0_.refs_5_, bf16[136,1152]{1,0:T(8,128)(2,1)S(1)} %labelled.2.refs_1_.refs_3_.refs_5_, ...), custom_call_target="tpu_custom_call" | custom-call | flops 2304 | bytes 2304 | tf_op jit(solution)/shard_map/early_sums/pallas_call | solution.py:92
  25.3 1.9 %early_sums.2 = (f32[128,1152]{1,0:T(8,128)S(1)}, f32[128,1152]{1,0:T(8,128)S(1)}, f32[128,1152]{1,0:T(8,128)S(1)}) custom-call(f32[1]{0:T(128)S(6)} %copy.17.refs_0_, f32[1]{0:T(128)S(6)} %copy.18.refs_1_, bf16[128,1152]{1,0:T(8,128)(2,1)S(1)} %held.2.refs_2_.refs_0_.refs_5_, bf16[136,1152]{1,0:T(8,128)(2,1)S(1)} %labelled.2.refs_1_.refs_3_.refs_5_, ...), custom_call_target="tpu_custom_call" | custom-call | flops 2304 | bytes 2304 | tf_op jit(solution)/shard_map/early_sums/pallas_call | solution.py:92
  27.3 2.4 %collective-permute-done.5.refs_2_.refs_8_ = bf16[128,1152]{1,0:T(8,128)(2,1)S(1)} collective-permute-done((bf16[128,1152]{1,0:T(8,128)(2,1)S(1)}, bf16[128,1152]{1,0:T(8,128)(2,1)S(1)}, u32[]{:S(2)}, u32[]{:S(2)}) %collective-permute-start.5) | collective-permute-done | bytes 294944 | tf_op jit(solution)/shard_map/ppermute | solution.py:273
  29.7 0.0 collective-permute-done.6.refs_3_.refs_8_
  29.7 0.0 collective-permute-start.9
  29.7 0.5 collective-permute-start.8
  30.2 1.1 %collective-permute-done.9.refs_8_.refs_9_ = bf16[136,1152]{1,0:T(8,128)(2,1)S(1)} collective-permute-done((bf16[136,1152]{1,0:T(8,128)(2,1)S(1)}, bf16[136,1152]{1,0:T(8,128)(2,1)S(1)}, u32[]{:S(2)}, u32[]{:S(2)}) %collective-permute-start.9) | collective-permute-done | bytes 313376 | tf_op jit(solution)/shard_map/ppermute | solution.py:273
  31.3 1.4 %late_rows.2.refs_9_ = s16[136,1152]{1,0:T(8,128)(2,1)S(1)} custom-call(f32[1]{0:T(128)S(6)} %copy.17.refs_0_, f32[1]{0:T(128)S(6)} %copy.18.refs_1_, bf16[128,1152]{1,0:T(8,128)(2,1)S(1)} %collective-permute-done.5.refs_2_.refs_8_, bf16[136,1152]{1,0:T(8,128)(2,1)S(1)} %collective-permute-done.6.refs_3_.refs_8_, ...), custom_call_target="tpu_custom_call" | custom-call | flops 1024 | bytes 1024 | tf_op jit(solution)/shard_map/late_rows/pallas_call | solution.py:92
  32.7 1.6 %collective-permute-start.11 = (s16[136,1152]{1,0:T(8,128)(2,1)S(1)}, s16[136,1152]{1,0:T(8,128)(2,1)S(1)}, u32[]{:S(2)}, u32[]{:S(2)}) collective-permute-start(s16[136,1152]{1,0:T(8,128)(2,1)S(1)} %late_rows.2.refs_9_), channel_id=1, source_target_pairs={{0,16},{8,24},{16,0},{24,8},{1,17},{9,25},{17,1},{25,9},{2,18},{10... | collective-permute-start | bytes 940040 | tf_op jit(solution)/shard_map/ppermute | solution.py:273
  34.3 0.0 collective-permute-done.8.refs_8_.refs_9_
  34.3 1.4 %late_rows.3.refs_13_ = s16[136,1152]{1,0:T(8,128)(2,1)S(1)} custom-call(f32[1]{0:T(128)S(6)} %copy.17.refs_0_, f32[1]{0:T(128)S(6)} %copy.18.refs_1_, bf16[128,1152]{1,0:T(8,128)(2,1)S(1)} %collective-permute-done.5.refs_2_.refs_8_, bf16[136,1152]{1,0:T(8,128)(2,1)S(1)} %collective-permute-done.6.refs_3_.refs_8_, bf16[128,1152]{1,0:T(8,128)(2,1)S(1)} %copy-done, ...), custom_call_target="tpu_custom_call" | custom-call | flops 1024 | bytes 1024 | tf_op jit(solution)/shard_map/late_rows/pallas_call | solution.py:92
  35.7 0.7 %collective-permute-start.10 = (s16[136,1152]{1,0:T(8,128)(2,1)S(1)}, s16[136,1152]{1,0:T(8,128)(2,1)S(1)}, u32[]{:S(2)}, u32[]{:S(2)}) collective-permute-start(s16[136,1152]{1,0:T(8,128)(2,1)S(1)} %late_rows.3.refs_13_), channel_id=1, source_target_pairs={{0,8},{8,0},{16,24},{24,16},{1,9},{9,1},{17,25},{25,17},{2,10},{10... | collective-permute-start | bytes 940040 | tf_op jit(solution)/shard_map/ppermute | solution.py:273
  36.4 1.3 %late_columns.2 = (f32[128,1152]{1,0:T(8,128)S(1)}, f32[128,1152]{1,0:T(8,128)S(1)}, s16[136,1152]{1,0:T(8,128)(2,1)S(1)}) custom-call(f32[1]{0:T(128)S(6)} %copy.17.refs_0_, f32[1]{0:T(128)S(6)} %copy.18.refs_1_, bf16[128,1152]{1,0:T(8,128)(2,1)S(1)} %held.2.refs_2_.refs_0_.refs_5_, bf16[136,1152]{1,0:T(8,128)(2,1)S(1)} %labelled.2.refs_1_.refs_3_.refs_5_, ...), custom_call_target="tpu_custom_call" | custom-call | flops 768 | bytes 768 | tf_op jit(solution)/shard_map/late_columns/pallas_call | solution.py:92
  37.7 1.3 %late_columns.3 = (f32[128,1152]{1,0:T(8,128)S(1)}, f32[128,1152]{1,0:T(8,128)S(1)}, s16[136,1152]{1,0:T(8,128)(2,1)S(1)}) custom-call(f32[1]{0:T(128)S(6)} %copy.17.refs_0_, f32[1]{0:T(128)S(6)} %copy.18.refs_1_, bf16[128,1152]{1,0:T(8,128)(2,1)S(1)} %held.2.refs_2_.refs_0_.refs_5_, bf16[136,1152]{1,0:T(8,128)(2,1)S(1)} %labelled.2.refs_1_.refs_3_.refs_5_, ...), custom_call_target="tpu_custom_call" | custom-call | flops 768 | bytes 768 | tf_op jit(solution)/shard_map/late_columns/pallas_call | solution.py:92
  39.0 3.2 %collective-permute-done.11.refs_1_ = s16[136,1152]{1,0:T(8,128)(2,1)S(1)} collective-permute-done((s16[136,1152]{1,0:T(8,128)(2,1)S(1)}, s16[136,1152]{1,0:T(8,128)(2,1)S(1)}, u32[]{:S(2)}, u32[]{:S(2)}) %collective-permute-start.11) | collective-permute-done | bytes 313376 | tf_op jit(solution)/shard_map/ppermute | solution.py:273
  42.2 0.2 passed_sum.2
  42.4 1.6 %collective-permute-start.14 = (s16[136,1152]{1,0:T(8,128)(2,1)S(1)}, s16[136,1152]{1,0:T(8,128)(2,1)S(1)}, u32[]{:S(2)}, u32[]{:S(2)}) collective-permute-start(s16[136,1152]{1,0:T(8,128)(2,1)S(1)} %get-tuple-element.51), channel_id=1, source_target_pairs={{0,16},{8,24},{16,0},{24,8},{1,17},{9,25},{17,1},{25,9},{2,18},{10... | collective-permute-start | bytes 940040 | tf_op jit(solution)/shard_map/ppermute | solution.py:273
  44.0 1.3 %collective-permute-start.15 = (s16[136,1152]{1,0:T(8,128)(2,1)S(1)}, s16[136,1152]{1,0:T(8,128)(2,1)S(1)}, u32[]{:S(2)}, u32[]{:S(2)}) collective-permute-start(s16[136,1152]{1,0:T(8,128)(2,1)S(1)} %get-tuple-element.46.refs_2_), channel_id=1, source_target_pairs={{0,4},{1,5},{2,6},{3,7},{4,0},{5,1},{6,2},{7,3},{8,12},{9,13},{10,... | collective-permute-start | bytes 940040 | tf_op jit(solution)/shard_map/ppermute | solution.py:273
  45.3 0.0 collective-permute-done.10.refs_1_
  45.3 0.2 passed_sum.3
  45.5 2.4 %collective-permute-start.12 = (s16[136,1152]{1,0:T(8,128)(2,1)S(1)}, s16[136,1152]{1,0:T(8,128)(2,1)S(1)}, u32[]{:S(2)}, u32[]{:S(2)}) collective-permute-start(s16[136,1152]{1,0:T(8,128)(2,1)S(1)} %get-tuple-element.48), channel_id=1, source_target_pairs={{0,2},{1,3},{2,0},{3,1},{4,6},{5,7},{6,4},{7,5},{8,10},{9,11},{10,... | collective-permute-start | bytes 940040 | tf_op jit(solution)/shard_map/ppermute | solution.py:273
  47.9 0.7 %collective-permute-start.13 = (s16[136,1152]{1,0:T(8,128)(2,1)S(1)}, s16[136,1152]{1,0:T(8,128)(2,1)S(1)}, u32[]{:S(2)}, u32[]{:S(2)}) collective-permute-start(s16[136,1152]{1,0:T(8,128)(2,1)S(1)} %get-tuple-element.49), channel_id=1, source_target_pairs={{0,8},{8,0},{16,24},{24,16},{1,9},{9,1},{17,25},{25,17},{2,10},{10... | collective-permute-start | bytes 940040 | tf_op jit(solution)/shard_map/ppermute | solution.py:273
  48.6 2.5 %collective-permute-done.14.refs_0_ = s16[136,1152]{1,0:T(8,128)(2,1)S(1)} collective-permute-done((s16[136,1152]{1,0:T(8,128)(2,1)S(1)}, s16[136,1152]{1,0:T(8,128)(2,1)S(1)}, u32[]{:S(2)}, u32[]{:S(2)}) %collective-permute-start.14) | collective-permute-done | bytes 313376 | tf_op jit(solution)/shard_map/ppermute | solution.py:273
  51.0 8.9 %collective-permute-done.15.refs_1_ = s16[136,1152]{1,0:T(8,128)(2,1)S(1)} collective-permute-done((s16[136,1152]{1,0:T(8,128)(2,1)S(1)}, s16[136,1152]{1,0:T(8,128)(2,1)S(1)}, u32[]{:S(2)}, u32[]{:S(2)}) %collective-permute-start.15) | collective-permute-done | bytes 313376 | tf_op jit(solution)/shard_map/ppermute | solution.py:273
  60.0 0.0 collective-permute-done.12.refs_2_
  60.0 0.0 collective-permute-done.13.refs_3_
  60.0 1.2 %output_sums.1 = (f32[128,1152]{1,0:T(8,128)}, f32[128,1152]{1,0:T(8,128)}) custom-call(f32[1]{0:T(128)S(6)} %copy.17.refs_0_, f32[128,1152]{1,0:T(8,128)S(1)} %get-tuple-element.43.refs_1_, s16[136,1152]{1,0:T(8,128)(2,1)S(1)} %collective-permute-done.12.refs_2_, s16[136,1152]{1,0:T(8,128)(2,1)S(1)} %collective-permute-done.13.refs_3_, ...), custom_call_target="tpu_custom_call" | custom-call | flops 128 | bytes 128 | tf_op jit(solution)/shard_map/output_sums/pallas_call | solution.py:92
  (5 shorter events, 0.1 us)
Async XLA Ops:
  0.6 17.8 %collective-permute-start = (bf16[128,1152]{1,0:T(8,128)(2,1)}, bf16[128,1152]{1,0:T(8,128)(2,1)S(1)}, u32[]{:S(2)}, u32[]{:S(2)}) collective-permute-start(bf16[128,1152]{1,0:T(8,128)(2,1)} %refs_6_.7), channel_id=1, source_target_pairs={{0,4},{1,5},{2,6},{3,7},{4,0},{5,1},{6,2},{7,3},{8,12},{9,13},{10,... | collective-permute-start | bytes 884744 | tf_op jit(solution)/shard_map/ppermute | solution.py:273
  4.7 13.9 %collective-permute-start.1 = (bf16[128,1152]{1,0:T(8,128)(2,1)}, bf16[128,1152]{1,0:T(8,128)(2,1)S(1)}, u32[]{:S(2)}, u32[]{:S(2)}) collective-permute-start(bf16[128,1152]{1,0:T(8,128)(2,1)} %refs_0_.8), channel_id=1, source_target_pairs={{0,2},{1,3},{2,0},{3,1},{4,6},{5,7},{6,4},{7,5},{8,10},{9,11},{10,... | collective-permute-start | bytes 884744 | tf_op jit(solution)/shard_map/ppermute | solution.py:273
  6.3 1.0 %copy-start.1 = (bf16[128,1152]{1,0:T(8,128)(2,1)S(1)}, bf16[128,1152]{1,0:T(8,128)(2,1)}, u32[]{:S(2)}) copy-start(bf16[128,1152]{1,0:T(8,128)(2,1)} %refs_0_.8) | copy-start | bytes 884740
  7.3 0.7 %copy-start.2 = (s32[128]{0:T(128)S(1)}, s32[128]{0:T(128)}, u32[]{:S(2)}) copy-start(s32[128]{0:T(128)} %param.7) | copy-start | bytes 1540
  8.0 10.8 %copy-start = (bf16[128,1152]{1,0:T(8,128)(2,1)S(1)}, bf16[128,1152]{1,0:T(8,128)(2,1)}, u32[]{:S(2)}) copy-start(bf16[128,1152]{1,0:T(8,128)(2,1)} %refs_6_.7) | copy-start | bytes 884740
  8.0 10.7 %collective-permute-start.4 = (bf16[136,1152]{1,0:T(8,128)(2,1)S(1)}, bf16[136,1152]{1,0:T(8,128)(2,1)S(1)}, u32[]{:S(2)}, u32[]{:S(2)}) collective-permute-start(bf16[136,1152]{1,0:T(8,128)(2,1)S(1)} %labelled.3.refs_2_.refs_7_.refs_4_), channel_id=1, source_target_pairs={{0,8},{8,0},{16,24},{24,16},{1,9},{9,1},{17,25},{25,17},{2,10},{10... | collective-permute-start | bytes 940040 | tf_op jit(solution)/shard_map/ppermute | solution.py:273
  9.6 9.2 %collective-permute-start.3 = (bf16[128,1152]{1,0:T(8,128)(2,1)}, bf16[128,1152]{1,0:T(8,128)(2,1)S(1)}, u32[]{:S(2)}, u32[]{:S(2)}) collective-permute-start(bf16[128,1152]{1,0:T(8,128)(2,1)} %refs_6_.7), channel_id=1, source_target_pairs={{0,16},{8,24},{16,0},{24,8},{1,17},{9,25},{17,1},{25,9},{2,18},{10... | collective-permute-start | bytes 884744 | tf_op jit(solution)/shard_map/ppermute | solution.py:273
  11.1 7.6 %collective-permute-start.2 = (s32[1,128]{1,0:T(1,128)S(1)}, s32[1,128]{1,0:T(1,128)S(1)}, u32[]{:S(2)}, u32[]{:S(2)}) collective-permute-start(s32[1,128]{1,0:T(1,128)S(1)} %bitcast.2), channel_id=1, source_target_pairs={{0,2},{1,3},{2,0},{3,1},{4,6},{5,7},{6,4},{7,5},{8,10},{9,11},{10,... | collective-permute-start | bytes 1544 | tf_op jit(solution)/shard_map/ppermute | solution.py:273
  18.9 4.5 %collective-permute-start.7 = (bf16[792,1152]{1,0:T(8,128)(2,1)S(1)}, bf16[792,1152]{1,0:T(8,128)(2,1)S(1)}, u32[]{:S(2)}, u32[]{:S(2)}) collective-permute-start(bf16[792,1152]{1,0:T(8,128)(2,1)S(1)} %bundled.3), channel_id=1, source_target_pairs={{0,1},{1,0},{2,3},{3,2},{4,5},{5,4},{6,7},{7,6},{8,9},{9,8},{10,11... | collective-permute-start | bytes 5474312 | tf_op jit(solution)/shard_map/ppermute | solution.py:273
  19.0 10.7 %collective-permute-start.6 = (bf16[136,1152]{1,0:T(8,128)(2,1)S(1)}, bf16[136,1152]{1,0:T(8,128)(2,1)S(1)}, u32[]{:S(2)}, u32[]{:S(2)}) collective-permute-start(bf16[136,1152]{1,0:T(8,128)(2,1)S(1)} %labelled.2.refs_1_.refs_3_.refs_5_), channel_id=1, source_target_pairs={{0,8},{8,0},{16,24},{24,16},{1,9},{9,1},{17,25},{25,17},{2,10},{10... | collective-permute-start | bytes 940040 | tf_op jit(solution)/shard_map/ppermute | solution.py:273
  20.6 9.1 %collective-permute-start.5 = (bf16[128,1152]{1,0:T(8,128)(2,1)S(1)}, bf16[128,1152]{1,0:T(8,128)(2,1)S(1)}, u32[]{:S(2)}, u32[]{:S(2)}) collective-permute-start(bf16[128,1152]{1,0:T(8,128)(2,1)S(1)} %held.2.refs_2_.refs_0_.refs_5_), channel_id=1, source_target_pairs={{0,16},{8,24},{16,0},{24,8},{1,17},{9,25},{17,1},{25,9},{2,18},{10... | collective-permute-start | bytes 884744 | tf_op jit(solution)/shard_map/ppermute | solution.py:273
  29.7 1.6 %collective-permute-start.9 = (bf16[136,1152]{1,0:T(8,128)(2,1)S(1)}, bf16[136,1152]{1,0:T(8,128)(2,1)S(1)}, u32[]{:S(2)}, u32[]{:S(2)}) collective-permute-start(bf16[136,1152]{1,0:T(8,128)(2,1)S(1)} %collective-permute-done.6.refs_3_.refs_8_), channel_id=1, source_target_pairs={{0,1},{1,0},{2,3},{3,2},{4,5},{5,4},{6,7},{7,6},{8,9},{9,8},{10,11... | collective-permute-start | bytes 940040 | tf_op jit(solution)/shard_map/ppermute | solution.py:273
  29.7 4.6 %collective-permute-start.8 = (bf16[128,1152]{1,0:T(8,128)(2,1)S(1)}, bf16[128,1152]{1,0:T(8,128)(2,1)S(1)}, u32[]{:S(2)}, u32[]{:S(2)}) collective-permute-start(bf16[128,1152]{1,0:T(8,128)(2,1)S(1)} %collective-permute-done.5.refs_2_.refs_8_), channel_id=1, source_target_pairs={{0,1},{1,0},{2,3},{3,2},{4,5},{5,4},{6,7},{7,6},{8,9},{9,8},{10,11... | collective-permute-start | bytes 884744 | tf_op jit(solution)/shard_map/ppermute | solution.py:273
  32.7 9.5 %collective-permute-start.11 = (s16[136,1152]{1,0:T(8,128)(2,1)S(1)}, s16[136,1152]{1,0:T(8,128)(2,1)S(1)}, u32[]{:S(2)}, u32[]{:S(2)}) collective-permute-start(s16[136,1152]{1,0:T(8,128)(2,1)S(1)} %late_rows.2.refs_9_), channel_id=1, source_target_pairs={{0,16},{8,24},{16,0},{24,8},{1,17},{9,25},{17,1},{25,9},{2,18},{10... | collective-permute-start | bytes 940040 | tf_op jit(solution)/shard_map/ppermute | solution.py:273
  35.7 9.6 %collective-permute-start.10 = (s16[136,1152]{1,0:T(8,128)(2,1)S(1)}, s16[136,1152]{1,0:T(8,128)(2,1)S(1)}, u32[]{:S(2)}, u32[]{:S(2)}) collective-permute-start(s16[136,1152]{1,0:T(8,128)(2,1)S(1)} %late_rows.3.refs_13_), channel_id=1, source_target_pairs={{0,8},{8,0},{16,24},{24,16},{1,9},{9,1},{17,25},{25,17},{2,10},{10... | collective-permute-start | bytes 940040 | tf_op jit(solution)/shard_map/ppermute | solution.py:273
  42.4 8.7 %collective-permute-start.14 = (s16[136,1152]{1,0:T(8,128)(2,1)S(1)}, s16[136,1152]{1,0:T(8,128)(2,1)S(1)}, u32[]{:S(2)}, u32[]{:S(2)}) collective-permute-start(s16[136,1152]{1,0:T(8,128)(2,1)S(1)} %get-tuple-element.51), channel_id=1, source_target_pairs={{0,16},{8,24},{16,0},{24,8},{1,17},{9,25},{17,1},{25,9},{2,18},{10... | collective-permute-start | bytes 940040 | tf_op jit(solution)/shard_map/ppermute | solution.py:273
  44.0 16.0 %collective-permute-start.15 = (s16[136,1152]{1,0:T(8,128)(2,1)S(1)}, s16[136,1152]{1,0:T(8,128)(2,1)S(1)}, u32[]{:S(2)}, u32[]{:S(2)}) collective-permute-start(s16[136,1152]{1,0:T(8,128)(2,1)S(1)} %get-tuple-element.46.refs_2_), channel_id=1, source_target_pairs={{0,4},{1,5},{2,6},{3,7},{4,0},{5,1},{6,2},{7,3},{8,12},{9,13},{10,... | collective-permute-start | bytes 940040 | tf_op jit(solution)/shard_map/ppermute | solution.py:273
  45.5 14.5 %collective-permute-start.12 = (s16[136,1152]{1,0:T(8,128)(2,1)S(1)}, s16[136,1152]{1,0:T(8,128)(2,1)S(1)}, u32[]{:S(2)}, u32[]{:S(2)}) collective-permute-start(s16[136,1152]{1,0:T(8,128)(2,1)S(1)} %get-tuple-element.48), channel_id=1, source_target_pairs={{0,2},{1,3},{2,0},{3,1},{4,6},{5,7},{6,4},{7,5},{8,10},{9,11},{10,... | collective-permute-start | bytes 940040 | tf_op jit(solution)/shard_map/ppermute | solution.py:273
  47.9 12.1 %collective-permute-start.13 = (s16[136,1152]{1,0:T(8,128)(2,1)S(1)}, s16[136,1152]{1,0:T(8,128)(2,1)S(1)}, u32[]{:S(2)}, u32[]{:S(2)}) collective-permute-start(s16[136,1152]{1,0:T(8,128)(2,1)S(1)} %get-tuple-element.49), channel_id=1, source_target_pairs={{0,8},{8,0},{16,24},{24,16},{1,9},{9,1},{17,25},{25,17},{2,10},{10... | collective-permute-start | bytes 940040 | tf_op jit(solution)/shard_map/ppermute | solution.py:273

commit v11 on v10

--- a/solution.py
+++ b/solution.py
@@ -25,7 +25,7 @@
 
 
 def part_widths(width):
-    first = min(3 * TILE, width - LANES)
+    first = (width // LANES + 1) // 2 * LANES
     return (first, width - first)
 
 
@@ -274,22 +274,24 @@
 
 
 def scattered(kept, coded, steps, after):
-    def sent(block, step):
-        return [(swapped(p, step), 0, 0) for p in block]
-
-    half, waiting = len(kept), coded[0]
-    received = [[]] + [[sent(c, steps[-1])] for c in coded[1:]]
+    def sent(array, step):
+        return (swapped(array, step), 0, 0)
+
+    half = len(kept)
+    received = [[]] + [[(sent(c[0], steps[-1]),)] for c in coded[1:]]
+    waiting, last = [c[1] for c in coded[1:]], [coded[0][0]]
     for s in reversed(range(len(steps) - 1)):
         for m in reversed(range(1 << s)):
             n = m | 1 << s
-            block = passed_sum(kept[n], received[n], None, waiting, after)
-            after = block[:1]
-            if n == half - 1:
-                block, *waiting = block
-                received[0].append(sent(waiting, steps[-1]))
-                waiting, block = (), [block]
-            received[m].append(sent(block, steps[s]))
-    return (kept[0], received[0][::-1]), after
+            first, *begun = passed_sum(kept[n], received[n], 0, waiting)
+            for r, c in zip(received[1:], begun):
+                r[0] = r[0] + (sent(c, steps[-1]),)
+            first = sent(first, steps[s])
+            second, *ended = passed_sum(kept[n], received[n], 1, last, [first[0], *after])
+            received[0] += [(sent(c, steps[-1]),) for c in ended]
+            received[m].append((first, sent(second, steps[s])))
+            waiting, last, after = (), (), [second]
+    return kept[0], received[0], after
 
 
 def in_order(arrays):
@@ -372,18 +374,18 @@
     every, after = list(range(count)), ()
     coded, kept = [[None] * half, [None] * half], [None, None]
     for k in (1, 0):
-        jobs, emits = [(list(range(len(late))), list(range(2 * count)))], ["whole"] * len(late)
+        jobs, emits = [(list(range(len(late))), list(range(2 * count)))], ["parts"] * len(late)
         coded[k][1:] = sums("late_rows", k, late, every, (0, 1), jobs, {}, emits, after)
         after = coded[k][1]
     for k in (1, 0):
         jobs, emits = [(early, list(range(2 * len(late))))], ["float"] * half + ["whole"]
         *whole_sums, coded[k][0] = sums("late_columns", k, early, late, (0, 1), jobs, before[k], emits, after)
         kept[k], after = [s for (s,) in whole_sums], coded[k][0]
-    texts, after = scattered(kept[1], coded[1], steps[1], ())
-    images, _ = scattered(kept[0], coded[0], steps[0], after)
-    kept_texts, blocks_in = texts
-    blocks_in = [whole(a) for a in in_order([a for ((a, _, _),) in blocks_in[::-1]])]
-    return tuple(output_sums(scalars[0], [images, (kept_texts, blocks_in)]))
+    kept_texts, text_blocks, after = scattered(kept[1], coded[1], steps[1], ())
+    kept_images, image_blocks, _ = scattered(kept[0], coded[0], steps[0], after)
+    parts = iter(in_order([part[0] for b in text_blocks for part in b]))
+    text_blocks = [tuple((next(parts), 0, 0) for _ in b) for b in text_blocks]
+    return tuple(output_sums(scalars[0], [(kept_images, image_blocks), (kept_texts, text_blocks)]))
 
 
 def solution(mesh):

time: 61.4 us -> 61.8 us (level)
  starting transfers between devices: 21.2 us -> 25.6 us
  waiting for transfers between devices: 25.2 us -> 21.2 us
    ppermute x16 -> x20, starting transfers between devices: 21.2 us -> 25.6 us  [swapped(): lax.ppermute(array, axis, [(i, i ^ bit) for i in range(lax.axis_size(axis...]
    ppermute x16 -> x20, waiting for transfers between devices: 25.2 us -> 21.2 us  [swapped(): lax.ppermute(array, axis, [(i, i ^ bit) for i in range(lax.axis_size(axis...]
    pallas_call x15 -> x17, Pallas kernels: 11.1 us -> 11.1 us  [call(): pl.pallas_call(body, out_shape=[*out_shape, *(jax.ShapeDtypeStruct(a.shap...]
  transfers between devices with their start and end apart: 16 -> 20, of which waited for: 7 -> 10; matrix products, arithmetic and copies ran while one was open for 0% -> 0% of each run, Pallas kernels for 16% -> 16%
where the time goes in v11:
time: 61.8 us; the launch traced here: 61.6 us
  starting transfers between devices  25.6 us (41%)
  waiting for transfers between devices  21.2 us (34%)
  Pallas kernels  11.1 us (18%)
  between operations  2.08 us (3%)
  local copies, waits for them, and re-layouts  1.66 us (3%)
    ppermute x20, starting transfers between devices, swapped(): lax.ppermute(array, axis, [(i, i ^ bit) for i in range(lax.axis_size(axis...  25.6 us
    ppermute x20, waiting for transfers between devices, swapped(): lax.ppermute(array, axis, [(i, i ^ bit) for i in range(lax.axis_size(axis...  21.2 us
    pallas_call x17, Pallas kernels, call(): pl.pallas_call(body, out_shape=[*out_shape, *(jax.ShapeDtypeStruct(a.shap...  11.1 us
    unnamed x6, local copies, waits for them, and re-layouts  1.66 us
  transfers between devices with their start and end apart: 20, of which 10 were waited for; matrix products, arithmetic and copies ran while one was open for 0% of the time, Pallas kernels for 16%

profile of v11, /device:TPU:0, one launch (start us, length us, event | category | flops | bytes accessed | tf_op | source)
XLA Modules:
  0.0 61.6 jit_solution(3266468456435199140)
XLA Ops:
  0.6 4.1 %collective-permute-start = (bf16[128,1152]{1,0:T(8,128)(2,1)}, bf16[128,1152]{1,0:T(8,128)(2,1)S(1)}, u32[]{:S(2)}, u32[]{:S(2)}) collective-permute-start(bf16[128,1152]{1,0:T(8,128)(2,1)} %refs_6_.7), channel_id=1, source_target_pairs={{0,4},{1,5},{2,6},{3,7},{4,0},{5,1},{6,2},{7,3},{8,12},{9,13},{10,... | collective-permute-start | bytes 884744 | tf_op jit(solution)/shard_map/ppermute | solution.py:273
  4.7 1.6 %collective-permute-start.1 = (bf16[128,1152]{1,0:T(8,128)(2,1)}, bf16[128,1152]{1,0:T(8,128)(2,1)S(1)}, u32[]{:S(2)}, u32[]{:S(2)}) collective-permute-start(bf16[128,1152]{1,0:T(8,128)(2,1)} %refs_0_.8), channel_id=1, source_target_pairs={{0,2},{1,3},{2,0},{3,1},{4,6},{5,7},{6,4},{7,5},{8,10},{9,11},{10,... | collective-permute-start | bytes 884744 | tf_op jit(solution)/shard_map/ppermute | solution.py:273
  6.3 0.0 copy-start.1
  6.3 1.0 %copy-done.1 = bf16[128,1152]{1,0:T(8,128)(2,1)S(1)} copy-done((bf16[128,1152]{1,0:T(8,128)(2,1)S(1)}, bf16[128,1152]{1,0:T(8,128)(2,1)}, u32[]{:S(2)}) %copy-start.1) | copy-done | bytes 294936
  7.3 0.0 copy-start.2
  7.3 0.7 %copy-done.2 = s32[128]{0:T(128)S(1)} copy-done((s32[128]{0:T(128)S(1)}, s32[128]{0:T(128)}, u32[]{:S(2)}) %copy-start.2) | copy-done | bytes 536
  8.0 0.0 copy-start
  8.0 1.6 %collective-permute-start.4 = (bf16[136,1152]{1,0:T(8,128)(2,1)S(1)}, bf16[136,1152]{1,0:T(8,128)(2,1)S(1)}, u32[]{:S(2)}, u32[]{:S(2)}) collective-permute-start(bf16[136,1152]{1,0:T(8,128)(2,1)S(1)} %labelled.3.refs_2_.refs_7_.refs_4_), channel_id=1, source_target_pairs={{0,8},{8,0},{16,24},{24,16},{1,9},{9,1},{17,25},{25,17},{2,10},{10... | collective-permute-start | bytes 940040 | tf_op jit(solution)/shard_map/ppermute | solution.py:273
  9.6 1.5 %collective-permute-start.3 = (bf16[128,1152]{1,0:T(8,128)(2,1)}, bf16[128,1152]{1,0:T(8,128)(2,1)S(1)}, u32[]{:S(2)}, u32[]{:S(2)}) collective-permute-start(bf16[128,1152]{1,0:T(8,128)(2,1)} %refs_6_.7), channel_id=1, source_target_pairs={{0,16},{8,24},{16,0},{24,8},{1,17},{9,25},{17,1},{25,9},{2,18},{10... | collective-permute-start | bytes 884744 | tf_op jit(solution)/shard_map/ppermute | solution.py:273
  11.1 0.4 collective-permute-start.2
  11.5 6.8 %collective-permute-done.refs_0_ = bf16[128,1152]{1,0:T(8,128)(2,1)S(1)} collective-permute-done((bf16[128,1152]{1,0:T(8,128)(2,1)}, bf16[128,1152]{1,0:T(8,128)(2,1)S(1)}, u32[]{:S(2)}, u32[]{:S(2)}) %collective-permute-start) | collective-permute-done | bytes 294944 | tf_op jit(solution)/shard_map/ppermute | solution.py:273
  18.4 0.3 collective-permute-done.2.refs_1_
  18.6 0.0 collective-permute-done.1.refs_0_
  18.7 0.0 collective-permute-done.3.refs_3_.refs_4_.refs_6_
  18.7 0.0 collective-permute-done.4.refs_4_.refs_5_.refs_6_
  18.7 0.0 copy-done
  18.8 0.1 bundled.3
  18.9 0.1 collective-permute-start.7
  19.0 1.6 %collective-permute-start.6 = (bf16[136,1152]{1,0:T(8,128)(2,1)S(1)}, bf16[136,1152]{1,0:T(8,128)(2,1)S(1)}, u32[]{:S(2)}, u32[]{:S(2)}) collective-permute-start(bf16[136,1152]{1,0:T(8,128)(2,1)S(1)} %labelled.2.refs_1_.refs_3_.refs_5_), channel_id=1, source_target_pairs={{0,8},{8,0},{16,24},{24,16},{1,9},{9,1},{17,25},{25,17},{2,10},{10... | collective-permute-start | bytes 940040 | tf_op jit(solution)/shard_map/ppermute | solution.py:273
  20.6 1.5 %collective-permute-start.5 = (bf16[128,1152]{1,0:T(8,128)(2,1)S(1)}, bf16[128,1152]{1,0:T(8,128)(2,1)S(1)}, u32[]{:S(2)}, u32[]{:S(2)}) collective-permute-start(bf16[128,1152]{1,0:T(8,128)(2,1)S(1)} %held.2.refs_2_.refs_0_.refs_5_), channel_id=1, source_target_pairs={{0,16},{8,24},{16,0},{24,8},{1,17},{9,25},{17,1},{25,9},{2,18},{10... | collective-permute-start | bytes 884744 | tf_op jit(solution)/shard_map/ppermute | solution.py:273
  23.4 0.0 collective-permute-done.7.refs_8_.refs_7_
  23.4 1.9 %early_sums.3 = (f32[128,1152]{1,0:T(8,128)S(1)}, f32[128,1152]{1,0:T(8,128)S(1)}, f32[128,1152]{1,0:T(8,128)S(1)}) custom-call(f32[1]{0:T(128)S(6)} %copy.23.refs_0_, f32[1]{0:T(128)S(6)} %copy.24.refs_1_, bf16[128,1152]{1,0:T(8,128)(2,1)S(1)} %held.2.refs_2_.refs_0_.refs_5_, bf16[136,1152]{1,0:T(8,128)(2,1)S(1)} %labelled.2.refs_1_.refs_3_.refs_5_, ...), custom_call_target="tpu_custom_call" | custom-call | flops 2304 | bytes 2304 | tf_op jit(solution)/shard_map/early_sums/pallas_call | solution.py:92
  25.3 1.9 %early_sums.2 = (f32[128,1152]{1,0:T(8,128)S(1)}, f32[128,1152]{1,0:T(8,128)S(1)}, f32[128,1152]{1,0:T(8,128)S(1)}) custom-call(f32[1]{0:T(128)S(6)} %copy.23.refs_0_, f32[1]{0:T(128)S(6)} %copy.24.refs_1_, bf16[128,1152]{1,0:T(8,128)(2,1)S(1)} %held.2.refs_2_.refs_0_.refs_5_, bf16[136,1152]{1,0:T(8,128)(2,1)S(1)} %labelled.2.refs_1_.refs_3_.refs_5_, ...), custom_call_target="tpu_custom_call" | custom-call | flops 2304 | bytes 2304 | tf_op jit(solution)/shard_map/early_sums/pallas_call | solution.py:92
  27.3 2.4 %collective-permute-done.5.refs_2_.refs_8_ = bf16[128,1152]{1,0:T(8,128)(2,1)S(1)} collective-permute-done((bf16[128,1152]{1,0:T(8,128)(2,1)S(1)}, bf16[128,1152]{1,0:T(8,128)(2,1)S(1)}, u32[]{:S(2)}, u32[]{:S(2)}) %collective-permute-start.5) | collective-permute-done | bytes 294944 | tf_op jit(solution)/shard_map/ppermute | solution.py:273
  29.7 0.0 collective-permute-done.6.refs_3_.refs_8_
  29.7 0.0 collective-permute-start.9
  29.7 0.5 collective-permute-start.8
  30.2 1.1 %collective-permute-done.9.refs_8_.refs_9_ = bf16[136,1152]{1,0:T(8,128)(2,1)S(1)} collective-permute-done((bf16[136,1152]{1,0:T(8,128)(2,1)S(1)}, bf16[136,1152]{1,0:T(8,128)(2,1)S(1)}, u32[]{:S(2)}, u32[]{:S(2)}) %collective-permute-start.9) | collective-permute-done | bytes 313376 | tf_op jit(solution)/shard_map/ppermute | solution.py:273
  31.3 1.4 %late_rows.2 = (s16[136,640]{1,0:T(8,128)(2,1)S(1)}, s16[136,512]{1,0:T(8,128)(2,1)S(1)}) custom-call(f32[1]{0:T(128)S(6)} %copy.23.refs_0_, f32[1]{0:T(128)S(6)} %copy.24.refs_1_, bf16[128,1152]{1,0:T(8,128)(2,1)S(1)} %collective-permute-done.5.refs_2_.refs_8_, bf16[136,1152]{1,0:T(8,128)(2,1)S(1)} %collective-permute-done.6.refs_3_.refs_8_, ...), custom_call_target="tpu_custom_call" | custom-call | flops 1024 | bytes 1024 | tf_op jit(solution)/shard_map/late_rows/pallas_call | solution.py:92
  32.7 1.6 %collective-permute-start.13 = (s16[136,640]{1,0:T(8,128)(2,1)S(1)}, s16[136,640]{1,0:T(8,128)(2,1)S(1)}, u32[]{:S(2)}, u32[]{:S(2)}) collective-permute-start(s16[136,640]{1,0:T(8,128)(2,1)S(1)} %get-tuple-element.51.refs_9_), channel_id=1, source_target_pairs={{0,16},{8,24},{16,0},{24,8},{1,17},{9,25},{17,1},{25,9},{2,18},{10... | collective-permute-start | bytes 522248 | tf_op jit(solution)/shard_map/ppermute | solution.py:273
  34.3 0.0 collective-permute-done.8.refs_8_.refs_9_
  34.3 1.4 %late_rows.3 = (s16[136,640]{1,0:T(8,128)(2,1)S(1)}, s16[136,512]{1,0:T(8,128)(2,1)S(1)}) custom-call(f32[1]{0:T(128)S(6)} %copy.23.refs_0_, f32[1]{0:T(128)S(6)} %copy.24.refs_1_, bf16[128,1152]{1,0:T(8,128)(2,1)S(1)} %collective-permute-done.5.refs_2_.refs_8_, bf16[136,1152]{1,0:T(8,128)(2,1)S(1)} %collective-permute-done.6.refs_3_.refs_8_, ...), custom_call_target="tpu_custom_call" | custom-call | flops 1024 | bytes 1024 | tf_op jit(solution)/shard_map/late_rows/pallas_call | solution.py:92
  35.7 0.7 %collective-permute-start.10 = (s16[136,640]{1,0:T(8,128)(2,1)S(1)}, s16[136,640]{1,0:T(8,128)(2,1)S(1)}, u32[]{:S(2)}, u32[]{:S(2)}) collective-permute-start(s16[136,640]{1,0:T(8,128)(2,1)S(1)} %get-tuple-element.53.refs_13_), channel_id=1, source_target_pairs={{0,8},{8,0},{16,24},{24,16},{1,9},{9,1},{17,25},{25,17},{2,10},{10... | collective-permute-start | bytes 522248 | tf_op jit(solution)/shard_map/ppermute | solution.py:273
  36.5 1.3 %late_columns.2 = (f32[128,1152]{1,0:T(8,128)S(1)}, f32[128,1152]{1,0:T(8,128)S(1)}, s16[136,1152]{1,0:T(8,128)(2,1)S(1)}) custom-call(f32[1]{0:T(128)S(6)} %copy.23.refs_0_, f32[1]{0:T(128)S(6)} %copy.24.refs_1_, bf16[128,1152]{1,0:T(8,128)(2,1)S(1)} %held.2.refs_2_.refs_0_.refs_5_, bf16[136,1152]{1,0:T(8,128)(2,1)S(1)} %labelled.2.refs_1_.refs_3_.refs_5_, ...), custom_call_target="tpu_custom_call" | custom-call | flops 768 | bytes 768 | tf_op jit(solution)/shard_map/late_columns/pallas_call | solution.py:92
  37.8 1.3 %late_columns.3 = (f32[128,1152]{1,0:T(8,128)S(1)}, f32[128,1152]{1,0:T(8,128)S(1)}, s16[136,1152]{1,0:T(8,128)(2,1)S(1)}) custom-call(f32[1]{0:T(128)S(6)} %copy.23.refs_0_, f32[1]{0:T(128)S(6)} %copy.24.refs_1_, bf16[128,1152]{1,0:T(8,128)(2,1)S(1)} %held.2.refs_2_.refs_0_.refs_5_, bf16[136,1152]{1,0:T(8,128)(2,1)S(1)} %labelled.2.refs_1_.refs_3_.refs_5_, ...), custom_call_target="tpu_custom_call" | custom-call | flops 768 | bytes 768 | tf_op jit(solution)/shard_map/late_columns/pallas_call | solution.py:92
  39.1 0.2 collective-permute-done.13.refs_1_
  39.2 0.1 passed_sum.5
  39.3 1.4 %collective-permute-start.15 = (s16[136,640]{1,0:T(8,128)(2,1)S(1)}, s16[136,640]{1,0:T(8,128)(2,1)S(1)}, u32[]{:S(2)}, u32[]{:S(2)}) collective-permute-start(s16[136,640]{1,0:T(8,128)(2,1)S(1)} %get-tuple-element.62), channel_id=1, source_target_pairs={{0,4},{1,5},{2,6},{3,7},{4,0},{5,1},{6,2},{7,3},{8,12},{9,13},{10,... | collective-permute-start | bytes 522248 | tf_op jit(solution)/shard_map/ppermute | solution.py:273
  40.7 1.2 %collective-permute-done.10.refs_1_ = s16[136,640]{1,0:T(8,128)(2,1)S(1)} collective-permute-done((s16[136,640]{1,0:T(8,128)(2,1)S(1)}, s16[136,640]{1,0:T(8,128)(2,1)S(1)}, u32[]{:S(2)}, u32[]{:S(2)}) %collective-permute-start.10) | collective-permute-done | bytes 174112 | tf_op jit(solution)/shard_map/ppermute | solution.py:273
  42.0 0.1 passed_sum.4
  42.1 1.5 %collective-permute-start.12 = (s16[136,640]{1,0:T(8,128)(2,1)S(1)}, s16[136,640]{1,0:T(8,128)(2,1)S(1)}, u32[]{:S(2)}, u32[]{:S(2)}) collective-permute-start(s16[136,640]{1,0:T(8,128)(2,1)S(1)} %get-tuple-element.59), channel_id=1, source_target_pairs={{0,2},{1,3},{2,0},{3,1},{4,6},{5,7},{6,4},{7,5},{8,10},{9,11},{10,... | collective-permute-start | bytes 522248 | tf_op jit(solution)/shard_map/ppermute | solution.py:273
  43.6 1.2 %collective-permute-start.14 = (s16[136,512]{1,0:T(8,128)(2,1)S(1)}, s16[136,512]{1,0:T(8,128)(2,1)S(1)}, u32[]{:S(2)}, u32[]{:S(2)}) collective-permute-start(s16[136,512]{1,0:T(8,128)(2,1)S(1)} %get-tuple-element.61), channel_id=1, source_target_pairs={{0,16},{8,24},{16,0},{24,8},{1,17},{9,25},{17,1},{25,9},{2,18},{10... | collective-permute-start | bytes 417800 | tf_op jit(solution)/shard_map/ppermute | solution.py:273
  44.8 0.7 %collective-permute-start.11 = (s16[136,512]{1,0:T(8,128)(2,1)S(1)}, s16[136,512]{1,0:T(8,128)(2,1)S(1)}, u32[]{:S(2)}, u32[]{:S(2)}) collective-permute-start(s16[136,512]{1,0:T(8,128)(2,1)S(1)} %get-tuple-element.58), channel_id=1, source_target_pairs={{0,8},{8,0},{16,24},{24,16},{1,9},{9,1},{17,25},{25,17},{2,10},{10... | collective-permute-start | bytes 417800 | tf_op jit(solution)/shard_map/ppermute | solution.py:273
  45.5 3.2 %collective-permute-done.14.refs_1_ = s16[136,512]{1,0:T(8,128)(2,1)S(1)} collective-permute-done((s16[136,512]{1,0:T(8,128)(2,1)S(1)}, s16[136,512]{1,0:T(8,128)(2,1)S(1)}, u32[]{:S(2)}, u32[]{:S(2)}) %collective-permute-start.14) | collective-permute-done | bytes 139296 | tf_op jit(solution)/shard_map/ppermute | solution.py:273
  48.6 1.2 %collective-permute-done.15.refs_2_.refs_1_ = s16[136,640]{1,0:T(8,128)(2,1)S(1)} collective-permute-done((s16[136,640]{1,0:T(8,128)(2,1)S(1)}, s16[136,640]{1,0:T(8,128)(2,1)S(1)}, u32[]{:S(2)}, u32[]{:S(2)}) %collective-permute-start.15) | collective-permute-done | bytes 174112 | tf_op jit(solution)/shard_map/ppermute | solution.py:273
  49.9 0.1 passed_sum.6
  50.0 1.4 %collective-permute-start.18 = (s16[136,1152]{1,0:T(8,128)(2,1)S(1)}, s16[136,1152]{1,0:T(8,128)(2,1)S(1)}, u32[]{:S(2)}, u32[]{:S(2)}) collective-permute-start(s16[136,1152]{1,0:T(8,128)(2,1)S(1)} %get-tuple-element.68), channel_id=1, source_target_pairs={{0,16},{8,24},{16,0},{24,8},{1,17},{9,25},{17,1},{25,9},{2,18},{10... | collective-permute-start | bytes 940040 | tf_op jit(solution)/shard_map/ppermute | solution.py:273
  51.4 0.0 collective-permute-done.11.refs_1_
  51.4 0.0 collective-permute-done.12.refs_2_.refs_3_
  51.4 0.1 passed_sum.7
  51.5 0.7 %collective-permute-start.16 = (s16[136,1152]{1,0:T(8,128)(2,1)S(1)}, s16[136,1152]{1,0:T(8,128)(2,1)S(1)}, u32[]{:S(2)}, u32[]{:S(2)}) collective-permute-start(s16[136,1152]{1,0:T(8,128)(2,1)S(1)} %get-tuple-element.65), channel_id=1, source_target_pairs={{0,8},{8,0},{16,24},{24,16},{1,9},{9,1},{17,25},{25,17},{2,10},{10... | collective-permute-start | bytes 940040 | tf_op jit(solution)/shard_map/ppermute | solution.py:273
  52.2 0.9 %collective-permute-start.19 = (s16[136,512]{1,0:T(8,128)(2,1)S(1)}, s16[136,512]{1,0:T(8,128)(2,1)S(1)}, u32[]{:S(2)}, u32[]{:S(2)}) collective-permute-start(s16[136,512]{1,0:T(8,128)(2,1)S(1)} %get-tuple-element.63.refs_3_), channel_id=1, source_target_pairs={{0,4},{1,5},{2,6},{3,7},{4,0},{5,1},{6,2},{7,3},{8,12},{9,13},{10,... | collective-permute-start | bytes 417800 | tf_op jit(solution)/shard_map/ppermute | solution.py:273
  53.2 2.5 %collective-permute-start.17 = (s16[136,512]{1,0:T(8,128)(2,1)S(1)}, s16[136,512]{1,0:T(8,128)(2,1)S(1)}, u32[]{:S(2)}, u32[]{:S(2)}) collective-permute-start(s16[136,512]{1,0:T(8,128)(2,1)S(1)} %get-tuple-element.66), channel_id=1, source_target_pairs={{0,2},{1,3},{2,0},{3,1},{4,6},{5,7},{6,4},{7,5},{8,10},{9,11},{10,... | collective-permute-start | bytes 417800 | tf_op jit(solution)/shard_map/ppermute | solution.py:273
  55.6 4.6 %collective-permute-done.19.refs_2_ = s16[136,512]{1,0:T(8,128)(2,1)S(1)} collective-permute-done((s16[136,512]{1,0:T(8,128)(2,1)S(1)}, s16[136,512]{1,0:T(8,128)(2,1)S(1)}, u32[]{:S(2)}, u32[]{:S(2)}) %collective-permute-start.19) | collective-permute-done | bytes 139296 | tf_op jit(solution)/shard_map/ppermute | solution.py:273
  60.3 0.0 collective-permute-done.18.refs_0_
  60.3 0.1 collective-permute-done.17.refs_4_
  60.4 0.0 collective-permute-done.16.refs_2_
  60.4 1.2 %output_sums.1 = (f32[128,1152]{1,0:T(8,128)}, f32[128,1152]{1,0:T(8,128)}) custom-call(f32[1]{0:T(128)S(6)} %copy.23.refs_0_, f32[128,1152]{1,0:T(8,128)S(1)} %get-tuple-element.56.refs_1_, s16[136,1152]{1,0:T(8,128)(2,1)S(1)} %collective-permute-done.16.refs_2_, s16[136,640]{1,0:T(8,128)(2,1)S(1)} %collective-permute-done.12.refs_2_.refs_3_, ...), custom_call_target="tpu_custom_call" | custom-call | flops 128 | bytes 128 | tf_op jit(solution)/shard_map/output_sums/pallas_call | solution.py:92
  (5 shorter events, 0.1 us)
Async XLA Ops:
  0.6 17.8 %collective-permute-start = (bf16[128,1152]{1,0:T(8,128)(2,1)}, bf16[128,1152]{1,0:T(8,128)(2,1)S(1)}, u32[]{:S(2)}, u32[]{:S(2)}) collective-permute-start(bf16[128,1152]{1,0:T(8,128)(2,1)} %refs_6_.7), channel_id=1, source_target_pairs={{0,4},{1,5},{2,6},{3,7},{4,0},{5,1},{6,2},{7,3},{8,12},{9,13},{10,... | collective-permute-start | bytes 884744 | tf_op jit(solution)/shard_map/ppermute | solution.py:273
  4.7 13.9 %collective-permute-start.1 = (bf16[128,1152]{1,0:T(8,128)(2,1)}, bf16[128,1152]{1,0:T(8,128)(2,1)S(1)}, u32[]{:S(2)}, u32[]{:S(2)}) collective-permute-start(bf16[128,1152]{1,0:T(8,128)(2,1)} %refs_0_.8), channel_id=1, source_target_pairs={{0,2},{1,3},{2,0},{3,1},{4,6},{5,7},{6,4},{7,5},{8,10},{9,11},{10,... | collective-permute-start | bytes 884744 | tf_op jit(solution)/shard_map/ppermute | solution.py:273
  6.3 1.0 %copy-start.1 = (bf16[128,1152]{1,0:T(8,128)(2,1)S(1)}, bf16[128,1152]{1,0:T(8,128)(2,1)}, u32[]{:S(2)}) copy-start(bf16[128,1152]{1,0:T(8,128)(2,1)} %refs_0_.8) | copy-start | bytes 884740
  7.3 0.7 %copy-start.2 = (s32[128]{0:T(128)S(1)}, s32[128]{0:T(128)}, u32[]{:S(2)}) copy-start(s32[128]{0:T(128)} %param.7) | copy-start | bytes 1540
  8.0 10.8 %copy-start = (bf16[128,1152]{1,0:T(8,128)(2,1)S(1)}, bf16[128,1152]{1,0:T(8,128)(2,1)}, u32[]{:S(2)}) copy-start(bf16[128,1152]{1,0:T(8,128)(2,1)} %refs_6_.7) | copy-start | bytes 884740
  8.0 10.7 %collective-permute-start.4 = (bf16[136,1152]{1,0:T(8,128)(2,1)S(1)}, bf16[136,1152]{1,0:T(8,128)(2,1)S(1)}, u32[]{:S(2)}, u32[]{:S(2)}) collective-permute-start(bf16[136,1152]{1,0:T(8,128)(2,1)S(1)} %labelled.3.refs_2_.refs_7_.refs_4_), channel_id=1, source_target_pairs={{0,8},{8,0},{16,24},{24,16},{1,9},{9,1},{17,25},{25,17},{2,10},{10... | collective-permute-start | bytes 940040 | tf_op jit(solution)/shard_map/ppermute | solution.py:273
  9.6 9.2 %collective-permute-start.3 = (bf16[128,1152]{1,0:T(8,128)(2,1)}, bf16[128,1152]{1,0:T(8,128)(2,1)S(1)}, u32[]{:S(2)}, u32[]{:S(2)}) collective-permute-start(bf16[128,1152]{1,0:T(8,128)(2,1)} %refs_6_.7), channel_id=1, source_target_pairs={{0,16},{8,24},{16,0},{24,8},{1,17},{9,25},{17,1},{25,9},{2,18},{10... | collective-permute-start | bytes 884744 | tf_op jit(solution)/shard_map/ppermute | solution.py:273
  11.1 7.6 %collective-permute-start.2 = (s32[1,128]{1,0:T(1,128)S(1)}, s32[1,128]{1,0:T(1,128)S(1)}, u32[]{:S(2)}, u32[]{:S(2)}) collective-permute-start(s32[1,128]{1,0:T(1,128)S(1)} %bitcast.2), channel_id=1, source_target_pairs={{0,2},{1,3},{2,0},{3,1},{4,6},{5,7},{6,4},{7,5},{8,10},{9,11},{10,... | collective-permute-start | bytes 1544 | tf_op jit(solution)/shard_map/ppermute | solution.py:273
  18.9 4.5 %collective-permute-start.7 = (bf16[792,1152]{1,0:T(8,128)(2,1)S(1)}, bf16[792,1152]{1,0:T(8,128)(2,1)S(1)}, u32[]{:S(2)}, u32[]{:S(2)}) collective-permute-start(bf16[792,1152]{1,0:T(8,128)(2,1)S(1)} %bundled.3), channel_id=1, source_target_pairs={{0,1},{1,0},{2,3},{3,2},{4,5},{5,4},{6,7},{7,6},{8,9},{9,8},{10,11... | collective-permute-start | bytes 5474312 | tf_op jit(solution)/shard_map/ppermute | solution.py:273
  19.0 10.7 %collective-permute-start.6 = (bf16[136,1152]{1,0:T(8,128)(2,1)S(1)}, bf16[136,1152]{1,0:T(8,128)(2,1)S(1)}, u32[]{:S(2)}, u32[]{:S(2)}) collective-permute-start(bf16[136,1152]{1,0:T(8,128)(2,1)S(1)} %labelled.2.refs_1_.refs_3_.refs_5_), channel_id=1, source_target_pairs={{0,8},{8,0},{16,24},{24,16},{1,9},{9,1},{17,25},{25,17},{2,10},{10... | collective-permute-start | bytes 940040 | tf_op jit(solution)/shard_map/ppermute | solution.py:273
  20.6 9.1 %collective-permute-start.5 = (bf16[128,1152]{1,0:T(8,128)(2,1)S(1)}, bf16[128,1152]{1,0:T(8,128)(2,1)S(1)}, u32[]{:S(2)}, u32[]{:S(2)}) collective-permute-start(bf16[128,1152]{1,0:T(8,128)(2,1)S(1)} %held.2.refs_2_.refs_0_.refs_5_), channel_id=1, source_target_pairs={{0,16},{8,24},{16,0},{24,8},{1,17},{9,25},{17,1},{25,9},{2,18},{10... | collective-permute-start | bytes 884744 | tf_op jit(solution)/shard_map/ppermute | solution.py:273
  29.7 1.6 %collective-permute-start.9 = (bf16[136,1152]{1,0:T(8,128)(2,1)S(1)}, bf16[136,1152]{1,0:T(8,128)(2,1)S(1)}, u32[]{:S(2)}, u32[]{:S(2)}) collective-permute-start(bf16[136,1152]{1,0:T(8,128)(2,1)S(1)} %collective-permute-done.6.refs_3_.refs_8_), channel_id=1, source_target_pairs={{0,1},{1,0},{2,3},{3,2},{4,5},{5,4},{6,7},{7,6},{8,9},{9,8},{10,11... | collective-permute-start | bytes 940040 | tf_op jit(solution)/shard_map/ppermute | solution.py:273
  29.7 4.6 %collective-permute-start.8 = (bf16[128,1152]{1,0:T(8,128)(2,1)S(1)}, bf16[128,1152]{1,0:T(8,128)(2,1)S(1)}, u32[]{:S(2)}, u32[]{:S(2)}) collective-permute-start(bf16[128,1152]{1,0:T(8,128)(2,1)S(1)} %collective-permute-done.5.refs_2_.refs_8_), channel_id=1, source_target_pairs={{0,1},{1,0},{2,3},{3,2},{4,5},{5,4},{6,7},{7,6},{8,9},{9,8},{10,11... | collective-permute-start | bytes 884744 | tf_op jit(solution)/shard_map/ppermute | solution.py:273
  32.7 6.5 %collective-permute-start.13 = (s16[136,640]{1,0:T(8,128)(2,1)S(1)}, s16[136,640]{1,0:T(8,128)(2,1)S(1)}, u32[]{:S(2)}, u32[]{:S(2)}) collective-permute-start(s16[136,640]{1,0:T(8,128)(2,1)S(1)} %get-tuple-element.51.refs_9_), channel_id=1, source_target_pairs={{0,16},{8,24},{16,0},{24,8},{1,17},{9,25},{17,1},{25,9},{2,18},{10... | collective-permute-start | bytes 522248 | tf_op jit(solution)/shard_map/ppermute | solution.py:273
  35.7 6.3 %collective-permute-start.10 = (s16[136,640]{1,0:T(8,128)(2,1)S(1)}, s16[136,640]{1,0:T(8,128)(2,1)S(1)}, u32[]{:S(2)}, u32[]{:S(2)}) collective-permute-start(s16[136,640]{1,0:T(8,128)(2,1)S(1)} %get-tuple-element.53.refs_13_), channel_id=1, source_target_pairs={{0,8},{8,0},{16,24},{24,16},{1,9},{9,1},{17,25},{25,17},{2,10},{10... | collective-permute-start | bytes 522248 | tf_op jit(solution)/shard_map/ppermute | solution.py:273
  39.3 10.5 %collective-permute-start.15 = (s16[136,640]{1,0:T(8,128)(2,1)S(1)}, s16[136,640]{1,0:T(8,128)(2,1)S(1)}, u32[]{:S(2)}, u32[]{:S(2)}) collective-permute-start(s16[136,640]{1,0:T(8,128)(2,1)S(1)} %get-tuple-element.62), channel_id=1, source_target_pairs={{0,4},{1,5},{2,6},{3,7},{4,0},{5,1},{6,2},{7,3},{8,12},{9,13},{10,... | collective-permute-start | bytes 522248 | tf_op jit(solution)/shard_map/ppermute | solution.py:273
  42.1 9.3 %collective-permute-start.12 = (s16[136,640]{1,0:T(8,128)(2,1)S(1)}, s16[136,640]{1,0:T(8,128)(2,1)S(1)}, u32[]{:S(2)}, u32[]{:S(2)}) collective-permute-start(s16[136,640]{1,0:T(8,128)(2,1)S(1)} %get-tuple-element.59), channel_id=1, source_target_pairs={{0,2},{1,3},{2,0},{3,1},{4,6},{5,7},{6,4},{7,5},{8,10},{9,11},{10,... | collective-permute-start | bytes 522248 | tf_op jit(solution)/shard_map/ppermute | solution.py:273
  43.6 5.1 %collective-permute-start.14 = (s16[136,512]{1,0:T(8,128)(2,1)S(1)}, s16[136,512]{1,0:T(8,128)(2,1)S(1)}, u32[]{:S(2)}, u32[]{:S(2)}) collective-permute-start(s16[136,512]{1,0:T(8,128)(2,1)S(1)} %get-tuple-element.61), channel_id=1, source_target_pairs={{0,16},{8,24},{16,0},{24,8},{1,17},{9,25},{17,1},{25,9},{2,18},{10... | collective-permute-start | bytes 417800 | tf_op jit(solution)/shard_map/ppermute | solution.py:273
  44.8 6.6 %collective-permute-start.11 = (s16[136,512]{1,0:T(8,128)(2,1)S(1)}, s16[136,512]{1,0:T(8,128)(2,1)S(1)}, u32[]{:S(2)}, u32[]{:S(2)}) collective-permute-start(s16[136,512]{1,0:T(8,128)(2,1)S(1)} %get-tuple-element.58), channel_id=1, source_target_pairs={{0,8},{8,0},{16,24},{24,16},{1,9},{9,1},{17,25},{25,17},{2,10},{10... | collective-permute-start | bytes 417800 | tf_op jit(solution)/shard_map/ppermute | solution.py:273
  50.0 10.3 %collective-permute-start.18 = (s16[136,1152]{1,0:T(8,128)(2,1)S(1)}, s16[136,1152]{1,0:T(8,128)(2,1)S(1)}, u32[]{:S(2)}, u32[]{:S(2)}) collective-permute-start(s16[136,1152]{1,0:T(8,128)(2,1)S(1)} %get-tuple-element.68), channel_id=1, source_target_pairs={{0,16},{8,24},{16,0},{24,8},{1,17},{9,25},{17,1},{25,9},{2,18},{10... | collective-permute-start | bytes 940040 | tf_op jit(solution)/shard_map/ppermute | solution.py:273
  51.5 8.9 %collective-permute-start.16 = (s16[136,1152]{1,0:T(8,128)(2,1)S(1)}, s16[136,1152]{1,0:T(8,128)(2,1)S(1)}, u32[]{:S(2)}, u32[]{:S(2)}) collective-permute-start(s16[136,1152]{1,0:T(8,128)(2,1)S(1)} %get-tuple-element.65), channel_id=1, source_target_pairs={{0,8},{8,0},{16,24},{24,16},{1,9},{9,1},{17,25},{25,17},{2,10},{10... | collective-permute-start | bytes 940040 | tf_op jit(solution)/shard_map/ppermute | solution.py:273
  52.2 8.1 %collective-permute-start.19 = (s16[136,512]{1,0:T(8,128)(2,1)S(1)}, s16[136,512]{1,0:T(8,128)(2,1)S(1)}, u32[]{:S(2)}, u32[]{:S(2)}) collective-permute-start(s16[136,512]{1,0:T(8,128)(2,1)S(1)} %get-tuple-element.63.refs_3_), channel_id=1, source_target_pairs={{0,4},{1,5},{2,6},{3,7},{4,0},{5,1},{6,2},{7,3},{8,12},{9,13},{10,... | collective-permute-start | bytes 417800 | tf_op jit(solution)/shard_map/ppermute | solution.py:273
  53.2 7.3 %collective-permute-start.17 = (s16[136,512]{1,0:T(8,128)(2,1)S(1)}, s16[136,512]{1,0:T(8,128)(2,1)S(1)}, u32[]{:S(2)}, u32[]{:S(2)}) collective-permute-start(s16[136,512]{1,0:T(8,128)(2,1)S(1)} %get-tuple-element.66), channel_id=1, source_target_pairs={{0,2},{1,3},{2,0},{3,1},{4,6},{5,7},{6,4},{7,5},{8,10},{9,11},{10,... | collective-permute-start | bytes 417800 | tf_op jit(solution)/shard_map/ppermute | solution.py:273

commit v12 on v10

--- a/solution.py
+++ b/solution.py
@@ -292,8 +292,8 @@
     return (kept[0], received[0][::-1]), after
 
 
-def in_order(arrays):
-    return call(lambda *refs: None, "held", [], [], [], 2**21, 1, (), arrays)
+def in_order(arrays, after=()):
+    return call(lambda *refs: None, "held", [], [], [], 2**21, 1, after, arrays)
 
 
 def bit_steps(axis):
@@ -337,12 +337,12 @@
         row = i * (2 * size + EXTRA_ROWS)
         others[1][m], others[0][m] = ((both, row, 0),), ((both, row + size, 0),)
 
-    def sums(name, kind, rows, columns, cores, jobs, before, emits, after=()):
+    def sums(name, kind, rows, columns, jobs, before, emits, after=()):
         other = 1 - kind
         x_blocks = [blocks[kind][m] for m in rows]
-        y_blocks = [(blocks, others)[c][other][m] for c in cores for m in columns]
+        y_blocks = [(blocks, others)[c][other][m] for c, m in columns]
         x_masks = [masks[kind][m] for m in rows]
-        y_masks = [masks[other][m + c * count] for c in cores for m in columns]
+        y_masks = [masks[other][m + c * count] for c, m in columns]
         return gradient_sums(
             name,
             size,
@@ -358,10 +358,17 @@
             after,
         )
 
+    def both_cores(chosen):
+        return [(c, m) for c in range(2) for m in chosen]
+
+    def every_pair(rows, columns):
+        return [(list(range(len(rows))), list(range(len(columns))))]
+
     before = []
     for k in range(2):
-        jobs = [(early, list(range(2 * len(early))))]
-        results = sums("early_sums", k, early, early, (0, 1), jobs, {}, ["float"] * len(early))
+        columns = both_cores(early)
+        jobs, emits = every_pair(early, columns), ["float"] * len(early)
+        results = sums("early_sums", k, early, columns, jobs, {}, emits)
         before.append({m: s for m, (s,) in zip(early, results)})
     arrays = [[b[m][0][0] for m in late] for b in blocks[::-1]]
     arrays, before = lax.optimization_barrier((arrays, before))
@@ -369,21 +376,32 @@
         for m, a in zip(late, arrays[1 - k]):
             blocks[k][m] = whole(a)
             others[k][m] = whole(swapped(a, core))
-    every, after = list(range(count)), ()
+    after, begun = (), [{}, {}]
     coded, kept = [[None] * half, [None] * half], [None, None]
     for k in (1, 0):
-        jobs, emits = [(list(range(len(late))), list(range(2 * count)))], ["whole"] * len(late)
-        coded[k][1:] = sums("late_rows", k, late, every, (0, 1), jobs, {}, emits, after)
+        columns = [(0, m) for m in range(count)] + [(1, m) for m in early]
+        jobs, emits = every_pair(late, columns), ["float"] * len(late)
+        results = sums("late_rows_begun", k, late, columns, jobs, {}, emits, after)
+        begun[k] = {i: s for i, (s,) in enumerate(results)}
+        after = results[-1]
+    for k in (1, 0):
+        columns = [(1, m) for m in late]
+        jobs, emits = every_pair(late, columns), ["whole"] * len(late)
+        coded[k][1:] = sums("late_rows", k, late, columns, jobs, begun[k], emits, after)
         after = coded[k][1]
     for k in (1, 0):
-        jobs, emits = [(early, list(range(2 * len(late))))], ["float"] * half + ["whole"]
-        *whole_sums, coded[k][0] = sums("late_columns", k, early, late, (0, 1), jobs, before[k], emits, after)
+        columns = both_cores(late)
+        jobs, emits = every_pair(early, columns), ["float"] * half + ["whole"]
+        *whole_sums, coded[k][0] = sums("late_columns", k, early, columns, jobs, before[k], emits, after)
         kept[k], after = [s for (s,) in whole_sums], coded[k][0]
     texts, after = scattered(kept[1], coded[1], steps[1], ())
     images, _ = scattered(kept[0], coded[0], steps[0], after)
-    kept_texts, blocks_in = texts
-    blocks_in = [whole(a) for a in in_order([a for ((a, _, _),) in blocks_in[::-1]])]
-    return tuple(output_sums(scalars[0], [images, (kept_texts, blocks_in)]))
+    (kept_texts, text_blocks), (kept_images, image_blocks) = texts, images
+    text_parts = in_order([b[0][0] for b in text_blocks[:-1]])
+    image_parts = in_order([b[0][0] for b in image_blocks[:-1]], text_parts)
+    text_blocks = [whole(a) for a in text_parts] + text_blocks[-1:]
+    image_blocks = [whole(a) for a in image_parts] + image_blocks[-1:]
+    return tuple(output_sums(scalars[0], [(kept_images, image_blocks), (kept_texts, text_blocks)]))
 
 
 def solution(mesh):

time: 61.4 us -> 60.7 us (0.989)
  waiting for transfers between devices: 25.2 us -> 23.7 us
  Pallas kernels: 11.1 us -> 12.1 us
    ppermute x16, waiting for transfers between devices: 25.2 us -> 23.7 us  [swapped(): lax.ppermute(array, axis, [(i, i ^ bit) for i in range(lax.axis_size(axis...]
    pallas_call x15 -> x18, Pallas kernels: 11.1 us -> 12.1 us  [call(): pl.pallas_call(body, out_shape=[*out_shape, *(jax.ShapeDtypeStruct(a.shap...]
  transfers between devices with their start and end apart: 16 -> 16, of which waited for: 7 -> 6; matrix products, arithmetic and copies ran while one was open for 0% -> 0% of each run, Pallas kernels for 16% -> 18%
where the time goes in v12:
time: 60.7 us; the launch traced here: 60.5 us
  waiting for transfers between devices  23.7 us (39%)
  starting transfers between devices  20.9 us (34%)
  Pallas kernels  12.1 us (20%)
  between operations  2.1 us (3%)
  local copies, waits for them, and re-layouts  1.66 us (3%)
    ppermute x16, waiting for transfers between devices, swapped(): lax.ppermute(array, axis, [(i, i ^ bit) for i in range(lax.axis_size(axis...  23.7 us
    ppermute x16, starting transfers between devices, swapped(): lax.ppermute(array, axis, [(i, i ^ bit) for i in range(lax.axis_size(axis...  20.9 us
    pallas_call x18, Pallas kernels, call(): pl.pallas_call(body, out_shape=[*out_shape, *(jax.ShapeDtypeStruct(a.shap...  12.1 us
    unnamed x6, local copies, waits for them, and re-layouts  1.66 us
  transfers between devices with their start and end apart: 16, of which 6 were waited for; matrix products, arithmetic and copies ran while one was open for 0% of the time, Pallas kernels for 18%

profile of v12, /device:TPU:0, one launch (start us, length us, event | category | flops | bytes accessed | tf_op | source)
XLA Modules:
  0.0 60.5 jit_solution(12753312916446210399)
XLA Ops:
  0.6 4.1 %collective-permute-start = (bf16[128,1152]{1,0:T(8,128)(2,1)}, bf16[128,1152]{1,0:T(8,128)(2,1)S(1)}, u32[]{:S(2)}, u32[]{:S(2)}) collective-permute-start(bf16[128,1152]{1,0:T(8,128)(2,1)} %refs_6_.7), channel_id=1, source_target_pairs={{0,4},{1,5},{2,6},{3,7},{4,0},{5,1},{6,2},{7,3},{8,12},{9,13},{10,... | collective-permute-start | bytes 884744 | tf_op jit(solution)/shard_map/ppermute | solution.py:273
  4.7 1.6 %collective-permute-start.1 = (bf16[128,1152]{1,0:T(8,128)(2,1)}, bf16[128,1152]{1,0:T(8,128)(2,1)S(1)}, u32[]{:S(2)}, u32[]{:S(2)}) collective-permute-start(bf16[128,1152]{1,0:T(8,128)(2,1)} %refs_0_.10), channel_id=1, source_target_pairs={{0,2},{1,3},{2,0},{3,1},{4,6},{5,7},{6,4},{7,5},{8,10},{9,11},{10,... | collective-permute-start | bytes 884744 | tf_op jit(solution)/shard_map/ppermute | solution.py:273
  6.3 0.0 copy-start.1
  6.3 1.0 %copy-done.1 = bf16[128,1152]{1,0:T(8,128)(2,1)S(1)} copy-done((bf16[128,1152]{1,0:T(8,128)(2,1)S(1)}, bf16[128,1152]{1,0:T(8,128)(2,1)}, u32[]{:S(2)}) %copy-start.1) | copy-done | bytes 294936
  7.3 0.0 copy-start.2
  7.3 0.7 %copy-done.2 = s32[128]{0:T(128)S(1)} copy-done((s32[128]{0:T(128)S(1)}, s32[128]{0:T(128)}, u32[]{:S(2)}) %copy-start.2) | copy-done | bytes 536
  8.0 0.0 copy-start
  8.0 1.6 %collective-permute-start.4 = (bf16[136,1152]{1,0:T(8,128)(2,1)S(1)}, bf16[136,1152]{1,0:T(8,128)(2,1)S(1)}, u32[]{:S(2)}, u32[]{:S(2)}) collective-permute-start(bf16[136,1152]{1,0:T(8,128)(2,1)S(1)} %labelled.3.refs_2_.refs_7_.refs_4_), channel_id=1, source_target_pairs={{0,8},{8,0},{16,24},{24,16},{1,9},{9,1},{17,25},{25,17},{2,10},{10... | collective-permute-start | bytes 940040 | tf_op jit(solution)/shard_map/ppermute | solution.py:273
  9.6 1.5 %collective-permute-start.3 = (bf16[128,1152]{1,0:T(8,128)(2,1)}, bf16[128,1152]{1,0:T(8,128)(2,1)S(1)}, u32[]{:S(2)}, u32[]{:S(2)}) collective-permute-start(bf16[128,1152]{1,0:T(8,128)(2,1)} %refs_6_.7), channel_id=1, source_target_pairs={{0,16},{8,24},{16,0},{24,8},{1,17},{9,25},{17,1},{25,9},{2,18},{10... | collective-permute-start | bytes 884744 | tf_op jit(solution)/shard_map/ppermute | solution.py:273
  11.1 0.4 collective-permute-start.2
  11.5 6.8 %collective-permute-done.refs_0_ = bf16[128,1152]{1,0:T(8,128)(2,1)S(1)} collective-permute-done((bf16[128,1152]{1,0:T(8,128)(2,1)}, bf16[128,1152]{1,0:T(8,128)(2,1)S(1)}, u32[]{:S(2)}, u32[]{:S(2)}) %collective-permute-start) | collective-permute-done | bytes 294944 | tf_op jit(solution)/shard_map/ppermute | solution.py:273
  18.4 0.3 collective-permute-done.2.refs_1_
  18.6 0.0 collective-permute-done.1.refs_0_
  18.7 0.0 collective-permute-done.3.refs_3_.refs_4_.refs_6_
  18.7 0.0 collective-permute-done.4.refs_4_.refs_5_.refs_6_
  18.7 0.0 copy-done
  18.8 0.1 bundled.3
  18.9 0.1 collective-permute-start.7
  19.0 1.6 %collective-permute-start.6 = (bf16[136,1152]{1,0:T(8,128)(2,1)S(1)}, bf16[136,1152]{1,0:T(8,128)(2,1)S(1)}, u32[]{:S(2)}, u32[]{:S(2)}) collective-permute-start(bf16[136,1152]{1,0:T(8,128)(2,1)S(1)} %labelled.2.refs_1_.refs_3_.refs_5_), channel_id=1, source_target_pairs={{0,8},{8,0},{16,24},{24,16},{1,9},{9,1},{17,25},{25,17},{2,10},{10... | collective-permute-start | bytes 940040 | tf_op jit(solution)/shard_map/ppermute | solution.py:273
  20.6 1.5 %collective-permute-start.5 = (bf16[128,1152]{1,0:T(8,128)(2,1)S(1)}, bf16[128,1152]{1,0:T(8,128)(2,1)S(1)}, u32[]{:S(2)}, u32[]{:S(2)}) collective-permute-start(bf16[128,1152]{1,0:T(8,128)(2,1)S(1)} %held.3.refs_2_.refs_0_.refs_5_), channel_id=1, source_target_pairs={{0,16},{8,24},{16,0},{24,8},{1,17},{9,25},{17,1},{25,9},{2,18},{10... | collective-permute-start | bytes 884744 | tf_op jit(solution)/shard_map/ppermute | solution.py:273
  23.4 0.0 collective-permute-done.7.refs_8_.refs_7_
  23.4 1.9 %early_sums.3 = (f32[128,1152]{1,0:T(8,128)S(1)}, f32[128,1152]{1,0:T(8,128)S(1)}, f32[128,1152]{1,0:T(8,128)S(1)}) custom-call(f32[1]{0:T(128)S(6)} %copy.17.refs_0_, f32[1]{0:T(128)S(6)} %copy.18.refs_1_, bf16[128,1152]{1,0:T(8,128)(2,1)S(1)} %held.3.refs_2_.refs_0_.refs_5_, bf16[136,1152]{1,0:T(8,128)(2,1)S(1)} %labelled.2.refs_1_.refs_3_.refs_5_, ...), custom_call_target="tpu_custom_call" | custom-call | flops 2304 | bytes 2304 | tf_op jit(solution)/shard_map/early_sums/pallas_call | solution.py:92
  25.3 1.9 %early_sums.2 = (f32[128,1152]{1,0:T(8,128)S(1)}, f32[128,1152]{1,0:T(8,128)S(1)}, f32[128,1152]{1,0:T(8,128)S(1)}) custom-call(f32[1]{0:T(128)S(6)} %copy.17.refs_0_, f32[1]{0:T(128)S(6)} %copy.18.refs_1_, bf16[128,1152]{1,0:T(8,128)(2,1)S(1)} %held.3.refs_2_.refs_0_.refs_5_, bf16[136,1152]{1,0:T(8,128)(2,1)S(1)} %labelled.2.refs_1_.refs_3_.refs_5_, ...), custom_call_target="tpu_custom_call" | custom-call | flops 2304 | bytes 2304 | tf_op jit(solution)/shard_map/early_sums/pallas_call | solution.py:92
  27.3 2.4 %collective-permute-done.5.refs_2_.refs_8_ = bf16[128,1152]{1,0:T(8,128)(2,1)S(1)} collective-permute-done((bf16[128,1152]{1,0:T(8,128)(2,1)S(1)}, bf16[128,1152]{1,0:T(8,128)(2,1)S(1)}, u32[]{:S(2)}, u32[]{:S(2)}) %collective-permute-start.5) | collective-permute-done | bytes 294944 | tf_op jit(solution)/shard_map/ppermute | solution.py:273
  29.7 0.0 collective-permute-done.6.refs_3_.refs_8_
  29.7 0.0 collective-permute-start.9
  29.7 0.5 collective-permute-start.8
  30.2 1.3 %late_rows_begun.2.refs_8_.refs_5_ = f32[128,1152]{1,0:T(8,128)S(1)} custom-call(f32[1]{0:T(128)S(6)} %copy.17.refs_0_, f32[1]{0:T(128)S(6)} %copy.18.refs_1_, bf16[128,1152]{1,0:T(8,128)(2,1)S(1)} %collective-permute-done.5.refs_2_.refs_8_, bf16[136,1152]{1,0:T(8,128)(2,1)S(1)} %collective-permute-done.6.refs_3_.refs_8_, ...), custom_call_target="tpu_custom_call" | custom-call | flops 896 | bytes 896 | tf_op jit(solution)/shard_map/late_rows_begun/pallas_call | solution.py:92
  31.5 1.3 %late_rows_begun.3.refs_6_.refs_5_ = f32[128,1152]{1,0:T(8,128)S(1)} custom-call(f32[1]{0:T(128)S(6)} %copy.17.refs_0_, f32[1]{0:T(128)S(6)} %copy.18.refs_1_, bf16[128,1152]{1,0:T(8,128)(2,1)S(1)} %collective-permute-done.5.refs_2_.refs_8_, bf16[136,1152]{1,0:T(8,128)(2,1)S(1)} %collective-permute-done.6.refs_3_.refs_8_, bf16[128,1152]{1,0:T(8,128)(2,1)S(1)} %copy-done, ...), custom_call_target="tpu_custom_call" | custom-call | flops 896 | bytes 896 | tf_op jit(solution)/shard_map/late_rows_begun/pallas_call | solution.py:92
  32.9 0.0 collective-permute-done.9.refs_4_.refs_9_
  32.9 0.6 %late_rows.2.refs_6_ = s16[136,1152]{1,0:T(8,128)(2,1)S(1)} custom-call(f32[1]{0:T(128)S(6)} %copy.17.refs_0_, f32[1]{0:T(128)S(6)} %copy.18.refs_1_, bf16[128,1152]{1,0:T(8,128)(2,1)S(1)} %collective-permute-done.5.refs_2_.refs_8_, bf16[136,1152]{1,0:T(8,128)(2,1)S(1)} %collective-permute-done.6.refs_3_.refs_8_, ...), custom_call_target="tpu_custom_call" | custom-call | flops 128 | bytes 128 | tf_op jit(solution)/shard_map/late_rows/pallas_call | solution.py:92
  33.5 1.6 %collective-permute-start.10 = (s16[136,1152]{1,0:T(8,128)(2,1)S(1)}, s16[136,1152]{1,0:T(8,128)(2,1)S(1)}, u32[]{:S(2)}, u32[]{:S(2)}) collective-permute-start(s16[136,1152]{1,0:T(8,128)(2,1)S(1)} %late_rows.2.refs_6_), channel_id=1, source_target_pairs={{0,16},{8,24},{16,0},{24,8},{1,17},{9,25},{17,1},{25,9},{2,18},{10... | collective-permute-start | bytes 940040 | tf_op jit(solution)/shard_map/ppermute | solution.py:273
  35.1 0.0 collective-permute-done.8.refs_4_.refs_9_
  35.1 0.6 %late_rows.3.refs_13_ = s16[136,1152]{1,0:T(8,128)(2,1)S(1)} custom-call(f32[1]{0:T(128)S(6)} %copy.17.refs_0_, f32[1]{0:T(128)S(6)} %copy.18.refs_1_, bf16[128,1152]{1,0:T(8,128)(2,1)S(1)} %collective-permute-done.5.refs_2_.refs_8_, bf16[136,1152]{1,0:T(8,128)(2,1)S(1)} %collective-permute-done.6.refs_3_.refs_8_, ...), custom_call_target="tpu_custom_call" | custom-call | flops 128 | bytes 128 | tf_op jit(solution)/shard_map/late_rows/pallas_call | solution.py:92
  35.7 0.7 %collective-permute-start.12 = (s16[136,1152]{1,0:T(8,128)(2,1)S(1)}, s16[136,1152]{1,0:T(8,128)(2,1)S(1)}, u32[]{:S(2)}, u32[]{:S(2)}) collective-permute-start(s16[136,1152]{1,0:T(8,128)(2,1)S(1)} %late_rows.3.refs_13_), channel_id=1, source_target_pairs={{0,8},{8,0},{16,24},{24,16},{1,9},{9,1},{17,25},{25,17},{2,10},{10... | collective-permute-start | bytes 940040 | tf_op jit(solution)/shard_map/ppermute | solution.py:273
  36.4 1.3 %late_columns.2 = (f32[128,1152]{1,0:T(8,128)S(1)}, f32[128,1152]{1,0:T(8,128)S(1)}, s16[136,1152]{1,0:T(8,128)(2,1)S(1)}) custom-call(f32[1]{0:T(128)S(6)} %copy.17.refs_0_, f32[1]{0:T(128)S(6)} %copy.18.refs_1_, bf16[128,1152]{1,0:T(8,128)(2,1)S(1)} %held.3.refs_2_.refs_0_.refs_5_, bf16[136,1152]{1,0:T(8,128)(2,1)S(1)} %labelled.2.refs_1_.refs_3_.refs_5_, ...), custom_call_target="tpu_custom_call" | custom-call | flops 768 | bytes 768 | tf_op jit(solution)/shard_map/late_columns/pallas_call | solution.py:92
  37.7 1.3 %late_columns.3 = (f32[128,1152]{1,0:T(8,128)S(1)}, f32[128,1152]{1,0:T(8,128)S(1)}, s16[136,1152]{1,0:T(8,128)(2,1)S(1)}) custom-call(f32[1]{0:T(128)S(6)} %copy.17.refs_0_, f32[1]{0:T(128)S(6)} %copy.18.refs_1_, bf16[128,1152]{1,0:T(8,128)(2,1)S(1)} %held.3.refs_2_.refs_0_.refs_5_, bf16[136,1152]{1,0:T(8,128)(2,1)S(1)} %labelled.2.refs_1_.refs_3_.refs_5_, ...), custom_call_target="tpu_custom_call" | custom-call | flops 768 | bytes 768 | tf_op jit(solution)/shard_map/late_columns/pallas_call | solution.py:92
  39.0 3.8 %collective-permute-done.10.refs_1_ = s16[136,1152]{1,0:T(8,128)(2,1)S(1)} collective-permute-done((s16[136,1152]{1,0:T(8,128)(2,1)S(1)}, s16[136,1152]{1,0:T(8,128)(2,1)S(1)}, u32[]{:S(2)}, u32[]{:S(2)}) %collective-permute-start.10) | collective-permute-done | bytes 313376 | tf_op jit(solution)/shard_map/ppermute | solution.py:273
  42.9 0.2 passed_sum.2
  43.0 1.4 %collective-permute-start.11 = (s16[136,1152]{1,0:T(8,128)(2,1)S(1)}, s16[136,1152]{1,0:T(8,128)(2,1)S(1)}, u32[]{:S(2)}, u32[]{:S(2)}) collective-permute-start(s16[136,1152]{1,0:T(8,128)(2,1)S(1)} %get-tuple-element.43.refs_2_), channel_id=1, source_target_pairs={{0,4},{1,5},{2,6},{3,7},{4,0},{5,1},{6,2},{7,3},{8,12},{9,13},{10,... | collective-permute-start | bytes 940040 | tf_op jit(solution)/shard_map/ppermute | solution.py:273
  44.4 0.4 collective-permute-done.12.refs_1_
  44.8 0.2 passed_sum.3
  45.0 2.1 %collective-permute-start.13 = (s16[136,1152]{1,0:T(8,128)(2,1)S(1)}, s16[136,1152]{1,0:T(8,128)(2,1)S(1)}, u32[]{:S(2)}, u32[]{:S(2)}) collective-permute-start(s16[136,1152]{1,0:T(8,128)(2,1)S(1)} %get-tuple-element.46), channel_id=1, source_target_pairs={{0,2},{1,3},{2,0},{3,1},{4,6},{5,7},{6,4},{7,5},{8,10},{9,11},{10,... | collective-permute-start | bytes 940040 | tf_op jit(solution)/shard_map/ppermute | solution.py:273
  47.1 0.7 %collective-permute-start.14 = (s16[136,1152]{1,0:T(8,128)(2,1)S(1)}, s16[136,1152]{1,0:T(8,128)(2,1)S(1)}, u32[]{:S(2)}, u32[]{:S(2)}) collective-permute-start(s16[136,1152]{1,0:T(8,128)(2,1)S(1)} %get-tuple-element.47), channel_id=1, source_target_pairs={{0,8},{8,0},{16,24},{24,16},{1,9},{9,1},{17,25},{25,17},{2,10},{10... | collective-permute-start | bytes 940040 | tf_op jit(solution)/shard_map/ppermute | solution.py:273
  47.7 1.5 %collective-permute-start.15 = (s16[136,1152]{1,0:T(8,128)(2,1)S(1)}, s16[136,1152]{1,0:T(8,128)(2,1)S(1)}, u32[]{:S(2)}, u32[]{:S(2)}) collective-permute-start(s16[136,1152]{1,0:T(8,128)(2,1)S(1)} %get-tuple-element.49), channel_id=1, source_target_pairs={{0,16},{8,24},{16,0},{24,8},{1,17},{9,25},{17,1},{25,9},{2,18},{10... | collective-permute-start | bytes 940040 | tf_op jit(solution)/shard_map/ppermute | solution.py:273
  49.3 10.0 %collective-permute-done.11.refs_0_ = s16[136,1152]{1,0:T(8,128)(2,1)S(1)} collective-permute-done((s16[136,1152]{1,0:T(8,128)(2,1)S(1)}, s16[136,1152]{1,0:T(8,128)(2,1)S(1)}, u32[]{:S(2)}, u32[]{:S(2)}) %collective-permute-start.11) | collective-permute-done | bytes 313376 | tf_op jit(solution)/shard_map/ppermute | solution.py:273
  59.3 0.0 collective-permute-done.13.refs_1_
  59.3 0.0 collective-permute-done.14.refs_3_
  59.3 0.0 collective-permute-done.15.refs_6_
  59.3 1.2 %output_sums.1 = (f32[128,1152]{1,0:T(8,128)}, f32[128,1152]{1,0:T(8,128)}) custom-call(f32[1]{0:T(128)S(6)} %copy.17.refs_0_, f32[128,1152]{1,0:T(8,128)S(1)} %get-tuple-element.41.refs_1_, s16[136,1152]{1,0:T(8,128)(2,1)S(1)} %held.5.refs_2_, s16[136,1152]{1,0:T(8,128)(2,1)S(1)} %collective-permute-done.14.refs_3_, ...), custom_call_target="tpu_custom_call" | custom-call | flops 128 | bytes 128 | tf_op jit(solution)/shard_map/output_sums/pallas_call | solution.py:92
  (6 shorter events, 0.1 us)
Async XLA Ops:
  0.6 17.8 %collective-permute-start = (bf16[128,1152]{1,0:T(8,128)(2,1)}, bf16[128,1152]{1,0:T(8,128)(2,1)S(1)}, u32[]{:S(2)}, u32[]{:S(2)}) collective-permute-start(bf16[128,1152]{1,0:T(8,128)(2,1)} %refs_6_.7), channel_id=1, source_target_pairs={{0,4},{1,5},{2,6},{3,7},{4,0},{5,1},{6,2},{7,3},{8,12},{9,13},{10,... | collective-permute-start | bytes 884744 | tf_op jit(solution)/shard_map/ppermute | solution.py:273
  4.7 13.9 %collective-permute-start.1 = (bf16[128,1152]{1,0:T(8,128)(2,1)}, bf16[128,1152]{1,0:T(8,128)(2,1)S(1)}, u32[]{:S(2)}, u32[]{:S(2)}) collective-permute-start(bf16[128,1152]{1,0:T(8,128)(2,1)} %refs_0_.10), channel_id=1, source_target_pairs={{0,2},{1,3},{2,0},{3,1},{4,6},{5,7},{6,4},{7,5},{8,10},{9,11},{10,... | collective-permute-start | bytes 884744 | tf_op jit(solution)/shard_map/ppermute | solution.py:273
  6.3 1.0 %copy-start.1 = (bf16[128,1152]{1,0:T(8,128)(2,1)S(1)}, bf16[128,1152]{1,0:T(8,128)(2,1)}, u32[]{:S(2)}) copy-start(bf16[128,1152]{1,0:T(8,128)(2,1)} %refs_0_.10) | copy-start | bytes 884740
  7.3 0.7 %copy-start.2 = (s32[128]{0:T(128)S(1)}, s32[128]{0:T(128)}, u32[]{:S(2)}) copy-start(s32[128]{0:T(128)} %param.7) | copy-start | bytes 1540
  8.0 10.8 %copy-start = (bf16[128,1152]{1,0:T(8,128)(2,1)S(1)}, bf16[128,1152]{1,0:T(8,128)(2,1)}, u32[]{:S(2)}) copy-start(bf16[128,1152]{1,0:T(8,128)(2,1)} %refs_6_.7) | copy-start | bytes 884740
  8.0 10.7 %collective-permute-start.4 = (bf16[136,1152]{1,0:T(8,128)(2,1)S(1)}, bf16[136,1152]{1,0:T(8,128)(2,1)S(1)}, u32[]{:S(2)}, u32[]{:S(2)}) collective-permute-start(bf16[136,1152]{1,0:T(8,128)(2,1)S(1)} %labelled.3.refs_2_.refs_7_.refs_4_), channel_id=1, source_target_pairs={{0,8},{8,0},{16,24},{24,16},{1,9},{9,1},{17,25},{25,17},{2,10},{10... | collective-permute-start | bytes 940040 | tf_op jit(solution)/shard_map/ppermute | solution.py:273
  9.6 9.2 %collective-permute-start.3 = (bf16[128,1152]{1,0:T(8,128)(2,1)}, bf16[128,1152]{1,0:T(8,128)(2,1)S(1)}, u32[]{:S(2)}, u32[]{:S(2)}) collective-permute-start(bf16[128,1152]{1,0:T(8,128)(2,1)} %refs_6_.7), channel_id=1, source_target_pairs={{0,16},{8,24},{16,0},{24,8},{1,17},{9,25},{17,1},{25,9},{2,18},{10... | collective-permute-start | bytes 884744 | tf_op jit(solution)/shard_map/ppermute | solution.py:273
  11.1 7.6 %collective-permute-start.2 = (s32[1,128]{1,0:T(1,128)S(1)}, s32[1,128]{1,0:T(1,128)S(1)}, u32[]{:S(2)}, u32[]{:S(2)}) collective-permute-start(s32[1,128]{1,0:T(1,128)S(1)} %bitcast.2), channel_id=1, source_target_pairs={{0,2},{1,3},{2,0},{3,1},{4,6},{5,7},{6,4},{7,5},{8,10},{9,11},{10,... | collective-permute-start | bytes 1544 | tf_op jit(solution)/shard_map/ppermute | solution.py:273
  18.9 4.5 %collective-permute-start.7 = (bf16[792,1152]{1,0:T(8,128)(2,1)S(1)}, bf16[792,1152]{1,0:T(8,128)(2,1)S(1)}, u32[]{:S(2)}, u32[]{:S(2)}) collective-permute-start(bf16[792,1152]{1,0:T(8,128)(2,1)S(1)} %bundled.3), channel_id=1, source_target_pairs={{0,1},{1,0},{2,3},{3,2},{4,5},{5,4},{6,7},{7,6},{8,9},{9,8},{10,11... | collective-permute-start | bytes 5474312 | tf_op jit(solution)/shard_map/ppermute | solution.py:273
  19.0 10.7 %collective-permute-start.6 = (bf16[136,1152]{1,0:T(8,128)(2,1)S(1)}, bf16[136,1152]{1,0:T(8,128)(2,1)S(1)}, u32[]{:S(2)}, u32[]{:S(2)}) collective-permute-start(bf16[136,1152]{1,0:T(8,128)(2,1)S(1)} %labelled.2.refs_1_.refs_3_.refs_5_), channel_id=1, source_target_pairs={{0,8},{8,0},{16,24},{24,16},{1,9},{9,1},{17,25},{25,17},{2,10},{10... | collective-permute-start | bytes 940040 | tf_op jit(solution)/shard_map/ppermute | solution.py:273
  20.6 9.1 %collective-permute-start.5 = (bf16[128,1152]{1,0:T(8,128)(2,1)S(1)}, bf16[128,1152]{1,0:T(8,128)(2,1)S(1)}, u32[]{:S(2)}, u32[]{:S(2)}) collective-permute-start(bf16[128,1152]{1,0:T(8,128)(2,1)S(1)} %held.3.refs_2_.refs_0_.refs_5_), channel_id=1, source_target_pairs={{0,16},{8,24},{16,0},{24,8},{1,17},{9,25},{17,1},{25,9},{2,18},{10... | collective-permute-start | bytes 884744 | tf_op jit(solution)/shard_map/ppermute | solution.py:273
  29.7 3.2 %collective-permute-start.9 = (bf16[136,1152]{1,0:T(8,128)(2,1)S(1)}, bf16[136,1152]{1,0:T(8,128)(2,1)S(1)}, u32[]{:S(2)}, u32[]{:S(2)}) collective-permute-start(bf16[136,1152]{1,0:T(8,128)(2,1)S(1)} %collective-permute-done.6.refs_3_.refs_8_), channel_id=1, source_target_pairs={{0,1},{1,0},{2,3},{3,2},{4,5},{5,4},{6,7},{7,6},{8,9},{9,8},{10,11... | collective-permute-start | bytes 940040 | tf_op jit(solution)/shard_map/ppermute | solution.py:273
  29.7 5.4 %collective-permute-start.8 = (bf16[128,1152]{1,0:T(8,128)(2,1)S(1)}, bf16[128,1152]{1,0:T(8,128)(2,1)S(1)}, u32[]{:S(2)}, u32[]{:S(2)}) collective-permute-start(bf16[128,1152]{1,0:T(8,128)(2,1)S(1)} %collective-permute-done.5.refs_2_.refs_8_), channel_id=1, source_target_pairs={{0,1},{1,0},{2,3},{3,2},{4,5},{5,4},{6,7},{7,6},{8,9},{9,8},{10,11... | collective-permute-start | bytes 884744 | tf_op jit(solution)/shard_map/ppermute | solution.py:273
  33.5 9.4 %collective-permute-start.10 = (s16[136,1152]{1,0:T(8,128)(2,1)S(1)}, s16[136,1152]{1,0:T(8,128)(2,1)S(1)}, u32[]{:S(2)}, u32[]{:S(2)}) collective-permute-start(s16[136,1152]{1,0:T(8,128)(2,1)S(1)} %late_rows.2.refs_6_), channel_id=1, source_target_pairs={{0,16},{8,24},{16,0},{24,8},{1,17},{9,25},{17,1},{25,9},{2,18},{10... | collective-permute-start | bytes 940040 | tf_op jit(solution)/shard_map/ppermute | solution.py:273
  35.7 9.1 %collective-permute-start.12 = (s16[136,1152]{1,0:T(8,128)(2,1)S(1)}, s16[136,1152]{1,0:T(8,128)(2,1)S(1)}, u32[]{:S(2)}, u32[]{:S(2)}) collective-permute-start(s16[136,1152]{1,0:T(8,128)(2,1)S(1)} %late_rows.3.refs_13_), channel_id=1, source_target_pairs={{0,8},{8,0},{16,24},{24,16},{1,9},{9,1},{17,25},{25,17},{2,10},{10... | collective-permute-start | bytes 940040 | tf_op jit(solution)/shard_map/ppermute | solution.py:273
  43.0 16.2 %collective-permute-start.11 = (s16[136,1152]{1,0:T(8,128)(2,1)S(1)}, s16[136,1152]{1,0:T(8,128)(2,1)S(1)}, u32[]{:S(2)}, u32[]{:S(2)}) collective-permute-start(s16[136,1152]{1,0:T(8,128)(2,1)S(1)} %get-tuple-element.43.refs_2_), channel_id=1, source_target_pairs={{0,4},{1,5},{2,6},{3,7},{4,0},{5,1},{6,2},{7,3},{8,12},{9,13},{10,... | collective-permute-start | bytes 940040 | tf_op jit(solution)/shard_map/ppermute | solution.py:273
  45.0 14.3 %collective-permute-start.13 = (s16[136,1152]{1,0:T(8,128)(2,1)S(1)}, s16[136,1152]{1,0:T(8,128)(2,1)S(1)}, u32[]{:S(2)}, u32[]{:S(2)}) collective-permute-start(s16[136,1152]{1,0:T(8,128)(2,1)S(1)} %get-tuple-element.46), channel_id=1, source_target_pairs={{0,2},{1,3},{2,0},{3,1},{4,6},{5,7},{6,4},{7,5},{8,10},{9,11},{10,... | collective-permute-start | bytes 940040 | tf_op jit(solution)/shard_map/ppermute | solution.py:273
  47.1 12.2 %collective-permute-start.14 = (s16[136,1152]{1,0:T(8,128)(2,1)S(1)}, s16[136,1152]{1,0:T(8,128)(2,1)S(1)}, u32[]{:S(2)}, u32[]{:S(2)}) collective-permute-start(s16[136,1152]{1,0:T(8,128)(2,1)S(1)} %get-tuple-element.47), channel_id=1, source_target_pairs={{0,8},{8,0},{16,24},{24,16},{1,9},{9,1},{17,25},{25,17},{2,10},{10... | collective-permute-start | bytes 940040 | tf_op jit(solution)/shard_map/ppermute | solution.py:273
  47.7 11.5 %collective-permute-start.15 = (s16[136,1152]{1,0:T(8,128)(2,1)S(1)}, s16[136,1152]{1,0:T(8,128)(2,1)S(1)}, u32[]{:S(2)}, u32[]{:S(2)}) collective-permute-start(s16[136,1152]{1,0:T(8,128)(2,1)S(1)} %get-tuple-element.49), channel_id=1, source_target_pairs={{0,16},{8,24},{16,0},{24,8},{1,17},{9,25},{17,1},{25,9},{2,18},{10... | collective-permute-start | bytes 940040 | tf_op jit(solution)/shard_map/ppermute | solution.py:273

commit v13 on v12

--- a/solution.py
+++ b/solution.py
@@ -376,18 +376,16 @@
         for m, a in zip(late, arrays[1 - k]):
             blocks[k][m] = whole(a)
             others[k][m] = whole(swapped(a, core))
-    after, begun = (), [{}, {}]
+    after = ()
     coded, kept = [[None] * half, [None] * half], [None, None]
     for k in (1, 0):
         columns = [(0, m) for m in range(count)] + [(1, m) for m in early]
         jobs, emits = every_pair(late, columns), ["float"] * len(late)
         results = sums("late_rows_begun", k, late, columns, jobs, {}, emits, after)
-        begun[k] = {i: s for i, (s,) in enumerate(results)}
-        after = results[-1]
-    for k in (1, 0):
+        begun = {i: s for i, (s,) in enumerate(results)}
         columns = [(1, m) for m in late]
         jobs, emits = every_pair(late, columns), ["whole"] * len(late)
-        coded[k][1:] = sums("late_rows", k, late, columns, jobs, begun[k], emits, after)
+        coded[k][1:] = sums("late_rows", k, late, columns, jobs, begun, emits)
         after = coded[k][1]
     for k in (1, 0):
         columns = both_cores(late)

time: 60.7 us -> 60.3 us (level)
  starting transfers between devices: 20.9 us -> 19.6 us
  waiting for transfers between devices: 23.7 us -> 24.7 us
    ppermute x16, starting transfers between devices: 20.9 us -> 19.6 us  [swapped(): lax.ppermute(array, axis, [(i, i ^ bit) for i in range(lax.axis_size(axis...]
    ppermute x16, waiting for transfers between devices: 23.7 us -> 24.7 us  [swapped(): lax.ppermute(array, axis, [(i, i ^ bit) for i in range(lax.axis_size(axis...]
  transfers between devices with their start and end apart: 16 -> 16, of which waited for: 6 -> 7; matrix products, arithmetic and copies ran while one was open for 0% -> 0% of each run, Pallas kernels for 18% -> 18%
where the time goes in v13:
time: 60.3 us; the launch traced here: 60.2 us
  waiting for transfers between devices  24.7 us (41%)
  starting transfers between devices  19.6 us (33%)
  Pallas kernels  12.1 us (20%)
  between operations  2.1 us (3%)
  local copies, waits for them, and re-layouts  1.66 us (3%)
    ppermute x16, waiting for transfers between devices, swapped(): lax.ppermute(array, axis, [(i, i ^ bit) for i in range(lax.axis_size(axis...  24.7 us
    ppermute x16, starting transfers between devices, swapped(): lax.ppermute(array, axis, [(i, i ^ bit) for i in range(lax.axis_size(axis...  19.6 us
    pallas_call x18, Pallas kernels, call(): pl.pallas_call(body, out_shape=[*out_shape, *(jax.ShapeDtypeStruct(a.shap...  12.1 us
    unnamed x6, local copies, waits for them, and re-layouts  1.66 us
  transfers between devices with their start and end apart: 16, of which 7 were waited for; matrix products, arithmetic and copies ran while one was open for 0% of the time, Pallas kernels for 18%

profile of v13, /device:TPU:0, one launch (start us, length us, event | category | flops | bytes accessed | tf_op | source)
XLA Modules:
  0.0 60.2 jit_solution(4645483482085434246)
XLA Ops:
  0.6 4.1 %collective-permute-start = (bf16[128,1152]{1,0:T(8,128)(2,1)}, bf16[128,1152]{1,0:T(8,128)(2,1)S(1)}, u32[]{:S(2)}, u32[]{:S(2)}) collective-permute-start(bf16[128,1152]{1,0:T(8,128)(2,1)} %refs_6_.7), channel_id=1, source_target_pairs={{0,4},{1,5},{2,6},{3,7},{4,0},{5,1},{6,2},{7,3},{8,12},{9,13},{10,... | collective-permute-start | bytes 884744 | tf_op jit(solution)/shard_map/ppermute | solution.py:273
  4.7 1.6 %collective-permute-start.1 = (bf16[128,1152]{1,0:T(8,128)(2,1)}, bf16[128,1152]{1,0:T(8,128)(2,1)S(1)}, u32[]{:S(2)}, u32[]{:S(2)}) collective-permute-start(bf16[128,1152]{1,0:T(8,128)(2,1)} %refs_0_.10), channel_id=1, source_target_pairs={{0,2},{1,3},{2,0},{3,1},{4,6},{5,7},{6,4},{7,5},{8,10},{9,11},{10,... | collective-permute-start | bytes 884744 | tf_op jit(solution)/shard_map/ppermute | solution.py:273
  6.3 0.0 copy-start.1
  6.3 1.0 %copy-done.1 = bf16[128,1152]{1,0:T(8,128)(2,1)S(1)} copy-done((bf16[128,1152]{1,0:T(8,128)(2,1)S(1)}, bf16[128,1152]{1,0:T(8,128)(2,1)}, u32[]{:S(2)}) %copy-start.1) | copy-done | bytes 294936
  7.3 0.0 copy-start.2
  7.3 0.7 %copy-done.2 = s32[128]{0:T(128)S(1)} copy-done((s32[128]{0:T(128)S(1)}, s32[128]{0:T(128)}, u32[]{:S(2)}) %copy-start.2) | copy-done | bytes 536
  8.0 0.0 copy-start
  8.0 1.6 %collective-permute-start.4 = (bf16[136,1152]{1,0:T(8,128)(2,1)S(1)}, bf16[136,1152]{1,0:T(8,128)(2,1)S(1)}, u32[]{:S(2)}, u32[]{:S(2)}) collective-permute-start(bf16[136,1152]{1,0:T(8,128)(2,1)S(1)} %labelled.3.refs_2_.refs_7_.refs_4_), channel_id=1, source_target_pairs={{0,8},{8,0},{16,24},{24,16},{1,9},{9,1},{17,25},{25,17},{2,10},{10... | collective-permute-start | bytes 940040 | tf_op jit(solution)/shard_map/ppermute | solution.py:273
  9.6 1.5 %collective-permute-start.3 = (bf16[128,1152]{1,0:T(8,128)(2,1)}, bf16[128,1152]{1,0:T(8,128)(2,1)S(1)}, u32[]{:S(2)}, u32[]{:S(2)}) collective-permute-start(bf16[128,1152]{1,0:T(8,128)(2,1)} %refs_6_.7), channel_id=1, source_target_pairs={{0,16},{8,24},{16,0},{24,8},{1,17},{9,25},{17,1},{25,9},{2,18},{10... | collective-permute-start | bytes 884744 | tf_op jit(solution)/shard_map/ppermute | solution.py:273
  11.1 0.4 collective-permute-start.2
  11.5 6.8 %collective-permute-done.refs_0_ = bf16[128,1152]{1,0:T(8,128)(2,1)S(1)} collective-permute-done((bf16[128,1152]{1,0:T(8,128)(2,1)}, bf16[128,1152]{1,0:T(8,128)(2,1)S(1)}, u32[]{:S(2)}, u32[]{:S(2)}) %collective-permute-start) | collective-permute-done | bytes 294944 | tf_op jit(solution)/shard_map/ppermute | solution.py:273
  18.4 0.3 collective-permute-done.2.refs_1_
  18.6 0.0 collective-permute-done.1.refs_0_
  18.7 0.0 collective-permute-done.3.refs_3_.refs_4_.refs_6_
  18.7 0.0 collective-permute-done.4.refs_4_.refs_5_.refs_6_
  18.7 0.0 copy-done
  18.8 0.1 bundled.3
  18.9 0.1 collective-permute-start.7
  19.0 1.6 %collective-permute-start.6 = (bf16[136,1152]{1,0:T(8,128)(2,1)S(1)}, bf16[136,1152]{1,0:T(8,128)(2,1)S(1)}, u32[]{:S(2)}, u32[]{:S(2)}) collective-permute-start(bf16[136,1152]{1,0:T(8,128)(2,1)S(1)} %labelled.2.refs_1_.refs_3_.refs_5_), channel_id=1, source_target_pairs={{0,8},{8,0},{16,24},{24,16},{1,9},{9,1},{17,25},{25,17},{2,10},{10... | collective-permute-start | bytes 940040 | tf_op jit(solution)/shard_map/ppermute | solution.py:273
  20.6 1.5 %collective-permute-start.5 = (bf16[128,1152]{1,0:T(8,128)(2,1)S(1)}, bf16[128,1152]{1,0:T(8,128)(2,1)S(1)}, u32[]{:S(2)}, u32[]{:S(2)}) collective-permute-start(bf16[128,1152]{1,0:T(8,128)(2,1)S(1)} %held.3.refs_2_.refs_0_.refs_5_), channel_id=1, source_target_pairs={{0,16},{8,24},{16,0},{24,8},{1,17},{9,25},{17,1},{25,9},{2,18},{10... | collective-permute-start | bytes 884744 | tf_op jit(solution)/shard_map/ppermute | solution.py:273
  23.4 0.0 collective-permute-done.7.refs_8_.refs_7_
  23.4 1.9 %early_sums.3 = (f32[128,1152]{1,0:T(8,128)S(1)}, f32[128,1152]{1,0:T(8,128)S(1)}, f32[128,1152]{1,0:T(8,128)S(1)}) custom-call(f32[1]{0:T(128)S(6)} %copy.17.refs_0_, f32[1]{0:T(128)S(6)} %copy.18.refs_1_, bf16[128,1152]{1,0:T(8,128)(2,1)S(1)} %held.3.refs_2_.refs_0_.refs_5_, bf16[136,1152]{1,0:T(8,128)(2,1)S(1)} %labelled.2.refs_1_.refs_3_.refs_5_, ...), custom_call_target="tpu_custom_call" | custom-call | flops 2304 | bytes 2304 | tf_op jit(solution)/shard_map/early_sums/pallas_call | solution.py:92
  25.3 1.9 %early_sums.2 = (f32[128,1152]{1,0:T(8,128)S(1)}, f32[128,1152]{1,0:T(8,128)S(1)}, f32[128,1152]{1,0:T(8,128)S(1)}) custom-call(f32[1]{0:T(128)S(6)} %copy.17.refs_0_, f32[1]{0:T(128)S(6)} %copy.18.refs_1_, bf16[128,1152]{1,0:T(8,128)(2,1)S(1)} %held.3.refs_2_.refs_0_.refs_5_, bf16[136,1152]{1,0:T(8,128)(2,1)S(1)} %labelled.2.refs_1_.refs_3_.refs_5_, ...), custom_call_target="tpu_custom_call" | custom-call | flops 2304 | bytes 2304 | tf_op jit(solution)/shard_map/early_sums/pallas_call | solution.py:92
  27.3 2.4 %collective-permute-done.5.refs_2_.refs_8_ = bf16[128,1152]{1,0:T(8,128)(2,1)S(1)} collective-permute-done((bf16[128,1152]{1,0:T(8,128)(2,1)S(1)}, bf16[128,1152]{1,0:T(8,128)(2,1)S(1)}, u32[]{:S(2)}, u32[]{:S(2)}) %collective-permute-start.5) | collective-permute-done | bytes 294944 | tf_op jit(solution)/shard_map/ppermute | solution.py:273
  29.7 0.0 collective-permute-done.6.refs_3_.refs_8_
  29.7 0.0 collective-permute-start.9
  29.7 0.5 collective-permute-start.8
  30.2 1.3 %late_rows_begun.2.refs_5_ = f32[128,1152]{1,0:T(8,128)S(1)} custom-call(f32[1]{0:T(128)S(6)} %copy.17.refs_0_, f32[1]{0:T(128)S(6)} %copy.18.refs_1_, bf16[128,1152]{1,0:T(8,128)(2,1)S(1)} %collective-permute-done.5.refs_2_.refs_8_, bf16[136,1152]{1,0:T(8,128)(2,1)S(1)} %collective-permute-done.6.refs_3_.refs_8_, ...), custom_call_target="tpu_custom_call" | custom-call | flops 896 | bytes 896 | tf_op jit(solution)/shard_map/late_rows_begun/pallas_call | solution.py:92
  31.5 0.0 collective-permute-done.9.refs_4_.refs_9_
  31.5 0.6 %late_rows.2.refs_8_ = s16[136,1152]{1,0:T(8,128)(2,1)S(1)} custom-call(f32[1]{0:T(128)S(6)} %copy.17.refs_0_, f32[1]{0:T(128)S(6)} %copy.18.refs_1_, bf16[128,1152]{1,0:T(8,128)(2,1)S(1)} %collective-permute-done.5.refs_2_.refs_8_, bf16[136,1152]{1,0:T(8,128)(2,1)S(1)} %collective-permute-done.6.refs_3_.refs_8_, ...), custom_call_target="tpu_custom_call" | custom-call | flops 128 | bytes 128 | tf_op jit(solution)/shard_map/late_rows/pallas_call | solution.py:92
  32.1 1.6 %collective-permute-start.10 = (s16[136,1152]{1,0:T(8,128)(2,1)S(1)}, s16[136,1152]{1,0:T(8,128)(2,1)S(1)}, u32[]{:S(2)}, u32[]{:S(2)}) collective-permute-start(s16[136,1152]{1,0:T(8,128)(2,1)S(1)} %late_rows.2.refs_8_), channel_id=1, source_target_pairs={{0,16},{8,24},{16,0},{24,8},{1,17},{9,25},{17,1},{25,9},{2,18},{10... | collective-permute-start | bytes 940040 | tf_op jit(solution)/shard_map/ppermute | solution.py:273
  33.7 1.3 %late_rows_begun.3.refs_5_ = f32[128,1152]{1,0:T(8,128)S(1)} custom-call(f32[1]{0:T(128)S(6)} %copy.17.refs_0_, f32[1]{0:T(128)S(6)} %copy.18.refs_1_, bf16[128,1152]{1,0:T(8,128)(2,1)S(1)} %collective-permute-done.5.refs_2_.refs_8_, bf16[136,1152]{1,0:T(8,128)(2,1)S(1)} %collective-permute-done.6.refs_3_.refs_8_, bf16[128,1152]{1,0:T(8,128)(2,1)S(1)} %copy-done, ...), custom_call_target="tpu_custom_call" | custom-call | flops 896 | bytes 896 | tf_op jit(solution)/shard_map/late_rows_begun/pallas_call | solution.py:92
  35.1 0.0 collective-permute-done.8.refs_4_.refs_9_
  35.1 0.6 %late_rows.3.refs_13_ = s16[136,1152]{1,0:T(8,128)(2,1)S(1)} custom-call(f32[1]{0:T(128)S(6)} %copy.17.refs_0_, f32[1]{0:T(128)S(6)} %copy.18.refs_1_, bf16[128,1152]{1,0:T(8,128)(2,1)S(1)} %collective-permute-done.5.refs_2_.refs_8_, bf16[136,1152]{1,0:T(8,128)(2,1)S(1)} %collective-permute-done.6.refs_3_.refs_8_, ...), custom_call_target="tpu_custom_call" | custom-call | flops 128 | bytes 128 | tf_op jit(solution)/shard_map/late_rows/pallas_call | solution.py:92
  35.7 0.7 %collective-permute-start.12 = (s16[136,1152]{1,0:T(8,128)(2,1)S(1)}, s16[136,1152]{1,0:T(8,128)(2,1)S(1)}, u32[]{:S(2)}, u32[]{:S(2)}) collective-permute-start(s16[136,1152]{1,0:T(8,128)(2,1)S(1)} %late_rows.3.refs_13_), channel_id=1, source_target_pairs={{0,8},{8,0},{16,24},{24,16},{1,9},{9,1},{17,25},{25,17},{2,10},{10... | collective-permute-start | bytes 940040 | tf_op jit(solution)/shard_map/ppermute | solution.py:273
  36.4 1.3 %late_columns.2 = (f32[128,1152]{1,0:T(8,128)S(1)}, f32[128,1152]{1,0:T(8,128)S(1)}, s16[136,1152]{1,0:T(8,128)(2,1)S(1)}) custom-call(f32[1]{0:T(128)S(6)} %copy.17.refs_0_, f32[1]{0:T(128)S(6)} %copy.18.refs_1_, bf16[128,1152]{1,0:T(8,128)(2,1)S(1)} %held.3.refs_2_.refs_0_.refs_5_, bf16[136,1152]{1,0:T(8,128)(2,1)S(1)} %labelled.2.refs_1_.refs_3_.refs_5_, ...), custom_call_target="tpu_custom_call" | custom-call | flops 768 | bytes 768 | tf_op jit(solution)/shard_map/late_columns/pallas_call | solution.py:92
  37.7 1.3 %late_columns.3 = (f32[128,1152]{1,0:T(8,128)S(1)}, f32[128,1152]{1,0:T(8,128)S(1)}, s16[136,1152]{1,0:T(8,128)(2,1)S(1)}) custom-call(f32[1]{0:T(128)S(6)} %copy.17.refs_0_, f32[1]{0:T(128)S(6)} %copy.18.refs_1_, bf16[128,1152]{1,0:T(8,128)(2,1)S(1)} %held.3.refs_2_.refs_0_.refs_5_, bf16[136,1152]{1,0:T(8,128)(2,1)S(1)} %labelled.2.refs_1_.refs_3_.refs_5_, ...), custom_call_target="tpu_custom_call" | custom-call | flops 768 | bytes 768 | tf_op jit(solution)/shard_map/late_columns/pallas_call | solution.py:92
  39.0 2.5 %collective-permute-done.10.refs_1_ = s16[136,1152]{1,0:T(8,128)(2,1)S(1)} collective-permute-done((s16[136,1152]{1,0:T(8,128)(2,1)S(1)}, s16[136,1152]{1,0:T(8,128)(2,1)S(1)}, u32[]{:S(2)}, u32[]{:S(2)}) %collective-permute-start.10) | collective-permute-done | bytes 313376 | tf_op jit(solution)/shard_map/ppermute | solution.py:273
  41.5 0.2 passed_sum.2
  41.7 1.4 %collective-permute-start.11 = (s16[136,1152]{1,0:T(8,128)(2,1)S(1)}, s16[136,1152]{1,0:T(8,128)(2,1)S(1)}, u32[]{:S(2)}, u32[]{:S(2)}) collective-permute-start(s16[136,1152]{1,0:T(8,128)(2,1)S(1)} %get-tuple-element.43.refs_2_), channel_id=1, source_target_pairs={{0,4},{1,5},{2,6},{3,7},{4,0},{5,1},{6,2},{7,3},{8,12},{9,13},{10,... | collective-permute-start | bytes 940040 | tf_op jit(solution)/shard_map/ppermute | solution.py:273
  43.1 1.7 %collective-permute-done.12.refs_1_ = s16[136,1152]{1,0:T(8,128)(2,1)S(1)} collective-permute-done((s16[136,1152]{1,0:T(8,128)(2,1)S(1)}, s16[136,1152]{1,0:T(8,128)(2,1)S(1)}, u32[]{:S(2)}, u32[]{:S(2)}) %collective-permute-start.12) | collective-permute-done | bytes 313376 | tf_op jit(solution)/shard_map/ppermute | solution.py:273
  44.8 0.2 passed_sum.3
  45.0 1.5 %collective-permute-start.13 = (s16[136,1152]{1,0:T(8,128)(2,1)S(1)}, s16[136,1152]{1,0:T(8,128)(2,1)S(1)}, u32[]{:S(2)}, u32[]{:S(2)}) collective-permute-start(s16[136,1152]{1,0:T(8,128)(2,1)S(1)} %get-tuple-element.46), channel_id=1, source_target_pairs={{0,2},{1,3},{2,0},{3,1},{4,6},{5,7},{6,4},{7,5},{8,10},{9,11},{10,... | collective-permute-start | bytes 940040 | tf_op jit(solution)/shard_map/ppermute | solution.py:273
  46.5 0.7 %collective-permute-start.14 = (s16[136,1152]{1,0:T(8,128)(2,1)S(1)}, s16[136,1152]{1,0:T(8,128)(2,1)S(1)}, u32[]{:S(2)}, u32[]{:S(2)}) collective-permute-start(s16[136,1152]{1,0:T(8,128)(2,1)S(1)} %get-tuple-element.47), channel_id=1, source_target_pairs={{0,8},{8,0},{16,24},{24,16},{1,9},{9,1},{17,25},{25,17},{2,10},{10... | collective-permute-start | bytes 940040 | tf_op jit(solution)/shard_map/ppermute | solution.py:273
  47.1 0.8 %collective-permute-start.15 = (s16[136,1152]{1,0:T(8,128)(2,1)S(1)}, s16[136,1152]{1,0:T(8,128)(2,1)S(1)}, u32[]{:S(2)}, u32[]{:S(2)}) collective-permute-start(s16[136,1152]{1,0:T(8,128)(2,1)S(1)} %get-tuple-element.49), channel_id=1, source_target_pairs={{0,16},{8,24},{16,0},{24,8},{1,17},{9,25},{17,1},{25,9},{2,18},{10... | collective-permute-start | bytes 940040 | tf_op jit(solution)/shard_map/ppermute | solution.py:273
  47.9 10.0 %collective-permute-done.11.refs_0_ = s16[136,1152]{1,0:T(8,128)(2,1)S(1)} collective-permute-done((s16[136,1152]{1,0:T(8,128)(2,1)S(1)}, s16[136,1152]{1,0:T(8,128)(2,1)S(1)}, u32[]{:S(2)}, u32[]{:S(2)}) %collective-permute-start.11) | collective-permute-done | bytes 313376 | tf_op jit(solution)/shard_map/ppermute | solution.py:273
  58.0 1.0 %collective-permute-done.13.refs_1_ = s16[136,1152]{1,0:T(8,128)(2,1)S(1)} collective-permute-done((s16[136,1152]{1,0:T(8,128)(2,1)S(1)}, s16[136,1152]{1,0:T(8,128)(2,1)S(1)}, u32[]{:S(2)}, u32[]{:S(2)}) %collective-permute-start.13) | collective-permute-done | bytes 313376 | tf_op jit(solution)/shard_map/ppermute | solution.py:273
  58.9 0.0 collective-permute-done.14.refs_3_
  58.9 0.0 collective-permute-done.15.refs_6_
  58.9 1.2 %output_sums.1 = (f32[128,1152]{1,0:T(8,128)}, f32[128,1152]{1,0:T(8,128)}) custom-call(f32[1]{0:T(128)S(6)} %copy.17.refs_0_, f32[128,1152]{1,0:T(8,128)S(1)} %get-tuple-element.41.refs_1_, s16[136,1152]{1,0:T(8,128)(2,1)S(1)} %held.5.refs_2_, s16[136,1152]{1,0:T(8,128)(2,1)S(1)} %collective-permute-done.14.refs_3_, ...), custom_call_target="tpu_custom_call" | custom-call | flops 128 | bytes 128 | tf_op jit(solution)/shard_map/output_sums/pallas_call | solution.py:92
  (6 shorter events, 0.1 us)
Async XLA Ops:
  0.6 17.8 %collective-permute-start = (bf16[128,1152]{1,0:T(8,128)(2,1)}, bf16[128,1152]{1,0:T(8,128)(2,1)S(1)}, u32[]{:S(2)}, u32[]{:S(2)}) collective-permute-start(bf16[128,1152]{1,0:T(8,128)(2,1)} %refs_6_.7), channel_id=1, source_target_pairs={{0,4},{1,5},{2,6},{3,7},{4,0},{5,1},{6,2},{7,3},{8,12},{9,13},{10,... | collective-permute-start | bytes 884744 | tf_op jit(solution)/shard_map/ppermute | solution.py:273
  4.7 13.9 %collective-permute-start.1 = (bf16[128,1152]{1,0:T(8,128)(2,1)}, bf16[128,1152]{1,0:T(8,128)(2,1)S(1)}, u32[]{:S(2)}, u32[]{:S(2)}) collective-permute-start(bf16[128,1152]{1,0:T(8,128)(2,1)} %refs_0_.10), channel_id=1, source_target_pairs={{0,2},{1,3},{2,0},{3,1},{4,6},{5,7},{6,4},{7,5},{8,10},{9,11},{10,... | collective-permute-start | bytes 884744 | tf_op jit(solution)/shard_map/ppermute | solution.py:273
  6.3 1.0 %copy-start.1 = (bf16[128,1152]{1,0:T(8,128)(2,1)S(1)}, bf16[128,1152]{1,0:T(8,128)(2,1)}, u32[]{:S(2)}) copy-start(bf16[128,1152]{1,0:T(8,128)(2,1)} %refs_0_.10) | copy-start | bytes 884740
  7.3 0.7 %copy-start.2 = (s32[128]{0:T(128)S(1)}, s32[128]{0:T(128)}, u32[]{:S(2)}) copy-start(s32[128]{0:T(128)} %param.7) | copy-start | bytes 1540
  8.0 10.8 %copy-start = (bf16[128,1152]{1,0:T(8,128)(2,1)S(1)}, bf16[128,1152]{1,0:T(8,128)(2,1)}, u32[]{:S(2)}) copy-start(bf16[128,1152]{1,0:T(8,128)(2,1)} %refs_6_.7) | copy-start | bytes 884740
  8.0 10.7 %collective-permute-start.4 = (bf16[136,1152]{1,0:T(8,128)(2,1)S(1)}, bf16[136,1152]{1,0:T(8,128)(2,1)S(1)}, u32[]{:S(2)}, u32[]{:S(2)}) collective-permute-start(bf16[136,1152]{1,0:T(8,128)(2,1)S(1)} %labelled.3.refs_2_.refs_7_.refs_4_), channel_id=1, source_target_pairs={{0,8},{8,0},{16,24},{24,16},{1,9},{9,1},{17,25},{25,17},{2,10},{10... | collective-permute-start | bytes 940040 | tf_op jit(solution)/shard_map/ppermute | solution.py:273
  9.6 9.2 %collective-permute-start.3 = (bf16[128,1152]{1,0:T(8,128)(2,1)}, bf16[128,1152]{1,0:T(8,128)(2,1)S(1)}, u32[]{:S(2)}, u32[]{:S(2)}) collective-permute-start(bf16[128,1152]{1,0:T(8,128)(2,1)} %refs_6_.7), channel_id=1, source_target_pairs={{0,16},{8,24},{16,0},{24,8},{1,17},{9,25},{17,1},{25,9},{2,18},{10... | collective-permute-start | bytes 884744 | tf_op jit(solution)/shard_map/ppermute | solution.py:273
  11.1 7.6 %collective-permute-start.2 = (s32[1,128]{1,0:T(1,128)S(1)}, s32[1,128]{1,0:T(1,128)S(1)}, u32[]{:S(2)}, u32[]{:S(2)}) collective-permute-start(s32[1,128]{1,0:T(1,128)S(1)} %bitcast.2), channel_id=1, source_target_pairs={{0,2},{1,3},{2,0},{3,1},{4,6},{5,7},{6,4},{7,5},{8,10},{9,11},{10,... | collective-permute-start | bytes 1544 | tf_op jit(solution)/shard_map/ppermute | solution.py:273
  18.9 4.5 %collective-permute-start.7 = (bf16[792,1152]{1,0:T(8,128)(2,1)S(1)}, bf16[792,1152]{1,0:T(8,128)(2,1)S(1)}, u32[]{:S(2)}, u32[]{:S(2)}) collective-permute-start(bf16[792,1152]{1,0:T(8,128)(2,1)S(1)} %bundled.3), channel_id=1, source_target_pairs={{0,1},{1,0},{2,3},{3,2},{4,5},{5,4},{6,7},{7,6},{8,9},{9,8},{10,11... | collective-permute-start | bytes 5474312 | tf_op jit(solution)/shard_map/ppermute | solution.py:273
  19.0 10.7 %collective-permute-start.6 = (bf16[136,1152]{1,0:T(8,128)(2,1)S(1)}, bf16[136,1152]{1,0:T(8,128)(2,1)S(1)}, u32[]{:S(2)}, u32[]{:S(2)}) collective-permute-start(bf16[136,1152]{1,0:T(8,128)(2,1)S(1)} %labelled.2.refs_1_.refs_3_.refs_5_), channel_id=1, source_target_pairs={{0,8},{8,0},{16,24},{24,16},{1,9},{9,1},{17,25},{25,17},{2,10},{10... | collective-permute-start | bytes 940040 | tf_op jit(solution)/shard_map/ppermute | solution.py:273
  20.6 9.1 %collective-permute-start.5 = (bf16[128,1152]{1,0:T(8,128)(2,1)S(1)}, bf16[128,1152]{1,0:T(8,128)(2,1)S(1)}, u32[]{:S(2)}, u32[]{:S(2)}) collective-permute-start(bf16[128,1152]{1,0:T(8,128)(2,1)S(1)} %held.3.refs_2_.refs_0_.refs_5_), channel_id=1, source_target_pairs={{0,16},{8,24},{16,0},{24,8},{1,17},{9,25},{17,1},{25,9},{2,18},{10... | collective-permute-start | bytes 884744 | tf_op jit(solution)/shard_map/ppermute | solution.py:273
  29.7 1.9 %collective-permute-start.9 = (bf16[136,1152]{1,0:T(8,128)(2,1)S(1)}, bf16[136,1152]{1,0:T(8,128)(2,1)S(1)}, u32[]{:S(2)}, u32[]{:S(2)}) collective-permute-start(bf16[136,1152]{1,0:T(8,128)(2,1)S(1)} %collective-permute-done.6.refs_3_.refs_8_), channel_id=1, source_target_pairs={{0,1},{1,0},{2,3},{3,2},{4,5},{5,4},{6,7},{7,6},{8,9},{9,8},{10,11... | collective-permute-start | bytes 940040 | tf_op jit(solution)/shard_map/ppermute | solution.py:273
  29.7 5.4 %collective-permute-start.8 = (bf16[128,1152]{1,0:T(8,128)(2,1)S(1)}, bf16[128,1152]{1,0:T(8,128)(2,1)S(1)}, u32[]{:S(2)}, u32[]{:S(2)}) collective-permute-start(bf16[128,1152]{1,0:T(8,128)(2,1)S(1)} %collective-permute-done.5.refs_2_.refs_8_), channel_id=1, source_target_pairs={{0,1},{1,0},{2,3},{3,2},{4,5},{5,4},{6,7},{7,6},{8,9},{9,8},{10,11... | collective-permute-start | bytes 884744 | tf_op jit(solution)/shard_map/ppermute | solution.py:273
  32.1 9.4 %collective-permute-start.10 = (s16[136,1152]{1,0:T(8,128)(2,1)S(1)}, s16[136,1152]{1,0:T(8,128)(2,1)S(1)}, u32[]{:S(2)}, u32[]{:S(2)}) collective-permute-start(s16[136,1152]{1,0:T(8,128)(2,1)S(1)} %late_rows.2.refs_8_), channel_id=1, source_target_pairs={{0,16},{8,24},{16,0},{24,8},{1,17},{9,25},{17,1},{25,9},{2,18},{10... | collective-permute-start | bytes 940040 | tf_op jit(solution)/shard_map/ppermute | solution.py:273
  35.7 9.1 %collective-permute-start.12 = (s16[136,1152]{1,0:T(8,128)(2,1)S(1)}, s16[136,1152]{1,0:T(8,128)(2,1)S(1)}, u32[]{:S(2)}, u32[]{:S(2)}) collective-permute-start(s16[136,1152]{1,0:T(8,128)(2,1)S(1)} %late_rows.3.refs_13_), channel_id=1, source_target_pairs={{0,8},{8,0},{16,24},{24,16},{1,9},{9,1},{17,25},{25,17},{2,10},{10... | collective-permute-start | bytes 940040 | tf_op jit(solution)/shard_map/ppermute | solution.py:273
  41.7 16.3 %collective-permute-start.11 = (s16[136,1152]{1,0:T(8,128)(2,1)S(1)}, s16[136,1152]{1,0:T(8,128)(2,1)S(1)}, u32[]{:S(2)}, u32[]{:S(2)}) collective-permute-start(s16[136,1152]{1,0:T(8,128)(2,1)S(1)} %get-tuple-element.43.refs_2_), channel_id=1, source_target_pairs={{0,4},{1,5},{2,6},{3,7},{4,0},{5,1},{6,2},{7,3},{8,12},{9,13},{10,... | collective-permute-start | bytes 940040 | tf_op jit(solution)/shard_map/ppermute | solution.py:273
  45.0 14.0 %collective-permute-start.13 = (s16[136,1152]{1,0:T(8,128)(2,1)S(1)}, s16[136,1152]{1,0:T(8,128)(2,1)S(1)}, u32[]{:S(2)}, u32[]{:S(2)}) collective-permute-start(s16[136,1152]{1,0:T(8,128)(2,1)S(1)} %get-tuple-element.46), channel_id=1, source_target_pairs={{0,2},{1,3},{2,0},{3,1},{4,6},{5,7},{6,4},{7,5},{8,10},{9,11},{10,... | collective-permute-start | bytes 940040 | tf_op jit(solution)/shard_map/ppermute | solution.py:273
  46.5 12.4 %collective-permute-start.14 = (s16[136,1152]{1,0:T(8,128)(2,1)S(1)}, s16[136,1152]{1,0:T(8,128)(2,1)S(1)}, u32[]{:S(2)}, u32[]{:S(2)}) collective-permute-start(s16[136,1152]{1,0:T(8,128)(2,1)S(1)} %get-tuple-element.47), channel_id=1, source_target_pairs={{0,8},{8,0},{16,24},{24,16},{1,9},{9,1},{17,25},{25,17},{2,10},{10... | collective-permute-start | bytes 940040 | tf_op jit(solution)/shard_map/ppermute | solution.py:273
  47.1 11.8 %collective-permute-start.15 = (s16[136,1152]{1,0:T(8,128)(2,1)S(1)}, s16[136,1152]{1,0:T(8,128)(2,1)S(1)}, u32[]{:S(2)}, u32[]{:S(2)}) collective-permute-start(s16[136,1152]{1,0:T(8,128)(2,1)S(1)} %get-tuple-element.49), channel_id=1, source_target_pairs={{0,16},{8,24},{16,0},{24,8},{1,17},{9,25},{17,1},{25,9},{2,18},{10... | collective-permute-start | bytes 940040 | tf_op jit(solution)/shard_map/ppermute | solution.py:273

commit v14 on v13

--- a/solution.py
+++ b/solution.py
@@ -15,6 +15,7 @@
 TILE = 256
 LANES = 128
 BUNDLE_COST = 6 * 10**8
+HELD_COST = 85 * 10**7
 SMEM = pl.BlockSpec(memory_space=pltpu.SMEM)
 VMEM = pl.BlockSpec(memory_space=pltpu.VMEM)
 ANY = pl.BlockSpec(memory_space=pl.ANY)
@@ -25,7 +26,7 @@
 
 
 def part_widths(width):
-    first = min(3 * TILE, width - LANES)
+    first = (width // LANES + 1) // 2 * LANES
     return (first, width - first)
 
 
@@ -274,26 +275,28 @@
 
 
 def scattered(kept, coded, steps, after):
-    def sent(block, step):
-        return [(swapped(p, step), 0, 0) for p in block]
-
-    half, waiting = len(kept), coded[0]
-    received = [[]] + [[sent(c, steps[-1])] for c in coded[1:]]
+    def sent(array, step):
+        return (swapped(array, step), 0, 0)
+
+    half = len(kept)
+    received = [[]] + [[(sent(c[0], steps[-1]),)] for c in coded[1:]]
+    waiting, last = [c[1] for c in coded[1:]], [coded[0][0]]
     for s in reversed(range(len(steps) - 1)):
         for m in reversed(range(1 << s)):
             n = m | 1 << s
-            block = passed_sum(kept[n], received[n], None, waiting, after)
-            after = block[:1]
-            if n == half - 1:
-                block, *waiting = block
-                received[0].append(sent(waiting, steps[-1]))
-                waiting, block = (), [block]
-            received[m].append(sent(block, steps[s]))
-    return (kept[0], received[0][::-1]), after
-
-
-def in_order(arrays, after=()):
-    return call(lambda *refs: None, "held", [], [], [], 2**21, 1, after, arrays)
+            first, *begun = passed_sum(kept[n], received[n], 0, waiting + last)
+            for r, c in zip(received[1:], begun):
+                r[0] = r[0] + (sent(c, steps[-1]),)
+            received[0] += [(sent(c, steps[-1]),) for c in begun[len(waiting) :]]
+            first = sent(first, steps[s])
+            (second,) = passed_sum(kept[n], received[n], 1, (), [first[0], *after])
+            received[m].append((first, sent(second, steps[s])))
+            waiting, last, after = [], [], [second]
+    return kept[0], received[0], after
+
+
+def in_order(arrays, after=(), cost=HELD_COST):
+    return call(lambda *refs: None, "held", [], [], [], 2**21, cost, after, arrays)
 
 
 def bit_steps(axis):
@@ -321,7 +324,7 @@
     half = count // 2
     early, late = list(range(half + 1)), list(range(half + 1, count))
     labels = matching_caption[None, :]
-    (first_texts,) = in_order([swapped(caption_vectors, steps[1][0])])
+    (first_texts,) = in_order([swapped(caption_vectors, steps[1][0])], (), 1)
     first_images = [swapped(a, steps[0][0]) for a in (picture_vectors, labels)]
     arrays = [{0: labelled(picture_vectors, labels), 1: labelled(*first_images, [first_texts])}, {0: caption_vectors, 1: first_texts}]
     for i in range(1, len(steps[0])):
@@ -384,7 +387,7 @@
         results = sums("late_rows_begun", k, late, columns, jobs, {}, emits, after)
         begun = {i: s for i, (s,) in enumerate(results)}
         columns = [(1, m) for m in late]
-        jobs, emits = every_pair(late, columns), ["whole"] * len(late)
+        jobs, emits = every_pair(late, columns), ["parts"] * len(late)
         coded[k][1:] = sums("late_rows", k, late, columns, jobs, begun, emits)
         after = coded[k][1]
     for k in (1, 0):
@@ -392,13 +395,13 @@
         jobs, emits = every_pair(early, columns), ["float"] * half + ["whole"]
         *whole_sums, coded[k][0] = sums("late_columns", k, early, columns, jobs, before[k], emits, after)
         kept[k], after = [s for (s,) in whole_sums], coded[k][0]
-    texts, after = scattered(kept[1], coded[1], steps[1], ())
-    images, _ = scattered(kept[0], coded[0], steps[0], after)
-    (kept_texts, text_blocks), (kept_images, image_blocks) = texts, images
-    text_parts = in_order([b[0][0] for b in text_blocks[:-1]])
-    image_parts = in_order([b[0][0] for b in image_blocks[:-1]], text_parts)
-    text_blocks = [whole(a) for a in text_parts] + text_blocks[-1:]
-    image_blocks = [whole(a) for a in image_parts] + image_blocks[-1:]
+    kept_texts, text_blocks, after = scattered(kept[1], coded[1], steps[1], ())
+    kept_images, image_blocks, _ = scattered(kept[0], coded[0], steps[0], after)
+    ends = ()
+    for blocks_in in (text_blocks, image_blocks):
+        ends = in_order([part[0] for b in blocks_in if len(b) > 1 for part in b], ends)
+        parts = iter(ends)
+        blocks_in[:] = [tuple((next(parts), 0, 0) for _ in b) if len(b) > 1 else b for b in blocks_in]
     return tuple(output_sums(scalars[0], [(kept_images, image_blocks), (kept_texts, text_blocks)]))
 
 

time: 60.3 us -> 60.1 us (level)
  waiting for transfers between devices: 24.7 us -> 18.9 us
  starting transfers between devices: 19.6 us -> 25.1 us
    ppermute x16 -> x20, waiting for transfers between devices: 24.7 us -> 18.9 us  [swapped(): lax.ppermute(array, axis, [(i, i ^ bit) for i in range(lax.axis_size(axis...]
    ppermute x16 -> x20, starting transfers between devices: 19.6 us -> 25.1 us  [swapped(): lax.ppermute(array, axis, [(i, i ^ bit) for i in range(lax.axis_size(axis...]
    pallas_call x18 -> x20, Pallas kernels: 12.1 us -> 12.2 us  [call(): pl.pallas_call(body, out_shape=[*out_shape, *(jax.ShapeDtypeStruct(a.shap...]
  transfers between devices with their start and end apart: 16 -> 20, of which waited for: 7 -> 8; matrix products, arithmetic and copies ran while one was open for 0% -> 0% of each run, Pallas kernels for 18% -> 18%
where the time goes in v14:
time: 60.1 us; the launch traced here: 59.9 us
  starting transfers between devices  25.1 us (42%)
  waiting for transfers between devices  18.9 us (31%)
  Pallas kernels  12.2 us (20%)
  between operations  2.13 us (4%)
  local copies, waits for them, and re-layouts  1.66 us (3%)
    ppermute x20, starting transfers between devices, swapped(): lax.ppermute(array, axis, [(i, i ^ bit) for i in range(lax.axis_size(axis...  25.1 us
    ppermute x20, waiting for transfers between devices, swapped(): lax.ppermute(array, axis, [(i, i ^ bit) for i in range(lax.axis_size(axis...  18.9 us
    pallas_call x20, Pallas kernels, call(): pl.pallas_call(body, out_shape=[*out_shape, *(jax.ShapeDtypeStruct(a.shap...  12.2 us
    unnamed x6, local copies, waits for them, and re-layouts  1.66 us
  transfers between devices with their start and end apart: 20, of which 8 were waited for; matrix products, arithmetic and copies ran while one was open for 0% of the time, Pallas kernels for 18%

profile of v14, /device:TPU:0, one launch (start us, length us, event | category | flops | bytes accessed | tf_op | source)
XLA Modules:
  0.0 59.9 jit_solution(10749634806486829264)
XLA Ops:
  0.6 4.1 %collective-permute-start = (bf16[128,1152]{1,0:T(8,128)(2,1)}, bf16[128,1152]{1,0:T(8,128)(2,1)S(1)}, u32[]{:S(2)}, u32[]{:S(2)}) collective-permute-start(bf16[128,1152]{1,0:T(8,128)(2,1)} %refs_6_.7), channel_id=1, source_target_pairs={{0,4},{1,5},{2,6},{3,7},{4,0},{5,1},{6,2},{7,3},{8,12},{9,13},{10,... | collective-permute-start | bytes 884744 | tf_op jit(solution)/shard_map/ppermute | solution.py:274
  4.7 1.6 %collective-permute-start.1 = (bf16[128,1152]{1,0:T(8,128)(2,1)}, bf16[128,1152]{1,0:T(8,128)(2,1)S(1)}, u32[]{:S(2)}, u32[]{:S(2)}) collective-permute-start(bf16[128,1152]{1,0:T(8,128)(2,1)} %refs_0_.10), channel_id=1, source_target_pairs={{0,2},{1,3},{2,0},{3,1},{4,6},{5,7},{6,4},{7,5},{8,10},{9,11},{10,... | collective-permute-start | bytes 884744 | tf_op jit(solution)/shard_map/ppermute | solution.py:274
  6.3 0.0 copy-start.1
  6.3 1.0 %copy-done.1 = bf16[128,1152]{1,0:T(8,128)(2,1)S(1)} copy-done((bf16[128,1152]{1,0:T(8,128)(2,1)S(1)}, bf16[128,1152]{1,0:T(8,128)(2,1)}, u32[]{:S(2)}) %copy-start.1) | copy-done | bytes 294936
  7.3 0.0 copy-start.2
  7.3 0.7 %copy-done.2 = s32[128]{0:T(128)S(1)} copy-done((s32[128]{0:T(128)S(1)}, s32[128]{0:T(128)}, u32[]{:S(2)}) %copy-start.2) | copy-done | bytes 536
  8.0 0.0 copy-start
  8.0 1.6 %collective-permute-start.4 = (bf16[136,1152]{1,0:T(8,128)(2,1)S(1)}, bf16[136,1152]{1,0:T(8,128)(2,1)S(1)}, u32[]{:S(2)}, u32[]{:S(2)}) collective-permute-start(bf16[136,1152]{1,0:T(8,128)(2,1)S(1)} %labelled.3.refs_2_.refs_7_.refs_4_), channel_id=1, source_target_pairs={{0,8},{8,0},{16,24},{24,16},{1,9},{9,1},{17,25},{25,17},{2,10},{10... | collective-permute-start | bytes 940040 | tf_op jit(solution)/shard_map/ppermute | solution.py:274
  9.6 1.5 %collective-permute-start.3 = (bf16[128,1152]{1,0:T(8,128)(2,1)}, bf16[128,1152]{1,0:T(8,128)(2,1)S(1)}, u32[]{:S(2)}, u32[]{:S(2)}) collective-permute-start(bf16[128,1152]{1,0:T(8,128)(2,1)} %refs_6_.7), channel_id=1, source_target_pairs={{0,16},{8,24},{16,0},{24,8},{1,17},{9,25},{17,1},{25,9},{2,18},{10... | collective-permute-start | bytes 884744 | tf_op jit(solution)/shard_map/ppermute | solution.py:274
  11.1 0.4 collective-permute-start.2
  11.5 6.8 %collective-permute-done.refs_0_ = bf16[128,1152]{1,0:T(8,128)(2,1)S(1)} collective-permute-done((bf16[128,1152]{1,0:T(8,128)(2,1)}, bf16[128,1152]{1,0:T(8,128)(2,1)S(1)}, u32[]{:S(2)}, u32[]{:S(2)}) %collective-permute-start) | collective-permute-done | bytes 294944 | tf_op jit(solution)/shard_map/ppermute | solution.py:274
  18.4 0.3 collective-permute-done.2.refs_1_
  18.6 0.0 collective-permute-done.1.refs_0_
  18.7 0.0 collective-permute-done.3.refs_3_.refs_4_.refs_6_
  18.7 0.0 collective-permute-done.4.refs_4_.refs_5_.refs_6_
  18.7 0.0 copy-done
  18.8 0.1 bundled.3
  18.9 0.1 collective-permute-start.7
  19.0 1.6 %collective-permute-start.6 = (bf16[136,1152]{1,0:T(8,128)(2,1)S(1)}, bf16[136,1152]{1,0:T(8,128)(2,1)S(1)}, u32[]{:S(2)}, u32[]{:S(2)}) collective-permute-start(bf16[136,1152]{1,0:T(8,128)(2,1)S(1)} %labelled.2.refs_1_.refs_3_.refs_5_), channel_id=1, source_target_pairs={{0,8},{8,0},{16,24},{24,16},{1,9},{9,1},{17,25},{25,17},{2,10},{10... | collective-permute-start | bytes 940040 | tf_op jit(solution)/shard_map/ppermute | solution.py:274
  20.6 1.5 %collective-permute-start.5 = (bf16[128,1152]{1,0:T(8,128)(2,1)S(1)}, bf16[128,1152]{1,0:T(8,128)(2,1)S(1)}, u32[]{:S(2)}, u32[]{:S(2)}) collective-permute-start(bf16[128,1152]{1,0:T(8,128)(2,1)S(1)} %held.3.refs_2_.refs_0_.refs_5_), channel_id=1, source_target_pairs={{0,16},{8,24},{16,0},{24,8},{1,17},{9,25},{17,1},{25,9},{2,18},{10... | collective-permute-start | bytes 884744 | tf_op jit(solution)/shard_map/ppermute | solution.py:274
  23.4 0.0 collective-permute-done.7.refs_8_.refs_7_
  23.4 1.9 %early_sums.3 = (f32[128,1152]{1,0:T(8,128)S(1)}, f32[128,1152]{1,0:T(8,128)S(1)}, f32[128,1152]{1,0:T(8,128)S(1)}) custom-call(f32[1]{0:T(128)S(6)} %copy.25.refs_0_, f32[1]{0:T(128)S(6)} %copy.26.refs_1_, bf16[128,1152]{1,0:T(8,128)(2,1)S(1)} %held.3.refs_2_.refs_0_.refs_5_, bf16[136,1152]{1,0:T(8,128)(2,1)S(1)} %labelled.2.refs_1_.refs_3_.refs_5_, ...), custom_call_target="tpu_custom_call" | custom-call | flops 2304 | bytes 2304 | tf_op jit(solution)/shard_map/early_sums/pallas_call | solution.py:93
  25.3 1.9 %early_sums.2 = (f32[128,1152]{1,0:T(8,128)S(1)}, f32[128,1152]{1,0:T(8,128)S(1)}, f32[128,1152]{1,0:T(8,128)S(1)}) custom-call(f32[1]{0:T(128)S(6)} %copy.25.refs_0_, f32[1]{0:T(128)S(6)} %copy.26.refs_1_, bf16[128,1152]{1,0:T(8,128)(2,1)S(1)} %held.3.refs_2_.refs_0_.refs_5_, bf16[136,1152]{1,0:T(8,128)(2,1)S(1)} %labelled.2.refs_1_.refs_3_.refs_5_, ...), custom_call_target="tpu_custom_call" | custom-call | flops 2304 | bytes 2304 | tf_op jit(solution)/shard_map/early_sums/pallas_call | solution.py:93
  27.3 2.4 %collective-permute-done.5.refs_2_.refs_8_ = bf16[128,1152]{1,0:T(8,128)(2,1)S(1)} collective-permute-done((bf16[128,1152]{1,0:T(8,128)(2,1)S(1)}, bf16[128,1152]{1,0:T(8,128)(2,1)S(1)}, u32[]{:S(2)}, u32[]{:S(2)}) %collective-permute-start.5) | collective-permute-done | bytes 294944 | tf_op jit(solution)/shard_map/ppermute | solution.py:274
  29.7 0.0 collective-permute-done.6.refs_3_.refs_8_
  29.7 0.0 collective-permute-start.9
  29.7 0.5 collective-permute-start.8
  30.2 1.3 %late_rows_begun.2.refs_5_ = f32[128,1152]{1,0:T(8,128)S(1)} custom-call(f32[1]{0:T(128)S(6)} %copy.25.refs_0_, f32[1]{0:T(128)S(6)} %copy.26.refs_1_, bf16[128,1152]{1,0:T(8,128)(2,1)S(1)} %collective-permute-done.5.refs_2_.refs_8_, bf16[136,1152]{1,0:T(8,128)(2,1)S(1)} %collective-permute-done.6.refs_3_.refs_8_, ...), custom_call_target="tpu_custom_call" | custom-call | flops 896 | bytes 896 | tf_op jit(solution)/shard_map/late_rows_begun/pallas_call | solution.py:93
  31.5 0.0 collective-permute-done.9.refs_4_.refs_9_
  31.5 0.6 %late_rows.2 = (s16[136,640]{1,0:T(8,128)(2,1)S(1)}, s16[136,512]{1,0:T(8,128)(2,1)S(1)}) custom-call(f32[1]{0:T(128)S(6)} %copy.25.refs_0_, f32[1]{0:T(128)S(6)} %copy.26.refs_1_, bf16[128,1152]{1,0:T(8,128)(2,1)S(1)} %collective-permute-done.5.refs_2_.refs_8_, bf16[136,1152]{1,0:T(8,128)(2,1)S(1)} %collective-permute-done.6.refs_3_.refs_8_, ...), custom_call_target="tpu_custom_call" | custom-call | flops 128 | bytes 128 | tf_op jit(solution)/shard_map/late_rows/pallas_call | solution.py:93
  32.2 1.6 %collective-permute-start.12 = (s16[136,640]{1,0:T(8,128)(2,1)S(1)}, s16[136,640]{1,0:T(8,128)(2,1)S(1)}, u32[]{:S(2)}, u32[]{:S(2)}) collective-permute-start(s16[136,640]{1,0:T(8,128)(2,1)S(1)} %get-tuple-element.50.refs_8_), channel_id=1, source_target_pairs={{0,16},{8,24},{16,0},{24,8},{1,17},{9,25},{17,1},{25,9},{2,18},{10... | collective-permute-start | bytes 522248 | tf_op jit(solution)/shard_map/ppermute | solution.py:274
  33.7 1.3 %late_rows_begun.3.refs_5_ = f32[128,1152]{1,0:T(8,128)S(1)} custom-call(f32[1]{0:T(128)S(6)} %copy.25.refs_0_, f32[1]{0:T(128)S(6)} %copy.26.refs_1_, bf16[128,1152]{1,0:T(8,128)(2,1)S(1)} %collective-permute-done.5.refs_2_.refs_8_, bf16[136,1152]{1,0:T(8,128)(2,1)S(1)} %collective-permute-done.6.refs_3_.refs_8_, bf16[128,1152]{1,0:T(8,128)(2,1)S(1)} %copy-done, ...), custom_call_target="tpu_custom_call" | custom-call | flops 896 | bytes 896 | tf_op jit(solution)/shard_map/late_rows_begun/pallas_call | solution.py:93
  35.1 0.0 collective-permute-done.8.refs_4_.refs_9_
  35.1 0.6 %late_rows.3 = (s16[136,640]{1,0:T(8,128)(2,1)S(1)}, s16[136,512]{1,0:T(8,128)(2,1)S(1)}) custom-call(f32[1]{0:T(128)S(6)} %copy.25.refs_0_, f32[1]{0:T(128)S(6)} %copy.26.refs_1_, bf16[128,1152]{1,0:T(8,128)(2,1)S(1)} %collective-permute-done.5.refs_2_.refs_8_, bf16[136,1152]{1,0:T(8,128)(2,1)S(1)} %collective-permute-done.6.refs_3_.refs_8_, ...), custom_call_target="tpu_custom_call" | custom-call | flops 128 | bytes 128 | tf_op jit(solution)/shard_map/late_rows/pallas_call | solution.py:93
  35.7 0.7 %collective-permute-start.10 = (s16[136,640]{1,0:T(8,128)(2,1)S(1)}, s16[136,640]{1,0:T(8,128)(2,1)S(1)}, u32[]{:S(2)}, u32[]{:S(2)}) collective-permute-start(s16[136,640]{1,0:T(8,128)(2,1)S(1)} %get-tuple-element.52.refs_13_), channel_id=1, source_target_pairs={{0,8},{8,0},{16,24},{24,16},{1,9},{9,1},{17,25},{25,17},{2,10},{10... | collective-permute-start | bytes 522248 | tf_op jit(solution)/shard_map/ppermute | solution.py:274
  36.4 1.3 %late_columns.2 = (f32[128,1152]{1,0:T(8,128)S(1)}, f32[128,1152]{1,0:T(8,128)S(1)}, s16[136,1152]{1,0:T(8,128)(2,1)S(1)}) custom-call(f32[1]{0:T(128)S(6)} %copy.25.refs_0_, f32[1]{0:T(128)S(6)} %copy.26.refs_1_, bf16[128,1152]{1,0:T(8,128)(2,1)S(1)} %held.3.refs_2_.refs_0_.refs_5_, bf16[136,1152]{1,0:T(8,128)(2,1)S(1)} %labelled.2.refs_1_.refs_3_.refs_5_, ...), custom_call_target="tpu_custom_call" | custom-call | flops 768 | bytes 768 | tf_op jit(solution)/shard_map/late_columns/pallas_call | solution.py:93
  37.7 1.3 %late_columns.3 = (f32[128,1152]{1,0:T(8,128)S(1)}, f32[128,1152]{1,0:T(8,128)S(1)}, s16[136,1152]{1,0:T(8,128)(2,1)S(1)}) custom-call(f32[1]{0:T(128)S(6)} %copy.25.refs_0_, f32[1]{0:T(128)S(6)} %copy.26.refs_1_, bf16[128,1152]{1,0:T(8,128)(2,1)S(1)} %held.3.refs_2_.refs_0_.refs_5_, bf16[136,1152]{1,0:T(8,128)(2,1)S(1)} %labelled.2.refs_1_.refs_3_.refs_5_, ...), custom_call_target="tpu_custom_call" | custom-call | flops 768 | bytes 768 | tf_op jit(solution)/shard_map/late_columns/pallas_call | solution.py:93
  39.0 0.0 collective-permute-done.12.refs_1_
  39.1 0.1 passed_sum.5
  39.2 1.4 %collective-permute-start.13 = (s16[136,640]{1,0:T(8,128)(2,1)S(1)}, s16[136,640]{1,0:T(8,128)(2,1)S(1)}, u32[]{:S(2)}, u32[]{:S(2)}) collective-permute-start(s16[136,640]{1,0:T(8,128)(2,1)S(1)} %get-tuple-element.60), channel_id=1, source_target_pairs={{0,4},{1,5},{2,6},{3,7},{4,0},{5,1},{6,2},{7,3},{8,12},{9,13},{10,... | collective-permute-start | bytes 522248 | tf_op jit(solution)/shard_map/ppermute | solution.py:274
  40.6 1.0 %collective-permute-start.14 = (s16[136,512]{1,0:T(8,128)(2,1)S(1)}, s16[136,512]{1,0:T(8,128)(2,1)S(1)}, u32[]{:S(2)}, u32[]{:S(2)}) collective-permute-start(s16[136,512]{1,0:T(8,128)(2,1)S(1)} %get-tuple-element.61), channel_id=1, source_target_pairs={{0,16},{8,24},{16,0},{24,8},{1,17},{9,25},{17,1},{25,9},{2,18},{10... | collective-permute-start | bytes 417800 | tf_op jit(solution)/shard_map/ppermute | solution.py:274
  41.6 0.2 collective-permute-done.10.refs_1_
  41.8 0.1 passed_sum.4
  41.9 2.2 %collective-permute-start.16 = (s16[136,640]{1,0:T(8,128)(2,1)S(1)}, s16[136,640]{1,0:T(8,128)(2,1)S(1)}, u32[]{:S(2)}, u32[]{:S(2)}) collective-permute-start(s16[136,640]{1,0:T(8,128)(2,1)S(1)} %get-tuple-element.64), channel_id=1, source_target_pairs={{0,2},{1,3},{2,0},{3,1},{4,6},{5,7},{6,4},{7,5},{8,10},{9,11},{10,... | collective-permute-start | bytes 522248 | tf_op jit(solution)/shard_map/ppermute | solution.py:274
  44.1 0.8 %collective-permute-start.17 = (s16[136,512]{1,0:T(8,128)(2,1)S(1)}, s16[136,512]{1,0:T(8,128)(2,1)S(1)}, u32[]{:S(2)}, u32[]{:S(2)}) collective-permute-start(s16[136,512]{1,0:T(8,128)(2,1)S(1)} %get-tuple-element.65), channel_id=1, source_target_pairs={{0,8},{8,0},{16,24},{24,16},{1,9},{9,1},{17,25},{25,17},{2,10},{10... | collective-permute-start | bytes 417800 | tf_op jit(solution)/shard_map/ppermute | solution.py:274
  45.0 1.5 %collective-permute-start.19 = (s16[136,1152]{1,0:T(8,128)(2,1)S(1)}, s16[136,1152]{1,0:T(8,128)(2,1)S(1)}, u32[]{:S(2)}, u32[]{:S(2)}) collective-permute-start(s16[136,1152]{1,0:T(8,128)(2,1)S(1)} %get-tuple-element.69), channel_id=1, source_target_pairs={{0,16},{8,24},{16,0},{24,8},{1,17},{9,25},{17,1},{25,9},{2,18},{10... | collective-permute-start | bytes 940040 | tf_op jit(solution)/shard_map/ppermute | solution.py:274
  46.5 0.0 collective-permute-done.14.refs_1_
  46.5 0.7 %collective-permute-start.11 = (s16[136,1152]{1,0:T(8,128)(2,1)S(1)}, s16[136,1152]{1,0:T(8,128)(2,1)S(1)}, u32[]{:S(2)}, u32[]{:S(2)}) collective-permute-start(s16[136,1152]{1,0:T(8,128)(2,1)S(1)} %get-tuple-element.58), channel_id=1, source_target_pairs={{0,8},{8,0},{16,24},{24,16},{1,9},{9,1},{17,25},{25,17},{2,10},{10... | collective-permute-start | bytes 940040 | tf_op jit(solution)/shard_map/ppermute | solution.py:274
  47.2 2.5 %collective-permute-done.13.refs_2_.refs_0_ = s16[136,640]{1,0:T(8,128)(2,1)S(1)} collective-permute-done((s16[136,640]{1,0:T(8,128)(2,1)S(1)}, s16[136,640]{1,0:T(8,128)(2,1)S(1)}, u32[]{:S(2)}, u32[]{:S(2)}) %collective-permute-start.13) | collective-permute-done | bytes 174112 | tf_op jit(solution)/shard_map/ppermute | solution.py:274
  49.7 0.1 passed_sum.6.refs_3_
  49.8 0.1 collective-permute-start.15
  49.9 0.7 %collective-permute-done.17.refs_1_ = s16[136,512]{1,0:T(8,128)(2,1)S(1)} collective-permute-done((s16[136,512]{1,0:T(8,128)(2,1)S(1)}, s16[136,512]{1,0:T(8,128)(2,1)S(1)}, u32[]{:S(2)}, u32[]{:S(2)}) %collective-permute-start.17) | collective-permute-done | bytes 139296 | tf_op jit(solution)/shard_map/ppermute | solution.py:274
  50.6 0.0 collective-permute-done.16.refs_2_
  50.6 0.1 passed_sum.7
  50.7 2.1 %collective-permute-start.18 = (s16[136,512]{1,0:T(8,128)(2,1)S(1)}, s16[136,512]{1,0:T(8,128)(2,1)S(1)}, u32[]{:S(2)}, u32[]{:S(2)}) collective-permute-start(s16[136,512]{1,0:T(8,128)(2,1)S(1)} %passed_sum.7), channel_id=1, source_target_pairs={{0,2},{1,3},{2,0},{3,1},{4,6},{5,7},{6,4},{7,5},{8,10},{9,11},{10,... | collective-permute-start | bytes 417800 | tf_op jit(solution)/shard_map/ppermute | solution.py:274
  52.9 5.6 %collective-permute-done.15.refs_1_ = s16[136,512]{1,0:T(8,128)(2,1)S(1)} collective-permute-done((s16[136,512]{1,0:T(8,128)(2,1)S(1)}, s16[136,512]{1,0:T(8,128)(2,1)S(1)}, u32[]{:S(2)}, u32[]{:S(2)}) %collective-permute-start.15) | collective-permute-done | bytes 139296 | tf_op jit(solution)/shard_map/ppermute | solution.py:274
  58.4 0.2 collective-permute-done.18.refs_3_
  58.7 0.0 collective-permute-done.19.refs_6_
  58.7 0.0 collective-permute-done.11.refs_2_
  58.7 1.2 %output_sums.1 = (f32[128,1152]{1,0:T(8,128)}, f32[128,1152]{1,0:T(8,128)}) custom-call(f32[1]{0:T(128)S(6)} %copy.25.refs_0_, f32[128,1152]{1,0:T(8,128)S(1)} %get-tuple-element.55.refs_1_, s16[136,1152]{1,0:T(8,128)(2,1)S(1)} %collective-permute-done.11.refs_2_, s16[136,640]{1,0:T(8,128)(2,1)S(1)} %get-tuple-element.66.refs_3_, ...), custom_call_target="tpu_custom_call" | custom-call | flops 128 | bytes 128 | tf_op jit(solution)/shard_map/output_sums/pallas_call | solution.py:93
  (6 shorter events, 0.1 us)
Async XLA Ops:
  0.6 17.8 %collective-permute-start = (bf16[128,1152]{1,0:T(8,128)(2,1)}, bf16[128,1152]{1,0:T(8,128)(2,1)S(1)}, u32[]{:S(2)}, u32[]{:S(2)}) collective-permute-start(bf16[128,1152]{1,0:T(8,128)(2,1)} %refs_6_.7), channel_id=1, source_target_pairs={{0,4},{1,5},{2,6},{3,7},{4,0},{5,1},{6,2},{7,3},{8,12},{9,13},{10,... | collective-permute-start | bytes 884744 | tf_op jit(solution)/shard_map/ppermute | solution.py:274
  4.7 13.9 %collective-permute-start.1 = (bf16[128,1152]{1,0:T(8,128)(2,1)}, bf16[128,1152]{1,0:T(8,128)(2,1)S(1)}, u32[]{:S(2)}, u32[]{:S(2)}) collective-permute-start(bf16[128,1152]{1,0:T(8,128)(2,1)} %refs_0_.10), channel_id=1, source_target_pairs={{0,2},{1,3},{2,0},{3,1},{4,6},{5,7},{6,4},{7,5},{8,10},{9,11},{10,... | collective-permute-start | bytes 884744 | tf_op jit(solution)/shard_map/ppermute | solution.py:274
  6.3 1.0 %copy-start.1 = (bf16[128,1152]{1,0:T(8,128)(2,1)S(1)}, bf16[128,1152]{1,0:T(8,128)(2,1)}, u32[]{:S(2)}) copy-start(bf16[128,1152]{1,0:T(8,128)(2,1)} %refs_0_.10) | copy-start | bytes 884740
  7.3 0.7 %copy-start.2 = (s32[128]{0:T(128)S(1)}, s32[128]{0:T(128)}, u32[]{:S(2)}) copy-start(s32[128]{0:T(128)} %param.7) | copy-start | bytes 1540
  8.0 10.8 %copy-start = (bf16[128,1152]{1,0:T(8,128)(2,1)S(1)}, bf16[128,1152]{1,0:T(8,128)(2,1)}, u32[]{:S(2)}) copy-start(bf16[128,1152]{1,0:T(8,128)(2,1)} %refs_6_.7) | copy-start | bytes 884740
  8.0 10.7 %collective-permute-start.4 = (bf16[136,1152]{1,0:T(8,128)(2,1)S(1)}, bf16[136,1152]{1,0:T(8,128)(2,1)S(1)}, u32[]{:S(2)}, u32[]{:S(2)}) collective-permute-start(bf16[136,1152]{1,0:T(8,128)(2,1)S(1)} %labelled.3.refs_2_.refs_7_.refs_4_), channel_id=1, source_target_pairs={{0,8},{8,0},{16,24},{24,16},{1,9},{9,1},{17,25},{25,17},{2,10},{10... | collective-permute-start | bytes 940040 | tf_op jit(solution)/shard_map/ppermute | solution.py:274
  9.6 9.2 %collective-permute-start.3 = (bf16[128,1152]{1,0:T(8,128)(2,1)}, bf16[128,1152]{1,0:T(8,128)(2,1)S(1)}, u32[]{:S(2)}, u32[]{:S(2)}) collective-permute-start(bf16[128,1152]{1,0:T(8,128)(2,1)} %refs_6_.7), channel_id=1, source_target_pairs={{0,16},{8,24},{16,0},{24,8},{1,17},{9,25},{17,1},{25,9},{2,18},{10... | collective-permute-start | bytes 884744 | tf_op jit(solution)/shard_map/ppermute | solution.py:274
  11.1 7.6 %collective-permute-start.2 = (s32[1,128]{1,0:T(1,128)S(1)}, s32[1,128]{1,0:T(1,128)S(1)}, u32[]{:S(2)}, u32[]{:S(2)}) collective-permute-start(s32[1,128]{1,0:T(1,128)S(1)} %bitcast.2), channel_id=1, source_target_pairs={{0,2},{1,3},{2,0},{3,1},{4,6},{5,7},{6,4},{7,5},{8,10},{9,11},{10,... | collective-permute-start | bytes 1544 | tf_op jit(solution)/shard_map/ppermute | solution.py:274
  18.9 4.5 %collective-permute-start.7 = (bf16[792,1152]{1,0:T(8,128)(2,1)S(1)}, bf16[792,1152]{1,0:T(8,128)(2,1)S(1)}, u32[]{:S(2)}, u32[]{:S(2)}) collective-permute-start(bf16[792,1152]{1,0:T(8,128)(2,1)S(1)} %bundled.3), channel_id=1, source_target_pairs={{0,1},{1,0},{2,3},{3,2},{4,5},{5,4},{6,7},{7,6},{8,9},{9,8},{10,11... | collective-permute-start | bytes 5474312 | tf_op jit(solution)/shard_map/ppermute | solution.py:274
  19.0 10.7 %collective-permute-start.6 = (bf16[136,1152]{1,0:T(8,128)(2,1)S(1)}, bf16[136,1152]{1,0:T(8,128)(2,1)S(1)}, u32[]{:S(2)}, u32[]{:S(2)}) collective-permute-start(bf16[136,1152]{1,0:T(8,128)(2,1)S(1)} %labelled.2.refs_1_.refs_3_.refs_5_), channel_id=1, source_target_pairs={{0,8},{8,0},{16,24},{24,16},{1,9},{9,1},{17,25},{25,17},{2,10},{10... | collective-permute-start | bytes 940040 | tf_op jit(solution)/shard_map/ppermute | solution.py:274
  20.6 9.1 %collective-permute-start.5 = (bf16[128,1152]{1,0:T(8,128)(2,1)S(1)}, bf16[128,1152]{1,0:T(8,128)(2,1)S(1)}, u32[]{:S(2)}, u32[]{:S(2)}) collective-permute-start(bf16[128,1152]{1,0:T(8,128)(2,1)S(1)} %held.3.refs_2_.refs_0_.refs_5_), channel_id=1, source_target_pairs={{0,16},{8,24},{16,0},{24,8},{1,17},{9,25},{17,1},{25,9},{2,18},{10... | collective-permute-start | bytes 884744 | tf_op jit(solution)/shard_map/ppermute | solution.py:274
  29.7 1.9 %collective-permute-start.9 = (bf16[136,1152]{1,0:T(8,128)(2,1)S(1)}, bf16[136,1152]{1,0:T(8,128)(2,1)S(1)}, u32[]{:S(2)}, u32[]{:S(2)}) collective-permute-start(bf16[136,1152]{1,0:T(8,128)(2,1)S(1)} %collective-permute-done.6.refs_3_.refs_8_), channel_id=1, source_target_pairs={{0,1},{1,0},{2,3},{3,2},{4,5},{5,4},{6,7},{7,6},{8,9},{9,8},{10,11... | collective-permute-start | bytes 940040 | tf_op jit(solution)/shard_map/ppermute | solution.py:274
  29.7 5.4 %collective-permute-start.8 = (bf16[128,1152]{1,0:T(8,128)(2,1)S(1)}, bf16[128,1152]{1,0:T(8,128)(2,1)S(1)}, u32[]{:S(2)}, u32[]{:S(2)}) collective-permute-start(bf16[128,1152]{1,0:T(8,128)(2,1)S(1)} %collective-permute-done.5.refs_2_.refs_8_), channel_id=1, source_target_pairs={{0,1},{1,0},{2,3},{3,2},{4,5},{5,4},{6,7},{7,6},{8,9},{9,8},{10,11... | collective-permute-start | bytes 884744 | tf_op jit(solution)/shard_map/ppermute | solution.py:274
  32.2 6.9 %collective-permute-start.12 = (s16[136,640]{1,0:T(8,128)(2,1)S(1)}, s16[136,640]{1,0:T(8,128)(2,1)S(1)}, u32[]{:S(2)}, u32[]{:S(2)}) collective-permute-start(s16[136,640]{1,0:T(8,128)(2,1)S(1)} %get-tuple-element.50.refs_8_), channel_id=1, source_target_pairs={{0,16},{8,24},{16,0},{24,8},{1,17},{9,25},{17,1},{25,9},{2,18},{10... | collective-permute-start | bytes 522248 | tf_op jit(solution)/shard_map/ppermute | solution.py:274
  35.7 6.1 %collective-permute-start.10 = (s16[136,640]{1,0:T(8,128)(2,1)S(1)}, s16[136,640]{1,0:T(8,128)(2,1)S(1)}, u32[]{:S(2)}, u32[]{:S(2)}) collective-permute-start(s16[136,640]{1,0:T(8,128)(2,1)S(1)} %get-tuple-element.52.refs_13_), channel_id=1, source_target_pairs={{0,8},{8,0},{16,24},{24,16},{1,9},{9,1},{17,25},{25,17},{2,10},{10... | collective-permute-start | bytes 522248 | tf_op jit(solution)/shard_map/ppermute | solution.py:274
  39.2 10.6 %collective-permute-start.13 = (s16[136,640]{1,0:T(8,128)(2,1)S(1)}, s16[136,640]{1,0:T(8,128)(2,1)S(1)}, u32[]{:S(2)}, u32[]{:S(2)}) collective-permute-start(s16[136,640]{1,0:T(8,128)(2,1)S(1)} %get-tuple-element.60), channel_id=1, source_target_pairs={{0,4},{1,5},{2,6},{3,7},{4,0},{5,1},{6,2},{7,3},{8,12},{9,13},{10,... | collective-permute-start | bytes 522248 | tf_op jit(solution)/shard_map/ppermute | solution.py:274
  40.6 5.9 %collective-permute-start.14 = (s16[136,512]{1,0:T(8,128)(2,1)S(1)}, s16[136,512]{1,0:T(8,128)(2,1)S(1)}, u32[]{:S(2)}, u32[]{:S(2)}) collective-permute-start(s16[136,512]{1,0:T(8,128)(2,1)S(1)} %get-tuple-element.61), channel_id=1, source_target_pairs={{0,16},{8,24},{16,0},{24,8},{1,17},{9,25},{17,1},{25,9},{2,18},{10... | collective-permute-start | bytes 417800 | tf_op jit(solution)/shard_map/ppermute | solution.py:274
  41.9 8.7 %collective-permute-start.16 = (s16[136,640]{1,0:T(8,128)(2,1)S(1)}, s16[136,640]{1,0:T(8,128)(2,1)S(1)}, u32[]{:S(2)}, u32[]{:S(2)}) collective-permute-start(s16[136,640]{1,0:T(8,128)(2,1)S(1)} %get-tuple-element.64), channel_id=1, source_target_pairs={{0,2},{1,3},{2,0},{3,1},{4,6},{5,7},{6,4},{7,5},{8,10},{9,11},{10,... | collective-permute-start | bytes 522248 | tf_op jit(solution)/shard_map/ppermute | solution.py:274
  44.1 6.5 %collective-permute-start.17 = (s16[136,512]{1,0:T(8,128)(2,1)S(1)}, s16[136,512]{1,0:T(8,128)(2,1)S(1)}, u32[]{:S(2)}, u32[]{:S(2)}) collective-permute-start(s16[136,512]{1,0:T(8,128)(2,1)S(1)} %get-tuple-element.65), channel_id=1, source_target_pairs={{0,8},{8,0},{16,24},{24,16},{1,9},{9,1},{17,25},{25,17},{2,10},{10... | collective-permute-start | bytes 417800 | tf_op jit(solution)/shard_map/ppermute | solution.py:274
  45.0 13.7 %collective-permute-start.19 = (s16[136,1152]{1,0:T(8,128)(2,1)S(1)}, s16[136,1152]{1,0:T(8,128)(2,1)S(1)}, u32[]{:S(2)}, u32[]{:S(2)}) collective-permute-start(s16[136,1152]{1,0:T(8,128)(2,1)S(1)} %get-tuple-element.69), channel_id=1, source_target_pairs={{0,16},{8,24},{16,0},{24,8},{1,17},{9,25},{17,1},{25,9},{2,18},{10... | collective-permute-start | bytes 940040 | tf_op jit(solution)/shard_map/ppermute | solution.py:274
  46.5 12.2 %collective-permute-start.11 = (s16[136,1152]{1,0:T(8,128)(2,1)S(1)}, s16[136,1152]{1,0:T(8,128)(2,1)S(1)}, u32[]{:S(2)}, u32[]{:S(2)}) collective-permute-start(s16[136,1152]{1,0:T(8,128)(2,1)S(1)} %get-tuple-element.58), channel_id=1, source_target_pairs={{0,8},{8,0},{16,24},{24,16},{1,9},{9,1},{17,25},{25,17},{2,10},{10... | collective-permute-start | bytes 940040 | tf_op jit(solution)/shard_map/ppermute | solution.py:274
  49.8 8.6 %collective-permute-start.15 = (s16[136,512]{1,0:T(8,128)(2,1)S(1)}, s16[136,512]{1,0:T(8,128)(2,1)S(1)}, u32[]{:S(2)}, u32[]{:S(2)}) collective-permute-start(s16[136,512]{1,0:T(8,128)(2,1)S(1)} %passed_sum.6.refs_3_), channel_id=1, source_target_pairs={{0,4},{1,5},{2,6},{3,7},{4,0},{5,1},{6,2},{7,3},{8,12},{9,13},{10,... | collective-permute-start | bytes 417800 | tf_op jit(solution)/shard_map/ppermute | solution.py:274
  50.7 8.0 %collective-permute-start.18 = (s16[136,512]{1,0:T(8,128)(2,1)S(1)}, s16[136,512]{1,0:T(8,128)(2,1)S(1)}, u32[]{:S(2)}, u32[]{:S(2)}) collective-permute-start(s16[136,512]{1,0:T(8,128)(2,1)S(1)} %passed_sum.7), channel_id=1, source_target_pairs={{0,2},{1,3},{2,0},{3,1},{4,6},{5,7},{6,4},{7,5},{8,10},{9,11},{10,... | collective-permute-start | bytes 417800 | tf_op jit(solution)/shard_map/ppermute | solution.py:274

commit v15 on v14

--- a/solution.py
+++ b/solution.py
@@ -15,7 +15,7 @@
 TILE = 256
 LANES = 128
 BUNDLE_COST = 6 * 10**8
-HELD_COST = 85 * 10**7
+HELD_COST = 3 * 10**8
 SMEM = pl.BlockSpec(memory_space=pltpu.SMEM)
 VMEM = pl.BlockSpec(memory_space=pltpu.VMEM)
 ANY = pl.BlockSpec(memory_space=pl.ANY)
@@ -26,7 +26,7 @@
 
 
 def part_widths(width):
-    first = (width // LANES + 1) // 2 * LANES
+    first = width // (2 * LANES) * LANES
     return (first, width - first)
 
 
@@ -285,6 +285,8 @@
         for m in reversed(range(1 << s)):
             n = m | 1 << s
             first, *begun = passed_sum(kept[n], received[n], 0, waiting + last)
+            if waiting:
+                begun_with = [first]
             for r, c in zip(received[1:], begun):
                 r[0] = r[0] + (sent(c, steps[-1]),)
             received[0] += [(sent(c, steps[-1]),) for c in begun[len(waiting) :]]
@@ -292,7 +294,7 @@
             (second,) = passed_sum(kept[n], received[n], 1, (), [first[0], *after])
             received[m].append((first, sent(second, steps[s])))
             waiting, last, after = [], [], [second]
-    return kept[0], received[0], after
+    return kept[0], received[0], after, begun_with
 
 
 def in_order(arrays, after=(), cost=HELD_COST):
@@ -380,23 +382,25 @@
             blocks[k][m] = whole(a)
             others[k][m] = whole(swapped(a, core))
     after = ()
-    coded, kept = [[None] * half, [None] * half], [None, None]
+    coded = [[None] * half, [None] * half]
     for k in (1, 0):
-        columns = [(0, m) for m in range(count)] + [(1, m) for m in early]
+        columns = both_cores(early)
         jobs, emits = every_pair(late, columns), ["float"] * len(late)
         results = sums("late_rows_begun", k, late, columns, jobs, {}, emits, after)
         begun = {i: s for i, (s,) in enumerate(results)}
-        columns = [(1, m) for m in late]
+        columns = both_cores(late)
         jobs, emits = every_pair(late, columns), ["parts"] * len(late)
         coded[k][1:] = sums("late_rows", k, late, columns, jobs, begun, emits)
         after = coded[k][1]
+    sums_in = [None, None]
+    ordering = ()
     for k in (1, 0):
         columns = both_cores(late)
         jobs, emits = every_pair(early, columns), ["float"] * half + ["whole"]
         *whole_sums, coded[k][0] = sums("late_columns", k, early, columns, jobs, before[k], emits, after)
-        kept[k], after = [s for (s,) in whole_sums], coded[k][0]
-    kept_texts, text_blocks, after = scattered(kept[1], coded[1], steps[1], ())
-    kept_images, image_blocks, _ = scattered(kept[0], coded[0], steps[0], after)
+        kept = [s for (s,) in whole_sums]
+        *sums_in[k], ordering, after = scattered(kept, coded[k], steps[k], ordering)
+    (kept_images, image_blocks), (kept_texts, text_blocks) = sums_in
     ends = ()
     for blocks_in in (text_blocks, image_blocks):
         ends = in_order([part[0] for b in blocks_in if len(b) > 1 for part in b], ends)

time: 60.1 us -> 60.3 us (level)
  starting transfers between devices: 25.1 us -> 26.3 us
  waiting for transfers between devices: 18.9 us -> 17.7 us
    ppermute x20, starting transfers between devices: 25.1 us -> 26.3 us  [swapped(): lax.ppermute(array, axis, [(i, i ^ bit) for i in range(lax.axis_size(axis...]
    ppermute x20, waiting for transfers between devices: 18.9 us -> 17.7 us  [swapped(): lax.ppermute(array, axis, [(i, i ^ bit) for i in range(lax.axis_size(axis...]
  transfers between devices with their start and end apart: 20 -> 20, of which waited for: 8 -> 7; matrix products, arithmetic and copies ran while one was open for 0% -> 0% of each run, Pallas kernels for 18% -> 18%
where the time goes in v15:
time: 60.3 us; the launch traced here: 60.2 us
  starting transfers between devices  26.3 us (44%)
  waiting for transfers between devices  17.7 us (29%)
  Pallas kernels  12.4 us (21%)
  between operations  2.13 us (4%)
  local copies, waits for them, and re-layouts  1.66 us (3%)
    ppermute x20, starting transfers between devices, swapped(): lax.ppermute(array, axis, [(i, i ^ bit) for i in range(lax.axis_size(axis...  26.3 us
    ppermute x20, waiting for transfers between devices, swapped(): lax.ppermute(array, axis, [(i, i ^ bit) for i in range(lax.axis_size(axis...  17.7 us
    pallas_call x20, Pallas kernels, call(): pl.pallas_call(body, out_shape=[*out_shape, *(jax.ShapeDtypeStruct(a.shap...  12.4 us
    unnamed x6, local copies, waits for them, and re-layouts  1.66 us
  transfers between devices with their start and end apart: 20, of which 7 were waited for; matrix products, arithmetic and copies ran while one was open for 0% of the time, Pallas kernels for 18%

profile of v15, /device:TPU:0, one launch (start us, length us, event | category | flops | bytes accessed | tf_op | source)
XLA Modules:
  0.0 60.2 jit_solution(9886259133466589902)
XLA Ops:
  0.6 4.1 %collective-permute-start = (bf16[128,1152]{1,0:T(8,128)(2,1)}, bf16[128,1152]{1,0:T(8,128)(2,1)S(1)}, u32[]{:S(2)}, u32[]{:S(2)}) collective-permute-start(bf16[128,1152]{1,0:T(8,128)(2,1)} %refs_6_.7), channel_id=1, source_target_pairs={{0,4},{1,5},{2,6},{3,7},{4,0},{5,1},{6,2},{7,3},{8,12},{9,13},{10,... | collective-permute-start | bytes 884744 | tf_op jit(solution)/shard_map/ppermute | solution.py:274
  4.7 1.6 %collective-permute-start.1 = (bf16[128,1152]{1,0:T(8,128)(2,1)}, bf16[128,1152]{1,0:T(8,128)(2,1)S(1)}, u32[]{:S(2)}, u32[]{:S(2)}) collective-permute-start(bf16[128,1152]{1,0:T(8,128)(2,1)} %refs_0_.10), channel_id=1, source_target_pairs={{0,2},{1,3},{2,0},{3,1},{4,6},{5,7},{6,4},{7,5},{8,10},{9,11},{10,... | collective-permute-start | bytes 884744 | tf_op jit(solution)/shard_map/ppermute | solution.py:274
  6.3 0.0 copy-start.1
  6.3 1.0 %copy-done.1 = bf16[128,1152]{1,0:T(8,128)(2,1)S(1)} copy-done((bf16[128,1152]{1,0:T(8,128)(2,1)S(1)}, bf16[128,1152]{1,0:T(8,128)(2,1)}, u32[]{:S(2)}) %copy-start.1) | copy-done | bytes 294936
  7.3 0.0 copy-start.2
  7.3 0.7 %copy-done.2 = s32[128]{0:T(128)S(1)} copy-done((s32[128]{0:T(128)S(1)}, s32[128]{0:T(128)}, u32[]{:S(2)}) %copy-start.2) | copy-done | bytes 536
  8.0 0.0 copy-start
  8.0 1.6 %collective-permute-start.4 = (bf16[136,1152]{1,0:T(8,128)(2,1)S(1)}, bf16[136,1152]{1,0:T(8,128)(2,1)S(1)}, u32[]{:S(2)}, u32[]{:S(2)}) collective-permute-start(bf16[136,1152]{1,0:T(8,128)(2,1)S(1)} %labelled.3.refs_2_.refs_7_.refs_4_), channel_id=1, source_target_pairs={{0,8},{8,0},{16,24},{24,16},{1,9},{9,1},{17,25},{25,17},{2,10},{10... | collective-permute-start | bytes 940040 | tf_op jit(solution)/shard_map/ppermute | solution.py:274
  9.6 1.5 %collective-permute-start.3 = (bf16[128,1152]{1,0:T(8,128)(2,1)}, bf16[128,1152]{1,0:T(8,128)(2,1)S(1)}, u32[]{:S(2)}, u32[]{:S(2)}) collective-permute-start(bf16[128,1152]{1,0:T(8,128)(2,1)} %refs_6_.7), channel_id=1, source_target_pairs={{0,16},{8,24},{16,0},{24,8},{1,17},{9,25},{17,1},{25,9},{2,18},{10... | collective-permute-start | bytes 884744 | tf_op jit(solution)/shard_map/ppermute | solution.py:274
  11.1 0.4 collective-permute-start.2
  11.5 6.8 %collective-permute-done.refs_0_ = bf16[128,1152]{1,0:T(8,128)(2,1)S(1)} collective-permute-done((bf16[128,1152]{1,0:T(8,128)(2,1)}, bf16[128,1152]{1,0:T(8,128)(2,1)S(1)}, u32[]{:S(2)}, u32[]{:S(2)}) %collective-permute-start) | collective-permute-done | bytes 294944 | tf_op jit(solution)/shard_map/ppermute | solution.py:274
  18.4 0.3 collective-permute-done.2.refs_1_
  18.6 0.0 collective-permute-done.1.refs_0_
  18.7 0.0 collective-permute-done.3.refs_3_.refs_4_.refs_6_
  18.7 0.0 collective-permute-done.4.refs_4_.refs_5_.refs_6_
  18.7 0.0 copy-done
  18.8 0.1 bundled.3
  18.9 0.1 collective-permute-start.7
  19.0 1.6 %collective-permute-start.6 = (bf16[136,1152]{1,0:T(8,128)(2,1)S(1)}, bf16[136,1152]{1,0:T(8,128)(2,1)S(1)}, u32[]{:S(2)}, u32[]{:S(2)}) collective-permute-start(bf16[136,1152]{1,0:T(8,128)(2,1)S(1)} %labelled.2.refs_1_.refs_3_.refs_5_), channel_id=1, source_target_pairs={{0,8},{8,0},{16,24},{24,16},{1,9},{9,1},{17,25},{25,17},{2,10},{10... | collective-permute-start | bytes 940040 | tf_op jit(solution)/shard_map/ppermute | solution.py:274
  20.6 1.5 %collective-permute-start.5 = (bf16[128,1152]{1,0:T(8,128)(2,1)S(1)}, bf16[128,1152]{1,0:T(8,128)(2,1)S(1)}, u32[]{:S(2)}, u32[]{:S(2)}) collective-permute-start(bf16[128,1152]{1,0:T(8,128)(2,1)S(1)} %held.3.refs_2_.refs_0_.refs_5_), channel_id=1, source_target_pairs={{0,16},{8,24},{16,0},{24,8},{1,17},{9,25},{17,1},{25,9},{2,18},{10... | collective-permute-start | bytes 884744 | tf_op jit(solution)/shard_map/ppermute | solution.py:274
  23.4 0.0 collective-permute-done.7.refs_8_.refs_7_
  23.4 1.9 %early_sums.3 = (f32[128,1152]{1,0:T(8,128)S(1)}, f32[128,1152]{1,0:T(8,128)S(1)}, f32[128,1152]{1,0:T(8,128)S(1)}) custom-call(f32[1]{0:T(128)S(6)} %copy.25.refs_0_, f32[1]{0:T(128)S(6)} %copy.26.refs_1_, bf16[128,1152]{1,0:T(8,128)(2,1)S(1)} %held.3.refs_2_.refs_0_.refs_5_, bf16[136,1152]{1,0:T(8,128)(2,1)S(1)} %labelled.2.refs_1_.refs_3_.refs_5_, ...), custom_call_target="tpu_custom_call" | custom-call | flops 2304 | bytes 2304 | tf_op jit(solution)/shard_map/early_sums/pallas_call | solution.py:93
  25.3 1.9 %early_sums.2 = (f32[128,1152]{1,0:T(8,128)S(1)}, f32[128,1152]{1,0:T(8,128)S(1)}, f32[128,1152]{1,0:T(8,128)S(1)}) custom-call(f32[1]{0:T(128)S(6)} %copy.25.refs_0_, f32[1]{0:T(128)S(6)} %copy.26.refs_1_, bf16[128,1152]{1,0:T(8,128)(2,1)S(1)} %held.3.refs_2_.refs_0_.refs_5_, bf16[136,1152]{1,0:T(8,128)(2,1)S(1)} %labelled.2.refs_1_.refs_3_.refs_5_, ...), custom_call_target="tpu_custom_call" | custom-call | flops 2304 | bytes 2304 | tf_op jit(solution)/shard_map/early_sums/pallas_call | solution.py:93
  27.3 2.4 %collective-permute-done.5.refs_2_.refs_8_ = bf16[128,1152]{1,0:T(8,128)(2,1)S(1)} collective-permute-done((bf16[128,1152]{1,0:T(8,128)(2,1)S(1)}, bf16[128,1152]{1,0:T(8,128)(2,1)S(1)}, u32[]{:S(2)}, u32[]{:S(2)}) %collective-permute-start.5) | collective-permute-done | bytes 294944 | tf_op jit(solution)/shard_map/ppermute | solution.py:274
  29.7 0.0 collective-permute-done.6.refs_3_.refs_8_
  29.7 0.0 collective-permute-start.9
  29.7 0.5 collective-permute-start.8
  30.2 1.3 %late_rows_begun.2.refs_5_ = f32[128,1152]{1,0:T(8,128)S(1)} custom-call(f32[1]{0:T(128)S(6)} %copy.25.refs_0_, f32[1]{0:T(128)S(6)} %copy.26.refs_1_, bf16[128,1152]{1,0:T(8,128)(2,1)S(1)} %collective-permute-done.5.refs_2_.refs_8_, bf16[136,1152]{1,0:T(8,128)(2,1)S(1)} %collective-permute-done.6.refs_3_.refs_8_, ...), custom_call_target="tpu_custom_call" | custom-call | flops 768 | bytes 768 | tf_op jit(solution)/shard_map/late_rows_begun/pallas_call | solution.py:93
  31.5 0.0 collective-permute-done.9.refs_4_.refs_9_
  31.5 0.7 %late_rows.2 = (s16[136,512]{1,0:T(8,128)(2,1)S(1)}, s16[136,640]{1,0:T(8,128)(2,1)S(1)}) custom-call(f32[1]{0:T(128)S(6)} %copy.25.refs_0_, f32[1]{0:T(128)S(6)} %copy.26.refs_1_, bf16[128,1152]{1,0:T(8,128)(2,1)S(1)} %collective-permute-done.5.refs_2_.refs_8_, bf16[136,1152]{1,0:T(8,128)(2,1)S(1)} %collective-permute-done.6.refs_3_.refs_8_, ...), custom_call_target="tpu_custom_call" | custom-call | flops 256 | bytes 256 | tf_op jit(solution)/shard_map/late_rows/pallas_call | solution.py:93
  32.3 1.6 %collective-permute-start.10 = (s16[136,512]{1,0:T(8,128)(2,1)S(1)}, s16[136,512]{1,0:T(8,128)(2,1)S(1)}, u32[]{:S(2)}, u32[]{:S(2)}) collective-permute-start(s16[136,512]{1,0:T(8,128)(2,1)S(1)} %get-tuple-element.50.refs_8_), channel_id=1, source_target_pairs={{0,16},{8,24},{16,0},{24,8},{1,17},{9,25},{17,1},{25,9},{2,18},{10... | collective-permute-start | bytes 417800 | tf_op jit(solution)/shard_map/ppermute | solution.py:274
  33.8 1.3 %late_rows_begun.3.refs_5_ = f32[128,1152]{1,0:T(8,128)S(1)} custom-call(f32[1]{0:T(128)S(6)} %copy.25.refs_0_, f32[1]{0:T(128)S(6)} %copy.26.refs_1_, bf16[128,1152]{1,0:T(8,128)(2,1)S(1)} %collective-permute-done.5.refs_2_.refs_8_, bf16[136,1152]{1,0:T(8,128)(2,1)S(1)} %collective-permute-done.6.refs_3_.refs_8_, bf16[128,1152]{1,0:T(8,128)(2,1)S(1)} %copy-done, ...), custom_call_target="tpu_custom_call" | custom-call | flops 768 | bytes 768 | tf_op jit(solution)/shard_map/late_rows_begun/pallas_call | solution.py:93
  35.2 0.0 collective-permute-done.8.refs_4_.refs_9_
  35.2 0.7 %late_rows.3 = (s16[136,512]{1,0:T(8,128)(2,1)S(1)}, s16[136,640]{1,0:T(8,128)(2,1)S(1)}) custom-call(f32[1]{0:T(128)S(6)} %copy.25.refs_0_, f32[1]{0:T(128)S(6)} %copy.26.refs_1_, bf16[128,1152]{1,0:T(8,128)(2,1)S(1)} %collective-permute-done.5.refs_2_.refs_8_, bf16[136,1152]{1,0:T(8,128)(2,1)S(1)} %collective-permute-done.6.refs_3_.refs_8_, ...), custom_call_target="tpu_custom_call" | custom-call | flops 256 | bytes 256 | tf_op jit(solution)/shard_map/late_rows/pallas_call | solution.py:93
  35.9 0.7 %collective-permute-start.11 = (s16[136,512]{1,0:T(8,128)(2,1)S(1)}, s16[136,512]{1,0:T(8,128)(2,1)S(1)}, u32[]{:S(2)}, u32[]{:S(2)}) collective-permute-start(s16[136,512]{1,0:T(8,128)(2,1)S(1)} %get-tuple-element.52.refs_13_), channel_id=1, source_target_pairs={{0,8},{8,0},{16,24},{24,16},{1,9},{9,1},{17,25},{25,17},{2,10},{10... | collective-permute-start | bytes 417800 | tf_op jit(solution)/shard_map/ppermute | solution.py:274
  36.7 1.3 %late_columns.2 = (f32[128,1152]{1,0:T(8,128)S(1)}, f32[128,1152]{1,0:T(8,128)S(1)}, s16[136,1152]{1,0:T(8,128)(2,1)S(1)}) custom-call(f32[1]{0:T(128)S(6)} %copy.25.refs_0_, f32[1]{0:T(128)S(6)} %copy.26.refs_1_, bf16[128,1152]{1,0:T(8,128)(2,1)S(1)} %held.3.refs_2_.refs_0_.refs_5_, bf16[136,1152]{1,0:T(8,128)(2,1)S(1)} %labelled.2.refs_1_.refs_3_.refs_5_, ...), custom_call_target="tpu_custom_call" | custom-call | flops 768 | bytes 768 | tf_op jit(solution)/shard_map/late_columns/pallas_call | solution.py:93
  38.0 0.0 collective-permute-done.10.refs_1_
  38.0 0.1 passed_sum.4
  38.1 1.4 %collective-permute-start.13 = (s16[136,512]{1,0:T(8,128)(2,1)S(1)}, s16[136,512]{1,0:T(8,128)(2,1)S(1)}, u32[]{:S(2)}, u32[]{:S(2)}) collective-permute-start(s16[136,512]{1,0:T(8,128)(2,1)S(1)} %get-tuple-element.56.refs_13_), channel_id=1, source_target_pairs={{0,4},{1,5},{2,6},{3,7},{4,0},{5,1},{6,2},{7,3},{8,12},{9,13},{10,... | collective-permute-start | bytes 417800 | tf_op jit(solution)/shard_map/ppermute | solution.py:274
  39.5 1.5 %collective-permute-start.14 = (s16[136,640]{1,0:T(8,128)(2,1)S(1)}, s16[136,640]{1,0:T(8,128)(2,1)S(1)}, u32[]{:S(2)}, u32[]{:S(2)}) collective-permute-start(s16[136,640]{1,0:T(8,128)(2,1)S(1)} %get-tuple-element.61), channel_id=1, source_target_pairs={{0,16},{8,24},{16,0},{24,8},{1,17},{9,25},{17,1},{25,9},{2,18},{10... | collective-permute-start | bytes 522248 | tf_op jit(solution)/shard_map/ppermute | solution.py:274
  40.9 1.3 %late_columns.3 = (f32[128,1152]{1,0:T(8,128)S(1)}, f32[128,1152]{1,0:T(8,128)S(1)}, s16[136,1152]{1,0:T(8,128)(2,1)S(1)}) custom-call(f32[1]{0:T(128)S(6)} %copy.25.refs_0_, f32[1]{0:T(128)S(6)} %copy.26.refs_1_, bf16[128,1152]{1,0:T(8,128)(2,1)S(1)} %held.3.refs_2_.refs_0_.refs_5_, bf16[136,1152]{1,0:T(8,128)(2,1)S(1)} %labelled.2.refs_1_.refs_3_.refs_5_, ...), custom_call_target="tpu_custom_call" | custom-call | flops 768 | bytes 768 | tf_op jit(solution)/shard_map/late_columns/pallas_call | solution.py:93
  42.2 0.0 collective-permute-done.11.refs_1_
  42.2 0.1 passed_sum.5
  42.3 0.7 %collective-permute-start.17 = (s16[136,640]{1,0:T(8,128)(2,1)S(1)}, s16[136,640]{1,0:T(8,128)(2,1)S(1)}, u32[]{:S(2)}, u32[]{:S(2)}) collective-permute-start(s16[136,640]{1,0:T(8,128)(2,1)S(1)} %get-tuple-element.65), channel_id=1, source_target_pairs={{0,8},{8,0},{16,24},{24,16},{1,9},{9,1},{17,25},{25,17},{2,10},{10... | collective-permute-start | bytes 522248 | tf_op jit(solution)/shard_map/ppermute | solution.py:274
  43.1 2.4 %collective-permute-start.16 = (s16[136,512]{1,0:T(8,128)(2,1)S(1)}, s16[136,512]{1,0:T(8,128)(2,1)S(1)}, u32[]{:S(2)}, u32[]{:S(2)}) collective-permute-start(s16[136,512]{1,0:T(8,128)(2,1)S(1)} %get-tuple-element.64), channel_id=1, source_target_pairs={{0,2},{1,3},{2,0},{3,1},{4,6},{5,7},{6,4},{7,5},{8,10},{9,11},{10,... | collective-permute-start | bytes 417800 | tf_op jit(solution)/shard_map/ppermute | solution.py:274
  45.4 1.4 %collective-permute-start.12 = (s16[136,1152]{1,0:T(8,128)(2,1)S(1)}, s16[136,1152]{1,0:T(8,128)(2,1)S(1)}, u32[]{:S(2)}, u32[]{:S(2)}) collective-permute-start(s16[136,1152]{1,0:T(8,128)(2,1)S(1)} %get-tuple-element.60), channel_id=1, source_target_pairs={{0,8},{8,0},{16,24},{24,16},{1,9},{9,1},{17,25},{25,17},{2,10},{10... | collective-permute-start | bytes 940040 | tf_op jit(solution)/shard_map/ppermute | solution.py:274
  46.8 0.4 collective-permute-done.13.refs_2_.refs_0_
  47.1 1.2 %collective-permute-start.19 = (s16[136,1152]{1,0:T(8,128)(2,1)S(1)}, s16[136,1152]{1,0:T(8,128)(2,1)S(1)}, u32[]{:S(2)}, u32[]{:S(2)}) collective-permute-start(s16[136,1152]{1,0:T(8,128)(2,1)S(1)} %get-tuple-element.69), channel_id=1, source_target_pairs={{0,16},{8,24},{16,0},{24,8},{1,17},{9,25},{17,1},{25,9},{2,18},{10... | collective-permute-start | bytes 940040 | tf_op jit(solution)/shard_map/ppermute | solution.py:274
  48.3 0.0 collective-permute-done.14.refs_1_
  48.3 0.1 passed_sum.6.refs_3_
  48.4 0.1 collective-permute-start.15
  48.5 1.1 %collective-permute-done.16.refs_2_ = s16[136,512]{1,0:T(8,128)(2,1)S(1)} collective-permute-done((s16[136,512]{1,0:T(8,128)(2,1)S(1)}, s16[136,512]{1,0:T(8,128)(2,1)S(1)}, u32[]{:S(2)}, u32[]{:S(2)}) %collective-permute-start.16) | collective-permute-done | bytes 139296 | tf_op jit(solution)/shard_map/ppermute | solution.py:274
  49.6 0.0 collective-permute-done.17.refs_1_
  49.6 0.1 passed_sum.7
  49.7 2.6 %collective-permute-start.18 = (s16[136,640]{1,0:T(8,128)(2,1)S(1)}, s16[136,640]{1,0:T(8,128)(2,1)S(1)}, u32[]{:S(2)}, u32[]{:S(2)}) collective-permute-start(s16[136,640]{1,0:T(8,128)(2,1)S(1)} %passed_sum.7), channel_id=1, source_target_pairs={{0,2},{1,3},{2,0},{3,1},{4,6},{5,7},{6,4},{7,5},{8,10},{9,11},{10,... | collective-permute-start | bytes 522248 | tf_op jit(solution)/shard_map/ppermute | solution.py:274
  52.3 6.0 %collective-permute-done.15.refs_1_ = s16[136,640]{1,0:T(8,128)(2,1)S(1)} collective-permute-done((s16[136,640]{1,0:T(8,128)(2,1)S(1)}, s16[136,640]{1,0:T(8,128)(2,1)S(1)}, u32[]{:S(2)}, u32[]{:S(2)}) %collective-permute-start.15) | collective-permute-done | bytes 174112 | tf_op jit(solution)/shard_map/ppermute | solution.py:274
  58.3 0.7 %collective-permute-done.18.refs_3_ = s16[136,640]{1,0:T(8,128)(2,1)S(1)} collective-permute-done((s16[136,640]{1,0:T(8,128)(2,1)S(1)}, s16[136,640]{1,0:T(8,128)(2,1)S(1)}, u32[]{:S(2)}, u32[]{:S(2)}) %collective-permute-start.18) | collective-permute-done | bytes 174112 | tf_op jit(solution)/shard_map/ppermute | solution.py:274
  58.9 0.0 collective-permute-done.12.refs_2_
  59.0 0.0 collective-permute-done.19.refs_6_
  59.0 1.2 %output_sums.1 = (f32[128,1152]{1,0:T(8,128)}, f32[128,1152]{1,0:T(8,128)}) custom-call(f32[1]{0:T(128)S(6)} %copy.25.refs_0_, f32[128,1152]{1,0:T(8,128)S(1)} %get-tuple-element.57.refs_1_, s16[136,1152]{1,0:T(8,128)(2,1)S(1)} %collective-permute-done.12.refs_2_, s16[136,512]{1,0:T(8,128)(2,1)S(1)} %get-tuple-element.66.refs_3_, ...), custom_call_target="tpu_custom_call" | custom-call | flops 128 | bytes 128 | tf_op jit(solution)/shard_map/output_sums/pallas_call | solution.py:93
  (6 shorter events, 0.1 us)
Async XLA Ops:
  0.6 17.8 %collective-permute-start = (bf16[128,1152]{1,0:T(8,128)(2,1)}, bf16[128,1152]{1,0:T(8,128)(2,1)S(1)}, u32[]{:S(2)}, u32[]{:S(2)}) collective-permute-start(bf16[128,1152]{1,0:T(8,128)(2,1)} %refs_6_.7), channel_id=1, source_target_pairs={{0,4},{1,5},{2,6},{3,7},{4,0},{5,1},{6,2},{7,3},{8,12},{9,13},{10,... | collective-permute-start | bytes 884744 | tf_op jit(solution)/shard_map/ppermute | solution.py:274
  4.7 13.9 %collective-permute-start.1 = (bf16[128,1152]{1,0:T(8,128)(2,1)}, bf16[128,1152]{1,0:T(8,128)(2,1)S(1)}, u32[]{:S(2)}, u32[]{:S(2)}) collective-permute-start(bf16[128,1152]{1,0:T(8,128)(2,1)} %refs_0_.10), channel_id=1, source_target_pairs={{0,2},{1,3},{2,0},{3,1},{4,6},{5,7},{6,4},{7,5},{8,10},{9,11},{10,... | collective-permute-start | bytes 884744 | tf_op jit(solution)/shard_map/ppermute | solution.py:274
  6.3 1.0 %copy-start.1 = (bf16[128,1152]{1,0:T(8,128)(2,1)S(1)}, bf16[128,1152]{1,0:T(8,128)(2,1)}, u32[]{:S(2)}) copy-start(bf16[128,1152]{1,0:T(8,128)(2,1)} %refs_0_.10) | copy-start | bytes 884740
  7.3 0.7 %copy-start.2 = (s32[128]{0:T(128)S(1)}, s32[128]{0:T(128)}, u32[]{:S(2)}) copy-start(s32[128]{0:T(128)} %param.7) | copy-start | bytes 1540
  8.0 10.8 %copy-start = (bf16[128,1152]{1,0:T(8,128)(2,1)S(1)}, bf16[128,1152]{1,0:T(8,128)(2,1)}, u32[]{:S(2)}) copy-start(bf16[128,1152]{1,0:T(8,128)(2,1)} %refs_6_.7) | copy-start | bytes 884740
  8.0 10.7 %collective-permute-start.4 = (bf16[136,1152]{1,0:T(8,128)(2,1)S(1)}, bf16[136,1152]{1,0:T(8,128)(2,1)S(1)}, u32[]{:S(2)}, u32[]{:S(2)}) collective-permute-start(bf16[136,1152]{1,0:T(8,128)(2,1)S(1)} %labelled.3.refs_2_.refs_7_.refs_4_), channel_id=1, source_target_pairs={{0,8},{8,0},{16,24},{24,16},{1,9},{9,1},{17,25},{25,17},{2,10},{10... | collective-permute-start | bytes 940040 | tf_op jit(solution)/shard_map/ppermute | solution.py:274
  9.6 9.2 %collective-permute-start.3 = (bf16[128,1152]{1,0:T(8,128)(2,1)}, bf16[128,1152]{1,0:T(8,128)(2,1)S(1)}, u32[]{:S(2)}, u32[]{:S(2)}) collective-permute-start(bf16[128,1152]{1,0:T(8,128)(2,1)} %refs_6_.7), channel_id=1, source_target_pairs={{0,16},{8,24},{16,0},{24,8},{1,17},{9,25},{17,1},{25,9},{2,18},{10... | collective-permute-start | bytes 884744 | tf_op jit(solution)/shard_map/ppermute | solution.py:274
  11.1 7.6 %collective-permute-start.2 = (s32[1,128]{1,0:T(1,128)S(1)}, s32[1,128]{1,0:T(1,128)S(1)}, u32[]{:S(2)}, u32[]{:S(2)}) collective-permute-start(s32[1,128]{1,0:T(1,128)S(1)} %bitcast.2), channel_id=1, source_target_pairs={{0,2},{1,3},{2,0},{3,1},{4,6},{5,7},{6,4},{7,5},{8,10},{9,11},{10,... | collective-permute-start | bytes 1544 | tf_op jit(solution)/shard_map/ppermute | solution.py:274
  18.9 4.5 %collective-permute-start.7 = (bf16[792,1152]{1,0:T(8,128)(2,1)S(1)}, bf16[792,1152]{1,0:T(8,128)(2,1)S(1)}, u32[]{:S(2)}, u32[]{:S(2)}) collective-permute-start(bf16[792,1152]{1,0:T(8,128)(2,1)S(1)} %bundled.3), channel_id=1, source_target_pairs={{0,1},{1,0},{2,3},{3,2},{4,5},{5,4},{6,7},{7,6},{8,9},{9,8},{10,11... | collective-permute-start | bytes 5474312 | tf_op jit(solution)/shard_map/ppermute | solution.py:274
  19.0 10.7 %collective-permute-start.6 = (bf16[136,1152]{1,0:T(8,128)(2,1)S(1)}, bf16[136,1152]{1,0:T(8,128)(2,1)S(1)}, u32[]{:S(2)}, u32[]{:S(2)}) collective-permute-start(bf16[136,1152]{1,0:T(8,128)(2,1)S(1)} %labelled.2.refs_1_.refs_3_.refs_5_), channel_id=1, source_target_pairs={{0,8},{8,0},{16,24},{24,16},{1,9},{9,1},{17,25},{25,17},{2,10},{10... | collective-permute-start | bytes 940040 | tf_op jit(solution)/shard_map/ppermute | solution.py:274
  20.6 9.1 %collective-permute-start.5 = (bf16[128,1152]{1,0:T(8,128)(2,1)S(1)}, bf16[128,1152]{1,0:T(8,128)(2,1)S(1)}, u32[]{:S(2)}, u32[]{:S(2)}) collective-permute-start(bf16[128,1152]{1,0:T(8,128)(2,1)S(1)} %held.3.refs_2_.refs_0_.refs_5_), channel_id=1, source_target_pairs={{0,16},{8,24},{16,0},{24,8},{1,17},{9,25},{17,1},{25,9},{2,18},{10... | collective-permute-start | bytes 884744 | tf_op jit(solution)/shard_map/ppermute | solution.py:274
  29.7 1.8 %collective-permute-start.9 = (bf16[136,1152]{1,0:T(8,128)(2,1)S(1)}, bf16[136,1152]{1,0:T(8,128)(2,1)S(1)}, u32[]{:S(2)}, u32[]{:S(2)}) collective-permute-start(bf16[136,1152]{1,0:T(8,128)(2,1)S(1)} %collective-permute-done.6.refs_3_.refs_8_), channel_id=1, source_target_pairs={{0,1},{1,0},{2,3},{3,2},{4,5},{5,4},{6,7},{7,6},{8,9},{9,8},{10,11... | collective-permute-start | bytes 940040 | tf_op jit(solution)/shard_map/ppermute | solution.py:274
  29.7 5.5 %collective-permute-start.8 = (bf16[128,1152]{1,0:T(8,128)(2,1)S(1)}, bf16[128,1152]{1,0:T(8,128)(2,1)S(1)}, u32[]{:S(2)}, u32[]{:S(2)}) collective-permute-start(bf16[128,1152]{1,0:T(8,128)(2,1)S(1)} %collective-permute-done.5.refs_2_.refs_8_), channel_id=1, source_target_pairs={{0,1},{1,0},{2,3},{3,2},{4,5},{5,4},{6,7},{7,6},{8,9},{9,8},{10,11... | collective-permute-start | bytes 884744 | tf_op jit(solution)/shard_map/ppermute | solution.py:274
  32.3 5.7 %collective-permute-start.10 = (s16[136,512]{1,0:T(8,128)(2,1)S(1)}, s16[136,512]{1,0:T(8,128)(2,1)S(1)}, u32[]{:S(2)}, u32[]{:S(2)}) collective-permute-start(s16[136,512]{1,0:T(8,128)(2,1)S(1)} %get-tuple-element.50.refs_8_), channel_id=1, source_target_pairs={{0,16},{8,24},{16,0},{24,8},{1,17},{9,25},{17,1},{25,9},{2,18},{10... | collective-permute-start | bytes 417800 | tf_op jit(solution)/shard_map/ppermute | solution.py:274
  35.9 6.3 %collective-permute-start.11 = (s16[136,512]{1,0:T(8,128)(2,1)S(1)}, s16[136,512]{1,0:T(8,128)(2,1)S(1)}, u32[]{:S(2)}, u32[]{:S(2)}) collective-permute-start(s16[136,512]{1,0:T(8,128)(2,1)S(1)} %get-tuple-element.52.refs_13_), channel_id=1, source_target_pairs={{0,8},{8,0},{16,24},{24,16},{1,9},{9,1},{17,25},{25,17},{2,10},{10... | collective-permute-start | bytes 417800 | tf_op jit(solution)/shard_map/ppermute | solution.py:274
  38.1 9.1 %collective-permute-start.13 = (s16[136,512]{1,0:T(8,128)(2,1)S(1)}, s16[136,512]{1,0:T(8,128)(2,1)S(1)}, u32[]{:S(2)}, u32[]{:S(2)}) collective-permute-start(s16[136,512]{1,0:T(8,128)(2,1)S(1)} %get-tuple-element.56.refs_13_), channel_id=1, source_target_pairs={{0,4},{1,5},{2,6},{3,7},{4,0},{5,1},{6,2},{7,3},{8,12},{9,13},{10,... | collective-permute-start | bytes 417800 | tf_op jit(solution)/shard_map/ppermute | solution.py:274
  39.5 8.9 %collective-permute-start.14 = (s16[136,640]{1,0:T(8,128)(2,1)S(1)}, s16[136,640]{1,0:T(8,128)(2,1)S(1)}, u32[]{:S(2)}, u32[]{:S(2)}) collective-permute-start(s16[136,640]{1,0:T(8,128)(2,1)S(1)} %get-tuple-element.61), channel_id=1, source_target_pairs={{0,16},{8,24},{16,0},{24,8},{1,17},{9,25},{17,1},{25,9},{2,18},{10... | collective-permute-start | bytes 522248 | tf_op jit(solution)/shard_map/ppermute | solution.py:274
  42.3 7.3 %collective-permute-start.17 = (s16[136,640]{1,0:T(8,128)(2,1)S(1)}, s16[136,640]{1,0:T(8,128)(2,1)S(1)}, u32[]{:S(2)}, u32[]{:S(2)}) collective-permute-start(s16[136,640]{1,0:T(8,128)(2,1)S(1)} %get-tuple-element.65), channel_id=1, source_target_pairs={{0,8},{8,0},{16,24},{24,16},{1,9},{9,1},{17,25},{25,17},{2,10},{10... | collective-permute-start | bytes 522248 | tf_op jit(solution)/shard_map/ppermute | solution.py:274
  43.1 6.5 %collective-permute-start.16 = (s16[136,512]{1,0:T(8,128)(2,1)S(1)}, s16[136,512]{1,0:T(8,128)(2,1)S(1)}, u32[]{:S(2)}, u32[]{:S(2)}) collective-permute-start(s16[136,512]{1,0:T(8,128)(2,1)S(1)} %get-tuple-element.64), channel_id=1, source_target_pairs={{0,2},{1,3},{2,0},{3,1},{4,6},{5,7},{6,4},{7,5},{8,10},{9,11},{10,... | collective-permute-start | bytes 417800 | tf_op jit(solution)/shard_map/ppermute | solution.py:274
  45.4 13.5 %collective-permute-start.12 = (s16[136,1152]{1,0:T(8,128)(2,1)S(1)}, s16[136,1152]{1,0:T(8,128)(2,1)S(1)}, u32[]{:S(2)}, u32[]{:S(2)}) collective-permute-start(s16[136,1152]{1,0:T(8,128)(2,1)S(1)} %get-tuple-element.60), channel_id=1, source_target_pairs={{0,8},{8,0},{16,24},{24,16},{1,9},{9,1},{17,25},{25,17},{2,10},{10... | collective-permute-start | bytes 940040 | tf_op jit(solution)/shard_map/ppermute | solution.py:274
  47.1 11.8 %collective-permute-start.19 = (s16[136,1152]{1,0:T(8,128)(2,1)S(1)}, s16[136,1152]{1,0:T(8,128)(2,1)S(1)}, u32[]{:S(2)}, u32[]{:S(2)}) collective-permute-start(s16[136,1152]{1,0:T(8,128)(2,1)S(1)} %get-tuple-element.69), channel_id=1, source_target_pairs={{0,16},{8,24},{16,0},{24,8},{1,17},{9,25},{17,1},{25,9},{2,18},{10... | collective-permute-start | bytes 940040 | tf_op jit(solution)/shard_map/ppermute | solution.py:274
  48.4 9.8 %collective-permute-start.15 = (s16[136,640]{1,0:T(8,128)(2,1)S(1)}, s16[136,640]{1,0:T(8,128)(2,1)S(1)}, u32[]{:S(2)}, u32[]{:S(2)}) collective-permute-start(s16[136,640]{1,0:T(8,128)(2,1)S(1)} %passed_sum.6.refs_3_), channel_id=1, source_target_pairs={{0,4},{1,5},{2,6},{3,7},{4,0},{5,1},{6,2},{7,3},{8,12},{9,13},{10,... | collective-permute-start | bytes 522248 | tf_op jit(solution)/shard_map/ppermute | solution.py:274
  49.7 9.2 %collective-permute-start.18 = (s16[136,640]{1,0:T(8,128)(2,1)S(1)}, s16[136,640]{1,0:T(8,128)(2,1)S(1)}, u32[]{:S(2)}, u32[]{:S(2)}) collective-permute-start(s16[136,640]{1,0:T(8,128)(2,1)S(1)} %passed_sum.7), channel_id=1, source_target_pairs={{0,2},{1,3},{2,0},{3,1},{4,6},{5,7},{6,4},{7,5},{8,10},{9,11},{10,... | collective-permute-start | bytes 522248 | tf_op jit(solution)/shard_map/ppermute | solution.py:274

commit v16 on v13

--- a/solution.py
+++ b/solution.py
@@ -148,33 +148,32 @@
     return parts[0:1] * LABEL_BASE + parts[1:2]
 
 
-def gradient_sums(name, size, scalars, x_blocks, y_blocks, masks, x_images, jobs, before, emits, sequence, after=()):
-    width = x_blocks[0][0][0].shape[1]
-    x_masks, y_masks = masks
+def core_number():
+    return lax.rem(lax.axis_index("grp"), 2)
+
+
+def gradient_sums(name, size, scalars, variants, emits, after=()):
+    width = variants[0][0][0][0][0].shape[1]
     per_tile = TILE // size
-    widths = part_widths(width)
-    shapes, where = [], {}
-
-    def result(extra, w, dtype):
-        shapes.append(jax.ShapeDtypeStruct((size + extra, w), dtype))
-        return len(shapes) - 1
-
-    for r, kind in enumerate(emits):
-        if kind == "float":
-            where[r] = [(result(0, width, jnp.float32), 0, 0)]
-        else:
-            cut = widths if kind == "parts" else (width,)
-            where[r] = [(result(EXTRA_ROWS, w, jnp.int16), 0, 0) for w in cut]
+    shapes = [
+        jax.ShapeDtypeStruct((size, width), jnp.float32)
+        if kind == "float"
+        else jax.ShapeDtypeStruct((size + EXTRA_ROWS, width), jnp.int16)
+        for kind in emits
+    ]
     operands = Operands()
     slope_at, shift_at = [operands.add(s, SMEM) for s in scalars]
-    for b in sequence:
-        operands.block(b)
-    x_views = [operands.block(b) for b in x_blocks]
-    y_views = [operands.block(b) for b in y_blocks]
-    before_at = {r: operands.add(b, VMEM) for r, b in before.items()}
-
-    def kernel(ins, refs):
-        outs, weights = refs[:-1], refs[-1]
+    views = []
+    for x_blocks, y_blocks, masks, x_images, jobs, before, sequence in variants:
+        for b in sequence:
+            operands.block(b)
+        x_views = [operands.block(b) for b in x_blocks]
+        y_views = [operands.block(b) for b in y_blocks]
+        before_at = {r: operands.add(b, VMEM) for r, b in before.items()}
+        views.append((x_views, y_views, masks, x_images, jobs, before_at))
+
+    def summed(ins, outs, weights, view):
+        x_views, y_views, (x_masks, y_masks), x_images, jobs, before_at = view
         slope, shift = ins[slope_at][0] * LOG2E, ins[shift_at][0] * LOG2E
         x_refs, y_refs = [v(ins) for v in x_views], [v(ins) for v in y_views]
 
@@ -217,36 +216,40 @@
                     block = sums[i * size : (i + 1) * size]
                     if r in before_at:
                         block = block + piece(whole(ins[before_at[r]]), (0, size), tile)[...]
-                    out = tuple((outs[o], row, column) for o, row, column in where[r])
                     if emits[r] == "float":
-                        piece(out, (0, size), tile)[...] = block
+                        piece(whole(outs[r]), (0, size), tile)[...] = block
                     else:
-                        encode(block, out, tile)
-
+                        encode(block, whole(outs[r]), tile)
+
+    def kernel(ins, refs):
+        outs, weights = refs[:-1], refs[-1]
+        if len(views) == 1:
+            summed(ins, outs, weights, views[0])
+            return
+        for core, view in enumerate(views):
+            pl.when(core_number() == core)(lambda view=view: summed(ins, outs, weights, view))
+
+    x_blocks, y_blocks, jobs = variants[0][0], variants[0][1], variants[0][4]
     pairs = sum(len(rows) * len(columns) for rows, columns in jobs)
     scratch = [pltpu.VMEM((len(x_blocks) * size, len(y_blocks) * size), jnp.bfloat16)]
     room = len(x_blocks) * len(y_blocks) * size * size * 2 + 8 * 2**20
-    results = call(kernel, name, operands.pairs, shapes, scratch, room, pairs * size, after)
-    return [tuple(results[o] for o, _, _ in where[r]) for r in range(len(emits))]
-
-
-def passed_sum(kept, received, part, held_back=(), after=()):
+    return call(kernel, name, operands.pairs, shapes, scratch, room, pairs * size, after)
+
+
+def passed_sum(kept, received, held_back=(), after=()):
     size, width = kept.shape
     operands = Operands()
     kept_at = operands.add(kept, VMEM)
-    views = [operands.block(b if part is None or len(b) == 1 else (b[part],) * 2) for b in received]
+    views = [operands.block(b) for b in received]
 
     def kernel(ins, outs):
         for tile in column_tiles(width):
-            p, inner, _, span = tile
-            if part is None or p == part:
-                total = piece(whole(ins[kept_at]), (0, size), tile)[...]
-                for view in views:
-                    total = total + decoded(view(ins), size, tile)
-                encode(total, whole(outs[0]), tile if part is None else (0, 0, inner, span))
-
-    cut = width if part is None else part_widths(width)[part]
-    shape = jax.ShapeDtypeStruct((size + EXTRA_ROWS, cut), jnp.int16)
+            total = piece(whole(ins[kept_at]), (0, size), tile)[...]
+            for view in views:
+                total = total + decoded(view(ins), size, tile)
+            encode(total, whole(outs[0]), tile)
+
+    shape = jax.ShapeDtypeStruct((size + EXTRA_ROWS, width), jnp.int16)
     return call(kernel, "passed_sum", operands.pairs, [shape], [], 2**21, size, after, held_back)
 
 
@@ -256,7 +259,7 @@
     sharpness_at = operands.add(sharpness, SMEM)
     views = [(operands.add(kept, VMEM), [operands.block(b) for b in blocks]) for kept, blocks in sums]
 
-    def kernel(ins, outs):
+    def write(ins, outs):
         for out, (kept_at, received) in zip(outs, views):
             for tile in column_tiles(width):
                 total = piece(whole(ins[kept_at]), (0, size), tile)[...]
@@ -264,6 +267,10 @@
                     total = total + decoded(view(ins), size, tile)
                 piece(whole(out), (0, size), tile)[...] = total * ins[sharpness_at][0]
 
+    def kernel(ins, outs):
+        for core, order in enumerate((outs[::-1], outs)):
+            pl.when(core_number() == core)(lambda order=order: write(ins, order))
+
     shapes = [jax.ShapeDtypeStruct((size, width), jnp.float32)] * len(sums)
     return call(kernel, "output_sums", operands.pairs, shapes, [], 2**21, size)
 
@@ -273,23 +280,31 @@
     return lax.ppermute(array, axis, [(i, i ^ bit) for i in range(lax.axis_size(axis))])
 
 
+def swapped_by_core(array, steps):
+    grp_count = lax.axis_size("grp")
+    route = []
+    for i in range(lax.axis_size("blk") * grp_count):
+        axis, bit = steps[i % 2]
+        route.append((i, i ^ (bit * grp_count if axis == "blk" else bit)))
+    return lax.ppermute(array, ("blk", "grp"), route)
+
+
 def scattered(kept, coded, steps, after):
-    def sent(block, step):
-        return [(swapped(p, step), 0, 0) for p in block]
-
-    half, waiting = len(kept), coded[0]
+    steps = list(zip(*steps))
+
+    def sent(array, step):
+        return whole(swapped_by_core(array, step))
+
+    half, waiting = len(kept), coded[:1]
     received = [[]] + [[sent(c, steps[-1])] for c in coded[1:]]
     for s in reversed(range(len(steps) - 1)):
         for m in reversed(range(1 << s)):
             n = m | 1 << s
-            block = passed_sum(kept[n], received[n], None, waiting, after)
-            after = block[:1]
-            if n == half - 1:
-                block, *waiting = block
-                received[0].append(sent(waiting, steps[-1]))
-                waiting, block = (), [block]
+            block, *held = passed_sum(kept[n], received[n], waiting, after)
+            received[0] += [sent(c, steps[-1]) for c in held]
             received[m].append(sent(block, steps[s]))
-    return (kept[0], received[0][::-1]), after
+            waiting, after = (), [block]
+    return kept[0], received[0][::-1], after
 
 
 def in_order(arrays, after=()):
@@ -337,26 +352,19 @@
         row = i * (2 * size + EXTRA_ROWS)
         others[1][m], others[0][m] = ((both, row, 0),), ((both, row + size, 0),)
 
-    def sums(name, kind, rows, columns, jobs, before, emits, after=()):
-        other = 1 - kind
-        x_blocks = [blocks[kind][m] for m in rows]
-        y_blocks = [(blocks, others)[c][other][m] for c, m in columns]
-        x_masks = [masks[kind][m] for m in rows]
-        y_masks = [masks[other][m + c * count] for c, m in columns]
-        return gradient_sums(
-            name,
-            size,
-            scalars,
-            x_blocks,
-            y_blocks,
-            (x_masks, y_masks),
-            kind == 0,
-            jobs,
-            before,
-            emits,
-            [blocks[k][m] for m in rows[1:] + rows[:1] for k in (1, 0)],
-            after,
-        )
+    def sums(name, kinds, rows, columns, jobs, befores, emits, after=()):
+        variants = []
+        for kind, before in zip(kinds, befores):
+            other = 1 - kind
+            x_blocks = [blocks[kind][m] for m in rows]
+            y_blocks = [(blocks, others)[c][other][m] for c, m in columns]
+            x_masks = [masks[kind][m] for m in rows]
+            y_masks = [masks[other][m + c * count] for c, m in columns]
+            sequence = [blocks[k][m] for m in rows[1:] + rows[:1] for k in (1, 0)]
+            variants.append(
+                (x_blocks, y_blocks, (x_masks, y_masks), kind == 0, jobs, before, sequence)
+            )
+        return gradient_sums(name, size, scalars, variants, emits, after)
 
     def both_cores(chosen):
         return [(c, m) for c in range(2) for m in chosen]
@@ -368,38 +376,39 @@
     for k in range(2):
         columns = both_cores(early)
         jobs, emits = every_pair(early, columns), ["float"] * len(early)
-        results = sums("early_sums", k, early, columns, jobs, {}, emits)
-        before.append({m: s for m, (s,) in zip(early, results)})
+        results = sums("early_sums", [k], early, columns, jobs, [{}], emits)
+        before.append(dict(zip(early, results)))
     arrays = [[b[m][0][0] for m in late] for b in blocks[::-1]]
     arrays, before = lax.optimization_barrier((arrays, before))
     for k in (1, 0):
         for m, a in zip(late, arrays[1 - k]):
             blocks[k][m] = whole(a)
             others[k][m] = whole(swapped(a, core))
-    after = ()
-    coded, kept = [[None] * half, [None] * half], [None, None]
-    for k in (1, 0):
+    turns, after = ((1, 0), (0, 1)), ()
+    coded, kept, received = [[None] * half, [None] * half], [None, None], [None, None]
+    for t, kinds in enumerate(turns):
         columns = [(0, m) for m in range(count)] + [(1, m) for m in early]
         jobs, emits = every_pair(late, columns), ["float"] * len(late)
-        results = sums("late_rows_begun", k, late, columns, jobs, {}, emits, after)
-        begun = {i: s for i, (s,) in enumerate(results)}
+        results = sums("late_rows_begun", kinds, late, columns, jobs, [{}, {}], emits, after)
+        begun = dict(enumerate(results))
         columns = [(1, m) for m in late]
-        jobs, emits = every_pair(late, columns), ["whole"] * len(late)
-        coded[k][1:] = sums("late_rows", k, late, columns, jobs, begun, emits)
-        after = coded[k][1]
-    for k in (1, 0):
+        jobs, emits = every_pair(late, columns), ["codes"] * len(late)
+        coded[t][1:] = sums("late_rows", kinds, late, columns, jobs, [begun, begun], emits)
+        after = coded[t][1:2]
+    for t, kinds in enumerate(turns):
         columns = both_cores(late)
-        jobs, emits = every_pair(early, columns), ["float"] * half + ["whole"]
-        *whole_sums, coded[k][0] = sums("late_columns", k, early, columns, jobs, before[k], emits, after)
-        kept[k], after = [s for (s,) in whole_sums], coded[k][0]
-    texts, after = scattered(kept[1], coded[1], steps[1], ())
-    images, _ = scattered(kept[0], coded[0], steps[0], after)
-    (kept_texts, text_blocks), (kept_images, image_blocks) = texts, images
-    text_parts = in_order([b[0][0] for b in text_blocks[:-1]])
-    image_parts = in_order([b[0][0] for b in image_blocks[:-1]], text_parts)
-    text_blocks = [whole(a) for a in text_parts] + text_blocks[-1:]
-    image_blocks = [whole(a) for a in image_parts] + image_blocks[-1:]
-    return tuple(output_sums(scalars[0], [(kept_images, image_blocks), (kept_texts, text_blocks)]))
+        jobs, emits = every_pair(early, columns), ["float"] * half + ["codes"]
+        *kept[t], coded[t][0] = sums(
+            "late_columns", kinds, early, columns, jobs, [before[k] for k in kinds], emits, after
+        )
+        after = coded[t][:1]
+    after, ends = (), ()
+    for t, kinds in enumerate(turns):
+        kept[t], received[t], after = scattered(kept[t], coded[t], [steps[k] for k in kinds], after)
+    for t in range(2):
+        ends = in_order([b[0][0] for b in received[t][:-1]], ends)
+        received[t] = [whole(a) for a in ends] + received[t][-1:]
+    return tuple(output_sums(scalars[0], list(zip(kept, received))))
 
 
 def solution(mesh):

time: 60.3 us -> 60.1 us (level)
  waiting for transfers between devices: 24.7 us -> 23.1 us
  starting transfers between devices: 19.6 us -> 20.3 us
    ppermute x16 -> x10, waiting for transfers between devices: 24.7 us -> 9.68 us  [swapped(): lax.ppermute(array, axis, [(i, i ^ bit) for i in range(lax.axis_size(axis...]
    ppermute x0 -> x6, waiting for transfers between devices: none -> 13.4 us  [swapped_by_core(): return lax.ppermute(array, ('blk', 'grp'), route)]
    ppermute x0 -> x6, starting transfers between devices: none -> 7.39 us  [swapped_by_core(): return lax.ppermute(array, ('blk', 'grp'), route)]
    ppermute x16 -> x10, starting transfers between devices: 19.6 us -> 12.9 us  [swapped(): lax.ppermute(array, axis, [(i, i ^ bit) for i in range(lax.axis_size(axis...]
  transfers between devices with their start and end apart: 16 -> 16, of which waited for: 7 -> 7; matrix products, arithmetic and copies ran while one was open for 0% -> 0% of each run, Pallas kernels for 18% -> 17%
where the time goes in v16:
time: 60.1 us; the launch traced here: 59.8 us
  waiting for transfers between devices  23.1 us (38%)
  starting transfers between devices  20.3 us (34%)
  Pallas kernels  12.6 us (21%)
  between operations  2.09 us (3%)
  local copies, waits for them, and re-layouts  1.66 us (3%)
    ppermute x6, waiting for transfers between devices, swapped_by_core(): return lax.ppermute(array, ('blk', 'grp'), route)  13.4 us
    ppermute x10, starting transfers between devices, swapped(): lax.ppermute(array, axis, [(i, i ^ bit) for i in range(lax.axis_size(axis...  12.9 us
    pallas_call x18, Pallas kernels, call(): pl.pallas_call(body, out_shape=[*out_shape, *(jax.ShapeDtypeStruct(a.shap...  12.6 us
    ppermute x10, waiting for transfers between devices, swapped(): lax.ppermute(array, axis, [(i, i ^ bit) for i in range(lax.axis_size(axis...  9.68 us
    ppermute x6, starting transfers between devices, swapped_by_core(): return lax.ppermute(array, ('blk', 'grp'), route)  7.39 us
    unnamed x6, local copies, waits for them, and re-layouts  1.66 us
  transfers between devices with their start and end apart: 16, of which 7 were waited for; matrix products, arithmetic and copies ran while one was open for 0% of the time, Pallas kernels for 17%

profile of v16, /device:TPU:0, one launch (start us, length us, event | category | flops | bytes accessed | tf_op | source)
XLA Modules:
  0.0 59.8 jit_solution(7320676577522338064)
XLA Ops:
  0.6 4.1 %collective-permute-start = (bf16[128,1152]{1,0:T(8,128)(2,1)}, bf16[128,1152]{1,0:T(8,128)(2,1)S(1)}, u32[]{:S(2)}, u32[]{:S(2)}) collective-permute-start(bf16[128,1152]{1,0:T(8,128)(2,1)} %refs_6_.7), channel_id=1, source_target_pairs={{0,4},{1,5},{2,6},{3,7},{4,0},{5,1},{6,2},{7,3},{8,12},{9,13},{10,... | collective-permute-start | bytes 884744 | tf_op jit(solution)/shard_map/ppermute | solution.py:280
  4.7 1.6 %collective-permute-start.1 = (bf16[128,1152]{1,0:T(8,128)(2,1)}, bf16[128,1152]{1,0:T(8,128)(2,1)S(1)}, u32[]{:S(2)}, u32[]{:S(2)}) collective-permute-start(bf16[128,1152]{1,0:T(8,128)(2,1)} %refs_0_.10), channel_id=1, source_target_pairs={{0,2},{1,3},{2,0},{3,1},{4,6},{5,7},{6,4},{7,5},{8,10},{9,11},{10,... | collective-permute-start | bytes 884744 | tf_op jit(solution)/shard_map/ppermute | solution.py:280
  6.3 0.0 copy-start.1
  6.3 1.0 %copy-done.1 = bf16[128,1152]{1,0:T(8,128)(2,1)S(1)} copy-done((bf16[128,1152]{1,0:T(8,128)(2,1)S(1)}, bf16[128,1152]{1,0:T(8,128)(2,1)}, u32[]{:S(2)}) %copy-start.1) | copy-done | bytes 294936
  7.3 0.0 copy-start.2
  7.3 0.7 %copy-done.2 = s32[128]{0:T(128)S(1)} copy-done((s32[128]{0:T(128)S(1)}, s32[128]{0:T(128)}, u32[]{:S(2)}) %copy-start.2) | copy-done | bytes 536
  8.0 0.0 copy-start
  8.0 1.6 %collective-permute-start.4 = (bf16[136,1152]{1,0:T(8,128)(2,1)S(1)}, bf16[136,1152]{1,0:T(8,128)(2,1)S(1)}, u32[]{:S(2)}, u32[]{:S(2)}) collective-permute-start(bf16[136,1152]{1,0:T(8,128)(2,1)S(1)} %labelled.3.refs_2_.refs_7_.refs_4_.refs_8_), channel_id=1, source_target_pairs={{0,8},{8,0},{16,24},{24,16},{1,9},{9,1},{17,25},{25,17},{2,10},{10... | collective-permute-start | bytes 940040 | tf_op jit(solution)/shard_map/ppermute | solution.py:280
  9.6 1.5 %collective-permute-start.3 = (bf16[128,1152]{1,0:T(8,128)(2,1)}, bf16[128,1152]{1,0:T(8,128)(2,1)S(1)}, u32[]{:S(2)}, u32[]{:S(2)}) collective-permute-start(bf16[128,1152]{1,0:T(8,128)(2,1)} %refs_6_.7), channel_id=1, source_target_pairs={{0,16},{8,24},{16,0},{24,8},{1,17},{9,25},{17,1},{25,9},{2,18},{10... | collective-permute-start | bytes 884744 | tf_op jit(solution)/shard_map/ppermute | solution.py:280
  11.1 0.4 collective-permute-start.2
  11.5 6.8 %collective-permute-done.refs_0_ = bf16[128,1152]{1,0:T(8,128)(2,1)S(1)} collective-permute-done((bf16[128,1152]{1,0:T(8,128)(2,1)}, bf16[128,1152]{1,0:T(8,128)(2,1)S(1)}, u32[]{:S(2)}, u32[]{:S(2)}) %collective-permute-start) | collective-permute-done | bytes 294944 | tf_op jit(solution)/shard_map/ppermute | solution.py:280
  18.4 0.3 collective-permute-done.2.refs_1_
  18.6 0.0 collective-permute-done.1.refs_0_
  18.7 0.0 collective-permute-done.3.refs_3_.refs_4_.refs_10_.refs_6_
  18.7 0.0 collective-permute-done.4.refs_4_.refs_5_.refs_6_.refs_10_
  18.7 0.0 copy-done
  18.8 0.1 bundled.3
  18.9 0.1 collective-permute-start.7
  19.0 1.6 %collective-permute-start.6 = (bf16[136,1152]{1,0:T(8,128)(2,1)S(1)}, bf16[136,1152]{1,0:T(8,128)(2,1)S(1)}, u32[]{:S(2)}, u32[]{:S(2)}) collective-permute-start(bf16[136,1152]{1,0:T(8,128)(2,1)S(1)} %labelled.2.refs_1_.refs_3_.refs_5_.refs_9_), channel_id=1, source_target_pairs={{0,8},{8,0},{16,24},{24,16},{1,9},{9,1},{17,25},{25,17},{2,10},{10... | collective-permute-start | bytes 940040 | tf_op jit(solution)/shard_map/ppermute | solution.py:280
  20.6 1.5 %collective-permute-start.5 = (bf16[128,1152]{1,0:T(8,128)(2,1)S(1)}, bf16[128,1152]{1,0:T(8,128)(2,1)S(1)}, u32[]{:S(2)}, u32[]{:S(2)}) collective-permute-start(bf16[128,1152]{1,0:T(8,128)(2,1)S(1)} %held.3.refs_2_.refs_0_.refs_9_.refs_5_), channel_id=1, source_target_pairs={{0,16},{8,24},{16,0},{24,8},{1,17},{9,25},{17,1},{25,9},{2,18},{10... | collective-permute-start | bytes 884744 | tf_op jit(solution)/shard_map/ppermute | solution.py:280
  23.4 0.0 collective-permute-done.7.refs_8_.refs_7_
  23.4 1.9 %early_sums.3 = (f32[128,1152]{1,0:T(8,128)S(1)}, f32[128,1152]{1,0:T(8,128)S(1)}, f32[128,1152]{1,0:T(8,128)S(1)}) custom-call(f32[1]{0:T(128)S(6)} %copy.17.refs_0_, f32[1]{0:T(128)S(6)} %copy.18.refs_1_, bf16[128,1152]{1,0:T(8,128)(2,1)S(1)} %held.3.refs_2_.refs_0_.refs_9_.refs_5_, bf16[136,1152]{1,0:T(8,128)(2,1)S(1)} %labelled.2.refs_1_.refs_3_.refs_5_.refs_9_, ...), custom_call_target="tpu_custom_call" | custom-call | flops 2304 | bytes 2304 | tf_op jit(solution)/shard_map/early_sums/pallas_call | solution.py:92
  25.3 1.9 %early_sums.2 = (f32[128,1152]{1,0:T(8,128)S(1)}, f32[128,1152]{1,0:T(8,128)S(1)}, f32[128,1152]{1,0:T(8,128)S(1)}) custom-call(f32[1]{0:T(128)S(6)} %copy.17.refs_0_, f32[1]{0:T(128)S(6)} %copy.18.refs_1_, bf16[128,1152]{1,0:T(8,128)(2,1)S(1)} %held.3.refs_2_.refs_0_.refs_9_.refs_5_, bf16[136,1152]{1,0:T(8,128)(2,1)S(1)} %labelled.2.refs_1_.refs_3_.refs_5_.refs_9_, ...), custom_call_target="tpu_custom_call" | custom-call | flops 2304 | bytes 2304 | tf_op jit(solution)/shard_map/early_sums/pallas_call | solution.py:92
  27.3 2.4 %collective-permute-done.5.refs_2_.refs_13_.refs_8_ = bf16[128,1152]{1,0:T(8,128)(2,1)S(1)} collective-permute-done((bf16[128,1152]{1,0:T(8,128)(2,1)S(1)}, bf16[128,1152]{1,0:T(8,128)(2,1)S(1)}, u32[]{:S(2)}, u32[]{:S(2)}) %collective-permute-start.5) | collective-permute-done | bytes 294944 | tf_op jit(solution)/shard_map/ppermute | solution.py:280
  29.7 0.0 collective-permute-done.6.refs_3_.refs_8_.refs_13_
  29.7 0.0 collective-permute-start.8
  29.7 0.5 collective-permute-start.9
  30.2 1.3 %late_rows_begun.2.refs_5_ = f32[128,1152]{1,0:T(8,128)S(1)} custom-call(f32[1]{0:T(128)S(6)} %copy.17.refs_0_, f32[1]{0:T(128)S(6)} %copy.18.refs_1_, bf16[128,1152]{1,0:T(8,128)(2,1)S(1)} %collective-permute-done.5.refs_2_.refs_13_.refs_8_, bf16[136,1152]{1,0:T(8,128)(2,1)S(1)} %collective-permute-done.6.refs_3_.refs_8_.refs_13_, ...), custom_call_target="tpu_custom_call" | custom-call | flops 896 | bytes 896 | tf_op jit(solution)/shard_map/late_rows_begun/pallas_call | solution.py:92
  31.5 0.2 collective-permute-done.9.refs_6_.refs_4_.refs_14_.refs_9_
  31.7 0.0 collective-permute-done.8.refs_4_.refs_6_.refs_9_.refs_14_
  31.7 0.6 %late_rows.2.refs_11_ = s16[136,1152]{1,0:T(8,128)(2,1)S(1)} custom-call(f32[1]{0:T(128)S(6)} %copy.17.refs_0_, f32[1]{0:T(128)S(6)} %copy.18.refs_1_, bf16[128,1152]{1,0:T(8,128)(2,1)S(1)} %collective-permute-done.5.refs_2_.refs_13_.refs_8_, bf16[136,1152]{1,0:T(8,128)(2,1)S(1)} %collective-permute-done.6.refs_3_.refs_8_.refs_13_, ...), custom_call_target="tpu_custom_call" | custom-call | flops 128 | bytes 128 | tf_op jit(solution)/shard_map/late_rows/pallas_call | solution.py:92
  32.3 1.6 %collective-permute-start.10 = (s16[136,1152]{1,0:T(8,128)(2,1)S(1)}, s16[136,1152]{1,0:T(8,128)(2,1)S(1)}, u32[]{:S(2)}, u32[]{:S(2)}) collective-permute-start(s16[136,1152]{1,0:T(8,128)(2,1)S(1)} %late_rows.2.refs_11_), channel_id=1, source_target_pairs={{0,16},{1,9},{2,18},{3,11},{4,20},{5,13},{6,22},{7,15},{8,24},{9,1... | collective-permute-start | bytes 940040 | tf_op jit(solution)/shard_map/ppermute | solution.py:289
  33.9 1.3 %late_rows_begun.3.refs_5_ = f32[128,1152]{1,0:T(8,128)S(1)} custom-call(f32[1]{0:T(128)S(6)} %copy.17.refs_0_, f32[1]{0:T(128)S(6)} %copy.18.refs_1_, bf16[128,1152]{1,0:T(8,128)(2,1)S(1)} %collective-permute-done.5.refs_2_.refs_13_.refs_8_, bf16[136,1152]{1,0:T(8,128)(2,1)S(1)} %collective-permute-done.6.refs_3_.refs_8_.refs_13_, ...), custom_call_target="tpu_custom_call" | custom-call | flops 896 | bytes 896 | tf_op jit(solution)/shard_map/late_rows_begun/pallas_call | solution.py:92
  35.3 0.6 %late_rows.3.refs_18_ = s16[136,1152]{1,0:T(8,128)(2,1)S(1)} custom-call(f32[1]{0:T(128)S(6)} %copy.17.refs_0_, f32[1]{0:T(128)S(6)} %copy.18.refs_1_, bf16[128,1152]{1,0:T(8,128)(2,1)S(1)} %collective-permute-done.5.refs_2_.refs_13_.refs_8_, bf16[136,1152]{1,0:T(8,128)(2,1)S(1)} %collective-permute-done.6.refs_3_.refs_8_.refs_13_, ...), custom_call_target="tpu_custom_call" | custom-call | flops 128 | bytes 128 | tf_op jit(solution)/shard_map/late_rows/pallas_call | solution.py:92
  35.9 0.7 %collective-permute-start.13 = (s16[136,1152]{1,0:T(8,128)(2,1)S(1)}, s16[136,1152]{1,0:T(8,128)(2,1)S(1)}, u32[]{:S(2)}, u32[]{:S(2)}) collective-permute-start(s16[136,1152]{1,0:T(8,128)(2,1)S(1)} %late_rows.3.refs_18_), channel_id=1, source_target_pairs={{0,8},{1,17},{2,10},{3,19},{4,12},{5,21},{6,14},{7,23},{8,0},{9,25... | collective-permute-start | bytes 940040 | tf_op jit(solution)/shard_map/ppermute | solution.py:289
  36.6 1.3 %late_columns.2 = (f32[128,1152]{1,0:T(8,128)S(1)}, f32[128,1152]{1,0:T(8,128)S(1)}, s16[136,1152]{1,0:T(8,128)(2,1)S(1)}) custom-call(f32[1]{0:T(128)S(6)} %copy.17.refs_0_, f32[1]{0:T(128)S(6)} %copy.18.refs_1_, bf16[128,1152]{1,0:T(8,128)(2,1)S(1)} %held.3.refs_2_.refs_0_.refs_9_.refs_5_, bf16[136,1152]{1,0:T(8,128)(2,1)S(1)} %labelled.2.refs_1_.refs_3_.refs_5_.refs_9_, ...), custom_call_target="tpu_custom_call" | custom-call | flops 768 | bytes 768 | tf_op jit(solution)/shard_map/late_columns/pallas_call | solution.py:92
  38.0 1.5 %late_columns.3 = (f32[128,1152]{1,0:T(8,128)S(1)}, f32[128,1152]{1,0:T(8,128)S(1)}, s16[136,1152]{1,0:T(8,128)(2,1)S(1)}) custom-call(f32[1]{0:T(128)S(6)} %copy.17.refs_0_, f32[1]{0:T(128)S(6)} %copy.18.refs_1_, bf16[128,1152]{1,0:T(8,128)(2,1)S(1)} %held.3.refs_2_.refs_0_.refs_9_.refs_5_, bf16[136,1152]{1,0:T(8,128)(2,1)S(1)} %labelled.2.refs_1_.refs_3_.refs_5_.refs_9_, ...), custom_call_target="tpu_custom_call" | custom-call | flops 768 | bytes 768 | tf_op jit(solution)/shard_map/late_columns/pallas_call | solution.py:92
  39.5 1.5 %collective-permute-done.10.refs_1_ = s16[136,1152]{1,0:T(8,128)(2,1)S(1)} collective-permute-done((s16[136,1152]{1,0:T(8,128)(2,1)S(1)}, s16[136,1152]{1,0:T(8,128)(2,1)S(1)}, u32[]{:S(2)}, u32[]{:S(2)}) %collective-permute-start.10) | collective-permute-done | bytes 313376 | tf_op jit(solution)/shard_map/ppermute | solution.py:289
  41.0 0.2 passed_sum.2
  41.2 1.4 %collective-permute-start.11 = (s16[136,1152]{1,0:T(8,128)(2,1)S(1)}, s16[136,1152]{1,0:T(8,128)(2,1)S(1)}, u32[]{:S(2)}, u32[]{:S(2)}) collective-permute-start(s16[136,1152]{1,0:T(8,128)(2,1)S(1)} %get-tuple-element.43.refs_2_), channel_id=1, source_target_pairs={{0,4},{1,3},{2,6},{3,1},{4,0},{5,7},{6,2},{7,5},{8,12},{9,11},{10,... | collective-permute-start | bytes 940040 | tf_op jit(solution)/shard_map/ppermute | solution.py:289
  42.6 0.3 collective-permute-done.13.refs_1_
  42.9 0.2 passed_sum.3
  43.1 2.1 %collective-permute-start.14 = (s16[136,1152]{1,0:T(8,128)(2,1)S(1)}, s16[136,1152]{1,0:T(8,128)(2,1)S(1)}, u32[]{:S(2)}, u32[]{:S(2)}) collective-permute-start(s16[136,1152]{1,0:T(8,128)(2,1)S(1)} %get-tuple-element.48), channel_id=1, source_target_pairs={{0,2},{1,5},{2,0},{3,7},{4,6},{5,1},{6,4},{7,3},{8,10},{9,13},{10,... | collective-permute-start | bytes 940040 | tf_op jit(solution)/shard_map/ppermute | solution.py:289
  45.2 0.0 collective-permute-start.15
  45.2 1.5 %collective-permute-start.12 = (s16[136,1152]{1,0:T(8,128)(2,1)S(1)}, s16[136,1152]{1,0:T(8,128)(2,1)S(1)}, u32[]{:S(2)}, u32[]{:S(2)}) collective-permute-start(s16[136,1152]{1,0:T(8,128)(2,1)S(1)} %get-tuple-element.44), channel_id=1, source_target_pairs={{0,16},{1,9},{2,18},{3,11},{4,20},{5,13},{6,22},{7,15},{8,24},{9,1... | collective-permute-start | bytes 940040 | tf_op jit(solution)/shard_map/ppermute | solution.py:289
  46.7 11.6 %collective-permute-done.11.refs_0_ = s16[136,1152]{1,0:T(8,128)(2,1)S(1)} collective-permute-done((s16[136,1152]{1,0:T(8,128)(2,1)S(1)}, s16[136,1152]{1,0:T(8,128)(2,1)S(1)}, u32[]{:S(2)}, u32[]{:S(2)}) %collective-permute-start.11) | collective-permute-done | bytes 313376 | tf_op jit(solution)/shard_map/ppermute | solution.py:289
  58.3 0.0 collective-permute-done.14.refs_1_
  58.4 0.0 collective-permute-done.15.refs_6_
  58.4 0.0 collective-permute-done.12.refs_3_
  58.4 1.4 %output_sums.1 = (f32[128,1152]{1,0:T(8,128)}, f32[128,1152]{1,0:T(8,128)}) custom-call(f32[1]{0:T(128)S(6)} %copy.17.refs_0_, f32[128,1152]{1,0:T(8,128)S(1)} %get-tuple-element.40.refs_1_, s16[136,1152]{1,0:T(8,128)(2,1)S(1)} %held.4.refs_0_.refs_2_, s16[136,1152]{1,0:T(8,128)(2,1)S(1)} %collective-permute-done.12.refs_3_, ...), custom_call_target="tpu_custom_call" | custom-call | flops 128 | bytes 128 | tf_op jit(solution)/shard_map/output_sums/pallas_call | solution.py:92
  (6 shorter events, 0.1 us)
Async XLA Ops:
  0.6 17.8 %collective-permute-start = (bf16[128,1152]{1,0:T(8,128)(2,1)}, bf16[128,1152]{1,0:T(8,128)(2,1)S(1)}, u32[]{:S(2)}, u32[]{:S(2)}) collective-permute-start(bf16[128,1152]{1,0:T(8,128)(2,1)} %refs_6_.7), channel_id=1, source_target_pairs={{0,4},{1,5},{2,6},{3,7},{4,0},{5,1},{6,2},{7,3},{8,12},{9,13},{10,... | collective-permute-start | bytes 884744 | tf_op jit(solution)/shard_map/ppermute | solution.py:280
  4.7 13.9 %collective-permute-start.1 = (bf16[128,1152]{1,0:T(8,128)(2,1)}, bf16[128,1152]{1,0:T(8,128)(2,1)S(1)}, u32[]{:S(2)}, u32[]{:S(2)}) collective-permute-start(bf16[128,1152]{1,0:T(8,128)(2,1)} %refs_0_.10), channel_id=1, source_target_pairs={{0,2},{1,3},{2,0},{3,1},{4,6},{5,7},{6,4},{7,5},{8,10},{9,11},{10,... | collective-permute-start | bytes 884744 | tf_op jit(solution)/shard_map/ppermute | solution.py:280
  6.3 1.0 %copy-start.1 = (bf16[128,1152]{1,0:T(8,128)(2,1)S(1)}, bf16[128,1152]{1,0:T(8,128)(2,1)}, u32[]{:S(2)}) copy-start(bf16[128,1152]{1,0:T(8,128)(2,1)} %refs_0_.10) | copy-start | bytes 884740
  7.3 0.7 %copy-start.2 = (s32[128]{0:T(128)S(1)}, s32[128]{0:T(128)}, u32[]{:S(2)}) copy-start(s32[128]{0:T(128)} %param.7) | copy-start | bytes 1540
  8.0 10.8 %copy-start = (bf16[128,1152]{1,0:T(8,128)(2,1)S(1)}, bf16[128,1152]{1,0:T(8,128)(2,1)}, u32[]{:S(2)}) copy-start(bf16[128,1152]{1,0:T(8,128)(2,1)} %refs_6_.7) | copy-start | bytes 884740
  8.0 10.7 %collective-permute-start.4 = (bf16[136,1152]{1,0:T(8,128)(2,1)S(1)}, bf16[136,1152]{1,0:T(8,128)(2,1)S(1)}, u32[]{:S(2)}, u32[]{:S(2)}) collective-permute-start(bf16[136,1152]{1,0:T(8,128)(2,1)S(1)} %labelled.3.refs_2_.refs_7_.refs_4_.refs_8_), channel_id=1, source_target_pairs={{0,8},{8,0},{16,24},{24,16},{1,9},{9,1},{17,25},{25,17},{2,10},{10... | collective-permute-start | bytes 940040 | tf_op jit(solution)/shard_map/ppermute | solution.py:280
  9.6 9.2 %collective-permute-start.3 = (bf16[128,1152]{1,0:T(8,128)(2,1)}, bf16[128,1152]{1,0:T(8,128)(2,1)S(1)}, u32[]{:S(2)}, u32[]{:S(2)}) collective-permute-start(bf16[128,1152]{1,0:T(8,128)(2,1)} %refs_6_.7), channel_id=1, source_target_pairs={{0,16},{8,24},{16,0},{24,8},{1,17},{9,25},{17,1},{25,9},{2,18},{10... | collective-permute-start | bytes 884744 | tf_op jit(solution)/shard_map/ppermute | solution.py:280
  11.1 7.6 %collective-permute-start.2 = (s32[1,128]{1,0:T(1,128)S(1)}, s32[1,128]{1,0:T(1,128)S(1)}, u32[]{:S(2)}, u32[]{:S(2)}) collective-permute-start(s32[1,128]{1,0:T(1,128)S(1)} %bitcast.2), channel_id=1, source_target_pairs={{0,2},{1,3},{2,0},{3,1},{4,6},{5,7},{6,4},{7,5},{8,10},{9,11},{10,... | collective-permute-start | bytes 1544 | tf_op jit(solution)/shard_map/ppermute | solution.py:280
  18.9 4.5 %collective-permute-start.7 = (bf16[792,1152]{1,0:T(8,128)(2,1)S(1)}, bf16[792,1152]{1,0:T(8,128)(2,1)S(1)}, u32[]{:S(2)}, u32[]{:S(2)}) collective-permute-start(bf16[792,1152]{1,0:T(8,128)(2,1)S(1)} %bundled.3), channel_id=1, source_target_pairs={{0,1},{1,0},{2,3},{3,2},{4,5},{5,4},{6,7},{7,6},{8,9},{9,8},{10,11... | collective-permute-start | bytes 5474312 | tf_op jit(solution)/shard_map/ppermute | solution.py:280
  19.0 10.7 %collective-permute-start.6 = (bf16[136,1152]{1,0:T(8,128)(2,1)S(1)}, bf16[136,1152]{1,0:T(8,128)(2,1)S(1)}, u32[]{:S(2)}, u32[]{:S(2)}) collective-permute-start(bf16[136,1152]{1,0:T(8,128)(2,1)S(1)} %labelled.2.refs_1_.refs_3_.refs_5_.refs_9_), channel_id=1, source_target_pairs={{0,8},{8,0},{16,24},{24,16},{1,9},{9,1},{17,25},{25,17},{2,10},{10... | collective-permute-start | bytes 940040 | tf_op jit(solution)/shard_map/ppermute | solution.py:280
  20.6 9.1 %collective-permute-start.5 = (bf16[128,1152]{1,0:T(8,128)(2,1)S(1)}, bf16[128,1152]{1,0:T(8,128)(2,1)S(1)}, u32[]{:S(2)}, u32[]{:S(2)}) collective-permute-start(bf16[128,1152]{1,0:T(8,128)(2,1)S(1)} %held.3.refs_2_.refs_0_.refs_9_.refs_5_), channel_id=1, source_target_pairs={{0,16},{8,24},{16,0},{24,8},{1,17},{9,25},{17,1},{25,9},{2,18},{10... | collective-permute-start | bytes 884744 | tf_op jit(solution)/shard_map/ppermute | solution.py:280
  29.7 2.0 %collective-permute-start.8 = (bf16[136,1152]{1,0:T(8,128)(2,1)S(1)}, bf16[136,1152]{1,0:T(8,128)(2,1)S(1)}, u32[]{:S(2)}, u32[]{:S(2)}) collective-permute-start(bf16[136,1152]{1,0:T(8,128)(2,1)S(1)} %collective-permute-done.6.refs_3_.refs_8_.refs_13_), channel_id=1, source_target_pairs={{0,1},{1,0},{2,3},{3,2},{4,5},{5,4},{6,7},{7,6},{8,9},{9,8},{10,11... | collective-permute-start | bytes 940040 | tf_op jit(solution)/shard_map/ppermute | solution.py:280
  29.7 2.0 %collective-permute-start.9 = (bf16[128,1152]{1,0:T(8,128)(2,1)S(1)}, bf16[128,1152]{1,0:T(8,128)(2,1)S(1)}, u32[]{:S(2)}, u32[]{:S(2)}) collective-permute-start(bf16[128,1152]{1,0:T(8,128)(2,1)S(1)} %collective-permute-done.5.refs_2_.refs_13_.refs_8_), channel_id=1, source_target_pairs={{0,1},{1,0},{2,3},{3,2},{4,5},{5,4},{6,7},{7,6},{8,9},{9,8},{10,11... | collective-permute-start | bytes 884744 | tf_op jit(solution)/shard_map/ppermute | solution.py:280
  32.3 8.7 %collective-permute-start.10 = (s16[136,1152]{1,0:T(8,128)(2,1)S(1)}, s16[136,1152]{1,0:T(8,128)(2,1)S(1)}, u32[]{:S(2)}, u32[]{:S(2)}) collective-permute-start(s16[136,1152]{1,0:T(8,128)(2,1)S(1)} %late_rows.2.refs_11_), channel_id=1, source_target_pairs={{0,16},{1,9},{2,18},{3,11},{4,20},{5,13},{6,22},{7,15},{8,24},{9,1... | collective-permute-start | bytes 940040 | tf_op jit(solution)/shard_map/ppermute | solution.py:289
  35.9 7.0 %collective-permute-start.13 = (s16[136,1152]{1,0:T(8,128)(2,1)S(1)}, s16[136,1152]{1,0:T(8,128)(2,1)S(1)}, u32[]{:S(2)}, u32[]{:S(2)}) collective-permute-start(s16[136,1152]{1,0:T(8,128)(2,1)S(1)} %late_rows.3.refs_18_), channel_id=1, source_target_pairs={{0,8},{1,17},{2,10},{3,19},{4,12},{5,21},{6,14},{7,23},{8,0},{9,25... | collective-permute-start | bytes 940040 | tf_op jit(solution)/shard_map/ppermute | solution.py:289
  41.2 17.2 %collective-permute-start.11 = (s16[136,1152]{1,0:T(8,128)(2,1)S(1)}, s16[136,1152]{1,0:T(8,128)(2,1)S(1)}, u32[]{:S(2)}, u32[]{:S(2)}) collective-permute-start(s16[136,1152]{1,0:T(8,128)(2,1)S(1)} %get-tuple-element.43.refs_2_), channel_id=1, source_target_pairs={{0,4},{1,3},{2,6},{3,1},{4,0},{5,7},{6,2},{7,5},{8,12},{9,11},{10,... | collective-permute-start | bytes 940040 | tf_op jit(solution)/shard_map/ppermute | solution.py:289
  43.1 15.3 %collective-permute-start.14 = (s16[136,1152]{1,0:T(8,128)(2,1)S(1)}, s16[136,1152]{1,0:T(8,128)(2,1)S(1)}, u32[]{:S(2)}, u32[]{:S(2)}) collective-permute-start(s16[136,1152]{1,0:T(8,128)(2,1)S(1)} %get-tuple-element.48), channel_id=1, source_target_pairs={{0,2},{1,5},{2,0},{3,7},{4,6},{5,1},{6,4},{7,3},{8,10},{9,13},{10,... | collective-permute-start | bytes 940040 | tf_op jit(solution)/shard_map/ppermute | solution.py:289
  45.2 13.1 %collective-permute-start.15 = (s16[136,1152]{1,0:T(8,128)(2,1)S(1)}, s16[136,1152]{1,0:T(8,128)(2,1)S(1)}, u32[]{:S(2)}, u32[]{:S(2)}) collective-permute-start(s16[136,1152]{1,0:T(8,128)(2,1)S(1)} %get-tuple-element.49), channel_id=1, source_target_pairs={{0,8},{1,17},{2,10},{3,19},{4,12},{5,21},{6,14},{7,23},{8,0},{9,25... | collective-permute-start | bytes 940040 | tf_op jit(solution)/shard_map/ppermute | solution.py:289
  45.2 13.1 %collective-permute-start.12 = (s16[136,1152]{1,0:T(8,128)(2,1)S(1)}, s16[136,1152]{1,0:T(8,128)(2,1)S(1)}, u32[]{:S(2)}, u32[]{:S(2)}) collective-permute-start(s16[136,1152]{1,0:T(8,128)(2,1)S(1)} %get-tuple-element.44), channel_id=1, source_target_pairs={{0,16},{1,9},{2,18},{3,11},{4,20},{5,13},{6,22},{7,15},{8,24},{9,1... | collective-permute-start | bytes 940040 | tf_op jit(solution)/shard_map/ppermute | solution.py:289

commit v17 on v14

--- a/solution.py
+++ b/solution.py
@@ -373,22 +373,18 @@
         jobs, emits = every_pair(early, columns), ["float"] * len(early)
         results = sums("early_sums", k, early, columns, jobs, {}, emits)
         before.append({m: s for m, (s,) in zip(early, results)})
-    arrays = [[b[m][0][0] for m in late] for b in blocks[::-1]]
-    arrays, before = lax.optimization_barrier((arrays, before))
-    for k in (1, 0):
-        for m, a in zip(late, arrays[1 - k]):
-            blocks[k][m] = whole(a)
-            others[k][m] = whole(swapped(a, core))
+    after = [s for k in range(2) for s in before[k].values()]
+    for k in range(2):
+        held = in_order([blocks[k][m][0][0] for m in late], after if k == 0 else (), (1, BUNDLE_COST)[k])
+        after = [swapped(a, core) for a in held]
+        for m, mine, other in zip(late, held, after):
+            blocks[k][m], others[k][m] = whole(mine), whole(other)
     after = ()
     coded, kept = [[None] * half, [None] * half], [None, None]
     for k in (1, 0):
-        columns = [(0, m) for m in range(count)] + [(1, m) for m in early]
-        jobs, emits = every_pair(late, columns), ["float"] * len(late)
-        results = sums("late_rows_begun", k, late, columns, jobs, {}, emits, after)
-        begun = {i: s for i, (s,) in enumerate(results)}
-        columns = [(1, m) for m in late]
+        columns = both_cores(range(count))
         jobs, emits = every_pair(late, columns), ["parts"] * len(late)
-        coded[k][1:] = sums("late_rows", k, late, columns, jobs, begun, emits)
+        coded[k][1:] = sums("late_rows", k, late, columns, jobs, {}, emits, after)
         after = coded[k][1]
     for k in (1, 0):
         columns = both_cores(late)

time: 60.1 us -> 60.2 us (level)
  Pallas kernels: 12.2 us -> 11.1 us
  starting transfers between devices: 25.1 us -> 25.9 us
    pallas_call x20, Pallas kernels: 12.2 us -> 11.1 us  [call(): pl.pallas_call(body, out_shape=[*out_shape, *(jax.ShapeDtypeStruct(a.shap...]
    ppermute x20, starting transfers between devices: 25.1 us -> 25.9 us  [swapped(): lax.ppermute(array, axis, [(i, i ^ bit) for i in range(lax.axis_size(axis...]
  transfers between devices with their start and end apart: 20 -> 20, of which waited for: 8 -> 9; matrix products, arithmetic and copies ran while one was open for 0% -> 0% of each run, Pallas kernels for 18% -> 16%
where the time goes in v17:
time: 60.2 us; the launch traced here: 60.1 us
  starting transfers between devices  25.9 us (43%)
  waiting for transfers between devices  19.3 us (32%)
  Pallas kernels  11.1 us (18%)
  between operations  2.1 us (3%)
  local copies, waits for them, and re-layouts  1.66 us (3%)
    ppermute x20, starting transfers between devices, swapped(): lax.ppermute(array, axis, [(i, i ^ bit) for i in range(lax.axis_size(axis...  25.9 us
    ppermute x20, waiting for transfers between devices, swapped(): lax.ppermute(array, axis, [(i, i ^ bit) for i in range(lax.axis_size(axis...  19.3 us
    pallas_call x20, Pallas kernels, call(): pl.pallas_call(body, out_shape=[*out_shape, *(jax.ShapeDtypeStruct(a.shap...  11.1 us
    unnamed x6, local copies, waits for them, and re-layouts  1.66 us
  transfers between devices with their start and end apart: 20, of which 9 were waited for; matrix products, arithmetic and copies ran while one was open for 0% of the time, Pallas kernels for 16%

profile of v17, /device:TPU:0, one launch (start us, length us, event | category | flops | bytes accessed | tf_op | source)
XLA Modules:
  0.0 60.1 jit_solution(11162929688179639330)
XLA Ops:
  0.6 4.1 %collective-permute-start = (bf16[128,1152]{1,0:T(8,128)(2,1)}, bf16[128,1152]{1,0:T(8,128)(2,1)S(1)}, u32[]{:S(2)}, u32[]{:S(2)}) collective-permute-start(bf16[128,1152]{1,0:T(8,128)(2,1)} %refs_6_.7), channel_id=1, source_target_pairs={{0,4},{1,5},{2,6},{3,7},{4,0},{5,1},{6,2},{7,3},{8,12},{9,13},{10,... | collective-permute-start | bytes 884744 | tf_op jit(solution)/shard_map/ppermute | solution.py:274
  4.7 1.6 %collective-permute-start.1 = (bf16[128,1152]{1,0:T(8,128)(2,1)}, bf16[128,1152]{1,0:T(8,128)(2,1)S(1)}, u32[]{:S(2)}, u32[]{:S(2)}) collective-permute-start(bf16[128,1152]{1,0:T(8,128)(2,1)} %refs_0_.8), channel_id=1, source_target_pairs={{0,2},{1,3},{2,0},{3,1},{4,6},{5,7},{6,4},{7,5},{8,10},{9,11},{10,... | collective-permute-start | bytes 884744 | tf_op jit(solution)/shard_map/ppermute | solution.py:274
  6.3 0.0 copy-start.1
  6.3 1.0 %copy-done.1 = bf16[128,1152]{1,0:T(8,128)(2,1)S(1)} copy-done((bf16[128,1152]{1,0:T(8,128)(2,1)S(1)}, bf16[128,1152]{1,0:T(8,128)(2,1)}, u32[]{:S(2)}) %copy-start.1) | copy-done | bytes 294936
  7.3 0.0 copy-start.2
  7.3 0.7 %copy-done.2 = s32[128]{0:T(128)S(1)} copy-done((s32[128]{0:T(128)S(1)}, s32[128]{0:T(128)}, u32[]{:S(2)}) %copy-start.2) | copy-done | bytes 536
  8.0 0.0 copy-start
  8.0 1.6 %collective-permute-start.4 = (bf16[136,1152]{1,0:T(8,128)(2,1)S(1)}, bf16[136,1152]{1,0:T(8,128)(2,1)S(1)}, u32[]{:S(2)}, u32[]{:S(2)}) collective-permute-start(bf16[136,1152]{1,0:T(8,128)(2,1)S(1)} %labelled.3.refs_2_.refs_7_.refs_4_), channel_id=1, source_target_pairs={{0,8},{8,0},{16,24},{24,16},{1,9},{9,1},{17,25},{25,17},{2,10},{10... | collective-permute-start | bytes 940040 | tf_op jit(solution)/shard_map/ppermute | solution.py:274
  9.6 1.5 %collective-permute-start.3 = (bf16[128,1152]{1,0:T(8,128)(2,1)}, bf16[128,1152]{1,0:T(8,128)(2,1)S(1)}, u32[]{:S(2)}, u32[]{:S(2)}) collective-permute-start(bf16[128,1152]{1,0:T(8,128)(2,1)} %refs_6_.7), channel_id=1, source_target_pairs={{0,16},{8,24},{16,0},{24,8},{1,17},{9,25},{17,1},{25,9},{2,18},{10... | collective-permute-start | bytes 884744 | tf_op jit(solution)/shard_map/ppermute | solution.py:274
  11.1 0.4 collective-permute-start.2
  11.5 6.8 %collective-permute-done.refs_0_ = bf16[128,1152]{1,0:T(8,128)(2,1)S(1)} collective-permute-done((bf16[128,1152]{1,0:T(8,128)(2,1)}, bf16[128,1152]{1,0:T(8,128)(2,1)S(1)}, u32[]{:S(2)}, u32[]{:S(2)}) %collective-permute-start) | collective-permute-done | bytes 294944 | tf_op jit(solution)/shard_map/ppermute | solution.py:274
  18.4 0.3 collective-permute-done.2.refs_1_
  18.6 0.0 collective-permute-done.1.refs_0_
  18.7 0.0 collective-permute-done.3.refs_3_.refs_4_.refs_6_
  18.7 0.0 collective-permute-done.4.refs_4_.refs_5_.refs_6_
  18.7 0.0 copy-done
  18.8 0.1 bundled.3
  18.9 0.1 collective-permute-start.7
  19.0 1.6 %collective-permute-start.8 = (bf16[136,1152]{1,0:T(8,128)(2,1)S(1)}, bf16[136,1152]{1,0:T(8,128)(2,1)S(1)}, u32[]{:S(2)}, u32[]{:S(2)}) collective-permute-start(bf16[136,1152]{1,0:T(8,128)(2,1)S(1)} %labelled.2.refs_1_.refs_3_.refs_5_), channel_id=1, source_target_pairs={{0,8},{8,0},{16,24},{24,16},{1,9},{9,1},{17,25},{25,17},{2,10},{10... | collective-permute-start | bytes 940040 | tf_op jit(solution)/shard_map/ppermute | solution.py:274
  20.6 1.5 %collective-permute-start.5 = (bf16[128,1152]{1,0:T(8,128)(2,1)S(1)}, bf16[128,1152]{1,0:T(8,128)(2,1)S(1)}, u32[]{:S(2)}, u32[]{:S(2)}) collective-permute-start(bf16[128,1152]{1,0:T(8,128)(2,1)S(1)} %held.5.refs_2_.refs_0_.refs_5_), channel_id=1, source_target_pairs={{0,16},{8,24},{16,0},{24,8},{1,17},{9,25},{17,1},{25,9},{2,18},{10... | collective-permute-start | bytes 884744 | tf_op jit(solution)/shard_map/ppermute | solution.py:274
  23.4 0.0 collective-permute-done.7.refs_8_.refs_7_
  23.4 1.9 %early_sums.3 = (f32[128,1152]{1,0:T(8,128)S(1)}, f32[128,1152]{1,0:T(8,128)S(1)}, f32[128,1152]{1,0:T(8,128)S(1)}) custom-call(f32[1]{0:T(128)S(6)} %copy.29.refs_0_, f32[1]{0:T(128)S(6)} %copy.30.refs_1_, bf16[128,1152]{1,0:T(8,128)(2,1)S(1)} %held.5.refs_2_.refs_0_.refs_5_, bf16[136,1152]{1,0:T(8,128)(2,1)S(1)} %labelled.2.refs_1_.refs_3_.refs_5_, ...), custom_call_target="tpu_custom_call" | custom-call | flops 2304 | bytes 2304 | tf_op jit(solution)/shard_map/early_sums/pallas_call | solution.py:93
  25.3 1.9 %early_sums.2 = (f32[128,1152]{1,0:T(8,128)S(1)}, f32[128,1152]{1,0:T(8,128)S(1)}, f32[128,1152]{1,0:T(8,128)S(1)}) custom-call(f32[1]{0:T(128)S(6)} %copy.29.refs_0_, f32[1]{0:T(128)S(6)} %copy.30.refs_1_, bf16[128,1152]{1,0:T(8,128)(2,1)S(1)} %held.5.refs_2_.refs_0_.refs_5_, bf16[136,1152]{1,0:T(8,128)(2,1)S(1)} %labelled.2.refs_1_.refs_3_.refs_5_, ...), custom_call_target="tpu_custom_call" | custom-call | flops 2304 | bytes 2304 | tf_op jit(solution)/shard_map/early_sums/pallas_call | solution.py:93
  27.3 1.5 %collective-permute-done.8.refs_6_ = bf16[136,1152]{1,0:T(8,128)(2,1)S(1)} collective-permute-done((bf16[136,1152]{1,0:T(8,128)(2,1)S(1)}, bf16[136,1152]{1,0:T(8,128)(2,1)S(1)}, u32[]{:S(2)}, u32[]{:S(2)}) %collective-permute-start.8) | collective-permute-done | bytes 313376 | tf_op jit(solution)/shard_map/ppermute | solution.py:274
  28.8 0.0 collective-permute-start.9
  28.8 0.9 %collective-permute-done.5.refs_0_ = bf16[128,1152]{1,0:T(8,128)(2,1)S(1)} collective-permute-done((bf16[128,1152]{1,0:T(8,128)(2,1)S(1)}, bf16[128,1152]{1,0:T(8,128)(2,1)S(1)}, u32[]{:S(2)}, u32[]{:S(2)}) %collective-permute-start.5) | collective-permute-done | bytes 294944 | tf_op jit(solution)/shard_map/ppermute | solution.py:274
  29.7 0.0 collective-permute-start.6
  29.7 0.7 %collective-permute-done.9.refs_8_.refs_9_ = bf16[136,1152]{1,0:T(8,128)(2,1)S(1)} collective-permute-done((bf16[136,1152]{1,0:T(8,128)(2,1)S(1)}, bf16[136,1152]{1,0:T(8,128)(2,1)S(1)}, u32[]{:S(2)}, u32[]{:S(2)}) %collective-permute-start.9) | collective-permute-done | bytes 313376 | tf_op jit(solution)/shard_map/ppermute | solution.py:274
  30.4 1.4 %late_rows.2 = (s16[136,640]{1,0:T(8,128)(2,1)S(1)}, s16[136,512]{1,0:T(8,128)(2,1)S(1)}) custom-call(f32[1]{0:T(128)S(6)} %copy.29.refs_0_, f32[1]{0:T(128)S(6)} %copy.30.refs_1_, bf16[128,1152]{1,0:T(8,128)(2,1)S(1)} %held.6.refs_2_.refs_8_, bf16[136,1152]{1,0:T(8,128)(2,1)S(1)} %held.7.refs_3_.refs_8_, ...), custom_call_target="tpu_custom_call" | custom-call | flops 1024 | bytes 1024 | tf_op jit(solution)/shard_map/late_rows/pallas_call | solution.py:93
  31.8 1.6 %collective-permute-start.12 = (s16[136,640]{1,0:T(8,128)(2,1)S(1)}, s16[136,640]{1,0:T(8,128)(2,1)S(1)}, u32[]{:S(2)}, u32[]{:S(2)}) collective-permute-start(s16[136,640]{1,0:T(8,128)(2,1)S(1)} %get-tuple-element.34.refs_9_), channel_id=1, source_target_pairs={{0,16},{8,24},{16,0},{24,8},{1,17},{9,25},{17,1},{25,9},{2,18},{10... | collective-permute-start | bytes 522248 | tf_op jit(solution)/shard_map/ppermute | solution.py:274
  33.5 0.0 collective-permute-done.6.refs_8_.refs_9_
  33.5 1.4 %late_rows.3 = (s16[136,640]{1,0:T(8,128)(2,1)S(1)}, s16[136,512]{1,0:T(8,128)(2,1)S(1)}) custom-call(f32[1]{0:T(128)S(6)} %copy.29.refs_0_, f32[1]{0:T(128)S(6)} %copy.30.refs_1_, bf16[128,1152]{1,0:T(8,128)(2,1)S(1)} %held.6.refs_2_.refs_8_, bf16[136,1152]{1,0:T(8,128)(2,1)S(1)} %held.7.refs_3_.refs_8_, bf16[128,1152]{1,0:T(8,128)(2,1)S(1)} %copy-done, ...), custom_call_target="tpu_custom_call" | custom-call | flops 1024 | bytes 1024 | tf_op jit(solution)/shard_map/late_rows/pallas_call | solution.py:93
  34.9 1.6 %collective-permute-start.10 = (s16[136,640]{1,0:T(8,128)(2,1)S(1)}, s16[136,640]{1,0:T(8,128)(2,1)S(1)}, u32[]{:S(2)}, u32[]{:S(2)}) collective-permute-start(s16[136,640]{1,0:T(8,128)(2,1)S(1)} %get-tuple-element.36.refs_13_), channel_id=1, source_target_pairs={{0,8},{8,0},{16,24},{24,16},{1,9},{9,1},{17,25},{25,17},{2,10},{10... | collective-permute-start | bytes 522248 | tf_op jit(solution)/shard_map/ppermute | solution.py:274
  36.4 1.3 %late_columns.2 = (f32[128,1152]{1,0:T(8,128)S(1)}, f32[128,1152]{1,0:T(8,128)S(1)}, s16[136,1152]{1,0:T(8,128)(2,1)S(1)}) custom-call(f32[1]{0:T(128)S(6)} %copy.29.refs_0_, f32[1]{0:T(128)S(6)} %copy.30.refs_1_, bf16[128,1152]{1,0:T(8,128)(2,1)S(1)} %held.5.refs_2_.refs_0_.refs_5_, bf16[136,1152]{1,0:T(8,128)(2,1)S(1)} %labelled.2.refs_1_.refs_3_.refs_5_, ...), custom_call_target="tpu_custom_call" | custom-call | flops 768 | bytes 768 | tf_op jit(solution)/shard_map/late_columns/pallas_call | solution.py:93
  37.7 1.3 %late_columns.3 = (f32[128,1152]{1,0:T(8,128)S(1)}, f32[128,1152]{1,0:T(8,128)S(1)}, s16[136,1152]{1,0:T(8,128)(2,1)S(1)}) custom-call(f32[1]{0:T(128)S(6)} %copy.29.refs_0_, f32[1]{0:T(128)S(6)} %copy.30.refs_1_, bf16[128,1152]{1,0:T(8,128)(2,1)S(1)} %held.5.refs_2_.refs_0_.refs_5_, bf16[136,1152]{1,0:T(8,128)(2,1)S(1)} %labelled.2.refs_1_.refs_3_.refs_5_, ...), custom_call_target="tpu_custom_call" | custom-call | flops 768 | bytes 768 | tf_op jit(solution)/shard_map/late_columns/pallas_call | solution.py:93
  39.1 0.0 collective-permute-done.12.refs_1_
  39.1 0.1 passed_sum.5
  39.2 1.4 %collective-permute-start.13 = (s16[136,640]{1,0:T(8,128)(2,1)S(1)}, s16[136,640]{1,0:T(8,128)(2,1)S(1)}, u32[]{:S(2)}, u32[]{:S(2)}) collective-permute-start(s16[136,640]{1,0:T(8,128)(2,1)S(1)} %get-tuple-element.44), channel_id=1, source_target_pairs={{0,4},{1,5},{2,6},{3,7},{4,0},{5,1},{6,2},{7,3},{8,12},{9,13},{10,... | collective-permute-start | bytes 522248 | tf_op jit(solution)/shard_map/ppermute | solution.py:274
  40.6 0.9 %collective-permute-start.14 = (s16[136,512]{1,0:T(8,128)(2,1)S(1)}, s16[136,512]{1,0:T(8,128)(2,1)S(1)}, u32[]{:S(2)}, u32[]{:S(2)}) collective-permute-start(s16[136,512]{1,0:T(8,128)(2,1)S(1)} %get-tuple-element.45), channel_id=1, source_target_pairs={{0,16},{8,24},{16,0},{24,8},{1,17},{9,25},{17,1},{25,9},{2,18},{10... | collective-permute-start | bytes 417800 | tf_op jit(solution)/shard_map/ppermute | solution.py:274
  41.4 0.0 collective-permute-done.10.refs_1_
  41.4 0.1 passed_sum.4
  41.6 2.4 %collective-permute-start.16 = (s16[136,640]{1,0:T(8,128)(2,1)S(1)}, s16[136,640]{1,0:T(8,128)(2,1)S(1)}, u32[]{:S(2)}, u32[]{:S(2)}) collective-permute-start(s16[136,640]{1,0:T(8,128)(2,1)S(1)} %get-tuple-element.48), channel_id=1, source_target_pairs={{0,2},{1,3},{2,0},{3,1},{4,6},{5,7},{6,4},{7,5},{8,10},{9,11},{10,... | collective-permute-start | bytes 522248 | tf_op jit(solution)/shard_map/ppermute | solution.py:274
  44.0 1.5 %collective-permute-start.17 = (s16[136,512]{1,0:T(8,128)(2,1)S(1)}, s16[136,512]{1,0:T(8,128)(2,1)S(1)}, u32[]{:S(2)}, u32[]{:S(2)}) collective-permute-start(s16[136,512]{1,0:T(8,128)(2,1)S(1)} %get-tuple-element.49), channel_id=1, source_target_pairs={{0,8},{8,0},{16,24},{24,16},{1,9},{9,1},{17,25},{25,17},{2,10},{10... | collective-permute-start | bytes 417800 | tf_op jit(solution)/shard_map/ppermute | solution.py:274
  45.5 0.5 collective-permute-start.19
  46.0 0.0 collective-permute-done.14.refs_1_
  46.0 1.2 %collective-permute-start.11 = (s16[136,1152]{1,0:T(8,128)(2,1)S(1)}, s16[136,1152]{1,0:T(8,128)(2,1)S(1)}, u32[]{:S(2)}, u32[]{:S(2)}) collective-permute-start(s16[136,1152]{1,0:T(8,128)(2,1)S(1)} %get-tuple-element.42), channel_id=1, source_target_pairs={{0,8},{8,0},{16,24},{24,16},{1,9},{9,1},{17,25},{25,17},{2,10},{10... | collective-permute-start | bytes 940040 | tf_op jit(solution)/shard_map/ppermute | solution.py:274
  47.2 2.7 %collective-permute-done.13.refs_2_.refs_0_ = s16[136,640]{1,0:T(8,128)(2,1)S(1)} collective-permute-done((s16[136,640]{1,0:T(8,128)(2,1)S(1)}, s16[136,640]{1,0:T(8,128)(2,1)S(1)}, u32[]{:S(2)}, u32[]{:S(2)}) %collective-permute-start.13) | collective-permute-done | bytes 174112 | tf_op jit(solution)/shard_map/ppermute | solution.py:274
  49.9 0.1 passed_sum.6.refs_3_
  50.0 0.1 collective-permute-start.15
  50.1 0.5 collective-permute-done.17.refs_1_
  50.6 0.0 collective-permute-done.16.refs_2_
  50.6 0.1 passed_sum.7
  50.7 2.3 %collective-permute-start.18 = (s16[136,512]{1,0:T(8,128)(2,1)S(1)}, s16[136,512]{1,0:T(8,128)(2,1)S(1)}, u32[]{:S(2)}, u32[]{:S(2)}) collective-permute-start(s16[136,512]{1,0:T(8,128)(2,1)S(1)} %passed_sum.7), channel_id=1, source_target_pairs={{0,2},{1,3},{2,0},{3,1},{4,6},{5,7},{6,4},{7,5},{8,10},{9,11},{10,... | collective-permute-start | bytes 417800 | tf_op jit(solution)/shard_map/ppermute | solution.py:274
  53.0 5.6 %collective-permute-done.15.refs_1_ = s16[136,512]{1,0:T(8,128)(2,1)S(1)} collective-permute-done((s16[136,512]{1,0:T(8,128)(2,1)S(1)}, s16[136,512]{1,0:T(8,128)(2,1)S(1)}, u32[]{:S(2)}, u32[]{:S(2)}) %collective-permute-start.15) | collective-permute-done | bytes 139296 | tf_op jit(solution)/shard_map/ppermute | solution.py:274
  58.6 0.3 collective-permute-done.18.refs_3_
  58.8 0.0 collective-permute-done.19.refs_6_
  58.8 0.0 collective-permute-done.11.refs_2_
  58.9 1.2 %output_sums.1 = (f32[128,1152]{1,0:T(8,128)}, f32[128,1152]{1,0:T(8,128)}) custom-call(f32[1]{0:T(128)S(6)} %copy.29.refs_0_, f32[128,1152]{1,0:T(8,128)S(1)} %get-tuple-element.39.refs_1_, s16[136,1152]{1,0:T(8,128)(2,1)S(1)} %collective-permute-done.11.refs_2_, s16[136,640]{1,0:T(8,128)(2,1)S(1)} %get-tuple-element.50.refs_3_, ...), custom_call_target="tpu_custom_call" | custom-call | flops 128 | bytes 128 | tf_op jit(solution)/shard_map/output_sums/pallas_call | solution.py:93
  (8 shorter events, 0.1 us)
Async XLA Ops:
  0.6 17.8 %collective-permute-start = (bf16[128,1152]{1,0:T(8,128)(2,1)}, bf16[128,1152]{1,0:T(8,128)(2,1)S(1)}, u32[]{:S(2)}, u32[]{:S(2)}) collective-permute-start(bf16[128,1152]{1,0:T(8,128)(2,1)} %refs_6_.7), channel_id=1, source_target_pairs={{0,4},{1,5},{2,6},{3,7},{4,0},{5,1},{6,2},{7,3},{8,12},{9,13},{10,... | collective-permute-start | bytes 884744 | tf_op jit(solution)/shard_map/ppermute | solution.py:274
  4.7 13.9 %collective-permute-start.1 = (bf16[128,1152]{1,0:T(8,128)(2,1)}, bf16[128,1152]{1,0:T(8,128)(2,1)S(1)}, u32[]{:S(2)}, u32[]{:S(2)}) collective-permute-start(bf16[128,1152]{1,0:T(8,128)(2,1)} %refs_0_.8), channel_id=1, source_target_pairs={{0,2},{1,3},{2,0},{3,1},{4,6},{5,7},{6,4},{7,5},{8,10},{9,11},{10,... | collective-permute-start | bytes 884744 | tf_op jit(solution)/shard_map/ppermute | solution.py:274
  6.3 1.0 %copy-start.1 = (bf16[128,1152]{1,0:T(8,128)(2,1)S(1)}, bf16[128,1152]{1,0:T(8,128)(2,1)}, u32[]{:S(2)}) copy-start(bf16[128,1152]{1,0:T(8,128)(2,1)} %refs_0_.8) | copy-start | bytes 884740
  7.3 0.7 %copy-start.2 = (s32[128]{0:T(128)S(1)}, s32[128]{0:T(128)}, u32[]{:S(2)}) copy-start(s32[128]{0:T(128)} %param.7) | copy-start | bytes 1540
  8.0 10.8 %copy-start = (bf16[128,1152]{1,0:T(8,128)(2,1)S(1)}, bf16[128,1152]{1,0:T(8,128)(2,1)}, u32[]{:S(2)}) copy-start(bf16[128,1152]{1,0:T(8,128)(2,1)} %refs_6_.7) | copy-start | bytes 884740
  8.0 10.7 %collective-permute-start.4 = (bf16[136,1152]{1,0:T(8,128)(2,1)S(1)}, bf16[136,1152]{1,0:T(8,128)(2,1)S(1)}, u32[]{:S(2)}, u32[]{:S(2)}) collective-permute-start(bf16[136,1152]{1,0:T(8,128)(2,1)S(1)} %labelled.3.refs_2_.refs_7_.refs_4_), channel_id=1, source_target_pairs={{0,8},{8,0},{16,24},{24,16},{1,9},{9,1},{17,25},{25,17},{2,10},{10... | collective-permute-start | bytes 940040 | tf_op jit(solution)/shard_map/ppermute | solution.py:274
  9.6 9.2 %collective-permute-start.3 = (bf16[128,1152]{1,0:T(8,128)(2,1)}, bf16[128,1152]{1,0:T(8,128)(2,1)S(1)}, u32[]{:S(2)}, u32[]{:S(2)}) collective-permute-start(bf16[128,1152]{1,0:T(8,128)(2,1)} %refs_6_.7), channel_id=1, source_target_pairs={{0,16},{8,24},{16,0},{24,8},{1,17},{9,25},{17,1},{25,9},{2,18},{10... | collective-permute-start | bytes 884744 | tf_op jit(solution)/shard_map/ppermute | solution.py:274
  11.1 7.6 %collective-permute-start.2 = (s32[1,128]{1,0:T(1,128)S(1)}, s32[1,128]{1,0:T(1,128)S(1)}, u32[]{:S(2)}, u32[]{:S(2)}) collective-permute-start(s32[1,128]{1,0:T(1,128)S(1)} %bitcast.2), channel_id=1, source_target_pairs={{0,2},{1,3},{2,0},{3,1},{4,6},{5,7},{6,4},{7,5},{8,10},{9,11},{10,... | collective-permute-start | bytes 1544 | tf_op jit(solution)/shard_map/ppermute | solution.py:274
  18.9 4.5 %collective-permute-start.7 = (bf16[792,1152]{1,0:T(8,128)(2,1)S(1)}, bf16[792,1152]{1,0:T(8,128)(2,1)S(1)}, u32[]{:S(2)}, u32[]{:S(2)}) collective-permute-start(bf16[792,1152]{1,0:T(8,128)(2,1)S(1)} %bundled.3), channel_id=1, source_target_pairs={{0,1},{1,0},{2,3},{3,2},{4,5},{5,4},{6,7},{7,6},{8,9},{9,8},{10,11... | collective-permute-start | bytes 5474312 | tf_op jit(solution)/shard_map/ppermute | solution.py:274
  19.0 9.8 %collective-permute-start.8 = (bf16[136,1152]{1,0:T(8,128)(2,1)S(1)}, bf16[136,1152]{1,0:T(8,128)(2,1)S(1)}, u32[]{:S(2)}, u32[]{:S(2)}) collective-permute-start(bf16[136,1152]{1,0:T(8,128)(2,1)S(1)} %labelled.2.refs_1_.refs_3_.refs_5_), channel_id=1, source_target_pairs={{0,8},{8,0},{16,24},{24,16},{1,9},{9,1},{17,25},{25,17},{2,10},{10... | collective-permute-start | bytes 940040 | tf_op jit(solution)/shard_map/ppermute | solution.py:274
  20.6 9.1 %collective-permute-start.5 = (bf16[128,1152]{1,0:T(8,128)(2,1)S(1)}, bf16[128,1152]{1,0:T(8,128)(2,1)S(1)}, u32[]{:S(2)}, u32[]{:S(2)}) collective-permute-start(bf16[128,1152]{1,0:T(8,128)(2,1)S(1)} %held.5.refs_2_.refs_0_.refs_5_), channel_id=1, source_target_pairs={{0,16},{8,24},{16,0},{24,8},{1,17},{9,25},{17,1},{25,9},{2,18},{10... | collective-permute-start | bytes 884744 | tf_op jit(solution)/shard_map/ppermute | solution.py:274
  28.8 1.6 %collective-permute-start.9 = (bf16[136,1152]{1,0:T(8,128)(2,1)S(1)}, bf16[136,1152]{1,0:T(8,128)(2,1)S(1)}, u32[]{:S(2)}, u32[]{:S(2)}) collective-permute-start(bf16[136,1152]{1,0:T(8,128)(2,1)S(1)} %held.7.refs_3_.refs_8_), channel_id=1, source_target_pairs={{0,1},{1,0},{2,3},{3,2},{4,5},{5,4},{6,7},{7,6},{8,9},{9,8},{10,11... | collective-permute-start | bytes 940040 | tf_op jit(solution)/shard_map/ppermute | solution.py:274
  29.7 3.8 %collective-permute-start.6 = (bf16[128,1152]{1,0:T(8,128)(2,1)S(1)}, bf16[128,1152]{1,0:T(8,128)(2,1)S(1)}, u32[]{:S(2)}, u32[]{:S(2)}) collective-permute-start(bf16[128,1152]{1,0:T(8,128)(2,1)S(1)} %held.6.refs_2_.refs_8_), channel_id=1, source_target_pairs={{0,1},{1,0},{2,3},{3,2},{4,5},{5,4},{6,7},{7,6},{8,9},{9,8},{10,11... | collective-permute-start | bytes 884744 | tf_op jit(solution)/shard_map/ppermute | solution.py:274
  31.8 7.2 %collective-permute-start.12 = (s16[136,640]{1,0:T(8,128)(2,1)S(1)}, s16[136,640]{1,0:T(8,128)(2,1)S(1)}, u32[]{:S(2)}, u32[]{:S(2)}) collective-permute-start(s16[136,640]{1,0:T(8,128)(2,1)S(1)} %get-tuple-element.34.refs_9_), channel_id=1, source_target_pairs={{0,16},{8,24},{16,0},{24,8},{1,17},{9,25},{17,1},{25,9},{2,18},{10... | collective-permute-start | bytes 522248 | tf_op jit(solution)/shard_map/ppermute | solution.py:274
  34.9 6.6 %collective-permute-start.10 = (s16[136,640]{1,0:T(8,128)(2,1)S(1)}, s16[136,640]{1,0:T(8,128)(2,1)S(1)}, u32[]{:S(2)}, u32[]{:S(2)}) collective-permute-start(s16[136,640]{1,0:T(8,128)(2,1)S(1)} %get-tuple-element.36.refs_13_), channel_id=1, source_target_pairs={{0,8},{8,0},{16,24},{24,16},{1,9},{9,1},{17,25},{25,17},{2,10},{10... | collective-permute-start | bytes 522248 | tf_op jit(solution)/shard_map/ppermute | solution.py:274
  39.2 10.7 %collective-permute-start.13 = (s16[136,640]{1,0:T(8,128)(2,1)S(1)}, s16[136,640]{1,0:T(8,128)(2,1)S(1)}, u32[]{:S(2)}, u32[]{:S(2)}) collective-permute-start(s16[136,640]{1,0:T(8,128)(2,1)S(1)} %get-tuple-element.44), channel_id=1, source_target_pairs={{0,4},{1,5},{2,6},{3,7},{4,0},{5,1},{6,2},{7,3},{8,12},{9,13},{10,... | collective-permute-start | bytes 522248 | tf_op jit(solution)/shard_map/ppermute | solution.py:274
  40.6 5.4 %collective-permute-start.14 = (s16[136,512]{1,0:T(8,128)(2,1)S(1)}, s16[136,512]{1,0:T(8,128)(2,1)S(1)}, u32[]{:S(2)}, u32[]{:S(2)}) collective-permute-start(s16[136,512]{1,0:T(8,128)(2,1)S(1)} %get-tuple-element.45), channel_id=1, source_target_pairs={{0,16},{8,24},{16,0},{24,8},{1,17},{9,25},{17,1},{25,9},{2,18},{10... | collective-permute-start | bytes 417800 | tf_op jit(solution)/shard_map/ppermute | solution.py:274
  41.6 9.0 %collective-permute-start.16 = (s16[136,640]{1,0:T(8,128)(2,1)S(1)}, s16[136,640]{1,0:T(8,128)(2,1)S(1)}, u32[]{:S(2)}, u32[]{:S(2)}) collective-permute-start(s16[136,640]{1,0:T(8,128)(2,1)S(1)} %get-tuple-element.48), channel_id=1, source_target_pairs={{0,2},{1,3},{2,0},{3,1},{4,6},{5,7},{6,4},{7,5},{8,10},{9,11},{10,... | collective-permute-start | bytes 522248 | tf_op jit(solution)/shard_map/ppermute | solution.py:274
  44.0 6.6 %collective-permute-start.17 = (s16[136,512]{1,0:T(8,128)(2,1)S(1)}, s16[136,512]{1,0:T(8,128)(2,1)S(1)}, u32[]{:S(2)}, u32[]{:S(2)}) collective-permute-start(s16[136,512]{1,0:T(8,128)(2,1)S(1)} %get-tuple-element.49), channel_id=1, source_target_pairs={{0,8},{8,0},{16,24},{24,16},{1,9},{9,1},{17,25},{25,17},{2,10},{10... | collective-permute-start | bytes 417800 | tf_op jit(solution)/shard_map/ppermute | solution.py:274
  45.5 13.4 %collective-permute-start.19 = (s16[136,1152]{1,0:T(8,128)(2,1)S(1)}, s16[136,1152]{1,0:T(8,128)(2,1)S(1)}, u32[]{:S(2)}, u32[]{:S(2)}) collective-permute-start(s16[136,1152]{1,0:T(8,128)(2,1)S(1)} %get-tuple-element.53), channel_id=1, source_target_pairs={{0,16},{8,24},{16,0},{24,8},{1,17},{9,25},{17,1},{25,9},{2,18},{10... | collective-permute-start | bytes 940040 | tf_op jit(solution)/shard_map/ppermute | solution.py:274
  46.0 12.9 %collective-permute-start.11 = (s16[136,1152]{1,0:T(8,128)(2,1)S(1)}, s16[136,1152]{1,0:T(8,128)(2,1)S(1)}, u32[]{:S(2)}, u32[]{:S(2)}) collective-permute-start(s16[136,1152]{1,0:T(8,128)(2,1)S(1)} %get-tuple-element.42), channel_id=1, source_target_pairs={{0,8},{8,0},{16,24},{24,16},{1,9},{9,1},{17,25},{25,17},{2,10},{10... | collective-permute-start | bytes 940040 | tf_op jit(solution)/shard_map/ppermute | solution.py:274
  50.0 8.6 %collective-permute-start.15 = (s16[136,512]{1,0:T(8,128)(2,1)S(1)}, s16[136,512]{1,0:T(8,128)(2,1)S(1)}, u32[]{:S(2)}, u32[]{:S(2)}) collective-permute-start(s16[136,512]{1,0:T(8,128)(2,1)S(1)} %passed_sum.6.refs_3_), channel_id=1, source_target_pairs={{0,4},{1,5},{2,6},{3,7},{4,0},{5,1},{6,2},{7,3},{8,12},{9,13},{10,... | collective-permute-start | bytes 417800 | tf_op jit(solution)/shard_map/ppermute | solution.py:274
  50.7 8.1 %collective-permute-start.18 = (s16[136,512]{1,0:T(8,128)(2,1)S(1)}, s16[136,512]{1,0:T(8,128)(2,1)S(1)}, u32[]{:S(2)}, u32[]{:S(2)}) collective-permute-start(s16[136,512]{1,0:T(8,128)(2,1)S(1)} %passed_sum.7), channel_id=1, source_target_pairs={{0,2},{1,3},{2,0},{3,1},{4,6},{5,7},{6,4},{7,5},{8,10},{9,11},{10,... | collective-permute-start | bytes 417800 | tf_op jit(solution)/shard_map/ppermute | solution.py:274

commit v18 on v14

--- a/solution.py
+++ b/solution.py
@@ -82,7 +82,7 @@
     return piece(block, (0, size), tile)[...].astype(jnp.int32).astype(jnp.float32) * gain
 
 
-def call(kernel, name, operands, out_shape, scratch, room, cost, after=(), held_back=()):
+def call(kernel, name, operands, out_shape, scratch, room, cost, after=(), held_back=(), out_spec=VMEM):
     arrays = [a for a, _ in operands]
     held = sum(math.prod(a.shape) * a.dtype.itemsize for a in [*arrays, *out_shape])
 
@@ -94,7 +94,7 @@
         body,
         out_shape=[*out_shape, *(jax.ShapeDtypeStruct(a.shape, a.dtype) for a in held_back)],
         in_specs=[s for _, s in operands] + [ANY] * (len(after) + len(held_back)),
-        out_specs=[VMEM] * len(out_shape) + [ANY] * len(held_back),
+        out_specs=[out_spec] * len(out_shape) + [ANY] * len(held_back),
         input_output_aliases={
             len(arrays) + len(after) + i: len(out_shape) + i for i in range(len(held_back))
         },
@@ -256,17 +256,28 @@
     operands = Operands()
     sharpness_at = operands.add(sharpness, SMEM)
     views = [(operands.add(kept, VMEM), [operands.block(b) for b in blocks]) for kept, blocks in sums]
-
-    def kernel(ins, outs):
-        for out, (kept_at, received) in zip(outs, views):
-            for tile in column_tiles(width):
+    tiles = column_tiles(width)
+
+    def kernel(ins, refs):
+        outs, held, sems = refs[: len(sums)], refs[len(sums) : -1], refs[-1]
+        copies = []
+        for k, (kept_at, received) in enumerate(views):
+            for n, tile in enumerate(tiles):
                 total = piece(whole(ins[kept_at]), (0, size), tile)[...]
                 for view in received:
                     total = total + decoded(view(ins), size, tile)
-                piece(whole(out), (0, size), tile)[...] = total * ins[sharpness_at][0]
+                source = piece(whole(held[k]), (0, size), tile)
+                source[...] = total * ins[sharpness_at][0]
+                target = piece(whole(outs[k]), (0, size), tile)
+                copies.append(pltpu.make_async_copy(source, target, sems.at[k, n]))
+                copies[-1].start()
+        for c in copies:
+            c.wait()
 
     shapes = [jax.ShapeDtypeStruct((size, width), jnp.float32)] * len(sums)
-    return call(kernel, "output_sums", operands.pairs, shapes, [], 2**21, size)
+    scratch = [pltpu.VMEM((size, width), jnp.float32) for _ in sums]
+    scratch += [pltpu.SemaphoreType.DMA((len(sums), len(tiles)))]
+    return call(kernel, "output_sums", operands.pairs, shapes, scratch, 2**22, size, out_spec=ANY)
 
 
 def swapped(array, step):

time: 60.1 us -> 60 us (level)
  no operation moved by 1% of the time
where the time goes in v18:
time: 60 us; the launch traced here: 59.8 us
  starting transfers between devices  25.1 us (42%)
  waiting for transfers between devices  18.9 us (31%)
  Pallas kernels  12.1 us (20%)
  between operations  2.13 us (4%)
  local copies, waits for them, and re-layouts  1.66 us (3%)
    ppermute x20, starting transfers between devices, swapped(): lax.ppermute(array, axis, [(i, i ^ bit) for i in range(lax.axis_size(axis...  25.1 us
    ppermute x20, waiting for transfers between devices, swapped(): lax.ppermute(array, axis, [(i, i ^ bit) for i in range(lax.axis_size(axis...  18.9 us
    pallas_call x20, Pallas kernels, call(): pl.pallas_call(body, out_shape=[*out_shape, *(jax.ShapeDtypeStruct(a.shap...  12.1 us
    unnamed x6, local copies, waits for them, and re-layouts  1.66 us
  transfers between devices with their start and end apart: 20, of which 8 were waited for; matrix products, arithmetic and copies ran while one was open for 0% of the time, Pallas kernels for 18%

profile of v18, /device:TPU:0, one launch (start us, length us, event | category | flops | bytes accessed | tf_op | source)
XLA Modules:
  0.0 59.8 jit_solution(12748639776557242188)
XLA Ops:
  0.6 4.1 %collective-permute-start = (bf16[128,1152]{1,0:T(8,128)(2,1)}, bf16[128,1152]{1,0:T(8,128)(2,1)S(1)}, u32[]{:S(2)}, u32[]{:S(2)}) collective-permute-start(bf16[128,1152]{1,0:T(8,128)(2,1)} %refs_6_.7), channel_id=1, source_target_pairs={{0,4},{1,5},{2,6},{3,7},{4,0},{5,1},{6,2},{7,3},{8,12},{9,13},{10,... | collective-permute-start | bytes 884744 | tf_op jit(solution)/shard_map/ppermute | solution.py:285
  4.7 1.6 %collective-permute-start.1 = (bf16[128,1152]{1,0:T(8,128)(2,1)}, bf16[128,1152]{1,0:T(8,128)(2,1)S(1)}, u32[]{:S(2)}, u32[]{:S(2)}) collective-permute-start(bf16[128,1152]{1,0:T(8,128)(2,1)} %refs_0_.10), channel_id=1, source_target_pairs={{0,2},{1,3},{2,0},{3,1},{4,6},{5,7},{6,4},{7,5},{8,10},{9,11},{10,... | collective-permute-start | bytes 884744 | tf_op jit(solution)/shard_map/ppermute | solution.py:285
  6.3 0.0 copy-start.1
  6.3 1.0 %copy-done.1 = bf16[128,1152]{1,0:T(8,128)(2,1)S(1)} copy-done((bf16[128,1152]{1,0:T(8,128)(2,1)S(1)}, bf16[128,1152]{1,0:T(8,128)(2,1)}, u32[]{:S(2)}) %copy-start.1) | copy-done | bytes 294936
  7.3 0.0 copy-start.2
  7.3 0.7 %copy-done.2 = s32[128]{0:T(128)S(1)} copy-done((s32[128]{0:T(128)S(1)}, s32[128]{0:T(128)}, u32[]{:S(2)}) %copy-start.2) | copy-done | bytes 536
  8.0 0.0 copy-start
  8.0 1.6 %collective-permute-start.4 = (bf16[136,1152]{1,0:T(8,128)(2,1)S(1)}, bf16[136,1152]{1,0:T(8,128)(2,1)S(1)}, u32[]{:S(2)}, u32[]{:S(2)}) collective-permute-start(bf16[136,1152]{1,0:T(8,128)(2,1)S(1)} %labelled.3.refs_2_.refs_7_.refs_4_), channel_id=1, source_target_pairs={{0,8},{8,0},{16,24},{24,16},{1,9},{9,1},{17,25},{25,17},{2,10},{10... | collective-permute-start | bytes 940040 | tf_op jit(solution)/shard_map/ppermute | solution.py:285
  9.6 1.5 %collective-permute-start.3 = (bf16[128,1152]{1,0:T(8,128)(2,1)}, bf16[128,1152]{1,0:T(8,128)(2,1)S(1)}, u32[]{:S(2)}, u32[]{:S(2)}) collective-permute-start(bf16[128,1152]{1,0:T(8,128)(2,1)} %refs_6_.7), channel_id=1, source_target_pairs={{0,16},{8,24},{16,0},{24,8},{1,17},{9,25},{17,1},{25,9},{2,18},{10... | collective-permute-start | bytes 884744 | tf_op jit(solution)/shard_map/ppermute | solution.py:285
  11.1 0.4 collective-permute-start.2
  11.5 6.8 %collective-permute-done.refs_0_ = bf16[128,1152]{1,0:T(8,128)(2,1)S(1)} collective-permute-done((bf16[128,1152]{1,0:T(8,128)(2,1)}, bf16[128,1152]{1,0:T(8,128)(2,1)S(1)}, u32[]{:S(2)}, u32[]{:S(2)}) %collective-permute-start) | collective-permute-done | bytes 294944 | tf_op jit(solution)/shard_map/ppermute | solution.py:285
  18.4 0.3 collective-permute-done.2.refs_1_
  18.6 0.0 collective-permute-done.1.refs_0_
  18.7 0.0 collective-permute-done.3.refs_3_.refs_4_.refs_6_
  18.7 0.0 collective-permute-done.4.refs_4_.refs_5_.refs_6_
  18.7 0.0 copy-done
  18.8 0.1 bundled.3
  18.9 0.1 collective-permute-start.7
  19.0 1.6 %collective-permute-start.6 = (bf16[136,1152]{1,0:T(8,128)(2,1)S(1)}, bf16[136,1152]{1,0:T(8,128)(2,1)S(1)}, u32[]{:S(2)}, u32[]{:S(2)}) collective-permute-start(bf16[136,1152]{1,0:T(8,128)(2,1)S(1)} %labelled.2.refs_1_.refs_3_.refs_5_), channel_id=1, source_target_pairs={{0,8},{8,0},{16,24},{24,16},{1,9},{9,1},{17,25},{25,17},{2,10},{10... | collective-permute-start | bytes 940040 | tf_op jit(solution)/shard_map/ppermute | solution.py:285
  20.6 1.5 %collective-permute-start.5 = (bf16[128,1152]{1,0:T(8,128)(2,1)S(1)}, bf16[128,1152]{1,0:T(8,128)(2,1)S(1)}, u32[]{:S(2)}, u32[]{:S(2)}) collective-permute-start(bf16[128,1152]{1,0:T(8,128)(2,1)S(1)} %held.3.refs_2_.refs_0_.refs_5_), channel_id=1, source_target_pairs={{0,16},{8,24},{16,0},{24,8},{1,17},{9,25},{17,1},{25,9},{2,18},{10... | collective-permute-start | bytes 884744 | tf_op jit(solution)/shard_map/ppermute | solution.py:285
  23.4 0.0 collective-permute-done.7.refs_8_.refs_7_
  23.4 1.9 %early_sums.3 = (f32[128,1152]{1,0:T(8,128)S(1)}, f32[128,1152]{1,0:T(8,128)S(1)}, f32[128,1152]{1,0:T(8,128)S(1)}) custom-call(f32[1]{0:T(128)S(6)} %copy.25.refs_0_, f32[1]{0:T(128)S(6)} %copy.26.refs_1_, bf16[128,1152]{1,0:T(8,128)(2,1)S(1)} %held.3.refs_2_.refs_0_.refs_5_, bf16[136,1152]{1,0:T(8,128)(2,1)S(1)} %labelled.2.refs_1_.refs_3_.refs_5_, ...), custom_call_target="tpu_custom_call" | custom-call | flops 2304 | bytes 2304 | tf_op jit(solution)/shard_map/early_sums/pallas_call | solution.py:93
  25.3 1.9 %early_sums.2 = (f32[128,1152]{1,0:T(8,128)S(1)}, f32[128,1152]{1,0:T(8,128)S(1)}, f32[128,1152]{1,0:T(8,128)S(1)}) custom-call(f32[1]{0:T(128)S(6)} %copy.25.refs_0_, f32[1]{0:T(128)S(6)} %copy.26.refs_1_, bf16[128,1152]{1,0:T(8,128)(2,1)S(1)} %held.3.refs_2_.refs_0_.refs_5_, bf16[136,1152]{1,0:T(8,128)(2,1)S(1)} %labelled.2.refs_1_.refs_3_.refs_5_, ...), custom_call_target="tpu_custom_call" | custom-call | flops 2304 | bytes 2304 | tf_op jit(solution)/shard_map/early_sums/pallas_call | solution.py:93
  27.3 2.4 %collective-permute-done.5.refs_2_.refs_8_ = bf16[128,1152]{1,0:T(8,128)(2,1)S(1)} collective-permute-done((bf16[128,1152]{1,0:T(8,128)(2,1)S(1)}, bf16[128,1152]{1,0:T(8,128)(2,1)S(1)}, u32[]{:S(2)}, u32[]{:S(2)}) %collective-permute-start.5) | collective-permute-done | bytes 294944 | tf_op jit(solution)/shard_map/ppermute | solution.py:285
  29.7 0.0 collective-permute-done.6.refs_3_.refs_8_
  29.7 0.0 collective-permute-start.9
  29.7 0.5 collective-permute-start.8
  30.2 1.3 %late_rows_begun.2.refs_5_ = f32[128,1152]{1,0:T(8,128)S(1)} custom-call(f32[1]{0:T(128)S(6)} %copy.25.refs_0_, f32[1]{0:T(128)S(6)} %copy.26.refs_1_, bf16[128,1152]{1,0:T(8,128)(2,1)S(1)} %collective-permute-done.5.refs_2_.refs_8_, bf16[136,1152]{1,0:T(8,128)(2,1)S(1)} %collective-permute-done.6.refs_3_.refs_8_, ...), custom_call_target="tpu_custom_call" | custom-call | flops 896 | bytes 896 | tf_op jit(solution)/shard_map/late_rows_begun/pallas_call | solution.py:93
  31.5 0.0 collective-permute-done.9.refs_4_.refs_9_
  31.5 0.6 %late_rows.2 = (s16[136,640]{1,0:T(8,128)(2,1)S(1)}, s16[136,512]{1,0:T(8,128)(2,1)S(1)}) custom-call(f32[1]{0:T(128)S(6)} %copy.25.refs_0_, f32[1]{0:T(128)S(6)} %copy.26.refs_1_, bf16[128,1152]{1,0:T(8,128)(2,1)S(1)} %collective-permute-done.5.refs_2_.refs_8_, bf16[136,1152]{1,0:T(8,128)(2,1)S(1)} %collective-permute-done.6.refs_3_.refs_8_, ...), custom_call_target="tpu_custom_call" | custom-call | flops 128 | bytes 128 | tf_op jit(solution)/shard_map/late_rows/pallas_call | solution.py:93
  32.2 1.6 %collective-permute-start.12 = (s16[136,640]{1,0:T(8,128)(2,1)S(1)}, s16[136,640]{1,0:T(8,128)(2,1)S(1)}, u32[]{:S(2)}, u32[]{:S(2)}) collective-permute-start(s16[136,640]{1,0:T(8,128)(2,1)S(1)} %get-tuple-element.50.refs_8_), channel_id=1, source_target_pairs={{0,16},{8,24},{16,0},{24,8},{1,17},{9,25},{17,1},{25,9},{2,18},{10... | collective-permute-start | bytes 522248 | tf_op jit(solution)/shard_map/ppermute | solution.py:285
  33.7 1.3 %late_rows_begun.3.refs_5_ = f32[128,1152]{1,0:T(8,128)S(1)} custom-call(f32[1]{0:T(128)S(6)} %copy.25.refs_0_, f32[1]{0:T(128)S(6)} %copy.26.refs_1_, bf16[128,1152]{1,0:T(8,128)(2,1)S(1)} %collective-permute-done.5.refs_2_.refs_8_, bf16[136,1152]{1,0:T(8,128)(2,1)S(1)} %collective-permute-done.6.refs_3_.refs_8_, bf16[128,1152]{1,0:T(8,128)(2,1)S(1)} %copy-done, ...), custom_call_target="tpu_custom_call" | custom-call | flops 896 | bytes 896 | tf_op jit(solution)/shard_map/late_rows_begun/pallas_call | solution.py:93
  35.1 0.0 collective-permute-done.8.refs_4_.refs_9_
  35.1 0.6 %late_rows.3 = (s16[136,640]{1,0:T(8,128)(2,1)S(1)}, s16[136,512]{1,0:T(8,128)(2,1)S(1)}) custom-call(f32[1]{0:T(128)S(6)} %copy.25.refs_0_, f32[1]{0:T(128)S(6)} %copy.26.refs_1_, bf16[128,1152]{1,0:T(8,128)(2,1)S(1)} %collective-permute-done.5.refs_2_.refs_8_, bf16[136,1152]{1,0:T(8,128)(2,1)S(1)} %collective-permute-done.6.refs_3_.refs_8_, ...), custom_call_target="tpu_custom_call" | custom-call | flops 128 | bytes 128 | tf_op jit(solution)/shard_map/late_rows/pallas_call | solution.py:93
  35.7 0.7 %collective-permute-start.10 = (s16[136,640]{1,0:T(8,128)(2,1)S(1)}, s16[136,640]{1,0:T(8,128)(2,1)S(1)}, u32[]{:S(2)}, u32[]{:S(2)}) collective-permute-start(s16[136,640]{1,0:T(8,128)(2,1)S(1)} %get-tuple-element.52.refs_13_), channel_id=1, source_target_pairs={{0,8},{8,0},{16,24},{24,16},{1,9},{9,1},{17,25},{25,17},{2,10},{10... | collective-permute-start | bytes 522248 | tf_op jit(solution)/shard_map/ppermute | solution.py:285
  36.4 1.3 %late_columns.2 = (f32[128,1152]{1,0:T(8,128)S(1)}, f32[128,1152]{1,0:T(8,128)S(1)}, s16[136,1152]{1,0:T(8,128)(2,1)S(1)}) custom-call(f32[1]{0:T(128)S(6)} %copy.25.refs_0_, f32[1]{0:T(128)S(6)} %copy.26.refs_1_, bf16[128,1152]{1,0:T(8,128)(2,1)S(1)} %held.3.refs_2_.refs_0_.refs_5_, bf16[136,1152]{1,0:T(8,128)(2,1)S(1)} %labelled.2.refs_1_.refs_3_.refs_5_, ...), custom_call_target="tpu_custom_call" | custom-call | flops 768 | bytes 768 | tf_op jit(solution)/shard_map/late_columns/pallas_call | solution.py:93
  37.7 1.3 %late_columns.3 = (f32[128,1152]{1,0:T(8,128)S(1)}, f32[128,1152]{1,0:T(8,128)S(1)}, s16[136,1152]{1,0:T(8,128)(2,1)S(1)}) custom-call(f32[1]{0:T(128)S(6)} %copy.25.refs_0_, f32[1]{0:T(128)S(6)} %copy.26.refs_1_, bf16[128,1152]{1,0:T(8,128)(2,1)S(1)} %held.3.refs_2_.refs_0_.refs_5_, bf16[136,1152]{1,0:T(8,128)(2,1)S(1)} %labelled.2.refs_1_.refs_3_.refs_5_, ...), custom_call_target="tpu_custom_call" | custom-call | flops 768 | bytes 768 | tf_op jit(solution)/shard_map/late_columns/pallas_call | solution.py:93
  39.0 0.0 collective-permute-done.12.refs_1_
  39.1 0.1 passed_sum.5
  39.2 1.4 %collective-permute-start.13 = (s16[136,640]{1,0:T(8,128)(2,1)S(1)}, s16[136,640]{1,0:T(8,128)(2,1)S(1)}, u32[]{:S(2)}, u32[]{:S(2)}) collective-permute-start(s16[136,640]{1,0:T(8,128)(2,1)S(1)} %get-tuple-element.60), channel_id=1, source_target_pairs={{0,4},{1,5},{2,6},{3,7},{4,0},{5,1},{6,2},{7,3},{8,12},{9,13},{10,... | collective-permute-start | bytes 522248 | tf_op jit(solution)/shard_map/ppermute | solution.py:285
  40.6 1.0 %collective-permute-start.14 = (s16[136,512]{1,0:T(8,128)(2,1)S(1)}, s16[136,512]{1,0:T(8,128)(2,1)S(1)}, u32[]{:S(2)}, u32[]{:S(2)}) collective-permute-start(s16[136,512]{1,0:T(8,128)(2,1)S(1)} %get-tuple-element.61), channel_id=1, source_target_pairs={{0,16},{8,24},{16,0},{24,8},{1,17},{9,25},{17,1},{25,9},{2,18},{10... | collective-permute-start | bytes 417800 | tf_op jit(solution)/shard_map/ppermute | solution.py:285
  41.6 0.2 collective-permute-done.10.refs_1_
  41.8 0.1 passed_sum.4
  41.9 2.2 %collective-permute-start.16 = (s16[136,640]{1,0:T(8,128)(2,1)S(1)}, s16[136,640]{1,0:T(8,128)(2,1)S(1)}, u32[]{:S(2)}, u32[]{:S(2)}) collective-permute-start(s16[136,640]{1,0:T(8,128)(2,1)S(1)} %get-tuple-element.64), channel_id=1, source_target_pairs={{0,2},{1,3},{2,0},{3,1},{4,6},{5,7},{6,4},{7,5},{8,10},{9,11},{10,... | collective-permute-start | bytes 522248 | tf_op jit(solution)/shard_map/ppermute | solution.py:285
  44.1 0.8 %collective-permute-start.17 = (s16[136,512]{1,0:T(8,128)(2,1)S(1)}, s16[136,512]{1,0:T(8,128)(2,1)S(1)}, u32[]{:S(2)}, u32[]{:S(2)}) collective-permute-start(s16[136,512]{1,0:T(8,128)(2,1)S(1)} %get-tuple-element.65), channel_id=1, source_target_pairs={{0,8},{8,0},{16,24},{24,16},{1,9},{9,1},{17,25},{25,17},{2,10},{10... | collective-permute-start | bytes 417800 | tf_op jit(solution)/shard_map/ppermute | solution.py:285
  45.0 1.5 %collective-permute-start.19 = (s16[136,1152]{1,0:T(8,128)(2,1)S(1)}, s16[136,1152]{1,0:T(8,128)(2,1)S(1)}, u32[]{:S(2)}, u32[]{:S(2)}) collective-permute-start(s16[136,1152]{1,0:T(8,128)(2,1)S(1)} %get-tuple-element.69), channel_id=1, source_target_pairs={{0,16},{8,24},{16,0},{24,8},{1,17},{9,25},{17,1},{25,9},{2,18},{10... | collective-permute-start | bytes 940040 | tf_op jit(solution)/shard_map/ppermute | solution.py:285
  46.5 0.0 collective-permute-done.14.refs_1_
  46.5 0.7 %collective-permute-start.11 = (s16[136,1152]{1,0:T(8,128)(2,1)S(1)}, s16[136,1152]{1,0:T(8,128)(2,1)S(1)}, u32[]{:S(2)}, u32[]{:S(2)}) collective-permute-start(s16[136,1152]{1,0:T(8,128)(2,1)S(1)} %get-tuple-element.58), channel_id=1, source_target_pairs={{0,8},{8,0},{16,24},{24,16},{1,9},{9,1},{17,25},{25,17},{2,10},{10... | collective-permute-start | bytes 940040 | tf_op jit(solution)/shard_map/ppermute | solution.py:285
  47.2 2.5 %collective-permute-done.13.refs_2_.refs_0_ = s16[136,640]{1,0:T(8,128)(2,1)S(1)} collective-permute-done((s16[136,640]{1,0:T(8,128)(2,1)S(1)}, s16[136,640]{1,0:T(8,128)(2,1)S(1)}, u32[]{:S(2)}, u32[]{:S(2)}) %collective-permute-start.13) | collective-permute-done | bytes 174112 | tf_op jit(solution)/shard_map/ppermute | solution.py:285
  49.7 0.1 passed_sum.6.refs_3_
  49.8 0.1 collective-permute-start.15
  49.9 0.7 %collective-permute-done.17.refs_1_ = s16[136,512]{1,0:T(8,128)(2,1)S(1)} collective-permute-done((s16[136,512]{1,0:T(8,128)(2,1)S(1)}, s16[136,512]{1,0:T(8,128)(2,1)S(1)}, u32[]{:S(2)}, u32[]{:S(2)}) %collective-permute-start.17) | collective-permute-done | bytes 139296 | tf_op jit(solution)/shard_map/ppermute | solution.py:285
  50.6 0.0 collective-permute-done.16.refs_2_
  50.6 0.1 passed_sum.7
  50.7 2.1 %collective-permute-start.18 = (s16[136,512]{1,0:T(8,128)(2,1)S(1)}, s16[136,512]{1,0:T(8,128)(2,1)S(1)}, u32[]{:S(2)}, u32[]{:S(2)}) collective-permute-start(s16[136,512]{1,0:T(8,128)(2,1)S(1)} %passed_sum.7), channel_id=1, source_target_pairs={{0,2},{1,3},{2,0},{3,1},{4,6},{5,7},{6,4},{7,5},{8,10},{9,11},{10,... | collective-permute-start | bytes 417800 | tf_op jit(solution)/shard_map/ppermute | solution.py:285
  52.9 5.6 %collective-permute-done.15.refs_1_ = s16[136,512]{1,0:T(8,128)(2,1)S(1)} collective-permute-done((s16[136,512]{1,0:T(8,128)(2,1)S(1)}, s16[136,512]{1,0:T(8,128)(2,1)S(1)}, u32[]{:S(2)}, u32[]{:S(2)}) %collective-permute-start.15) | collective-permute-done | bytes 139296 | tf_op jit(solution)/shard_map/ppermute | solution.py:285
  58.4 0.2 collective-permute-done.18.refs_3_
  58.7 0.0 collective-permute-done.19.refs_6_
  58.7 0.0 collective-permute-done.11.refs_2_
  58.7 1.1 %output_sums.1 = (f32[128,1152]{1,0:T(8,128)}, f32[128,1152]{1,0:T(8,128)}) custom-call(f32[1]{0:T(128)S(6)} %copy.25.refs_0_, f32[128,1152]{1,0:T(8,128)S(1)} %get-tuple-element.55.refs_1_, s16[136,1152]{1,0:T(8,128)(2,1)S(1)} %collective-permute-done.11.refs_2_, s16[136,640]{1,0:T(8,128)(2,1)S(1)} %get-tuple-element.66.refs_3_, ...), custom_call_target="tpu_custom_call" | custom-call | flops 128 | bytes 128 | tf_op jit(solution)/shard_map/output_sums/pallas_call | solution.py:93
  (6 shorter events, 0.1 us)
Async XLA Ops:
  0.6 17.8 %collective-permute-start = (bf16[128,1152]{1,0:T(8,128)(2,1)}, bf16[128,1152]{1,0:T(8,128)(2,1)S(1)}, u32[]{:S(2)}, u32[]{:S(2)}) collective-permute-start(bf16[128,1152]{1,0:T(8,128)(2,1)} %refs_6_.7), channel_id=1, source_target_pairs={{0,4},{1,5},{2,6},{3,7},{4,0},{5,1},{6,2},{7,3},{8,12},{9,13},{10,... | collective-permute-start | bytes 884744 | tf_op jit(solution)/shard_map/ppermute | solution.py:285
  4.7 13.9 %collective-permute-start.1 = (bf16[128,1152]{1,0:T(8,128)(2,1)}, bf16[128,1152]{1,0:T(8,128)(2,1)S(1)}, u32[]{:S(2)}, u32[]{:S(2)}) collective-permute-start(bf16[128,1152]{1,0:T(8,128)(2,1)} %refs_0_.10), channel_id=1, source_target_pairs={{0,2},{1,3},{2,0},{3,1},{4,6},{5,7},{6,4},{7,5},{8,10},{9,11},{10,... | collective-permute-start | bytes 884744 | tf_op jit(solution)/shard_map/ppermute | solution.py:285
  6.3 1.0 %copy-start.1 = (bf16[128,1152]{1,0:T(8,128)(2,1)S(1)}, bf16[128,1152]{1,0:T(8,128)(2,1)}, u32[]{:S(2)}) copy-start(bf16[128,1152]{1,0:T(8,128)(2,1)} %refs_0_.10) | copy-start | bytes 884740
  7.3 0.7 %copy-start.2 = (s32[128]{0:T(128)S(1)}, s32[128]{0:T(128)}, u32[]{:S(2)}) copy-start(s32[128]{0:T(128)} %param.7) | copy-start | bytes 1540
  8.0 10.8 %copy-start = (bf16[128,1152]{1,0:T(8,128)(2,1)S(1)}, bf16[128,1152]{1,0:T(8,128)(2,1)}, u32[]{:S(2)}) copy-start(bf16[128,1152]{1,0:T(8,128)(2,1)} %refs_6_.7) | copy-start | bytes 884740
  8.0 10.7 %collective-permute-start.4 = (bf16[136,1152]{1,0:T(8,128)(2,1)S(1)}, bf16[136,1152]{1,0:T(8,128)(2,1)S(1)}, u32[]{:S(2)}, u32[]{:S(2)}) collective-permute-start(bf16[136,1152]{1,0:T(8,128)(2,1)S(1)} %labelled.3.refs_2_.refs_7_.refs_4_), channel_id=1, source_target_pairs={{0,8},{8,0},{16,24},{24,16},{1,9},{9,1},{17,25},{25,17},{2,10},{10... | collective-permute-start | bytes 940040 | tf_op jit(solution)/shard_map/ppermute | solution.py:285
  9.6 9.2 %collective-permute-start.3 = (bf16[128,1152]{1,0:T(8,128)(2,1)}, bf16[128,1152]{1,0:T(8,128)(2,1)S(1)}, u32[]{:S(2)}, u32[]{:S(2)}) collective-permute-start(bf16[128,1152]{1,0:T(8,128)(2,1)} %refs_6_.7), channel_id=1, source_target_pairs={{0,16},{8,24},{16,0},{24,8},{1,17},{9,25},{17,1},{25,9},{2,18},{10... | collective-permute-start | bytes 884744 | tf_op jit(solution)/shard_map/ppermute | solution.py:285
  11.1 7.6 %collective-permute-start.2 = (s32[1,128]{1,0:T(1,128)S(1)}, s32[1,128]{1,0:T(1,128)S(1)}, u32[]{:S(2)}, u32[]{:S(2)}) collective-permute-start(s32[1,128]{1,0:T(1,128)S(1)} %bitcast.2), channel_id=1, source_target_pairs={{0,2},{1,3},{2,0},{3,1},{4,6},{5,7},{6,4},{7,5},{8,10},{9,11},{10,... | collective-permute-start | bytes 1544 | tf_op jit(solution)/shard_map/ppermute | solution.py:285
  18.9 4.5 %collective-permute-start.7 = (bf16[792,1152]{1,0:T(8,128)(2,1)S(1)}, bf16[792,1152]{1,0:T(8,128)(2,1)S(1)}, u32[]{:S(2)}, u32[]{:S(2)}) collective-permute-start(bf16[792,1152]{1,0:T(8,128)(2,1)S(1)} %bundled.3), channel_id=1, source_target_pairs={{0,1},{1,0},{2,3},{3,2},{4,5},{5,4},{6,7},{7,6},{8,9},{9,8},{10,11... | collective-permute-start | bytes 5474312 | tf_op jit(solution)/shard_map/ppermute | solution.py:285
  19.0 10.7 %collective-permute-start.6 = (bf16[136,1152]{1,0:T(8,128)(2,1)S(1)}, bf16[136,1152]{1,0:T(8,128)(2,1)S(1)}, u32[]{:S(2)}, u32[]{:S(2)}) collective-permute-start(bf16[136,1152]{1,0:T(8,128)(2,1)S(1)} %labelled.2.refs_1_.refs_3_.refs_5_), channel_id=1, source_target_pairs={{0,8},{8,0},{16,24},{24,16},{1,9},{9,1},{17,25},{25,17},{2,10},{10... | collective-permute-start | bytes 940040 | tf_op jit(solution)/shard_map/ppermute | solution.py:285
  20.6 9.1 %collective-permute-start.5 = (bf16[128,1152]{1,0:T(8,128)(2,1)S(1)}, bf16[128,1152]{1,0:T(8,128)(2,1)S(1)}, u32[]{:S(2)}, u32[]{:S(2)}) collective-permute-start(bf16[128,1152]{1,0:T(8,128)(2,1)S(1)} %held.3.refs_2_.refs_0_.refs_5_), channel_id=1, source_target_pairs={{0,16},{8,24},{16,0},{24,8},{1,17},{9,25},{17,1},{25,9},{2,18},{10... | collective-permute-start | bytes 884744 | tf_op jit(solution)/shard_map/ppermute | solution.py:285
  29.7 1.9 %collective-permute-start.9 = (bf16[136,1152]{1,0:T(8,128)(2,1)S(1)}, bf16[136,1152]{1,0:T(8,128)(2,1)S(1)}, u32[]{:S(2)}, u32[]{:S(2)}) collective-permute-start(bf16[136,1152]{1,0:T(8,128)(2,1)S(1)} %collective-permute-done.6.refs_3_.refs_8_), channel_id=1, source_target_pairs={{0,1},{1,0},{2,3},{3,2},{4,5},{5,4},{6,7},{7,6},{8,9},{9,8},{10,11... | collective-permute-start | bytes 940040 | tf_op jit(solution)/shard_map/ppermute | solution.py:285
  29.7 5.4 %collective-permute-start.8 = (bf16[128,1152]{1,0:T(8,128)(2,1)S(1)}, bf16[128,1152]{1,0:T(8,128)(2,1)S(1)}, u32[]{:S(2)}, u32[]{:S(2)}) collective-permute-start(bf16[128,1152]{1,0:T(8,128)(2,1)S(1)} %collective-permute-done.5.refs_2_.refs_8_), channel_id=1, source_target_pairs={{0,1},{1,0},{2,3},{3,2},{4,5},{5,4},{6,7},{7,6},{8,9},{9,8},{10,11... | collective-permute-start | bytes 884744 | tf_op jit(solution)/shard_map/ppermute | solution.py:285
  32.2 6.9 %collective-permute-start.12 = (s16[136,640]{1,0:T(8,128)(2,1)S(1)}, s16[136,640]{1,0:T(8,128)(2,1)S(1)}, u32[]{:S(2)}, u32[]{:S(2)}) collective-permute-start(s16[136,640]{1,0:T(8,128)(2,1)S(1)} %get-tuple-element.50.refs_8_), channel_id=1, source_target_pairs={{0,16},{8,24},{16,0},{24,8},{1,17},{9,25},{17,1},{25,9},{2,18},{10... | collective-permute-start | bytes 522248 | tf_op jit(solution)/shard_map/ppermute | solution.py:285
  35.7 6.1 %collective-permute-start.10 = (s16[136,640]{1,0:T(8,128)(2,1)S(1)}, s16[136,640]{1,0:T(8,128)(2,1)S(1)}, u32[]{:S(2)}, u32[]{:S(2)}) collective-permute-start(s16[136,640]{1,0:T(8,128)(2,1)S(1)} %get-tuple-element.52.refs_13_), channel_id=1, source_target_pairs={{0,8},{8,0},{16,24},{24,16},{1,9},{9,1},{17,25},{25,17},{2,10},{10... | collective-permute-start | bytes 522248 | tf_op jit(solution)/shard_map/ppermute | solution.py:285
  39.2 10.6 %collective-permute-start.13 = (s16[136,640]{1,0:T(8,128)(2,1)S(1)}, s16[136,640]{1,0:T(8,128)(2,1)S(1)}, u32[]{:S(2)}, u32[]{:S(2)}) collective-permute-start(s16[136,640]{1,0:T(8,128)(2,1)S(1)} %get-tuple-element.60), channel_id=1, source_target_pairs={{0,4},{1,5},{2,6},{3,7},{4,0},{5,1},{6,2},{7,3},{8,12},{9,13},{10,... | collective-permute-start | bytes 522248 | tf_op jit(solution)/shard_map/ppermute | solution.py:285
  40.6 5.9 %collective-permute-start.14 = (s16[136,512]{1,0:T(8,128)(2,1)S(1)}, s16[136,512]{1,0:T(8,128)(2,1)S(1)}, u32[]{:S(2)}, u32[]{:S(2)}) collective-permute-start(s16[136,512]{1,0:T(8,128)(2,1)S(1)} %get-tuple-element.61), channel_id=1, source_target_pairs={{0,16},{8,24},{16,0},{24,8},{1,17},{9,25},{17,1},{25,9},{2,18},{10... | collective-permute-start | bytes 417800 | tf_op jit(solution)/shard_map/ppermute | solution.py:285
  41.9 8.7 %collective-permute-start.16 = (s16[136,640]{1,0:T(8,128)(2,1)S(1)}, s16[136,640]{1,0:T(8,128)(2,1)S(1)}, u32[]{:S(2)}, u32[]{:S(2)}) collective-permute-start(s16[136,640]{1,0:T(8,128)(2,1)S(1)} %get-tuple-element.64), channel_id=1, source_target_pairs={{0,2},{1,3},{2,0},{3,1},{4,6},{5,7},{6,4},{7,5},{8,10},{9,11},{10,... | collective-permute-start | bytes 522248 | tf_op jit(solution)/shard_map/ppermute | solution.py:285
  44.1 6.5 %collective-permute-start.17 = (s16[136,512]{1,0:T(8,128)(2,1)S(1)}, s16[136,512]{1,0:T(8,128)(2,1)S(1)}, u32[]{:S(2)}, u32[]{:S(2)}) collective-permute-start(s16[136,512]{1,0:T(8,128)(2,1)S(1)} %get-tuple-element.65), channel_id=1, source_target_pairs={{0,8},{8,0},{16,24},{24,16},{1,9},{9,1},{17,25},{25,17},{2,10},{10... | collective-permute-start | bytes 417800 | tf_op jit(solution)/shard_map/ppermute | solution.py:285
  45.0 13.7 %collective-permute-start.19 = (s16[136,1152]{1,0:T(8,128)(2,1)S(1)}, s16[136,1152]{1,0:T(8,128)(2,1)S(1)}, u32[]{:S(2)}, u32[]{:S(2)}) collective-permute-start(s16[136,1152]{1,0:T(8,128)(2,1)S(1)} %get-tuple-element.69), channel_id=1, source_target_pairs={{0,16},{8,24},{16,0},{24,8},{1,17},{9,25},{17,1},{25,9},{2,18},{10... | collective-permute-start | bytes 940040 | tf_op jit(solution)/shard_map/ppermute | solution.py:285
  46.5 12.2 %collective-permute-start.11 = (s16[136,1152]{1,0:T(8,128)(2,1)S(1)}, s16[136,1152]{1,0:T(8,128)(2,1)S(1)}, u32[]{:S(2)}, u32[]{:S(2)}) collective-permute-start(s16[136,1152]{1,0:T(8,128)(2,1)S(1)} %get-tuple-element.58), channel_id=1, source_target_pairs={{0,8},{8,0},{16,24},{24,16},{1,9},{9,1},{17,25},{25,17},{2,10},{10... | collective-permute-start | bytes 940040 | tf_op jit(solution)/shard_map/ppermute | solution.py:285
  49.8 8.6 %collective-permute-start.15 = (s16[136,512]{1,0:T(8,128)(2,1)S(1)}, s16[136,512]{1,0:T(8,128)(2,1)S(1)}, u32[]{:S(2)}, u32[]{:S(2)}) collective-permute-start(s16[136,512]{1,0:T(8,128)(2,1)S(1)} %passed_sum.6.refs_3_), channel_id=1, source_target_pairs={{0,4},{1,5},{2,6},{3,7},{4,0},{5,1},{6,2},{7,3},{8,12},{9,13},{10,... | collective-permute-start | bytes 417800 | tf_op jit(solution)/shard_map/ppermute | solution.py:285
  50.7 8.0 %collective-permute-start.18 = (s16[136,512]{1,0:T(8,128)(2,1)S(1)}, s16[136,512]{1,0:T(8,128)(2,1)S(1)}, u32[]{:S(2)}, u32[]{:S(2)}) collective-permute-start(s16[136,512]{1,0:T(8,128)(2,1)S(1)} %passed_sum.7), channel_id=1, source_target_pairs={{0,2},{1,3},{2,0},{3,1},{4,6},{5,7},{6,4},{7,5},{8,10},{9,11},{10,... | collective-permute-start | bytes 417800 | tf_op jit(solution)/shard_map/ppermute | solution.py:285

commit v19 on v16

--- a/solution.py
+++ b/solution.py
@@ -119,6 +119,22 @@
     shape = jax.ShapeDtypeStruct((size + EXTRA_ROWS, width), jnp.bfloat16)
     operands = [(images, VMEM), (labels, VMEM)]
     return call(kernel, "labelled", operands, [shape], [], 2**21, size, after)[0]
+
+
+def crossed(texts, images):
+    size = texts.shape[0]
+
+    def kernel(ins, outs):
+        def write(texts_out, images_out):
+            texts_out[pl.ds(0, size), :] = ins[0][...]
+            texts_out[pl.ds(size, EXTRA_ROWS), :] = jnp.zeros((EXTRA_ROWS, texts.shape[1]), jnp.bfloat16)
+            images_out[...] = ins[1][...]
+
+        for core, order in enumerate((outs, outs[::-1])):
+            pl.when(core_number() == core)(lambda order=order: write(*order))
+
+    shapes = [jax.ShapeDtypeStruct(images.shape, jnp.bfloat16)] * 2
+    return call(kernel, "crossed", [(texts, VMEM), (images, VMEM)], shapes, [], 2**21, size)
 
 
 def bundled(arrays, cost):
@@ -259,17 +275,13 @@
     sharpness_at = operands.add(sharpness, SMEM)
     views = [(operands.add(kept, VMEM), [operands.block(b) for b in blocks]) for kept, blocks in sums]
 
-    def write(ins, outs):
+    def kernel(ins, outs):
         for out, (kept_at, received) in zip(outs, views):
             for tile in column_tiles(width):
                 total = piece(whole(ins[kept_at]), (0, size), tile)[...]
                 for view in received:
                     total = total + decoded(view(ins), size, tile)
                 piece(whole(out), (0, size), tile)[...] = total * ins[sharpness_at][0]
-
-    def kernel(ins, outs):
-        for core, order in enumerate((outs[::-1], outs)):
-            pl.when(core_number() == core)(lambda order=order: write(ins, order))
 
     shapes = [jax.ShapeDtypeStruct((size, width), jnp.float32)] * len(sums)
     return call(kernel, "output_sums", operands.pairs, shapes, [], 2**21, size)
@@ -290,10 +302,8 @@
 
 
 def scattered(kept, coded, steps, after):
-    steps = list(zip(*steps))
-
     def sent(array, step):
-        return whole(swapped_by_core(array, step))
+        return whole(swapped(array, step))
 
     half, waiting = len(kept), coded[:1]
     received = [[]] + [[sent(c, steps[-1])] for c in coded[1:]]
@@ -340,10 +350,16 @@
     first_images = [swapped(a, steps[0][0]) for a in (picture_vectors, labels)]
     arrays = [{0: labelled(picture_vectors, labels), 1: labelled(*first_images, [first_texts])}, {0: caption_vectors, 1: first_texts}]
     for i in range(1, len(steps[0])):
-        for k in (1, 0):
-            for m in range(1 << i):
-                arrays[k][m | 1 << i] = swapped(arrays[k][m], steps[k][i])
-    blocks = [[whole(a[m]) for m in range(count)] for a in arrays]
+        for m in range(1 << i):
+            if (m | 1 << i) not in late:
+                for k in (1, 0):
+                    arrays[k][m | 1 << i] = swapped(arrays[k][m], steps[k][i])
+    lasts = [steps[1][-1], steps[0][-1]]
+    relayed = {}
+    for m in late:
+        pair = crossed(arrays[1][m - half], arrays[0][m - half])
+        relayed[m] = [swapped_by_core(p, o) for p, o in zip(pair, (lasts, lasts[::-1]))]
+    blocks = [{m: whole(a[m]) for m in early} for a in arrays]
     others = [{}, {}]
     both = bundled([arrays[1][1], arrays[0][1]], BUNDLE_COST)
     rest = [m for m in early if m != 1]
@@ -352,17 +368,18 @@
         row = i * (2 * size + EXTRA_ROWS)
         others[1][m], others[0][m] = ((both, row, 0),), ((both, row + size, 0),)
 
-    def sums(name, kinds, rows, columns, jobs, befores, emits, after=()):
-        variants = []
-        for kind, before in zip(kinds, befores):
-            other = 1 - kind
-            x_blocks = [blocks[kind][m] for m in rows]
-            y_blocks = [(blocks, others)[c][other][m] for c, m in columns]
+    tables = [(blocks, others)]
+
+    def sums(name, kind, rows, columns, jobs, before, emits, after=()):
+        other, variants = 1 - kind, []
+        for table in tables:
+            x_blocks = [table[0][kind][m] for m in rows]
+            y_blocks = [table[c][other][m] for c, m in columns]
             x_masks = [masks[kind][m] for m in rows]
             y_masks = [masks[other][m + c * count] for c, m in columns]
-            sequence = [blocks[k][m] for m in rows[1:] + rows[:1] for k in (1, 0)]
+            sequence = [blocks[k][m] for m in early[1:] + early[:1] for k in (1, 0)]
             variants.append(
-                (x_blocks, y_blocks, (x_masks, y_masks), kind == 0, jobs, before, sequence)
+                (x_blocks, y_blocks, (x_masks, y_masks), kind == 0, jobs, before, sequence if rows == early else [])
             )
         return gradient_sums(name, size, scalars, variants, emits, after)
 
@@ -376,38 +393,38 @@
     for k in range(2):
         columns = both_cores(early)
         jobs, emits = every_pair(early, columns), ["float"] * len(early)
-        results = sums("early_sums", [k], early, columns, jobs, [{}], emits)
+        results = sums("early_sums", k, early, columns, jobs, {}, emits)
         before.append(dict(zip(early, results)))
-    arrays = [[b[m][0][0] for m in late] for b in blocks[::-1]]
-    arrays, before = lax.optimization_barrier((arrays, before))
+    relayed, before = lax.optimization_barrier((relayed, before))
+    swaps = {m: [swapped(a, core) for a in relayed[m]] for m in late}
+    tables = []
+    for c in range(2):
+        own, other = [dict(b) for b in blocks], [dict(o) for o in others]
+        for m in late:
+            own[1 - c][m], own[c][m] = [whole(a) for a in relayed[m]]
+            other[c][m], other[1 - c][m] = [whole(a) for a in swaps[m]]
+        tables.append((own, other))
+    after = ()
+    coded, kept, received = [[None] * half, [None] * half], [None, None], [None, None]
     for k in (1, 0):
-        for m, a in zip(late, arrays[1 - k]):
-            blocks[k][m] = whole(a)
-            others[k][m] = whole(swapped(a, core))
-    turns, after = ((1, 0), (0, 1)), ()
-    coded, kept, received = [[None] * half, [None] * half], [None, None], [None, None]
-    for t, kinds in enumerate(turns):
         columns = [(0, m) for m in range(count)] + [(1, m) for m in early]
         jobs, emits = every_pair(late, columns), ["float"] * len(late)
-        results = sums("late_rows_begun", kinds, late, columns, jobs, [{}, {}], emits, after)
-        begun = dict(enumerate(results))
+        begun = dict(enumerate(sums("late_rows_begun", k, late, columns, jobs, {}, emits, after)))
         columns = [(1, m) for m in late]
         jobs, emits = every_pair(late, columns), ["codes"] * len(late)
-        coded[t][1:] = sums("late_rows", kinds, late, columns, jobs, [begun, begun], emits)
-        after = coded[t][1:2]
-    for t, kinds in enumerate(turns):
+        coded[k][1:] = sums("late_rows", k, late, columns, jobs, begun, emits)
+        after = coded[k][1:2]
+    for k in (1, 0):
         columns = both_cores(late)
         jobs, emits = every_pair(early, columns), ["float"] * half + ["codes"]
-        *kept[t], coded[t][0] = sums(
-            "late_columns", kinds, early, columns, jobs, [before[k] for k in kinds], emits, after
-        )
-        after = coded[t][:1]
+        *kept[k], coded[k][0] = sums("late_columns", k, early, columns, jobs, before[k], emits, after)
+        after = coded[k][:1]
     after, ends = (), ()
-    for t, kinds in enumerate(turns):
-        kept[t], received[t], after = scattered(kept[t], coded[t], [steps[k] for k in kinds], after)
-    for t in range(2):
-        ends = in_order([b[0][0] for b in received[t][:-1]], ends)
-        received[t] = [whole(a) for a in ends] + received[t][-1:]
+    for k in (1, 0):
+        kept[k], received[k], after = scattered(kept[k], coded[k], steps[k], after)
+    for k in (1, 0):
+        ends = in_order([b[0][0] for b in received[k][:-1]], ends)
+        received[k] = [whole(a) for a in ends] + received[k][-1:]
     return tuple(output_sums(scalars[0], list(zip(kept, received))))
 
 

time: 60.1 us -> 60.4 us (level)
  starting transfers between devices: 20.3 us -> 21.6 us
  waiting for transfers between devices: 23.1 us -> 22.4 us
    ppermute x6 -> x2, waiting for transfers between devices: 13.4 us -> 1.56 us  [swapped_by_core(): return lax.ppermute(array, ('blk', 'grp'), route)]
    ppermute x10 -> x14, waiting for transfers between devices: 9.68 us -> 20.8 us  [swapped(): lax.ppermute(array, axis, [(i, i ^ bit) for i in range(lax.axis_size(axis...]
    ppermute x10 -> x14, starting transfers between devices: 12.9 us -> 18.5 us  [swapped(): lax.ppermute(array, axis, [(i, i ^ bit) for i in range(lax.axis_size(axis...]
    ppermute x6 -> x2, starting transfers between devices: 7.39 us -> 3.13 us  [swapped_by_core(): return lax.ppermute(array, ('blk', 'grp'), route)]
    pallas_call x18 -> x19, Pallas kernels: 12.6 us -> 12.5 us  [call(): pl.pallas_call(body, out_shape=[*out_shape, *(jax.ShapeDtypeStruct(a.shap...]
  transfers between devices with their start and end apart: 16 -> 16, of which waited for: 7 -> 9; matrix products, arithmetic and copies ran while one was open for 0% -> 0% of each run, Pallas kernels for 17% -> 17%
where the time goes in v19:
time: 60.4 us; the launch traced here: 60.3 us
  waiting for transfers between devices  22.4 us (37%)
  starting transfers between devices  21.6 us (36%)
  Pallas kernels  12.5 us (21%)
  between operations  2.1 us (3%)
  local copies, waits for them, and re-layouts  1.66 us (3%)
    ppermute x14, waiting for transfers between devices, swapped(): lax.ppermute(array, axis, [(i, i ^ bit) for i in range(lax.axis_size(axis...  20.8 us
    ppermute x14, starting transfers between devices, swapped(): lax.ppermute(array, axis, [(i, i ^ bit) for i in range(lax.axis_size(axis...  18.5 us
    pallas_call x19, Pallas kernels, call(): pl.pallas_call(body, out_shape=[*out_shape, *(jax.ShapeDtypeStruct(a.shap...  12.5 us
    ppermute x2, starting transfers between devices, swapped_by_core(): return lax.ppermute(array, ('blk', 'grp'), route)  3.13 us
    unnamed x6, local copies, waits for them, and re-layouts  1.66 us
    ppermute x2, waiting for transfers between devices, swapped_by_core(): return lax.ppermute(array, ('blk', 'grp'), route)  1.56 us
  transfers between devices with their start and end apart: 16, of which 9 were waited for; matrix products, arithmetic and copies ran while one was open for 0% of the time, Pallas kernels for 17%

profile of v19, /device:TPU:0, one launch (start us, length us, event | category | flops | bytes accessed | tf_op | source)
XLA Modules:
  0.0 60.3 jit_solution(10053003103361569195)
XLA Ops:
  0.6 4.1 %collective-permute-start = (bf16[128,1152]{1,0:T(8,128)(2,1)}, bf16[128,1152]{1,0:T(8,128)(2,1)S(1)}, u32[]{:S(2)}, u32[]{:S(2)}) collective-permute-start(bf16[128,1152]{1,0:T(8,128)(2,1)} %refs_6_.7), channel_id=1, source_target_pairs={{0,4},{1,5},{2,6},{3,7},{4,0},{5,1},{6,2},{7,3},{8,12},{9,13},{10,... | collective-permute-start | bytes 884744 | tf_op jit(solution)/shard_map/ppermute | solution.py:292
  4.7 1.6 %collective-permute-start.1 = (bf16[128,1152]{1,0:T(8,128)(2,1)}, bf16[128,1152]{1,0:T(8,128)(2,1)S(1)}, u32[]{:S(2)}, u32[]{:S(2)}) collective-permute-start(bf16[128,1152]{1,0:T(8,128)(2,1)} %refs_0_.10), channel_id=1, source_target_pairs={{0,2},{1,3},{2,0},{3,1},{4,6},{5,7},{6,4},{7,5},{8,10},{9,11},{10,... | collective-permute-start | bytes 884744 | tf_op jit(solution)/shard_map/ppermute | solution.py:292
  6.3 0.0 copy-start.1
  6.3 1.0 %copy-done.1 = bf16[128,1152]{1,0:T(8,128)(2,1)S(1)} copy-done((bf16[128,1152]{1,0:T(8,128)(2,1)S(1)}, bf16[128,1152]{1,0:T(8,128)(2,1)}, u32[]{:S(2)}) %copy-start.1) | copy-done | bytes 294936
  7.3 0.0 copy-start.2
  7.3 0.7 %copy-done.2 = s32[128]{0:T(128)S(1)} copy-done((s32[128]{0:T(128)S(1)}, s32[128]{0:T(128)}, u32[]{:S(2)}) %copy-start.2) | copy-done | bytes 536
  8.0 0.0 copy-start
  8.0 1.6 %collective-permute-start.4 = (bf16[136,1152]{1,0:T(8,128)(2,1)S(1)}, bf16[136,1152]{1,0:T(8,128)(2,1)S(1)}, u32[]{:S(2)}, u32[]{:S(2)}) collective-permute-start(bf16[136,1152]{1,0:T(8,128)(2,1)S(1)} %labelled.3.refs_2_.refs_7_.refs_3_), channel_id=1, source_target_pairs={{0,8},{8,0},{16,24},{24,16},{1,9},{9,1},{17,25},{25,17},{2,10},{10... | collective-permute-start | bytes 940040 | tf_op jit(solution)/shard_map/ppermute | solution.py:292
  9.6 1.5 %collective-permute-start.3 = (bf16[128,1152]{1,0:T(8,128)(2,1)}, bf16[128,1152]{1,0:T(8,128)(2,1)S(1)}, u32[]{:S(2)}, u32[]{:S(2)}) collective-permute-start(bf16[128,1152]{1,0:T(8,128)(2,1)} %refs_6_.7), channel_id=1, source_target_pairs={{0,16},{8,24},{16,0},{24,8},{1,17},{9,25},{17,1},{25,9},{2,18},{10... | collective-permute-start | bytes 884744 | tf_op jit(solution)/shard_map/ppermute | solution.py:292
  11.1 0.4 collective-permute-start.2
  11.5 6.8 %collective-permute-done.refs_0_ = bf16[128,1152]{1,0:T(8,128)(2,1)S(1)} collective-permute-done((bf16[128,1152]{1,0:T(8,128)(2,1)}, bf16[128,1152]{1,0:T(8,128)(2,1)S(1)}, u32[]{:S(2)}, u32[]{:S(2)}) %collective-permute-start) | collective-permute-done | bytes 294944 | tf_op jit(solution)/shard_map/ppermute | solution.py:292
  18.4 0.3 collective-permute-done.2.refs_1_
  18.6 0.0 collective-permute-done.1.refs_0_
  18.7 0.0 collective-permute-done.3.refs_3_.refs_4_.refs_5_
  18.7 0.0 collective-permute-done.4.refs_4_.refs_5_
  18.7 0.0 copy-done
  18.8 0.1 bundled.3
  18.9 0.1 collective-permute-start.7
  19.0 0.1 crossed.1
  19.0 1.6 %collective-permute-start.5 = (bf16[136,1152]{1,0:T(8,128)(2,1)S(1)}, bf16[136,1152]{1,0:T(8,128)(2,1)S(1)}, u32[]{:S(2)}, u32[]{:S(2)}) collective-permute-start(bf16[136,1152]{1,0:T(8,128)(2,1)S(1)} %get-tuple-element.28), channel_id=1, source_target_pairs={{0,16},{1,9},{2,18},{3,11},{4,20},{5,13},{6,22},{7,15},{8,24},{9,1... | collective-permute-start | bytes 940040 | tf_op jit(solution)/shard_map/ppermute | solution.py:301
  20.7 1.5 %collective-permute-start.6 = (bf16[136,1152]{1,0:T(8,128)(2,1)S(1)}, bf16[136,1152]{1,0:T(8,128)(2,1)S(1)}, u32[]{:S(2)}, u32[]{:S(2)}) collective-permute-start(bf16[136,1152]{1,0:T(8,128)(2,1)S(1)} %get-tuple-element.29), channel_id=1, source_target_pairs={{0,8},{1,17},{2,10},{3,19},{4,12},{5,21},{6,14},{7,23},{8,0},{9,25... | collective-permute-start | bytes 940040 | tf_op jit(solution)/shard_map/ppermute | solution.py:301
  23.5 0.0 collective-permute-done.7.refs_8_.refs_7_
  23.5 1.9 %early_sums.3 = (f32[128,1152]{1,0:T(8,128)S(1)}, f32[128,1152]{1,0:T(8,128)S(1)}, f32[128,1152]{1,0:T(8,128)S(1)}) custom-call(f32[1]{0:T(128)S(6)} %copy.17.refs_0_, f32[1]{0:T(128)S(6)} %copy.18.refs_1_, bf16[128,1152]{1,0:T(8,128)(2,1)S(1)} %held.3.refs_2_.refs_0_.refs_4_, bf16[136,1152]{1,0:T(8,128)(2,1)S(1)} %labelled.2.refs_1_.refs_3_.refs_4_, ...), custom_call_target="tpu_custom_call" | custom-call | flops 2304 | bytes 2304 | tf_op jit(solution)/shard_map/early_sums/pallas_call | solution.py:92
  25.4 1.9 %early_sums.2 = (f32[128,1152]{1,0:T(8,128)S(1)}, f32[128,1152]{1,0:T(8,128)S(1)}, f32[128,1152]{1,0:T(8,128)S(1)}) custom-call(f32[1]{0:T(128)S(6)} %copy.17.refs_0_, f32[1]{0:T(128)S(6)} %copy.18.refs_1_, bf16[128,1152]{1,0:T(8,128)(2,1)S(1)} %held.3.refs_2_.refs_0_.refs_4_, bf16[136,1152]{1,0:T(8,128)(2,1)S(1)} %labelled.2.refs_1_.refs_3_.refs_4_, ...), custom_call_target="tpu_custom_call" | custom-call | flops 2304 | bytes 2304 | tf_op jit(solution)/shard_map/early_sums/pallas_call | solution.py:92
  27.3 1.3 %collective-permute-done.5.refs_2_.refs_6_.refs_5_.refs_13_.refs_8_ = bf16[136,1152]{1,0:T(8,128)(2,1)S(1)} collective-permute-done((bf16[136,1152]{1,0:T(8,128)(2,1)S(1)}, bf16[136,1152]{1,0:T(8,128)(2,1)S(1)}, u32[]{:S(2)}, u32[]{:S(2)}) %collective-permute-start.5) | collective-permute-done | bytes 313376 | tf_op jit(solution)/shard_map/ppermute | solution.py:301
  28.7 0.2 collective-permute-done.6.refs_6_.refs_5_.refs_2_.refs_8_.refs_13_
  28.9 0.3 collective-permute-start.9
  29.2 0.2 collective-permute-start.8
  29.4 1.3 %late_rows_begun.2.refs_4_ = f32[128,1152]{1,0:T(8,128)S(1)} custom-call(f32[1]{0:T(128)S(6)} %copy.17.refs_0_, f32[1]{0:T(128)S(6)} %copy.18.refs_1_, bf16[136,1152]{1,0:T(8,128)(2,1)S(1)} %collective-permute-done.5.refs_2_.refs_6_.refs_5_.refs_13_.refs_8_, bf16[136,1152]{1,0:T(8,128)(2,1)S(1)} %labelled.3.refs_2_.refs_7_.refs_3_, ...), custom_call_target="tpu_custom_call" | custom-call | flops 896 | bytes 896 | tf_op jit(solution)/shard_map/late_rows_begun/pallas_call | solution.py:92
  30.8 0.0 collective-permute-done.9.refs_3_.refs_6_.refs_9_.refs_14_
  30.8 0.2 collective-permute-done.8.refs_6_.refs_3_.refs_14_.refs_9_
  31.0 0.6 %late_rows.2.refs_8_ = s16[136,1152]{1,0:T(8,128)(2,1)S(1)} custom-call(f32[1]{0:T(128)S(6)} %copy.17.refs_0_, f32[1]{0:T(128)S(6)} %copy.18.refs_1_, bf16[136,1152]{1,0:T(8,128)(2,1)S(1)} %collective-permute-done.5.refs_2_.refs_6_.refs_5_.refs_13_.refs_8_, bf16[136,1152]{1,0:T(8,128)(2,1)S(1)} %collective-permute-done.9.refs_3_.refs_6_.refs_9_.refs_14_, ...), custom_call_target="tpu_custom_call" | custom-call | flops 128 | bytes 128 | tf_op jit(solution)/shard_map/late_rows/pallas_call | solution.py:92
  31.6 1.6 %collective-permute-start.10 = (s16[136,1152]{1,0:T(8,128)(2,1)S(1)}, s16[136,1152]{1,0:T(8,128)(2,1)S(1)}, u32[]{:S(2)}, u32[]{:S(2)}) collective-permute-start(s16[136,1152]{1,0:T(8,128)(2,1)S(1)} %late_rows.2.refs_8_), channel_id=1, source_target_pairs={{0,16},{8,24},{16,0},{24,8},{1,17},{9,25},{17,1},{25,9},{2,18},{10... | collective-permute-start | bytes 940040 | tf_op jit(solution)/shard_map/ppermute | solution.py:292
  33.2 1.4 %late_rows_begun.3.refs_4_ = f32[128,1152]{1,0:T(8,128)S(1)} custom-call(f32[1]{0:T(128)S(6)} %copy.17.refs_0_, f32[1]{0:T(128)S(6)} %copy.18.refs_1_, bf16[136,1152]{1,0:T(8,128)(2,1)S(1)} %collective-permute-done.6.refs_6_.refs_5_.refs_2_.refs_8_.refs_13_, bf16[128,1152]{1,0:T(8,128)(2,1)S(1)} %copy-done, ...), custom_call_target="tpu_custom_call" | custom-call | flops 896 | bytes 896 | tf_op jit(solution)/shard_map/late_rows_begun/pallas_call | solution.py:92
  34.6 0.6 %late_rows.3.refs_15_ = s16[136,1152]{1,0:T(8,128)(2,1)S(1)} custom-call(f32[1]{0:T(128)S(6)} %copy.17.refs_0_, f32[1]{0:T(128)S(6)} %copy.18.refs_1_, bf16[136,1152]{1,0:T(8,128)(2,1)S(1)} %collective-permute-done.6.refs_6_.refs_5_.refs_2_.refs_8_.refs_13_, bf16[136,1152]{1,0:T(8,128)(2,1)S(1)} %collective-permute-done.8.refs_6_.refs_3_.refs_14_.refs_9_, ...), custom_call_target="tpu_custom_call" | custom-call | flops 128 | bytes 128 | tf_op jit(solution)/shard_map/late_rows/pallas_call | solution.py:92
  35.2 1.8 %collective-permute-start.12 = (s16[136,1152]{1,0:T(8,128)(2,1)S(1)}, s16[136,1152]{1,0:T(8,128)(2,1)S(1)}, u32[]{:S(2)}, u32[]{:S(2)}) collective-permute-start(s16[136,1152]{1,0:T(8,128)(2,1)S(1)} %late_rows.3.refs_15_), channel_id=1, source_target_pairs={{0,8},{8,0},{16,24},{24,16},{1,9},{9,1},{17,25},{25,17},{2,10},{10... | collective-permute-start | bytes 940040 | tf_op jit(solution)/shard_map/ppermute | solution.py:292
  37.0 1.3 %late_columns.2 = (f32[128,1152]{1,0:T(8,128)S(1)}, f32[128,1152]{1,0:T(8,128)S(1)}, s16[136,1152]{1,0:T(8,128)(2,1)S(1)}) custom-call(f32[1]{0:T(128)S(6)} %copy.17.refs_0_, f32[1]{0:T(128)S(6)} %copy.18.refs_1_, bf16[128,1152]{1,0:T(8,128)(2,1)S(1)} %held.3.refs_2_.refs_0_.refs_4_, bf16[136,1152]{1,0:T(8,128)(2,1)S(1)} %labelled.2.refs_1_.refs_3_.refs_4_, ...), custom_call_target="tpu_custom_call" | custom-call | flops 768 | bytes 768 | tf_op jit(solution)/shard_map/late_columns/pallas_call | solution.py:92
  38.4 1.5 %late_columns.3 = (f32[128,1152]{1,0:T(8,128)S(1)}, f32[128,1152]{1,0:T(8,128)S(1)}, s16[136,1152]{1,0:T(8,128)(2,1)S(1)}) custom-call(f32[1]{0:T(128)S(6)} %copy.17.refs_0_, f32[1]{0:T(128)S(6)} %copy.18.refs_1_, bf16[128,1152]{1,0:T(8,128)(2,1)S(1)} %held.3.refs_2_.refs_0_.refs_4_, bf16[136,1152]{1,0:T(8,128)(2,1)S(1)} %labelled.2.refs_1_.refs_3_.refs_4_, ...), custom_call_target="tpu_custom_call" | custom-call | flops 768 | bytes 768 | tf_op jit(solution)/shard_map/late_columns/pallas_call | solution.py:92
  39.9 1.4 %collective-permute-done.10.refs_1_ = s16[136,1152]{1,0:T(8,128)(2,1)S(1)} collective-permute-done((s16[136,1152]{1,0:T(8,128)(2,1)S(1)}, s16[136,1152]{1,0:T(8,128)(2,1)S(1)}, u32[]{:S(2)}, u32[]{:S(2)}) %collective-permute-start.10) | collective-permute-done | bytes 313376 | tf_op jit(solution)/shard_map/ppermute | solution.py:292
  41.3 0.2 passed_sum.2
  41.5 1.4 %collective-permute-start.11 = (s16[136,1152]{1,0:T(8,128)(2,1)S(1)}, s16[136,1152]{1,0:T(8,128)(2,1)S(1)}, u32[]{:S(2)}, u32[]{:S(2)}) collective-permute-start(s16[136,1152]{1,0:T(8,128)(2,1)S(1)} %get-tuple-element.47.refs_2_), channel_id=1, source_target_pairs={{0,4},{1,5},{2,6},{3,7},{4,0},{5,1},{6,2},{7,3},{8,12},{9,13},{10,... | collective-permute-start | bytes 940040 | tf_op jit(solution)/shard_map/ppermute | solution.py:292
  42.9 1.7 %collective-permute-done.12.refs_1_ = s16[136,1152]{1,0:T(8,128)(2,1)S(1)} collective-permute-done((s16[136,1152]{1,0:T(8,128)(2,1)S(1)}, s16[136,1152]{1,0:T(8,128)(2,1)S(1)}, u32[]{:S(2)}, u32[]{:S(2)}) %collective-permute-start.12) | collective-permute-done | bytes 313376 | tf_op jit(solution)/shard_map/ppermute | solution.py:292
  44.6 0.2 passed_sum.3
  44.8 1.5 %collective-permute-start.13 = (s16[136,1152]{1,0:T(8,128)(2,1)S(1)}, s16[136,1152]{1,0:T(8,128)(2,1)S(1)}, u32[]{:S(2)}, u32[]{:S(2)}) collective-permute-start(s16[136,1152]{1,0:T(8,128)(2,1)S(1)} %get-tuple-element.50), channel_id=1, source_target_pairs={{0,2},{1,3},{2,0},{3,1},{4,6},{5,7},{6,4},{7,5},{8,10},{9,11},{10,... | collective-permute-start | bytes 940040 | tf_op jit(solution)/shard_map/ppermute | solution.py:292
  46.3 1.6 %collective-permute-start.14 = (s16[136,1152]{1,0:T(8,128)(2,1)S(1)}, s16[136,1152]{1,0:T(8,128)(2,1)S(1)}, u32[]{:S(2)}, u32[]{:S(2)}) collective-permute-start(s16[136,1152]{1,0:T(8,128)(2,1)S(1)} %get-tuple-element.51), channel_id=1, source_target_pairs={{0,8},{8,0},{16,24},{24,16},{1,9},{9,1},{17,25},{25,17},{2,10},{10... | collective-permute-start | bytes 940040 | tf_op jit(solution)/shard_map/ppermute | solution.py:292
  47.9 0.7 %collective-permute-start.15 = (s16[136,1152]{1,0:T(8,128)(2,1)S(1)}, s16[136,1152]{1,0:T(8,128)(2,1)S(1)}, u32[]{:S(2)}, u32[]{:S(2)}) collective-permute-start(s16[136,1152]{1,0:T(8,128)(2,1)S(1)} %get-tuple-element.53), channel_id=1, source_target_pairs={{0,16},{8,24},{16,0},{24,8},{1,17},{9,25},{17,1},{25,9},{2,18},{10... | collective-permute-start | bytes 940040 | tf_op jit(solution)/shard_map/ppermute | solution.py:292
  48.6 9.4 %collective-permute-done.11.refs_0_ = s16[136,1152]{1,0:T(8,128)(2,1)S(1)} collective-permute-done((s16[136,1152]{1,0:T(8,128)(2,1)S(1)}, s16[136,1152]{1,0:T(8,128)(2,1)S(1)}, u32[]{:S(2)}, u32[]{:S(2)}) %collective-permute-start.11) | collective-permute-done | bytes 313376 | tf_op jit(solution)/shard_map/ppermute | solution.py:292
  58.1 1.0 %collective-permute-done.13.refs_1_ = s16[136,1152]{1,0:T(8,128)(2,1)S(1)} collective-permute-done((s16[136,1152]{1,0:T(8,128)(2,1)S(1)}, s16[136,1152]{1,0:T(8,128)(2,1)S(1)}, u32[]{:S(2)}, u32[]{:S(2)}) %collective-permute-start.13) | collective-permute-done | bytes 313376 | tf_op jit(solution)/shard_map/ppermute | solution.py:292
  59.0 0.0 collective-permute-done.14.refs_3_
  59.1 0.0 collective-permute-done.15.refs_6_
  59.1 1.2 %output_sums.1 = (f32[128,1152]{1,0:T(8,128)}, f32[128,1152]{1,0:T(8,128)}) custom-call(f32[1]{0:T(128)S(6)} %copy.17.refs_0_, f32[128,1152]{1,0:T(8,128)S(1)} %get-tuple-element.45.refs_1_, s16[136,1152]{1,0:T(8,128)(2,1)S(1)} %held.5.refs_2_, s16[136,1152]{1,0:T(8,128)(2,1)S(1)} %collective-permute-done.14.refs_3_, ...), custom_call_target="tpu_custom_call" | custom-call | flops 128 | bytes 128 | tf_op jit(solution)/shard_map/output_sums/pallas_call | solution.py:92
  (6 shorter events, 0.1 us)
Async XLA Ops:
  0.6 17.8 %collective-permute-start = (bf16[128,1152]{1,0:T(8,128)(2,1)}, bf16[128,1152]{1,0:T(8,128)(2,1)S(1)}, u32[]{:S(2)}, u32[]{:S(2)}) collective-permute-start(bf16[128,1152]{1,0:T(8,128)(2,1)} %refs_6_.7), channel_id=1, source_target_pairs={{0,4},{1,5},{2,6},{3,7},{4,0},{5,1},{6,2},{7,3},{8,12},{9,13},{10,... | collective-permute-start | bytes 884744 | tf_op jit(solution)/shard_map/ppermute | solution.py:292
  4.7 13.9 %collective-permute-start.1 = (bf16[128,1152]{1,0:T(8,128)(2,1)}, bf16[128,1152]{1,0:T(8,128)(2,1)S(1)}, u32[]{:S(2)}, u32[]{:S(2)}) collective-permute-start(bf16[128,1152]{1,0:T(8,128)(2,1)} %refs_0_.10), channel_id=1, source_target_pairs={{0,2},{1,3},{2,0},{3,1},{4,6},{5,7},{6,4},{7,5},{8,10},{9,11},{10,... | collective-permute-start | bytes 884744 | tf_op jit(solution)/shard_map/ppermute | solution.py:292
  6.3 1.0 %copy-start.1 = (bf16[128,1152]{1,0:T(8,128)(2,1)S(1)}, bf16[128,1152]{1,0:T(8,128)(2,1)}, u32[]{:S(2)}) copy-start(bf16[128,1152]{1,0:T(8,128)(2,1)} %refs_0_.10) | copy-start | bytes 884740
  7.3 0.7 %copy-start.2 = (s32[128]{0:T(128)S(1)}, s32[128]{0:T(128)}, u32[]{:S(2)}) copy-start(s32[128]{0:T(128)} %param.7) | copy-start | bytes 1540
  8.0 10.8 %copy-start = (bf16[128,1152]{1,0:T(8,128)(2,1)S(1)}, bf16[128,1152]{1,0:T(8,128)(2,1)}, u32[]{:S(2)}) copy-start(bf16[128,1152]{1,0:T(8,128)(2,1)} %refs_6_.7) | copy-start | bytes 884740
  8.0 10.7 %collective-permute-start.4 = (bf16[136,1152]{1,0:T(8,128)(2,1)S(1)}, bf16[136,1152]{1,0:T(8,128)(2,1)S(1)}, u32[]{:S(2)}, u32[]{:S(2)}) collective-permute-start(bf16[136,1152]{1,0:T(8,128)(2,1)S(1)} %labelled.3.refs_2_.refs_7_.refs_3_), channel_id=1, source_target_pairs={{0,8},{8,0},{16,24},{24,16},{1,9},{9,1},{17,25},{25,17},{2,10},{10... | collective-permute-start | bytes 940040 | tf_op jit(solution)/shard_map/ppermute | solution.py:292
  9.6 9.2 %collective-permute-start.3 = (bf16[128,1152]{1,0:T(8,128)(2,1)}, bf16[128,1152]{1,0:T(8,128)(2,1)S(1)}, u32[]{:S(2)}, u32[]{:S(2)}) collective-permute-start(bf16[128,1152]{1,0:T(8,128)(2,1)} %refs_6_.7), channel_id=1, source_target_pairs={{0,16},{8,24},{16,0},{24,8},{1,17},{9,25},{17,1},{25,9},{2,18},{10... | collective-permute-start | bytes 884744 | tf_op jit(solution)/shard_map/ppermute | solution.py:292
  11.1 7.6 %collective-permute-start.2 = (s32[1,128]{1,0:T(1,128)S(1)}, s32[1,128]{1,0:T(1,128)S(1)}, u32[]{:S(2)}, u32[]{:S(2)}) collective-permute-start(s32[1,128]{1,0:T(1,128)S(1)} %bitcast.2), channel_id=1, source_target_pairs={{0,2},{1,3},{2,0},{3,1},{4,6},{5,7},{6,4},{7,5},{8,10},{9,11},{10,... | collective-permute-start | bytes 1544 | tf_op jit(solution)/shard_map/ppermute | solution.py:292
  18.9 4.6 %collective-permute-start.7 = (bf16[792,1152]{1,0:T(8,128)(2,1)S(1)}, bf16[792,1152]{1,0:T(8,128)(2,1)S(1)}, u32[]{:S(2)}, u32[]{:S(2)}) collective-permute-start(bf16[792,1152]{1,0:T(8,128)(2,1)S(1)} %bundled.3), channel_id=1, source_target_pairs={{0,1},{1,0},{2,3},{3,2},{4,5},{5,4},{6,7},{7,6},{8,9},{9,8},{10,11... | collective-permute-start | bytes 5474312 | tf_op jit(solution)/shard_map/ppermute | solution.py:292
  19.0 9.6 %collective-permute-start.5 = (bf16[136,1152]{1,0:T(8,128)(2,1)S(1)}, bf16[136,1152]{1,0:T(8,128)(2,1)S(1)}, u32[]{:S(2)}, u32[]{:S(2)}) collective-permute-start(bf16[136,1152]{1,0:T(8,128)(2,1)S(1)} %get-tuple-element.28), channel_id=1, source_target_pairs={{0,16},{1,9},{2,18},{3,11},{4,20},{5,13},{6,22},{7,15},{8,24},{9,1... | collective-permute-start | bytes 940040 | tf_op jit(solution)/shard_map/ppermute | solution.py:301
  20.7 8.2 %collective-permute-start.6 = (bf16[136,1152]{1,0:T(8,128)(2,1)S(1)}, bf16[136,1152]{1,0:T(8,128)(2,1)S(1)}, u32[]{:S(2)}, u32[]{:S(2)}) collective-permute-start(bf16[136,1152]{1,0:T(8,128)(2,1)S(1)} %get-tuple-element.29), channel_id=1, source_target_pairs={{0,8},{1,17},{2,10},{3,19},{4,12},{5,21},{6,14},{7,23},{8,0},{9,25... | collective-permute-start | bytes 940040 | tf_op jit(solution)/shard_map/ppermute | solution.py:301
  28.9 1.9 %collective-permute-start.9 = (bf16[136,1152]{1,0:T(8,128)(2,1)S(1)}, bf16[136,1152]{1,0:T(8,128)(2,1)S(1)}, u32[]{:S(2)}, u32[]{:S(2)}) collective-permute-start(bf16[136,1152]{1,0:T(8,128)(2,1)S(1)} %collective-permute-done.5.refs_2_.refs_6_.refs_5_.refs_13_.refs_8_), channel_id=1, source_target_pairs={{0,1},{1,0},{2,3},{3,2},{4,5},{5,4},{6,7},{7,6},{8,9},{9,8},{10,11... | collective-permute-start | bytes 940040 | tf_op jit(solution)/shard_map/ppermute | solution.py:292
  29.2 1.7 %collective-permute-start.8 = (bf16[136,1152]{1,0:T(8,128)(2,1)S(1)}, bf16[136,1152]{1,0:T(8,128)(2,1)S(1)}, u32[]{:S(2)}, u32[]{:S(2)}) collective-permute-start(bf16[136,1152]{1,0:T(8,128)(2,1)S(1)} %collective-permute-done.6.refs_6_.refs_5_.refs_2_.refs_8_.refs_13_), channel_id=1, source_target_pairs={{0,1},{1,0},{2,3},{3,2},{4,5},{5,4},{6,7},{7,6},{8,9},{9,8},{10,11... | collective-permute-start | bytes 940040 | tf_op jit(solution)/shard_map/ppermute | solution.py:292
  31.6 9.7 %collective-permute-start.10 = (s16[136,1152]{1,0:T(8,128)(2,1)S(1)}, s16[136,1152]{1,0:T(8,128)(2,1)S(1)}, u32[]{:S(2)}, u32[]{:S(2)}) collective-permute-start(s16[136,1152]{1,0:T(8,128)(2,1)S(1)} %late_rows.2.refs_8_), channel_id=1, source_target_pairs={{0,16},{8,24},{16,0},{24,8},{1,17},{9,25},{17,1},{25,9},{2,18},{10... | collective-permute-start | bytes 940040 | tf_op jit(solution)/shard_map/ppermute | solution.py:292
  35.2 9.4 %collective-permute-start.12 = (s16[136,1152]{1,0:T(8,128)(2,1)S(1)}, s16[136,1152]{1,0:T(8,128)(2,1)S(1)}, u32[]{:S(2)}, u32[]{:S(2)}) collective-permute-start(s16[136,1152]{1,0:T(8,128)(2,1)S(1)} %late_rows.3.refs_15_), channel_id=1, source_target_pairs={{0,8},{8,0},{16,24},{24,16},{1,9},{9,1},{17,25},{25,17},{2,10},{10... | collective-permute-start | bytes 940040 | tf_op jit(solution)/shard_map/ppermute | solution.py:292
  41.5 16.6 %collective-permute-start.11 = (s16[136,1152]{1,0:T(8,128)(2,1)S(1)}, s16[136,1152]{1,0:T(8,128)(2,1)S(1)}, u32[]{:S(2)}, u32[]{:S(2)}) collective-permute-start(s16[136,1152]{1,0:T(8,128)(2,1)S(1)} %get-tuple-element.47.refs_2_), channel_id=1, source_target_pairs={{0,4},{1,5},{2,6},{3,7},{4,0},{5,1},{6,2},{7,3},{8,12},{9,13},{10,... | collective-permute-start | bytes 940040 | tf_op jit(solution)/shard_map/ppermute | solution.py:292
  44.8 14.2 %collective-permute-start.13 = (s16[136,1152]{1,0:T(8,128)(2,1)S(1)}, s16[136,1152]{1,0:T(8,128)(2,1)S(1)}, u32[]{:S(2)}, u32[]{:S(2)}) collective-permute-start(s16[136,1152]{1,0:T(8,128)(2,1)S(1)} %get-tuple-element.50), channel_id=1, source_target_pairs={{0,2},{1,3},{2,0},{3,1},{4,6},{5,7},{6,4},{7,5},{8,10},{9,11},{10,... | collective-permute-start | bytes 940040 | tf_op jit(solution)/shard_map/ppermute | solution.py:292
  46.3 12.7 %collective-permute-start.14 = (s16[136,1152]{1,0:T(8,128)(2,1)S(1)}, s16[136,1152]{1,0:T(8,128)(2,1)S(1)}, u32[]{:S(2)}, u32[]{:S(2)}) collective-permute-start(s16[136,1152]{1,0:T(8,128)(2,1)S(1)} %get-tuple-element.51), channel_id=1, source_target_pairs={{0,8},{8,0},{16,24},{24,16},{1,9},{9,1},{17,25},{25,17},{2,10},{10... | collective-permute-start | bytes 940040 | tf_op jit(solution)/shard_map/ppermute | solution.py:292
  47.9 11.2 %collective-permute-start.15 = (s16[136,1152]{1,0:T(8,128)(2,1)S(1)}, s16[136,1152]{1,0:T(8,128)(2,1)S(1)}, u32[]{:S(2)}, u32[]{:S(2)}) collective-permute-start(s16[136,1152]{1,0:T(8,128)(2,1)S(1)} %get-tuple-element.53), channel_id=1, source_target_pairs={{0,16},{8,24},{16,0},{24,8},{1,17},{9,25},{17,1},{25,9},{2,18},{10... | collective-permute-start | bytes 940040 | tf_op jit(solution)/shard_map/ppermute | solution.py:292

commit v20 on v19

--- a/solution.py
+++ b/solution.py
@@ -15,6 +15,7 @@
 TILE = 256
 LANES = 128
 BUNDLE_COST = 6 * 10**8
+HELD_COST = 85 * 10**7
 SMEM = pl.BlockSpec(memory_space=pltpu.SMEM)
 VMEM = pl.BlockSpec(memory_space=pltpu.VMEM)
 ANY = pl.BlockSpec(memory_space=pl.ANY)
@@ -25,7 +26,7 @@
 
 
 def part_widths(width):
-    first = min(3 * TILE, width - LANES)
+    first = (width // LANES + 1) // 2 * LANES
     return (first, width - first)
 
 
@@ -171,12 +172,15 @@
 def gradient_sums(name, size, scalars, variants, emits, after=()):
     width = variants[0][0][0][0][0].shape[1]
     per_tile = TILE // size
-    shapes = [
-        jax.ShapeDtypeStruct((size, width), jnp.float32)
-        if kind == "float"
-        else jax.ShapeDtypeStruct((size + EXTRA_ROWS, width), jnp.int16)
-        for kind in emits
-    ]
+    shapes, where = [], []
+    for kind in emits:
+        cut = part_widths(width) if kind == "parts" else (width,)
+        where.append((len(shapes), len(shapes) + len(cut)))
+        for w in cut:
+            if kind == "float":
+                shapes.append(jax.ShapeDtypeStruct((size, w), jnp.float32))
+            else:
+                shapes.append(jax.ShapeDtypeStruct((size + EXTRA_ROWS, w), jnp.int16))
     operands = Operands()
     slope_at, shift_at = [operands.add(s, SMEM) for s in scalars]
     views = []
@@ -232,10 +236,11 @@
                     block = sums[i * size : (i + 1) * size]
                     if r in before_at:
                         block = block + piece(whole(ins[before_at[r]]), (0, size), tile)[...]
+                    out = tuple((o, 0, 0) for o in outs[where[r][0] : where[r][1]])
                     if emits[r] == "float":
-                        piece(whole(outs[r]), (0, size), tile)[...] = block
+                        piece(out, (0, size), tile)[...] = block
                     else:
-                        encode(block, whole(outs[r]), tile)
+                        encode(block, out, tile)
 
     def kernel(ins, refs):
         outs, weights = refs[:-1], refs[-1]
@@ -249,23 +254,27 @@
     pairs = sum(len(rows) * len(columns) for rows, columns in jobs)
     scratch = [pltpu.VMEM((len(x_blocks) * size, len(y_blocks) * size), jnp.bfloat16)]
     room = len(x_blocks) * len(y_blocks) * size * size * 2 + 8 * 2**20
-    return call(kernel, name, operands.pairs, shapes, scratch, room, pairs * size, after)
-
-
-def passed_sum(kept, received, held_back=(), after=()):
+    results = call(kernel, name, operands.pairs, shapes, scratch, room, pairs * size, after)
+    return [tuple(results[a:b]) for a, b in where]
+
+
+def passed_sum(kept, received, part, held_back=(), after=()):
     size, width = kept.shape
     operands = Operands()
     kept_at = operands.add(kept, VMEM)
-    views = [operands.block(b) for b in received]
+    views = [operands.block(b if part is None or len(b) == 1 else (b[part],) * 2) for b in received]
 
     def kernel(ins, outs):
         for tile in column_tiles(width):
-            total = piece(whole(ins[kept_at]), (0, size), tile)[...]
-            for view in views:
-                total = total + decoded(view(ins), size, tile)
-            encode(total, whole(outs[0]), tile)
-
-    shape = jax.ShapeDtypeStruct((size + EXTRA_ROWS, width), jnp.int16)
+            p, inner, _, span = tile
+            if part is None or p == part:
+                total = piece(whole(ins[kept_at]), (0, size), tile)[...]
+                for view in views:
+                    total = total + decoded(view(ins), size, tile)
+                encode(total, whole(outs[0]), tile if part is None else (0, 0, inner, span))
+
+    cut = width if part is None else part_widths(width)[part]
+    shape = jax.ShapeDtypeStruct((size + EXTRA_ROWS, cut), jnp.int16)
     return call(kernel, "passed_sum", operands.pairs, [shape], [], 2**21, size, after, held_back)
 
 
@@ -303,22 +312,27 @@
 
 def scattered(kept, coded, steps, after):
     def sent(array, step):
-        return whole(swapped(array, step))
-
-    half, waiting = len(kept), coded[:1]
-    received = [[]] + [[sent(c, steps[-1])] for c in coded[1:]]
+        return (swapped(array, step), 0, 0)
+
+    half = len(kept)
+    received = [[]] + [[(sent(c[0], steps[-1]),)] for c in coded[1:]]
+    waiting, last = [c[1] for c in coded[1:]], [coded[0][0]]
     for s in reversed(range(len(steps) - 1)):
         for m in reversed(range(1 << s)):
             n = m | 1 << s
-            block, *held = passed_sum(kept[n], received[n], waiting, after)
-            received[0] += [sent(c, steps[-1]) for c in held]
-            received[m].append(sent(block, steps[s]))
-            waiting, after = (), [block]
-    return kept[0], received[0][::-1], after
-
-
-def in_order(arrays, after=()):
-    return call(lambda *refs: None, "held", [], [], [], 2**21, 1, after, arrays)
+            first, *begun = passed_sum(kept[n], received[n], 0, waiting + last)
+            for r, c in zip(received[1:], begun):
+                r[0] = r[0] + (sent(c, steps[-1]),)
+            received[0] += [(sent(c, steps[-1]),) for c in begun[len(waiting) :]]
+            first = sent(first, steps[s])
+            (second,) = passed_sum(kept[n], received[n], 1, (), [first[0], *after])
+            received[m].append((first, sent(second, steps[s])))
+            waiting, last, after = [], [], [second]
+    return kept[0], received[0], after
+
+
+def in_order(arrays, after=(), cost=HELD_COST):
+    return call(lambda *refs: None, "held", [], [], [], 2**21, cost, after, arrays)
 
 
 def bit_steps(axis):
@@ -346,7 +360,7 @@
     half = count // 2
     early, late = list(range(half + 1)), list(range(half + 1, count))
     labels = matching_caption[None, :]
-    (first_texts,) = in_order([swapped(caption_vectors, steps[1][0])])
+    (first_texts,) = in_order([swapped(caption_vectors, steps[1][0])], (), 1)
     first_images = [swapped(a, steps[0][0]) for a in (picture_vectors, labels)]
     arrays = [{0: labelled(picture_vectors, labels), 1: labelled(*first_images, [first_texts])}, {0: caption_vectors, 1: first_texts}]
     for i in range(1, len(steps[0])):
@@ -394,7 +408,7 @@
         columns = both_cores(early)
         jobs, emits = every_pair(early, columns), ["float"] * len(early)
         results = sums("early_sums", k, early, columns, jobs, {}, emits)
-        before.append(dict(zip(early, results)))
+        before.append({m: s for m, (s,) in zip(early, results)})
     relayed, before = lax.optimization_barrier((relayed, before))
     swaps = {m: [swapped(a, core) for a in relayed[m]] for m in late}
     tables = []
@@ -405,27 +419,29 @@
             other[c][m], other[1 - c][m] = [whole(a) for a in swaps[m]]
         tables.append((own, other))
     after = ()
-    coded, kept, received = [[None] * half, [None] * half], [None, None], [None, None]
+    coded, kept = [[None] * half, [None] * half], [None, None]
     for k in (1, 0):
         columns = [(0, m) for m in range(count)] + [(1, m) for m in early]
         jobs, emits = every_pair(late, columns), ["float"] * len(late)
-        begun = dict(enumerate(sums("late_rows_begun", k, late, columns, jobs, {}, emits, after)))
+        results = sums("late_rows_begun", k, late, columns, jobs, {}, emits, after)
+        begun = {i: s for i, (s,) in enumerate(results)}
         columns = [(1, m) for m in late]
-        jobs, emits = every_pair(late, columns), ["codes"] * len(late)
+        jobs, emits = every_pair(late, columns), ["parts"] * len(late)
         coded[k][1:] = sums("late_rows", k, late, columns, jobs, begun, emits)
-        after = coded[k][1:2]
+        after = coded[k][1]
     for k in (1, 0):
         columns = both_cores(late)
-        jobs, emits = every_pair(early, columns), ["float"] * half + ["codes"]
-        *kept[k], coded[k][0] = sums("late_columns", k, early, columns, jobs, before[k], emits, after)
-        after = coded[k][:1]
-    after, ends = (), ()
-    for k in (1, 0):
-        kept[k], received[k], after = scattered(kept[k], coded[k], steps[k], after)
-    for k in (1, 0):
-        ends = in_order([b[0][0] for b in received[k][:-1]], ends)
-        received[k] = [whole(a) for a in ends] + received[k][-1:]
-    return tuple(output_sums(scalars[0], list(zip(kept, received))))
+        jobs, emits = every_pair(early, columns), ["float"] * half + ["whole"]
+        *whole_sums, coded[k][0] = sums("late_columns", k, early, columns, jobs, before[k], emits, after)
+        kept[k], after = [s for (s,) in whole_sums], coded[k][0]
+    kept_texts, text_blocks, after = scattered(kept[1], coded[1], steps[1], ())
+    kept_images, image_blocks, _ = scattered(kept[0], coded[0], steps[0], after)
+    ends = ()
+    for blocks_in in (text_blocks, image_blocks):
+        ends = in_order([part[0] for b in blocks_in if len(b) > 1 for part in b], ends)
+        parts = iter(ends)
+        blocks_in[:] = [tuple((next(parts), 0, 0) for _ in b) if len(b) > 1 else b for b in blocks_in]
+    return tuple(output_sums(scalars[0], [(kept_images, image_blocks), (kept_texts, text_blocks)]))
 
 
 def solution(mesh):

time: 60.4 us -> 61 us (level)
  starting transfers between devices: 21.6 us -> 26.6 us
  waiting for transfers between devices: 22.4 us -> 17.9 us
    ppermute x14 -> x18, starting transfers between devices: 18.5 us -> 23.5 us  [swapped(): lax.ppermute(array, axis, [(i, i ^ bit) for i in range(lax.axis_size(axis...]
    ppermute x14 -> x18, waiting for transfers between devices: 20.8 us -> 16.4 us  [swapped(): lax.ppermute(array, axis, [(i, i ^ bit) for i in range(lax.axis_size(axis...]
    pallas_call x19 -> x21, Pallas kernels: 12.5 us -> 12.5 us  [call(): pl.pallas_call(body, out_shape=[*out_shape, *(jax.ShapeDtypeStruct(a.shap...]
  transfers between devices with their start and end apart: 16 -> 20, of which waited for: 9 -> 10; matrix products, arithmetic and copies ran while one was open for 0% -> 0% of each run, Pallas kernels for 17% -> 17%
where the time goes in v20:
time: 61 us; the launch traced here: 60.9 us
  starting transfers between devices  26.6 us (44%)
  waiting for transfers between devices  17.9 us (29%)
  Pallas kernels  12.5 us (20%)
  between operations  2.13 us (3%)
  local copies, waits for them, and re-layouts  1.66 us (3%)
    ppermute x18, starting transfers between devices, swapped(): lax.ppermute(array, axis, [(i, i ^ bit) for i in range(lax.axis_size(axis...  23.5 us
    ppermute x18, waiting for transfers between devices, swapped(): lax.ppermute(array, axis, [(i, i ^ bit) for i in range(lax.axis_size(axis...  16.4 us
    pallas_call x21, Pallas kernels, call(): pl.pallas_call(body, out_shape=[*out_shape, *(jax.ShapeDtypeStruct(a.shap...  12.5 us
    ppermute x2, starting transfers between devices, swapped_by_core(): return lax.ppermute(array, ('blk', 'grp'), route)  3.13 us
    unnamed x6, local copies, waits for them, and re-layouts  1.66 us
    ppermute x2, waiting for transfers between devices, swapped_by_core(): return lax.ppermute(array, ('blk', 'grp'), route)  1.57 us
  transfers between devices with their start and end apart: 20, of which 10 were waited for; matrix products, arithmetic and copies ran while one was open for 0% of the time, Pallas kernels for 17%

profile of v20, /device:TPU:0, one launch (start us, length us, event | category | flops | bytes accessed | tf_op | source)
XLA Modules:
  0.0 60.9 jit_solution(14468130536702098581)
XLA Ops:
  0.6 4.1 %collective-permute-start = (bf16[128,1152]{1,0:T(8,128)(2,1)}, bf16[128,1152]{1,0:T(8,128)(2,1)S(1)}, u32[]{:S(2)}, u32[]{:S(2)}) collective-permute-start(bf16[128,1152]{1,0:T(8,128)(2,1)} %refs_6_.7), channel_id=1, source_target_pairs={{0,4},{1,5},{2,6},{3,7},{4,0},{5,1},{6,2},{7,3},{8,12},{9,13},{10,... | collective-permute-start | bytes 884744 | tf_op jit(solution)/shard_map/ppermute | solution.py:301
  4.7 1.6 %collective-permute-start.1 = (bf16[128,1152]{1,0:T(8,128)(2,1)}, bf16[128,1152]{1,0:T(8,128)(2,1)S(1)}, u32[]{:S(2)}, u32[]{:S(2)}) collective-permute-start(bf16[128,1152]{1,0:T(8,128)(2,1)} %refs_0_.10), channel_id=1, source_target_pairs={{0,2},{1,3},{2,0},{3,1},{4,6},{5,7},{6,4},{7,5},{8,10},{9,11},{10,... | collective-permute-start | bytes 884744 | tf_op jit(solution)/shard_map/ppermute | solution.py:301
  6.3 0.0 copy-start.1
  6.3 1.0 %copy-done.1 = bf16[128,1152]{1,0:T(8,128)(2,1)S(1)} copy-done((bf16[128,1152]{1,0:T(8,128)(2,1)S(1)}, bf16[128,1152]{1,0:T(8,128)(2,1)}, u32[]{:S(2)}) %copy-start.1) | copy-done | bytes 294936
  7.3 0.0 copy-start.2
  7.3 0.7 %copy-done.2 = s32[128]{0:T(128)S(1)} copy-done((s32[128]{0:T(128)S(1)}, s32[128]{0:T(128)}, u32[]{:S(2)}) %copy-start.2) | copy-done | bytes 536
  8.0 0.0 copy-start
  8.0 1.6 %collective-permute-start.4 = (bf16[136,1152]{1,0:T(8,128)(2,1)S(1)}, bf16[136,1152]{1,0:T(8,128)(2,1)S(1)}, u32[]{:S(2)}, u32[]{:S(2)}) collective-permute-start(bf16[136,1152]{1,0:T(8,128)(2,1)S(1)} %labelled.3.refs_2_.refs_7_.refs_3_), channel_id=1, source_target_pairs={{0,8},{8,0},{16,24},{24,16},{1,9},{9,1},{17,25},{25,17},{2,10},{10... | collective-permute-start | bytes 940040 | tf_op jit(solution)/shard_map/ppermute | solution.py:301
  9.6 1.5 %collective-permute-start.3 = (bf16[128,1152]{1,0:T(8,128)(2,1)}, bf16[128,1152]{1,0:T(8,128)(2,1)S(1)}, u32[]{:S(2)}, u32[]{:S(2)}) collective-permute-start(bf16[128,1152]{1,0:T(8,128)(2,1)} %refs_6_.7), channel_id=1, source_target_pairs={{0,16},{8,24},{16,0},{24,8},{1,17},{9,25},{17,1},{25,9},{2,18},{10... | collective-permute-start | bytes 884744 | tf_op jit(solution)/shard_map/ppermute | solution.py:301
  11.1 0.4 collective-permute-start.2
  11.5 6.8 %collective-permute-done.refs_0_ = bf16[128,1152]{1,0:T(8,128)(2,1)S(1)} collective-permute-done((bf16[128,1152]{1,0:T(8,128)(2,1)}, bf16[128,1152]{1,0:T(8,128)(2,1)S(1)}, u32[]{:S(2)}, u32[]{:S(2)}) %collective-permute-start) | collective-permute-done | bytes 294944 | tf_op jit(solution)/shard_map/ppermute | solution.py:301
  18.4 0.3 collective-permute-done.2.refs_1_
  18.6 0.0 collective-permute-done.1.refs_0_
  18.7 0.0 collective-permute-done.3.refs_3_.refs_4_.refs_5_
  18.7 0.0 collective-permute-done.4.refs_4_.refs_5_
  18.7 0.0 copy-done
  18.8 0.1 bundled.3
  18.9 0.1 collective-permute-start.7
  19.0 0.1 crossed.1
  19.0 1.6 %collective-permute-start.5 = (bf16[136,1152]{1,0:T(8,128)(2,1)S(1)}, bf16[136,1152]{1,0:T(8,128)(2,1)S(1)}, u32[]{:S(2)}, u32[]{:S(2)}) collective-permute-start(bf16[136,1152]{1,0:T(8,128)(2,1)S(1)} %get-tuple-element.38), channel_id=1, source_target_pairs={{0,16},{1,9},{2,18},{3,11},{4,20},{5,13},{6,22},{7,15},{8,24},{9,1... | collective-permute-start | bytes 940040 | tf_op jit(solution)/shard_map/ppermute | solution.py:310
  20.7 1.5 %collective-permute-start.6 = (bf16[136,1152]{1,0:T(8,128)(2,1)S(1)}, bf16[136,1152]{1,0:T(8,128)(2,1)S(1)}, u32[]{:S(2)}, u32[]{:S(2)}) collective-permute-start(bf16[136,1152]{1,0:T(8,128)(2,1)S(1)} %get-tuple-element.39), channel_id=1, source_target_pairs={{0,8},{1,17},{2,10},{3,19},{4,12},{5,21},{6,14},{7,23},{8,0},{9,25... | collective-permute-start | bytes 940040 | tf_op jit(solution)/shard_map/ppermute | solution.py:310
  23.5 0.0 collective-permute-done.7.refs_8_.refs_7_
  23.5 1.9 %early_sums.3 = (f32[128,1152]{1,0:T(8,128)S(1)}, f32[128,1152]{1,0:T(8,128)S(1)}, f32[128,1152]{1,0:T(8,128)S(1)}) custom-call(f32[1]{0:T(128)S(6)} %copy.25.refs_0_, f32[1]{0:T(128)S(6)} %copy.26.refs_1_, bf16[128,1152]{1,0:T(8,128)(2,1)S(1)} %held.3.refs_2_.refs_0_.refs_4_, bf16[136,1152]{1,0:T(8,128)(2,1)S(1)} %labelled.2.refs_1_.refs_3_.refs_4_, ...), custom_call_target="tpu_custom_call" | custom-call | flops 2304 | bytes 2304 | tf_op jit(solution)/shard_map/early_sums/pallas_call | solution.py:93
  25.4 1.9 %early_sums.2 = (f32[128,1152]{1,0:T(8,128)S(1)}, f32[128,1152]{1,0:T(8,128)S(1)}, f32[128,1152]{1,0:T(8,128)S(1)}) custom-call(f32[1]{0:T(128)S(6)} %copy.25.refs_0_, f32[1]{0:T(128)S(6)} %copy.26.refs_1_, bf16[128,1152]{1,0:T(8,128)(2,1)S(1)} %held.3.refs_2_.refs_0_.refs_4_, bf16[136,1152]{1,0:T(8,128)(2,1)S(1)} %labelled.2.refs_1_.refs_3_.refs_4_, ...), custom_call_target="tpu_custom_call" | custom-call | flops 2304 | bytes 2304 | tf_op jit(solution)/shard_map/early_sums/pallas_call | solution.py:93
  27.3 1.3 %collective-permute-done.5.refs_2_.refs_6_.refs_5_.refs_13_.refs_8_ = bf16[136,1152]{1,0:T(8,128)(2,1)S(1)} collective-permute-done((bf16[136,1152]{1,0:T(8,128)(2,1)S(1)}, bf16[136,1152]{1,0:T(8,128)(2,1)S(1)}, u32[]{:S(2)}, u32[]{:S(2)}) %collective-permute-start.5) | collective-permute-done | bytes 313376 | tf_op jit(solution)/shard_map/ppermute | solution.py:310
  28.7 0.2 collective-permute-done.6.refs_6_.refs_5_.refs_2_.refs_8_.refs_13_
  28.9 0.3 collective-permute-start.9
  29.2 0.2 collective-permute-start.8
  29.4 1.3 %late_rows_begun.2.refs_4_ = f32[128,1152]{1,0:T(8,128)S(1)} custom-call(f32[1]{0:T(128)S(6)} %copy.25.refs_0_, f32[1]{0:T(128)S(6)} %copy.26.refs_1_, bf16[136,1152]{1,0:T(8,128)(2,1)S(1)} %collective-permute-done.5.refs_2_.refs_6_.refs_5_.refs_13_.refs_8_, bf16[136,1152]{1,0:T(8,128)(2,1)S(1)} %labelled.3.refs_2_.refs_7_.refs_3_, ...), custom_call_target="tpu_custom_call" | custom-call | flops 896 | bytes 896 | tf_op jit(solution)/shard_map/late_rows_begun/pallas_call | solution.py:93
  30.8 0.0 collective-permute-done.9.refs_3_.refs_6_.refs_9_.refs_14_
  30.8 0.2 collective-permute-done.8.refs_6_.refs_3_.refs_14_.refs_9_
  31.0 0.6 %late_rows.2 = (s16[136,640]{1,0:T(8,128)(2,1)S(1)}, s16[136,512]{1,0:T(8,128)(2,1)S(1)}) custom-call(f32[1]{0:T(128)S(6)} %copy.25.refs_0_, f32[1]{0:T(128)S(6)} %copy.26.refs_1_, bf16[136,1152]{1,0:T(8,128)(2,1)S(1)} %collective-permute-done.5.refs_2_.refs_6_.refs_5_.refs_13_.refs_8_, ...), custom_call_target="tpu_custom_call" | custom-call | flops 128 | bytes 128 | tf_op jit(solution)/shard_map/late_rows/pallas_call | solution.py:93
  31.6 1.6 %collective-permute-start.12 = (s16[136,640]{1,0:T(8,128)(2,1)S(1)}, s16[136,640]{1,0:T(8,128)(2,1)S(1)}, u32[]{:S(2)}, u32[]{:S(2)}) collective-permute-start(s16[136,640]{1,0:T(8,128)(2,1)S(1)} %get-tuple-element.54.refs_8_), channel_id=1, source_target_pairs={{0,16},{8,24},{16,0},{24,8},{1,17},{9,25},{17,1},{25,9},{2,18},{10... | collective-permute-start | bytes 522248 | tf_op jit(solution)/shard_map/ppermute | solution.py:301
  33.2 1.4 %late_rows_begun.3.refs_4_ = f32[128,1152]{1,0:T(8,128)S(1)} custom-call(f32[1]{0:T(128)S(6)} %copy.25.refs_0_, f32[1]{0:T(128)S(6)} %copy.26.refs_1_, bf16[136,1152]{1,0:T(8,128)(2,1)S(1)} %collective-permute-done.6.refs_6_.refs_5_.refs_2_.refs_8_.refs_13_, bf16[128,1152]{1,0:T(8,128)(2,1)S(1)} %copy-done, ...), custom_call_target="tpu_custom_call" | custom-call | flops 896 | bytes 896 | tf_op jit(solution)/shard_map/late_rows_begun/pallas_call | solution.py:93
  34.6 0.6 %late_rows.3 = (s16[136,640]{1,0:T(8,128)(2,1)S(1)}, s16[136,512]{1,0:T(8,128)(2,1)S(1)}) custom-call(f32[1]{0:T(128)S(6)} %copy.25.refs_0_, f32[1]{0:T(128)S(6)} %copy.26.refs_1_, bf16[136,1152]{1,0:T(8,128)(2,1)S(1)} %collective-permute-done.6.refs_6_.refs_5_.refs_2_.refs_8_.refs_13_, ...), custom_call_target="tpu_custom_call" | custom-call | flops 128 | bytes 128 | tf_op jit(solution)/shard_map/late_rows/pallas_call | solution.py:93
  35.2 1.8 %collective-permute-start.10 = (s16[136,640]{1,0:T(8,128)(2,1)S(1)}, s16[136,640]{1,0:T(8,128)(2,1)S(1)}, u32[]{:S(2)}, u32[]{:S(2)}) collective-permute-start(s16[136,640]{1,0:T(8,128)(2,1)S(1)} %get-tuple-element.56.refs_15_), channel_id=1, source_target_pairs={{0,8},{8,0},{16,24},{24,16},{1,9},{9,1},{17,25},{25,17},{2,10},{10... | collective-permute-start | bytes 522248 | tf_op jit(solution)/shard_map/ppermute | solution.py:301
  37.0 1.3 %late_columns.2 = (f32[128,1152]{1,0:T(8,128)S(1)}, f32[128,1152]{1,0:T(8,128)S(1)}, s16[136,1152]{1,0:T(8,128)(2,1)S(1)}) custom-call(f32[1]{0:T(128)S(6)} %copy.25.refs_0_, f32[1]{0:T(128)S(6)} %copy.26.refs_1_, bf16[128,1152]{1,0:T(8,128)(2,1)S(1)} %held.3.refs_2_.refs_0_.refs_4_, bf16[136,1152]{1,0:T(8,128)(2,1)S(1)} %labelled.2.refs_1_.refs_3_.refs_4_, ...), custom_call_target="tpu_custom_call" | custom-call | flops 768 | bytes 768 | tf_op jit(solution)/shard_map/late_columns/pallas_call | solution.py:93
  38.3 1.5 %late_columns.3 = (f32[128,1152]{1,0:T(8,128)S(1)}, f32[128,1152]{1,0:T(8,128)S(1)}, s16[136,1152]{1,0:T(8,128)(2,1)S(1)}) custom-call(f32[1]{0:T(128)S(6)} %copy.25.refs_0_, f32[1]{0:T(128)S(6)} %copy.26.refs_1_, bf16[128,1152]{1,0:T(8,128)(2,1)S(1)} %held.3.refs_2_.refs_0_.refs_4_, bf16[136,1152]{1,0:T(8,128)(2,1)S(1)} %labelled.2.refs_1_.refs_3_.refs_4_, ...), custom_call_target="tpu_custom_call" | custom-call | flops 768 | bytes 768 | tf_op jit(solution)/shard_map/late_columns/pallas_call | solution.py:93
  39.9 0.0 collective-permute-done.12.refs_1_
  39.9 0.1 passed_sum.5
  40.0 1.4 %collective-permute-start.13 = (s16[136,640]{1,0:T(8,128)(2,1)S(1)}, s16[136,640]{1,0:T(8,128)(2,1)S(1)}, u32[]{:S(2)}, u32[]{:S(2)}) collective-permute-start(s16[136,640]{1,0:T(8,128)(2,1)S(1)} %get-tuple-element.64), channel_id=1, source_target_pairs={{0,4},{1,5},{2,6},{3,7},{4,0},{5,1},{6,2},{7,3},{8,12},{9,13},{10,... | collective-permute-start | bytes 522248 | tf_op jit(solution)/shard_map/ppermute | solution.py:301
  41.4 0.5 collective-permute-start.14
  41.9 0.0 collective-permute-done.10.refs_1_
  41.9 0.1 passed_sum.4
  42.0 2.4 %collective-permute-start.16 = (s16[136,640]{1,0:T(8,128)(2,1)S(1)}, s16[136,640]{1,0:T(8,128)(2,1)S(1)}, u32[]{:S(2)}, u32[]{:S(2)}) collective-permute-start(s16[136,640]{1,0:T(8,128)(2,1)S(1)} %get-tuple-element.68), channel_id=1, source_target_pairs={{0,2},{1,3},{2,0},{3,1},{4,6},{5,7},{6,4},{7,5},{8,10},{9,11},{10,... | collective-permute-start | bytes 522248 | tf_op jit(solution)/shard_map/ppermute | solution.py:301
  44.4 1.0 %collective-permute-start.17 = (s16[136,512]{1,0:T(8,128)(2,1)S(1)}, s16[136,512]{1,0:T(8,128)(2,1)S(1)}, u32[]{:S(2)}, u32[]{:S(2)}) collective-permute-start(s16[136,512]{1,0:T(8,128)(2,1)S(1)} %get-tuple-element.69), channel_id=1, source_target_pairs={{0,8},{8,0},{16,24},{24,16},{1,9},{9,1},{17,25},{25,17},{2,10},{10... | collective-permute-start | bytes 417800 | tf_op jit(solution)/shard_map/ppermute | solution.py:301
  45.5 0.8 %collective-permute-start.19 = (s16[136,1152]{1,0:T(8,128)(2,1)S(1)}, s16[136,1152]{1,0:T(8,128)(2,1)S(1)}, u32[]{:S(2)}, u32[]{:S(2)}) collective-permute-start(s16[136,1152]{1,0:T(8,128)(2,1)S(1)} %get-tuple-element.73), channel_id=1, source_target_pairs={{0,16},{8,24},{16,0},{24,8},{1,17},{9,25},{17,1},{25,9},{2,18},{10... | collective-permute-start | bytes 940040 | tf_op jit(solution)/shard_map/ppermute | solution.py:301
  46.2 0.3 collective-permute-done.14.refs_1_
  46.6 1.4 %collective-permute-start.11 = (s16[136,1152]{1,0:T(8,128)(2,1)S(1)}, s16[136,1152]{1,0:T(8,128)(2,1)S(1)}, u32[]{:S(2)}, u32[]{:S(2)}) collective-permute-start(s16[136,1152]{1,0:T(8,128)(2,1)S(1)} %get-tuple-element.62), channel_id=1, source_target_pairs={{0,8},{8,0},{16,24},{24,16},{1,9},{9,1},{17,25},{25,17},{2,10},{10... | collective-permute-start | bytes 940040 | tf_op jit(solution)/shard_map/ppermute | solution.py:301
  48.0 2.7 %collective-permute-done.13.refs_2_.refs_0_ = s16[136,640]{1,0:T(8,128)(2,1)S(1)} collective-permute-done((s16[136,640]{1,0:T(8,128)(2,1)S(1)}, s16[136,640]{1,0:T(8,128)(2,1)S(1)}, u32[]{:S(2)}, u32[]{:S(2)}) %collective-permute-start.13) | collective-permute-done | bytes 174112 | tf_op jit(solution)/shard_map/ppermute | solution.py:301
  50.7 0.1 passed_sum.6.refs_3_
  50.8 0.1 collective-permute-start.15
  50.9 0.2 collective-permute-done.17.refs_1_
  51.1 0.0 collective-permute-done.16.refs_2_
  51.1 0.1 passed_sum.7
  51.2 2.7 %collective-permute-start.18 = (s16[136,512]{1,0:T(8,128)(2,1)S(1)}, s16[136,512]{1,0:T(8,128)(2,1)S(1)}, u32[]{:S(2)}, u32[]{:S(2)}) collective-permute-start(s16[136,512]{1,0:T(8,128)(2,1)S(1)} %passed_sum.7), channel_id=1, source_target_pairs={{0,2},{1,3},{2,0},{3,1},{4,6},{5,7},{6,4},{7,5},{8,10},{9,11},{10,... | collective-permute-start | bytes 417800 | tf_op jit(solution)/shard_map/ppermute | solution.py:301
  53.8 5.6 %collective-permute-done.15.refs_1_ = s16[136,512]{1,0:T(8,128)(2,1)S(1)} collective-permute-done((s16[136,512]{1,0:T(8,128)(2,1)S(1)}, s16[136,512]{1,0:T(8,128)(2,1)S(1)}, u32[]{:S(2)}, u32[]{:S(2)}) %collective-permute-start.15) | collective-permute-done | bytes 139296 | tf_op jit(solution)/shard_map/ppermute | solution.py:301
  59.4 0.2 collective-permute-done.18.refs_3_
  59.6 0.0 collective-permute-done.19.refs_6_
  59.6 0.0 collective-permute-done.11.refs_2_
  59.6 1.2 %output_sums.1 = (f32[128,1152]{1,0:T(8,128)}, f32[128,1152]{1,0:T(8,128)}) custom-call(f32[1]{0:T(128)S(6)} %copy.25.refs_0_, f32[128,1152]{1,0:T(8,128)S(1)} %get-tuple-element.59.refs_1_, s16[136,1152]{1,0:T(8,128)(2,1)S(1)} %collective-permute-done.11.refs_2_, s16[136,640]{1,0:T(8,128)(2,1)S(1)} %get-tuple-element.70.refs_3_, ...), custom_call_target="tpu_custom_call" | custom-call | flops 128 | bytes 128 | tf_op jit(solution)/shard_map/output_sums/pallas_call | solution.py:93
  (6 shorter events, 0.1 us)
Async XLA Ops:
  0.6 17.8 %collective-permute-start = (bf16[128,1152]{1,0:T(8,128)(2,1)}, bf16[128,1152]{1,0:T(8,128)(2,1)S(1)}, u32[]{:S(2)}, u32[]{:S(2)}) collective-permute-start(bf16[128,1152]{1,0:T(8,128)(2,1)} %refs_6_.7), channel_id=1, source_target_pairs={{0,4},{1,5},{2,6},{3,7},{4,0},{5,1},{6,2},{7,3},{8,12},{9,13},{10,... | collective-permute-start | bytes 884744 | tf_op jit(solution)/shard_map/ppermute | solution.py:301
  4.7 13.9 %collective-permute-start.1 = (bf16[128,1152]{1,0:T(8,128)(2,1)}, bf16[128,1152]{1,0:T(8,128)(2,1)S(1)}, u32[]{:S(2)}, u32[]{:S(2)}) collective-permute-start(bf16[128,1152]{1,0:T(8,128)(2,1)} %refs_0_.10), channel_id=1, source_target_pairs={{0,2},{1,3},{2,0},{3,1},{4,6},{5,7},{6,4},{7,5},{8,10},{9,11},{10,... | collective-permute-start | bytes 884744 | tf_op jit(solution)/shard_map/ppermute | solution.py:301
  6.3 1.0 %copy-start.1 = (bf16[128,1152]{1,0:T(8,128)(2,1)S(1)}, bf16[128,1152]{1,0:T(8,128)(2,1)}, u32[]{:S(2)}) copy-start(bf16[128,1152]{1,0:T(8,128)(2,1)} %refs_0_.10) | copy-start | bytes 884740
  7.3 0.7 %copy-start.2 = (s32[128]{0:T(128)S(1)}, s32[128]{0:T(128)}, u32[]{:S(2)}) copy-start(s32[128]{0:T(128)} %param.7) | copy-start | bytes 1540
  8.0 10.8 %copy-start = (bf16[128,1152]{1,0:T(8,128)(2,1)S(1)}, bf16[128,1152]{1,0:T(8,128)(2,1)}, u32[]{:S(2)}) copy-start(bf16[128,1152]{1,0:T(8,128)(2,1)} %refs_6_.7) | copy-start | bytes 884740
  8.0 10.7 %collective-permute-start.4 = (bf16[136,1152]{1,0:T(8,128)(2,1)S(1)}, bf16[136,1152]{1,0:T(8,128)(2,1)S(1)}, u32[]{:S(2)}, u32[]{:S(2)}) collective-permute-start(bf16[136,1152]{1,0:T(8,128)(2,1)S(1)} %labelled.3.refs_2_.refs_7_.refs_3_), channel_id=1, source_target_pairs={{0,8},{8,0},{16,24},{24,16},{1,9},{9,1},{17,25},{25,17},{2,10},{10... | collective-permute-start | bytes 940040 | tf_op jit(solution)/shard_map/ppermute | solution.py:301
  9.6 9.2 %collective-permute-start.3 = (bf16[128,1152]{1,0:T(8,128)(2,1)}, bf16[128,1152]{1,0:T(8,128)(2,1)S(1)}, u32[]{:S(2)}, u32[]{:S(2)}) collective-permute-start(bf16[128,1152]{1,0:T(8,128)(2,1)} %refs_6_.7), channel_id=1, source_target_pairs={{0,16},{8,24},{16,0},{24,8},{1,17},{9,25},{17,1},{25,9},{2,18},{10... | collective-permute-start | bytes 884744 | tf_op jit(solution)/shard_map/ppermute | solution.py:301
  11.1 7.6 %collective-permute-start.2 = (s32[1,128]{1,0:T(1,128)S(1)}, s32[1,128]{1,0:T(1,128)S(1)}, u32[]{:S(2)}, u32[]{:S(2)}) collective-permute-start(s32[1,128]{1,0:T(1,128)S(1)} %bitcast.2), channel_id=1, source_target_pairs={{0,2},{1,3},{2,0},{3,1},{4,6},{5,7},{6,4},{7,5},{8,10},{9,11},{10,... | collective-permute-start | bytes 1544 | tf_op jit(solution)/shard_map/ppermute | solution.py:301
  18.9 4.6 %collective-permute-start.7 = (bf16[792,1152]{1,0:T(8,128)(2,1)S(1)}, bf16[792,1152]{1,0:T(8,128)(2,1)S(1)}, u32[]{:S(2)}, u32[]{:S(2)}) collective-permute-start(bf16[792,1152]{1,0:T(8,128)(2,1)S(1)} %bundled.3), channel_id=1, source_target_pairs={{0,1},{1,0},{2,3},{3,2},{4,5},{5,4},{6,7},{7,6},{8,9},{9,8},{10,11... | collective-permute-start | bytes 5474312 | tf_op jit(solution)/shard_map/ppermute | solution.py:301
  19.0 9.6 %collective-permute-start.5 = (bf16[136,1152]{1,0:T(8,128)(2,1)S(1)}, bf16[136,1152]{1,0:T(8,128)(2,1)S(1)}, u32[]{:S(2)}, u32[]{:S(2)}) collective-permute-start(bf16[136,1152]{1,0:T(8,128)(2,1)S(1)} %get-tuple-element.38), channel_id=1, source_target_pairs={{0,16},{1,9},{2,18},{3,11},{4,20},{5,13},{6,22},{7,15},{8,24},{9,1... | collective-permute-start | bytes 940040 | tf_op jit(solution)/shard_map/ppermute | solution.py:310
  20.7 8.2 %collective-permute-start.6 = (bf16[136,1152]{1,0:T(8,128)(2,1)S(1)}, bf16[136,1152]{1,0:T(8,128)(2,1)S(1)}, u32[]{:S(2)}, u32[]{:S(2)}) collective-permute-start(bf16[136,1152]{1,0:T(8,128)(2,1)S(1)} %get-tuple-element.39), channel_id=1, source_target_pairs={{0,8},{1,17},{2,10},{3,19},{4,12},{5,21},{6,14},{7,23},{8,0},{9,25... | collective-permute-start | bytes 940040 | tf_op jit(solution)/shard_map/ppermute | solution.py:310
  28.9 1.9 %collective-permute-start.9 = (bf16[136,1152]{1,0:T(8,128)(2,1)S(1)}, bf16[136,1152]{1,0:T(8,128)(2,1)S(1)}, u32[]{:S(2)}, u32[]{:S(2)}) collective-permute-start(bf16[136,1152]{1,0:T(8,128)(2,1)S(1)} %collective-permute-done.5.refs_2_.refs_6_.refs_5_.refs_13_.refs_8_), channel_id=1, source_target_pairs={{0,1},{1,0},{2,3},{3,2},{4,5},{5,4},{6,7},{7,6},{8,9},{9,8},{10,11... | collective-permute-start | bytes 940040 | tf_op jit(solution)/shard_map/ppermute | solution.py:301
  29.2 1.7 %collective-permute-start.8 = (bf16[136,1152]{1,0:T(8,128)(2,1)S(1)}, bf16[136,1152]{1,0:T(8,128)(2,1)S(1)}, u32[]{:S(2)}, u32[]{:S(2)}) collective-permute-start(bf16[136,1152]{1,0:T(8,128)(2,1)S(1)} %collective-permute-done.6.refs_6_.refs_5_.refs_2_.refs_8_.refs_13_), channel_id=1, source_target_pairs={{0,1},{1,0},{2,3},{3,2},{4,5},{5,4},{6,7},{7,6},{8,9},{9,8},{10,11... | collective-permute-start | bytes 940040 | tf_op jit(solution)/shard_map/ppermute | solution.py:301
  31.6 8.3 %collective-permute-start.12 = (s16[136,640]{1,0:T(8,128)(2,1)S(1)}, s16[136,640]{1,0:T(8,128)(2,1)S(1)}, u32[]{:S(2)}, u32[]{:S(2)}) collective-permute-start(s16[136,640]{1,0:T(8,128)(2,1)S(1)} %get-tuple-element.54.refs_8_), channel_id=1, source_target_pairs={{0,16},{8,24},{16,0},{24,8},{1,17},{9,25},{17,1},{25,9},{2,18},{10... | collective-permute-start | bytes 522248 | tf_op jit(solution)/shard_map/ppermute | solution.py:301
  35.2 6.7 %collective-permute-start.10 = (s16[136,640]{1,0:T(8,128)(2,1)S(1)}, s16[136,640]{1,0:T(8,128)(2,1)S(1)}, u32[]{:S(2)}, u32[]{:S(2)}) collective-permute-start(s16[136,640]{1,0:T(8,128)(2,1)S(1)} %get-tuple-element.56.refs_15_), channel_id=1, source_target_pairs={{0,8},{8,0},{16,24},{24,16},{1,9},{9,1},{17,25},{25,17},{2,10},{10... | collective-permute-start | bytes 522248 | tf_op jit(solution)/shard_map/ppermute | solution.py:301
  40.0 10.7 %collective-permute-start.13 = (s16[136,640]{1,0:T(8,128)(2,1)S(1)}, s16[136,640]{1,0:T(8,128)(2,1)S(1)}, u32[]{:S(2)}, u32[]{:S(2)}) collective-permute-start(s16[136,640]{1,0:T(8,128)(2,1)S(1)} %get-tuple-element.64), channel_id=1, source_target_pairs={{0,4},{1,5},{2,6},{3,7},{4,0},{5,1},{6,2},{7,3},{8,12},{9,13},{10,... | collective-permute-start | bytes 522248 | tf_op jit(solution)/shard_map/ppermute | solution.py:301
  41.4 5.2 %collective-permute-start.14 = (s16[136,512]{1,0:T(8,128)(2,1)S(1)}, s16[136,512]{1,0:T(8,128)(2,1)S(1)}, u32[]{:S(2)}, u32[]{:S(2)}) collective-permute-start(s16[136,512]{1,0:T(8,128)(2,1)S(1)} %get-tuple-element.65), channel_id=1, source_target_pairs={{0,16},{8,24},{16,0},{24,8},{1,17},{9,25},{17,1},{25,9},{2,18},{10... | collective-permute-start | bytes 417800 | tf_op jit(solution)/shard_map/ppermute | solution.py:301
  42.0 9.0 %collective-permute-start.16 = (s16[136,640]{1,0:T(8,128)(2,1)S(1)}, s16[136,640]{1,0:T(8,128)(2,1)S(1)}, u32[]{:S(2)}, u32[]{:S(2)}) collective-permute-start(s16[136,640]{1,0:T(8,128)(2,1)S(1)} %get-tuple-element.68), channel_id=1, source_target_pairs={{0,2},{1,3},{2,0},{3,1},{4,6},{5,7},{6,4},{7,5},{8,10},{9,11},{10,... | collective-permute-start | bytes 522248 | tf_op jit(solution)/shard_map/ppermute | solution.py:301
  44.4 6.6 %collective-permute-start.17 = (s16[136,512]{1,0:T(8,128)(2,1)S(1)}, s16[136,512]{1,0:T(8,128)(2,1)S(1)}, u32[]{:S(2)}, u32[]{:S(2)}) collective-permute-start(s16[136,512]{1,0:T(8,128)(2,1)S(1)} %get-tuple-element.69), channel_id=1, source_target_pairs={{0,8},{8,0},{16,24},{24,16},{1,9},{9,1},{17,25},{25,17},{2,10},{10... | collective-permute-start | bytes 417800 | tf_op jit(solution)/shard_map/ppermute | solution.py:301
  45.5 14.2 %collective-permute-start.19 = (s16[136,1152]{1,0:T(8,128)(2,1)S(1)}, s16[136,1152]{1,0:T(8,128)(2,1)S(1)}, u32[]{:S(2)}, u32[]{:S(2)}) collective-permute-start(s16[136,1152]{1,0:T(8,128)(2,1)S(1)} %get-tuple-element.73), channel_id=1, source_target_pairs={{0,16},{8,24},{16,0},{24,8},{1,17},{9,25},{17,1},{25,9},{2,18},{10... | collective-permute-start | bytes 940040 | tf_op jit(solution)/shard_map/ppermute | solution.py:301
  46.6 13.1 %collective-permute-start.11 = (s16[136,1152]{1,0:T(8,128)(2,1)S(1)}, s16[136,1152]{1,0:T(8,128)(2,1)S(1)}, u32[]{:S(2)}, u32[]{:S(2)}) collective-permute-start(s16[136,1152]{1,0:T(8,128)(2,1)S(1)} %get-tuple-element.62), channel_id=1, source_target_pairs={{0,8},{8,0},{16,24},{24,16},{1,9},{9,1},{17,25},{25,17},{2,10},{10... | collective-permute-start | bytes 940040 | tf_op jit(solution)/shard_map/ppermute | solution.py:301
  50.8 8.6 %collective-permute-start.15 = (s16[136,512]{1,0:T(8,128)(2,1)S(1)}, s16[136,512]{1,0:T(8,128)(2,1)S(1)}, u32[]{:S(2)}, u32[]{:S(2)}) collective-permute-start(s16[136,512]{1,0:T(8,128)(2,1)S(1)} %passed_sum.6.refs_3_), channel_id=1, source_target_pairs={{0,4},{1,5},{2,6},{3,7},{4,0},{5,1},{6,2},{7,3},{8,12},{9,13},{10,... | collective-permute-start | bytes 417800 | tf_op jit(solution)/shard_map/ppermute | solution.py:301
  51.2 8.5 %collective-permute-start.18 = (s16[136,512]{1,0:T(8,128)(2,1)S(1)}, s16[136,512]{1,0:T(8,128)(2,1)S(1)}, u32[]{:S(2)}, u32[]{:S(2)}) collective-permute-start(s16[136,512]{1,0:T(8,128)(2,1)S(1)} %passed_sum.7), channel_id=1, source_target_pairs={{0,2},{1,3},{2,0},{3,1},{4,6},{5,7},{6,4},{7,5},{8,10},{9,11},{10,... | collective-permute-start | bytes 417800 | tf_op jit(solution)/shard_map/ppermute | solution.py:301

commit v21 on v20

--- a/solution.py
+++ b/solution.py
@@ -321,6 +321,8 @@
         for m in reversed(range(1 << s)):
             n = m | 1 << s
             first, *begun = passed_sum(kept[n], received[n], 0, waiting + last)
+            if waiting:
+                begun_with = [first]
             for r, c in zip(received[1:], begun):
                 r[0] = r[0] + (sent(c, steps[-1]),)
             received[0] += [(sent(c, steps[-1]),) for c in begun[len(waiting) :]]
@@ -328,7 +330,7 @@
             (second,) = passed_sum(kept[n], received[n], 1, (), [first[0], *after])
             received[m].append((first, sent(second, steps[s])))
             waiting, last, after = [], [], [second]
-    return kept[0], received[0], after
+    return kept[0], received[0], after, begun_with
 
 
 def in_order(arrays, after=(), cost=HELD_COST):
@@ -419,7 +421,7 @@
             other[c][m], other[1 - c][m] = [whole(a) for a in swaps[m]]
         tables.append((own, other))
     after = ()
-    coded, kept = [[None] * half, [None] * half], [None, None]
+    coded = [[None] * half, [None] * half]
     for k in (1, 0):
         columns = [(0, m) for m in range(count)] + [(1, m) for m in early]
         jobs, emits = every_pair(late, columns), ["float"] * len(late)
@@ -429,13 +431,15 @@
         jobs, emits = every_pair(late, columns), ["parts"] * len(late)
         coded[k][1:] = sums("late_rows", k, late, columns, jobs, begun, emits)
         after = coded[k][1]
+    sums_in = [None, None]
+    ordering = ()
     for k in (1, 0):
         columns = both_cores(late)
         jobs, emits = every_pair(early, columns), ["float"] * half + ["whole"]
         *whole_sums, coded[k][0] = sums("late_columns", k, early, columns, jobs, before[k], emits, after)
-        kept[k], after = [s for (s,) in whole_sums], coded[k][0]
-    kept_texts, text_blocks, after = scattered(kept[1], coded[1], steps[1], ())
-    kept_images, image_blocks, _ = scattered(kept[0], coded[0], steps[0], after)
+        kept = [s for (s,) in whole_sums]
+        *sums_in[k], ordering, after = scattered(kept, coded[k], steps[k], ordering)
+    (kept_images, image_blocks), (kept_texts, text_blocks) = sums_in
     ends = ()
     for blocks_in in (text_blocks, image_blocks):
         ends = in_order([part[0] for b in blocks_in if len(b) > 1 for part in b], ends)

time: 61 us -> 60.4 us (level)
  starting transfers between devices: 26.6 us -> 24.6 us
  waiting for transfers between devices: 17.9 us -> 19.5 us
    ppermute x18, starting transfers between devices: 23.5 us -> 21.5 us  [swapped(): lax.ppermute(array, axis, [(i, i ^ bit) for i in range(lax.axis_size(axis...]
    ppermute x18, waiting for transfers between devices: 16.4 us -> 17.9 us  [swapped(): lax.ppermute(array, axis, [(i, i ^ bit) for i in range(lax.axis_size(axis...]
  transfers between devices with their start and end apart: 20 -> 20, of which waited for: 10 -> 9; matrix products, arithmetic and copies ran while one was open for 0% -> 0% of each run, Pallas kernels for 17% -> 17%
where the time goes in v21:
time: 60.4 us; the launch traced here: 60.3 us
  starting transfers between devices  24.6 us (41%)
  waiting for transfers between devices  19.5 us (32%)
  Pallas kernels  12.3 us (20%)
  between operations  2.14 us (4%)
  local copies, waits for them, and re-layouts  1.66 us (3%)
    ppermute x18, starting transfers between devices, swapped(): lax.ppermute(array, axis, [(i, i ^ bit) for i in range(lax.axis_size(axis...  21.5 us
    ppermute x18, waiting for transfers between devices, swapped(): lax.ppermute(array, axis, [(i, i ^ bit) for i in range(lax.axis_size(axis...  17.9 us
    pallas_call x21, Pallas kernels, call(): pl.pallas_call(body, out_shape=[*out_shape, *(jax.ShapeDtypeStruct(a.shap...  12.3 us
    ppermute x2, starting transfers between devices, swapped_by_core(): return lax.ppermute(array, ('blk', 'grp'), route)  3.13 us
    unnamed x6, local copies, waits for them, and re-layouts  1.66 us
    ppermute x2, waiting for transfers between devices, swapped_by_core(): return lax.ppermute(array, ('blk', 'grp'), route)  1.57 us
  transfers between devices with their start and end apart: 20, of which 9 were waited for; matrix products, arithmetic and copies ran while one was open for 0% of the time, Pallas kernels for 17%

profile of v21, /device:TPU:0, one launch (start us, length us, event | category | flops | bytes accessed | tf_op | source)
XLA Modules:
  0.0 60.3 jit_solution(4207653574076155387)
XLA Ops:
  0.6 4.1 %collective-permute-start = (bf16[128,1152]{1,0:T(8,128)(2,1)}, bf16[128,1152]{1,0:T(8,128)(2,1)S(1)}, u32[]{:S(2)}, u32[]{:S(2)}) collective-permute-start(bf16[128,1152]{1,0:T(8,128)(2,1)} %refs_6_.7), channel_id=1, source_target_pairs={{0,4},{1,5},{2,6},{3,7},{4,0},{5,1},{6,2},{7,3},{8,12},{9,13},{10,... | collective-permute-start | bytes 884744 | tf_op jit(solution)/shard_map/ppermute | solution.py:301
  4.7 1.6 %collective-permute-start.1 = (bf16[128,1152]{1,0:T(8,128)(2,1)}, bf16[128,1152]{1,0:T(8,128)(2,1)S(1)}, u32[]{:S(2)}, u32[]{:S(2)}) collective-permute-start(bf16[128,1152]{1,0:T(8,128)(2,1)} %refs_0_.10), channel_id=1, source_target_pairs={{0,2},{1,3},{2,0},{3,1},{4,6},{5,7},{6,4},{7,5},{8,10},{9,11},{10,... | collective-permute-start | bytes 884744 | tf_op jit(solution)/shard_map/ppermute | solution.py:301
  6.3 0.0 copy-start.1
  6.3 1.0 %copy-done.1 = bf16[128,1152]{1,0:T(8,128)(2,1)S(1)} copy-done((bf16[128,1152]{1,0:T(8,128)(2,1)S(1)}, bf16[128,1152]{1,0:T(8,128)(2,1)}, u32[]{:S(2)}) %copy-start.1) | copy-done | bytes 294936
  7.3 0.0 copy-start.2
  7.3 0.7 %copy-done.2 = s32[128]{0:T(128)S(1)} copy-done((s32[128]{0:T(128)S(1)}, s32[128]{0:T(128)}, u32[]{:S(2)}) %copy-start.2) | copy-done | bytes 536
  8.0 0.0 copy-start
  8.0 1.6 %collective-permute-start.4 = (bf16[136,1152]{1,0:T(8,128)(2,1)S(1)}, bf16[136,1152]{1,0:T(8,128)(2,1)S(1)}, u32[]{:S(2)}, u32[]{:S(2)}) collective-permute-start(bf16[136,1152]{1,0:T(8,128)(2,1)S(1)} %labelled.3.refs_2_.refs_7_.refs_3_), channel_id=1, source_target_pairs={{0,8},{8,0},{16,24},{24,16},{1,9},{9,1},{17,25},{25,17},{2,10},{10... | collective-permute-start | bytes 940040 | tf_op jit(solution)/shard_map/ppermute | solution.py:301
  9.6 1.5 %collective-permute-start.3 = (bf16[128,1152]{1,0:T(8,128)(2,1)}, bf16[128,1152]{1,0:T(8,128)(2,1)S(1)}, u32[]{:S(2)}, u32[]{:S(2)}) collective-permute-start(bf16[128,1152]{1,0:T(8,128)(2,1)} %refs_6_.7), channel_id=1, source_target_pairs={{0,16},{8,24},{16,0},{24,8},{1,17},{9,25},{17,1},{25,9},{2,18},{10... | collective-permute-start | bytes 884744 | tf_op jit(solution)/shard_map/ppermute | solution.py:301
  11.1 0.4 collective-permute-start.2
  11.5 6.8 %collective-permute-done.refs_0_ = bf16[128,1152]{1,0:T(8,128)(2,1)S(1)} collective-permute-done((bf16[128,1152]{1,0:T(8,128)(2,1)}, bf16[128,1152]{1,0:T(8,128)(2,1)S(1)}, u32[]{:S(2)}, u32[]{:S(2)}) %collective-permute-start) | collective-permute-done | bytes 294944 | tf_op jit(solution)/shard_map/ppermute | solution.py:301
  18.4 0.3 collective-permute-done.2.refs_1_
  18.6 0.0 collective-permute-done.1.refs_0_
  18.7 0.0 collective-permute-done.3.refs_3_.refs_4_.refs_5_
  18.7 0.0 collective-permute-done.4.refs_4_.refs_5_
  18.7 0.0 copy-done
  18.8 0.1 bundled.3
  18.9 0.1 collective-permute-start.7
  19.0 0.1 crossed.1
  19.0 1.6 %collective-permute-start.5 = (bf16[136,1152]{1,0:T(8,128)(2,1)S(1)}, bf16[136,1152]{1,0:T(8,128)(2,1)S(1)}, u32[]{:S(2)}, u32[]{:S(2)}) collective-permute-start(bf16[136,1152]{1,0:T(8,128)(2,1)S(1)} %get-tuple-element.38), channel_id=1, source_target_pairs={{0,16},{1,9},{2,18},{3,11},{4,20},{5,13},{6,22},{7,15},{8,24},{9,1... | collective-permute-start | bytes 940040 | tf_op jit(solution)/shard_map/ppermute | solution.py:310
  20.7 1.5 %collective-permute-start.6 = (bf16[136,1152]{1,0:T(8,128)(2,1)S(1)}, bf16[136,1152]{1,0:T(8,128)(2,1)S(1)}, u32[]{:S(2)}, u32[]{:S(2)}) collective-permute-start(bf16[136,1152]{1,0:T(8,128)(2,1)S(1)} %get-tuple-element.39), channel_id=1, source_target_pairs={{0,8},{1,17},{2,10},{3,19},{4,12},{5,21},{6,14},{7,23},{8,0},{9,25... | collective-permute-start | bytes 940040 | tf_op jit(solution)/shard_map/ppermute | solution.py:310
  23.5 0.0 collective-permute-done.7.refs_8_.refs_7_
  23.5 1.9 %early_sums.3 = (f32[128,1152]{1,0:T(8,128)S(1)}, f32[128,1152]{1,0:T(8,128)S(1)}, f32[128,1152]{1,0:T(8,128)S(1)}) custom-call(f32[1]{0:T(128)S(6)} %copy.25.refs_0_, f32[1]{0:T(128)S(6)} %copy.26.refs_1_, bf16[128,1152]{1,0:T(8,128)(2,1)S(1)} %held.3.refs_2_.refs_0_.refs_4_, bf16[136,1152]{1,0:T(8,128)(2,1)S(1)} %labelled.2.refs_1_.refs_3_.refs_4_, ...), custom_call_target="tpu_custom_call" | custom-call | flops 2304 | bytes 2304 | tf_op jit(solution)/shard_map/early_sums/pallas_call | solution.py:93
  25.4 1.9 %early_sums.2 = (f32[128,1152]{1,0:T(8,128)S(1)}, f32[128,1152]{1,0:T(8,128)S(1)}, f32[128,1152]{1,0:T(8,128)S(1)}) custom-call(f32[1]{0:T(128)S(6)} %copy.25.refs_0_, f32[1]{0:T(128)S(6)} %copy.26.refs_1_, bf16[128,1152]{1,0:T(8,128)(2,1)S(1)} %held.3.refs_2_.refs_0_.refs_4_, bf16[136,1152]{1,0:T(8,128)(2,1)S(1)} %labelled.2.refs_1_.refs_3_.refs_4_, ...), custom_call_target="tpu_custom_call" | custom-call | flops 2304 | bytes 2304 | tf_op jit(solution)/shard_map/early_sums/pallas_call | solution.py:93
  27.3 1.3 %collective-permute-done.5.refs_2_.refs_6_.refs_5_.refs_13_.refs_8_ = bf16[136,1152]{1,0:T(8,128)(2,1)S(1)} collective-permute-done((bf16[136,1152]{1,0:T(8,128)(2,1)S(1)}, bf16[136,1152]{1,0:T(8,128)(2,1)S(1)}, u32[]{:S(2)}, u32[]{:S(2)}) %collective-permute-start.5) | collective-permute-done | bytes 313376 | tf_op jit(solution)/shard_map/ppermute | solution.py:310
  28.7 0.2 collective-permute-done.6.refs_6_.refs_5_.refs_2_.refs_8_.refs_13_
  28.9 0.3 collective-permute-start.9
  29.2 0.2 collective-permute-start.8
  29.4 1.3 %late_rows_begun.2.refs_4_ = f32[128,1152]{1,0:T(8,128)S(1)} custom-call(f32[1]{0:T(128)S(6)} %copy.25.refs_0_, f32[1]{0:T(128)S(6)} %copy.26.refs_1_, bf16[136,1152]{1,0:T(8,128)(2,1)S(1)} %collective-permute-done.5.refs_2_.refs_6_.refs_5_.refs_13_.refs_8_, bf16[136,1152]{1,0:T(8,128)(2,1)S(1)} %labelled.3.refs_2_.refs_7_.refs_3_, ...), custom_call_target="tpu_custom_call" | custom-call | flops 896 | bytes 896 | tf_op jit(solution)/shard_map/late_rows_begun/pallas_call | solution.py:93
  30.8 0.0 collective-permute-done.9.refs_3_.refs_6_.refs_9_.refs_14_
  30.8 0.2 collective-permute-done.8.refs_6_.refs_3_.refs_14_.refs_9_
  31.0 0.6 %late_rows.2 = (s16[136,640]{1,0:T(8,128)(2,1)S(1)}, s16[136,512]{1,0:T(8,128)(2,1)S(1)}) custom-call(f32[1]{0:T(128)S(6)} %copy.25.refs_0_, f32[1]{0:T(128)S(6)} %copy.26.refs_1_, bf16[136,1152]{1,0:T(8,128)(2,1)S(1)} %collective-permute-done.5.refs_2_.refs_6_.refs_5_.refs_13_.refs_8_, ...), custom_call_target="tpu_custom_call" | custom-call | flops 128 | bytes 128 | tf_op jit(solution)/shard_map/late_rows/pallas_call | solution.py:93
  31.6 1.6 %collective-permute-start.10 = (s16[136,640]{1,0:T(8,128)(2,1)S(1)}, s16[136,640]{1,0:T(8,128)(2,1)S(1)}, u32[]{:S(2)}, u32[]{:S(2)}) collective-permute-start(s16[136,640]{1,0:T(8,128)(2,1)S(1)} %get-tuple-element.54.refs_8_), channel_id=1, source_target_pairs={{0,16},{8,24},{16,0},{24,8},{1,17},{9,25},{17,1},{25,9},{2,18},{10... | collective-permute-start | bytes 522248 | tf_op jit(solution)/shard_map/ppermute | solution.py:301
  33.2 1.4 %late_rows_begun.3.refs_4_ = f32[128,1152]{1,0:T(8,128)S(1)} custom-call(f32[1]{0:T(128)S(6)} %copy.25.refs_0_, f32[1]{0:T(128)S(6)} %copy.26.refs_1_, bf16[136,1152]{1,0:T(8,128)(2,1)S(1)} %collective-permute-done.6.refs_6_.refs_5_.refs_2_.refs_8_.refs_13_, bf16[128,1152]{1,0:T(8,128)(2,1)S(1)} %copy-done, ...), custom_call_target="tpu_custom_call" | custom-call | flops 896 | bytes 896 | tf_op jit(solution)/shard_map/late_rows_begun/pallas_call | solution.py:93
  34.6 0.6 %late_rows.3 = (s16[136,640]{1,0:T(8,128)(2,1)S(1)}, s16[136,512]{1,0:T(8,128)(2,1)S(1)}) custom-call(f32[1]{0:T(128)S(6)} %copy.25.refs_0_, f32[1]{0:T(128)S(6)} %copy.26.refs_1_, bf16[136,1152]{1,0:T(8,128)(2,1)S(1)} %collective-permute-done.6.refs_6_.refs_5_.refs_2_.refs_8_.refs_13_, ...), custom_call_target="tpu_custom_call" | custom-call | flops 128 | bytes 128 | tf_op jit(solution)/shard_map/late_rows/pallas_call | solution.py:93
  35.2 1.8 %collective-permute-start.11 = (s16[136,640]{1,0:T(8,128)(2,1)S(1)}, s16[136,640]{1,0:T(8,128)(2,1)S(1)}, u32[]{:S(2)}, u32[]{:S(2)}) collective-permute-start(s16[136,640]{1,0:T(8,128)(2,1)S(1)} %get-tuple-element.56.refs_15_), channel_id=1, source_target_pairs={{0,8},{8,0},{16,24},{24,16},{1,9},{9,1},{17,25},{25,17},{2,10},{10... | collective-permute-start | bytes 522248 | tf_op jit(solution)/shard_map/ppermute | solution.py:301
  37.0 1.3 %late_columns.2 = (f32[128,1152]{1,0:T(8,128)S(1)}, f32[128,1152]{1,0:T(8,128)S(1)}, s16[136,1152]{1,0:T(8,128)(2,1)S(1)}) custom-call(f32[1]{0:T(128)S(6)} %copy.25.refs_0_, f32[1]{0:T(128)S(6)} %copy.26.refs_1_, bf16[128,1152]{1,0:T(8,128)(2,1)S(1)} %held.3.refs_2_.refs_0_.refs_4_, bf16[136,1152]{1,0:T(8,128)(2,1)S(1)} %labelled.2.refs_1_.refs_3_.refs_4_, ...), custom_call_target="tpu_custom_call" | custom-call | flops 768 | bytes 768 | tf_op jit(solution)/shard_map/late_columns/pallas_call | solution.py:93
  38.3 0.0 collective-permute-done.10.refs_1_
  38.4 0.1 passed_sum.4
  38.5 1.4 %collective-permute-start.13 = (s16[136,640]{1,0:T(8,128)(2,1)S(1)}, s16[136,640]{1,0:T(8,128)(2,1)S(1)}, u32[]{:S(2)}, u32[]{:S(2)}) collective-permute-start(s16[136,640]{1,0:T(8,128)(2,1)S(1)} %get-tuple-element.60.refs_15_), channel_id=1, source_target_pairs={{0,4},{1,5},{2,6},{3,7},{4,0},{5,1},{6,2},{7,3},{8,12},{9,13},{10,... | collective-permute-start | bytes 522248 | tf_op jit(solution)/shard_map/ppermute | solution.py:301
  39.9 1.5 %collective-permute-start.14 = (s16[136,512]{1,0:T(8,128)(2,1)S(1)}, s16[136,512]{1,0:T(8,128)(2,1)S(1)}, u32[]{:S(2)}, u32[]{:S(2)}) collective-permute-start(s16[136,512]{1,0:T(8,128)(2,1)S(1)} %get-tuple-element.65), channel_id=1, source_target_pairs={{0,16},{8,24},{16,0},{24,8},{1,17},{9,25},{17,1},{25,9},{2,18},{10... | collective-permute-start | bytes 417800 | tf_op jit(solution)/shard_map/ppermute | solution.py:301
  41.3 1.3 %late_columns.3 = (f32[128,1152]{1,0:T(8,128)S(1)}, f32[128,1152]{1,0:T(8,128)S(1)}, s16[136,1152]{1,0:T(8,128)(2,1)S(1)}) custom-call(f32[1]{0:T(128)S(6)} %copy.25.refs_0_, f32[1]{0:T(128)S(6)} %copy.26.refs_1_, bf16[128,1152]{1,0:T(8,128)(2,1)S(1)} %held.3.refs_2_.refs_0_.refs_4_, bf16[136,1152]{1,0:T(8,128)(2,1)S(1)} %labelled.2.refs_1_.refs_3_.refs_4_, ...), custom_call_target="tpu_custom_call" | custom-call | flops 768 | bytes 768 | tf_op jit(solution)/shard_map/late_columns/pallas_call | solution.py:93
  42.7 0.0 collective-permute-done.11.refs_1_
  42.7 0.1 passed_sum.5
  42.8 2.4 %collective-permute-start.16 = (s16[136,640]{1,0:T(8,128)(2,1)S(1)}, s16[136,640]{1,0:T(8,128)(2,1)S(1)}, u32[]{:S(2)}, u32[]{:S(2)}) collective-permute-start(s16[136,640]{1,0:T(8,128)(2,1)S(1)} %get-tuple-element.68), channel_id=1, source_target_pairs={{0,2},{1,3},{2,0},{3,1},{4,6},{5,7},{6,4},{7,5},{8,10},{9,11},{10,... | collective-permute-start | bytes 522248 | tf_op jit(solution)/shard_map/ppermute | solution.py:301
  45.2 1.6 %collective-permute-start.17 = (s16[136,512]{1,0:T(8,128)(2,1)S(1)}, s16[136,512]{1,0:T(8,128)(2,1)S(1)}, u32[]{:S(2)}, u32[]{:S(2)}) collective-permute-start(s16[136,512]{1,0:T(8,128)(2,1)S(1)} %get-tuple-element.69), channel_id=1, source_target_pairs={{0,8},{8,0},{16,24},{24,16},{1,9},{9,1},{17,25},{25,17},{2,10},{10... | collective-permute-start | bytes 417800 | tf_op jit(solution)/shard_map/ppermute | solution.py:301
  46.8 0.5 collective-permute-start.12
  47.3 0.0 collective-permute-done.14.refs_1_
  47.3 0.5 collective-permute-start.19
  47.8 1.4 %collective-permute-done.13.refs_2_.refs_0_ = s16[136,640]{1,0:T(8,128)(2,1)S(1)} collective-permute-done((s16[136,640]{1,0:T(8,128)(2,1)S(1)}, s16[136,640]{1,0:T(8,128)(2,1)S(1)}, u32[]{:S(2)}, u32[]{:S(2)}) %collective-permute-start.13) | collective-permute-done | bytes 174112 | tf_op jit(solution)/shard_map/ppermute | solution.py:301
  49.2 0.1 passed_sum.6.refs_3_
  49.3 0.1 collective-permute-start.15
  49.3 2.5 %collective-permute-done.17.refs_1_ = s16[136,512]{1,0:T(8,128)(2,1)S(1)} collective-permute-done((s16[136,512]{1,0:T(8,128)(2,1)S(1)}, s16[136,512]{1,0:T(8,128)(2,1)S(1)}, u32[]{:S(2)}, u32[]{:S(2)}) %collective-permute-start.17) | collective-permute-done | bytes 139296 | tf_op jit(solution)/shard_map/ppermute | solution.py:301
  51.8 0.0 collective-permute-done.16.refs_2_
  51.8 0.1 passed_sum.7
  51.9 0.3 collective-permute-start.18
  52.3 5.6 %collective-permute-done.15.refs_1_ = s16[136,512]{1,0:T(8,128)(2,1)S(1)} collective-permute-done((s16[136,512]{1,0:T(8,128)(2,1)S(1)}, s16[136,512]{1,0:T(8,128)(2,1)S(1)}, u32[]{:S(2)}, u32[]{:S(2)}) %collective-permute-start.15) | collective-permute-done | bytes 139296 | tf_op jit(solution)/shard_map/ppermute | solution.py:301
  57.9 1.1 %collective-permute-done.18.refs_3_ = s16[136,512]{1,0:T(8,128)(2,1)S(1)} collective-permute-done((s16[136,512]{1,0:T(8,128)(2,1)S(1)}, s16[136,512]{1,0:T(8,128)(2,1)S(1)}, u32[]{:S(2)}, u32[]{:S(2)}) %collective-permute-start.18) | collective-permute-done | bytes 139296 | tf_op jit(solution)/shard_map/ppermute | solution.py:301
  59.1 0.0 collective-permute-done.12.refs_2_
  59.1 0.0 collective-permute-done.19.refs_6_
  59.1 1.2 %output_sums.1 = (f32[128,1152]{1,0:T(8,128)}, f32[128,1152]{1,0:T(8,128)}) custom-call(f32[1]{0:T(128)S(6)} %copy.25.refs_0_, f32[128,1152]{1,0:T(8,128)S(1)} %get-tuple-element.61.refs_1_, s16[136,1152]{1,0:T(8,128)(2,1)S(1)} %collective-permute-done.12.refs_2_, s16[136,640]{1,0:T(8,128)(2,1)S(1)} %get-tuple-element.70.refs_3_, ...), custom_call_target="tpu_custom_call" | custom-call | flops 128 | bytes 128 | tf_op jit(solution)/shard_map/output_sums/pallas_call | solution.py:93
  (6 shorter events, 0.1 us)
Async XLA Ops:
  0.6 17.8 %collective-permute-start = (bf16[128,1152]{1,0:T(8,128)(2,1)}, bf16[128,1152]{1,0:T(8,128)(2,1)S(1)}, u32[]{:S(2)}, u32[]{:S(2)}) collective-permute-start(bf16[128,1152]{1,0:T(8,128)(2,1)} %refs_6_.7), channel_id=1, source_target_pairs={{0,4},{1,5},{2,6},{3,7},{4,0},{5,1},{6,2},{7,3},{8,12},{9,13},{10,... | collective-permute-start | bytes 884744 | tf_op jit(solution)/shard_map/ppermute | solution.py:301
  4.7 13.9 %collective-permute-start.1 = (bf16[128,1152]{1,0:T(8,128)(2,1)}, bf16[128,1152]{1,0:T(8,128)(2,1)S(1)}, u32[]{:S(2)}, u32[]{:S(2)}) collective-permute-start(bf16[128,1152]{1,0:T(8,128)(2,1)} %refs_0_.10), channel_id=1, source_target_pairs={{0,2},{1,3},{2,0},{3,1},{4,6},{5,7},{6,4},{7,5},{8,10},{9,11},{10,... | collective-permute-start | bytes 884744 | tf_op jit(solution)/shard_map/ppermute | solution.py:301
  6.3 1.0 %copy-start.1 = (bf16[128,1152]{1,0:T(8,128)(2,1)S(1)}, bf16[128,1152]{1,0:T(8,128)(2,1)}, u32[]{:S(2)}) copy-start(bf16[128,1152]{1,0:T(8,128)(2,1)} %refs_0_.10) | copy-start | bytes 884740
  7.3 0.7 %copy-start.2 = (s32[128]{0:T(128)S(1)}, s32[128]{0:T(128)}, u32[]{:S(2)}) copy-start(s32[128]{0:T(128)} %param.7) | copy-start | bytes 1540
  8.0 10.8 %copy-start = (bf16[128,1152]{1,0:T(8,128)(2,1)S(1)}, bf16[128,1152]{1,0:T(8,128)(2,1)}, u32[]{:S(2)}) copy-start(bf16[128,1152]{1,0:T(8,128)(2,1)} %refs_6_.7) | copy-start | bytes 884740
  8.0 10.7 %collective-permute-start.4 = (bf16[136,1152]{1,0:T(8,128)(2,1)S(1)}, bf16[136,1152]{1,0:T(8,128)(2,1)S(1)}, u32[]{:S(2)}, u32[]{:S(2)}) collective-permute-start(bf16[136,1152]{1,0:T(8,128)(2,1)S(1)} %labelled.3.refs_2_.refs_7_.refs_3_), channel_id=1, source_target_pairs={{0,8},{8,0},{16,24},{24,16},{1,9},{9,1},{17,25},{25,17},{2,10},{10... | collective-permute-start | bytes 940040 | tf_op jit(solution)/shard_map/ppermute | solution.py:301
  9.6 9.2 %collective-permute-start.3 = (bf16[128,1152]{1,0:T(8,128)(2,1)}, bf16[128,1152]{1,0:T(8,128)(2,1)S(1)}, u32[]{:S(2)}, u32[]{:S(2)}) collective-permute-start(bf16[128,1152]{1,0:T(8,128)(2,1)} %refs_6_.7), channel_id=1, source_target_pairs={{0,16},{8,24},{16,0},{24,8},{1,17},{9,25},{17,1},{25,9},{2,18},{10... | collective-permute-start | bytes 884744 | tf_op jit(solution)/shard_map/ppermute | solution.py:301
  11.1 7.6 %collective-permute-start.2 = (s32[1,128]{1,0:T(1,128)S(1)}, s32[1,128]{1,0:T(1,128)S(1)}, u32[]{:S(2)}, u32[]{:S(2)}) collective-permute-start(s32[1,128]{1,0:T(1,128)S(1)} %bitcast.2), channel_id=1, source_target_pairs={{0,2},{1,3},{2,0},{3,1},{4,6},{5,7},{6,4},{7,5},{8,10},{9,11},{10,... | collective-permute-start | bytes 1544 | tf_op jit(solution)/shard_map/ppermute | solution.py:301
  18.9 4.6 %collective-permute-start.7 = (bf16[792,1152]{1,0:T(8,128)(2,1)S(1)}, bf16[792,1152]{1,0:T(8,128)(2,1)S(1)}, u32[]{:S(2)}, u32[]{:S(2)}) collective-permute-start(bf16[792,1152]{1,0:T(8,128)(2,1)S(1)} %bundled.3), channel_id=1, source_target_pairs={{0,1},{1,0},{2,3},{3,2},{4,5},{5,4},{6,7},{7,6},{8,9},{9,8},{10,11... | collective-permute-start | bytes 5474312 | tf_op jit(solution)/shard_map/ppermute | solution.py:301
  19.0 9.6 %collective-permute-start.5 = (bf16[136,1152]{1,0:T(8,128)(2,1)S(1)}, bf16[136,1152]{1,0:T(8,128)(2,1)S(1)}, u32[]{:S(2)}, u32[]{:S(2)}) collective-permute-start(bf16[136,1152]{1,0:T(8,128)(2,1)S(1)} %get-tuple-element.38), channel_id=1, source_target_pairs={{0,16},{1,9},{2,18},{3,11},{4,20},{5,13},{6,22},{7,15},{8,24},{9,1... | collective-permute-start | bytes 940040 | tf_op jit(solution)/shard_map/ppermute | solution.py:310
  20.7 8.2 %collective-permute-start.6 = (bf16[136,1152]{1,0:T(8,128)(2,1)S(1)}, bf16[136,1152]{1,0:T(8,128)(2,1)S(1)}, u32[]{:S(2)}, u32[]{:S(2)}) collective-permute-start(bf16[136,1152]{1,0:T(8,128)(2,1)S(1)} %get-tuple-element.39), channel_id=1, source_target_pairs={{0,8},{1,17},{2,10},{3,19},{4,12},{5,21},{6,14},{7,23},{8,0},{9,25... | collective-permute-start | bytes 940040 | tf_op jit(solution)/shard_map/ppermute | solution.py:310
  28.9 1.9 %collective-permute-start.9 = (bf16[136,1152]{1,0:T(8,128)(2,1)S(1)}, bf16[136,1152]{1,0:T(8,128)(2,1)S(1)}, u32[]{:S(2)}, u32[]{:S(2)}) collective-permute-start(bf16[136,1152]{1,0:T(8,128)(2,1)S(1)} %collective-permute-done.5.refs_2_.refs_6_.refs_5_.refs_13_.refs_8_), channel_id=1, source_target_pairs={{0,1},{1,0},{2,3},{3,2},{4,5},{5,4},{6,7},{7,6},{8,9},{9,8},{10,11... | collective-permute-start | bytes 940040 | tf_op jit(solution)/shard_map/ppermute | solution.py:301
  29.2 1.7 %collective-permute-start.8 = (bf16[136,1152]{1,0:T(8,128)(2,1)S(1)}, bf16[136,1152]{1,0:T(8,128)(2,1)S(1)}, u32[]{:S(2)}, u32[]{:S(2)}) collective-permute-start(bf16[136,1152]{1,0:T(8,128)(2,1)S(1)} %collective-permute-done.6.refs_6_.refs_5_.refs_2_.refs_8_.refs_13_), channel_id=1, source_target_pairs={{0,1},{1,0},{2,3},{3,2},{4,5},{5,4},{6,7},{7,6},{8,9},{9,8},{10,11... | collective-permute-start | bytes 940040 | tf_op jit(solution)/shard_map/ppermute | solution.py:301
  31.6 6.8 %collective-permute-start.10 = (s16[136,640]{1,0:T(8,128)(2,1)S(1)}, s16[136,640]{1,0:T(8,128)(2,1)S(1)}, u32[]{:S(2)}, u32[]{:S(2)}) collective-permute-start(s16[136,640]{1,0:T(8,128)(2,1)S(1)} %get-tuple-element.54.refs_8_), channel_id=1, source_target_pairs={{0,16},{8,24},{16,0},{24,8},{1,17},{9,25},{17,1},{25,9},{2,18},{10... | collective-permute-start | bytes 522248 | tf_op jit(solution)/shard_map/ppermute | solution.py:301
  35.2 7.5 %collective-permute-start.11 = (s16[136,640]{1,0:T(8,128)(2,1)S(1)}, s16[136,640]{1,0:T(8,128)(2,1)S(1)}, u32[]{:S(2)}, u32[]{:S(2)}) collective-permute-start(s16[136,640]{1,0:T(8,128)(2,1)S(1)} %get-tuple-element.56.refs_15_), channel_id=1, source_target_pairs={{0,8},{8,0},{16,24},{24,16},{1,9},{9,1},{17,25},{25,17},{2,10},{10... | collective-permute-start | bytes 522248 | tf_op jit(solution)/shard_map/ppermute | solution.py:301
  38.5 10.7 %collective-permute-start.13 = (s16[136,640]{1,0:T(8,128)(2,1)S(1)}, s16[136,640]{1,0:T(8,128)(2,1)S(1)}, u32[]{:S(2)}, u32[]{:S(2)}) collective-permute-start(s16[136,640]{1,0:T(8,128)(2,1)S(1)} %get-tuple-element.60.refs_15_), channel_id=1, source_target_pairs={{0,4},{1,5},{2,6},{3,7},{4,0},{5,1},{6,2},{7,3},{8,12},{9,13},{10,... | collective-permute-start | bytes 522248 | tf_op jit(solution)/shard_map/ppermute | solution.py:301
  39.9 7.4 %collective-permute-start.14 = (s16[136,512]{1,0:T(8,128)(2,1)S(1)}, s16[136,512]{1,0:T(8,128)(2,1)S(1)}, u32[]{:S(2)}, u32[]{:S(2)}) collective-permute-start(s16[136,512]{1,0:T(8,128)(2,1)S(1)} %get-tuple-element.65), channel_id=1, source_target_pairs={{0,16},{8,24},{16,0},{24,8},{1,17},{9,25},{17,1},{25,9},{2,18},{10... | collective-permute-start | bytes 417800 | tf_op jit(solution)/shard_map/ppermute | solution.py:301
  42.8 9.0 %collective-permute-start.16 = (s16[136,640]{1,0:T(8,128)(2,1)S(1)}, s16[136,640]{1,0:T(8,128)(2,1)S(1)}, u32[]{:S(2)}, u32[]{:S(2)}) collective-permute-start(s16[136,640]{1,0:T(8,128)(2,1)S(1)} %get-tuple-element.68), channel_id=1, source_target_pairs={{0,2},{1,3},{2,0},{3,1},{4,6},{5,7},{6,4},{7,5},{8,10},{9,11},{10,... | collective-permute-start | bytes 522248 | tf_op jit(solution)/shard_map/ppermute | solution.py:301
  45.2 6.6 %collective-permute-start.17 = (s16[136,512]{1,0:T(8,128)(2,1)S(1)}, s16[136,512]{1,0:T(8,128)(2,1)S(1)}, u32[]{:S(2)}, u32[]{:S(2)}) collective-permute-start(s16[136,512]{1,0:T(8,128)(2,1)S(1)} %get-tuple-element.69), channel_id=1, source_target_pairs={{0,8},{8,0},{16,24},{24,16},{1,9},{9,1},{17,25},{25,17},{2,10},{10... | collective-permute-start | bytes 417800 | tf_op jit(solution)/shard_map/ppermute | solution.py:301
  46.8 12.3 %collective-permute-start.12 = (s16[136,1152]{1,0:T(8,128)(2,1)S(1)}, s16[136,1152]{1,0:T(8,128)(2,1)S(1)}, u32[]{:S(2)}, u32[]{:S(2)}) collective-permute-start(s16[136,1152]{1,0:T(8,128)(2,1)S(1)} %get-tuple-element.64), channel_id=1, source_target_pairs={{0,8},{8,0},{16,24},{24,16},{1,9},{9,1},{17,25},{25,17},{2,10},{10... | collective-permute-start | bytes 940040 | tf_op jit(solution)/shard_map/ppermute | solution.py:301
  47.3 11.8 %collective-permute-start.19 = (s16[136,1152]{1,0:T(8,128)(2,1)S(1)}, s16[136,1152]{1,0:T(8,128)(2,1)S(1)}, u32[]{:S(2)}, u32[]{:S(2)}) collective-permute-start(s16[136,1152]{1,0:T(8,128)(2,1)S(1)} %get-tuple-element.73), channel_id=1, source_target_pairs={{0,16},{8,24},{16,0},{24,8},{1,17},{9,25},{17,1},{25,9},{2,18},{10... | collective-permute-start | bytes 940040 | tf_op jit(solution)/shard_map/ppermute | solution.py:301
  49.3 8.7 %collective-permute-start.15 = (s16[136,512]{1,0:T(8,128)(2,1)S(1)}, s16[136,512]{1,0:T(8,128)(2,1)S(1)}, u32[]{:S(2)}, u32[]{:S(2)}) collective-permute-start(s16[136,512]{1,0:T(8,128)(2,1)S(1)} %passed_sum.6.refs_3_), channel_id=1, source_target_pairs={{0,4},{1,5},{2,6},{3,7},{4,0},{5,1},{6,2},{7,3},{8,12},{9,13},{10,... | collective-permute-start | bytes 417800 | tf_op jit(solution)/shard_map/ppermute | solution.py:301
  51.9 7.1 %collective-permute-start.18 = (s16[136,512]{1,0:T(8,128)(2,1)S(1)}, s16[136,512]{1,0:T(8,128)(2,1)S(1)}, u32[]{:S(2)}, u32[]{:S(2)}) collective-permute-start(s16[136,512]{1,0:T(8,128)(2,1)S(1)} %passed_sum.7), channel_id=1, source_target_pairs={{0,2},{1,3},{2,0},{3,1},{4,6},{5,7},{6,4},{7,5},{8,10},{9,11},{10,... | collective-permute-start | bytes 417800 | tf_op jit(solution)/shard_map/ppermute | solution.py:301

commit v22 on v14

--- a/solution.py
+++ b/solution.py
@@ -149,6 +149,11 @@
     return parts[0:1] * LABEL_BASE + parts[1:2]
 
 
+def reciprocal(value):
+    near = pl.reciprocal(value, approx=True)
+    return near * (2.0 - value * near)
+
+
 def gradient_sums(name, size, scalars, x_blocks, y_blocks, masks, x_images, jobs, before, emits, sequence, after=()):
     width = x_blocks[0][0][0].shape[1]
     x_masks, y_masks = masks
@@ -176,7 +181,7 @@
 
     def kernel(ins, refs):
         outs, weights = refs[:-1], refs[-1]
-        slope, shift = ins[slope_at][0] * LOG2E, ins[shift_at][0] * LOG2E
+        slope, shift = ins[slope_at][0] * -LOG2E, ins[shift_at][0] * -LOG2E
         x_refs, y_refs = [v(ins) for v in x_views], [v(ins) for v in y_views]
 
         def stacked(chosen):
@@ -204,7 +209,7 @@
                 )
                 for i in range(len(rows)):
                     z = scores[i * size : (i + 1) * size] * slope + shift
-                    sig = 1.0 / (1.0 + jnp.exp2(-z))
+                    sig = reciprocal(1.0 + jnp.exp2(jnp.minimum(z, 126.0)))
                     w = jnp.where(jnp.tile(keys[i], (1, len(chosen))) == other, sig - 1.0, sig)
                     there = pl.ds(n * size, len(chosen) * size)
                     weights[pl.ds(i * size, size), there] = w.astype(jnp.bfloat16)

time: 60.1 us -> 60.2 us (level)
  transfers between devices with their start and end apart: 20 -> 20, of which waited for: 8 -> 8; matrix products, arithmetic and copies ran while one was open for 0% -> 0% of each run, Pallas kernels for 18% -> 19%
where the time goes in v22:
time: 60.2 us; the launch traced here: 60 us
  starting transfers between devices  25.2 us (42%)
  waiting for transfers between devices  18.5 us (31%)
  Pallas kernels  12.5 us (21%)
  between operations  2.13 us (4%)
  local copies, waits for them, and re-layouts  1.66 us (3%)
    ppermute x20, starting transfers between devices, swapped(): lax.ppermute(array, axis, [(i, i ^ bit) for i in range(lax.axis_size(axis...  25.2 us
    ppermute x20, waiting for transfers between devices, swapped(): lax.ppermute(array, axis, [(i, i ^ bit) for i in range(lax.axis_size(axis...  18.5 us
    pallas_call x20, Pallas kernels, call(): pl.pallas_call(body, out_shape=[*out_shape, *(jax.ShapeDtypeStruct(a.shap...  12.5 us
    unnamed x6, local copies, waits for them, and re-layouts  1.66 us
  transfers between devices with their start and end apart: 20, of which 8 were waited for; matrix products, arithmetic and copies ran while one was open for 0% of the time, Pallas kernels for 19%

profile of v22, /device:TPU:0, one launch (start us, length us, event | category | flops | bytes accessed | tf_op | source)
XLA Modules:
  0.0 60.0 jit_solution(13126830714190845031)
XLA Ops:
  0.6 4.1 %collective-permute-start = (bf16[128,1152]{1,0:T(8,128)(2,1)}, bf16[128,1152]{1,0:T(8,128)(2,1)S(1)}, u32[]{:S(2)}, u32[]{:S(2)}) collective-permute-start(bf16[128,1152]{1,0:T(8,128)(2,1)} %refs_6_.7), channel_id=1, source_target_pairs={{0,4},{1,5},{2,6},{3,7},{4,0},{5,1},{6,2},{7,3},{8,12},{9,13},{10,... | collective-permute-start | bytes 884744 | tf_op jit(solution)/shard_map/ppermute | solution.py:279
  4.7 1.6 %collective-permute-start.1 = (bf16[128,1152]{1,0:T(8,128)(2,1)}, bf16[128,1152]{1,0:T(8,128)(2,1)S(1)}, u32[]{:S(2)}, u32[]{:S(2)}) collective-permute-start(bf16[128,1152]{1,0:T(8,128)(2,1)} %refs_0_.10), channel_id=1, source_target_pairs={{0,2},{1,3},{2,0},{3,1},{4,6},{5,7},{6,4},{7,5},{8,10},{9,11},{10,... | collective-permute-start | bytes 884744 | tf_op jit(solution)/shard_map/ppermute | solution.py:279
  6.3 0.0 copy-start.1
  6.3 1.0 %copy-done.1 = bf16[128,1152]{1,0:T(8,128)(2,1)S(1)} copy-done((bf16[128,1152]{1,0:T(8,128)(2,1)S(1)}, bf16[128,1152]{1,0:T(8,128)(2,1)}, u32[]{:S(2)}) %copy-start.1) | copy-done | bytes 294936
  7.3 0.0 copy-start.2
  7.3 0.7 %copy-done.2 = s32[128]{0:T(128)S(1)} copy-done((s32[128]{0:T(128)S(1)}, s32[128]{0:T(128)}, u32[]{:S(2)}) %copy-start.2) | copy-done | bytes 536
  8.0 0.0 copy-start
  8.0 1.6 %collective-permute-start.4 = (bf16[136,1152]{1,0:T(8,128)(2,1)S(1)}, bf16[136,1152]{1,0:T(8,128)(2,1)S(1)}, u32[]{:S(2)}, u32[]{:S(2)}) collective-permute-start(bf16[136,1152]{1,0:T(8,128)(2,1)S(1)} %labelled.3.refs_2_.refs_7_.refs_4_), channel_id=1, source_target_pairs={{0,8},{8,0},{16,24},{24,16},{1,9},{9,1},{17,25},{25,17},{2,10},{10... | collective-permute-start | bytes 940040 | tf_op jit(solution)/shard_map/ppermute | solution.py:279
  9.6 1.5 %collective-permute-start.3 = (bf16[128,1152]{1,0:T(8,128)(2,1)}, bf16[128,1152]{1,0:T(8,128)(2,1)S(1)}, u32[]{:S(2)}, u32[]{:S(2)}) collective-permute-start(bf16[128,1152]{1,0:T(8,128)(2,1)} %refs_6_.7), channel_id=1, source_target_pairs={{0,16},{8,24},{16,0},{24,8},{1,17},{9,25},{17,1},{25,9},{2,18},{10... | collective-permute-start | bytes 884744 | tf_op jit(solution)/shard_map/ppermute | solution.py:279
  11.1 0.4 collective-permute-start.2
  11.5 6.8 %collective-permute-done.refs_0_ = bf16[128,1152]{1,0:T(8,128)(2,1)S(1)} collective-permute-done((bf16[128,1152]{1,0:T(8,128)(2,1)}, bf16[128,1152]{1,0:T(8,128)(2,1)S(1)}, u32[]{:S(2)}, u32[]{:S(2)}) %collective-permute-start) | collective-permute-done | bytes 294944 | tf_op jit(solution)/shard_map/ppermute | solution.py:279
  18.4 0.3 collective-permute-done.2.refs_1_
  18.6 0.0 collective-permute-done.1.refs_0_
  18.7 0.0 collective-permute-done.3.refs_3_.refs_4_.refs_6_
  18.7 0.0 collective-permute-done.4.refs_4_.refs_5_.refs_6_
  18.7 0.0 copy-done
  18.8 0.1 bundled.3
  18.9 0.1 collective-permute-start.7
  19.0 1.6 %collective-permute-start.6 = (bf16[136,1152]{1,0:T(8,128)(2,1)S(1)}, bf16[136,1152]{1,0:T(8,128)(2,1)S(1)}, u32[]{:S(2)}, u32[]{:S(2)}) collective-permute-start(bf16[136,1152]{1,0:T(8,128)(2,1)S(1)} %labelled.2.refs_1_.refs_3_.refs_5_), channel_id=1, source_target_pairs={{0,8},{8,0},{16,24},{24,16},{1,9},{9,1},{17,25},{25,17},{2,10},{10... | collective-permute-start | bytes 940040 | tf_op jit(solution)/shard_map/ppermute | solution.py:279
  20.6 1.5 %collective-permute-start.5 = (bf16[128,1152]{1,0:T(8,128)(2,1)S(1)}, bf16[128,1152]{1,0:T(8,128)(2,1)S(1)}, u32[]{:S(2)}, u32[]{:S(2)}) collective-permute-start(bf16[128,1152]{1,0:T(8,128)(2,1)S(1)} %held.3.refs_2_.refs_0_.refs_5_), channel_id=1, source_target_pairs={{0,16},{8,24},{16,0},{24,8},{1,17},{9,25},{17,1},{25,9},{2,18},{10... | collective-permute-start | bytes 884744 | tf_op jit(solution)/shard_map/ppermute | solution.py:279
  23.4 0.0 collective-permute-done.7.refs_8_.refs_7_
  23.4 2.0 %early_sums.3 = (f32[128,1152]{1,0:T(8,128)S(1)}, f32[128,1152]{1,0:T(8,128)S(1)}, f32[128,1152]{1,0:T(8,128)S(1)}) custom-call(f32[1]{0:T(128)S(6)} %copy.25.refs_0_, f32[1]{0:T(128)S(6)} %copy.26.refs_1_, bf16[128,1152]{1,0:T(8,128)(2,1)S(1)} %held.3.refs_2_.refs_0_.refs_5_, bf16[136,1152]{1,0:T(8,128)(2,1)S(1)} %labelled.2.refs_1_.refs_3_.refs_5_, ...), custom_call_target="tpu_custom_call" | custom-call | flops 2304 | bytes 2304 | tf_op jit(solution)/shard_map/early_sums/pallas_call | solution.py:93
  25.4 2.0 %early_sums.2 = (f32[128,1152]{1,0:T(8,128)S(1)}, f32[128,1152]{1,0:T(8,128)S(1)}, f32[128,1152]{1,0:T(8,128)S(1)}) custom-call(f32[1]{0:T(128)S(6)} %copy.25.refs_0_, f32[1]{0:T(128)S(6)} %copy.26.refs_1_, bf16[128,1152]{1,0:T(8,128)(2,1)S(1)} %held.3.refs_2_.refs_0_.refs_5_, bf16[136,1152]{1,0:T(8,128)(2,1)S(1)} %labelled.2.refs_1_.refs_3_.refs_5_, ...), custom_call_target="tpu_custom_call" | custom-call | flops 2304 | bytes 2304 | tf_op jit(solution)/shard_map/early_sums/pallas_call | solution.py:93
  27.4 2.2 %collective-permute-done.5.refs_2_.refs_8_ = bf16[128,1152]{1,0:T(8,128)(2,1)S(1)} collective-permute-done((bf16[128,1152]{1,0:T(8,128)(2,1)S(1)}, bf16[128,1152]{1,0:T(8,128)(2,1)S(1)}, u32[]{:S(2)}, u32[]{:S(2)}) %collective-permute-start.5) | collective-permute-done | bytes 294944 | tf_op jit(solution)/shard_map/ppermute | solution.py:279
  29.7 0.0 collective-permute-done.6.refs_3_.refs_8_
  29.7 0.0 collective-permute-start.9
  29.7 0.5 collective-permute-start.8
  30.2 1.4 %late_rows_begun.2.refs_5_ = f32[128,1152]{1,0:T(8,128)S(1)} custom-call(f32[1]{0:T(128)S(6)} %copy.25.refs_0_, f32[1]{0:T(128)S(6)} %copy.26.refs_1_, bf16[128,1152]{1,0:T(8,128)(2,1)S(1)} %collective-permute-done.5.refs_2_.refs_8_, bf16[136,1152]{1,0:T(8,128)(2,1)S(1)} %collective-permute-done.6.refs_3_.refs_8_, ...), custom_call_target="tpu_custom_call" | custom-call | flops 896 | bytes 896 | tf_op jit(solution)/shard_map/late_rows_begun/pallas_call | solution.py:93
  31.5 0.0 collective-permute-done.9.refs_4_.refs_9_
  31.6 0.6 %late_rows.2 = (s16[136,640]{1,0:T(8,128)(2,1)S(1)}, s16[136,512]{1,0:T(8,128)(2,1)S(1)}) custom-call(f32[1]{0:T(128)S(6)} %copy.25.refs_0_, f32[1]{0:T(128)S(6)} %copy.26.refs_1_, bf16[128,1152]{1,0:T(8,128)(2,1)S(1)} %collective-permute-done.5.refs_2_.refs_8_, bf16[136,1152]{1,0:T(8,128)(2,1)S(1)} %collective-permute-done.6.refs_3_.refs_8_, ...), custom_call_target="tpu_custom_call" | custom-call | flops 128 | bytes 128 | tf_op jit(solution)/shard_map/late_rows/pallas_call | solution.py:93
  32.2 1.6 %collective-permute-start.12 = (s16[136,640]{1,0:T(8,128)(2,1)S(1)}, s16[136,640]{1,0:T(8,128)(2,1)S(1)}, u32[]{:S(2)}, u32[]{:S(2)}) collective-permute-start(s16[136,640]{1,0:T(8,128)(2,1)S(1)} %get-tuple-element.50.refs_8_), channel_id=1, source_target_pairs={{0,16},{8,24},{16,0},{24,8},{1,17},{9,25},{17,1},{25,9},{2,18},{10... | collective-permute-start | bytes 522248 | tf_op jit(solution)/shard_map/ppermute | solution.py:279
  33.7 1.3 %late_rows_begun.3.refs_5_ = f32[128,1152]{1,0:T(8,128)S(1)} custom-call(f32[1]{0:T(128)S(6)} %copy.25.refs_0_, f32[1]{0:T(128)S(6)} %copy.26.refs_1_, bf16[128,1152]{1,0:T(8,128)(2,1)S(1)} %collective-permute-done.5.refs_2_.refs_8_, bf16[136,1152]{1,0:T(8,128)(2,1)S(1)} %collective-permute-done.6.refs_3_.refs_8_, bf16[128,1152]{1,0:T(8,128)(2,1)S(1)} %copy-done, ...), custom_call_target="tpu_custom_call" | custom-call | flops 896 | bytes 896 | tf_op jit(solution)/shard_map/late_rows_begun/pallas_call | solution.py:93
  35.1 0.0 collective-permute-done.8.refs_4_.refs_9_
  35.1 0.6 %late_rows.3 = (s16[136,640]{1,0:T(8,128)(2,1)S(1)}, s16[136,512]{1,0:T(8,128)(2,1)S(1)}) custom-call(f32[1]{0:T(128)S(6)} %copy.25.refs_0_, f32[1]{0:T(128)S(6)} %copy.26.refs_1_, bf16[128,1152]{1,0:T(8,128)(2,1)S(1)} %collective-permute-done.5.refs_2_.refs_8_, bf16[136,1152]{1,0:T(8,128)(2,1)S(1)} %collective-permute-done.6.refs_3_.refs_8_, ...), custom_call_target="tpu_custom_call" | custom-call | flops 128 | bytes 128 | tf_op jit(solution)/shard_map/late_rows/pallas_call | solution.py:93
  35.7 0.7 %collective-permute-start.10 = (s16[136,640]{1,0:T(8,128)(2,1)S(1)}, s16[136,640]{1,0:T(8,128)(2,1)S(1)}, u32[]{:S(2)}, u32[]{:S(2)}) collective-permute-start(s16[136,640]{1,0:T(8,128)(2,1)S(1)} %get-tuple-element.52.refs_13_), channel_id=1, source_target_pairs={{0,8},{8,0},{16,24},{24,16},{1,9},{9,1},{17,25},{25,17},{2,10},{10... | collective-permute-start | bytes 522248 | tf_op jit(solution)/shard_map/ppermute | solution.py:279
  36.5 1.3 %late_columns.2 = (f32[128,1152]{1,0:T(8,128)S(1)}, f32[128,1152]{1,0:T(8,128)S(1)}, s16[136,1152]{1,0:T(8,128)(2,1)S(1)}) custom-call(f32[1]{0:T(128)S(6)} %copy.25.refs_0_, f32[1]{0:T(128)S(6)} %copy.26.refs_1_, bf16[128,1152]{1,0:T(8,128)(2,1)S(1)} %held.3.refs_2_.refs_0_.refs_5_, bf16[136,1152]{1,0:T(8,128)(2,1)S(1)} %labelled.2.refs_1_.refs_3_.refs_5_, ...), custom_call_target="tpu_custom_call" | custom-call | flops 768 | bytes 768 | tf_op jit(solution)/shard_map/late_columns/pallas_call | solution.py:93
  37.8 1.3 %late_columns.3 = (f32[128,1152]{1,0:T(8,128)S(1)}, f32[128,1152]{1,0:T(8,128)S(1)}, s16[136,1152]{1,0:T(8,128)(2,1)S(1)}) custom-call(f32[1]{0:T(128)S(6)} %copy.25.refs_0_, f32[1]{0:T(128)S(6)} %copy.26.refs_1_, bf16[128,1152]{1,0:T(8,128)(2,1)S(1)} %held.3.refs_2_.refs_0_.refs_5_, bf16[136,1152]{1,0:T(8,128)(2,1)S(1)} %labelled.2.refs_1_.refs_3_.refs_5_, ...), custom_call_target="tpu_custom_call" | custom-call | flops 768 | bytes 768 | tf_op jit(solution)/shard_map/late_columns/pallas_call | solution.py:93
  39.1 0.0 collective-permute-done.12.refs_1_
  39.2 0.1 passed_sum.5
  39.3 1.4 %collective-permute-start.13 = (s16[136,640]{1,0:T(8,128)(2,1)S(1)}, s16[136,640]{1,0:T(8,128)(2,1)S(1)}, u32[]{:S(2)}, u32[]{:S(2)}) collective-permute-start(s16[136,640]{1,0:T(8,128)(2,1)S(1)} %get-tuple-element.60), channel_id=1, source_target_pairs={{0,4},{1,5},{2,6},{3,7},{4,0},{5,1},{6,2},{7,3},{8,12},{9,13},{10,... | collective-permute-start | bytes 522248 | tf_op jit(solution)/shard_map/ppermute | solution.py:279
  40.7 0.9 %collective-permute-start.14 = (s16[136,512]{1,0:T(8,128)(2,1)S(1)}, s16[136,512]{1,0:T(8,128)(2,1)S(1)}, u32[]{:S(2)}, u32[]{:S(2)}) collective-permute-start(s16[136,512]{1,0:T(8,128)(2,1)S(1)} %get-tuple-element.61), channel_id=1, source_target_pairs={{0,16},{8,24},{16,0},{24,8},{1,17},{9,25},{17,1},{25,9},{2,18},{10... | collective-permute-start | bytes 417800 | tf_op jit(solution)/shard_map/ppermute | solution.py:279
  41.6 0.2 collective-permute-done.10.refs_1_
  41.8 0.1 passed_sum.4
  42.0 2.2 %collective-permute-start.16 = (s16[136,640]{1,0:T(8,128)(2,1)S(1)}, s16[136,640]{1,0:T(8,128)(2,1)S(1)}, u32[]{:S(2)}, u32[]{:S(2)}) collective-permute-start(s16[136,640]{1,0:T(8,128)(2,1)S(1)} %get-tuple-element.64), channel_id=1, source_target_pairs={{0,2},{1,3},{2,0},{3,1},{4,6},{5,7},{6,4},{7,5},{8,10},{9,11},{10,... | collective-permute-start | bytes 522248 | tf_op jit(solution)/shard_map/ppermute | solution.py:279
  44.2 1.0 %collective-permute-start.17 = (s16[136,512]{1,0:T(8,128)(2,1)S(1)}, s16[136,512]{1,0:T(8,128)(2,1)S(1)}, u32[]{:S(2)}, u32[]{:S(2)}) collective-permute-start(s16[136,512]{1,0:T(8,128)(2,1)S(1)} %get-tuple-element.65), channel_id=1, source_target_pairs={{0,8},{8,0},{16,24},{24,16},{1,9},{9,1},{17,25},{25,17},{2,10},{10... | collective-permute-start | bytes 417800 | tf_op jit(solution)/shard_map/ppermute | solution.py:279
  45.1 1.5 %collective-permute-start.19 = (s16[136,1152]{1,0:T(8,128)(2,1)S(1)}, s16[136,1152]{1,0:T(8,128)(2,1)S(1)}, u32[]{:S(2)}, u32[]{:S(2)}) collective-permute-start(s16[136,1152]{1,0:T(8,128)(2,1)S(1)} %get-tuple-element.69), channel_id=1, source_target_pairs={{0,16},{8,24},{16,0},{24,8},{1,17},{9,25},{17,1},{25,9},{2,18},{10... | collective-permute-start | bytes 940040 | tf_op jit(solution)/shard_map/ppermute | solution.py:279
  46.6 0.0 collective-permute-done.14.refs_1_
  46.6 0.7 %collective-permute-start.11 = (s16[136,1152]{1,0:T(8,128)(2,1)S(1)}, s16[136,1152]{1,0:T(8,128)(2,1)S(1)}, u32[]{:S(2)}, u32[]{:S(2)}) collective-permute-start(s16[136,1152]{1,0:T(8,128)(2,1)S(1)} %get-tuple-element.58), channel_id=1, source_target_pairs={{0,8},{8,0},{16,24},{24,16},{1,9},{9,1},{17,25},{25,17},{2,10},{10... | collective-permute-start | bytes 940040 | tf_op jit(solution)/shard_map/ppermute | solution.py:279
  47.3 2.5 %collective-permute-done.13.refs_2_.refs_0_ = s16[136,640]{1,0:T(8,128)(2,1)S(1)} collective-permute-done((s16[136,640]{1,0:T(8,128)(2,1)S(1)}, s16[136,640]{1,0:T(8,128)(2,1)S(1)}, u32[]{:S(2)}, u32[]{:S(2)}) %collective-permute-start.13) | collective-permute-done | bytes 174112 | tf_op jit(solution)/shard_map/ppermute | solution.py:279
  49.9 0.1 passed_sum.6.refs_3_
  50.0 0.1 collective-permute-start.15
  50.0 0.6 collective-permute-done.17.refs_1_
  50.6 0.0 collective-permute-done.16.refs_2_
  50.6 0.1 passed_sum.7
  50.7 2.3 %collective-permute-start.18 = (s16[136,512]{1,0:T(8,128)(2,1)S(1)}, s16[136,512]{1,0:T(8,128)(2,1)S(1)}, u32[]{:S(2)}, u32[]{:S(2)}) collective-permute-start(s16[136,512]{1,0:T(8,128)(2,1)S(1)} %passed_sum.7), channel_id=1, source_target_pairs={{0,2},{1,3},{2,0},{3,1},{4,6},{5,7},{6,4},{7,5},{8,10},{9,11},{10,... | collective-permute-start | bytes 417800 | tf_op jit(solution)/shard_map/ppermute | solution.py:279
  53.0 5.6 %collective-permute-done.15.refs_1_ = s16[136,512]{1,0:T(8,128)(2,1)S(1)} collective-permute-done((s16[136,512]{1,0:T(8,128)(2,1)S(1)}, s16[136,512]{1,0:T(8,128)(2,1)S(1)}, u32[]{:S(2)}, u32[]{:S(2)}) %collective-permute-start.15) | collective-permute-done | bytes 139296 | tf_op jit(solution)/shard_map/ppermute | solution.py:279
  58.6 0.2 collective-permute-done.18.refs_3_
  58.8 0.0 collective-permute-done.19.refs_6_
  58.8 0.0 collective-permute-done.11.refs_2_
  58.8 1.2 %output_sums.1 = (f32[128,1152]{1,0:T(8,128)}, f32[128,1152]{1,0:T(8,128)}) custom-call(f32[1]{0:T(128)S(6)} %copy.25.refs_0_, f32[128,1152]{1,0:T(8,128)S(1)} %get-tuple-element.55.refs_1_, s16[136,1152]{1,0:T(8,128)(2,1)S(1)} %collective-permute-done.11.refs_2_, s16[136,640]{1,0:T(8,128)(2,1)S(1)} %get-tuple-element.66.refs_3_, ...), custom_call_target="tpu_custom_call" | custom-call | flops 128 | bytes 128 | tf_op jit(solution)/shard_map/output_sums/pallas_call | solution.py:93
  (6 shorter events, 0.1 us)
Async XLA Ops:
  0.6 17.8 %collective-permute-start = (bf16[128,1152]{1,0:T(8,128)(2,1)}, bf16[128,1152]{1,0:T(8,128)(2,1)S(1)}, u32[]{:S(2)}, u32[]{:S(2)}) collective-permute-start(bf16[128,1152]{1,0:T(8,128)(2,1)} %refs_6_.7), channel_id=1, source_target_pairs={{0,4},{1,5},{2,6},{3,7},{4,0},{5,1},{6,2},{7,3},{8,12},{9,13},{10,... | collective-permute-start | bytes 884744 | tf_op jit(solution)/shard_map/ppermute | solution.py:279
  4.7 13.9 %collective-permute-start.1 = (bf16[128,1152]{1,0:T(8,128)(2,1)}, bf16[128,1152]{1,0:T(8,128)(2,1)S(1)}, u32[]{:S(2)}, u32[]{:S(2)}) collective-permute-start(bf16[128,1152]{1,0:T(8,128)(2,1)} %refs_0_.10), channel_id=1, source_target_pairs={{0,2},{1,3},{2,0},{3,1},{4,6},{5,7},{6,4},{7,5},{8,10},{9,11},{10,... | collective-permute-start | bytes 884744 | tf_op jit(solution)/shard_map/ppermute | solution.py:279
  6.3 1.0 %copy-start.1 = (bf16[128,1152]{1,0:T(8,128)(2,1)S(1)}, bf16[128,1152]{1,0:T(8,128)(2,1)}, u32[]{:S(2)}) copy-start(bf16[128,1152]{1,0:T(8,128)(2,1)} %refs_0_.10) | copy-start | bytes 884740
  7.3 0.7 %copy-start.2 = (s32[128]{0:T(128)S(1)}, s32[128]{0:T(128)}, u32[]{:S(2)}) copy-start(s32[128]{0:T(128)} %param.7) | copy-start | bytes 1540
  8.0 10.8 %copy-start = (bf16[128,1152]{1,0:T(8,128)(2,1)S(1)}, bf16[128,1152]{1,0:T(8,128)(2,1)}, u32[]{:S(2)}) copy-start(bf16[128,1152]{1,0:T(8,128)(2,1)} %refs_6_.7) | copy-start | bytes 884740
  8.0 10.7 %collective-permute-start.4 = (bf16[136,1152]{1,0:T(8,128)(2,1)S(1)}, bf16[136,1152]{1,0:T(8,128)(2,1)S(1)}, u32[]{:S(2)}, u32[]{:S(2)}) collective-permute-start(bf16[136,1152]{1,0:T(8,128)(2,1)S(1)} %labelled.3.refs_2_.refs_7_.refs_4_), channel_id=1, source_target_pairs={{0,8},{8,0},{16,24},{24,16},{1,9},{9,1},{17,25},{25,17},{2,10},{10... | collective-permute-start | bytes 940040 | tf_op jit(solution)/shard_map/ppermute | solution.py:279
  9.6 9.2 %collective-permute-start.3 = (bf16[128,1152]{1,0:T(8,128)(2,1)}, bf16[128,1152]{1,0:T(8,128)(2,1)S(1)}, u32[]{:S(2)}, u32[]{:S(2)}) collective-permute-start(bf16[128,1152]{1,0:T(8,128)(2,1)} %refs_6_.7), channel_id=1, source_target_pairs={{0,16},{8,24},{16,0},{24,8},{1,17},{9,25},{17,1},{25,9},{2,18},{10... | collective-permute-start | bytes 884744 | tf_op jit(solution)/shard_map/ppermute | solution.py:279
  11.1 7.6 %collective-permute-start.2 = (s32[1,128]{1,0:T(1,128)S(1)}, s32[1,128]{1,0:T(1,128)S(1)}, u32[]{:S(2)}, u32[]{:S(2)}) collective-permute-start(s32[1,128]{1,0:T(1,128)S(1)} %bitcast.2), channel_id=1, source_target_pairs={{0,2},{1,3},{2,0},{3,1},{4,6},{5,7},{6,4},{7,5},{8,10},{9,11},{10,... | collective-permute-start | bytes 1544 | tf_op jit(solution)/shard_map/ppermute | solution.py:279
  18.9 4.5 %collective-permute-start.7 = (bf16[792,1152]{1,0:T(8,128)(2,1)S(1)}, bf16[792,1152]{1,0:T(8,128)(2,1)S(1)}, u32[]{:S(2)}, u32[]{:S(2)}) collective-permute-start(bf16[792,1152]{1,0:T(8,128)(2,1)S(1)} %bundled.3), channel_id=1, source_target_pairs={{0,1},{1,0},{2,3},{3,2},{4,5},{5,4},{6,7},{7,6},{8,9},{9,8},{10,11... | collective-permute-start | bytes 5474312 | tf_op jit(solution)/shard_map/ppermute | solution.py:279
  19.0 10.7 %collective-permute-start.6 = (bf16[136,1152]{1,0:T(8,128)(2,1)S(1)}, bf16[136,1152]{1,0:T(8,128)(2,1)S(1)}, u32[]{:S(2)}, u32[]{:S(2)}) collective-permute-start(bf16[136,1152]{1,0:T(8,128)(2,1)S(1)} %labelled.2.refs_1_.refs_3_.refs_5_), channel_id=1, source_target_pairs={{0,8},{8,0},{16,24},{24,16},{1,9},{9,1},{17,25},{25,17},{2,10},{10... | collective-permute-start | bytes 940040 | tf_op jit(solution)/shard_map/ppermute | solution.py:279
  20.6 9.1 %collective-permute-start.5 = (bf16[128,1152]{1,0:T(8,128)(2,1)S(1)}, bf16[128,1152]{1,0:T(8,128)(2,1)S(1)}, u32[]{:S(2)}, u32[]{:S(2)}) collective-permute-start(bf16[128,1152]{1,0:T(8,128)(2,1)S(1)} %held.3.refs_2_.refs_0_.refs_5_), channel_id=1, source_target_pairs={{0,16},{8,24},{16,0},{24,8},{1,17},{9,25},{17,1},{25,9},{2,18},{10... | collective-permute-start | bytes 884744 | tf_op jit(solution)/shard_map/ppermute | solution.py:279
  29.7 1.9 %collective-permute-start.9 = (bf16[136,1152]{1,0:T(8,128)(2,1)S(1)}, bf16[136,1152]{1,0:T(8,128)(2,1)S(1)}, u32[]{:S(2)}, u32[]{:S(2)}) collective-permute-start(bf16[136,1152]{1,0:T(8,128)(2,1)S(1)} %collective-permute-done.6.refs_3_.refs_8_), channel_id=1, source_target_pairs={{0,1},{1,0},{2,3},{3,2},{4,5},{5,4},{6,7},{7,6},{8,9},{9,8},{10,11... | collective-permute-start | bytes 940040 | tf_op jit(solution)/shard_map/ppermute | solution.py:279
  29.7 5.4 %collective-permute-start.8 = (bf16[128,1152]{1,0:T(8,128)(2,1)S(1)}, bf16[128,1152]{1,0:T(8,128)(2,1)S(1)}, u32[]{:S(2)}, u32[]{:S(2)}) collective-permute-start(bf16[128,1152]{1,0:T(8,128)(2,1)S(1)} %collective-permute-done.5.refs_2_.refs_8_), channel_id=1, source_target_pairs={{0,1},{1,0},{2,3},{3,2},{4,5},{5,4},{6,7},{7,6},{8,9},{9,8},{10,11... | collective-permute-start | bytes 884744 | tf_op jit(solution)/shard_map/ppermute | solution.py:279
  32.2 7.0 %collective-permute-start.12 = (s16[136,640]{1,0:T(8,128)(2,1)S(1)}, s16[136,640]{1,0:T(8,128)(2,1)S(1)}, u32[]{:S(2)}, u32[]{:S(2)}) collective-permute-start(s16[136,640]{1,0:T(8,128)(2,1)S(1)} %get-tuple-element.50.refs_8_), channel_id=1, source_target_pairs={{0,16},{8,24},{16,0},{24,8},{1,17},{9,25},{17,1},{25,9},{2,18},{10... | collective-permute-start | bytes 522248 | tf_op jit(solution)/shard_map/ppermute | solution.py:279
  35.7 6.1 %collective-permute-start.10 = (s16[136,640]{1,0:T(8,128)(2,1)S(1)}, s16[136,640]{1,0:T(8,128)(2,1)S(1)}, u32[]{:S(2)}, u32[]{:S(2)}) collective-permute-start(s16[136,640]{1,0:T(8,128)(2,1)S(1)} %get-tuple-element.52.refs_13_), channel_id=1, source_target_pairs={{0,8},{8,0},{16,24},{24,16},{1,9},{9,1},{17,25},{25,17},{2,10},{10... | collective-permute-start | bytes 522248 | tf_op jit(solution)/shard_map/ppermute | solution.py:279
  39.3 10.6 %collective-permute-start.13 = (s16[136,640]{1,0:T(8,128)(2,1)S(1)}, s16[136,640]{1,0:T(8,128)(2,1)S(1)}, u32[]{:S(2)}, u32[]{:S(2)}) collective-permute-start(s16[136,640]{1,0:T(8,128)(2,1)S(1)} %get-tuple-element.60), channel_id=1, source_target_pairs={{0,4},{1,5},{2,6},{3,7},{4,0},{5,1},{6,2},{7,3},{8,12},{9,13},{10,... | collective-permute-start | bytes 522248 | tf_op jit(solution)/shard_map/ppermute | solution.py:279
  40.7 5.9 %collective-permute-start.14 = (s16[136,512]{1,0:T(8,128)(2,1)S(1)}, s16[136,512]{1,0:T(8,128)(2,1)S(1)}, u32[]{:S(2)}, u32[]{:S(2)}) collective-permute-start(s16[136,512]{1,0:T(8,128)(2,1)S(1)} %get-tuple-element.61), channel_id=1, source_target_pairs={{0,16},{8,24},{16,0},{24,8},{1,17},{9,25},{17,1},{25,9},{2,18},{10... | collective-permute-start | bytes 417800 | tf_op jit(solution)/shard_map/ppermute | solution.py:279
  42.0 8.7 %collective-permute-start.16 = (s16[136,640]{1,0:T(8,128)(2,1)S(1)}, s16[136,640]{1,0:T(8,128)(2,1)S(1)}, u32[]{:S(2)}, u32[]{:S(2)}) collective-permute-start(s16[136,640]{1,0:T(8,128)(2,1)S(1)} %get-tuple-element.64), channel_id=1, source_target_pairs={{0,2},{1,3},{2,0},{3,1},{4,6},{5,7},{6,4},{7,5},{8,10},{9,11},{10,... | collective-permute-start | bytes 522248 | tf_op jit(solution)/shard_map/ppermute | solution.py:279
  44.2 6.5 %collective-permute-start.17 = (s16[136,512]{1,0:T(8,128)(2,1)S(1)}, s16[136,512]{1,0:T(8,128)(2,1)S(1)}, u32[]{:S(2)}, u32[]{:S(2)}) collective-permute-start(s16[136,512]{1,0:T(8,128)(2,1)S(1)} %get-tuple-element.65), channel_id=1, source_target_pairs={{0,8},{8,0},{16,24},{24,16},{1,9},{9,1},{17,25},{25,17},{2,10},{10... | collective-permute-start | bytes 417800 | tf_op jit(solution)/shard_map/ppermute | solution.py:279
  45.1 13.7 %collective-permute-start.19 = (s16[136,1152]{1,0:T(8,128)(2,1)S(1)}, s16[136,1152]{1,0:T(8,128)(2,1)S(1)}, u32[]{:S(2)}, u32[]{:S(2)}) collective-permute-start(s16[136,1152]{1,0:T(8,128)(2,1)S(1)} %get-tuple-element.69), channel_id=1, source_target_pairs={{0,16},{8,24},{16,0},{24,8},{1,17},{9,25},{17,1},{25,9},{2,18},{10... | collective-permute-start | bytes 940040 | tf_op jit(solution)/shard_map/ppermute | solution.py:279
  46.6 12.2 %collective-permute-start.11 = (s16[136,1152]{1,0:T(8,128)(2,1)S(1)}, s16[136,1152]{1,0:T(8,128)(2,1)S(1)}, u32[]{:S(2)}, u32[]{:S(2)}) collective-permute-start(s16[136,1152]{1,0:T(8,128)(2,1)S(1)} %get-tuple-element.58), channel_id=1, source_target_pairs={{0,8},{8,0},{16,24},{24,16},{1,9},{9,1},{17,25},{25,17},{2,10},{10... | collective-permute-start | bytes 940040 | tf_op jit(solution)/shard_map/ppermute | solution.py:279
  50.0 8.6 %collective-permute-start.15 = (s16[136,512]{1,0:T(8,128)(2,1)S(1)}, s16[136,512]{1,0:T(8,128)(2,1)S(1)}, u32[]{:S(2)}, u32[]{:S(2)}) collective-permute-start(s16[136,512]{1,0:T(8,128)(2,1)S(1)} %passed_sum.6.refs_3_), channel_id=1, source_target_pairs={{0,4},{1,5},{2,6},{3,7},{4,0},{5,1},{6,2},{7,3},{8,12},{9,13},{10,... | collective-permute-start | bytes 417800 | tf_op jit(solution)/shard_map/ppermute | solution.py:279
  50.7 8.1 %collective-permute-start.18 = (s16[136,512]{1,0:T(8,128)(2,1)S(1)}, s16[136,512]{1,0:T(8,128)(2,1)S(1)}, u32[]{:S(2)}, u32[]{:S(2)}) collective-permute-start(s16[136,512]{1,0:T(8,128)(2,1)S(1)} %passed_sum.7), channel_id=1, source_target_pairs={{0,2},{1,3},{2,0},{3,1},{4,6},{5,7},{6,4},{7,5},{8,10},{9,11},{10,... | collective-permute-start | bytes 417800 | tf_op jit(solution)/shard_map/ppermute | solution.py:279

commit v23 on v14

--- a/solution.py
+++ b/solution.py
@@ -15,7 +15,7 @@
 TILE = 256
 LANES = 128
 BUNDLE_COST = 6 * 10**8
-HELD_COST = 85 * 10**7
+HELD_COST = 3 * 10**8
 SMEM = pl.BlockSpec(memory_space=pltpu.SMEM)
 VMEM = pl.BlockSpec(memory_space=pltpu.VMEM)
 ANY = pl.BlockSpec(memory_space=pl.ANY)
@@ -26,7 +26,7 @@
 
 
 def part_widths(width):
-    first = (width // LANES + 1) // 2 * LANES
+    first = width // (2 * LANES) * LANES
     return (first, width - first)
 
 
@@ -280,11 +280,13 @@
 
     half = len(kept)
     received = [[]] + [[(sent(c[0], steps[-1]),)] for c in coded[1:]]
-    waiting, last = [c[1] for c in coded[1:]], [coded[0][0]]
+    waiting, last = [c[1] for c in coded[1:]], []
     for s in reversed(range(len(steps) - 1)):
         for m in reversed(range(1 << s)):
             n = m | 1 << s
             first, *begun = passed_sum(kept[n], received[n], 0, waiting + last)
+            if waiting:
+                begun_with = [first]
             for r, c in zip(received[1:], begun):
                 r[0] = r[0] + (sent(c, steps[-1]),)
             received[0] += [(sent(c, steps[-1]),) for c in begun[len(waiting) :]]
@@ -292,7 +294,7 @@
             (second,) = passed_sum(kept[n], received[n], 1, (), [first[0], *after])
             received[m].append((first, sent(second, steps[s])))
             waiting, last, after = [], [], [second]
-    return kept[0], received[0], after
+    return received[0], after, begun_with
 
 
 def in_order(arrays, after=(), cost=HELD_COST):
@@ -390,13 +392,23 @@
         jobs, emits = every_pair(late, columns), ["parts"] * len(late)
         coded[k][1:] = sums("late_rows", k, late, columns, jobs, begun, emits)
         after = coded[k][1]
+    def last_columns(k, rows, emits, after):
+        columns = both_cores(late)
+        begun = {i: before[k][m] for i, m in enumerate(rows)}
+        return [r[0] for r in sums("late_columns", k, rows, columns, every_pair(rows, columns), begun, emits, after)]
+
+    middle = list(range(1, half))
     for k in (1, 0):
-        columns = both_cores(late)
-        jobs, emits = every_pair(early, columns), ["float"] * half + ["whole"]
-        *whole_sums, coded[k][0] = sums("late_columns", k, early, columns, jobs, before[k], emits, after)
-        kept[k], after = [s for (s,) in whole_sums], coded[k][0]
-    kept_texts, text_blocks, after = scattered(kept[1], coded[1], steps[1], ())
-    kept_images, image_blocks, _ = scattered(kept[0], coded[0], steps[0], after)
+        kept[k] = [None] + last_columns(k, middle, ["float"] * len(middle), after)
+        after = kept[k][-1:]
+    text_blocks, after, _ = scattered(kept[1], coded[1], steps[1], ())
+    image_blocks, _, after = scattered(kept[0], coded[0], steps[0], after)
+    ends_at = [image_blocks, text_blocks]
+    for k in (1, 0):
+        kept[k][0], code = last_columns(k, [0, half], ["float", "whole"], after)
+        ends_at[k].append(whole(swapped(code, steps[k][-1])))
+        after = [code]
+    kept_images, kept_texts = kept[0][0], kept[1][0]
     ends = ()
     for blocks_in in (text_blocks, image_blocks):
         ends = in_order([part[0] for b in blocks_in if len(b) > 1 for part in b], ends)

time: 60.1 us -> 59.3 us (0.987)
  waiting for transfers between devices: 18.9 us -> 16.7 us
  Pallas kernels: 12.2 us -> 12.9 us
    ppermute x20, waiting for transfers between devices: 18.9 us -> 16.7 us  [swapped(): lax.ppermute(array, axis, [(i, i ^ bit) for i in range(lax.axis_size(axis...]
    pallas_call x20 -> x22, Pallas kernels: 12.2 us -> 12.9 us  [call(): pl.pallas_call(body, out_shape=[*out_shape, *(jax.ShapeDtypeStruct(a.shap...]
    ppermute x20, starting transfers between devices: 25.1 us -> 25.7 us  [swapped(): lax.ppermute(array, axis, [(i, i ^ bit) for i in range(lax.axis_size(axis...]
  transfers between devices with their start and end apart: 20 -> 20, of which waited for: 8 -> 6; matrix products, arithmetic and copies ran while one was open for 0% -> 0% of each run, Pallas kernels for 18% -> 20%
where the time goes in v23:
time: 59.3 us; the launch traced here: 59.1 us
  starting transfers between devices  25.7 us (43%)
  waiting for transfers between devices  16.7 us (28%)
  Pallas kernels  12.9 us (22%)
  between operations  2.13 us (4%)
  local copies, waits for them, and re-layouts  1.66 us (3%)
    ppermute x20, starting transfers between devices, swapped(): lax.ppermute(array, axis, [(i, i ^ bit) for i in range(lax.axis_size(axis...  25.7 us
    ppermute x20, waiting for transfers between devices, swapped(): lax.ppermute(array, axis, [(i, i ^ bit) for i in range(lax.axis_size(axis...  16.7 us
    pallas_call x22, Pallas kernels, call(): pl.pallas_call(body, out_shape=[*out_shape, *(jax.ShapeDtypeStruct(a.shap...  12.9 us
    unnamed x6, local copies, waits for them, and re-layouts  1.66 us
  transfers between devices with their start and end apart: 20, of which 6 were waited for; matrix products, arithmetic and copies ran while one was open for 0% of the time, Pallas kernels for 20%

profile of v23, /device:TPU:0, one launch (start us, length us, event | category | flops | bytes accessed | tf_op | source)
XLA Modules:
  0.0 59.1 jit_solution(7937323267661593163)
XLA Ops:
  0.6 4.1 %collective-permute-start.2 = (bf16[128,1152]{1,0:T(8,128)(2,1)}, bf16[128,1152]{1,0:T(8,128)(2,1)S(1)}, u32[]{:S(2)}, u32[]{:S(2)}) collective-permute-start(bf16[128,1152]{1,0:T(8,128)(2,1)} %refs_4_.5), channel_id=1, source_target_pairs={{0,4},{1,5},{2,6},{3,7},{4,0},{5,1},{6,2},{7,3},{8,12},{9,13},{10,... | collective-permute-start | bytes 884744 | tf_op jit(solution)/shard_map/ppermute | solution.py:274
  4.7 1.6 %collective-permute-start.4 = (bf16[128,1152]{1,0:T(8,128)(2,1)}, bf16[128,1152]{1,0:T(8,128)(2,1)S(1)}, u32[]{:S(2)}, u32[]{:S(2)}) collective-permute-start(bf16[128,1152]{1,0:T(8,128)(2,1)} %refs_0_.12), channel_id=1, source_target_pairs={{0,2},{1,3},{2,0},{3,1},{4,6},{5,7},{6,4},{7,5},{8,10},{9,11},{10,... | collective-permute-start | bytes 884744 | tf_op jit(solution)/shard_map/ppermute | solution.py:274
  6.3 0.0 copy-start.1
  6.3 1.0 %copy-done.1 = bf16[128,1152]{1,0:T(8,128)(2,1)S(1)} copy-done((bf16[128,1152]{1,0:T(8,128)(2,1)S(1)}, bf16[128,1152]{1,0:T(8,128)(2,1)}, u32[]{:S(2)}) %copy-start.1) | copy-done | bytes 294936
  7.3 0.0 copy-start.2
  7.3 0.7 %copy-done.2 = s32[128]{0:T(128)S(1)} copy-done((s32[128]{0:T(128)S(1)}, s32[128]{0:T(128)}, u32[]{:S(2)}) %copy-start.2) | copy-done | bytes 536
  8.0 0.0 copy-start
  8.0 1.6 %collective-permute-start.1 = (bf16[136,1152]{1,0:T(8,128)(2,1)S(1)}, bf16[136,1152]{1,0:T(8,128)(2,1)S(1)}, u32[]{:S(2)}, u32[]{:S(2)}) collective-permute-start(bf16[136,1152]{1,0:T(8,128)(2,1)S(1)} %labelled.2.refs_2_.refs_7_.refs_4_.refs_5_), channel_id=1, source_target_pairs={{0,8},{8,0},{16,24},{24,16},{1,9},{9,1},{17,25},{25,17},{2,10},{10... | collective-permute-start | bytes 940040 | tf_op jit(solution)/shard_map/ppermute | solution.py:274
  9.6 1.5 %collective-permute-start = (bf16[128,1152]{1,0:T(8,128)(2,1)}, bf16[128,1152]{1,0:T(8,128)(2,1)S(1)}, u32[]{:S(2)}, u32[]{:S(2)}) collective-permute-start(bf16[128,1152]{1,0:T(8,128)(2,1)} %refs_4_.5), channel_id=1, source_target_pairs={{0,16},{8,24},{16,0},{24,8},{1,17},{9,25},{17,1},{25,9},{2,18},{10... | collective-permute-start | bytes 884744 | tf_op jit(solution)/shard_map/ppermute | solution.py:274
  11.1 0.4 collective-permute-start.5
  11.5 6.8 %collective-permute-done.2.refs_0_ = bf16[128,1152]{1,0:T(8,128)(2,1)S(1)} collective-permute-done((bf16[128,1152]{1,0:T(8,128)(2,1)}, bf16[128,1152]{1,0:T(8,128)(2,1)S(1)}, u32[]{:S(2)}, u32[]{:S(2)}) %collective-permute-start.2) | collective-permute-done | bytes 294944 | tf_op jit(solution)/shard_map/ppermute | solution.py:274
  18.4 0.3 collective-permute-done.5.refs_1_
  18.6 0.0 collective-permute-done.4.refs_0_
  18.7 0.0 collective-permute-done.refs_3_.refs_4_.refs_6_.refs_2_
  18.7 0.0 collective-permute-done.1.refs_4_.refs_5_.refs_6_.refs_3_
  18.7 0.0 copy-done
  18.8 0.1 bundled.3
  18.9 0.1 collective-permute-start.7
  19.0 1.6 %collective-permute-start.6 = (bf16[136,1152]{1,0:T(8,128)(2,1)S(1)}, bf16[136,1152]{1,0:T(8,128)(2,1)S(1)}, u32[]{:S(2)}, u32[]{:S(2)}) collective-permute-start(bf16[136,1152]{1,0:T(8,128)(2,1)S(1)} %labelled.3.refs_1_.refs_3_.refs_5_), channel_id=1, source_target_pairs={{0,8},{8,0},{16,24},{24,16},{1,9},{9,1},{17,25},{25,17},{2,10},{10... | collective-permute-start | bytes 940040 | tf_op jit(solution)/shard_map/ppermute | solution.py:274
  20.6 1.5 %collective-permute-start.3 = (bf16[128,1152]{1,0:T(8,128)(2,1)S(1)}, bf16[128,1152]{1,0:T(8,128)(2,1)S(1)}, u32[]{:S(2)}, u32[]{:S(2)}) collective-permute-start(bf16[128,1152]{1,0:T(8,128)(2,1)S(1)} %held.3.refs_2_.refs_0_.refs_5_), channel_id=1, source_target_pairs={{0,16},{8,24},{16,0},{24,8},{1,17},{9,25},{17,1},{25,9},{2,18},{10... | collective-permute-start | bytes 884744 | tf_op jit(solution)/shard_map/ppermute | solution.py:274
  23.4 0.0 collective-permute-done.7.refs_8_.refs_7_
  23.4 1.9 %early_sums.3 = (f32[128,1152]{1,0:T(8,128)S(1)}, f32[128,1152]{1,0:T(8,128)S(1)}, f32[128,1152]{1,0:T(8,128)S(1)}) custom-call(f32[1]{0:T(128)S(6)} %copy.21.refs_0_, f32[1]{0:T(128)S(6)} %copy.22.refs_1_, bf16[128,1152]{1,0:T(8,128)(2,1)S(1)} %held.3.refs_2_.refs_0_.refs_5_, bf16[136,1152]{1,0:T(8,128)(2,1)S(1)} %labelled.3.refs_1_.refs_3_.refs_5_, ...), custom_call_target="tpu_custom_call" | custom-call | flops 2304 | bytes 2304 | tf_op jit(solution)/shard_map/early_sums/pallas_call | solution.py:93
  25.3 1.9 %early_sums.2 = (f32[128,1152]{1,0:T(8,128)S(1)}, f32[128,1152]{1,0:T(8,128)S(1)}, f32[128,1152]{1,0:T(8,128)S(1)}) custom-call(f32[1]{0:T(128)S(6)} %copy.21.refs_0_, f32[1]{0:T(128)S(6)} %copy.22.refs_1_, bf16[128,1152]{1,0:T(8,128)(2,1)S(1)} %held.3.refs_2_.refs_0_.refs_5_, bf16[136,1152]{1,0:T(8,128)(2,1)S(1)} %labelled.3.refs_1_.refs_3_.refs_5_, ...), custom_call_target="tpu_custom_call" | custom-call | flops 2304 | bytes 2304 | tf_op jit(solution)/shard_map/early_sums/pallas_call | solution.py:93
  27.3 2.4 %collective-permute-done.3.refs_2_.refs_4_.refs_6_ = bf16[128,1152]{1,0:T(8,128)(2,1)S(1)} collective-permute-done((bf16[128,1152]{1,0:T(8,128)(2,1)S(1)}, bf16[128,1152]{1,0:T(8,128)(2,1)S(1)}, u32[]{:S(2)}, u32[]{:S(2)}) %collective-permute-start.3) | collective-permute-done | bytes 294944 | tf_op jit(solution)/shard_map/ppermute | solution.py:274
  29.7 0.0 collective-permute-done.6.refs_3_.refs_4_.refs_6_
  29.7 0.0 collective-permute-start.9
  29.7 0.5 collective-permute-start.8
  30.2 1.3 %late_rows_begun.2.refs_5_ = f32[128,1152]{1,0:T(8,128)S(1)} custom-call(f32[1]{0:T(128)S(6)} %copy.21.refs_0_, f32[1]{0:T(128)S(6)} %copy.22.refs_1_, bf16[128,1152]{1,0:T(8,128)(2,1)S(1)} %collective-permute-done.3.refs_2_.refs_4_.refs_6_, bf16[136,1152]{1,0:T(8,128)(2,1)S(1)} %collective-permute-done.6.refs_3_.refs_4_.refs_6_, ...), custom_call_target="tpu_custom_call" | custom-call | flops 896 | bytes 896 | tf_op jit(solution)/shard_map/late_rows_begun/pallas_call | solution.py:93
  31.5 0.0 collective-permute-done.9.refs_4_.refs_5_.refs_7_
  31.5 0.6 %late_rows.2 = (s16[136,512]{1,0:T(8,128)(2,1)S(1)}, s16[136,640]{1,0:T(8,128)(2,1)S(1)}) custom-call(f32[1]{0:T(128)S(6)} %copy.21.refs_0_, f32[1]{0:T(128)S(6)} %copy.22.refs_1_, bf16[128,1152]{1,0:T(8,128)(2,1)S(1)} %collective-permute-done.3.refs_2_.refs_4_.refs_6_, bf16[136,1152]{1,0:T(8,128)(2,1)S(1)} %collective-permute-done.6.refs_3_.refs_4_.refs_6_, ...), custom_call_target="tpu_custom_call" | custom-call | flops 128 | bytes 128 | tf_op jit(solution)/shard_map/late_rows/pallas_call | solution.py:93
  32.1 1.6 %collective-permute-start.11 = (s16[136,512]{1,0:T(8,128)(2,1)S(1)}, s16[136,512]{1,0:T(8,128)(2,1)S(1)}, u32[]{:S(2)}, u32[]{:S(2)}) collective-permute-start(s16[136,512]{1,0:T(8,128)(2,1)S(1)} %get-tuple-element.46.refs_8_), channel_id=1, source_target_pairs={{0,16},{8,24},{16,0},{24,8},{1,17},{9,25},{17,1},{25,9},{2,18},{10... | collective-permute-start | bytes 417800 | tf_op jit(solution)/shard_map/ppermute | solution.py:274
  33.7 1.3 %late_rows_begun.3.refs_5_ = f32[128,1152]{1,0:T(8,128)S(1)} custom-call(f32[1]{0:T(128)S(6)} %copy.21.refs_0_, f32[1]{0:T(128)S(6)} %copy.22.refs_1_, bf16[128,1152]{1,0:T(8,128)(2,1)S(1)} %collective-permute-done.3.refs_2_.refs_4_.refs_6_, bf16[136,1152]{1,0:T(8,128)(2,1)S(1)} %collective-permute-done.6.refs_3_.refs_4_.refs_6_, ...), custom_call_target="tpu_custom_call" | custom-call | flops 896 | bytes 896 | tf_op jit(solution)/shard_map/late_rows_begun/pallas_call | solution.py:93
  35.0 0.0 collective-permute-done.8.refs_4_.refs_5_.refs_7_
  35.1 0.6 %late_rows.3 = (s16[136,512]{1,0:T(8,128)(2,1)S(1)}, s16[136,640]{1,0:T(8,128)(2,1)S(1)}) custom-call(f32[1]{0:T(128)S(6)} %copy.21.refs_0_, f32[1]{0:T(128)S(6)} %copy.22.refs_1_, bf16[128,1152]{1,0:T(8,128)(2,1)S(1)} %collective-permute-done.3.refs_2_.refs_4_.refs_6_, bf16[136,1152]{1,0:T(8,128)(2,1)S(1)} %collective-permute-done.6.refs_3_.refs_4_.refs_6_, ...), custom_call_target="tpu_custom_call" | custom-call | flops 128 | bytes 128 | tf_op jit(solution)/shard_map/late_rows/pallas_call | solution.py:93
  35.7 0.7 %collective-permute-start.10 = (s16[136,512]{1,0:T(8,128)(2,1)S(1)}, s16[136,512]{1,0:T(8,128)(2,1)S(1)}, u32[]{:S(2)}, u32[]{:S(2)}) collective-permute-start(s16[136,512]{1,0:T(8,128)(2,1)S(1)} %get-tuple-element.48.refs_7_), channel_id=1, source_target_pairs={{0,8},{8,0},{16,24},{24,16},{1,9},{9,1},{17,25},{25,17},{2,10},{10... | collective-permute-start | bytes 417800 | tf_op jit(solution)/shard_map/ppermute | solution.py:274
  36.4 0.7 %late_columns.4.refs_7_.refs_0_ = f32[128,1152]{1,0:T(8,128)S(1)} custom-call(f32[1]{0:T(128)S(6)} %copy.21.refs_0_, f32[1]{0:T(128)S(6)} %copy.22.refs_1_, bf16[128,1152]{1,0:T(8,128)(2,1)S(1)} %held.3.refs_2_.refs_0_.refs_5_, bf16[136,1152]{1,0:T(8,128)(2,1)S(1)} %labelled.3.refs_1_.refs_3_.refs_5_, ...), custom_call_target="tpu_custom_call" | custom-call | flops 256 | bytes 256 | tf_op jit(solution)/shard_map/late_columns/pallas_call | solution.py:93
  37.1 0.7 %collective-permute-done.11.refs_1_ = s16[136,512]{1,0:T(8,128)(2,1)S(1)} collective-permute-done((s16[136,512]{1,0:T(8,128)(2,1)S(1)}, s16[136,512]{1,0:T(8,128)(2,1)S(1)}, u32[]{:S(2)}, u32[]{:S(2)}) %collective-permute-start.11) | collective-permute-done | bytes 139296 | tf_op jit(solution)/shard_map/ppermute | solution.py:274
  37.8 0.1 passed_sum.5
  37.9 1.4 %collective-permute-start.12 = (s16[136,512]{1,0:T(8,128)(2,1)S(1)}, s16[136,512]{1,0:T(8,128)(2,1)S(1)}, u32[]{:S(2)}, u32[]{:S(2)}) collective-permute-start(s16[136,512]{1,0:T(8,128)(2,1)S(1)} %get-tuple-element.53), channel_id=1, source_target_pairs={{0,4},{1,5},{2,6},{3,7},{4,0},{5,1},{6,2},{7,3},{8,12},{9,13},{10,... | collective-permute-start | bytes 417800 | tf_op jit(solution)/shard_map/ppermute | solution.py:274
  39.3 1.5 %collective-permute-start.13 = (s16[136,640]{1,0:T(8,128)(2,1)S(1)}, s16[136,640]{1,0:T(8,128)(2,1)S(1)}, u32[]{:S(2)}, u32[]{:S(2)}) collective-permute-start(s16[136,640]{1,0:T(8,128)(2,1)S(1)} %get-tuple-element.54), channel_id=1, source_target_pairs={{0,16},{8,24},{16,0},{24,8},{1,17},{9,25},{17,1},{25,9},{2,18},{10... | collective-permute-start | bytes 522248 | tf_op jit(solution)/shard_map/ppermute | solution.py:274
  40.8 0.7 %late_columns.5.refs_0_ = f32[128,1152]{1,0:T(8,128)S(1)} custom-call(f32[1]{0:T(128)S(6)} %copy.21.refs_0_, f32[1]{0:T(128)S(6)} %copy.22.refs_1_, bf16[128,1152]{1,0:T(8,128)(2,1)S(1)} %held.3.refs_2_.refs_0_.refs_5_, bf16[136,1152]{1,0:T(8,128)(2,1)S(1)} %labelled.3.refs_1_.refs_3_.refs_5_, ...), custom_call_target="tpu_custom_call" | custom-call | flops 256 | bytes 256 | tf_op jit(solution)/shard_map/late_columns/pallas_call | solution.py:93
  41.5 0.0 collective-permute-done.10.refs_1_
  41.5 0.1 passed_sum.4
  41.6 0.7 %collective-permute-start.16 = (s16[136,640]{1,0:T(8,128)(2,1)S(1)}, s16[136,640]{1,0:T(8,128)(2,1)S(1)}, u32[]{:S(2)}, u32[]{:S(2)}) collective-permute-start(s16[136,640]{1,0:T(8,128)(2,1)S(1)} %get-tuple-element.57), channel_id=1, source_target_pairs={{0,8},{8,0},{16,24},{24,16},{1,9},{9,1},{17,25},{25,17},{2,10},{10... | collective-permute-start | bytes 522248 | tf_op jit(solution)/shard_map/ppermute | solution.py:274
  42.3 2.4 %collective-permute-start.15 = (s16[136,512]{1,0:T(8,128)(2,1)S(1)}, s16[136,512]{1,0:T(8,128)(2,1)S(1)}, u32[]{:S(2)}, u32[]{:S(2)}) collective-permute-start(s16[136,512]{1,0:T(8,128)(2,1)S(1)} %get-tuple-element.50.refs_10_), channel_id=1, source_target_pairs={{0,2},{1,3},{2,0},{3,1},{4,6},{5,7},{6,4},{7,5},{8,10},{9,11},{10,... | collective-permute-start | bytes 417800 | tf_op jit(solution)/shard_map/ppermute | solution.py:274
  44.7 1.0 %late_columns.6 = (f32[128,1152]{1,0:T(8,128)S(1)}, s16[136,1152]{1,0:T(8,128)(2,1)S(1)}) custom-call(f32[1]{0:T(128)S(6)} %copy.21.refs_0_, f32[1]{0:T(128)S(6)} %copy.22.refs_1_, bf16[128,1152]{1,0:T(8,128)(2,1)S(1)} %collective-permute-done.refs_3_.refs_4_.refs_6_.refs_2_, bf16[136,1152]{1,0:T(8,128)(2,1)S(1)} %collective-permute-done.1.refs_4_.refs_5_.refs_6_.refs_3_, ...), custom_call_target="tpu_custom_call" | custom-call | flops 512 | bytes 512 | tf_op jit(solution)/shard_map/late_columns/pallas_call | solution.py:93
  45.7 1.0 %late_columns.7 = (f32[128,1152]{1,0:T(8,128)S(1)}, s16[136,1152]{1,0:T(8,128)(2,1)S(1)}) custom-call(f32[1]{0:T(128)S(6)} %copy.21.refs_0_, f32[1]{0:T(128)S(6)} %copy.22.refs_1_, bf16[128,1152]{1,0:T(8,128)(2,1)S(1)} %collective-permute-done.refs_3_.refs_4_.refs_6_.refs_2_, bf16[136,1152]{1,0:T(8,128)(2,1)S(1)} %collective-permute-done.1.refs_4_.refs_5_.refs_6_.refs_3_, ...), custom_call_target="tpu_custom_call" | custom-call | flops 512 | bytes 512 | tf_op jit(solution)/shard_map/late_columns/pallas_call | solution.py:93
  46.7 1.4 %collective-permute-start.18 = (s16[136,1152]{1,0:T(8,128)(2,1)S(1)}, s16[136,1152]{1,0:T(8,128)(2,1)S(1)}, u32[]{:S(2)}, u32[]{:S(2)}) collective-permute-start(s16[136,1152]{1,0:T(8,128)(2,1)S(1)} %get-tuple-element.60), channel_id=1, source_target_pairs={{0,8},{8,0},{16,24},{24,16},{1,9},{9,1},{17,25},{25,17},{2,10},{10... | collective-permute-start | bytes 940040 | tf_op jit(solution)/shard_map/ppermute | solution.py:274
  48.1 0.0 collective-permute-done.12.refs_2_.refs_0_
  48.1 0.5 collective-permute-start.19
  48.6 0.0 collective-permute-done.13.refs_1_
  48.6 0.1 passed_sum.6.refs_3_
  48.7 0.9 %collective-permute-start.14 = (s16[136,640]{1,0:T(8,128)(2,1)S(1)}, s16[136,640]{1,0:T(8,128)(2,1)S(1)}, u32[]{:S(2)}, u32[]{:S(2)}) collective-permute-start(s16[136,640]{1,0:T(8,128)(2,1)S(1)} %passed_sum.6.refs_3_), channel_id=1, source_target_pairs={{0,4},{1,5},{2,6},{3,7},{4,0},{5,1},{6,2},{7,3},{8,12},{9,13},{10,... | collective-permute-start | bytes 522248 | tf_op jit(solution)/shard_map/ppermute | solution.py:274
  49.7 0.0 collective-permute-done.15.refs_2_
  49.7 0.0 collective-permute-done.16.refs_1_
  49.7 0.1 passed_sum.7
  49.8 1.6 %collective-permute-start.17 = (s16[136,640]{1,0:T(8,128)(2,1)S(1)}, s16[136,640]{1,0:T(8,128)(2,1)S(1)}, u32[]{:S(2)}, u32[]{:S(2)}) collective-permute-start(s16[136,640]{1,0:T(8,128)(2,1)S(1)} %passed_sum.7), channel_id=1, source_target_pairs={{0,2},{1,3},{2,0},{3,1},{4,6},{5,7},{6,4},{7,5},{8,10},{9,11},{10,... | collective-permute-start | bytes 522248 | tf_op jit(solution)/shard_map/ppermute | solution.py:274
  51.4 6.2 %collective-permute-done.14.refs_1_ = s16[136,640]{1,0:T(8,128)(2,1)S(1)} collective-permute-done((s16[136,640]{1,0:T(8,128)(2,1)S(1)}, s16[136,640]{1,0:T(8,128)(2,1)S(1)}, u32[]{:S(2)}, u32[]{:S(2)}) %collective-permute-start.14) | collective-permute-done | bytes 174112 | tf_op jit(solution)/shard_map/ppermute | solution.py:274
  57.6 0.3 collective-permute-done.17.refs_3_
  57.9 0.0 collective-permute-done.18.refs_4_
  57.9 0.0 collective-permute-done.19.refs_8_
  57.9 1.2 %output_sums.1 = (f32[128,1152]{1,0:T(8,128)}, f32[128,1152]{1,0:T(8,128)}) custom-call(f32[1]{0:T(128)S(6)} %copy.21.refs_0_, f32[128,1152]{1,0:T(8,128)S(1)} %get-tuple-element.52.refs_1_, s16[136,512]{1,0:T(8,128)(2,1)S(1)} %get-tuple-element.58.refs_2_, s16[136,640]{1,0:T(8,128)(2,1)S(1)} %get-tuple-element.59.refs_3_, ...), custom_call_target="tpu_custom_call" | custom-call | flops 128 | bytes 128 | tf_op jit(solution)/shard_map/output_sums/pallas_call | solution.py:93
  (6 shorter events, 0.1 us)
Async XLA Ops:
  0.6 17.8 %collective-permute-start.2 = (bf16[128,1152]{1,0:T(8,128)(2,1)}, bf16[128,1152]{1,0:T(8,128)(2,1)S(1)}, u32[]{:S(2)}, u32[]{:S(2)}) collective-permute-start(bf16[128,1152]{1,0:T(8,128)(2,1)} %refs_4_.5), channel_id=1, source_target_pairs={{0,4},{1,5},{2,6},{3,7},{4,0},{5,1},{6,2},{7,3},{8,12},{9,13},{10,... | collective-permute-start | bytes 884744 | tf_op jit(solution)/shard_map/ppermute | solution.py:274
  4.7 13.9 %collective-permute-start.4 = (bf16[128,1152]{1,0:T(8,128)(2,1)}, bf16[128,1152]{1,0:T(8,128)(2,1)S(1)}, u32[]{:S(2)}, u32[]{:S(2)}) collective-permute-start(bf16[128,1152]{1,0:T(8,128)(2,1)} %refs_0_.12), channel_id=1, source_target_pairs={{0,2},{1,3},{2,0},{3,1},{4,6},{5,7},{6,4},{7,5},{8,10},{9,11},{10,... | collective-permute-start | bytes 884744 | tf_op jit(solution)/shard_map/ppermute | solution.py:274
  6.3 1.0 %copy-start.1 = (bf16[128,1152]{1,0:T(8,128)(2,1)S(1)}, bf16[128,1152]{1,0:T(8,128)(2,1)}, u32[]{:S(2)}) copy-start(bf16[128,1152]{1,0:T(8,128)(2,1)} %refs_0_.12) | copy-start | bytes 884740
  7.3 0.7 %copy-start.2 = (s32[128]{0:T(128)S(1)}, s32[128]{0:T(128)}, u32[]{:S(2)}) copy-start(s32[128]{0:T(128)} %param.7) | copy-start | bytes 1540
  8.0 10.8 %copy-start = (bf16[128,1152]{1,0:T(8,128)(2,1)S(1)}, bf16[128,1152]{1,0:T(8,128)(2,1)}, u32[]{:S(2)}) copy-start(bf16[128,1152]{1,0:T(8,128)(2,1)} %refs_4_.5) | copy-start | bytes 884740
  8.0 10.7 %collective-permute-start.1 = (bf16[136,1152]{1,0:T(8,128)(2,1)S(1)}, bf16[136,1152]{1,0:T(8,128)(2,1)S(1)}, u32[]{:S(2)}, u32[]{:S(2)}) collective-permute-start(bf16[136,1152]{1,0:T(8,128)(2,1)S(1)} %labelled.2.refs_2_.refs_7_.refs_4_.refs_5_), channel_id=1, source_target_pairs={{0,8},{8,0},{16,24},{24,16},{1,9},{9,1},{17,25},{25,17},{2,10},{10... | collective-permute-start | bytes 940040 | tf_op jit(solution)/shard_map/ppermute | solution.py:274
  9.6 9.2 %collective-permute-start = (bf16[128,1152]{1,0:T(8,128)(2,1)}, bf16[128,1152]{1,0:T(8,128)(2,1)S(1)}, u32[]{:S(2)}, u32[]{:S(2)}) collective-permute-start(bf16[128,1152]{1,0:T(8,128)(2,1)} %refs_4_.5), channel_id=1, source_target_pairs={{0,16},{8,24},{16,0},{24,8},{1,17},{9,25},{17,1},{25,9},{2,18},{10... | collective-permute-start | bytes 884744 | tf_op jit(solution)/shard_map/ppermute | solution.py:274
  11.1 7.6 %collective-permute-start.5 = (s32[1,128]{1,0:T(1,128)}, s32[1,128]{1,0:T(1,128)S(1)}, u32[]{:S(2)}, u32[]{:S(2)}) collective-permute-start(s32[1,128]{1,0:T(1,128)} %bitcast.1), channel_id=1, source_target_pairs={{0,2},{1,3},{2,0},{3,1},{4,6},{5,7},{6,4},{7,5},{8,10},{9,11},{10,... | collective-permute-start | bytes 1544 | tf_op jit(solution)/shard_map/ppermute | solution.py:274
  18.9 4.5 %collective-permute-start.7 = (bf16[792,1152]{1,0:T(8,128)(2,1)S(1)}, bf16[792,1152]{1,0:T(8,128)(2,1)S(1)}, u32[]{:S(2)}, u32[]{:S(2)}) collective-permute-start(bf16[792,1152]{1,0:T(8,128)(2,1)S(1)} %bundled.3), channel_id=1, source_target_pairs={{0,1},{1,0},{2,3},{3,2},{4,5},{5,4},{6,7},{7,6},{8,9},{9,8},{10,11... | collective-permute-start | bytes 5474312 | tf_op jit(solution)/shard_map/ppermute | solution.py:274
  19.0 10.7 %collective-permute-start.6 = (bf16[136,1152]{1,0:T(8,128)(2,1)S(1)}, bf16[136,1152]{1,0:T(8,128)(2,1)S(1)}, u32[]{:S(2)}, u32[]{:S(2)}) collective-permute-start(bf16[136,1152]{1,0:T(8,128)(2,1)S(1)} %labelled.3.refs_1_.refs_3_.refs_5_), channel_id=1, source_target_pairs={{0,8},{8,0},{16,24},{24,16},{1,9},{9,1},{17,25},{25,17},{2,10},{10... | collective-permute-start | bytes 940040 | tf_op jit(solution)/shard_map/ppermute | solution.py:274
  20.6 9.1 %collective-permute-start.3 = (bf16[128,1152]{1,0:T(8,128)(2,1)S(1)}, bf16[128,1152]{1,0:T(8,128)(2,1)S(1)}, u32[]{:S(2)}, u32[]{:S(2)}) collective-permute-start(bf16[128,1152]{1,0:T(8,128)(2,1)S(1)} %held.3.refs_2_.refs_0_.refs_5_), channel_id=1, source_target_pairs={{0,16},{8,24},{16,0},{24,8},{1,17},{9,25},{17,1},{25,9},{2,18},{10... | collective-permute-start | bytes 884744 | tf_op jit(solution)/shard_map/ppermute | solution.py:274
  29.7 1.9 %collective-permute-start.9 = (bf16[136,1152]{1,0:T(8,128)(2,1)S(1)}, bf16[136,1152]{1,0:T(8,128)(2,1)S(1)}, u32[]{:S(2)}, u32[]{:S(2)}) collective-permute-start(bf16[136,1152]{1,0:T(8,128)(2,1)S(1)} %collective-permute-done.6.refs_3_.refs_4_.refs_6_), channel_id=1, source_target_pairs={{0,1},{1,0},{2,3},{3,2},{4,5},{5,4},{6,7},{7,6},{8,9},{9,8},{10,11... | collective-permute-start | bytes 940040 | tf_op jit(solution)/shard_map/ppermute | solution.py:274
  29.7 5.4 %collective-permute-start.8 = (bf16[128,1152]{1,0:T(8,128)(2,1)S(1)}, bf16[128,1152]{1,0:T(8,128)(2,1)S(1)}, u32[]{:S(2)}, u32[]{:S(2)}) collective-permute-start(bf16[128,1152]{1,0:T(8,128)(2,1)S(1)} %collective-permute-done.3.refs_2_.refs_4_.refs_6_), channel_id=1, source_target_pairs={{0,1},{1,0},{2,3},{3,2},{4,5},{5,4},{6,7},{7,6},{8,9},{9,8},{10,11... | collective-permute-start | bytes 884744 | tf_op jit(solution)/shard_map/ppermute | solution.py:274
  32.1 5.6 %collective-permute-start.11 = (s16[136,512]{1,0:T(8,128)(2,1)S(1)}, s16[136,512]{1,0:T(8,128)(2,1)S(1)}, u32[]{:S(2)}, u32[]{:S(2)}) collective-permute-start(s16[136,512]{1,0:T(8,128)(2,1)S(1)} %get-tuple-element.46.refs_8_), channel_id=1, source_target_pairs={{0,16},{8,24},{16,0},{24,8},{1,17},{9,25},{17,1},{25,9},{2,18},{10... | collective-permute-start | bytes 417800 | tf_op jit(solution)/shard_map/ppermute | solution.py:274
  35.7 5.8 %collective-permute-start.10 = (s16[136,512]{1,0:T(8,128)(2,1)S(1)}, s16[136,512]{1,0:T(8,128)(2,1)S(1)}, u32[]{:S(2)}, u32[]{:S(2)}) collective-permute-start(s16[136,512]{1,0:T(8,128)(2,1)S(1)} %get-tuple-element.48.refs_7_), channel_id=1, source_target_pairs={{0,8},{8,0},{16,24},{24,16},{1,9},{9,1},{17,25},{25,17},{2,10},{10... | collective-permute-start | bytes 417800 | tf_op jit(solution)/shard_map/ppermute | solution.py:274
  37.9 10.2 %collective-permute-start.12 = (s16[136,512]{1,0:T(8,128)(2,1)S(1)}, s16[136,512]{1,0:T(8,128)(2,1)S(1)}, u32[]{:S(2)}, u32[]{:S(2)}) collective-permute-start(s16[136,512]{1,0:T(8,128)(2,1)S(1)} %get-tuple-element.53), channel_id=1, source_target_pairs={{0,4},{1,5},{2,6},{3,7},{4,0},{5,1},{6,2},{7,3},{8,12},{9,13},{10,... | collective-permute-start | bytes 417800 | tf_op jit(solution)/shard_map/ppermute | solution.py:274
  39.3 9.3 %collective-permute-start.13 = (s16[136,640]{1,0:T(8,128)(2,1)S(1)}, s16[136,640]{1,0:T(8,128)(2,1)S(1)}, u32[]{:S(2)}, u32[]{:S(2)}) collective-permute-start(s16[136,640]{1,0:T(8,128)(2,1)S(1)} %get-tuple-element.54), channel_id=1, source_target_pairs={{0,16},{8,24},{16,0},{24,8},{1,17},{9,25},{17,1},{25,9},{2,18},{10... | collective-permute-start | bytes 522248 | tf_op jit(solution)/shard_map/ppermute | solution.py:274
  41.6 8.1 %collective-permute-start.16 = (s16[136,640]{1,0:T(8,128)(2,1)S(1)}, s16[136,640]{1,0:T(8,128)(2,1)S(1)}, u32[]{:S(2)}, u32[]{:S(2)}) collective-permute-start(s16[136,640]{1,0:T(8,128)(2,1)S(1)} %get-tuple-element.57), channel_id=1, source_target_pairs={{0,8},{8,0},{16,24},{24,16},{1,9},{9,1},{17,25},{25,17},{2,10},{10... | collective-permute-start | bytes 522248 | tf_op jit(solution)/shard_map/ppermute | solution.py:274
  42.3 7.3 %collective-permute-start.15 = (s16[136,512]{1,0:T(8,128)(2,1)S(1)}, s16[136,512]{1,0:T(8,128)(2,1)S(1)}, u32[]{:S(2)}, u32[]{:S(2)}) collective-permute-start(s16[136,512]{1,0:T(8,128)(2,1)S(1)} %get-tuple-element.50.refs_10_), channel_id=1, source_target_pairs={{0,2},{1,3},{2,0},{3,1},{4,6},{5,7},{6,4},{7,5},{8,10},{9,11},{10,... | collective-permute-start | bytes 417800 | tf_op jit(solution)/shard_map/ppermute | solution.py:274
  46.7 11.2 %collective-permute-start.18 = (s16[136,1152]{1,0:T(8,128)(2,1)S(1)}, s16[136,1152]{1,0:T(8,128)(2,1)S(1)}, u32[]{:S(2)}, u32[]{:S(2)}) collective-permute-start(s16[136,1152]{1,0:T(8,128)(2,1)S(1)} %get-tuple-element.60), channel_id=1, source_target_pairs={{0,8},{8,0},{16,24},{24,16},{1,9},{9,1},{17,25},{25,17},{2,10},{10... | collective-permute-start | bytes 940040 | tf_op jit(solution)/shard_map/ppermute | solution.py:274
  48.1 9.8 %collective-permute-start.19 = (s16[136,1152]{1,0:T(8,128)(2,1)S(1)}, s16[136,1152]{1,0:T(8,128)(2,1)S(1)}, u32[]{:S(2)}, u32[]{:S(2)}) collective-permute-start(s16[136,1152]{1,0:T(8,128)(2,1)S(1)} %get-tuple-element.51.refs_10_), channel_id=1, source_target_pairs={{0,16},{8,24},{16,0},{24,8},{1,17},{9,25},{17,1},{25,9},{2,18},{10... | collective-permute-start | bytes 940040 | tf_op jit(solution)/shard_map/ppermute | solution.py:274
  48.7 8.9 %collective-permute-start.14 = (s16[136,640]{1,0:T(8,128)(2,1)S(1)}, s16[136,640]{1,0:T(8,128)(2,1)S(1)}, u32[]{:S(2)}, u32[]{:S(2)}) collective-permute-start(s16[136,640]{1,0:T(8,128)(2,1)S(1)} %passed_sum.6.refs_3_), channel_id=1, source_target_pairs={{0,4},{1,5},{2,6},{3,7},{4,0},{5,1},{6,2},{7,3},{8,12},{9,13},{10,... | collective-permute-start | bytes 522248 | tf_op jit(solution)/shard_map/ppermute | solution.py:274
  49.8 8.1 %collective-permute-start.17 = (s16[136,640]{1,0:T(8,128)(2,1)S(1)}, s16[136,640]{1,0:T(8,128)(2,1)S(1)}, u32[]{:S(2)}, u32[]{:S(2)}) collective-permute-start(s16[136,640]{1,0:T(8,128)(2,1)S(1)} %passed_sum.7), channel_id=1, source_target_pairs={{0,2},{1,3},{2,0},{3,1},{4,6},{5,7},{6,4},{7,5},{8,10},{9,11},{10,... | collective-permute-start | bytes 522248 | tf_op jit(solution)/shard_map/ppermute | solution.py:274

commit v24 on v23

--- a/solution.py
+++ b/solution.py
@@ -26,7 +26,7 @@
 
 
 def part_widths(width):
-    first = width // (2 * LANES) * LANES
+    first = (width // LANES + 1) // 2 * LANES
     return (first, width - first)
 
 

time: 59.3 us -> 64.1 us (1.081)
  waiting for transfers between devices: 16.7 us -> 23.4 us
  starting transfers between devices: 25.7 us -> 23.8 us
    ppermute x20, waiting for transfers between devices: 16.7 us -> 23.4 us  [swapped(): lax.ppermute(array, axis, [(i, i ^ bit) for i in range(lax.axis_size(axis...]
    ppermute x20, starting transfers between devices: 25.7 us -> 23.8 us  [swapped(): lax.ppermute(array, axis, [(i, i ^ bit) for i in range(lax.axis_size(axis...]
  transfers between devices with their start and end apart: 20 -> 20, of which waited for: 6 -> 8; matrix products, arithmetic and copies ran while one was open for 0% -> 0% of each run, Pallas kernels for 20% -> 18%
where the time goes in v24:
time: 64.1 us; the launch traced here: 63.9 us
  starting transfers between devices  23.8 us (37%)
  waiting for transfers between devices  23.4 us (37%)
  Pallas kernels  13 us (20%)
  between operations  2.13 us (3%)
  local copies, waits for them, and re-layouts  1.66 us (3%)
    ppermute x20, starting transfers between devices, swapped(): lax.ppermute(array, axis, [(i, i ^ bit) for i in range(lax.axis_size(axis...  23.8 us
    ppermute x20, waiting for transfers between devices, swapped(): lax.ppermute(array, axis, [(i, i ^ bit) for i in range(lax.axis_size(axis...  23.4 us
    pallas_call x22, Pallas kernels, call(): pl.pallas_call(body, out_shape=[*out_shape, *(jax.ShapeDtypeStruct(a.shap...  13 us
    unnamed x6, local copies, waits for them, and re-layouts  1.66 us
  transfers between devices with their start and end apart: 20, of which 8 were waited for; matrix products, arithmetic and copies ran while one was open for 0% of the time, Pallas kernels for 18%

profile of v24, /device:TPU:0, one launch (start us, length us, event | category | flops | bytes accessed | tf_op | source)
XLA Modules:
  0.0 63.9 jit_solution(3588668992484799890)
XLA Ops:
  0.6 4.1 %collective-permute-start.2 = (bf16[128,1152]{1,0:T(8,128)(2,1)}, bf16[128,1152]{1,0:T(8,128)(2,1)S(1)}, u32[]{:S(2)}, u32[]{:S(2)}) collective-permute-start(bf16[128,1152]{1,0:T(8,128)(2,1)} %refs_4_.5), channel_id=1, source_target_pairs={{0,4},{1,5},{2,6},{3,7},{4,0},{5,1},{6,2},{7,3},{8,12},{9,13},{10,... | collective-permute-start | bytes 884744 | tf_op jit(solution)/shard_map/ppermute | solution.py:274
  4.7 1.6 %collective-permute-start.4 = (bf16[128,1152]{1,0:T(8,128)(2,1)}, bf16[128,1152]{1,0:T(8,128)(2,1)S(1)}, u32[]{:S(2)}, u32[]{:S(2)}) collective-permute-start(bf16[128,1152]{1,0:T(8,128)(2,1)} %refs_0_.12), channel_id=1, source_target_pairs={{0,2},{1,3},{2,0},{3,1},{4,6},{5,7},{6,4},{7,5},{8,10},{9,11},{10,... | collective-permute-start | bytes 884744 | tf_op jit(solution)/shard_map/ppermute | solution.py:274
  6.3 0.0 copy-start.1
  6.3 1.0 %copy-done.1 = bf16[128,1152]{1,0:T(8,128)(2,1)S(1)} copy-done((bf16[128,1152]{1,0:T(8,128)(2,1)S(1)}, bf16[128,1152]{1,0:T(8,128)(2,1)}, u32[]{:S(2)}) %copy-start.1) | copy-done | bytes 294936
  7.3 0.0 copy-start.2
  7.3 0.7 %copy-done.2 = s32[128]{0:T(128)S(1)} copy-done((s32[128]{0:T(128)S(1)}, s32[128]{0:T(128)}, u32[]{:S(2)}) %copy-start.2) | copy-done | bytes 536
  8.0 0.0 copy-start
  8.0 1.6 %collective-permute-start.1 = (bf16[136,1152]{1,0:T(8,128)(2,1)S(1)}, bf16[136,1152]{1,0:T(8,128)(2,1)S(1)}, u32[]{:S(2)}, u32[]{:S(2)}) collective-permute-start(bf16[136,1152]{1,0:T(8,128)(2,1)S(1)} %labelled.2.refs_2_.refs_7_.refs_4_.refs_5_), channel_id=1, source_target_pairs={{0,8},{8,0},{16,24},{24,16},{1,9},{9,1},{17,25},{25,17},{2,10},{10... | collective-permute-start | bytes 940040 | tf_op jit(solution)/shard_map/ppermute | solution.py:274
  9.6 1.5 %collective-permute-start = (bf16[128,1152]{1,0:T(8,128)(2,1)}, bf16[128,1152]{1,0:T(8,128)(2,1)S(1)}, u32[]{:S(2)}, u32[]{:S(2)}) collective-permute-start(bf16[128,1152]{1,0:T(8,128)(2,1)} %refs_4_.5), channel_id=1, source_target_pairs={{0,16},{8,24},{16,0},{24,8},{1,17},{9,25},{17,1},{25,9},{2,18},{10... | collective-permute-start | bytes 884744 | tf_op jit(solution)/shard_map/ppermute | solution.py:274
  11.1 0.4 collective-permute-start.5
  11.5 6.8 %collective-permute-done.2.refs_0_ = bf16[128,1152]{1,0:T(8,128)(2,1)S(1)} collective-permute-done((bf16[128,1152]{1,0:T(8,128)(2,1)}, bf16[128,1152]{1,0:T(8,128)(2,1)S(1)}, u32[]{:S(2)}, u32[]{:S(2)}) %collective-permute-start.2) | collective-permute-done | bytes 294944 | tf_op jit(solution)/shard_map/ppermute | solution.py:274
  18.4 0.3 collective-permute-done.5.refs_1_
  18.6 0.0 collective-permute-done.4.refs_0_
  18.7 0.0 collective-permute-done.refs_3_.refs_4_.refs_6_.refs_2_
  18.7 0.0 collective-permute-done.1.refs_4_.refs_5_.refs_6_.refs_3_
  18.7 0.0 copy-done
  18.8 0.1 bundled.3
  18.9 0.1 collective-permute-start.7
  19.0 1.6 %collective-permute-start.6 = (bf16[136,1152]{1,0:T(8,128)(2,1)S(1)}, bf16[136,1152]{1,0:T(8,128)(2,1)S(1)}, u32[]{:S(2)}, u32[]{:S(2)}) collective-permute-start(bf16[136,1152]{1,0:T(8,128)(2,1)S(1)} %labelled.3.refs_1_.refs_3_.refs_5_), channel_id=1, source_target_pairs={{0,8},{8,0},{16,24},{24,16},{1,9},{9,1},{17,25},{25,17},{2,10},{10... | collective-permute-start | bytes 940040 | tf_op jit(solution)/shard_map/ppermute | solution.py:274
  20.6 1.5 %collective-permute-start.3 = (bf16[128,1152]{1,0:T(8,128)(2,1)S(1)}, bf16[128,1152]{1,0:T(8,128)(2,1)S(1)}, u32[]{:S(2)}, u32[]{:S(2)}) collective-permute-start(bf16[128,1152]{1,0:T(8,128)(2,1)S(1)} %held.3.refs_2_.refs_0_.refs_5_), channel_id=1, source_target_pairs={{0,16},{8,24},{16,0},{24,8},{1,17},{9,25},{17,1},{25,9},{2,18},{10... | collective-permute-start | bytes 884744 | tf_op jit(solution)/shard_map/ppermute | solution.py:274
  23.4 0.0 collective-permute-done.7.refs_8_.refs_7_
  23.4 1.9 %early_sums.3 = (f32[128,1152]{1,0:T(8,128)S(1)}, f32[128,1152]{1,0:T(8,128)S(1)}, f32[128,1152]{1,0:T(8,128)S(1)}) custom-call(f32[1]{0:T(128)S(6)} %copy.21.refs_0_, f32[1]{0:T(128)S(6)} %copy.22.refs_1_, bf16[128,1152]{1,0:T(8,128)(2,1)S(1)} %held.3.refs_2_.refs_0_.refs_5_, bf16[136,1152]{1,0:T(8,128)(2,1)S(1)} %labelled.3.refs_1_.refs_3_.refs_5_, ...), custom_call_target="tpu_custom_call" | custom-call | flops 2304 | bytes 2304 | tf_op jit(solution)/shard_map/early_sums/pallas_call | solution.py:93
  25.3 1.9 %early_sums.2 = (f32[128,1152]{1,0:T(8,128)S(1)}, f32[128,1152]{1,0:T(8,128)S(1)}, f32[128,1152]{1,0:T(8,128)S(1)}) custom-call(f32[1]{0:T(128)S(6)} %copy.21.refs_0_, f32[1]{0:T(128)S(6)} %copy.22.refs_1_, bf16[128,1152]{1,0:T(8,128)(2,1)S(1)} %held.3.refs_2_.refs_0_.refs_5_, bf16[136,1152]{1,0:T(8,128)(2,1)S(1)} %labelled.3.refs_1_.refs_3_.refs_5_, ...), custom_call_target="tpu_custom_call" | custom-call | flops 2304 | bytes 2304 | tf_op jit(solution)/shard_map/early_sums/pallas_call | solution.py:93
  27.3 2.4 %collective-permute-done.3.refs_2_.refs_4_.refs_6_ = bf16[128,1152]{1,0:T(8,128)(2,1)S(1)} collective-permute-done((bf16[128,1152]{1,0:T(8,128)(2,1)S(1)}, bf16[128,1152]{1,0:T(8,128)(2,1)S(1)}, u32[]{:S(2)}, u32[]{:S(2)}) %collective-permute-start.3) | collective-permute-done | bytes 294944 | tf_op jit(solution)/shard_map/ppermute | solution.py:274
  29.7 0.0 collective-permute-done.6.refs_3_.refs_4_.refs_6_
  29.7 0.0 collective-permute-start.9
  29.7 0.5 collective-permute-start.8
  30.2 1.4 %late_rows_begun.2.refs_5_ = f32[128,1152]{1,0:T(8,128)S(1)} custom-call(f32[1]{0:T(128)S(6)} %copy.21.refs_0_, f32[1]{0:T(128)S(6)} %copy.22.refs_1_, bf16[128,1152]{1,0:T(8,128)(2,1)S(1)} %collective-permute-done.3.refs_2_.refs_4_.refs_6_, bf16[136,1152]{1,0:T(8,128)(2,1)S(1)} %collective-permute-done.6.refs_3_.refs_4_.refs_6_, ...), custom_call_target="tpu_custom_call" | custom-call | flops 896 | bytes 896 | tf_op jit(solution)/shard_map/late_rows_begun/pallas_call | solution.py:93
  31.5 0.0 collective-permute-done.9.refs_4_.refs_5_.refs_7_
  31.6 0.6 late_rows.2
  32.2 1.6 %collective-permute-start.11 = (s16[136,640]{1,0:T(8,128)(2,1)S(1)}, s16[136,640]{1,0:T(8,128)(2,1)S(1)}, u32[]{:S(2)}, u32[]{:S(2)}) collective-permute-start(s16[136,640]{1,0:T(8,128)(2,1)S(1)} %get-tuple-element.46.refs_8_), channel_id=1, source_target_pairs={{0,16},{8,24},{16,0},{24,8},{1,17},{9,25},{17,1},{25,9},{2,18},{10... | collective-permute-start | bytes 522248 | tf_op jit(solution)/shard_map/ppermute | solution.py:274
  33.8 1.3 %late_rows_begun.3.refs_5_ = f32[128,1152]{1,0:T(8,128)S(1)} custom-call(f32[1]{0:T(128)S(6)} %copy.21.refs_0_, f32[1]{0:T(128)S(6)} %copy.22.refs_1_, bf16[128,1152]{1,0:T(8,128)(2,1)S(1)} %collective-permute-done.3.refs_2_.refs_4_.refs_6_, bf16[136,1152]{1,0:T(8,128)(2,1)S(1)} %collective-permute-done.6.refs_3_.refs_4_.refs_6_, ...), custom_call_target="tpu_custom_call" | custom-call | flops 896 | bytes 896 | tf_op jit(solution)/shard_map/late_rows_begun/pallas_call | solution.py:93
  35.1 0.0 collective-permute-done.8.refs_4_.refs_5_.refs_7_
  35.1 0.6 late_rows.3
  35.7 0.7 %collective-permute-start.10 = (s16[136,640]{1,0:T(8,128)(2,1)S(1)}, s16[136,640]{1,0:T(8,128)(2,1)S(1)}, u32[]{:S(2)}, u32[]{:S(2)}) collective-permute-start(s16[136,640]{1,0:T(8,128)(2,1)S(1)} %get-tuple-element.48.refs_7_), channel_id=1, source_target_pairs={{0,8},{8,0},{16,24},{24,16},{1,9},{9,1},{17,25},{25,17},{2,10},{10... | collective-permute-start | bytes 522248 | tf_op jit(solution)/shard_map/ppermute | solution.py:274
  36.4 0.7 %late_columns.4.refs_7_.refs_0_ = f32[128,1152]{1,0:T(8,128)S(1)} custom-call(f32[1]{0:T(128)S(6)} %copy.21.refs_0_, f32[1]{0:T(128)S(6)} %copy.22.refs_1_, bf16[128,1152]{1,0:T(8,128)(2,1)S(1)} %held.3.refs_2_.refs_0_.refs_5_, bf16[136,1152]{1,0:T(8,128)(2,1)S(1)} %labelled.3.refs_1_.refs_3_.refs_5_, ...), custom_call_target="tpu_custom_call" | custom-call | flops 256 | bytes 256 | tf_op jit(solution)/shard_map/late_columns/pallas_call | solution.py:93
  37.1 1.4 %collective-permute-done.11.refs_1_ = s16[136,640]{1,0:T(8,128)(2,1)S(1)} collective-permute-done((s16[136,640]{1,0:T(8,128)(2,1)S(1)}, s16[136,640]{1,0:T(8,128)(2,1)S(1)}, u32[]{:S(2)}, u32[]{:S(2)}) %collective-permute-start.11) | collective-permute-done | bytes 174112 | tf_op jit(solution)/shard_map/ppermute | solution.py:274
  38.6 0.1 passed_sum.5
  38.7 1.6 %collective-permute-start.13 = (s16[136,512]{1,0:T(8,128)(2,1)S(1)}, s16[136,512]{1,0:T(8,128)(2,1)S(1)}, u32[]{:S(2)}, u32[]{:S(2)}) collective-permute-start(s16[136,512]{1,0:T(8,128)(2,1)S(1)} %get-tuple-element.54), channel_id=1, source_target_pairs={{0,16},{8,24},{16,0},{24,8},{1,17},{9,25},{17,1},{25,9},{2,18},{10... | collective-permute-start | bytes 417800 | tf_op jit(solution)/shard_map/ppermute | solution.py:274
  40.2 1.3 %collective-permute-start.12 = (s16[136,640]{1,0:T(8,128)(2,1)S(1)}, s16[136,640]{1,0:T(8,128)(2,1)S(1)}, u32[]{:S(2)}, u32[]{:S(2)}) collective-permute-start(s16[136,640]{1,0:T(8,128)(2,1)S(1)} %get-tuple-element.53), channel_id=1, source_target_pairs={{0,4},{1,5},{2,6},{3,7},{4,0},{5,1},{6,2},{7,3},{8,12},{9,13},{10,... | collective-permute-start | bytes 522248 | tf_op jit(solution)/shard_map/ppermute | solution.py:274
  41.6 0.7 %late_columns.5.refs_0_ = f32[128,1152]{1,0:T(8,128)S(1)} custom-call(f32[1]{0:T(128)S(6)} %copy.21.refs_0_, f32[1]{0:T(128)S(6)} %copy.22.refs_1_, bf16[128,1152]{1,0:T(8,128)(2,1)S(1)} %held.3.refs_2_.refs_0_.refs_5_, bf16[136,1152]{1,0:T(8,128)(2,1)S(1)} %labelled.3.refs_1_.refs_3_.refs_5_, ...), custom_call_target="tpu_custom_call" | custom-call | flops 256 | bytes 256 | tf_op jit(solution)/shard_map/late_columns/pallas_call | solution.py:93
  42.3 0.0 collective-permute-done.10.refs_1_
  42.3 0.1 passed_sum.4
  42.4 2.4 %collective-permute-start.15 = (s16[136,640]{1,0:T(8,128)(2,1)S(1)}, s16[136,640]{1,0:T(8,128)(2,1)S(1)}, u32[]{:S(2)}, u32[]{:S(2)}) collective-permute-start(s16[136,640]{1,0:T(8,128)(2,1)S(1)} %get-tuple-element.50.refs_10_), channel_id=1, source_target_pairs={{0,2},{1,3},{2,0},{3,1},{4,6},{5,7},{6,4},{7,5},{8,10},{9,11},{10,... | collective-permute-start | bytes 522248 | tf_op jit(solution)/shard_map/ppermute | solution.py:274
  44.8 1.0 %late_columns.6 = (f32[128,1152]{1,0:T(8,128)S(1)}, s16[136,1152]{1,0:T(8,128)(2,1)S(1)}) custom-call(f32[1]{0:T(128)S(6)} %copy.21.refs_0_, f32[1]{0:T(128)S(6)} %copy.22.refs_1_, bf16[128,1152]{1,0:T(8,128)(2,1)S(1)} %collective-permute-done.refs_3_.refs_4_.refs_6_.refs_2_, bf16[136,1152]{1,0:T(8,128)(2,1)S(1)} %collective-permute-done.1.refs_4_.refs_5_.refs_6_.refs_3_, ...), custom_call_target="tpu_custom_call" | custom-call | flops 512 | bytes 512 | tf_op jit(solution)/shard_map/late_columns/pallas_call | solution.py:93
  45.8 1.0 %late_columns.7 = (f32[128,1152]{1,0:T(8,128)S(1)}, s16[136,1152]{1,0:T(8,128)(2,1)S(1)}) custom-call(f32[1]{0:T(128)S(6)} %copy.21.refs_0_, f32[1]{0:T(128)S(6)} %copy.22.refs_1_, bf16[128,1152]{1,0:T(8,128)(2,1)S(1)} %collective-permute-done.refs_3_.refs_4_.refs_6_.refs_2_, bf16[136,1152]{1,0:T(8,128)(2,1)S(1)} %collective-permute-done.1.refs_4_.refs_5_.refs_6_.refs_3_, ...), custom_call_target="tpu_custom_call" | custom-call | flops 512 | bytes 512 | tf_op jit(solution)/shard_map/late_columns/pallas_call | solution.py:93
  46.8 0.7 %collective-permute-start.18 = (s16[136,1152]{1,0:T(8,128)(2,1)S(1)}, s16[136,1152]{1,0:T(8,128)(2,1)S(1)}, u32[]{:S(2)}, u32[]{:S(2)}) collective-permute-start(s16[136,1152]{1,0:T(8,128)(2,1)S(1)} %get-tuple-element.60), channel_id=1, source_target_pairs={{0,8},{8,0},{16,24},{24,16},{1,9},{9,1},{17,25},{25,17},{2,10},{10... | collective-permute-start | bytes 940040 | tf_op jit(solution)/shard_map/ppermute | solution.py:274
  47.5 0.5 collective-permute-start.19
  48.1 0.0 collective-permute-done.13.refs_1_
  48.1 1.4 %collective-permute-start.16 = (s16[136,512]{1,0:T(8,128)(2,1)S(1)}, s16[136,512]{1,0:T(8,128)(2,1)S(1)}, u32[]{:S(2)}, u32[]{:S(2)}) collective-permute-start(s16[136,512]{1,0:T(8,128)(2,1)S(1)} %get-tuple-element.57), channel_id=1, source_target_pairs={{0,8},{8,0},{16,24},{24,16},{1,9},{9,1},{17,25},{25,17},{2,10},{10... | collective-permute-start | bytes 417800 | tf_op jit(solution)/shard_map/ppermute | solution.py:274
  49.4 0.7 %collective-permute-done.12.refs_2_.refs_0_ = s16[136,640]{1,0:T(8,128)(2,1)S(1)} collective-permute-done((s16[136,640]{1,0:T(8,128)(2,1)S(1)}, s16[136,640]{1,0:T(8,128)(2,1)S(1)}, u32[]{:S(2)}, u32[]{:S(2)}) %collective-permute-start.12) | collective-permute-done | bytes 174112 | tf_op jit(solution)/shard_map/ppermute | solution.py:274
  50.1 0.1 passed_sum.6.refs_3_
  50.2 0.3 collective-permute-start.14
  50.5 7.0 %collective-permute-done.16.refs_1_ = s16[136,512]{1,0:T(8,128)(2,1)S(1)} collective-permute-done((s16[136,512]{1,0:T(8,128)(2,1)S(1)}, s16[136,512]{1,0:T(8,128)(2,1)S(1)}, u32[]{:S(2)}, u32[]{:S(2)}) %collective-permute-start.16) | collective-permute-done | bytes 139296 | tf_op jit(solution)/shard_map/ppermute | solution.py:274
  57.5 0.0 collective-permute-done.15.refs_2_
  57.5 0.1 passed_sum.7
  57.6 0.4 collective-permute-start.17
  58.0 0.4 collective-permute-done.14.refs_1_
  58.4 4.3 %collective-permute-done.17.refs_3_ = s16[136,512]{1,0:T(8,128)(2,1)S(1)} collective-permute-done((s16[136,512]{1,0:T(8,128)(2,1)S(1)}, s16[136,512]{1,0:T(8,128)(2,1)S(1)}, u32[]{:S(2)}, u32[]{:S(2)}) %collective-permute-start.17) | collective-permute-done | bytes 139296 | tf_op jit(solution)/shard_map/ppermute | solution.py:274
  62.7 0.0 collective-permute-done.18.refs_4_
  62.7 0.0 collective-permute-done.19.refs_8_
  62.7 1.2 %output_sums.1 = (f32[128,1152]{1,0:T(8,128)}, f32[128,1152]{1,0:T(8,128)}) custom-call(f32[1]{0:T(128)S(6)} %copy.21.refs_0_, f32[128,1152]{1,0:T(8,128)S(1)} %get-tuple-element.52.refs_1_, s16[136,640]{1,0:T(8,128)(2,1)S(1)} %get-tuple-element.58.refs_2_, s16[136,512]{1,0:T(8,128)(2,1)S(1)} %get-tuple-element.59.refs_3_, ...), custom_call_target="tpu_custom_call" | custom-call | flops 128 | bytes 128 | tf_op jit(solution)/shard_map/output_sums/pallas_call | solution.py:93
  (6 shorter events, 0.1 us)
Async XLA Ops:
  0.6 17.8 %collective-permute-start.2 = (bf16[128,1152]{1,0:T(8,128)(2,1)}, bf16[128,1152]{1,0:T(8,128)(2,1)S(1)}, u32[]{:S(2)}, u32[]{:S(2)}) collective-permute-start(bf16[128,1152]{1,0:T(8,128)(2,1)} %refs_4_.5), channel_id=1, source_target_pairs={{0,4},{1,5},{2,6},{3,7},{4,0},{5,1},{6,2},{7,3},{8,12},{9,13},{10,... | collective-permute-start | bytes 884744 | tf_op jit(solution)/shard_map/ppermute | solution.py:274
  4.7 13.9 %collective-permute-start.4 = (bf16[128,1152]{1,0:T(8,128)(2,1)}, bf16[128,1152]{1,0:T(8,128)(2,1)S(1)}, u32[]{:S(2)}, u32[]{:S(2)}) collective-permute-start(bf16[128,1152]{1,0:T(8,128)(2,1)} %refs_0_.12), channel_id=1, source_target_pairs={{0,2},{1,3},{2,0},{3,1},{4,6},{5,7},{6,4},{7,5},{8,10},{9,11},{10,... | collective-permute-start | bytes 884744 | tf_op jit(solution)/shard_map/ppermute | solution.py:274
  6.3 1.0 %copy-start.1 = (bf16[128,1152]{1,0:T(8,128)(2,1)S(1)}, bf16[128,1152]{1,0:T(8,128)(2,1)}, u32[]{:S(2)}) copy-start(bf16[128,1152]{1,0:T(8,128)(2,1)} %refs_0_.12) | copy-start | bytes 884740
  7.3 0.7 %copy-start.2 = (s32[128]{0:T(128)S(1)}, s32[128]{0:T(128)}, u32[]{:S(2)}) copy-start(s32[128]{0:T(128)} %param.7) | copy-start | bytes 1540
  8.0 10.8 %copy-start = (bf16[128,1152]{1,0:T(8,128)(2,1)S(1)}, bf16[128,1152]{1,0:T(8,128)(2,1)}, u32[]{:S(2)}) copy-start(bf16[128,1152]{1,0:T(8,128)(2,1)} %refs_4_.5) | copy-start | bytes 884740
  8.0 10.7 %collective-permute-start.1 = (bf16[136,1152]{1,0:T(8,128)(2,1)S(1)}, bf16[136,1152]{1,0:T(8,128)(2,1)S(1)}, u32[]{:S(2)}, u32[]{:S(2)}) collective-permute-start(bf16[136,1152]{1,0:T(8,128)(2,1)S(1)} %labelled.2.refs_2_.refs_7_.refs_4_.refs_5_), channel_id=1, source_target_pairs={{0,8},{8,0},{16,24},{24,16},{1,9},{9,1},{17,25},{25,17},{2,10},{10... | collective-permute-start | bytes 940040 | tf_op jit(solution)/shard_map/ppermute | solution.py:274
  9.6 9.2 %collective-permute-start = (bf16[128,1152]{1,0:T(8,128)(2,1)}, bf16[128,1152]{1,0:T(8,128)(2,1)S(1)}, u32[]{:S(2)}, u32[]{:S(2)}) collective-permute-start(bf16[128,1152]{1,0:T(8,128)(2,1)} %refs_4_.5), channel_id=1, source_target_pairs={{0,16},{8,24},{16,0},{24,8},{1,17},{9,25},{17,1},{25,9},{2,18},{10... | collective-permute-start | bytes 884744 | tf_op jit(solution)/shard_map/ppermute | solution.py:274
  11.1 7.6 %collective-permute-start.5 = (s32[1,128]{1,0:T(1,128)}, s32[1,128]{1,0:T(1,128)S(1)}, u32[]{:S(2)}, u32[]{:S(2)}) collective-permute-start(s32[1,128]{1,0:T(1,128)} %bitcast.1), channel_id=1, source_target_pairs={{0,2},{1,3},{2,0},{3,1},{4,6},{5,7},{6,4},{7,5},{8,10},{9,11},{10,... | collective-permute-start | bytes 1544 | tf_op jit(solution)/shard_map/ppermute | solution.py:274
  18.9 4.5 %collective-permute-start.7 = (bf16[792,1152]{1,0:T(8,128)(2,1)S(1)}, bf16[792,1152]{1,0:T(8,128)(2,1)S(1)}, u32[]{:S(2)}, u32[]{:S(2)}) collective-permute-start(bf16[792,1152]{1,0:T(8,128)(2,1)S(1)} %bundled.3), channel_id=1, source_target_pairs={{0,1},{1,0},{2,3},{3,2},{4,5},{5,4},{6,7},{7,6},{8,9},{9,8},{10,11... | collective-permute-start | bytes 5474312 | tf_op jit(solution)/shard_map/ppermute | solution.py:274
  19.0 10.7 %collective-permute-start.6 = (bf16[136,1152]{1,0:T(8,128)(2,1)S(1)}, bf16[136,1152]{1,0:T(8,128)(2,1)S(1)}, u32[]{:S(2)}, u32[]{:S(2)}) collective-permute-start(bf16[136,1152]{1,0:T(8,128)(2,1)S(1)} %labelled.3.refs_1_.refs_3_.refs_5_), channel_id=1, source_target_pairs={{0,8},{8,0},{16,24},{24,16},{1,9},{9,1},{17,25},{25,17},{2,10},{10... | collective-permute-start | bytes 940040 | tf_op jit(solution)/shard_map/ppermute | solution.py:274
  20.6 9.1 %collective-permute-start.3 = (bf16[128,1152]{1,0:T(8,128)(2,1)S(1)}, bf16[128,1152]{1,0:T(8,128)(2,1)S(1)}, u32[]{:S(2)}, u32[]{:S(2)}) collective-permute-start(bf16[128,1152]{1,0:T(8,128)(2,1)S(1)} %held.3.refs_2_.refs_0_.refs_5_), channel_id=1, source_target_pairs={{0,16},{8,24},{16,0},{24,8},{1,17},{9,25},{17,1},{25,9},{2,18},{10... | collective-permute-start | bytes 884744 | tf_op jit(solution)/shard_map/ppermute | solution.py:274
  29.7 1.9 %collective-permute-start.9 = (bf16[136,1152]{1,0:T(8,128)(2,1)S(1)}, bf16[136,1152]{1,0:T(8,128)(2,1)S(1)}, u32[]{:S(2)}, u32[]{:S(2)}) collective-permute-start(bf16[136,1152]{1,0:T(8,128)(2,1)S(1)} %collective-permute-done.6.refs_3_.refs_4_.refs_6_), channel_id=1, source_target_pairs={{0,1},{1,0},{2,3},{3,2},{4,5},{5,4},{6,7},{7,6},{8,9},{9,8},{10,11... | collective-permute-start | bytes 940040 | tf_op jit(solution)/shard_map/ppermute | solution.py:274
  29.7 5.4 %collective-permute-start.8 = (bf16[128,1152]{1,0:T(8,128)(2,1)S(1)}, bf16[128,1152]{1,0:T(8,128)(2,1)S(1)}, u32[]{:S(2)}, u32[]{:S(2)}) collective-permute-start(bf16[128,1152]{1,0:T(8,128)(2,1)S(1)} %collective-permute-done.3.refs_2_.refs_4_.refs_6_), channel_id=1, source_target_pairs={{0,1},{1,0},{2,3},{3,2},{4,5},{5,4},{6,7},{7,6},{8,9},{9,8},{10,11... | collective-permute-start | bytes 884744 | tf_op jit(solution)/shard_map/ppermute | solution.py:274
  32.2 6.4 %collective-permute-start.11 = (s16[136,640]{1,0:T(8,128)(2,1)S(1)}, s16[136,640]{1,0:T(8,128)(2,1)S(1)}, u32[]{:S(2)}, u32[]{:S(2)}) collective-permute-start(s16[136,640]{1,0:T(8,128)(2,1)S(1)} %get-tuple-element.46.refs_8_), channel_id=1, source_target_pairs={{0,16},{8,24},{16,0},{24,8},{1,17},{9,25},{17,1},{25,9},{2,18},{10... | collective-permute-start | bytes 522248 | tf_op jit(solution)/shard_map/ppermute | solution.py:274
  35.7 6.5 %collective-permute-start.10 = (s16[136,640]{1,0:T(8,128)(2,1)S(1)}, s16[136,640]{1,0:T(8,128)(2,1)S(1)}, u32[]{:S(2)}, u32[]{:S(2)}) collective-permute-start(s16[136,640]{1,0:T(8,128)(2,1)S(1)} %get-tuple-element.48.refs_7_), channel_id=1, source_target_pairs={{0,8},{8,0},{16,24},{24,16},{1,9},{9,1},{17,25},{25,17},{2,10},{10... | collective-permute-start | bytes 522248 | tf_op jit(solution)/shard_map/ppermute | solution.py:274
  38.7 9.4 %collective-permute-start.13 = (s16[136,512]{1,0:T(8,128)(2,1)S(1)}, s16[136,512]{1,0:T(8,128)(2,1)S(1)}, u32[]{:S(2)}, u32[]{:S(2)}) collective-permute-start(s16[136,512]{1,0:T(8,128)(2,1)S(1)} %get-tuple-element.54), channel_id=1, source_target_pairs={{0,16},{8,24},{16,0},{24,8},{1,17},{9,25},{17,1},{25,9},{2,18},{10... | collective-permute-start | bytes 417800 | tf_op jit(solution)/shard_map/ppermute | solution.py:274
  40.2 9.9 %collective-permute-start.12 = (s16[136,640]{1,0:T(8,128)(2,1)S(1)}, s16[136,640]{1,0:T(8,128)(2,1)S(1)}, u32[]{:S(2)}, u32[]{:S(2)}) collective-permute-start(s16[136,640]{1,0:T(8,128)(2,1)S(1)} %get-tuple-element.53), channel_id=1, source_target_pairs={{0,4},{1,5},{2,6},{3,7},{4,0},{5,1},{6,2},{7,3},{8,12},{9,13},{10,... | collective-permute-start | bytes 522248 | tf_op jit(solution)/shard_map/ppermute | solution.py:274
  42.4 15.1 %collective-permute-start.15 = (s16[136,640]{1,0:T(8,128)(2,1)S(1)}, s16[136,640]{1,0:T(8,128)(2,1)S(1)}, u32[]{:S(2)}, u32[]{:S(2)}) collective-permute-start(s16[136,640]{1,0:T(8,128)(2,1)S(1)} %get-tuple-element.50.refs_10_), channel_id=1, source_target_pairs={{0,2},{1,3},{2,0},{3,1},{4,6},{5,7},{6,4},{7,5},{8,10},{9,11},{10,... | collective-permute-start | bytes 522248 | tf_op jit(solution)/shard_map/ppermute | solution.py:274
  46.8 15.9 %collective-permute-start.18 = (s16[136,1152]{1,0:T(8,128)(2,1)S(1)}, s16[136,1152]{1,0:T(8,128)(2,1)S(1)}, u32[]{:S(2)}, u32[]{:S(2)}) collective-permute-start(s16[136,1152]{1,0:T(8,128)(2,1)S(1)} %get-tuple-element.60), channel_id=1, source_target_pairs={{0,8},{8,0},{16,24},{24,16},{1,9},{9,1},{17,25},{25,17},{2,10},{10... | collective-permute-start | bytes 940040 | tf_op jit(solution)/shard_map/ppermute | solution.py:274
  47.5 15.2 %collective-permute-start.19 = (s16[136,1152]{1,0:T(8,128)(2,1)S(1)}, s16[136,1152]{1,0:T(8,128)(2,1)S(1)}, u32[]{:S(2)}, u32[]{:S(2)}) collective-permute-start(s16[136,1152]{1,0:T(8,128)(2,1)S(1)} %get-tuple-element.51.refs_10_), channel_id=1, source_target_pairs={{0,16},{8,24},{16,0},{24,8},{1,17},{9,25},{17,1},{25,9},{2,18},{10... | collective-permute-start | bytes 940040 | tf_op jit(solution)/shard_map/ppermute | solution.py:274
  48.1 9.4 %collective-permute-start.16 = (s16[136,512]{1,0:T(8,128)(2,1)S(1)}, s16[136,512]{1,0:T(8,128)(2,1)S(1)}, u32[]{:S(2)}, u32[]{:S(2)}) collective-permute-start(s16[136,512]{1,0:T(8,128)(2,1)S(1)} %get-tuple-element.57), channel_id=1, source_target_pairs={{0,8},{8,0},{16,24},{24,16},{1,9},{9,1},{17,25},{25,17},{2,10},{10... | collective-permute-start | bytes 417800 | tf_op jit(solution)/shard_map/ppermute | solution.py:274
  50.2 8.2 %collective-permute-start.14 = (s16[136,512]{1,0:T(8,128)(2,1)S(1)}, s16[136,512]{1,0:T(8,128)(2,1)S(1)}, u32[]{:S(2)}, u32[]{:S(2)}) collective-permute-start(s16[136,512]{1,0:T(8,128)(2,1)S(1)} %passed_sum.6.refs_3_), channel_id=1, source_target_pairs={{0,4},{1,5},{2,6},{3,7},{4,0},{5,1},{6,2},{7,3},{8,12},{9,13},{10,... | collective-permute-start | bytes 417800 | tf_op jit(solution)/shard_map/ppermute | solution.py:274
  57.6 5.1 %collective-permute-start.17 = (s16[136,512]{1,0:T(8,128)(2,1)S(1)}, s16[136,512]{1,0:T(8,128)(2,1)S(1)}, u32[]{:S(2)}, u32[]{:S(2)}) collective-permute-start(s16[136,512]{1,0:T(8,128)(2,1)S(1)} %passed_sum.7), channel_id=1, source_target_pairs={{0,2},{1,3},{2,0},{3,1},{4,6},{5,7},{6,4},{7,5},{8,10},{9,11},{10,... | collective-permute-start | bytes 417800 | tf_op jit(solution)/shard_map/ppermute | solution.py:274

commit v25 on v23

--- a/solution.py
+++ b/solution.py
@@ -15,7 +15,7 @@
 TILE = 256
 LANES = 128
 BUNDLE_COST = 6 * 10**8
-HELD_COST = 3 * 10**8
+HELD_COST = 85 * 10**7
 SMEM = pl.BlockSpec(memory_space=pltpu.SMEM)
 VMEM = pl.BlockSpec(memory_space=pltpu.VMEM)
 ANY = pl.BlockSpec(memory_space=pl.ANY)

time: 59.3 us -> 62.2 us (1.049)
  waiting for transfers between devices: 16.7 us -> 19.5 us
    ppermute x20, waiting for transfers between devices: 16.7 us -> 19.5 us  [swapped(): lax.ppermute(array, axis, [(i, i ^ bit) for i in range(lax.axis_size(axis...]
  transfers between devices with their start and end apart: 20 -> 20, of which waited for: 6 -> 7; matrix products, arithmetic and copies ran while one was open for 0% -> 0% of each run, Pallas kernels for 20% -> 19%
where the time goes in v25:
time: 62.2 us; the launch traced here: 62 us
  starting transfers between devices  25.8 us (41%)
  waiting for transfers between devices  19.5 us (31%)
  Pallas kernels  12.9 us (21%)
  between operations  2.14 us (3%)
  local copies, waits for them, and re-layouts  1.66 us (3%)
    ppermute x20, starting transfers between devices, swapped(): lax.ppermute(array, axis, [(i, i ^ bit) for i in range(lax.axis_size(axis...  25.8 us
    ppermute x20, waiting for transfers between devices, swapped(): lax.ppermute(array, axis, [(i, i ^ bit) for i in range(lax.axis_size(axis...  19.5 us
    pallas_call x22, Pallas kernels, call(): pl.pallas_call(body, out_shape=[*out_shape, *(jax.ShapeDtypeStruct(a.shap...  12.9 us
    unnamed x6, local copies, waits for them, and re-layouts  1.66 us
  transfers between devices with their start and end apart: 20, of which 7 were waited for; matrix products, arithmetic and copies ran while one was open for 0% of the time, Pallas kernels for 19%

profile of v25, /device:TPU:0, one launch (start us, length us, event | category | flops | bytes accessed | tf_op | source)
XLA Modules:
  0.0 62.0 jit_solution(7397684894030841961)
XLA Ops:
  0.6 4.1 %collective-permute-start.2 = (bf16[128,1152]{1,0:T(8,128)(2,1)}, bf16[128,1152]{1,0:T(8,128)(2,1)S(1)}, u32[]{:S(2)}, u32[]{:S(2)}) collective-permute-start(bf16[128,1152]{1,0:T(8,128)(2,1)} %refs_4_.5), channel_id=1, source_target_pairs={{0,4},{1,5},{2,6},{3,7},{4,0},{5,1},{6,2},{7,3},{8,12},{9,13},{10,... | collective-permute-start | bytes 884744 | tf_op jit(solution)/shard_map/ppermute | solution.py:274
  4.7 1.6 %collective-permute-start.4 = (bf16[128,1152]{1,0:T(8,128)(2,1)}, bf16[128,1152]{1,0:T(8,128)(2,1)S(1)}, u32[]{:S(2)}, u32[]{:S(2)}) collective-permute-start(bf16[128,1152]{1,0:T(8,128)(2,1)} %refs_0_.12), channel_id=1, source_target_pairs={{0,2},{1,3},{2,0},{3,1},{4,6},{5,7},{6,4},{7,5},{8,10},{9,11},{10,... | collective-permute-start | bytes 884744 | tf_op jit(solution)/shard_map/ppermute | solution.py:274
  6.3 0.0 copy-start.1
  6.3 1.0 %copy-done.1 = bf16[128,1152]{1,0:T(8,128)(2,1)S(1)} copy-done((bf16[128,1152]{1,0:T(8,128)(2,1)S(1)}, bf16[128,1152]{1,0:T(8,128)(2,1)}, u32[]{:S(2)}) %copy-start.1) | copy-done | bytes 294936
  7.3 0.0 copy-start.2
  7.3 0.7 %copy-done.2 = s32[128]{0:T(128)S(1)} copy-done((s32[128]{0:T(128)S(1)}, s32[128]{0:T(128)}, u32[]{:S(2)}) %copy-start.2) | copy-done | bytes 536
  8.0 0.0 copy-start
  8.0 1.6 %collective-permute-start.1 = (bf16[136,1152]{1,0:T(8,128)(2,1)S(1)}, bf16[136,1152]{1,0:T(8,128)(2,1)S(1)}, u32[]{:S(2)}, u32[]{:S(2)}) collective-permute-start(bf16[136,1152]{1,0:T(8,128)(2,1)S(1)} %labelled.2.refs_2_.refs_7_.refs_4_.refs_5_), channel_id=1, source_target_pairs={{0,8},{8,0},{16,24},{24,16},{1,9},{9,1},{17,25},{25,17},{2,10},{10... | collective-permute-start | bytes 940040 | tf_op jit(solution)/shard_map/ppermute | solution.py:274
  9.6 1.5 %collective-permute-start = (bf16[128,1152]{1,0:T(8,128)(2,1)}, bf16[128,1152]{1,0:T(8,128)(2,1)S(1)}, u32[]{:S(2)}, u32[]{:S(2)}) collective-permute-start(bf16[128,1152]{1,0:T(8,128)(2,1)} %refs_4_.5), channel_id=1, source_target_pairs={{0,16},{8,24},{16,0},{24,8},{1,17},{9,25},{17,1},{25,9},{2,18},{10... | collective-permute-start | bytes 884744 | tf_op jit(solution)/shard_map/ppermute | solution.py:274
  11.1 0.4 collective-permute-start.5
  11.5 6.8 %collective-permute-done.2.refs_0_ = bf16[128,1152]{1,0:T(8,128)(2,1)S(1)} collective-permute-done((bf16[128,1152]{1,0:T(8,128)(2,1)}, bf16[128,1152]{1,0:T(8,128)(2,1)S(1)}, u32[]{:S(2)}, u32[]{:S(2)}) %collective-permute-start.2) | collective-permute-done | bytes 294944 | tf_op jit(solution)/shard_map/ppermute | solution.py:274
  18.4 0.3 collective-permute-done.5.refs_1_
  18.6 0.0 collective-permute-done.4.refs_0_
  18.7 0.0 collective-permute-done.refs_3_.refs_4_.refs_6_.refs_2_
  18.7 0.0 collective-permute-done.1.refs_4_.refs_5_.refs_6_.refs_3_
  18.7 0.0 copy-done
  18.8 0.1 bundled.3
  18.9 0.1 collective-permute-start.7
  19.0 1.6 %collective-permute-start.6 = (bf16[136,1152]{1,0:T(8,128)(2,1)S(1)}, bf16[136,1152]{1,0:T(8,128)(2,1)S(1)}, u32[]{:S(2)}, u32[]{:S(2)}) collective-permute-start(bf16[136,1152]{1,0:T(8,128)(2,1)S(1)} %labelled.3.refs_1_.refs_3_.refs_5_), channel_id=1, source_target_pairs={{0,8},{8,0},{16,24},{24,16},{1,9},{9,1},{17,25},{25,17},{2,10},{10... | collective-permute-start | bytes 940040 | tf_op jit(solution)/shard_map/ppermute | solution.py:274
  20.6 1.5 %collective-permute-start.3 = (bf16[128,1152]{1,0:T(8,128)(2,1)S(1)}, bf16[128,1152]{1,0:T(8,128)(2,1)S(1)}, u32[]{:S(2)}, u32[]{:S(2)}) collective-permute-start(bf16[128,1152]{1,0:T(8,128)(2,1)S(1)} %held.3.refs_2_.refs_0_.refs_5_), channel_id=1, source_target_pairs={{0,16},{8,24},{16,0},{24,8},{1,17},{9,25},{17,1},{25,9},{2,18},{10... | collective-permute-start | bytes 884744 | tf_op jit(solution)/shard_map/ppermute | solution.py:274
  23.4 0.0 collective-permute-done.7.refs_8_.refs_7_
  23.4 1.9 %early_sums.3 = (f32[128,1152]{1,0:T(8,128)S(1)}, f32[128,1152]{1,0:T(8,128)S(1)}, f32[128,1152]{1,0:T(8,128)S(1)}) custom-call(f32[1]{0:T(128)S(6)} %copy.21.refs_0_, f32[1]{0:T(128)S(6)} %copy.22.refs_1_, bf16[128,1152]{1,0:T(8,128)(2,1)S(1)} %held.3.refs_2_.refs_0_.refs_5_, bf16[136,1152]{1,0:T(8,128)(2,1)S(1)} %labelled.3.refs_1_.refs_3_.refs_5_, ...), custom_call_target="tpu_custom_call" | custom-call | flops 2304 | bytes 2304 | tf_op jit(solution)/shard_map/early_sums/pallas_call | solution.py:93
  25.3 1.9 %early_sums.2 = (f32[128,1152]{1,0:T(8,128)S(1)}, f32[128,1152]{1,0:T(8,128)S(1)}, f32[128,1152]{1,0:T(8,128)S(1)}) custom-call(f32[1]{0:T(128)S(6)} %copy.21.refs_0_, f32[1]{0:T(128)S(6)} %copy.22.refs_1_, bf16[128,1152]{1,0:T(8,128)(2,1)S(1)} %held.3.refs_2_.refs_0_.refs_5_, bf16[136,1152]{1,0:T(8,128)(2,1)S(1)} %labelled.3.refs_1_.refs_3_.refs_5_, ...), custom_call_target="tpu_custom_call" | custom-call | flops 2304 | bytes 2304 | tf_op jit(solution)/shard_map/early_sums/pallas_call | solution.py:93
  27.3 2.4 %collective-permute-done.3.refs_2_.refs_4_.refs_6_ = bf16[128,1152]{1,0:T(8,128)(2,1)S(1)} collective-permute-done((bf16[128,1152]{1,0:T(8,128)(2,1)S(1)}, bf16[128,1152]{1,0:T(8,128)(2,1)S(1)}, u32[]{:S(2)}, u32[]{:S(2)}) %collective-permute-start.3) | collective-permute-done | bytes 294944 | tf_op jit(solution)/shard_map/ppermute | solution.py:274
  29.7 0.0 collective-permute-done.6.refs_3_.refs_4_.refs_6_
  29.7 0.0 collective-permute-start.9
  29.7 0.5 collective-permute-start.8
  30.2 1.3 %late_rows_begun.2.refs_5_ = f32[128,1152]{1,0:T(8,128)S(1)} custom-call(f32[1]{0:T(128)S(6)} %copy.21.refs_0_, f32[1]{0:T(128)S(6)} %copy.22.refs_1_, bf16[128,1152]{1,0:T(8,128)(2,1)S(1)} %collective-permute-done.3.refs_2_.refs_4_.refs_6_, bf16[136,1152]{1,0:T(8,128)(2,1)S(1)} %collective-permute-done.6.refs_3_.refs_4_.refs_6_, ...), custom_call_target="tpu_custom_call" | custom-call | flops 896 | bytes 896 | tf_op jit(solution)/shard_map/late_rows_begun/pallas_call | solution.py:93
  31.5 0.0 collective-permute-done.9.refs_4_.refs_5_.refs_7_
  31.5 0.6 late_rows.2
  32.1 1.6 %collective-permute-start.11 = (s16[136,512]{1,0:T(8,128)(2,1)S(1)}, s16[136,512]{1,0:T(8,128)(2,1)S(1)}, u32[]{:S(2)}, u32[]{:S(2)}) collective-permute-start(s16[136,512]{1,0:T(8,128)(2,1)S(1)} %get-tuple-element.46.refs_8_), channel_id=1, source_target_pairs={{0,16},{8,24},{16,0},{24,8},{1,17},{9,25},{17,1},{25,9},{2,18},{10... | collective-permute-start | bytes 417800 | tf_op jit(solution)/shard_map/ppermute | solution.py:274
  33.7 1.3 %late_rows_begun.3.refs_5_ = f32[128,1152]{1,0:T(8,128)S(1)} custom-call(f32[1]{0:T(128)S(6)} %copy.21.refs_0_, f32[1]{0:T(128)S(6)} %copy.22.refs_1_, bf16[128,1152]{1,0:T(8,128)(2,1)S(1)} %collective-permute-done.3.refs_2_.refs_4_.refs_6_, bf16[136,1152]{1,0:T(8,128)(2,1)S(1)} %collective-permute-done.6.refs_3_.refs_4_.refs_6_, ...), custom_call_target="tpu_custom_call" | custom-call | flops 896 | bytes 896 | tf_op jit(solution)/shard_map/late_rows_begun/pallas_call | solution.py:93
  35.1 0.0 collective-permute-done.8.refs_4_.refs_5_.refs_7_
  35.1 0.6 late_rows.3
  35.7 0.7 %collective-permute-start.10 = (s16[136,512]{1,0:T(8,128)(2,1)S(1)}, s16[136,512]{1,0:T(8,128)(2,1)S(1)}, u32[]{:S(2)}, u32[]{:S(2)}) collective-permute-start(s16[136,512]{1,0:T(8,128)(2,1)S(1)} %get-tuple-element.48.refs_7_), channel_id=1, source_target_pairs={{0,8},{8,0},{16,24},{24,16},{1,9},{9,1},{17,25},{25,17},{2,10},{10... | collective-permute-start | bytes 417800 | tf_op jit(solution)/shard_map/ppermute | solution.py:274
  36.4 0.7 %late_columns.4.refs_7_.refs_0_ = f32[128,1152]{1,0:T(8,128)S(1)} custom-call(f32[1]{0:T(128)S(6)} %copy.21.refs_0_, f32[1]{0:T(128)S(6)} %copy.22.refs_1_, bf16[128,1152]{1,0:T(8,128)(2,1)S(1)} %held.3.refs_2_.refs_0_.refs_5_, bf16[136,1152]{1,0:T(8,128)(2,1)S(1)} %labelled.3.refs_1_.refs_3_.refs_5_, ...), custom_call_target="tpu_custom_call" | custom-call | flops 256 | bytes 256 | tf_op jit(solution)/shard_map/late_columns/pallas_call | solution.py:93
  37.1 0.7 %collective-permute-done.11.refs_1_ = s16[136,512]{1,0:T(8,128)(2,1)S(1)} collective-permute-done((s16[136,512]{1,0:T(8,128)(2,1)S(1)}, s16[136,512]{1,0:T(8,128)(2,1)S(1)}, u32[]{:S(2)}, u32[]{:S(2)}) %collective-permute-start.11) | collective-permute-done | bytes 139296 | tf_op jit(solution)/shard_map/ppermute | solution.py:274
  37.8 0.1 passed_sum.5
  37.9 1.6 %collective-permute-start.13 = (s16[136,640]{1,0:T(8,128)(2,1)S(1)}, s16[136,640]{1,0:T(8,128)(2,1)S(1)}, u32[]{:S(2)}, u32[]{:S(2)}) collective-permute-start(s16[136,640]{1,0:T(8,128)(2,1)S(1)} %get-tuple-element.54), channel_id=1, source_target_pairs={{0,16},{8,24},{16,0},{24,8},{1,17},{9,25},{17,1},{25,9},{2,18},{10... | collective-permute-start | bytes 522248 | tf_op jit(solution)/shard_map/ppermute | solution.py:274
  39.5 1.3 %collective-permute-start.12 = (s16[136,512]{1,0:T(8,128)(2,1)S(1)}, s16[136,512]{1,0:T(8,128)(2,1)S(1)}, u32[]{:S(2)}, u32[]{:S(2)}) collective-permute-start(s16[136,512]{1,0:T(8,128)(2,1)S(1)} %get-tuple-element.53), channel_id=1, source_target_pairs={{0,4},{1,5},{2,6},{3,7},{4,0},{5,1},{6,2},{7,3},{8,12},{9,13},{10,... | collective-permute-start | bytes 417800 | tf_op jit(solution)/shard_map/ppermute | solution.py:274
  40.8 0.7 %late_columns.5.refs_0_ = f32[128,1152]{1,0:T(8,128)S(1)} custom-call(f32[1]{0:T(128)S(6)} %copy.21.refs_0_, f32[1]{0:T(128)S(6)} %copy.22.refs_1_, bf16[128,1152]{1,0:T(8,128)(2,1)S(1)} %held.3.refs_2_.refs_0_.refs_5_, bf16[136,1152]{1,0:T(8,128)(2,1)S(1)} %labelled.3.refs_1_.refs_3_.refs_5_, ...), custom_call_target="tpu_custom_call" | custom-call | flops 256 | bytes 256 | tf_op jit(solution)/shard_map/late_columns/pallas_call | solution.py:93
  41.5 0.0 collective-permute-done.10.refs_1_
  41.5 0.1 passed_sum.4
  41.6 0.7 %collective-permute-start.16 = (s16[136,640]{1,0:T(8,128)(2,1)S(1)}, s16[136,640]{1,0:T(8,128)(2,1)S(1)}, u32[]{:S(2)}, u32[]{:S(2)}) collective-permute-start(s16[136,640]{1,0:T(8,128)(2,1)S(1)} %get-tuple-element.57), channel_id=1, source_target_pairs={{0,8},{8,0},{16,24},{24,16},{1,9},{9,1},{17,25},{25,17},{2,10},{10... | collective-permute-start | bytes 522248 | tf_op jit(solution)/shard_map/ppermute | solution.py:274
  42.4 2.4 %collective-permute-start.15 = (s16[136,512]{1,0:T(8,128)(2,1)S(1)}, s16[136,512]{1,0:T(8,128)(2,1)S(1)}, u32[]{:S(2)}, u32[]{:S(2)}) collective-permute-start(s16[136,512]{1,0:T(8,128)(2,1)S(1)} %get-tuple-element.50.refs_10_), channel_id=1, source_target_pairs={{0,2},{1,3},{2,0},{3,1},{4,6},{5,7},{6,4},{7,5},{8,10},{9,11},{10,... | collective-permute-start | bytes 417800 | tf_op jit(solution)/shard_map/ppermute | solution.py:274
  44.7 3.1 %collective-permute-done.12.refs_2_.refs_0_ = s16[136,512]{1,0:T(8,128)(2,1)S(1)} collective-permute-done((s16[136,512]{1,0:T(8,128)(2,1)S(1)}, s16[136,512]{1,0:T(8,128)(2,1)S(1)}, u32[]{:S(2)}, u32[]{:S(2)}) %collective-permute-start.12) | collective-permute-done | bytes 139296 | tf_op jit(solution)/shard_map/ppermute | solution.py:274
  47.9 0.0 collective-permute-done.13.refs_1_
  47.9 0.1 passed_sum.6.refs_3_
  48.0 0.1 collective-permute-start.14
  48.1 1.0 %late_columns.6 = (f32[128,1152]{1,0:T(8,128)S(1)}, s16[136,1152]{1,0:T(8,128)(2,1)S(1)}) custom-call(f32[1]{0:T(128)S(6)} %copy.21.refs_0_, f32[1]{0:T(128)S(6)} %copy.22.refs_1_, bf16[128,1152]{1,0:T(8,128)(2,1)S(1)} %collective-permute-done.refs_3_.refs_4_.refs_6_.refs_2_, bf16[136,1152]{1,0:T(8,128)(2,1)S(1)} %collective-permute-done.1.refs_4_.refs_5_.refs_6_.refs_3_, ...), custom_call_target="tpu_custom_call" | custom-call | flops 512 | bytes 512 | tf_op jit(solution)/shard_map/late_columns/pallas_call | solution.py:93
  49.0 1.0 %late_columns.7 = (f32[128,1152]{1,0:T(8,128)S(1)}, s16[136,1152]{1,0:T(8,128)(2,1)S(1)}) custom-call(f32[1]{0:T(128)S(6)} %copy.21.refs_0_, f32[1]{0:T(128)S(6)} %copy.22.refs_1_, bf16[128,1152]{1,0:T(8,128)(2,1)S(1)} %collective-permute-done.refs_3_.refs_4_.refs_6_.refs_2_, bf16[136,1152]{1,0:T(8,128)(2,1)S(1)} %collective-permute-done.1.refs_4_.refs_5_.refs_6_.refs_3_, ...), custom_call_target="tpu_custom_call" | custom-call | flops 512 | bytes 512 | tf_op jit(solution)/shard_map/late_columns/pallas_call | solution.py:93
  50.0 0.7 %collective-permute-start.18 = (s16[136,1152]{1,0:T(8,128)(2,1)S(1)}, s16[136,1152]{1,0:T(8,128)(2,1)S(1)}, u32[]{:S(2)}, u32[]{:S(2)}) collective-permute-start(s16[136,1152]{1,0:T(8,128)(2,1)S(1)} %get-tuple-element.60), channel_id=1, source_target_pairs={{0,8},{8,0},{16,24},{24,16},{1,9},{9,1},{17,25},{25,17},{2,10},{10... | collective-permute-start | bytes 940040 | tf_op jit(solution)/shard_map/ppermute | solution.py:274
  50.8 0.9 %collective-permute-start.19 = (s16[136,1152]{1,0:T(8,128)(2,1)S(1)}, s16[136,1152]{1,0:T(8,128)(2,1)S(1)}, u32[]{:S(2)}, u32[]{:S(2)}) collective-permute-start(s16[136,1152]{1,0:T(8,128)(2,1)S(1)} %get-tuple-element.51.refs_10_), channel_id=1, source_target_pairs={{0,16},{8,24},{16,0},{24,8},{1,17},{9,25},{17,1},{25,9},{2,18},{10... | collective-permute-start | bytes 940040 | tf_op jit(solution)/shard_map/ppermute | solution.py:274
  51.6 0.0 collective-permute-done.15.refs_2_
  51.6 0.0 collective-permute-done.16.refs_1_
  51.6 0.1 passed_sum.7
  51.7 2.9 %collective-permute-start.17 = (s16[136,640]{1,0:T(8,128)(2,1)S(1)}, s16[136,640]{1,0:T(8,128)(2,1)S(1)}, u32[]{:S(2)}, u32[]{:S(2)}) collective-permute-start(s16[136,640]{1,0:T(8,128)(2,1)S(1)} %passed_sum.7), channel_id=1, source_target_pairs={{0,2},{1,3},{2,0},{3,1},{4,6},{5,7},{6,4},{7,5},{8,10},{9,11},{10,... | collective-permute-start | bytes 522248 | tf_op jit(solution)/shard_map/ppermute | solution.py:274
  54.6 2.5 %collective-permute-done.14.refs_1_ = s16[136,640]{1,0:T(8,128)(2,1)S(1)} collective-permute-done((s16[136,640]{1,0:T(8,128)(2,1)S(1)}, s16[136,640]{1,0:T(8,128)(2,1)S(1)}, u32[]{:S(2)}, u32[]{:S(2)}) %collective-permute-start.14) | collective-permute-done | bytes 174112 | tf_op jit(solution)/shard_map/ppermute | solution.py:274
  57.1 3.6 %collective-permute-done.17.refs_3_ = s16[136,640]{1,0:T(8,128)(2,1)S(1)} collective-permute-done((s16[136,640]{1,0:T(8,128)(2,1)S(1)}, s16[136,640]{1,0:T(8,128)(2,1)S(1)}, u32[]{:S(2)}, u32[]{:S(2)}) %collective-permute-start.17) | collective-permute-done | bytes 174112 | tf_op jit(solution)/shard_map/ppermute | solution.py:274
  60.8 0.0 collective-permute-done.18.refs_4_
  60.8 0.0 collective-permute-done.19.refs_8_
  60.8 1.2 %output_sums.1 = (f32[128,1152]{1,0:T(8,128)}, f32[128,1152]{1,0:T(8,128)}) custom-call(f32[1]{0:T(128)S(6)} %copy.21.refs_0_, f32[128,1152]{1,0:T(8,128)S(1)} %get-tuple-element.52.refs_1_, s16[136,512]{1,0:T(8,128)(2,1)S(1)} %get-tuple-element.58.refs_2_, s16[136,640]{1,0:T(8,128)(2,1)S(1)} %get-tuple-element.59.refs_3_, ...), custom_call_target="tpu_custom_call" | custom-call | flops 128 | bytes 128 | tf_op jit(solution)/shard_map/output_sums/pallas_call | solution.py:93
  (6 shorter events, 0.1 us)
Async XLA Ops:
  0.6 17.8 %collective-permute-start.2 = (bf16[128,1152]{1,0:T(8,128)(2,1)}, bf16[128,1152]{1,0:T(8,128)(2,1)S(1)}, u32[]{:S(2)}, u32[]{:S(2)}) collective-permute-start(bf16[128,1152]{1,0:T(8,128)(2,1)} %refs_4_.5), channel_id=1, source_target_pairs={{0,4},{1,5},{2,6},{3,7},{4,0},{5,1},{6,2},{7,3},{8,12},{9,13},{10,... | collective-permute-start | bytes 884744 | tf_op jit(solution)/shard_map/ppermute | solution.py:274
  4.7 13.9 %collective-permute-start.4 = (bf16[128,1152]{1,0:T(8,128)(2,1)}, bf16[128,1152]{1,0:T(8,128)(2,1)S(1)}, u32[]{:S(2)}, u32[]{:S(2)}) collective-permute-start(bf16[128,1152]{1,0:T(8,128)(2,1)} %refs_0_.12), channel_id=1, source_target_pairs={{0,2},{1,3},{2,0},{3,1},{4,6},{5,7},{6,4},{7,5},{8,10},{9,11},{10,... | collective-permute-start | bytes 884744 | tf_op jit(solution)/shard_map/ppermute | solution.py:274
  6.3 1.0 %copy-start.1 = (bf16[128,1152]{1,0:T(8,128)(2,1)S(1)}, bf16[128,1152]{1,0:T(8,128)(2,1)}, u32[]{:S(2)}) copy-start(bf16[128,1152]{1,0:T(8,128)(2,1)} %refs_0_.12) | copy-start | bytes 884740
  7.3 0.7 %copy-start.2 = (s32[128]{0:T(128)S(1)}, s32[128]{0:T(128)}, u32[]{:S(2)}) copy-start(s32[128]{0:T(128)} %param.7) | copy-start | bytes 1540
  8.0 10.8 %copy-start = (bf16[128,1152]{1,0:T(8,128)(2,1)S(1)}, bf16[128,1152]{1,0:T(8,128)(2,1)}, u32[]{:S(2)}) copy-start(bf16[128,1152]{1,0:T(8,128)(2,1)} %refs_4_.5) | copy-start | bytes 884740
  8.0 10.7 %collective-permute-start.1 = (bf16[136,1152]{1,0:T(8,128)(2,1)S(1)}, bf16[136,1152]{1,0:T(8,128)(2,1)S(1)}, u32[]{:S(2)}, u32[]{:S(2)}) collective-permute-start(bf16[136,1152]{1,0:T(8,128)(2,1)S(1)} %labelled.2.refs_2_.refs_7_.refs_4_.refs_5_), channel_id=1, source_target_pairs={{0,8},{8,0},{16,24},{24,16},{1,9},{9,1},{17,25},{25,17},{2,10},{10... | collective-permute-start | bytes 940040 | tf_op jit(solution)/shard_map/ppermute | solution.py:274
  9.6 9.2 %collective-permute-start = (bf16[128,1152]{1,0:T(8,128)(2,1)}, bf16[128,1152]{1,0:T(8,128)(2,1)S(1)}, u32[]{:S(2)}, u32[]{:S(2)}) collective-permute-start(bf16[128,1152]{1,0:T(8,128)(2,1)} %refs_4_.5), channel_id=1, source_target_pairs={{0,16},{8,24},{16,0},{24,8},{1,17},{9,25},{17,1},{25,9},{2,18},{10... | collective-permute-start | bytes 884744 | tf_op jit(solution)/shard_map/ppermute | solution.py:274
  11.1 7.6 %collective-permute-start.5 = (s32[1,128]{1,0:T(1,128)S(1)}, s32[1,128]{1,0:T(1,128)S(1)}, u32[]{:S(2)}, u32[]{:S(2)}) collective-permute-start(s32[1,128]{1,0:T(1,128)S(1)} %bitcast.2), channel_id=1, source_target_pairs={{0,2},{1,3},{2,0},{3,1},{4,6},{5,7},{6,4},{7,5},{8,10},{9,11},{10,... | collective-permute-start | bytes 1544 | tf_op jit(solution)/shard_map/ppermute | solution.py:274
  18.9 4.5 %collective-permute-start.7 = (bf16[792,1152]{1,0:T(8,128)(2,1)S(1)}, bf16[792,1152]{1,0:T(8,128)(2,1)S(1)}, u32[]{:S(2)}, u32[]{:S(2)}) collective-permute-start(bf16[792,1152]{1,0:T(8,128)(2,1)S(1)} %bundled.3), channel_id=1, source_target_pairs={{0,1},{1,0},{2,3},{3,2},{4,5},{5,4},{6,7},{7,6},{8,9},{9,8},{10,11... | collective-permute-start | bytes 5474312 | tf_op jit(solution)/shard_map/ppermute | solution.py:274
  19.0 10.7 %collective-permute-start.6 = (bf16[136,1152]{1,0:T(8,128)(2,1)S(1)}, bf16[136,1152]{1,0:T(8,128)(2,1)S(1)}, u32[]{:S(2)}, u32[]{:S(2)}) collective-permute-start(bf16[136,1152]{1,0:T(8,128)(2,1)S(1)} %labelled.3.refs_1_.refs_3_.refs_5_), channel_id=1, source_target_pairs={{0,8},{8,0},{16,24},{24,16},{1,9},{9,1},{17,25},{25,17},{2,10},{10... | collective-permute-start | bytes 940040 | tf_op jit(solution)/shard_map/ppermute | solution.py:274
  20.6 9.1 %collective-permute-start.3 = (bf16[128,1152]{1,0:T(8,128)(2,1)S(1)}, bf16[128,1152]{1,0:T(8,128)(2,1)S(1)}, u32[]{:S(2)}, u32[]{:S(2)}) collective-permute-start(bf16[128,1152]{1,0:T(8,128)(2,1)S(1)} %held.3.refs_2_.refs_0_.refs_5_), channel_id=1, source_target_pairs={{0,16},{8,24},{16,0},{24,8},{1,17},{9,25},{17,1},{25,9},{2,18},{10... | collective-permute-start | bytes 884744 | tf_op jit(solution)/shard_map/ppermute | solution.py:274
  29.7 1.9 %collective-permute-start.9 = (bf16[136,1152]{1,0:T(8,128)(2,1)S(1)}, bf16[136,1152]{1,0:T(8,128)(2,1)S(1)}, u32[]{:S(2)}, u32[]{:S(2)}) collective-permute-start(bf16[136,1152]{1,0:T(8,128)(2,1)S(1)} %collective-permute-done.6.refs_3_.refs_4_.refs_6_), channel_id=1, source_target_pairs={{0,1},{1,0},{2,3},{3,2},{4,5},{5,4},{6,7},{7,6},{8,9},{9,8},{10,11... | collective-permute-start | bytes 940040 | tf_op jit(solution)/shard_map/ppermute | solution.py:274
  29.7 5.4 %collective-permute-start.8 = (bf16[128,1152]{1,0:T(8,128)(2,1)S(1)}, bf16[128,1152]{1,0:T(8,128)(2,1)S(1)}, u32[]{:S(2)}, u32[]{:S(2)}) collective-permute-start(bf16[128,1152]{1,0:T(8,128)(2,1)S(1)} %collective-permute-done.3.refs_2_.refs_4_.refs_6_), channel_id=1, source_target_pairs={{0,1},{1,0},{2,3},{3,2},{4,5},{5,4},{6,7},{7,6},{8,9},{9,8},{10,11... | collective-permute-start | bytes 884744 | tf_op jit(solution)/shard_map/ppermute | solution.py:274
  32.1 5.6 %collective-permute-start.11 = (s16[136,512]{1,0:T(8,128)(2,1)S(1)}, s16[136,512]{1,0:T(8,128)(2,1)S(1)}, u32[]{:S(2)}, u32[]{:S(2)}) collective-permute-start(s16[136,512]{1,0:T(8,128)(2,1)S(1)} %get-tuple-element.46.refs_8_), channel_id=1, source_target_pairs={{0,16},{8,24},{16,0},{24,8},{1,17},{9,25},{17,1},{25,9},{2,18},{10... | collective-permute-start | bytes 417800 | tf_op jit(solution)/shard_map/ppermute | solution.py:274
  35.7 5.8 %collective-permute-start.10 = (s16[136,512]{1,0:T(8,128)(2,1)S(1)}, s16[136,512]{1,0:T(8,128)(2,1)S(1)}, u32[]{:S(2)}, u32[]{:S(2)}) collective-permute-start(s16[136,512]{1,0:T(8,128)(2,1)S(1)} %get-tuple-element.48.refs_7_), channel_id=1, source_target_pairs={{0,8},{8,0},{16,24},{24,16},{1,9},{9,1},{17,25},{25,17},{2,10},{10... | collective-permute-start | bytes 417800 | tf_op jit(solution)/shard_map/ppermute | solution.py:274
  37.9 10.0 %collective-permute-start.13 = (s16[136,640]{1,0:T(8,128)(2,1)S(1)}, s16[136,640]{1,0:T(8,128)(2,1)S(1)}, u32[]{:S(2)}, u32[]{:S(2)}) collective-permute-start(s16[136,640]{1,0:T(8,128)(2,1)S(1)} %get-tuple-element.54), channel_id=1, source_target_pairs={{0,16},{8,24},{16,0},{24,8},{1,17},{9,25},{17,1},{25,9},{2,18},{10... | collective-permute-start | bytes 522248 | tf_op jit(solution)/shard_map/ppermute | solution.py:274
  39.5 8.4 %collective-permute-start.12 = (s16[136,512]{1,0:T(8,128)(2,1)S(1)}, s16[136,512]{1,0:T(8,128)(2,1)S(1)}, u32[]{:S(2)}, u32[]{:S(2)}) collective-permute-start(s16[136,512]{1,0:T(8,128)(2,1)S(1)} %get-tuple-element.53), channel_id=1, source_target_pairs={{0,4},{1,5},{2,6},{3,7},{4,0},{5,1},{6,2},{7,3},{8,12},{9,13},{10,... | collective-permute-start | bytes 417800 | tf_op jit(solution)/shard_map/ppermute | solution.py:274
  41.6 10.0 %collective-permute-start.16 = (s16[136,640]{1,0:T(8,128)(2,1)S(1)}, s16[136,640]{1,0:T(8,128)(2,1)S(1)}, u32[]{:S(2)}, u32[]{:S(2)}) collective-permute-start(s16[136,640]{1,0:T(8,128)(2,1)S(1)} %get-tuple-element.57), channel_id=1, source_target_pairs={{0,8},{8,0},{16,24},{24,16},{1,9},{9,1},{17,25},{25,17},{2,10},{10... | collective-permute-start | bytes 522248 | tf_op jit(solution)/shard_map/ppermute | solution.py:274
  42.4 9.3 %collective-permute-start.15 = (s16[136,512]{1,0:T(8,128)(2,1)S(1)}, s16[136,512]{1,0:T(8,128)(2,1)S(1)}, u32[]{:S(2)}, u32[]{:S(2)}) collective-permute-start(s16[136,512]{1,0:T(8,128)(2,1)S(1)} %get-tuple-element.50.refs_10_), channel_id=1, source_target_pairs={{0,2},{1,3},{2,0},{3,1},{4,6},{5,7},{6,4},{7,5},{8,10},{9,11},{10,... | collective-permute-start | bytes 417800 | tf_op jit(solution)/shard_map/ppermute | solution.py:274
  48.0 9.2 %collective-permute-start.14 = (s16[136,640]{1,0:T(8,128)(2,1)S(1)}, s16[136,640]{1,0:T(8,128)(2,1)S(1)}, u32[]{:S(2)}, u32[]{:S(2)}) collective-permute-start(s16[136,640]{1,0:T(8,128)(2,1)S(1)} %passed_sum.6.refs_3_), channel_id=1, source_target_pairs={{0,4},{1,5},{2,6},{3,7},{4,0},{5,1},{6,2},{7,3},{8,12},{9,13},{10,... | collective-permute-start | bytes 522248 | tf_op jit(solution)/shard_map/ppermute | solution.py:274
  50.0 10.7 %collective-permute-start.18 = (s16[136,1152]{1,0:T(8,128)(2,1)S(1)}, s16[136,1152]{1,0:T(8,128)(2,1)S(1)}, u32[]{:S(2)}, u32[]{:S(2)}) collective-permute-start(s16[136,1152]{1,0:T(8,128)(2,1)S(1)} %get-tuple-element.60), channel_id=1, source_target_pairs={{0,8},{8,0},{16,24},{24,16},{1,9},{9,1},{17,25},{25,17},{2,10},{10... | collective-permute-start | bytes 940040 | tf_op jit(solution)/shard_map/ppermute | solution.py:274
  50.8 10.0 %collective-permute-start.19 = (s16[136,1152]{1,0:T(8,128)(2,1)S(1)}, s16[136,1152]{1,0:T(8,128)(2,1)S(1)}, u32[]{:S(2)}, u32[]{:S(2)}) collective-permute-start(s16[136,1152]{1,0:T(8,128)(2,1)S(1)} %get-tuple-element.51.refs_10_), channel_id=1, source_target_pairs={{0,16},{8,24},{16,0},{24,8},{1,17},{9,25},{17,1},{25,9},{2,18},{10... | collective-permute-start | bytes 940040 | tf_op jit(solution)/shard_map/ppermute | solution.py:274
  51.7 9.0 %collective-permute-start.17 = (s16[136,640]{1,0:T(8,128)(2,1)S(1)}, s16[136,640]{1,0:T(8,128)(2,1)S(1)}, u32[]{:S(2)}, u32[]{:S(2)}) collective-permute-start(s16[136,640]{1,0:T(8,128)(2,1)S(1)} %passed_sum.7), channel_id=1, source_target_pairs={{0,2},{1,3},{2,0},{3,1},{4,6},{5,7},{6,4},{7,5},{8,10},{9,11},{10,... | collective-permute-start | bytes 522248 | tf_op jit(solution)/shard_map/ppermute | solution.py:274
